TPU v7x, 32 devices: a whole 2x2x4 slice. The times are simulated.
32 devices in a mesh: cuts: 8 (over z, y), loop: 4 (over x, core).
Axes of the slice: x: 2, y: 2, z: 4, core: 2. Of those that a mesh axis runs over, the one named last changes fastest.
Arguments:
- image_features: bfloat16 [8192, 1152], P(('cuts', 'loop')), may hold values from -0.1796875 to 0.1796875
- text_features: bfloat16 [8192, 1152], P(('cuts', 'loop')), may hold values from -0.1796875 to 0.1796875
- image_head: bfloat16 [1152, 1152], replicated, may hold values from -0.1875 to 0.1875
- text_head: bfloat16 [1152, 1152], replicated, may hold values from -0.1875 to 0.1875
Outputs:
- image_grad: float32 [8192, 1152], P(('cuts', 'loop'))
- text_grad: float32 [8192, 1152], P(('cuts', 'loop'))
- image_head_grad: float32 [1152, 1152], P('loop')
- text_head_grad: float32 [1152, 1152], P('loop')
All inputs are finite; a program needn't handle non-finite values.
Results may differ from a plain program's by a relative error of at most 0.024.
Values may be sent and summed in bfloat16 or wider, within the bound.
No kernel may reach another device: no remote copies, remote signals or barrier semaphores. Data moves between devices by JAX's collectives and lax.ppermute only.
A program may use at most 128 MiB of HBM per device.

v0:
```python
import jax
import jax.numpy as jnp
from jax import lax
from jax.sharding import PartitionSpec as P

SCORE_SCALE = 10.0
SCORE_BIAS = -2.5
EPSILON = 1e-06


def normalize(features, weight_matrix):
    projected = jnp.dot(features, weight_matrix, preferred_element_type=jnp.float32)
    factor = lax.rsqrt(jnp.sum(projected * projected, axis=-1, keepdims=True) + EPSILON)
    return (projected * factor, factor)


def pair_weights(image_vectors, text_vectors, image_offset):
    pair_scores = (
        SCORE_SCALE
        * lax.dot_general(
            image_vectors,
            text_vectors,
            (((1,), (1,)), ((), ())),
            preferred_element_type=jnp.float32,
        )
        + SCORE_BIAS
    )
    row_ids = image_offset + lax.broadcasted_iota(jnp.int32, pair_scores.shape, 0)
    col_ids = lax.broadcasted_iota(jnp.int32, pair_scores.shape, 1)
    match_targets = jnp.where(row_ids == col_ids, 1.0, -1.0).astype(jnp.float32)
    return (SCORE_SCALE * -match_targets * jax.nn.sigmoid(-match_targets * pair_scores)).astype(
        jnp.bfloat16
    )


def norm_back(unit, factor, gradient):
    return (factor * (gradient - unit * jnp.sum(unit * gradient, axis=-1, keepdims=True))).astype(
        jnp.bfloat16
    )


def contract_rows(left, right):
    return lax.dot_general(
        left, right, (((0,), (0,)), ((), ())), preferred_element_type=jnp.float32
    )


def per_device(image_features, text_features, image_head, text_head):
    row_count = image_features.shape[0]
    my_place = lax.axis_index("loop")
    own_start = my_place * row_count
    image_unit, image_factor = normalize(image_features, image_head)
    text_unit, text_factor = normalize(text_features, text_head)
    image_vectors = image_unit.astype(jnp.bfloat16)
    text_vectors = text_unit.astype(jnp.bfloat16)
    arrived = lax.all_gather(text_vectors, "loop", axis=0, tiled=True)
    weights = pair_weights(image_vectors, arrived, own_start)
    summed = jnp.dot(weights, arrived, preferred_element_type=jnp.float32)
    text_attraction = lax.psum_scatter(
        contract_rows(weights, image_vectors).astype(jnp.bfloat16),
        "loop",
        scatter_dimension=0,
        tiled=True,
    ).astype(jnp.float32)
    image_back = norm_back(image_unit, image_factor, summed)
    text_back = norm_back(text_unit, text_factor, text_attraction)
    image_grad = lax.dot_general(
        image_back, image_head, (((1,), (1,)), ((), ())), preferred_element_type=jnp.float32
    )
    text_grad = lax.dot_general(
        text_back, text_head, (((1,), (1,)), ((), ())), preferred_element_type=jnp.float32
    )
    image_wgrad = contract_rows(image_features, image_back).astype(jnp.bfloat16)
    text_wgrad = contract_rows(text_features, text_back).astype(jnp.bfloat16)
    image_part, text_part = (
        lax.psum_scatter(image_wgrad, "loop", scatter_dimension=0, tiled=True).astype(jnp.float32),
        lax.psum_scatter(text_wgrad, "loop", scatter_dimension=0, tiled=True).astype(jnp.float32),
    )
    image_head_grad, text_head_grad = (
        lax.psum(image_part.astype(jnp.bfloat16), "cuts").astype(jnp.float32),
        lax.psum(text_part.astype(jnp.bfloat16), "cuts").astype(jnp.float32),
    )
    return (image_grad, text_grad, image_head_grad, text_head_grad)


def solution(mesh):
    placed = (P(("cuts", "loop"), None), P(("cuts", "loop"), None), P(), P())
    return jax.shard_map(
        per_device,
        mesh=mesh,
        in_specs=placed,
        out_specs=(
            P(("cuts", "loop"), None),
            P(("cuts", "loop"), None),
            P("loop", None),
            P("loop", None),
        ),
        check_vma=False,
    )
```

profile of v0, /device:TPU:0, one launch (start us, length us, event | category | flops | bytes accessed | tf_op | source)
XLA Modules:
  0.0 262.0 jit_solution(7458655789808462947)
XLA Ops:
  7.2 3.2 %multiply_reduce_fusion.1 = (f32[256]{0:T(256)S(1)}, f32[256,1152]{1,0:T(8,128)S(1)}) fusion(bf16[256,1152]{1,0:T(8,128)(2,1)} %param.5, bf16[1152,1152]{1,0:T(8,128)(2,1)} %param.7), kind=kOutput, calls=%fused_computation.21 | convolution fusion | flops 680066816 | bytes 4424704 | tf_op jit(solution)/shard_map/dot_general | solution.py:12
  10.4 1.0 copy-done.3
  11.4 0.9 multiply_convert_fusion.1
  12.4 0.0 reduce-scatter.8.cloned.1.call-start
  12.5 0.1 copy-done.9
  12.5 2.0 multiply_reduce_fusion.2
  14.6 24.7 %all-gather.2.cloned.1.call-done = bf16[1024,1152]{1,0:T(8,128)(2,1)} async-done(((bf16[256,1152]{1,0:T(8,128)(2,1)}), bf16[1024,1152]{1,0:T(8,128)(2,1)}) %all-gather.2.cloned.1.call-update) | async-done | bytes 2359312 | tf_op jit(solution)/shard_map/all_gather | solution.py:56
  39.3 3.3 %fusion.9 = bf16[256,1024]{1,0:T(8,128)(2,1)S(1)} fusion(bf16[1024,1152]{1,0:T(8,128)(2,1)} %all-gather.2.cloned.1.call-done, s32[256]{0:T(256)S(1)} %iota_add_fusion, f32[256,1152]{1,0:T(8,128)} %get-tuple-element.17, f32[256]{0:T(256)S(1)} %add_rsqrt_fusion.1), kind=kOutput, calls=%fused_computation.15 | convolution fusion | flops 607715328 | bytes 4065280 | tf_op jit(solution)/shard_map/dot_general | solution.py:20
  42.6 2.4 convolution_convert_fusion.2
  45.1 3.0 %multiply_reduce_fusion = (f32[256]{0:T(256)S(1)}, f32[256,1152]{1,0:T(8,128)S(1)}) fusion(f32[256,1152]{1,0:T(8,128)} %get-tuple-element.17, f32[256]{0:T(256)S(1)} %add_rsqrt_fusion.1, bf16[256,1024]{1,0:T(8,128)(2,1)S(1)} %fusion.9, bf16[1024,1152]{1,0:T(8,128)(2,1)} %all-gather.2.cloned.1.call-done), kind=kOutput, calls=%fused_computation.20 | convolution fusion | flops 604864256 | bytes 5244928 | tf_op jit(solution)/shard_map/dot_general | solution.py:58
  48.1 0.2 multiply_convert_fusion
  48.3 0.8 copy-done.10
  49.2 2.6 fusion
  51.7 5.4 %copy.12 = bf16[1152,1152]{1,0:T(8,128)(2,1)} copy(bf16[1152,1152]{0,1:T(8,128)(2,1)} %fusion) | data formatting | bytes 5308416
  57.1 0.0 reduce-scatter.12.cloned.1.call-start
  57.2 21.0 %reduce-scatter.8.cloned.1.call-done = bf16[256,1152]{1,0:T(8,128)(2,1)} async-done(((bf16[1024,1152]{1,0:T(8,128)(2,1)}), bf16[256,1152]{1,0:T(8,128)(2,1)}) %reduce-scatter.8.cloned.1.call-update) | async-done | bytes 589840 | tf_op jit(solution)/shard_map/reduce_scatter | solution.py:59
  78.2 1.9 fusion.10
  80.1 0.1 copy-done.7
  80.2 0.3 fusion.12
  80.5 0.8 copy-done.5
  81.3 2.5 fusion.1
  83.8 5.3 %copy.14 = bf16[1152,1152]{1,0:T(8,128)(2,1)} copy(bf16[1152,1152]{0,1:T(8,128)(2,1)} %fusion.1) | data formatting | bytes 5308416
  89.1 0.0 all-reduce.3.cloned.1.call-start
  89.1 26.7 %reduce-scatter.10.cloned.1.call-done = bf16[288,1152]{1,0:T(8,128)(2,1)} async-done(((bf16[1152,1152]{1,0:T(8,128)(2,1)}), bf16[288,1152]{1,0:T(8,128)(2,1)}) %reduce-scatter.10.cloned.1.call-update) | async-done | bytes 663568
  115.8 2.3 copy.13
  118.1 35.0 %reduce-scatter.12.cloned.1.call-done = bf16[288,1152]{1,0:T(8,128)(2,1)} async-done(((bf16[1152,1152]{1,0:T(8,128)(2,1)}), bf16[288,1152]{1,0:T(8,128)(2,1)}) %reduce-scatter.12.cloned.1.call-update) | async-done | bytes 663568
  153.1 2.3 copy.15
  155.5 2.0 fusion.13
  157.5 2.1 fusion.14
  159.6 91.9 %all-reduce.3.cloned.1.call-done = (bf16[288,1152]{0,1:T(8,128)(2,1)}, bf16[288,1152]{0,1:T(8,128)(2,1)}) async-done(((bf16[288,1152]{0,1:T(8,128)(2,1)}, bf16[288,1152]{0,1:T(8,128)(2,1)}), (bf16[288,1152]{0,1:T(8,128)(2,1)}, bf16[288,1152]{0,1:T(8,128)(2,1)})) %all-reduce.3.cloned.1.call-update) | async-done | bytes 1327120 | tf_op jit(solution)/shard_map/psum | solution.py:80
  251.5 2.6 copy.10
  254.1 1.4 copy.11
  (31 shorter events, 0.2 us)
Async XLA Ops:
  7.2 5.3 %copy-start = (bf16[1152,1152]{1,0:T(8,128)(2,1)S(1)}, bf16[1152,1152]{1,0:T(8,128)(2,1)}, u32[]{:S(2)}) copy-start(bf16[1152,1152]{1,0:T(8,128)(2,1)} %param.6) | copy-start | bytes 7962628
  7.2 32.1 %all-gather.2.cloned.1.call-start = ((), (), s32[]{:S(2)}) async-start(), calls=%async_computation.3 | async-start | bytes 2949120 | tf_op jit(solution)/shard_map/all_gather | solution.py:56
  10.4 1.0 copy-start.3
  11.4 1.1 copy-start.9
  12.4 65.8 %reduce-scatter.8.cloned.1.call-start = ((), (), s32[]{:S(2)}) async-start(), calls=%async_computation.4 | async-start | bytes 2949120 | tf_op jit(solution)/shard_map/reduce_scatter | solution.py:59
  39.3 3.3 %copy-start.1 = (f32[256,1152]{1,0:T(8,128)S(1)}, f32[256,1152]{1,0:T(8,128)}, u32[]{:S(2)}) copy-start(f32[256,1152]{1,0:T(8,128)} %get-tuple-element.17) | copy-start | bytes 3538948
  45.0 70.8 %reduce-scatter.10.cloned.1.call-start = ((), (), s32[]{:S(2)}) async-start(), calls=%async_computation.5 | async-start | bytes 3317760
  45.1 3.0 %copy-start.2 = (f32[256,1152]{1,0:T(8,128)S(1)}, f32[256,1152]{1,0:T(8,128)}, u32[]{:S(2)}) copy-start(f32[256,1152]{1,0:T(8,128)} %get-tuple-element.17) | copy-start | bytes 3538948
  48.1 1.1 copy-start.10
  57.1 96.0 %reduce-scatter.12.cloned.1.call-start = ((), (), s32[]{:S(2)}) async-start(), calls=%async_computation.6 | async-start | bytes 3317760
  78.2 1.9 copy-start.4
  78.2 1.9 copy-start.7
  80.2 1.1 copy-start.11
  80.5 0.8 copy-start.5
  89.1 162.4 %all-reduce.3.cloned.1.call-start = ((), (), s32[]{:S(2)}) async-start(), calls=%async_computation.7 | async-start | bytes 3538944 | tf_op jit(solution)/shard_map/psum | solution.py:80
  155.5 2.1 copy-start.6
  155.5 2.1 copy-start.12
  251.5 2.6 copy-start.8
Sparse Core Ops, SparseCore 0:
  12.5 26.7 all-gather.1
  45.1 33.0 reduce-scatter.7
  80.9 34.8 reduce-scatter.9
  118.2 34.8 reduce-scatter.11
  157.6 93.8 all-reduce.2
where the time goes:
time: 263 us; the launch traced here: 262 us
  waiting for transfers between devices  199 us (76%)
  matrix products  23 us (9%)
  local copies, waits for them, and re-layouts  22 us (8%)
  between operations  13.9 us (5%)
  other arithmetic  3.36 us (1%)
    psum x1, waiting for transfers between devices, per_device(): lax.psum(image_part.astype(jnp.bfloat16), 'cuts').astype(jnp.float32)  91.9 us
    unnamed x7, waiting for transfers between devices  61.8 us
    all_gather x1, waiting for transfers between devices, per_device(): arrived = lax.all_gather(text_vectors, 'loop', axis=0, tiled=True)  24.7 us
    unnamed x32, local copies, waits for them, and re-layouts  22 us
    reduce_scatter x1, waiting for transfers between devices, per_device(): lax.psum_scatter(contract_rows(weights, image_vectors).astype(jnp.bfloat1...  21 us
    dot_general x3, matrix products, contract_rows(): lax.dot_general(left, right, (((0,), (0,)), ((), ())), preferred_element_...  7.51 us
  transfers between devices with their start and end apart: 5, of which 5 were waited for; matrix products, arithmetic and copies ran while one was open for 11% of the time, Pallas kernels for 0%

commit v1 on v0

v1 whole, which is shorter than its diff:
```python
import functools

import jax
import jax.numpy as jnp
from jax import lax
from jax.experimental import pallas as pl
from jax.experimental.pallas import tpu as pltpu
from jax.sharding import PartitionSpec as P

SCORE_SCALE = 10.0
SCORE_BIAS = -2.5
EPSILON = 1e-06
QUAD = 4
STRIP = 32
F32 = jnp.float32
BF16 = jnp.bfloat16
VMEM_LIMIT = 56 * 1024 * 1024


def normalize(features, weight_matrix):
    projected = jnp.dot(features, weight_matrix, preferred_element_type=jnp.float32)
    factor = lax.rsqrt(jnp.sum(projected * projected, axis=-1, keepdims=True) + EPSILON)
    return (projected * factor, factor)


def pair_weights(image_vectors, text_vectors, image_offset):
    pair_scores = SCORE_SCALE * dot_nt(image_vectors, text_vectors) + SCORE_BIAS
    row_ids = image_offset + lax.broadcasted_iota(jnp.int32, pair_scores.shape, 0)
    col_ids = lax.broadcasted_iota(jnp.int32, pair_scores.shape, 1)
    match_targets = jnp.where(row_ids == col_ids, 1.0, -1.0).astype(jnp.float32)
    return (SCORE_SCALE * -match_targets * jax.nn.sigmoid(-match_targets * pair_scores)).astype(
        jnp.bfloat16
    )


def norm_back(unit, factor, gradient):
    return (factor * (gradient - unit * jnp.sum(unit * gradient, axis=-1, keepdims=True))).astype(
        jnp.bfloat16
    )


def dot_nn(left, right):
    return lax.dot_general(left, right, (((1,), (0,)), ((), ())), preferred_element_type=F32)


def dot_nt(left, right):
    return lax.dot_general(left, right, (((1,), (1,)), ((), ())), preferred_element_type=F32)


def dot_tn(left, right):
    return lax.dot_general(left, right, (((0,), (0,)), ((), ())), preferred_element_type=F32)


def plain_device(image_features, text_features, image_head, text_head):
    row_count = image_features.shape[0]
    own_start = lax.axis_index("loop") * row_count
    image_unit, image_factor = normalize(image_features, image_head)
    text_unit, text_factor = normalize(text_features, text_head)
    image_vectors = image_unit.astype(jnp.bfloat16)
    text_vectors = text_unit.astype(jnp.bfloat16)
    arrived = lax.all_gather(text_vectors, "loop", axis=0, tiled=True)
    weights = pair_weights(image_vectors, arrived, own_start)
    summed = jnp.dot(weights, arrived, preferred_element_type=jnp.float32)
    text_attraction = lax.psum_scatter(
        dot_tn(weights, image_vectors).astype(jnp.bfloat16), "loop", scatter_dimension=0, tiled=True
    ).astype(jnp.float32)
    image_back = norm_back(image_unit, image_factor, summed)
    text_back = norm_back(text_unit, text_factor, text_attraction)
    heads = []
    for features, back in ((image_features, image_back), (text_features, text_back)):
        term = dot_tn(features, back).astype(jnp.bfloat16)
        part = lax.psum_scatter(term, "loop", scatter_dimension=0, tiled=True)
        heads.append(lax.psum(part, "cuts").astype(jnp.float32))
    return (dot_nt(image_back, image_head), dot_nt(text_back, text_head), heads[0], heads[1])


def strips(rows, body):
    def step(index, carry):
        body(pl.ds(pl.multiple_of(index * STRIP, STRIP), STRIP), index * STRIP)
        return carry

    lax.fori_loop(0, rows // STRIP, step, 0, unroll=2)


def unit_rows(projected_ref, vectors_ref):
    def body(rows, first):
        p = projected_ref[rows, :]
        factor = lax.rsqrt(jnp.sum(p * p, axis=-1, keepdims=True) + EPSILON)
        vectors_ref[rows, :] = (p * factor).astype(BF16)

    strips(projected_ref.shape[0], body)


def back_rows(projected_ref, gradient_ref, back_ref):
    def body(rows, first):
        p = projected_ref[rows, :]
        factor = lax.rsqrt(jnp.sum(p * p, axis=-1, keepdims=True) + EPSILON)
        unit = p * factor
        g = gradient_ref[rows, :]
        back_ref[rows, :] = (
            factor * (g - unit * jnp.sum(unit * g, axis=-1, keepdims=True))
        ).astype(BF16)

    strips(projected_ref.shape[0], body)


def weight_rows(dots_ref, weights_ref, has_pairs):
    count = dots_ref.shape[1]

    def body(rows, first):
        score = SCORE_SCALE * dots_ref[rows, :] + SCORE_BIAS
        if has_pairs:
            same = first + lax.broadcasted_iota(jnp.int32, (STRIP, count), 0) == (
                lax.broadcasted_iota(jnp.int32, (STRIP, count), 1)
            )
            value = jax.nn.sigmoid(jnp.where(same, -score, score))
            value = jnp.where(same, -SCORE_SCALE, SCORE_SCALE) * value
        else:
            value = SCORE_SCALE * jax.nn.sigmoid(score)
        weights_ref[rows, :] = value.astype(BF16)

    strips(dots_ref.shape[0], body)


def picker(place_ref, rows, width):
    part = rows // QUAD
    pieces = []
    for k in range(QUAD):
        first = place_ref[0] * rows + (place_ref[1] ^ k) * part
        wanted = first + lax.broadcasted_iota(jnp.int32, (part, width), 0)
        column = lax.broadcasted_iota(jnp.int32, (part, width), 1)
        pieces.append(jnp.where(wanted == column, 1.0, 0.0))
    return jnp.concatenate(pieces, axis=0).astype(BF16)


def near_kernel(t0, t1, i0, i1, text_head, image_head, q_a, y_a, p_a, x_a, w_aa, dots):
    half = t0.shape[0]
    for block, (t, i) in enumerate(((t0, i0), (t1, i1))):
        rows = slice(block * half, (block + 1) * half)
        q_a[rows, :] = dot_nn(t[...], text_head[...])
        p_a[rows, :] = dot_nn(i[...], image_head[...])
    unit_rows(q_a, y_a)
    unit_rows(p_a, x_a)
    dots[...] = dot_nt(x_a[...], y_a[...])
    weight_rows(dots, w_aa, True)


def text_kernel(
    place, t0, t1, t2, t3, i0, i1, text_head, y_a, p_a, x_a, w_aa,
    q_b, y_b, dp_a, gy_a, gy_b, text_pick, image_pick, dots, gx, w_ab,
):
    half = t2.shape[0]
    rows_out = text_pick.shape[0]
    for block, t in enumerate((t2, t3)):
        q_b[block * half : (block + 1) * half, :] = dot_nn(t[...], text_head[...])
    unit_rows(q_b, y_b)
    dots[...] = dot_nt(x_a[...], y_b[...])
    weight_rows(dots, w_ab, False)
    gx[...] = dot_nn(w_aa[...], y_a[...])
    gx[...] += dot_nn(w_ab[...], y_b[...])
    back_rows(p_a, gx, dp_a)
    gy_a[...] = dot_tn(w_aa[...], x_a[...])
    gy_b[...] = dot_tn(w_ab[...], x_a[...])
    pick = picker(place, rows_out, t0.shape[1])
    for block, t in enumerate((t0, t1, t2, t3)):
        text_pick[:, block * half : (block + 1) * half] = dot_nt(pick, t[...]).astype(BF16)
    for block, i in enumerate((i0, i1)):
        image_pick[:, block * half : (block + 1) * half] = dot_nt(pick, i[...]).astype(BF16)


def last_kernel(
    place, i2, i3, image_head, y_a, y_b, q_a, q_b, gy_a_in, gy_b_in, dp_a, text_pick, image_pick,
    h0, h1, h2, h3, k0, k1, k2, k3, dq_own,
    p_b, x_b, w_ba, w_bb, dots, gx, gy, dp_b, dq_a, dq_b,
):
    half = i2.shape[0]
    rows_out = text_pick.shape[0]
    part = rows_out // QUAD
    for block, i in enumerate((i2, i3)):
        p_b[block * half : (block + 1) * half, :] = dot_nn(i[...], image_head[...])
    unit_rows(p_b, x_b)
    dots[...] = dot_nt(x_b[...], y_a[...])
    weight_rows(dots, w_ba, False)
    dots[...] = dot_nt(x_b[...], y_b[...])
    weight_rows(dots, w_bb, True)
    gx[...] = dot_nn(w_ba[...], y_a[...])
    gx[...] += dot_nn(w_bb[...], y_b[...])
    back_rows(p_b, gx, dp_b)
    pick = picker(place, rows_out, i2.shape[1])
    far = jnp.concatenate([dot_nt(pick, i2[...]), dot_nt(pick, i3[...])], axis=1).astype(BF16)
    head = dot_nn(image_pick[...], dp_a[...]) + dot_nn(far, dp_b[...])
    for k, out in enumerate((h0, h1, h2, h3)):
        out[...] = head[k * part : (k + 1) * part, :].astype(BF16)
    gy[...] = gy_a_in[...] + dot_tn(w_ba[...], x_b[...])
    back_rows(q_a, gy, dq_a)
    gy[...] = gy_b_in[...] + dot_tn(w_bb[...], x_b[...])
    back_rows(q_b, gy, dq_b)
    dq_own[...] = dq_a[:half, :]
    head = dot_nn(text_pick[:, : 2 * half], dq_a[...]) + dot_nn(text_pick[:, 2 * half :], dq_b[...])
    for k, out in enumerate((k0, k1, k2, k3)):
        out[...] = head[k * part : (k + 1) * part, :].astype(BF16)


def place_kernel(place, h0, h1, h2, h3, k0, k1, k2, k3, image_out, text_out):
    part = h0.shape[0]
    for out, pieces in ((image_out, (h0, h1, h2, h3)), (text_out, (k0, k1, k2, k3))):
        for k, piece in enumerate(pieces):
            first = pl.multiple_of((place[1] ^ k) * part, part)
            out[pl.ds(first, part), :] = piece[...].astype(F32)


def call(kernel, outs, scratch, args, flops, has_place=False):
    specs = [pl.BlockSpec(memory_space=pltpu.VMEM)] * len(args)
    if has_place:
        specs[0] = pl.BlockSpec(memory_space=pltpu.SMEM)
    moved = sum(a.size * a.dtype.itemsize for a in args)
    return pl.pallas_call(
        kernel,
        out_shape=[jax.ShapeDtypeStruct(s, t) for s, t in outs],
        in_specs=specs,
        out_specs=[pl.BlockSpec(memory_space=pltpu.VMEM)] * len(outs),
        scratch_shapes=[pltpu.VMEM(s, t) for s, t in scratch],
        compiler_params=pltpu.CompilerParams(vmem_limit_bytes=VMEM_LIMIT),
        cost_estimate=pl.CostEstimate(flops=flops, bytes_accessed=moved, transcendentals=0),
    )(*args)


def swap(array, axis, size, mask):
    return lax.ppermute(array, axis, [(i, i ^ mask) for i in range(size)])


def per_device(n_loop, n_cuts, image_features, text_features, image_head, text_head):
    half, width = image_features.shape
    near = 2 * half
    rows_out = width // n_loop
    part = rows_out // QUAD
    cut = lax.axis_index("cuts")
    place = jnp.stack([lax.axis_index("loop"), cut & (QUAD - 1)]).astype(jnp.int32)
    loop = functools.partial(swap, axis="loop", size=n_loop)
    cuts = functools.partial(swap, axis="cuts", size=n_cuts)
    macs = half * width * width

    t0, i0 = text_features, image_features
    t2 = loop(t0, mask=2)
    t1 = loop(t0, mask=1)
    i1 = loop(i0, mask=1)
    i2 = loop(i0, mask=2)
    q_a, y_a, p_a, x_a, w_aa = call(
        near_kernel,
        [((near, width), F32), ((near, width), BF16), ((near, width), F32), ((near, width), BF16),
         ((near, near), BF16)],
        [((near, near), F32)],
        (t0, t1, i0, i1, text_head, image_head),
        2 * 5 * macs,
    )
    t3 = loop(t2, mask=1)
    i3 = loop(i2, mask=1)
    q_b, y_b, dp_a, gy_a, gy_b, text_pick, image_pick = call(
        text_kernel,
        [((near, width), F32), ((near, width), BF16), ((near, width), BF16), ((near, width), F32),
         ((near, width), F32), ((rows_out, 2 * near), BF16), ((rows_out, near), BF16)],
        [((near, near), F32), ((near, width), F32), ((near, near), BF16)],
        (place, t0, t1, t2, t3, i0, i1, text_head, y_a, p_a, x_a, w_aa),
        2 * 8 * macs,
        True,
    )
    image_grad = dot_nt(dp_a[:half], image_head)
    pieces = call(
        last_kernel,
        [((part, width), BF16)] * (2 * QUAD) + [((half, width), BF16)],
        [((near, width), F32), ((near, width), BF16), ((near, near), BF16), ((near, near), BF16),
         ((near, near), F32), ((near, width), F32), ((near, width), F32), ((near, width), BF16),
         ((near, width), BF16), ((near, width), BF16)],
        (place, i2, i3, image_head, y_a, y_b, q_a, q_b, gy_a, gy_b, dp_a, text_pick, image_pick),
        2 * 9 * macs,
        True,
    )
    dq_own = pieces[-1]
    sums = []
    for own, *others in (pieces[:QUAD], pieces[QUAD : 2 * QUAD]):
        total = own.astype(F32)
        for k, other in enumerate(others):
            total = total + cuts(other, mask=k + 1).astype(F32)
        sums.append(total)
    text_grad = dot_nt(dq_own, text_head)
    upper = (cut & QUAD) != 0
    kept = jnp.where(upper, sums[1], sums[0])
    sent = jnp.where(upper, sums[0], sums[1]).astype(BF16)
    mine = (kept + cuts(sent, mask=QUAD).astype(F32)).astype(BF16)
    theirs = cuts(mine, mask=QUAD)
    mine_all = [mine] + [cuts(mine, mask=k) for k in range(1, QUAD)]
    theirs_all = [theirs] + [cuts(theirs, mask=k) for k in range(1, QUAD)]
    images = [jnp.where(upper, b, a) for a, b in zip(mine_all, theirs_all)]
    texts = [jnp.where(upper, a, b) for a, b in zip(mine_all, theirs_all)]
    image_out, text_out = call(
        place_kernel,
        [((rows_out, width), F32)] * 2,
        [],
        (place, *images, *texts),
        rows_out * width,
        True,
    )
    return (image_grad, text_grad, image_out, text_out)


def solution(mesh):
    n_loop, n_cuts = mesh.shape["loop"], mesh.shape["cuts"]
    if n_loop == 4 and n_cuts == 2 * QUAD:
        body = functools.partial(per_device, n_loop, n_cuts)
    else:
        body = plain_device
    placed = (P(("cuts", "loop"), None), P(("cuts", "loop"), None), P(), P())
    return jax.shard_map(
        body,
        mesh=mesh,
        in_specs=placed,
        out_specs=(
            P(("cuts", "loop"), None),
            P(("cuts", "loop"), None),
            P("loop", None),
            P("loop", None),
        ),
        check_vma=False,
    )
```

time: 263 us -> 145 us (0.55)
  waiting for transfers between devices: 199 us -> 49.8 us
  Pallas kernels: 0 us -> 56.3 us
  starting transfers between devices: 0.21 us -> 23.8 us
  local copies, waits for them, and re-layouts: 22 us -> 3.32 us
  matrix products: 23 us -> 5.87 us
  between operations: 13.9 us -> 0.77 us
    psum x1 -> x0, waiting for transfers between devices: 91.9 us -> none  [per_device(): lax.psum(image_part.astype(jnp.bfloat16), 'cuts').astype(jnp.float32)]
    unnamed x7 -> x0, waiting for transfers between devices: 61.8 us -> none
    pallas_call x0 -> x4, Pallas kernels: none -> 56.3 us  [call(): pl.pallas_call(kernel, out_shape=[jax.ShapeDtypeStruct(s, t) for s, t in...]
    ppermute x0 -> x20, waiting for transfers between devices: none -> 49.8 us  [swap(): return lax.ppermute(array, axis, [(i, i ^ mask) for i in range(size)])]
    all_gather x1 -> x0, waiting for transfers between devices: 24.7 us -> none  [per_device(): arrived = lax.all_gather(text_vectors, 'loop', axis=0, tiled=True)]
    ppermute x0 -> x20, starting transfers between devices: none -> 23.8 us  [swap(): return lax.ppermute(array, axis, [(i, i ^ mask) for i in range(size)])]
    reduce_scatter x1 -> x0, waiting for transfers between devices: 21 us -> none  [per_device(): lax.psum_scatter(contract_rows(weights, image_vectors).astype(jnp.bfloat1...]
    unnamed x32 -> x22, local copies, waits for them, and re-layouts: 22 us -> 3.32 us
  transfers between devices with their start and end apart: 5 -> 20, of which waited for: 5 -> 13; matrix products, arithmetic and copies ran while one was open for 11% -> 6% of each run, Pallas kernels for 0% -> 20%
where the time goes in v1:
time: 145 us
  Pallas kernels  56.3 us (39%)
  waiting for transfers between devices  49.8 us (34%)
  starting transfers between devices  23.8 us (16%)
  matrix products  5.87 us (4%)
  other arithmetic  5.22 us (4%)
  local copies, waits for them, and re-layouts  3.32 us (2%)
    pallas_call x4, Pallas kernels, call(): pl.pallas_call(kernel, out_shape=[jax.ShapeDtypeStruct(s, t) for s, t in...  56.3 us
    ppermute x20, waiting for transfers between devices, swap(): return lax.ppermute(array, axis, [(i, i ^ mask) for i in range(size)])  49.8 us
    ppermute x20, starting transfers between devices, swap(): return lax.ppermute(array, axis, [(i, i ^ mask) for i in range(size)])  23.8 us
    dot_general x2, matrix products, dot_nt(): lax.dot_general(left, right, (((1,), (1,)), ((), ())), preferred_element_...  5.87 us
    unnamed x22, local copies, waits for them, and re-layouts  3.32 us
    select_n x4, other arithmetic, per_device(): texts = [jnp.where(upper, a, b) for a, b in zip(mine_all, theirs_all)]  3.09 us
  transfers between devices with their start and end apart: 20, of which 13 were waited for; matrix products, arithmetic and copies ran while one was open for 6% of the time, Pallas kernels for 20%

profile of v1, /device:TPU:0, one launch (start us, length us, event | category | flops | bytes accessed | tf_op | source)
XLA Modules:
  0.0 145.1 jit_solution(17190818225916721626)
XLA Ops:
  0.6 3.0 %collective-permute-start.1 = (bf16[256,1152]{1,0:T(8,128)(2,1)}, bf16[256,1152]{1,0:T(8,128)(2,1)S(1)}, u32[]{:S(2)}, u32[]{:S(2)}) collective-permute-start(bf16[256,1152]{1,0:T(8,128)(2,1)} %t0.3), channel_id=1, source_target_pairs={{0,2},{1,3},{2,0},{3,1},{4,6},{5,7},{6,4},{7,5},{8,10},{9,11},{10,... | collective-permute-start | bytes 1769480 | tf_op jit(solution)/shard_map/ppermute | solution.py:229
  4.2 13.8 %collective-permute-done.1.t2 = bf16[256,1152]{1,0:T(8,128)(2,1)S(1)} collective-permute-done((bf16[256,1152]{1,0:T(8,128)(2,1)}, bf16[256,1152]{1,0:T(8,128)(2,1)S(1)}, u32[]{:S(2)}, u32[]{:S(2)}) %collective-permute-start.1) | collective-permute-done | bytes 589856 | tf_op jit(solution)/shard_map/ppermute | solution.py:229
  18.7 11.1 %collective-permute-done.4.i2 = bf16[256,1152]{1,0:T(8,128)(2,1)S(1)} collective-permute-done((bf16[256,1152]{1,0:T(8,128)(2,1)}, bf16[256,1152]{1,0:T(8,128)(2,1)S(1)}, u32[]{:S(2)}, u32[]{:S(2)}) %collective-permute-start.4) | collective-permute-done | bytes 589856 | tf_op jit(solution)/shard_map/ppermute | solution.py:229
  29.8 0.8 copy-done.5
  30.7 0.8 copy-done.6
  31.5 13.1 %shard_map.75 = (f32[512,1152]{1,0:T(8,128)}, bf16[512,1152]{1,0:T(8,128)(2,1)}, f32[512,1152]{1,0:T(8,128)}, bf16[512,1152]{1,0:T(8,128)(2,1)}, bf16[512,512]{1,0:T(8,128)(2,1)}) custom-call(bf16[256,1152]{1,0:T(8,128)(2,1)} %t0.3, bf16[256,1152]{1,0:T(8,128)(2,1)} %copy-done.5, bf16[256,1152]{1,0:T(8,128)(2,1)} %i0.3, bf16[256,1152]{1,0:T(8,128)(2,1)} %copy-done.6, ...), custom_call_target="tpu_custom_call" | custom-call | flops 3397386240 | bytes 7667712 | tf_op jit(solution)/shard_map/pallas_call | solution.py:217
  44.6 0.8 copy-done.7
  45.4 16.2 %shard_map.76 = (f32[512,1152]{1,0:T(8,128)}, bf16[512,1152]{1,0:T(8,128)(2,1)}, bf16[512,1152]{1,0:T(8,128)(2,1)}, f32[512,1152]{1,0:T(8,128)}, f32[512,1152]{1...) custom-call(s32[2]{0:T(128)} %pad_add_fusion.place, bf16[256,1152]{1,0:T(8,128)(2,1)} %t0.3, ...), custom_call_target="tpu_custom_call" | custom-call | flops 5435817984 | bytes 11436040 | tf_op jit(solution)/shard_map/pallas_call | solution.py:217
  61.7 0.8 copy-done.8
  62.5 24.0 %shard_map.77 = (bf16[72,1152]{1,0:T(8,128)(2,1)}, bf16[72,1152]{1,0:T(8,128)(2,1)}, bf16[72,1152]{1,0:T(8,128)(2,1)}, bf16[72,1152]{1,0:T(8,128)(2,1)}, bf16[72...) custom-call(s32[2]{0:T(128)} %pad_add_fusion.place, ...), custom_call_target="tpu_custom_call" | custom-call | flops 6115295232 | bytes 17694728 | tf_op jit(solution)/shard_map/pallas_call | solution.py:217
  86.4 1.8 %collective-permute-start.10 = (bf16[72,1152]{1,0:T(8,128)(2,1)}, bf16[72,1152]{1,0:T(8,128)(2,1)S(1)}, u32[]{:S(2)}, u32[]{:S(2)}) collective-permute-start(bf16[72,1152]{1,0:T(8,128)(2,1)} %get-tuple-element.46), channel_id=1, source_target_pairs={{0,8},{4,12},{8,0},{12,4},{16,24},{20,28},{24,16},{28,20},{1,9},{5... | collective-permute-start | bytes 497672 | tf_op jit(solution)/shard_map/ppermute | solution.py:229
  88.3 1.4 collective-permute-start.11
  89.9 1.8 %collective-permute-start.7 = (bf16[72,1152]{1,0:T(8,128)(2,1)}, bf16[72,1152]{1,0:T(8,128)(2,1)S(1)}, u32[]{:S(2)}, u32[]{:S(2)}) collective-permute-start(bf16[72,1152]{1,0:T(8,128)(2,1)} %get-tuple-element.42), channel_id=1, source_target_pairs={{0,8},{4,12},{8,0},{12,4},{16,24},{20,28},{24,16},{28,20},{1,9},{5... | collective-permute-start | bytes 497672 | tf_op jit(solution)/shard_map/ppermute | solution.py:229
  91.8 1.4 collective-permute-start.8
  93.7 1.8 %collective-permute-start.9 = (bf16[72,1152]{1,0:T(8,128)(2,1)}, bf16[72,1152]{1,0:T(8,128)(2,1)S(1)}, u32[]{:S(2)}, u32[]{:S(2)}) collective-permute-start(bf16[72,1152]{1,0:T(8,128)(2,1)} %get-tuple-element.45), channel_id=1, source_target_pairs={{0,4},{4,0},{8,12},{12,8},{16,20},{20,16},{24,28},{28,24},{1,5},{5... | collective-permute-start | bytes 497672 | tf_op jit(solution)/shard_map/ppermute | solution.py:229
  95.5 3.0 %collective-permute-done.11 = bf16[72,1152]{1,0:T(8,128)(2,1)S(1)} collective-permute-done((bf16[72,1152]{1,0:T(8,128)(2,1)}, bf16[72,1152]{1,0:T(8,128)(2,1)S(1)}, u32[]{:S(2)}, u32[]{:S(2)}) %collective-permute-start.11) | collective-permute-done | bytes 165920 | tf_op jit(solution)/shard_map/ppermute | solution.py:229
  98.5 2.1 %collective-permute-done.6 = bf16[72,1152]{1,0:T(8,128)(2,1)S(1)} collective-permute-done((bf16[72,1152]{1,0:T(8,128)(2,1)}, bf16[72,1152]{1,0:T(8,128)(2,1)S(1)}, u32[]{:S(2)}, u32[]{:S(2)}) %collective-permute-start.6) | collective-permute-done | bytes 165920 | tf_op jit(solution)/shard_map/ppermute | solution.py:229
  100.8 4.4 %collective-permute-done.8 = bf16[72,1152]{1,0:T(8,128)(2,1)S(1)} collective-permute-done((bf16[72,1152]{1,0:T(8,128)(2,1)}, bf16[72,1152]{1,0:T(8,128)(2,1)S(1)}, u32[]{:S(2)}, u32[]{:S(2)}) %collective-permute-start.8) | collective-permute-done | bytes 165920 | tf_op jit(solution)/shard_map/ppermute | solution.py:229
  105.3 1.3 collective-permute-done.9
  106.6 1.2 select_convert_fusion
  107.8 2.7 %collective-permute-start.12 = (bf16[72,1152]{1,0:T(8,128)(2,1)S(1)}, bf16[72,1152]{1,0:T(8,128)(2,1)S(1)}, u32[]{:S(2)}, u32[]{:S(2)}) collective-permute-start(bf16[72,1152]{1,0:T(8,128)(2,1)S(1)} %select_convert_fusion), channel_id=1, source_target_pairs={{0,16},{4,20},{8,24},{12,28},{16,0},{20,4},{24,8},{28,12},{1,17},{... | collective-permute-start | bytes 497672 | tf_op jit(solution)/shard_map/ppermute | solution.py:229
  110.5 3.8 %fusion = f32[256,1152]{1,0:T(8,128)} fusion(bf16[1152,1152]{1,0:T(8,128)(2,1)} %image_head.3, bf16[512,1152]{1,0:T(8,128)(2,1)S(1)} %copy-done.9), kind=kOutput, calls=%fused_computation | convolution fusion | flops 679477248 | bytes 4423680 | tf_op jit(solution)/shard_map/dot_general | solution.py:47
  114.3 3.2 %collective-permute-done.12 = bf16[72,1152]{1,0:T(8,128)(2,1)S(1)} collective-permute-done((bf16[72,1152]{1,0:T(8,128)(2,1)S(1)}, bf16[72,1152]{1,0:T(8,128)(2,1)S(1)}, u32[]{:S(2)}, u32[]{:S(2)}) %collective-permute-start.12) | collective-permute-done | bytes 165920 | tf_op jit(solution)/shard_map/ppermute | solution.py:229
  117.9 2.1 %fusion.2 = f32[256,1152]{1,0:T(8,128)} fusion(bf16[256,1152]{1,0:T(8,128)(2,1)S(1)} %copy-done.10, bf16[1152,1152]{1,0:T(8,128)(2,1)S(1)} %copy-done.2), kind=kOutput, calls=%fused_computation.15 | convolution fusion | flops 679477248 | bytes 4423680 | tf_op jit(solution)/shard_map/dot_general | solution.py:47
  119.9 4.0 %collective-permute-start.19 = (bf16[72,1152]{1,0:T(8,128)(2,1)S(1)}, bf16[72,1152]{1,0:T(8,128)(2,1)S(1)}, u32[]{:S(2)}, u32[]{:S(2)}) collective-permute-start(bf16[72,1152]{1,0:T(8,128)(2,1)S(1)} %add_convert_fusion), channel_id=1, source_target_pairs={{0,12},{4,8},{8,4},{12,0},{16,28},{20,24},{24,20},{28,16},{1,13},{... | collective-permute-start | bytes 497672 | tf_op jit(solution)/shard_map/ppermute | solution.py:229
  124.0 1.5 %collective-permute-start.15 = (bf16[72,1152]{1,0:T(8,128)(2,1)S(1)}, bf16[72,1152]{1,0:T(8,128)(2,1)S(1)}, u32[]{:S(2)}, u32[]{:S(2)}) collective-permute-start(bf16[72,1152]{1,0:T(8,128)(2,1)S(1)} %add_convert_fusion), channel_id=1, source_target_pairs={{0,4},{4,0},{8,12},{12,8},{16,20},{20,16},{24,28},{28,24},{1,5},{5... | collective-permute-start | bytes 497672 | tf_op jit(solution)/shard_map/ppermute | solution.py:229
  125.4 2.1 %collective-permute-done.13 = bf16[72,1152]{1,0:T(8,128)(2,1)S(1)} collective-permute-done((bf16[72,1152]{1,0:T(8,128)(2,1)S(1)}, bf16[72,1152]{1,0:T(8,128)(2,1)S(1)}, u32[]{:S(2)}, u32[]{:S(2)}) %collective-permute-start.13) | collective-permute-done | bytes 165920 | tf_op jit(solution)/shard_map/ppermute | solution.py:229
  127.6 2.0 %collective-permute-start.16 = (bf16[72,1152]{1,0:T(8,128)(2,1)S(1)}, bf16[72,1152]{1,0:T(8,128)(2,1)S(1)}, u32[]{:S(2)}, u32[]{:S(2)}) collective-permute-start(bf16[72,1152]{1,0:T(8,128)(2,1)S(1)} %collective-permute-done.13), channel_id=1, source_target_pairs={{0,8},{4,12},{8,0},{12,4},{16,24},{20,28},{24,16},{28,20},{1,9},{5... | collective-permute-start | bytes 497672 | tf_op jit(solution)/shard_map/ppermute | solution.py:229
  130.6 1.5 %collective-permute-start.14 = (bf16[72,1152]{1,0:T(8,128)(2,1)S(1)}, bf16[72,1152]{1,0:T(8,128)(2,1)S(1)}, u32[]{:S(2)}, u32[]{:S(2)}) collective-permute-start(bf16[72,1152]{1,0:T(8,128)(2,1)S(1)} %collective-permute-done.13), channel_id=1, source_target_pairs={{0,4},{4,0},{8,12},{12,8},{16,20},{20,16},{24,28},{28,24},{1,5},{5... | collective-permute-start | bytes 497672 | tf_op jit(solution)/shard_map/ppermute | solution.py:229
  132.1 5.7 %collective-permute-done.18 = bf16[72,1152]{1,0:T(8,128)(2,1)S(1)} collective-permute-done((bf16[72,1152]{1,0:T(8,128)(2,1)S(1)}, bf16[72,1152]{1,0:T(8,128)(2,1)S(1)}, u32[]{:S(2)}, u32[]{:S(2)}) %collective-permute-start.18) | collective-permute-done | bytes 165920 | tf_op jit(solution)/shard_map/ppermute | solution.py:229
  138.5 2.0 %collective-permute-done.16 = bf16[72,1152]{1,0:T(8,128)(2,1)S(1)} collective-permute-done((bf16[72,1152]{1,0:T(8,128)(2,1)S(1)}, bf16[72,1152]{1,0:T(8,128)(2,1)S(1)}, u32[]{:S(2)}, u32[]{:S(2)}) %collective-permute-start.16) | collective-permute-done | bytes 165920 | tf_op jit(solution)/shard_map/ppermute | solution.py:229
  142.0 3.1 %shard_map.78 = (f32[288,1152]{1,0:T(8,128)}, f32[288,1152]{1,0:T(8,128)}) custom-call(s32[2]{0:T(128)} %pad_add_fusion.place, bf16[72,1152]{1,0:T(8,128)(2,1)} %get-tuple-element.57.h0, bf16[72,1152]{1,0:T(8,128)(2,1)} %get-tuple-element.55.h1, bf16[72,1152]{1,0:T(8,128)(2,1)} %get-tuple-element.53.h2, bf16[72,1152]{1,0:T(8,128)(2,1)} %get-tuple-element.51.h3, ...), custom_call_target="tpu_custom_call" | custom-call | flops 331776 | bytes 1327112 | tf_op jit(solution)/shard_map/pallas_call | solution.py:217
  (43 shorter events, 6.1 us)
Async XLA Ops:
  0.6 17.4 %collective-permute-start.1 = (bf16[256,1152]{1,0:T(8,128)(2,1)}, bf16[256,1152]{1,0:T(8,128)(2,1)S(1)}, u32[]{:S(2)}, u32[]{:S(2)}) collective-permute-start(bf16[256,1152]{1,0:T(8,128)(2,1)} %t0.3), channel_id=1, source_target_pairs={{0,2},{1,3},{2,0},{3,1},{4,6},{5,7},{6,4},{7,5},{8,10},{9,11},{10,... | collective-permute-start | bytes 1769480 | tf_op jit(solution)/shard_map/ppermute | solution.py:229
  3.6 26.2 %collective-permute-start.4 = (bf16[256,1152]{1,0:T(8,128)(2,1)}, bf16[256,1152]{1,0:T(8,128)(2,1)S(1)}, u32[]{:S(2)}, u32[]{:S(2)}) collective-permute-start(bf16[256,1152]{1,0:T(8,128)(2,1)} %i0.3), channel_id=1, source_target_pairs={{0,2},{1,3},{2,0},{3,1},{4,6},{5,7},{6,4},{7,5},{8,10},{9,11},{10,... | collective-permute-start | bytes 1769480 | tf_op jit(solution)/shard_map/ppermute | solution.py:229
  3.7 26.1 %collective-permute-start = (bf16[256,1152]{1,0:T(8,128)(2,1)}, bf16[256,1152]{1,0:T(8,128)(2,1)S(1)}, u32[]{:S(2)}, u32[]{:S(2)}) collective-permute-start(bf16[256,1152]{1,0:T(8,128)(2,1)} %t0.3), channel_id=1, source_target_pairs={{0,1},{1,0},{2,3},{3,2},{4,5},{5,4},{6,7},{7,6},{8,9},{9,8},{10,11... | collective-permute-start | bytes 1769480 | tf_op jit(solution)/shard_map/ppermute | solution.py:229
  3.7 26.1 %collective-permute-start.3 = (bf16[256,1152]{1,0:T(8,128)(2,1)}, bf16[256,1152]{1,0:T(8,128)(2,1)S(1)}, u32[]{:S(2)}, u32[]{:S(2)}) collective-permute-start(bf16[256,1152]{1,0:T(8,128)(2,1)} %i0.3), channel_id=1, source_target_pairs={{0,1},{1,0},{2,3},{3,2},{4,5},{5,4},{6,7},{7,6},{8,9},{9,8},{10,11... | collective-permute-start | bytes 1769480 | tf_op jit(solution)/shard_map/ppermute | solution.py:229
  18.0 26.6 %copy-start.4 = (bf16[256,1152]{1,0:T(8,128)(2,1)}, bf16[256,1152]{1,0:T(8,128)(2,1)S(1)}, u32[]{:S(2)}) copy-start(bf16[256,1152]{1,0:T(8,128)(2,1)S(1)} %collective-permute-done.1.t2) | copy-start | bytes 1769476
  18.0 26.6 %collective-permute-start.2 = (bf16[256,1152]{1,0:T(8,128)(2,1)S(1)}, bf16[256,1152]{1,0:T(8,128)(2,1)S(1)}, u32[]{:S(2)}, u32[]{:S(2)}) collective-permute-start(bf16[256,1152]{1,0:T(8,128)(2,1)S(1)} %collective-permute-done.1.t2), channel_id=1, source_target_pairs={{0,1},{1,0},{2,3},{3,2},{4,5},{5,4},{6,7},{7,6},{8,9},{9,8},{10,11... | collective-permute-start | bytes 1769480 | tf_op jit(solution)/shard_map/ppermute | solution.py:229
  29.8 14.8 %copy-start.3 = (bf16[256,1152]{1,0:T(8,128)(2,1)}, bf16[256,1152]{1,0:T(8,128)(2,1)S(1)}, u32[]{:S(2)}) copy-start(bf16[256,1152]{1,0:T(8,128)(2,1)S(1)} %collective-permute-done.4.i2) | copy-start | bytes 1769476
  29.8 31.8 %collective-permute-start.5 = (bf16[256,1152]{1,0:T(8,128)(2,1)S(1)}, bf16[256,1152]{1,0:T(8,128)(2,1)S(1)}, u32[]{:S(2)}, u32[]{:S(2)}) collective-permute-start(bf16[256,1152]{1,0:T(8,128)(2,1)S(1)} %collective-permute-done.4.i2), channel_id=1, source_target_pairs={{0,1},{1,0},{2,3},{3,2},{4,5},{5,4},{6,7},{7,6},{8,9},{9,8},{10,11... | collective-permute-start | bytes 1769480 | tf_op jit(solution)/shard_map/ppermute | solution.py:229
  29.8 0.8 copy-start.5
  30.7 0.8 copy-start.6
  44.6 0.8 copy-start.7
  61.6 0.8 copy-start.8
  62.5 48.0 %copy-start.9 = (bf16[512,1152]{1,0:T(8,128)(2,1)S(1)}, bf16[512,1152]{1,0:T(8,128)(2,1)}, u32[]{:S(2)}) copy-start(bf16[512,1152]{1,0:T(8,128)(2,1)} %get-tuple-element.31.dp_a) | copy-start | bytes 3538948
  86.4 7.2 %collective-permute-start.10 = (bf16[72,1152]{1,0:T(8,128)(2,1)}, bf16[72,1152]{1,0:T(8,128)(2,1)S(1)}, u32[]{:S(2)}, u32[]{:S(2)}) collective-permute-start(bf16[72,1152]{1,0:T(8,128)(2,1)} %get-tuple-element.46), channel_id=1, source_target_pairs={{0,8},{4,12},{8,0},{12,4},{16,24},{20,28},{24,16},{28,20},{1,9},{5... | collective-permute-start | bytes 497672 | tf_op jit(solution)/shard_map/ppermute | solution.py:229
  88.3 10.2 %collective-permute-start.11 = (bf16[72,1152]{1,0:T(8,128)(2,1)}, bf16[72,1152]{1,0:T(8,128)(2,1)S(1)}, u32[]{:S(2)}, u32[]{:S(2)}) collective-permute-start(bf16[72,1152]{1,0:T(8,128)(2,1)} %get-tuple-element.47), channel_id=1, source_target_pairs={{0,12},{4,8},{8,4},{12,0},{16,28},{20,24},{24,20},{28,16},{1,13},{... | collective-permute-start | bytes 497672 | tf_op jit(solution)/shard_map/ppermute | solution.py:229
  89.7 10.9 %collective-permute-start.6 = (bf16[72,1152]{1,0:T(8,128)(2,1)}, bf16[72,1152]{1,0:T(8,128)(2,1)S(1)}, u32[]{:S(2)}, u32[]{:S(2)}) collective-permute-start(bf16[72,1152]{1,0:T(8,128)(2,1)} %get-tuple-element.41), channel_id=1, source_target_pairs={{0,4},{4,0},{8,12},{12,8},{16,20},{20,16},{24,28},{28,24},{1,5},{5... | collective-permute-start | bytes 497672 | tf_op jit(solution)/shard_map/ppermute | solution.py:229
  89.9 10.9 %collective-permute-start.7 = (bf16[72,1152]{1,0:T(8,128)(2,1)}, bf16[72,1152]{1,0:T(8,128)(2,1)S(1)}, u32[]{:S(2)}, u32[]{:S(2)}) collective-permute-start(bf16[72,1152]{1,0:T(8,128)(2,1)} %get-tuple-element.42), channel_id=1, source_target_pairs={{0,8},{4,12},{8,0},{12,4},{16,24},{20,28},{24,16},{28,20},{1,9},{5... | collective-permute-start | bytes 497672 | tf_op jit(solution)/shard_map/ppermute | solution.py:229
  91.8 13.5 %collective-permute-start.8 = (bf16[72,1152]{1,0:T(8,128)(2,1)}, bf16[72,1152]{1,0:T(8,128)(2,1)S(1)}, u32[]{:S(2)}, u32[]{:S(2)}) collective-permute-start(bf16[72,1152]{1,0:T(8,128)(2,1)} %get-tuple-element.43), channel_id=1, source_target_pairs={{0,12},{4,8},{8,4},{12,0},{16,28},{20,24},{24,20},{28,16},{1,13},{... | collective-permute-start | bytes 497672 | tf_op jit(solution)/shard_map/ppermute | solution.py:229
  93.7 12.9 %collective-permute-start.9 = (bf16[72,1152]{1,0:T(8,128)(2,1)}, bf16[72,1152]{1,0:T(8,128)(2,1)S(1)}, u32[]{:S(2)}, u32[]{:S(2)}) collective-permute-start(bf16[72,1152]{1,0:T(8,128)(2,1)} %get-tuple-element.45), channel_id=1, source_target_pairs={{0,4},{4,0},{8,12},{12,8},{16,20},{20,16},{24,28},{28,24},{1,5},{5... | collective-permute-start | bytes 497672 | tf_op jit(solution)/shard_map/ppermute | solution.py:229
  107.8 9.7 %copy-start = (bf16[72,1152]{1,0:T(8,128)(2,1)S(1)}, bf16[72,1152]{1,0:T(8,128)(2,1)}, u32[]{:S(2)}) copy-start(bf16[72,1152]{1,0:T(8,128)(2,1)} %get-tuple-element.44) | copy-start | bytes 497668
  107.8 9.7 %copy-start.1 = (bf16[72,1152]{1,0:T(8,128)(2,1)S(1)}, bf16[72,1152]{1,0:T(8,128)(2,1)}, u32[]{:S(2)}) copy-start(bf16[72,1152]{1,0:T(8,128)(2,1)} %get-tuple-element.40) | copy-start | bytes 497668
  107.8 10.0 %copy-start.2 = (bf16[1152,1152]{1,0:T(8,128)(2,1)S(1)}, bf16[1152,1152]{1,0:T(8,128)(2,1)}, u32[]{:S(2)}) copy-start(bf16[1152,1152]{1,0:T(8,128)(2,1)} %text_head.3) | copy-start | bytes 7962628
  107.8 10.0 %copy-start.10 = (bf16[256,1152]{1,0:T(8,128)(2,1)S(1)}, bf16[256,1152]{1,0:T(8,128)(2,1)}, u32[]{:S(2)}) copy-start(bf16[256,1152]{1,0:T(8,128)(2,1)} %get-tuple-element.39) | copy-start | bytes 1769476
  107.8 9.7 %collective-permute-start.12 = (bf16[72,1152]{1,0:T(8,128)(2,1)S(1)}, bf16[72,1152]{1,0:T(8,128)(2,1)S(1)}, u32[]{:S(2)}, u32[]{:S(2)}) collective-permute-start(bf16[72,1152]{1,0:T(8,128)(2,1)S(1)} %select_convert_fusion), channel_id=1, source_target_pairs={{0,16},{4,20},{8,24},{12,28},{16,0},{20,4},{24,8},{28,12},{1,17},{... | collective-permute-start | bytes 497672 | tf_op jit(solution)/shard_map/ppermute | solution.py:229
  117.8 9.8 %collective-permute-start.13 = (bf16[72,1152]{1,0:T(8,128)(2,1)S(1)}, bf16[72,1152]{1,0:T(8,128)(2,1)S(1)}, u32[]{:S(2)}, u32[]{:S(2)}) collective-permute-start(bf16[72,1152]{1,0:T(8,128)(2,1)S(1)} %add_convert_fusion), channel_id=1, source_target_pairs={{0,16},{4,20},{8,24},{12,28},{16,0},{20,4},{24,8},{28,12},{1,17},{... | collective-permute-start | bytes 497672 | tf_op jit(solution)/shard_map/ppermute | solution.py:229
  119.9 10.7 %collective-permute-start.19 = (bf16[72,1152]{1,0:T(8,128)(2,1)S(1)}, bf16[72,1152]{1,0:T(8,128)(2,1)S(1)}, u32[]{:S(2)}, u32[]{:S(2)}) collective-permute-start(bf16[72,1152]{1,0:T(8,128)(2,1)S(1)} %add_convert_fusion), channel_id=1, source_target_pairs={{0,12},{4,8},{8,4},{12,0},{16,28},{20,24},{24,20},{28,16},{1,13},{... | collective-permute-start | bytes 497672 | tf_op jit(solution)/shard_map/ppermute | solution.py:229
  123.9 14.6 %collective-permute-start.17 = (bf16[72,1152]{1,0:T(8,128)(2,1)S(1)}, bf16[72,1152]{1,0:T(8,128)(2,1)S(1)}, u32[]{:S(2)}, u32[]{:S(2)}) collective-permute-start(bf16[72,1152]{1,0:T(8,128)(2,1)S(1)} %add_convert_fusion), channel_id=1, source_target_pairs={{0,8},{4,12},{8,0},{12,4},{16,24},{20,28},{24,16},{28,20},{1,9},{5... | collective-permute-start | bytes 497672 | tf_op jit(solution)/shard_map/ppermute | solution.py:229
  124.0 17.3 %collective-permute-start.15 = (bf16[72,1152]{1,0:T(8,128)(2,1)S(1)}, bf16[72,1152]{1,0:T(8,128)(2,1)S(1)}, u32[]{:S(2)}, u32[]{:S(2)}) collective-permute-start(bf16[72,1152]{1,0:T(8,128)(2,1)S(1)} %add_convert_fusion), channel_id=1, source_target_pairs={{0,4},{4,0},{8,12},{12,8},{16,20},{20,16},{24,28},{28,24},{1,5},{5... | collective-permute-start | bytes 497672 | tf_op jit(solution)/shard_map/ppermute | solution.py:229
  127.6 10.2 %collective-permute-start.18 = (bf16[72,1152]{1,0:T(8,128)(2,1)S(1)}, bf16[72,1152]{1,0:T(8,128)(2,1)S(1)}, u32[]{:S(2)}, u32[]{:S(2)}) collective-permute-start(bf16[72,1152]{1,0:T(8,128)(2,1)S(1)} %collective-permute-done.13), channel_id=1, source_target_pairs={{0,12},{4,8},{8,4},{12,0},{16,28},{20,24},{24,20},{28,16},{1,13},{... | collective-permute-start | bytes 497672 | tf_op jit(solution)/shard_map/ppermute | solution.py:229
  127.6 12.9 %collective-permute-start.16 = (bf16[72,1152]{1,0:T(8,128)(2,1)S(1)}, bf16[72,1152]{1,0:T(8,128)(2,1)S(1)}, u32[]{:S(2)}, u32[]{:S(2)}) collective-permute-start(bf16[72,1152]{1,0:T(8,128)(2,1)S(1)} %collective-permute-done.13), channel_id=1, source_target_pairs={{0,8},{4,12},{8,0},{12,4},{16,24},{20,28},{24,16},{28,20},{1,9},{5... | collective-permute-start | bytes 497672 | tf_op jit(solution)/shard_map/ppermute | solution.py:229
  130.6 10.7 %collective-permute-start.14 = (bf16[72,1152]{1,0:T(8,128)(2,1)S(1)}, bf16[72,1152]{1,0:T(8,128)(2,1)S(1)}, u32[]{:S(2)}, u32[]{:S(2)}) collective-permute-start(bf16[72,1152]{1,0:T(8,128)(2,1)S(1)} %collective-permute-done.13), channel_id=1, source_target_pairs={{0,4},{4,0},{8,12},{12,8},{16,20},{20,16},{24,28},{28,24},{1,5},{5... | collective-permute-start | bytes 497672 | tf_op jit(solution)/shard_map/ppermute | solution.py:229

commit v2 on v1

v2 whole, which is shorter than its diff:
```python
import functools

import jax
import jax.numpy as jnp
from jax import lax
from jax.experimental import pallas as pl
from jax.experimental.pallas import tpu as pltpu
from jax.sharding import PartitionSpec as P

SCORE_SCALE = 10.0
SCORE_BIAS = -2.5
EPSILON = 1e-06
QUAD = 4
STRIP = 16
F32 = jnp.float32
BF16 = jnp.bfloat16
VMEM_LIMIT = 24 * 1024 * 1024


def normalize(features, weight_matrix):
    projected = jnp.dot(features, weight_matrix, preferred_element_type=jnp.float32)
    factor = lax.rsqrt(jnp.sum(projected * projected, axis=-1, keepdims=True) + EPSILON)
    return (projected * factor, factor)


def pair_weights(image_vectors, text_vectors, image_offset):
    pair_scores = SCORE_SCALE * dot_nt(image_vectors, text_vectors) + SCORE_BIAS
    row_ids = image_offset + lax.broadcasted_iota(jnp.int32, pair_scores.shape, 0)
    col_ids = lax.broadcasted_iota(jnp.int32, pair_scores.shape, 1)
    match_targets = jnp.where(row_ids == col_ids, 1.0, -1.0).astype(jnp.float32)
    return (SCORE_SCALE * -match_targets * jax.nn.sigmoid(-match_targets * pair_scores)).astype(
        jnp.bfloat16
    )


def norm_back(unit, factor, gradient):
    return (factor * (gradient - unit * jnp.sum(unit * gradient, axis=-1, keepdims=True))).astype(
        jnp.bfloat16
    )


def dot_nn(left, right):
    return lax.dot_general(left, right, (((1,), (0,)), ((), ())), preferred_element_type=F32)


def dot_nt(left, right):
    return lax.dot_general(left, right, (((1,), (1,)), ((), ())), preferred_element_type=F32)


def dot_tn(left, right):
    return lax.dot_general(left, right, (((0,), (0,)), ((), ())), preferred_element_type=F32)


def plain_device(image_features, text_features, image_head, text_head):
    row_count = image_features.shape[0]
    own_start = lax.axis_index("loop") * row_count
    image_unit, image_factor = normalize(image_features, image_head)
    text_unit, text_factor = normalize(text_features, text_head)
    image_vectors = image_unit.astype(jnp.bfloat16)
    text_vectors = text_unit.astype(jnp.bfloat16)
    arrived = lax.all_gather(text_vectors, "loop", axis=0, tiled=True)
    weights = pair_weights(image_vectors, arrived, own_start)
    summed = jnp.dot(weights, arrived, preferred_element_type=jnp.float32)
    text_attraction = lax.psum_scatter(
        dot_tn(weights, image_vectors).astype(jnp.bfloat16), "loop", scatter_dimension=0, tiled=True
    ).astype(jnp.float32)
    image_back = norm_back(image_unit, image_factor, summed)
    text_back = norm_back(text_unit, text_factor, text_attraction)
    heads = []
    for features, back in ((image_features, image_back), (text_features, text_back)):
        term = dot_tn(features, back).astype(jnp.bfloat16)
        part = lax.psum_scatter(term, "loop", scatter_dimension=0, tiled=True)
        heads.append(lax.psum(part, "cuts").astype(jnp.float32))
    return (dot_nt(image_back, image_head), dot_nt(text_back, text_head), heads[0], heads[1])


def factor_of(p):
    return lax.rsqrt(jnp.sum(p * p, axis=-1, keepdims=True) + EPSILON)


def unit_rows(projected_ref, vectors_ref):
    for first in range(0, projected_ref.shape[0], STRIP):
        p = projected_ref[first : first + STRIP, :]
        vectors_ref[first : first + STRIP, :] = (p * factor_of(p)).astype(BF16)


def back_rows(projected_ref, gradient_ref, back_ref):
    for first in range(0, projected_ref.shape[0], STRIP):
        p = projected_ref[first : first + STRIP, :]
        g = gradient_ref[first : first + STRIP, :]
        factor = factor_of(p)
        along = factor * factor * factor * jnp.sum(p * g, axis=-1, keepdims=True)
        back_ref[first : first + STRIP, :] = (factor * g - along * p).astype(BF16)


def weights_of(dots, pairs_from=None):
    score = SCORE_SCALE * dots + SCORE_BIAS
    if pairs_from is None:
        return (SCORE_SCALE * jax.nn.sigmoid(score)).astype(BF16)
    row = pairs_from + lax.broadcasted_iota(jnp.int32, dots.shape, 0)
    same = row == lax.broadcasted_iota(jnp.int32, dots.shape, 1)
    value = jax.nn.sigmoid(jnp.where(same, -score, score))
    return (jnp.where(same, -SCORE_SCALE, SCORE_SCALE) * value).astype(BF16)


def weight_rows(dots_ref, weights_ref, pairs_from=None):
    for first in range(0, dots_ref.shape[0], STRIP):
        pairs = None if pairs_from is None else pairs_from + first
        weights_ref[first : first + STRIP, :] = weights_of(dots_ref[first : first + STRIP, :], pairs)


def picker(place_ref, rows, width):
    part = rows // QUAD
    pieces = []
    for k in range(QUAD):
        first = place_ref[0] * rows + (place_ref[1] ^ k) * part
        wanted = first + lax.broadcasted_iota(jnp.int32, (part, width), 0)
        column = lax.broadcasted_iota(jnp.int32, (part, width), 1)
        pieces.append(jnp.where(wanted == column, 1.0, 0.0))
    return jnp.concatenate(pieces, axis=0).astype(BF16)


def near_kernel(t0, t1, i0, i1, text_head, image_head, q_a, y_a, p_a, x_a, w_aa, dots):
    half = t0.shape[0]
    q_a[:half, :] = dot_nn(t0[...], text_head[...])
    q_a[half:, :] = dot_nn(t1[...], text_head[...])
    unit_rows(q_a, y_a)
    p_a[:half, :] = dot_nn(i0[...], image_head[...])
    p_a[half:, :] = dot_nn(i1[...], image_head[...])
    unit_rows(p_a, x_a)
    dots[...] = dot_nt(x_a[...], y_a[...])
    weight_rows(dots, w_aa, 0)


def text_kernel(
    place, t0, t1, t2, t3, t4, i0, i1, text_head, y_a, p_a, x_a, w_aa,
    q_b, y_b, dp_a, gy_a, gy_b, text_pick, image_pick, dots, gx, w_ab,
):
    half = t2.shape[0]
    q_b[:half, :] = dot_nn(t2[...], text_head[...])
    t3 = jnp.concatenate([t3[...], t4[...]], axis=0)
    q_b[half:, :] = dot_nn(t3, text_head[...])
    unit_rows(q_b, y_b)
    dots[...] = dot_nt(x_a[...], y_b[...])
    weight_rows(dots, w_ab)
    gx[...] = dot_nn(w_aa[...], y_a[...]) + dot_nn(w_ab[...], y_b[...])
    back_rows(p_a, gx, dp_a)
    gy_a[...] = dot_tn(w_aa[...], x_a[...])
    gy_b[...] = dot_tn(w_ab[...], x_a[...])
    pick = picker(place, text_pick.shape[0], t0.shape[1])
    for block, t in enumerate((t0, t1, t2, t3)):
        text_pick[:, block * half : (block + 1) * half] = dot_nt(pick, t[...]).astype(BF16)
    for block, i in enumerate((i0, i1)):
        image_pick[:, block * half : (block + 1) * half] = dot_nt(pick, i[...]).astype(BF16)


def image_block(place, i, image_head, y_a, y_b, x_b, w_ba, w_bb, pick, dp_b, p_b, gx, d_a, d_b, block):
    p_b[...] = dot_nn(i[...], image_head[...])
    unit_rows(p_b, x_b)
    d_a[...] = dot_nt(x_b[...], y_a[...])
    d_b[...] = dot_nt(x_b[...], y_b[...])
    weight_rows(d_a, w_ba)
    weight_rows(d_b, w_bb, block * i.shape[0])
    gx[...] = dot_nn(w_ba[...], y_a[...]) + dot_nn(w_bb[...], y_b[...])
    back_rows(p_b, gx, dp_b)
    pick[...] = dot_nt(picker(place, pick.shape[0], i.shape[1]), i[...]).astype(BF16)


def third_kernel(place, i2, image_head, y_a, y_b, x_b, w_ba, w_bb, pick, dp_b, p_b, gx, d_a, d_b):
    image_block(place, i2, image_head, y_a, y_b, x_b, w_ba, w_bb, pick, dp_b, p_b, gx, d_a, d_b, 0)


def split_head(head, outs):
    part = head.shape[0] // QUAD
    for k, out in enumerate(outs):
        out[...] = head[k * part : (k + 1) * part, :].astype(BF16)


def fourth_kernel(
    place, i3, image_head, y_a, y_b, dp_a, dp_2, image_pick, pick_2,
    x_b, w_ba, w_bb, h0, h1, h2, h3, pick, dp_b, p_b, gx, d_a, d_b,
):
    image_block(place, i3, image_head, y_a, y_b, x_b, w_ba, w_bb, pick, dp_b, p_b, gx, d_a, d_b, 1)
    head = dot_nn(image_pick[...], dp_a[...]) + dot_nn(pick_2[...], dp_2[...])
    split_head(head + dot_nn(pick[...], dp_b[...]), (h0, h1, h2, h3))


def fifth_kernel(
    x_2, w_2a, w_2b, x_3, w_3a, w_3b, q_a, q_b, gy_a_in, gy_b_in, text_pick,
    k0, k1, k2, k3, dq_own, gy_a, gy_b, dq_a, dq_b,
):
    half = x_2.shape[0]
    gy_a[...] = gy_a_in[...] + dot_tn(w_2a[...], x_2[...]) + dot_tn(w_3a[...], x_3[...])
    gy_b[...] = gy_b_in[...] + dot_tn(w_2b[...], x_2[...]) + dot_tn(w_3b[...], x_3[...])
    back_rows(q_a, gy_a, dq_a)
    back_rows(q_b, gy_b, dq_b)
    dq_own[...] = dq_a[:half, :]
    head = dot_nn(text_pick[:, : 2 * half], dq_a[...]) + dot_nn(text_pick[:, 2 * half :], dq_b[...])
    split_head(head, (k0, k1, k2, k3))


def place_kernel(place, *refs):
    mine, theirs, outs = refs[:QUAD], refs[QUAD : 2 * QUAD], refs[2 * QUAD :]
    part = mine[0].shape[0]
    for head, out in enumerate(outs):
        for wanted, pieces in ((head, mine), (1 - head, theirs)):

            @pl.when(place[2] == wanted)
            def _(out=out, pieces=pieces):
                for k, piece in enumerate(pieces):
                    first = pl.multiple_of((place[1] ^ k) * part, part)
                    out[pl.ds(first, part), :] = piece[...].astype(F32)


def call(kernel, outs, scratch, args, macs, place=None, keep=True):
    args = [pltpu.with_memory_space_constraint(a, pltpu.VMEM) for a in args]
    specs = [pl.BlockSpec(memory_space=pltpu.VMEM)] * len(args)
    if place is not None:
        args, specs = [place, *args], [pl.BlockSpec(memory_space=pltpu.SMEM), *specs]
    shape = pltpu.VMEM if keep else jax.ShapeDtypeStruct
    return pl.pallas_call(
        kernel,
        out_shape=[shape(s, t) for s, t in outs],
        in_specs=specs,
        out_specs=[pl.BlockSpec(memory_space=pltpu.VMEM)] * len(outs),
        scratch_shapes=[pltpu.VMEM(s, t) for s, t in scratch],
        compiler_params=pltpu.CompilerParams(vmem_limit_bytes=VMEM_LIMIT),
        cost_estimate=pl.CostEstimate(flops=2 * (macs > 0), bytes_accessed=0, transcendentals=0),
    )(*args)


def swap(array, axis, size, mask):
    return lax.ppermute(array, axis, [(i, i ^ mask) for i in range(size)])


def after(value, other):
    return lax.optimization_barrier((value, other))[0]


def per_device(n_loop, n_cuts, image_features, text_features, image_head, text_head):
    half, width = image_features.shape
    near = 2 * half
    rows_out = width // n_loop
    part = rows_out // QUAD
    cut = lax.axis_index("cuts")
    upper = cut // QUAD
    place = jnp.stack([lax.axis_index("loop"), cut & (QUAD - 1), upper]).astype(jnp.int32)
    loop = functools.partial(swap, axis="loop", size=n_loop)
    cuts = functools.partial(swap, axis="cuts", size=n_cuts)
    macs = half * width * width

    t0, i0 = text_features, image_features
    t2 = loop(t0, mask=2)
    i2 = loop(i0, mask=2)
    t1 = loop(t0, mask=1)
    i1 = loop(i0, mask=1)
    wide, wide_b = ((near, width), F32), ((near, width), BF16)
    tall, tall_b = ((half, width), F32), ((half, width), BF16)
    square, block_w = ((near, near), BF16), ((half, near), BF16)
    pieces_out = [((part, width), BF16)] * QUAD
    q_a, y_a, p_a, x_a, w_aa = call(
        near_kernel,
        [wide, wide_b, wide, wide_b, square],
        [((near, near), F32)],
        (t0, t1, i0, i1, text_head, image_head),
        5 * macs,
    )
    t2 = after(t2, w_aa)
    t3 = [loop(t2[: half // 2], mask=1), loop(t2[half // 2 :], mask=1)]
    q_b, y_b, dp_a, gy_a, gy_b, text_pick, image_pick = call(
        text_kernel,
        [wide, wide_b, wide_b, wide, wide, ((rows_out, 2 * near), BF16), ((rows_out, near), BF16)],
        [((near, near), F32), wide, square],
        (t0, t1, t2, *t3, i0, i1, text_head, y_a, p_a, x_a, w_aa),
        8 * macs,
        place,
    )
    i2 = after(i2, dp_a)
    i3 = loop(i2, mask=1)
    block_scratch = [tall, tall, ((half, near), F32), ((half, near), F32)]
    x_2, w_2a, w_2b, pick_2, dp_2 = call(
        third_kernel,
        [tall_b, block_w, block_w, ((rows_out, half), BF16), tall_b],
        block_scratch,
        (i2, image_head, y_a, y_b),
        2 * macs,
        place,
    )
    x_3, w_3a, w_3b, *image_parts = call(
        fourth_kernel,
        [tall_b, block_w, block_w] + pieces_out,
        [((rows_out, half), BF16), tall_b] + block_scratch,
        (i3, image_head, y_a, y_b, dp_a, dp_2, image_pick, pick_2),
        3 * macs,
        place,
    )
    arrived = [cuts(image_parts[k], mask=k) for k in range(1, QUAD)]
    *text_parts, dq_own = call(
        fifth_kernel,
        pieces_out + [tall_b],
        [wide, wide, wide_b, wide_b],
        (x_2, w_2a, w_2b, x_3, w_3a, w_3b, q_a, q_b, gy_a, gy_b, text_pick),
        4 * macs,
    )
    image_sum = sum((a.astype(F32) for a in arrived), image_parts[0].astype(F32))
    arrived = [cuts(text_parts[k], mask=k) for k in range(1, QUAD)]
    image_grad = dot_nt(dp_a[:half], image_head)
    text_grad = dot_nt(dq_own, text_head)
    text_sum = sum((a.astype(F32) for a in arrived), text_parts[0].astype(F32))
    kept = jnp.where(upper == 1, text_sum, image_sum)
    sent = jnp.where(upper == 1, image_sum, text_sum).astype(BF16)
    mine = (kept + cuts(sent, mask=QUAD).astype(F32)).astype(BF16)
    theirs = cuts(mine, mask=QUAD)
    mine_all = [mine] + [cuts(mine, mask=k) for k in range(1, QUAD)]
    theirs_all = [theirs] + [cuts(theirs, mask=k) for k in range(1, QUAD)]
    image_out, text_out = call(
        place_kernel,
        [((rows_out, width), F32)] * 2,
        [],
        (*mine_all, *theirs_all),
        rows_out * width,
        place,
        keep=False,
    )
    return (image_grad, text_grad, image_out, text_out)


def solution(mesh):
    n_loop, n_cuts = mesh.shape["loop"], mesh.shape["cuts"]
    if n_loop == 4 and n_cuts == 2 * QUAD:
        body = functools.partial(per_device, n_loop, n_cuts)
    else:
        body = plain_device
    placed = (P(("cuts", "loop"), None), P(("cuts", "loop"), None), P(), P())
    return jax.shard_map(
        body,
        mesh=mesh,
        in_specs=placed,
        out_specs=(
            P(("cuts", "loop"), None),
            P(("cuts", "loop"), None),
            P("loop", None),
            P("loop", None),
        ),
        check_vma=False,
    )
```

time: 145 us -> 117 us (0.81)
  Pallas kernels: 56.3 us -> 28.3 us
  waiting for transfers between devices: 49.8 us -> 26.8 us
  local copies, waits for them, and re-layouts: 3.32 us -> 26.1 us
  starting transfers between devices: 23.8 us -> 26.9 us
  other arithmetic: 5.22 us -> 3.06 us
  matrix products: 5.87 us -> 4.13 us
    pallas_call x4 -> x6, Pallas kernels: 56.3 us -> 28.3 us  [call(): pl.pallas_call(kernel, out_shape=[shape(s, t) for s, t in outs], in_specs...]
    ppermute x20 -> x21, waiting for transfers between devices: 49.8 us -> 26.8 us  [swap(): return lax.ppermute(array, axis, [(i, i ^ mask) for i in range(size)])]
    unnamed x22 -> x62, local copies, waits for them, and re-layouts: 3.32 us -> 26 us
    ppermute x20 -> x21, starting transfers between devices: 23.8 us -> 26.9 us  [swap(): return lax.ppermute(array, axis, [(i, i ^ mask) for i in range(size)])]
    select_n x4 -> x0, other arithmetic: 3.09 us -> none  [per_device(): texts = [jnp.where(upper, a, b) for a, b in zip(mine_all, theirs_all)]]
    dot_general x2, matrix products: 5.87 us -> 4.13 us  [dot_nt(): lax.dot_general(left, right, (((1,), (1,)), ((), ())), preferred_element_...]
  transfers between devices with their start and end apart: 20 -> 21, of which waited for: 13 -> 12; matrix products, arithmetic and copies ran while one was open for 6% -> 4% of each run, Pallas kernels for 20% -> 14%
where the time goes in v2:
time: 117 us; the launch traced here: 116 us
  Pallas kernels  28.3 us (24%)
  starting transfers between devices  26.9 us (23%)
  waiting for transfers between devices  26.8 us (23%)
  local copies, waits for them, and re-layouts  26.1 us (22%)
  matrix products  4.13 us (4%)
  other arithmetic  3.06 us (3%)
    pallas_call x6, Pallas kernels, call(): pl.pallas_call(kernel, out_shape=[shape(s, t) for s, t in outs], in_specs...  28.3 us
    ppermute x21, starting transfers between devices, swap(): return lax.ppermute(array, axis, [(i, i ^ mask) for i in range(size)])  26.9 us
    ppermute x21, waiting for transfers between devices, swap(): return lax.ppermute(array, axis, [(i, i ^ mask) for i in range(size)])  26.8 us
    unnamed x62, local copies, waits for them, and re-layouts  26 us
    dot_general x2, matrix products, dot_nt(): lax.dot_general(left, right, (((1,), (1,)), ((), ())), preferred_element_...  4.13 us
  transfers between devices with their start and end apart: 21, of which 12 were waited for; matrix products, arithmetic and copies ran while one was open for 4% of the time, Pallas kernels for 14%

profile of v2, /device:TPU:0, one launch (start us, length us, event | category | flops | bytes accessed | tf_op | source)
XLA Modules:
  0.0 116.1 jit_solution(11896064623277709896)
XLA Ops:
  1.2 2.9 %collective-permute-start.1 = (bf16[256,1152]{1,0:T(8,128)(2,1)}, bf16[256,1152]{1,0:T(8,128)(2,1)S(1)}, u32[]{:S(2)}, u32[]{:S(2)}) collective-permute-start(bf16[256,1152]{1,0:T(8,128)(2,1)} %t0.3), channel_id=1, source_target_pairs={{0,2},{1,3},{2,0},{3,1},{4,6},{5,7},{6,4},{7,5},{8,10},{9,11},{10,... | collective-permute-start | bytes 1769480 | tf_op jit(solution)/shard_map/ppermute | solution.py:233
  4.2 2.0 %copy-done = bf16[1152,1152]{1,0:T(8,128)(2,1)S(1)} copy-done((bf16[1152,1152]{1,0:T(8,128)(2,1)S(1)}, bf16[1152,1152]{1,0:T(8,128)(2,1)}, u32[]{:S(2)}) %copy-start) | copy-done | bytes 2654232
  6.2 1.7 %copy-done.2 = bf16[1152,1152]{1,0:T(8,128)(2,1)S(1)} copy-done((bf16[1152,1152]{1,0:T(8,128)(2,1)S(1)}, bf16[1152,1152]{1,0:T(8,128)(2,1)}, u32[]{:S(2)}) %copy-start.2) | copy-done | bytes 2654232
  10.0 4.6 %shard_map.75 = (f32[512,1152]{1,0:T(8,128)S(1)}, bf16[512,1152]{1,0:T(8,128)(2,1)S(1)}, f32[512,1152]{1,0:T(8,128)S(1)}, bf16[512,1152]{1,0:T(8,128)(2,1)S(1)}, bf16[512,512]{1,0:T(8,128)(2,1)S(1)}) custom-call(bf16[256,1152]{1,0:T(8,128)(2,1)S(1)} %copy-done.12, bf16[256,1152]{1,0:T(8,128)(2,1)S(1)} %collective-permute-done.t1, ...), custom_call_target="tpu_custom_call" | custom-call | flops 2 | tf_op jit(solution)/shard_map/pallas_call | solution.py:221
  17.1 1.5 %copy-done.10 = f32[512,1152]{1,0:T(8,128)} copy-done((f32[512,1152]{1,0:T(8,128)}, f32[512,1152]{1,0:T(8,128)S(1)}, u32[]{:S(2)}) %copy-start.10) | copy-done | bytes 2359320
  23.3 1.7 %copy-done.3 = bf16[1152,1152]{1,0:T(8,128)(2,1)S(1)} copy-done((bf16[1152,1152]{1,0:T(8,128)(2,1)S(1)}, bf16[1152,1152]{1,0:T(8,128)(2,1)}, u32[]{:S(2)}) %copy-start.3) | copy-done | bytes 2654232
  26.3 1.7 %copy-done.11 = f32[512,1152]{1,0:T(8,128)S(1)} copy-done((f32[512,1152]{1,0:T(8,128)S(1)}, f32[512,1152]{1,0:T(8,128)}, u32[]{:S(2)}) %copy-start.11) | copy-done | bytes 2359320
  35.5 7.6 %shard_map.76 = (f32[512,1152]{1,0:T(8,128)S(1)}, bf16[512,1152]{1,0:T(8,128)(2,1)S(1)}, bf16[512,1152]{1,0:T(8,128)(2,1)S(1)}, f32[512,1152]{1,0:T(8,128)S(1)},...) custom-call(s32[3]{0:T(128)S(1)} %pad_add_fusion.place, ...), custom_call_target="tpu_custom_call" | custom-call | flops 2 | tf_op jit(solution)/shard_map/pallas_call | solution.py:221
  43.3 4.5 %shard_map.77 = (bf16[256,1152]{1,0:T(8,128)(2,1)S(1)}, bf16[256,512]{1,0:T(8,128)(2,1)S(1)}, bf16[256,512]{1,0:T(8,128)(2,1)S(1)}, bf16[288,256]{1,0:T(8,128)(2,1)S(1)}, bf16[256,1152]{1,0:T(8,128)(2,1)S(1)}) custom-call(s32[3]{0:T(128)S(1)} %pad_add_fusion.place, bf16[256,1152]{1,0:T(8,128)(2,1)} %collective-permute-done.5.i2, ...), custom_call_target="tpu_custom_call" | custom-call | flops 2 | tf_op jit(solution)/shard_map/pallas_call | solution.py:221
  47.9 4.5 %shard_map.78 = (bf16[256,1152]{1,0:T(8,128)(2,1)S(1)}, bf16[256,512]{1,0:T(8,128)(2,1)S(1)}, bf16[256,512]{1,0:T(8,128)(2,1)S(1)}, bf16[72,1152]{1,0:T(8,128)(2...) custom-call(s32[3]{0:T(128)S(1)} %pad_add_fusion.place, ...), custom_call_target="tpu_custom_call" | custom-call | flops 2 | tf_op jit(solution)/shard_map/pallas_call | solution.py:221
  52.4 4.8 %shard_map.79 = (bf16[72,1152]{1,0:T(8,128)(2,1)S(1)}, bf16[72,1152]{1,0:T(8,128)(2,1)S(1)}, bf16[72,1152]{1,0:T(8,128)(2,1)}, bf16[72,1152]{1,0:T(8,128)(2,1)}, bf16[256,1152]{1,0:T(8,128)(2,1)S(1)}) custom-call(bf16[256,1152]{1,0:T(8,128)(2,1)S(1)} %get-tuple-element.45.x_2, bf16[256,512]{1,0:T(8,128)(2,1)S(1)} %get-tuple-element.46.w_2a, ...), custom_call_target="tpu_custom_call" | custom-call | flops 2 | tf_op jit(solution)/shard_map/pallas_call | solution.py:221
  58.0 2.3 %collective-permute-start.7 = (bf16[72,1152]{1,0:T(8,128)(2,1)S(1)}, bf16[72,1152]{1,0:T(8,128)(2,1)S(1)}, u32[]{:S(2)}, u32[]{:S(2)}) collective-permute-start(bf16[72,1152]{1,0:T(8,128)(2,1)S(1)} %get-tuple-element.61), channel_id=1, source_target_pairs={{0,4},{4,0},{8,12},{12,8},{16,20},{20,16},{24,28},{28,24},{1,5},{5... | collective-permute-start | bytes 497672 | tf_op jit(solution)/shard_map/ppermute | solution.py:233
  60.3 1.6 %collective-permute-start.8 = (bf16[72,1152]{1,0:T(8,128)(2,1)}, bf16[72,1152]{1,0:T(8,128)(2,1)}, u32[]{:S(2)}, u32[]{:S(2)}) collective-permute-start(bf16[72,1152]{1,0:T(8,128)(2,1)} %get-tuple-element.62), channel_id=1, source_target_pairs={{0,8},{4,12},{8,0},{12,4},{16,24},{20,28},{24,16},{28,20},{1,9},{5... | collective-permute-start | bytes 497672 | tf_op jit(solution)/shard_map/ppermute | solution.py:233
  61.9 1.9 %collective-permute-start.10 = (bf16[72,1152]{1,0:T(8,128)(2,1)S(1)}, bf16[72,1152]{1,0:T(8,128)(2,1)}, u32[]{:S(2)}, u32[]{:S(2)}) collective-permute-start(bf16[72,1152]{1,0:T(8,128)(2,1)S(1)} %get-tuple-element.65), channel_id=1, source_target_pairs={{0,4},{4,0},{8,12},{12,8},{16,20},{20,16},{24,28},{28,24},{1,5},{5... | collective-permute-start | bytes 497672 | tf_op jit(solution)/shard_map/ppermute | solution.py:233
  63.8 1.6 %collective-permute-start.11 = (bf16[72,1152]{1,0:T(8,128)(2,1)S(1)}, bf16[72,1152]{1,0:T(8,128)(2,1)}, u32[]{:S(2)}, u32[]{:S(2)}) collective-permute-start(bf16[72,1152]{1,0:T(8,128)(2,1)S(1)} %get-tuple-element.66), channel_id=1, source_target_pairs={{0,8},{4,12},{8,0},{12,4},{16,24},{20,28},{24,16},{28,20},{1,9},{5... | collective-permute-start | bytes 497672 | tf_op jit(solution)/shard_map/ppermute | solution.py:233
  66.0 3.5 %collective-permute-start.12 = (bf16[72,1152]{1,0:T(8,128)(2,1)S(1)}, bf16[72,1152]{1,0:T(8,128)(2,1)}, u32[]{:S(2)}, u32[]{:S(2)}) collective-permute-start(bf16[72,1152]{1,0:T(8,128)(2,1)S(1)} %get-tuple-element.67), channel_id=1, source_target_pairs={{0,12},{4,8},{8,4},{12,0},{16,28},{20,24},{24,20},{28,16},{1,13},{... | collective-permute-start | bytes 497672 | tf_op jit(solution)/shard_map/ppermute | solution.py:233
  72.1 2.8 %collective-permute-done.11 = bf16[72,1152]{1,0:T(8,128)(2,1)} collective-permute-done((bf16[72,1152]{1,0:T(8,128)(2,1)S(1)}, bf16[72,1152]{1,0:T(8,128)(2,1)}, u32[]{:S(2)}, u32[]{:S(2)}) %collective-permute-start.11) | collective-permute-done | bytes 165920 | tf_op jit(solution)/shard_map/ppermute | solution.py:233
  74.9 2.2 %collective-permute-done.12 = bf16[72,1152]{1,0:T(8,128)(2,1)} collective-permute-done((bf16[72,1152]{1,0:T(8,128)(2,1)S(1)}, bf16[72,1152]{1,0:T(8,128)(2,1)}, u32[]{:S(2)}, u32[]{:S(2)}) %collective-permute-start.12) | collective-permute-done | bytes 165920 | tf_op jit(solution)/shard_map/ppermute | solution.py:233
  77.1 1.5 %select_convert_fusion = bf16[72,1152]{1,0:T(8,128)(2,1)S(1)} fusion(pred[]{:T(512)S(6)} %eq.4, bf16[72,1152]{1,0:T(8,128)(2,1)} %collective-permute-done.9, bf16[72,1152]{1,0:T(8,128)(2,1)} %collective-permute-done.8, bf16[72,1152]{1,0:T(8,128)(2,1)} %copy-done.30, bf16[72,1152]{1,0:T(8,128)(2,1)S(1)} %get-tuple-element.60, ...), kind=kLoop, calls=%fused_computation.3 | loop fusion | flops 1327104 | bytes 1492993 | tf_op jit(solution)/shard_map/convert_element_type | solution.py:311
  78.6 2.8 %collective-permute-start.13 = (bf16[72,1152]{1,0:T(8,128)(2,1)S(1)}, bf16[72,1152]{1,0:T(8,128)(2,1)S(1)}, u32[]{:S(2)}, u32[]{:S(2)}) collective-permute-start(bf16[72,1152]{1,0:T(8,128)(2,1)S(1)} %select_convert_fusion), channel_id=1, source_target_pairs={{0,16},{4,20},{8,24},{12,28},{16,0},{20,4},{24,8},{28,12},{1,17},{... | collective-permute-start | bytes 497672 | tf_op jit(solution)/shard_map/ppermute | solution.py:233
  81.4 7.2 %collective-permute-done.13 = bf16[72,1152]{1,0:T(8,128)(2,1)S(1)} collective-permute-done((bf16[72,1152]{1,0:T(8,128)(2,1)S(1)}, bf16[72,1152]{1,0:T(8,128)(2,1)S(1)}, u32[]{:S(2)}, u32[]{:S(2)}) %collective-permute-start.13) | collective-permute-done | bytes 165920 | tf_op jit(solution)/shard_map/ppermute | solution.py:233
  88.6 1.5 %add_convert_fusion.refs_0_ = bf16[72,1152]{1,0:T(8,128)(2,1)S(1)} fusion(bf16[72,1152]{1,0:T(8,128)(2,1)S(1)} %collective-permute-done.13, pred[]{:T(512)S(6)} %eq.4, bf16[72,1152]{1,0:T(8,128)(2,1)} %collective-permute-done.9, bf16[72,1152]{1,0:T(8,128)(2,1)} %collective-permute-done.8, bf16[72,1152]{1,0:T(8,128)(2,1)} %copy-done.30, ...), kind=kLoop, calls=%fused_computation.2 | loop fusion | flops 1492992 | bytes 1658881 | tf_op jit(solution)/shard_map/convert_element_type | solution.py:312
  90.2 1.4 %collective-permute-start.14 = (bf16[72,1152]{1,0:T(8,128)(2,1)S(1)}, bf16[72,1152]{1,0:T(8,128)(2,1)S(1)}, u32[]{:S(2)}, u32[]{:S(2)}) collective-permute-start(bf16[72,1152]{1,0:T(8,128)(2,1)S(1)} %add_convert_fusion.refs_0_), channel_id=1, source_target_pairs={{0,4},{4,0},{8,12},{12,8},{16,20},{20,16},{24,28},{28,24},{1,5},{5... | collective-permute-start | bytes 497672 | tf_op jit(solution)/shard_map/ppermute | solution.py:233
  91.7 2.1 %fusion = f32[256,1152]{1,0:T(8,128)} fusion(bf16[1152,1152]{1,0:T(8,128)(2,1)S(1)} %copy-done.1, bf16[512,1152]{1,0:T(8,128)(2,1)S(1)} %copy-done.21), kind=kOutput, calls=%fused_computation | convolution fusion | flops 679477248 | bytes 4423680 | tf_op jit(solution)/shard_map/dot_general | solution.py:47
  93.8 4.0 %collective-permute-start.15 = (bf16[72,1152]{1,0:T(8,128)(2,1)S(1)}, bf16[72,1152]{1,0:T(8,128)(2,1)S(1)}, u32[]{:S(2)}, u32[]{:S(2)}) collective-permute-start(bf16[72,1152]{1,0:T(8,128)(2,1)S(1)} %add_convert_fusion.refs_0_), channel_id=1, source_target_pairs={{0,8},{4,12},{8,0},{12,4},{16,24},{20,28},{24,16},{28,20},{1,9},{5... | collective-permute-start | bytes 497672 | tf_op jit(solution)/shard_map/ppermute | solution.py:233
  97.7 2.3 %collective-permute-done.17.refs_4_ = bf16[72,1152]{1,0:T(8,128)(2,1)S(1)} collective-permute-done((bf16[72,1152]{1,0:T(8,128)(2,1)S(1)}, bf16[72,1152]{1,0:T(8,128)(2,1)S(1)}, u32[]{:S(2)}, u32[]{:S(2)}) %collective-permute-start.17) | collective-permute-done | bytes 165920 | tf_op jit(solution)/shard_map/ppermute | solution.py:233
  101.3 2.2 %collective-permute-start.20 = (bf16[72,1152]{1,0:T(8,128)(2,1)S(1)}, bf16[72,1152]{1,0:T(8,128)(2,1)S(1)}, u32[]{:S(2)}, u32[]{:S(2)}) collective-permute-start(bf16[72,1152]{1,0:T(8,128)(2,1)S(1)} %collective-permute-done.17.refs_4_), channel_id=1, source_target_pairs={{0,12},{4,8},{8,4},{12,0},{16,28},{20,24},{24,20},{28,16},{1,13},{... | collective-permute-start | bytes 497672 | tf_op jit(solution)/shard_map/ppermute | solution.py:233
  103.5 2.1 %fusion.3 = f32[256,1152]{1,0:T(8,128)} fusion(bf16[256,1152]{1,0:T(8,128)(2,1)S(1)} %copy-done.29, bf16[1152,1152]{1,0:T(8,128)(2,1)S(1)} %copy-done.4), kind=kOutput, calls=%fused_computation.8 | convolution fusion | flops 679477248 | bytes 4423680 | tf_op jit(solution)/shard_map/dot_general | solution.py:47
  105.6 2.0 %collective-permute-done.16.refs_3_ = bf16[72,1152]{1,0:T(8,128)(2,1)S(1)} collective-permute-done((bf16[72,1152]{1,0:T(8,128)(2,1)S(1)}, bf16[72,1152]{1,0:T(8,128)(2,1)S(1)}, u32[]{:S(2)}, u32[]{:S(2)}) %collective-permute-start.16) | collective-permute-done | bytes 165920 | tf_op jit(solution)/shard_map/ppermute | solution.py:233
  108.3 2.5 %collective-permute-done.19.refs_6_ = bf16[72,1152]{1,0:T(8,128)(2,1)S(1)} collective-permute-done((bf16[72,1152]{1,0:T(8,128)(2,1)S(1)}, bf16[72,1152]{1,0:T(8,128)(2,1)S(1)}, u32[]{:S(2)}, u32[]{:S(2)}) %collective-permute-start.19) | collective-permute-done | bytes 165920 | tf_op jit(solution)/shard_map/ppermute | solution.py:233
  110.7 3.1 %collective-permute-done.20.refs_7_ = bf16[72,1152]{1,0:T(8,128)(2,1)S(1)} collective-permute-done((bf16[72,1152]{1,0:T(8,128)(2,1)S(1)}, bf16[72,1152]{1,0:T(8,128)(2,1)S(1)}, u32[]{:S(2)}, u32[]{:S(2)}) %collective-permute-start.20) | collective-permute-done | bytes 165920 | tf_op jit(solution)/shard_map/ppermute | solution.py:233
  113.9 2.2 %shard_map.80 = (f32[288,1152]{1,0:T(8,128)}, f32[288,1152]{1,0:T(8,128)}) custom-call(s32[3]{0:T(128)S(1)} %pad_add_fusion.place, bf16[72,1152]{1,0:T(8,128)(2,1)S(1)} %add_convert_fusion.refs_0_, bf16[72,1152]{1,0:T(8,128)(2,1)S(1)} %collective-permute-done.14.refs_1_, bf16[72,1152]{1,0:T(8,128)(2,1)S(1)} %collective-permute-done.15.refs_2_, ...), custom_call_target="tpu_custom_call" | custom-call | flops 2 | tf_op jit(solution)/shard_map/pallas_call | solution.py:221
  (84 shorter events, 24.9 us)
Async XLA Ops:
  0.6 3.6 %collective-permute-start = (bf16[256,1152]{1,0:T(8,128)(2,1)}, bf16[256,1152]{1,0:T(8,128)(2,1)S(1)}, u32[]{:S(2)}, u32[]{:S(2)}) collective-permute-start(bf16[256,1152]{1,0:T(8,128)(2,1)} %t0.3), channel_id=1, source_target_pairs={{0,1},{1,0},{2,3},{3,2},{4,5},{5,4},{6,7},{7,6},{8,9},{9,8},{10,11... | collective-permute-start | bytes 1769480 | tf_op jit(solution)/shard_map/ppermute | solution.py:233
  1.1 3.0 %collective-permute-start.2 = (bf16[256,1152]{1,0:T(8,128)(2,1)}, bf16[256,1152]{1,0:T(8,128)(2,1)S(1)}, u32[]{:S(2)}, u32[]{:S(2)}) collective-permute-start(bf16[256,1152]{1,0:T(8,128)(2,1)} %i0.3), channel_id=1, source_target_pairs={{0,1},{1,0},{2,3},{3,2},{4,5},{5,4},{6,7},{7,6},{8,9},{9,8},{10,11... | collective-permute-start | bytes 1769480 | tf_op jit(solution)/shard_map/ppermute | solution.py:233
  1.2 19.2 %collective-permute-start.1 = (bf16[256,1152]{1,0:T(8,128)(2,1)}, bf16[256,1152]{1,0:T(8,128)(2,1)S(1)}, u32[]{:S(2)}, u32[]{:S(2)}) collective-permute-start(bf16[256,1152]{1,0:T(8,128)(2,1)} %t0.3), channel_id=1, source_target_pairs={{0,2},{1,3},{2,0},{3,1},{4,6},{5,7},{6,4},{7,5},{8,10},{9,11},{10,... | collective-permute-start | bytes 1769480 | tf_op jit(solution)/shard_map/ppermute | solution.py:233
  4.1 39.0 %collective-permute-start.5 = (bf16[256,1152]{1,0:T(8,128)(2,1)}, bf16[256,1152]{1,0:T(8,128)(2,1)}, u32[]{:S(2)}, u32[]{:S(2)}) collective-permute-start(bf16[256,1152]{1,0:T(8,128)(2,1)} %i0.3), channel_id=1, source_target_pairs={{0,2},{1,3},{2,0},{3,1},{4,6},{5,7},{6,4},{7,5},{8,10},{9,11},{10,... | collective-permute-start | bytes 1769480 | tf_op jit(solution)/shard_map/ppermute | solution.py:233
  4.2 10.5 %copy-start.16 = (bf16[256,1152]{1,0:T(8,128)(2,1)}, bf16[256,1152]{1,0:T(8,128)(2,1)S(1)}, u32[]{:S(2)}) copy-start(bf16[256,1152]{1,0:T(8,128)(2,1)S(1)} %collective-permute-done.t1) | copy-start | bytes 1769476
  4.2 2.0 %copy-start = (bf16[1152,1152]{1,0:T(8,128)(2,1)S(1)}, bf16[1152,1152]{1,0:T(8,128)(2,1)}, u32[]{:S(2)}) copy-start(bf16[1152,1152]{1,0:T(8,128)(2,1)} %image_head.5) | copy-start | bytes 7962628
  6.2 1.7 %copy-start.2 = (bf16[1152,1152]{1,0:T(8,128)(2,1)S(1)}, bf16[1152,1152]{1,0:T(8,128)(2,1)}, u32[]{:S(2)}) copy-start(bf16[1152,1152]{1,0:T(8,128)(2,1)} %text_head.3) | copy-start | bytes 7962628
  10.0 4.7 %copy-start.18 = (bf16[256,1152]{1,0:T(8,128)(2,1)}, bf16[256,1152]{1,0:T(8,128)(2,1)S(1)}, u32[]{:S(2)}) copy-start(bf16[256,1152]{1,0:T(8,128)(2,1)S(1)} %collective-permute-done.2.i1) | copy-start | bytes 1769476
  20.5 1.6 %collective-permute-start.3 = (bf16[128,1152]{1,0:T(8,128)(2,1)S(1)}, bf16[128,1152]{1,0:T(8,128)(2,1)S(1)}, u32[]{:S(2)}, u32[]{:S(2)}) collective-permute-start(bf16[128,1152]{1,0:T(8,128)(2,1)S(1)} %get-tuple-element.71), channel_id=1, source_target_pairs={{0,1},{1,0},{2,3},{3,2},{4,5},{5,4},{6,7},{7,6},{8,9},{9,8},{10,11... | collective-permute-start | bytes 884744 | tf_op jit(solution)/shard_map/ppermute | solution.py:233
  20.5 2.0 %collective-permute-start.4 = (bf16[128,1152]{1,0:T(8,128)(2,1)S(1)}, bf16[128,1152]{1,0:T(8,128)(2,1)S(1)}, u32[]{:S(2)}, u32[]{:S(2)}) collective-permute-start(bf16[128,1152]{1,0:T(8,128)(2,1)S(1)} %get-tuple-element.70), channel_id=1, source_target_pairs={{0,1},{1,0},{2,3},{3,2},{4,5},{5,4},{6,7},{7,6},{8,9},{9,8},{10,11... | collective-permute-start | bytes 884744 | tf_op jit(solution)/shard_map/ppermute | solution.py:233
  35.5 7.8 %copy-start.1 = (bf16[1152,1152]{1,0:T(8,128)(2,1)S(1)}, bf16[1152,1152]{1,0:T(8,128)(2,1)}, u32[]{:S(2)}) copy-start(bf16[1152,1152]{1,0:T(8,128)(2,1)} %image_head.5) | copy-start | bytes 7962628
  35.5 7.8 %copy-start.7 = (bf16[512,1152]{1,0:T(8,128)(2,1)S(1)}, bf16[512,1152]{1,0:T(8,128)(2,1)}, u32[]{:S(2)}) copy-start(bf16[512,1152]{1,0:T(8,128)(2,1)} %copy-done.5) | copy-start | bytes 3538948
  43.1 4.7 %copy-start.20 = (bf16[512,1152]{1,0:T(8,128)(2,1)}, bf16[512,1152]{1,0:T(8,128)(2,1)S(1)}, u32[]{:S(2)}) copy-start(bf16[512,1152]{1,0:T(8,128)(2,1)S(1)} %get-tuple-element.42.dp_a) | copy-start | bytes 3538948
  43.1 4.7 %collective-permute-start.6 = (bf16[256,1152]{1,0:T(8,128)(2,1)}, bf16[256,1152]{1,0:T(8,128)(2,1)S(1)}, u32[]{:S(2)}, u32[]{:S(2)}) collective-permute-start(bf16[256,1152]{1,0:T(8,128)(2,1)} %collective-permute-done.5.i2), channel_id=1, source_target_pairs={{0,1},{1,0},{2,3},{3,2},{4,5},{5,4},{6,7},{7,6},{8,9},{9,8},{10,11... | collective-permute-start | bytes 1769480 | tf_op jit(solution)/shard_map/ppermute | solution.py:233
  47.9 4.5 %copy-start.9 = (f32[512,1152]{1,0:T(8,128)S(1)}, f32[512,1152]{1,0:T(8,128)}, u32[]{:S(2)}) copy-start(f32[512,1152]{1,0:T(8,128)} %copy-done.8) | copy-start | bytes 7077892
  58.0 7.4 %collective-permute-start.7 = (bf16[72,1152]{1,0:T(8,128)(2,1)S(1)}, bf16[72,1152]{1,0:T(8,128)(2,1)S(1)}, u32[]{:S(2)}, u32[]{:S(2)}) collective-permute-start(bf16[72,1152]{1,0:T(8,128)(2,1)S(1)} %get-tuple-element.61), channel_id=1, source_target_pairs={{0,4},{4,0},{8,12},{12,8},{16,20},{20,16},{24,28},{28,24},{1,5},{5... | collective-permute-start | bytes 497672 | tf_op jit(solution)/shard_map/ppermute | solution.py:233
  60.3 9.2 %collective-permute-start.8 = (bf16[72,1152]{1,0:T(8,128)(2,1)}, bf16[72,1152]{1,0:T(8,128)(2,1)}, u32[]{:S(2)}, u32[]{:S(2)}) collective-permute-start(bf16[72,1152]{1,0:T(8,128)(2,1)} %get-tuple-element.62), channel_id=1, source_target_pairs={{0,8},{4,12},{8,0},{12,4},{16,24},{20,28},{24,16},{28,20},{1,9},{5... | collective-permute-start | bytes 497672 | tf_op jit(solution)/shard_map/ppermute | solution.py:233
  61.9 8.9 %collective-permute-start.9 = (bf16[72,1152]{1,0:T(8,128)(2,1)}, bf16[72,1152]{1,0:T(8,128)(2,1)}, u32[]{:S(2)}, u32[]{:S(2)}) collective-permute-start(bf16[72,1152]{1,0:T(8,128)(2,1)} %get-tuple-element.63), channel_id=1, source_target_pairs={{0,12},{4,8},{8,4},{12,0},{16,28},{20,24},{24,20},{28,16},{1,13},{... | collective-permute-start | bytes 497672 | tf_op jit(solution)/shard_map/ppermute | solution.py:233
  61.9 10.2 %collective-permute-start.10 = (bf16[72,1152]{1,0:T(8,128)(2,1)S(1)}, bf16[72,1152]{1,0:T(8,128)(2,1)}, u32[]{:S(2)}, u32[]{:S(2)}) collective-permute-start(bf16[72,1152]{1,0:T(8,128)(2,1)S(1)} %get-tuple-element.65), channel_id=1, source_target_pairs={{0,4},{4,0},{8,12},{12,8},{16,20},{20,16},{24,28},{28,24},{1,5},{5... | collective-permute-start | bytes 497672 | tf_op jit(solution)/shard_map/ppermute | solution.py:233
  63.8 11.1 %collective-permute-start.11 = (bf16[72,1152]{1,0:T(8,128)(2,1)S(1)}, bf16[72,1152]{1,0:T(8,128)(2,1)}, u32[]{:S(2)}, u32[]{:S(2)}) collective-permute-start(bf16[72,1152]{1,0:T(8,128)(2,1)S(1)} %get-tuple-element.66), channel_id=1, source_target_pairs={{0,8},{4,12},{8,0},{12,4},{16,24},{20,28},{24,16},{28,20},{1,9},{5... | collective-permute-start | bytes 497672 | tf_op jit(solution)/shard_map/ppermute | solution.py:233
  66.0 11.1 %collective-permute-start.12 = (bf16[72,1152]{1,0:T(8,128)(2,1)S(1)}, bf16[72,1152]{1,0:T(8,128)(2,1)}, u32[]{:S(2)}, u32[]{:S(2)}) collective-permute-start(bf16[72,1152]{1,0:T(8,128)(2,1)S(1)} %get-tuple-element.67), channel_id=1, source_target_pairs={{0,12},{4,8},{8,4},{12,0},{16,28},{20,24},{24,20},{28,16},{1,13},{... | collective-permute-start | bytes 497672 | tf_op jit(solution)/shard_map/ppermute | solution.py:233
  69.5 22.2 %copy-start.21 = (bf16[512,1152]{1,0:T(8,128)(2,1)S(1)}, bf16[512,1152]{1,0:T(8,128)(2,1)}, u32[]{:S(2)}) copy-start(bf16[512,1152]{1,0:T(8,128)(2,1)} %copy-done.20) | copy-start | bytes 3538948
  78.6 10.0 %collective-permute-start.13 = (bf16[72,1152]{1,0:T(8,128)(2,1)S(1)}, bf16[72,1152]{1,0:T(8,128)(2,1)S(1)}, u32[]{:S(2)}, u32[]{:S(2)}) collective-permute-start(bf16[72,1152]{1,0:T(8,128)(2,1)S(1)} %select_convert_fusion), channel_id=1, source_target_pairs={{0,16},{4,20},{8,24},{12,28},{16,0},{20,4},{24,8},{28,12},{1,17},{... | collective-permute-start | bytes 497672 | tf_op jit(solution)/shard_map/ppermute | solution.py:233
  90.1 13.4 %copy-start.4 = (bf16[1152,1152]{1,0:T(8,128)(2,1)S(1)}, bf16[1152,1152]{1,0:T(8,128)(2,1)}, u32[]{:S(2)}) copy-start(bf16[1152,1152]{1,0:T(8,128)(2,1)} %text_head.3) | copy-start | bytes 7962628
  90.2 13.4 %copy-start.29 = (bf16[256,1152]{1,0:T(8,128)(2,1)S(1)}, bf16[256,1152]{1,0:T(8,128)(2,1)}, u32[]{:S(2)}) copy-start(bf16[256,1152]{1,0:T(8,128)(2,1)} %copy-done.28) | copy-start | bytes 1769476
  90.2 9.9 %collective-permute-start.17 = (bf16[72,1152]{1,0:T(8,128)(2,1)S(1)}, bf16[72,1152]{1,0:T(8,128)(2,1)S(1)}, u32[]{:S(2)}, u32[]{:S(2)}) collective-permute-start(bf16[72,1152]{1,0:T(8,128)(2,1)S(1)} %add_convert_fusion.refs_0_), channel_id=1, source_target_pairs={{0,16},{4,20},{8,24},{12,28},{16,0},{20,4},{24,8},{28,12},{1,17},{... | collective-permute-start | bytes 497672 | tf_op jit(solution)/shard_map/ppermute | solution.py:233
  90.2 11.1 %collective-permute-start.14 = (bf16[72,1152]{1,0:T(8,128)(2,1)S(1)}, bf16[72,1152]{1,0:T(8,128)(2,1)S(1)}, u32[]{:S(2)}, u32[]{:S(2)}) collective-permute-start(bf16[72,1152]{1,0:T(8,128)(2,1)S(1)} %add_convert_fusion.refs_0_), channel_id=1, source_target_pairs={{0,4},{4,0},{8,12},{12,8},{16,20},{20,16},{24,28},{28,24},{1,5},{5... | collective-permute-start | bytes 497672 | tf_op jit(solution)/shard_map/ppermute | solution.py:233
  93.8 11.8 %collective-permute-start.15 = (bf16[72,1152]{1,0:T(8,128)(2,1)S(1)}, bf16[72,1152]{1,0:T(8,128)(2,1)S(1)}, u32[]{:S(2)}, u32[]{:S(2)}) collective-permute-start(bf16[72,1152]{1,0:T(8,128)(2,1)S(1)} %add_convert_fusion.refs_0_), channel_id=1, source_target_pairs={{0,8},{4,12},{8,0},{12,4},{16,24},{20,28},{24,16},{28,20},{1,9},{5... | collective-permute-start | bytes 497672 | tf_op jit(solution)/shard_map/ppermute | solution.py:233
  97.7 9.9 %collective-permute-start.16 = (bf16[72,1152]{1,0:T(8,128)(2,1)S(1)}, bf16[72,1152]{1,0:T(8,128)(2,1)S(1)}, u32[]{:S(2)}, u32[]{:S(2)}) collective-permute-start(bf16[72,1152]{1,0:T(8,128)(2,1)S(1)} %add_convert_fusion.refs_0_), channel_id=1, source_target_pairs={{0,12},{4,8},{8,4},{12,0},{16,28},{20,24},{24,20},{28,16},{1,13},{... | collective-permute-start | bytes 497672 | tf_op jit(solution)/shard_map/ppermute | solution.py:233
  100.0 8.2 %collective-permute-start.18 = (bf16[72,1152]{1,0:T(8,128)(2,1)S(1)}, bf16[72,1152]{1,0:T(8,128)(2,1)S(1)}, u32[]{:S(2)}, u32[]{:S(2)}) collective-permute-start(bf16[72,1152]{1,0:T(8,128)(2,1)S(1)} %collective-permute-done.17.refs_4_), channel_id=1, source_target_pairs={{0,4},{4,0},{8,12},{12,8},{16,20},{20,16},{24,28},{28,24},{1,5},{5... | collective-permute-start | bytes 497672 | tf_op jit(solution)/shard_map/ppermute | solution.py:233
  101.3 9.4 %collective-permute-start.19 = (bf16[72,1152]{1,0:T(8,128)(2,1)S(1)}, bf16[72,1152]{1,0:T(8,128)(2,1)S(1)}, u32[]{:S(2)}, u32[]{:S(2)}) collective-permute-start(bf16[72,1152]{1,0:T(8,128)(2,1)S(1)} %collective-permute-done.17.refs_4_), channel_id=1, source_target_pairs={{0,8},{4,12},{8,0},{12,4},{16,24},{20,28},{24,16},{28,20},{1,9},{5... | collective-permute-start | bytes 497672 | tf_op jit(solution)/shard_map/ppermute | solution.py:233
  101.3 12.5 %collective-permute-start.20 = (bf16[72,1152]{1,0:T(8,128)(2,1)S(1)}, bf16[72,1152]{1,0:T(8,128)(2,1)S(1)}, u32[]{:S(2)}, u32[]{:S(2)}) collective-permute-start(bf16[72,1152]{1,0:T(8,128)(2,1)S(1)} %collective-permute-done.17.refs_4_), channel_id=1, source_target_pairs={{0,12},{4,8},{8,4},{12,0},{16,28},{20,24},{24,20},{28,16},{1,13},{... | collective-permute-start | bytes 497672 | tf_op jit(solution)/shard_map/ppermute | solution.py:233
  (20 other events, 22.3 us)

commit v3 on v2

--- a/solution.py
+++ b/solution.py
@@ -14,7 +14,6 @@
 STRIP = 16
 F32 = jnp.float32
 BF16 = jnp.bfloat16
-VMEM_LIMIT = 24 * 1024 * 1024
 
 
 def normalize(features, weight_matrix):
@@ -110,14 +109,9 @@
 
 
 def picker(place_ref, rows, width):
-    part = rows // QUAD
-    pieces = []
-    for k in range(QUAD):
-        first = place_ref[0] * rows + (place_ref[1] ^ k) * part
-        wanted = first + lax.broadcasted_iota(jnp.int32, (part, width), 0)
-        column = lax.broadcasted_iota(jnp.int32, (part, width), 1)
-        pieces.append(jnp.where(wanted == column, 1.0, 0.0))
-    return jnp.concatenate(pieces, axis=0).astype(BF16)
+    wanted = place_ref[0] * rows + lax.broadcasted_iota(jnp.int32, (rows, width), 0)
+    column = lax.broadcasted_iota(jnp.int32, (rows, width), 1)
+    return jnp.where(wanted == column, 1.0, 0.0).astype(BF16)
 
 
 def near_kernel(t0, t1, i0, i1, text_head, image_head, q_a, y_a, p_a, x_a, w_aa, dots):
@@ -170,24 +164,18 @@
     image_block(place, i2, image_head, y_a, y_b, x_b, w_ba, w_bb, pick, dp_b, p_b, gx, d_a, d_b, 0)
 
 
-def split_head(head, outs):
-    part = head.shape[0] // QUAD
-    for k, out in enumerate(outs):
-        out[...] = head[k * part : (k + 1) * part, :].astype(BF16)
-
-
 def fourth_kernel(
     place, i3, image_head, y_a, y_b, dp_a, dp_2, image_pick, pick_2,
-    x_b, w_ba, w_bb, h0, h1, h2, h3, pick, dp_b, p_b, gx, d_a, d_b,
+    x_b, w_ba, w_bb, head_out, pick, dp_b, p_b, gx, d_a, d_b,
 ):
     image_block(place, i3, image_head, y_a, y_b, x_b, w_ba, w_bb, pick, dp_b, p_b, gx, d_a, d_b, 1)
     head = dot_nn(image_pick[...], dp_a[...]) + dot_nn(pick_2[...], dp_2[...])
-    split_head(head + dot_nn(pick[...], dp_b[...]), (h0, h1, h2, h3))
+    head_out[...] = (head + dot_nn(pick[...], dp_b[...])).astype(BF16)
 
 
 def fifth_kernel(
     x_2, w_2a, w_2b, x_3, w_3a, w_3b, q_a, q_b, gy_a_in, gy_b_in, text_pick,
-    k0, k1, k2, k3, dq_own, gy_a, gy_b, dq_a, dq_b,
+    head_out, dq_own, gy_a, gy_b, dq_a, dq_b,
 ):
     half = x_2.shape[0]
     gy_a[...] = gy_a_in[...] + dot_tn(w_2a[...], x_2[...]) + dot_tn(w_3a[...], x_3[...])
@@ -196,36 +184,22 @@
     back_rows(q_b, gy_b, dq_b)
     dq_own[...] = dq_a[:half, :]
     head = dot_nn(text_pick[:, : 2 * half], dq_a[...]) + dot_nn(text_pick[:, 2 * half :], dq_b[...])
-    split_head(head, (k0, k1, k2, k3))
-
-
-def place_kernel(place, *refs):
-    mine, theirs, outs = refs[:QUAD], refs[QUAD : 2 * QUAD], refs[2 * QUAD :]
-    part = mine[0].shape[0]
-    for head, out in enumerate(outs):
-        for wanted, pieces in ((head, mine), (1 - head, theirs)):
-
-            @pl.when(place[2] == wanted)
-            def _(out=out, pieces=pieces):
-                for k, piece in enumerate(pieces):
-                    first = pl.multiple_of((place[1] ^ k) * part, part)
-                    out[pl.ds(first, part), :] = piece[...].astype(F32)
-
-
-def call(kernel, outs, scratch, args, macs, place=None, keep=True):
+    head_out[...] = head.astype(BF16)
+
+
+def call(kernel, outs, scratch, args, mib, place=None, macs=1):
     args = [pltpu.with_memory_space_constraint(a, pltpu.VMEM) for a in args]
     specs = [pl.BlockSpec(memory_space=pltpu.VMEM)] * len(args)
     if place is not None:
         args, specs = [place, *args], [pl.BlockSpec(memory_space=pltpu.SMEM), *specs]
-    shape = pltpu.VMEM if keep else jax.ShapeDtypeStruct
     return pl.pallas_call(
         kernel,
-        out_shape=[shape(s, t) for s, t in outs],
+        out_shape=[pltpu.VMEM(s, t) for s, t in outs],
         in_specs=specs,
         out_specs=[pl.BlockSpec(memory_space=pltpu.VMEM)] * len(outs),
         scratch_shapes=[pltpu.VMEM(s, t) for s, t in scratch],
-        compiler_params=pltpu.CompilerParams(vmem_limit_bytes=VMEM_LIMIT),
-        cost_estimate=pl.CostEstimate(flops=2 * (macs > 0), bytes_accessed=0, transcendentals=0),
+        compiler_params=pltpu.CompilerParams(vmem_limit_bytes=mib * 1024 * 1024),
+        cost_estimate=pl.CostEstimate(flops=2 * macs, bytes_accessed=0, transcendentals=0),
     )(*args)
 
 
@@ -244,9 +218,13 @@
     part = rows_out // QUAD
     cut = lax.axis_index("cuts")
     upper = cut // QUAD
-    place = jnp.stack([lax.axis_index("loop"), cut & (QUAD - 1), upper]).astype(jnp.int32)
+    place = lax.axis_index("loop").astype(jnp.int32).reshape(1)
     loop = functools.partial(swap, axis="loop", size=n_loop)
     cuts = functools.partial(swap, axis="cuts", size=n_cuts)
+    quads = functools.partial(
+        lax.all_to_all, axis_name="cuts", split_axis=0, concat_axis=0, tiled=True,
+        axis_index_groups=[list(range(g, g + QUAD)) for g in range(0, n_cuts, QUAD)],
+    )
     macs = half * width * width
 
     t0, i0 = text_features, image_features
@@ -257,13 +235,13 @@
     wide, wide_b = ((near, width), F32), ((near, width), BF16)
     tall, tall_b = ((half, width), F32), ((half, width), BF16)
     square, block_w = ((near, near), BF16), ((half, near), BF16)
-    pieces_out = [((part, width), BF16)] * QUAD
+    head_term = ((rows_out, width), BF16)
     q_a, y_a, p_a, x_a, w_aa = call(
         near_kernel,
         [wide, wide_b, wide, wide_b, square],
         [((near, near), F32)],
         (t0, t1, i0, i1, text_head, image_head),
-        5 * macs,
+        8,
     )
     t2 = after(t2, w_aa)
     t3 = [loop(t2[: half // 2], mask=1), loop(t2[half // 2 :], mask=1)]
@@ -272,7 +250,7 @@
         [wide, wide_b, wide_b, wide, wide, ((rows_out, 2 * near), BF16), ((rows_out, near), BF16)],
         [((near, near), F32), wide, square],
         (t0, t1, t2, *t3, i0, i1, text_head, y_a, p_a, x_a, w_aa),
-        8 * macs,
+        8,
         place,
     )
     i2 = after(i2, dp_a)
@@ -283,45 +261,41 @@
         [tall_b, block_w, block_w, ((rows_out, half), BF16), tall_b],
         block_scratch,
         (i2, image_head, y_a, y_b),
-        2 * macs,
+        8,
         place,
     )
-    x_3, w_3a, w_3b, *image_parts = call(
+    x_3, w_3a, w_3b, image_term = call(
         fourth_kernel,
-        [tall_b, block_w, block_w] + pieces_out,
+        [tall_b, block_w, block_w, head_term],
         [((rows_out, half), BF16), tall_b] + block_scratch,
         (i3, image_head, y_a, y_b, dp_a, dp_2, image_pick, pick_2),
-        3 * macs,
+        8,
         place,
     )
-    arrived = [cuts(image_parts[k], mask=k) for k in range(1, QUAD)]
-    *text_parts, dq_own = call(
+    image_terms = quads(image_term)
+    text_term, dq_own = call(
         fifth_kernel,
-        pieces_out + [tall_b],
+        [head_term, tall_b],
         [wide, wide, wide_b, wide_b],
         (x_2, w_2a, w_2b, x_3, w_3a, w_3b, q_a, q_b, gy_a, gy_b, text_pick),
-        4 * macs,
-    )
-    image_sum = sum((a.astype(F32) for a in arrived), image_parts[0].astype(F32))
-    arrived = [cuts(text_parts[k], mask=k) for k in range(1, QUAD)]
+        14,
+        macs=4 * macs,
+    )
+    text_terms = quads(text_term)
     image_grad = dot_nt(dp_a[:half], image_head)
     text_grad = dot_nt(dq_own, text_head)
-    text_sum = sum((a.astype(F32) for a in arrived), text_parts[0].astype(F32))
+    image_sum, text_sum = (
+        jnp.sum(terms.reshape(QUAD, part, width).astype(F32), axis=0)
+        for terms in (image_terms, text_terms)
+    )
     kept = jnp.where(upper == 1, text_sum, image_sum)
     sent = jnp.where(upper == 1, image_sum, text_sum).astype(BF16)
     mine = (kept + cuts(sent, mask=QUAD).astype(F32)).astype(BF16)
     theirs = cuts(mine, mask=QUAD)
-    mine_all = [mine] + [cuts(mine, mask=k) for k in range(1, QUAD)]
-    theirs_all = [theirs] + [cuts(theirs, mask=k) for k in range(1, QUAD)]
-    image_out, text_out = call(
-        place_kernel,
-        [((rows_out, width), F32)] * 2,
-        [],
-        (*mine_all, *theirs_all),
-        rows_out * width,
-        place,
-        keep=False,
-    )
+    mine_all = quads(jnp.tile(mine, (QUAD, 1)))
+    theirs_all = quads(jnp.tile(theirs, (QUAD, 1)))
+    image_out = jnp.where(upper == 1, theirs_all, mine_all).astype(F32)
+    text_out = jnp.where(upper == 1, mine_all, theirs_all).astype(F32)
     return (image_grad, text_grad, image_out, text_out)
 
 

time: 117 us -> 131 us (1.12)
  blocking collectives: 0 us -> 15.2 us
  starting transfers between devices: 26.9 us -> 20.1 us
  other arithmetic: 3.06 us -> 7.48 us
  Pallas kernels: 28.3 us -> 24 us
  waiting for transfers between devices: 26.8 us -> 30.8 us
    ppermute x21 -> x9, starting transfers between devices: 26.9 us -> 6.2 us  [swap(): return lax.ppermute(array, axis, [(i, i ^ mask) for i in range(size)])]
    all_to_all x0 -> x1, blocking collectives: none -> 15.2 us  [per_device(): text_terms = quads(text_term)]
    all_to_all x0 -> x3, starting transfers between devices: none -> 14 us  [the longest x1 5.61 us: per_device(): theirs_all = quads(jnp.tile(theirs, (QUAD, 1)))]
    all_to_all x0 -> x3, waiting for transfers between devices: none -> 13.8 us  [the longest x1 7.06 us: per_device(): image_terms = quads(image_term)]
    ppermute x21 -> x9, waiting for transfers between devices: 26.8 us -> 17 us  [swap(): return lax.ppermute(array, axis, [(i, i ^ mask) for i in range(size)])]
    pallas_call x6 -> x5, Pallas kernels: 28.3 us -> 24 us  [call(): pl.pallas_call(kernel, out_shape=[pltpu.VMEM(s, t) for s, t in outs], in_...]
    reduce_sum x0 -> x2, other arithmetic: none -> 3.2 us  [per_device(): jnp.sum(terms.reshape(QUAD, part, width).astype(F32), axis=0)]
    another operation x0 -> x2, local copies, waits for them, and re-layouts: none -> 2.69 us  [the longest x1 1.8 us: per_device(): theirs_all = quads(jnp.tile(theirs, (QUAD, 1)))]
  transfers between devices with their start and end apart: 21 -> 12, of which waited for: 12 -> 7; matrix products, arithmetic and copies ran while one was open for 4% -> 6% of each run, Pallas kernels for 14% -> 12%
where the time goes in v3:
time: 131 us; the launch traced here: 130 us
  waiting for transfers between devices  30.8 us (24%)
  local copies, waits for them, and re-layouts  26.2 us (20%)
  Pallas kernels  24 us (18%)
  starting transfers between devices  20.1 us (15%)
  blocking collectives  15.2 us (12%)
  other arithmetic  7.48 us (6%)
  matrix products  5.32 us (4%)
    pallas_call x5, Pallas kernels, call(): pl.pallas_call(kernel, out_shape=[pltpu.VMEM(s, t) for s, t in outs], in_...  24 us
    unnamed x56, local copies, waits for them, and re-layouts  23.5 us
    ppermute x9, waiting for transfers between devices, swap(): return lax.ppermute(array, axis, [(i, i ^ mask) for i in range(size)])  17 us
    all_to_all x1, blocking collectives, per_device(): text_terms = quads(text_term)  15.2 us
    all_to_all x1, waiting for transfers between devices, per_device(): image_terms = quads(image_term)  7.06 us
    ppermute x9, starting transfers between devices, swap(): return lax.ppermute(array, axis, [(i, i ^ mask) for i in range(size)])  6.2 us
    all_to_all x1, starting transfers between devices, per_device(): theirs_all = quads(jnp.tile(theirs, (QUAD, 1)))  5.61 us
    dot_general x2, matrix products, dot_nt(): lax.dot_general(left, right, (((1,), (1,)), ((), ())), preferred_element_...  5.32 us
  transfers between devices with their start and end apart: 12, of which 7 were waited for; matrix products, arithmetic and copies ran while one was open for 6% of the time, Pallas kernels for 12%

profile of v3, /device:TPU:0, one launch (start us, length us, event | category | flops | bytes accessed | tf_op | source)
XLA Modules:
  0.0 130.1 jit_solution(13002258735379710855)
XLA Ops:
  1.2 2.9 %collective-permute-start.1 = (bf16[256,1152]{1,0:T(8,128)(2,1)}, bf16[256,1152]{1,0:T(8,128)(2,1)S(1)}, u32[]{:S(2)}, u32[]{:S(2)}) collective-permute-start(bf16[256,1152]{1,0:T(8,128)(2,1)} %t0.3), channel_id=1, source_target_pairs={{0,2},{1,3},{2,0},{3,1},{4,6},{5,7},{6,4},{7,5},{8,10},{9,11},{10,... | collective-permute-start | bytes 1769480 | tf_op jit(solution)/shard_map/ppermute | solution.py:207
  4.2 2.0 %copy-done = bf16[1152,1152]{1,0:T(8,128)(2,1)S(1)} copy-done((bf16[1152,1152]{1,0:T(8,128)(2,1)S(1)}, bf16[1152,1152]{1,0:T(8,128)(2,1)}, u32[]{:S(2)}) %copy-start) | copy-done | bytes 2654232
  6.2 1.7 %copy-done.2 = bf16[1152,1152]{1,0:T(8,128)(2,1)S(1)} copy-done((bf16[1152,1152]{1,0:T(8,128)(2,1)S(1)}, bf16[1152,1152]{1,0:T(8,128)(2,1)}, u32[]{:S(2)}) %copy-start.2) | copy-done | bytes 2654232
  10.0 4.5 %shard_map.75 = (f32[512,1152]{1,0:T(8,128)S(1)}, bf16[512,1152]{1,0:T(8,128)(2,1)S(1)}, f32[512,1152]{1,0:T(8,128)S(1)}, bf16[512,1152]{1,0:T(8,128)(2,1)S(1)}, bf16[512,512]{1,0:T(8,128)(2,1)S(1)}) custom-call(bf16[256,1152]{1,0:T(8,128)(2,1)S(1)} %copy-done.12, bf16[256,1152]{1,0:T(8,128)(2,1)S(1)} %collective-permute-done.t1, ...), custom_call_target="tpu_custom_call" | custom-call | flops 2 | tf_op jit(solution)/shard_map/pallas_call | solution.py:195
  15.6 1.4 %copy-done.8 = f32[512,1152]{1,0:T(8,128)} copy-done((f32[512,1152]{1,0:T(8,128)}, f32[512,1152]{1,0:T(8,128)S(1)}, u32[]{:S(2)}) %copy-start.8) | copy-done | bytes 2359320
  17.0 1.4 %copy-done.10 = f32[512,1152]{1,0:T(8,128)} copy-done((f32[512,1152]{1,0:T(8,128)}, f32[512,1152]{1,0:T(8,128)S(1)}, u32[]{:S(2)}) %copy-start.10) | copy-done | bytes 2359320
  19.9 1.1 collective-permute-done.3.t3
  22.1 1.7 %copy-done.3 = bf16[1152,1152]{1,0:T(8,128)(2,1)S(1)} copy-done((bf16[1152,1152]{1,0:T(8,128)(2,1)S(1)}, bf16[1152,1152]{1,0:T(8,128)(2,1)}, u32[]{:S(2)}) %copy-start.3) | copy-done | bytes 2654232
  23.9 1.3 copy-done.6
  25.1 1.7 %copy-done.11 = f32[512,1152]{1,0:T(8,128)S(1)} copy-done((f32[512,1152]{1,0:T(8,128)S(1)}, f32[512,1152]{1,0:T(8,128)}, u32[]{:S(2)}) %copy-start.11) | copy-done | bytes 2359320
  31.1 1.3 copy-done.22
  34.3 6.8 %shard_map.76 = (f32[512,1152]{1,0:T(8,128)S(1)}, bf16[512,1152]{1,0:T(8,128)(2,1)S(1)}, bf16[512,1152]{1,0:T(8,128)(2,1)S(1)}, f32[512,1152]{1,0:T(8,128)S(1)},...) custom-call(s32[1]{0:T(128)} %bitcast.place, ...), custom_call_target="tpu_custom_call" | custom-call | flops 2 | tf_op jit(solution)/shard_map/pallas_call | solution.py:195
  41.4 4.5 %shard_map.77 = (bf16[256,1152]{1,0:T(8,128)(2,1)S(1)}, bf16[256,512]{1,0:T(8,128)(2,1)S(1)}, bf16[256,512]{1,0:T(8,128)(2,1)S(1)}, bf16[288,256]{1,0:T(8,128)(2,1)S(1)}, bf16[256,1152]{1,0:T(8,128)(2,1)S(1)}) custom-call(s32[1]{0:T(128)} %bitcast.place, bf16[256,1152]{1,0:T(8,128)(2,1)} %collective-permute-done.5.i2, bf16[1152,1152]{1,0:T(8,128)(2,1)S(1)} %copy-done.1, ...), custom_call_target="tpu_custom_call" | custom-call | flops 2 | tf_op jit(solution)/shard_map/pallas_call | solution.py:195
  45.9 4.7 %shard_map.78 = (bf16[256,1152]{1,0:T(8,128)(2,1)S(1)}, bf16[256,512]{1,0:T(8,128)(2,1)S(1)}, bf16[256,512]{1,0:T(8,128)(2,1)S(1)}, bf16[288,1152]{1,0:T(8,128)(2,1)}) custom-call(s32[1]{0:T(128)} %bitcast.place, bf16[256,1152]{1,0:T(8,128)(2,1)S(1)} %collective-permute-done.6.i3, bf16[1152,1152]{1,0:T(8,128)(2,1)S(1)} %copy-done.1, ...), custom_call_target="tpu_custom_call" | custom-call | flops 2 | tf_op jit(solution)/shard_map/pallas_call | solution.py:195
  50.6 3.6 %shard_map.79 = (bf16[288,1152]{1,0:T(8,128)(2,1)S(1)}, bf16[256,1152]{1,0:T(8,128)(2,1)S(1)}) custom-call(bf16[256,1152]{1,0:T(8,128)(2,1)S(1)} %get-tuple-element.37.x_2, bf16[256,512]{1,0:T(8,128)(2,1)S(1)} %get-tuple-element.38.w_2a, bf16[256,512]{1,0:T(8,128)(2,1)S(1)} %get-tuple-element.39.w_2b, bf16[256,1152]{1,0:T(8,128)(2,1)S(1)} %get-tuple-element.43.x_3, ...), custom_call_target="tpu_custom_call" | custom-call | flops 2717908992 | tf_op jit(solution)/shard_map/pallas_call | solution.py:195
  54.2 15.2 %all_to_all.30 = bf16[4,72,1152]{2,1,0:T(8,128)(2,1)} all-to-all(bf16[4,72,1152]{2,1,0:T(8,128)(2,1)S(1)} %bitcast.12), channel_id=1, replica_groups={{0,4,8,12},{16,20,24,28},{1,5,9,13},{17,21,25,29},{2,6,10,14},{18,22,26..., dimensions={0} | all-to-all | bytes 1327104 | tf_op jit(solution)/shard_map/all_to_all | solution.py:284
  69.4 4.2 %all-to-all-start.1 = ((bf16[4,72,1152]{2,1,0:T(8,128)(2,1)}), bf16[4,72,1152]{2,1,0:T(8,128)(2,1)}, u32[]{:S(2)}, u32[]{:S(2)}) async-start(bf16[4,72,1152]{2,1,0:T(8,128)(2,1)} %bitcast.2), calls=%async_computation.1 | async-start | bytes 1327104 | tf_op jit(solution)/shard_map/all_to_all | solution.py:275
  73.6 1.9 %convert_reduce_fusion.1 = f32[72,1152]{1,0:T(8,128)} fusion(bf16[4,72,1152]{2,1,0:T(8,128)(2,1)} %all_to_all.30), kind=kLoop, calls=%fused_computation.1 | loop fusion | flops 580608 | bytes 995328 | tf_op jit(solution)/shard_map/reduce_sum | solution.py:288
  75.5 7.1 %all-to-all-done.1 = bf16[4,72,1152]{2,1,0:T(8,128)(2,1)} async-done(((bf16[4,72,1152]{2,1,0:T(8,128)(2,1)}), bf16[4,72,1152]{2,1,0:T(8,128)(2,1)}, u32[]{:S(2)}, u32[]{:S(2)}) %all-to-all-start.1) | async-done | bytes 663584 | tf_op jit(solution)/shard_map/all_to_all | solution.py:275
  82.6 1.3 convert_reduce_fusion
  84.8 1.7 %collective-permute-start.7 = (bf16[72,1152]{1,0:T(8,128)(2,1)S(1)}, bf16[72,1152]{1,0:T(8,128)(2,1)S(1)}, u32[]{:S(2)}, u32[]{:S(2)}) collective-permute-start(bf16[72,1152]{1,0:T(8,128)(2,1)S(1)} %select_convert_fusion), channel_id=1, source_target_pairs={{0,16},{4,20},{8,24},{12,28},{16,0},{20,4},{24,8},{28,12},{1,17},{... | collective-permute-start | bytes 497672 | tf_op jit(solution)/shard_map/ppermute | solution.py:207
  86.5 8.0 %collective-permute-done.7 = bf16[72,1152]{1,0:T(8,128)(2,1)S(1)} collective-permute-done((bf16[72,1152]{1,0:T(8,128)(2,1)S(1)}, bf16[72,1152]{1,0:T(8,128)(2,1)S(1)}, u32[]{:S(2)}, u32[]{:S(2)}) %collective-permute-start.7) | collective-permute-done | bytes 165920 | tf_op jit(solution)/shard_map/ppermute | solution.py:207
  95.5 4.2 %all-to-all-start.3 = ((bf16[4,72,1152]{2,1,0:T(8,128)(2,1)}), bf16[4,72,1152]{2,1,0:T(8,128)(2,1)}, u32[]{:S(2)}, u32[]{:S(2)}) async-start(bf16[4,72,1152]{2,1,0:T(8,128)(2,1)} %tile.5), calls=%async_computation.3 | async-start | bytes 1327104 | tf_op jit(solution)/shard_map/all_to_all | solution.py:295
  99.8 7.6 %collective-permute-done.8 = bf16[72,1152]{1,0:T(8,128)(2,1)} collective-permute-done((bf16[72,1152]{1,0:T(8,128)(2,1)S(1)}, bf16[72,1152]{1,0:T(8,128)(2,1)}, u32[]{:S(2)}, u32[]{:S(2)}) %collective-permute-start.8) | collective-permute-done | bytes 165920 | tf_op jit(solution)/shard_map/ppermute | solution.py:207
  107.4 2.8 %all-to-all-done.3 = bf16[4,72,1152]{2,1,0:T(8,128)(2,1)} async-done(((bf16[4,72,1152]{2,1,0:T(8,128)(2,1)}), bf16[4,72,1152]{2,1,0:T(8,128)(2,1)}, u32[]{:S(2)}, u32[]{:S(2)}) %all-to-all-start.3) | async-done | bytes 663584 | tf_op jit(solution)/shard_map/all_to_all | solution.py:295
  110.2 1.8 %tile.4 = bf16[4,72,1152]{2,1,0:T(8,128)(2,1)} broadcast(bf16[72,1152]{1,0:T(8,128)(2,1)} %collective-permute-done.8), dimensions={1,2} | broadcast | bytes 829440 | tf_op jit(solution)/shard_map/tile | solution.py:296
  112.0 5.6 %all-to-all-start.2 = ((bf16[4,72,1152]{2,1,0:T(8,128)(2,1)}), bf16[4,72,1152]{2,1,0:T(8,128)(2,1)}, u32[]{:S(2)}, u32[]{:S(2)}) async-start(bf16[4,72,1152]{2,1,0:T(8,128)(2,1)} %tile.4), calls=%async_computation.2 | async-start | bytes 1327104 | tf_op jit(solution)/shard_map/all_to_all | solution.py:296
  117.6 3.3 %fusion = f32[256,1152]{1,0:T(8,128)} fusion(bf16[1152,1152]{1,0:T(8,128)(2,1)S(1)} %copy-done.1, bf16[512,1152]{1,0:T(8,128)(2,1)} %copy-done.20), kind=kOutput, calls=%fused_computation.6 | convolution fusion | flops 679477248 | bytes 4423680 | tf_op jit(solution)/shard_map/dot_general | solution.py:46
  120.9 2.1 %fusion.3 = f32[256,1152]{1,0:T(8,128)} fusion(bf16[256,1152]{1,0:T(8,128)(2,1)S(1)} %get-tuple-element.51, bf16[1152,1152]{1,0:T(8,128)(2,1)S(1)} %copy-done.4), kind=kOutput, calls=%fused_computation.11 | convolution fusion | flops 679477248 | bytes 4423680 | tf_op jit(solution)/shard_map/dot_general | solution.py:46
  123.0 3.9 %all-to-all-done.2 = bf16[4,72,1152]{2,1,0:T(8,128)(2,1)} async-done(((bf16[4,72,1152]{2,1,0:T(8,128)(2,1)}), bf16[4,72,1152]{2,1,0:T(8,128)(2,1)}, u32[]{:S(2)}, u32[]{:S(2)}) %all-to-all-start.2) | async-done | bytes 663584 | tf_op jit(solution)/shard_map/all_to_all | solution.py:296
  126.9 1.4 %broadcast_select_fusion = (bf16[4,72,1152]{2,1,0:T(8,128)(2,1)S(1)}, bf16[4,72,1152]{2,1,0:T(8,128)(2,1)S(1)}) fusion(bf16[4,72,1152]{2,1,0:T(8,128)(2,1)} %all-to-all-done.3, bf16[4,72,1152]{2,1,0:T(8,128)(2,1)} %all-to-all-done.2, pred[]{:T(512)S(6)} %eq.2), kind=kLoop, calls=%fused_computation.4 | loop fusion | flops 663552 | bytes 2654209 | tf_op jit(solution)/shard_map/jit(_where)/select_n | solution.py:298
  128.3 1.8 %bitcast_convert_fusion = (f32[288,1152]{1,0:T(8,128)}, f32[288,1152]{1,0:T(8,128)}) fusion(bf16[4,72,1152]{2,1,0:T(8,128)(2,1)S(1)} %get-tuple-element.54, bf16[4,72,1152]{2,1,0:T(8,128)(2,1)S(1)} %get-tuple-element.55), kind=kLoop, calls=%fused_computation.2 | loop fusion | flops 663552 | bytes 3981312 | tf_op jit(solution)/shard_map/convert_element_type | solution.py:298
  (65 shorter events, 15.0 us)
Async XLA Ops:
  0.6 3.6 %collective-permute-start = (bf16[256,1152]{1,0:T(8,128)(2,1)}, bf16[256,1152]{1,0:T(8,128)(2,1)S(1)}, u32[]{:S(2)}, u32[]{:S(2)}) collective-permute-start(bf16[256,1152]{1,0:T(8,128)(2,1)} %t0.3), channel_id=1, source_target_pairs={{0,1},{1,0},{2,3},{3,2},{4,5},{5,4},{6,7},{7,6},{8,9},{9,8},{10,11... | collective-permute-start | bytes 1769480 | tf_op jit(solution)/shard_map/ppermute | solution.py:207
  1.1 3.0 %collective-permute-start.2 = (bf16[256,1152]{1,0:T(8,128)(2,1)}, bf16[256,1152]{1,0:T(8,128)(2,1)S(1)}, u32[]{:S(2)}, u32[]{:S(2)}) collective-permute-start(bf16[256,1152]{1,0:T(8,128)(2,1)} %i0.3), channel_id=1, source_target_pairs={{0,1},{1,0},{2,3},{3,2},{4,5},{5,4},{6,7},{7,6},{8,9},{9,8},{10,11... | collective-permute-start | bytes 1769480 | tf_op jit(solution)/shard_map/ppermute | solution.py:207
  1.2 18.0 %collective-permute-start.1 = (bf16[256,1152]{1,0:T(8,128)(2,1)}, bf16[256,1152]{1,0:T(8,128)(2,1)S(1)}, u32[]{:S(2)}, u32[]{:S(2)}) collective-permute-start(bf16[256,1152]{1,0:T(8,128)(2,1)} %t0.3), channel_id=1, source_target_pairs={{0,2},{1,3},{2,0},{3,1},{4,6},{5,7},{6,4},{7,5},{8,10},{9,11},{10,... | collective-permute-start | bytes 1769480 | tf_op jit(solution)/shard_map/ppermute | solution.py:207
  4.1 37.0 %collective-permute-start.5 = (bf16[256,1152]{1,0:T(8,128)(2,1)}, bf16[256,1152]{1,0:T(8,128)(2,1)}, u32[]{:S(2)}, u32[]{:S(2)}) collective-permute-start(bf16[256,1152]{1,0:T(8,128)(2,1)} %i0.3), channel_id=1, source_target_pairs={{0,2},{1,3},{2,0},{3,1},{4,6},{5,7},{6,4},{7,5},{8,10},{9,11},{10,... | collective-permute-start | bytes 1769480 | tf_op jit(solution)/shard_map/ppermute | solution.py:207
  4.2 10.4 %copy-start.16 = (bf16[256,1152]{1,0:T(8,128)(2,1)}, bf16[256,1152]{1,0:T(8,128)(2,1)S(1)}, u32[]{:S(2)}) copy-start(bf16[256,1152]{1,0:T(8,128)(2,1)S(1)} %collective-permute-done.t1) | copy-start | bytes 1769476
  4.2 2.0 %copy-start = (bf16[1152,1152]{1,0:T(8,128)(2,1)S(1)}, bf16[1152,1152]{1,0:T(8,128)(2,1)}, u32[]{:S(2)}) copy-start(bf16[1152,1152]{1,0:T(8,128)(2,1)} %image_head.5) | copy-start | bytes 7962628
  6.2 1.7 %copy-start.2 = (bf16[1152,1152]{1,0:T(8,128)(2,1)S(1)}, bf16[1152,1152]{1,0:T(8,128)(2,1)}, u32[]{:S(2)}) copy-start(bf16[1152,1152]{1,0:T(8,128)(2,1)} %text_head.3) | copy-start | bytes 7962628
  7.9 1.1 copy-start.12
  9.0 1.1 copy-start.14
  10.0 4.5 %copy-start.18 = (bf16[256,1152]{1,0:T(8,128)(2,1)}, bf16[256,1152]{1,0:T(8,128)(2,1)S(1)}, u32[]{:S(2)}) copy-start(bf16[256,1152]{1,0:T(8,128)(2,1)S(1)} %collective-permute-done.2.i1) | copy-start | bytes 1769476
  15.6 1.4 %copy-start.8 = (f32[512,1152]{1,0:T(8,128)}, f32[512,1152]{1,0:T(8,128)S(1)}, u32[]{:S(2)}) copy-start(f32[512,1152]{1,0:T(8,128)S(1)} %get-tuple-element.46.q_a) | copy-start | bytes 7077892
  17.0 1.4 %copy-start.10 = (f32[512,1152]{1,0:T(8,128)}, f32[512,1152]{1,0:T(8,128)S(1)}, u32[]{:S(2)}) copy-start(f32[512,1152]{1,0:T(8,128)S(1)} %get-tuple-element.32.p_a) | copy-start | bytes 7077892
  19.3 2.9 %copy-start.21 = (bf16[512,1152]{1,0:T(8,128)(2,1)}, bf16[512,1152]{1,0:T(8,128)(2,1)S(1)}, u32[]{:S(2)}) copy-start(bf16[512,1152]{1,0:T(8,128)(2,1)S(1)} %get-tuple-element.33.x_a) | copy-start | bytes 3538948
  19.3 1.6 %collective-permute-start.3 = (bf16[128,1152]{1,0:T(8,128)(2,1)S(1)}, bf16[128,1152]{1,0:T(8,128)(2,1)S(1)}, u32[]{:S(2)}, u32[]{:S(2)}) collective-permute-start(bf16[128,1152]{1,0:T(8,128)(2,1)S(1)} %get-tuple-element.57), channel_id=1, source_target_pairs={{0,1},{1,0},{2,3},{3,2},{4,5},{5,4},{6,7},{7,6},{8,9},{9,8},{10,11... | collective-permute-start | bytes 884744 | tf_op jit(solution)/shard_map/ppermute | solution.py:207
  19.4 2.0 %collective-permute-start.4 = (bf16[128,1152]{1,0:T(8,128)(2,1)S(1)}, bf16[128,1152]{1,0:T(8,128)(2,1)S(1)}, u32[]{:S(2)}, u32[]{:S(2)}) collective-permute-start(bf16[128,1152]{1,0:T(8,128)(2,1)S(1)} %get-tuple-element.56), channel_id=1, source_target_pairs={{0,1},{1,0},{2,3},{3,2},{4,5},{5,4},{6,7},{7,6},{8,9},{9,8},{10,11... | collective-permute-start | bytes 884744 | tf_op jit(solution)/shard_map/ppermute | solution.py:207
  22.1 1.8 %copy-start.3 = (bf16[1152,1152]{1,0:T(8,128)(2,1)S(1)}, bf16[1152,1152]{1,0:T(8,128)(2,1)}, u32[]{:S(2)}) copy-start(bf16[1152,1152]{1,0:T(8,128)(2,1)} %text_head.3) | copy-start | bytes 7962628
  23.9 1.3 copy-start.6
  25.1 1.7 %copy-start.11 = (f32[512,1152]{1,0:T(8,128)S(1)}, f32[512,1152]{1,0:T(8,128)}, u32[]{:S(2)}) copy-start(f32[512,1152]{1,0:T(8,128)} %copy-done.10) | copy-start | bytes 7077892
  30.0 1.1 copy-start.19
  31.1 1.3 copy-start.22
  34.3 7.1 %copy-start.1 = (bf16[1152,1152]{1,0:T(8,128)(2,1)S(1)}, bf16[1152,1152]{1,0:T(8,128)(2,1)}, u32[]{:S(2)}) copy-start(bf16[1152,1152]{1,0:T(8,128)(2,1)} %image_head.5) | copy-start | bytes 7962628
  34.3 7.1 %copy-start.7 = (bf16[512,1152]{1,0:T(8,128)(2,1)S(1)}, bf16[512,1152]{1,0:T(8,128)(2,1)}, u32[]{:S(2)}) copy-start(bf16[512,1152]{1,0:T(8,128)(2,1)} %copy-done.5) | copy-start | bytes 3538948
  41.2 4.7 %copy-start.20 = (bf16[512,1152]{1,0:T(8,128)(2,1)}, bf16[512,1152]{1,0:T(8,128)(2,1)S(1)}, u32[]{:S(2)}) copy-start(bf16[512,1152]{1,0:T(8,128)(2,1)S(1)} %get-tuple-element.34.dp_a) | copy-start | bytes 3538948
  41.2 4.7 %collective-permute-start.6 = (bf16[256,1152]{1,0:T(8,128)(2,1)}, bf16[256,1152]{1,0:T(8,128)(2,1)S(1)}, u32[]{:S(2)}, u32[]{:S(2)}) collective-permute-start(bf16[256,1152]{1,0:T(8,128)(2,1)} %collective-permute-done.5.i2), channel_id=1, source_target_pairs={{0,1},{1,0},{2,3},{3,2},{4,5},{5,4},{6,7},{7,6},{8,9},{9,8},{10,11... | collective-permute-start | bytes 1769480 | tf_op jit(solution)/shard_map/ppermute | solution.py:207
  45.9 4.7 %copy-start.9 = (f32[512,1152]{1,0:T(8,128)S(1)}, f32[512,1152]{1,0:T(8,128)}, u32[]{:S(2)}) copy-start(f32[512,1152]{1,0:T(8,128)} %copy-done.8) | copy-start | bytes 7077892
  69.4 13.2 %all-to-all-start.1 = ((bf16[4,72,1152]{2,1,0:T(8,128)(2,1)}), bf16[4,72,1152]{2,1,0:T(8,128)(2,1)}, u32[]{:S(2)}, u32[]{:S(2)}) async-start(bf16[4,72,1152]{2,1,0:T(8,128)(2,1)} %bitcast.2), calls=%async_computation.1 | async-start | bytes 1327104 | tf_op jit(solution)/shard_map/all_to_all | solution.py:275
  82.6 11.9 %copy-start.27 = (f32[72,1152]{1,0:T(8,128)S(1)}, f32[72,1152]{1,0:T(8,128)}, u32[]{:S(2)}) copy-start(f32[72,1152]{1,0:T(8,128)} %convert_reduce_fusion.1) | copy-start | bytes 995332
  84.8 9.7 %collective-permute-start.7 = (bf16[72,1152]{1,0:T(8,128)(2,1)S(1)}, bf16[72,1152]{1,0:T(8,128)(2,1)S(1)}, u32[]{:S(2)}, u32[]{:S(2)}) collective-permute-start(bf16[72,1152]{1,0:T(8,128)(2,1)S(1)} %select_convert_fusion), channel_id=1, source_target_pairs={{0,16},{4,20},{8,24},{12,28},{16,0},{20,4},{24,8},{28,12},{1,17},{... | collective-permute-start | bytes 497672 | tf_op jit(solution)/shard_map/ppermute | solution.py:207
  95.5 14.7 %all-to-all-start.3 = ((bf16[4,72,1152]{2,1,0:T(8,128)(2,1)}), bf16[4,72,1152]{2,1,0:T(8,128)(2,1)}, u32[]{:S(2)}, u32[]{:S(2)}) async-start(bf16[4,72,1152]{2,1,0:T(8,128)(2,1)} %tile.5), calls=%async_computation.3 | async-start | bytes 1327104 | tf_op jit(solution)/shard_map/all_to_all | solution.py:295
  99.6 7.8 %collective-permute-start.8 = (bf16[72,1152]{1,0:T(8,128)(2,1)S(1)}, bf16[72,1152]{1,0:T(8,128)(2,1)}, u32[]{:S(2)}, u32[]{:S(2)}) collective-permute-start(bf16[72,1152]{1,0:T(8,128)(2,1)S(1)} %add_convert_fusion), channel_id=1, source_target_pairs={{0,16},{4,20},{8,24},{12,28},{16,0},{20,4},{24,8},{28,12},{1,17},{... | collective-permute-start | bytes 497672 | tf_op jit(solution)/shard_map/ppermute | solution.py:207
  112.0 14.8 %all-to-all-start.2 = ((bf16[4,72,1152]{2,1,0:T(8,128)(2,1)}), bf16[4,72,1152]{2,1,0:T(8,128)(2,1)}, u32[]{:S(2)}, u32[]{:S(2)}) async-start(bf16[4,72,1152]{2,1,0:T(8,128)(2,1)} %tile.4), calls=%async_computation.2 | async-start | bytes 1327104 | tf_op jit(solution)/shard_map/all_to_all | solution.py:296
  117.6 3.3 %copy-start.4 = (bf16[1152,1152]{1,0:T(8,128)(2,1)S(1)}, bf16[1152,1152]{1,0:T(8,128)(2,1)}, u32[]{:S(2)}) copy-start(bf16[1152,1152]{1,0:T(8,128)(2,1)} %text_head.3) | copy-start | bytes 7962628
  (8 other events, 7.7 us)

commit v4 on v3

--- a/solution.py
+++ b/solution.py
@@ -108,13 +108,31 @@
         weights_ref[first : first + STRIP, :] = weights_of(dots_ref[first : first + STRIP, :], pairs)
 
 
-def picker(place_ref, rows, width):
-    wanted = place_ref[0] * rows + lax.broadcasted_iota(jnp.int32, (rows, width), 0)
+def one_hot(first, rows, width):
+    wanted = first + lax.broadcasted_iota(jnp.int32, (rows, width), 0)
     column = lax.broadcasted_iota(jnp.int32, (rows, width), 1)
-    return jnp.where(wanted == column, 1.0, 0.0).astype(BF16)
-
-
-def near_kernel(t0, t1, i0, i1, text_head, image_head, q_a, y_a, p_a, x_a, w_aa, dots):
+    return jnp.where(wanted == column, 1.0, 0.0)
+
+
+def picker(place_ref, rows, width, sides):
+    part = rows // QUAD
+    pieces = []
+    for k in range(QUAD):
+        for side in sides:
+            first = (place_ref[0] ^ side) * rows + (place_ref[1] ^ k) * part
+            pieces.append(one_hot(first, part, width))
+    return jnp.concatenate(pieces, axis=0).astype(BF16)
+
+
+def split_head(head, outs):
+    part = head.shape[0] // QUAD
+    for k, out in enumerate(outs):
+        out[...] = head[k * part : (k + 1) * part, :].astype(BF16)
+
+
+def near_kernel(
+    place, t0, t1, i0, i1, text_head, image_head, q_a, y_a, p_a, x_a, w_aa, pick_i, pick_t, dots
+):
     half = t0.shape[0]
     q_a[:half, :] = dot_nn(t0[...], text_head[...])
     q_a[half:, :] = dot_nn(t1[...], text_head[...])
@@ -124,58 +142,54 @@
     unit_rows(p_a, x_a)
     dots[...] = dot_nt(x_a[...], y_a[...])
     weight_rows(dots, w_aa, 0)
-
-
-def text_kernel(
-    place, t0, t1, t2, t3, t4, i0, i1, text_head, y_a, p_a, x_a, w_aa,
-    q_b, y_b, dp_a, gy_a, gy_b, text_pick, image_pick, dots, gx, w_ab,
+    rows = pick_t.shape[0]
+    pick = picker(place, rows, t0.shape[1], (0,))
+    pick_t[:, :half] = dot_nt(pick, t0[...]).astype(BF16)
+    pick_t[:, half:] = dot_nt(pick, t1[...]).astype(BF16)
+    pick = picker(place, rows, t0.shape[1], (0, 2))
+    pick_i[:, :half] = dot_nt(pick, i0[...]).astype(BF16)
+    pick_i[:, half:] = dot_nt(pick, i1[...]).astype(BF16)
+
+
+def image_kernel(
+    t2, t3, t4, t5, t6, text_head, y_a, p_a, x_a, w_aa, pick_i,
+    q_b, y_b, w_ab, dp_a, h0, h1, h2, h3, dots, gx,
 ):
     half = t2.shape[0]
     q_b[:half, :] = dot_nn(t2[...], text_head[...])
-    t3 = jnp.concatenate([t3[...], t4[...]], axis=0)
-    q_b[half:, :] = dot_nn(t3, text_head[...])
+    q_b[half:, :] = dot_nn(jnp.concatenate([t3[...], t4[...], t5[...], t6[...]], axis=0), text_head[...])
     unit_rows(q_b, y_b)
     dots[...] = dot_nt(x_a[...], y_b[...])
     weight_rows(dots, w_ab)
     gx[...] = dot_nn(w_aa[...], y_a[...]) + dot_nn(w_ab[...], y_b[...])
     back_rows(p_a, gx, dp_a)
+    split_head(dot_nn(pick_i[...], dp_a[...]), (h0, h1, h2, h3))
+
+
+def pull_kernel(place, t2, t3, t4, t5, t6, x_a, w_aa, w_ab, gy_a, gy_b, pick_t):
+    half = t2.shape[0]
     gy_a[...] = dot_tn(w_aa[...], x_a[...])
     gy_b[...] = dot_tn(w_ab[...], x_a[...])
-    pick = picker(place, text_pick.shape[0], t0.shape[1])
-    for block, t in enumerate((t0, t1, t2, t3)):
-        text_pick[:, block * half : (block + 1) * half] = dot_nt(pick, t[...]).astype(BF16)
-    for block, i in enumerate((i0, i1)):
-        image_pick[:, block * half : (block + 1) * half] = dot_nt(pick, i[...]).astype(BF16)
-
-
-def image_block(place, i, image_head, y_a, y_b, x_b, w_ba, w_bb, pick, dp_b, p_b, gx, d_a, d_b, block):
-    p_b[...] = dot_nn(i[...], image_head[...])
+    pick = picker(place, pick_t.shape[0], t2.shape[1], (0,))
+    pick_t[:, :half] = dot_nt(pick, t2[...]).astype(BF16)
+    far = jnp.concatenate([t3[...], t4[...], t5[...], t6[...]], axis=0)
+    pick_t[:, half:] = dot_nt(pick, far).astype(BF16)
+
+
+def block_kernel(block, *refs):
+    *features, image_head, y_a, y_b, x_b, w_ba, w_bb, p_b, d_a, d_b = refs
+    features = jnp.concatenate([i[...] for i in features], axis=0)
+    p_b[...] = dot_nn(features, image_head[...])
     unit_rows(p_b, x_b)
     d_a[...] = dot_nt(x_b[...], y_a[...])
     d_b[...] = dot_nt(x_b[...], y_b[...])
     weight_rows(d_a, w_ba)
-    weight_rows(d_b, w_bb, block * i.shape[0])
-    gx[...] = dot_nn(w_ba[...], y_a[...]) + dot_nn(w_bb[...], y_b[...])
-    back_rows(p_b, gx, dp_b)
-    pick[...] = dot_nt(picker(place, pick.shape[0], i.shape[1]), i[...]).astype(BF16)
-
-
-def third_kernel(place, i2, image_head, y_a, y_b, x_b, w_ba, w_bb, pick, dp_b, p_b, gx, d_a, d_b):
-    image_block(place, i2, image_head, y_a, y_b, x_b, w_ba, w_bb, pick, dp_b, p_b, gx, d_a, d_b, 0)
-
-
-def fourth_kernel(
-    place, i3, image_head, y_a, y_b, dp_a, dp_2, image_pick, pick_2,
-    x_b, w_ba, w_bb, head_out, pick, dp_b, p_b, gx, d_a, d_b,
-):
-    image_block(place, i3, image_head, y_a, y_b, x_b, w_ba, w_bb, pick, dp_b, p_b, gx, d_a, d_b, 1)
-    head = dot_nn(image_pick[...], dp_a[...]) + dot_nn(pick_2[...], dp_2[...])
-    head_out[...] = (head + dot_nn(pick[...], dp_b[...])).astype(BF16)
-
-
-def fifth_kernel(
-    x_2, w_2a, w_2b, x_3, w_3a, w_3b, q_a, q_b, gy_a_in, gy_b_in, text_pick,
-    head_out, dq_own, gy_a, gy_b, dq_a, dq_b,
+    weight_rows(d_b, w_bb, block * x_b.shape[0])
+
+
+def last_kernel(
+    x_2, w_2a, w_2b, x_3, w_3a, w_3b, q_a, q_b, gy_a_in, gy_b_in, pick_a, pick_b,
+    h0, h1, h2, h3, dq_own, gy_a, gy_b, dq_a, dq_b,
 ):
     half = x_2.shape[0]
     gy_a[...] = gy_a_in[...] + dot_tn(w_2a[...], x_2[...]) + dot_tn(w_3a[...], x_3[...])
@@ -183,18 +197,29 @@
     back_rows(q_a, gy_a, dq_a)
     back_rows(q_b, gy_b, dq_b)
     dq_own[...] = dq_a[:half, :]
-    head = dot_nn(text_pick[:, : 2 * half], dq_a[...]) + dot_nn(text_pick[:, 2 * half :], dq_b[...])
-    head_out[...] = head.astype(BF16)
-
-
-def call(kernel, outs, scratch, args, mib, place=None, macs=1):
+    split_head(dot_nn(pick_a[...], dq_a[...]) + dot_nn(pick_b[...], dq_b[...]), (h0, h1, h2, h3))
+
+
+def grad_kernel(back, head, out):
+    out[...] = dot_nt(back[: out.shape[0], :], head[...])
+
+
+def place_kernel(place, h0, h1, h2, h3, out):
+    part = h0.shape[0]
+    for k, piece in enumerate((h0, h1, h2, h3)):
+        first = pl.multiple_of((place[1] ^ k) * part, part)
+        out[pl.ds(first, part), :] = piece[...].astype(F32)
+
+
+def call(kernel, outs, scratch, args, mib, place=None, macs=1, keep=True):
     args = [pltpu.with_memory_space_constraint(a, pltpu.VMEM) for a in args]
     specs = [pl.BlockSpec(memory_space=pltpu.VMEM)] * len(args)
     if place is not None:
         args, specs = [place, *args], [pl.BlockSpec(memory_space=pltpu.SMEM), *specs]
+    shape = pltpu.VMEM if keep else jax.ShapeDtypeStruct
     return pl.pallas_call(
         kernel,
-        out_shape=[pltpu.VMEM(s, t) for s, t in outs],
+        out_shape=[shape(s, t) for s, t in outs],
         in_specs=specs,
         out_specs=[pl.BlockSpec(memory_space=pltpu.VMEM)] * len(outs),
         scratch_shapes=[pltpu.VMEM(s, t) for s, t in scratch],
@@ -216,87 +241,86 @@
     near = 2 * half
     rows_out = width // n_loop
     part = rows_out // QUAD
-    cut = lax.axis_index("cuts")
-    upper = cut // QUAD
-    place = lax.axis_index("loop").astype(jnp.int32).reshape(1)
     loop = functools.partial(swap, axis="loop", size=n_loop)
     cuts = functools.partial(swap, axis="cuts", size=n_cuts)
-    quads = functools.partial(
-        lax.all_to_all, axis_name="cuts", split_axis=0, concat_axis=0, tiled=True,
-        axis_index_groups=[list(range(g, g + QUAD)) for g in range(0, n_cuts, QUAD)],
-    )
     macs = half * width * width
 
-    t0, i0 = text_features, image_features
-    t2 = loop(t0, mask=2)
-    i2 = loop(i0, mask=2)
+    def add(own, others):
+        return sum((other.astype(F32) for other in others), own.astype(F32)).astype(BF16)
+
+    def finish(total):
+        total = add(total, [cuts(total, mask=QUAD)])
+        pieces = [total] + [cuts(total, mask=k) for k in range(1, QUAD)]
+        outs = [((rows_out, width), F32)]
+        return call(place_kernel, outs, [], pieces, 4, place, keep=False)[0]
+
+    t2 = loop(text_features, mask=2)
+    i2 = loop(image_features, mask=2)
+    place = jnp.stack([lax.axis_index("loop"), lax.axis_index("cuts") & (QUAD - 1)])
+    place = place.astype(jnp.int32)
+    t0, i0, place = lax.optimization_barrier((text_features, image_features, place))
     t1 = loop(t0, mask=1)
     i1 = loop(i0, mask=1)
     wide, wide_b = ((near, width), F32), ((near, width), BF16)
     tall, tall_b = ((half, width), F32), ((half, width), BF16)
-    square, block_w = ((near, near), BF16), ((half, near), BF16)
-    head_term = ((rows_out, width), BF16)
-    q_a, y_a, p_a, x_a, w_aa = call(
+    square, dots = ((near, near), BF16), ((near, near), F32)
+    block_w, block_dots = ((half, near), BF16), ((half, near), F32)
+    pick_one, pick_two = ((rows_out, near), BF16), ((2 * rows_out, near), BF16)
+    q_a, y_a, p_a, x_a, w_aa, pick_i, pick_a = call(
         near_kernel,
-        [wide, wide_b, wide, wide_b, square],
-        [((near, near), F32)],
+        [wide, wide_b, wide, wide_b, square, pick_two, pick_one],
+        [dots],
         (t0, t1, i0, i1, text_head, image_head),
         8,
+        place,
     )
     t2 = after(t2, w_aa)
-    t3 = [loop(t2[: half // 2], mask=1), loop(t2[half // 2 :], mask=1)]
-    q_b, y_b, dp_a, gy_a, gy_b, text_pick, image_pick = call(
-        text_kernel,
-        [wide, wide_b, wide_b, wide, wide, ((rows_out, 2 * near), BF16), ((rows_out, near), BF16)],
-        [((near, near), F32), wide, square],
-        (t0, t1, t2, *t3, i0, i1, text_head, y_a, p_a, x_a, w_aa),
+    t3 = [loop(rows, mask=1) for rows in jnp.split(t2, 4)]
+    q_b, y_b, w_ab, dp_a, *image_parts = call(
+        image_kernel,
+        [wide, wide_b, square, wide_b] + [((2 * part, width), BF16)] * QUAD,
+        [dots, wide],
+        (t2, *t3, text_head, y_a, p_a, x_a, w_aa, pick_i),
+        8,
+    )
+    image_others = [cuts(image_parts[k], mask=k) for k in range(1, QUAD)]
+    gy_a, gy_b, pick_b = call(
+        pull_kernel,
+        [wide, wide, pick_one],
+        [],
+        (t2, *t3, x_a, w_aa, w_ab),
         8,
         place,
     )
-    i2 = after(i2, dp_a)
-    i3 = loop(i2, mask=1)
-    block_scratch = [tall, tall, ((half, near), F32), ((half, near), F32)]
-    x_2, w_2a, w_2b, pick_2, dp_2 = call(
-        third_kernel,
-        [tall_b, block_w, block_w, ((rows_out, half), BF16), tall_b],
-        block_scratch,
-        (i2, image_head, y_a, y_b),
-        8,
-        place,
-    )
-    x_3, w_3a, w_3b, image_term = call(
-        fourth_kernel,
-        [tall_b, block_w, block_w, head_term],
-        [((rows_out, half), BF16), tall_b] + block_scratch,
-        (i3, image_head, y_a, y_b, dp_a, dp_2, image_pick, pick_2),
-        8,
-        place,
-    )
-    image_terms = quads(image_term)
-    text_term, dq_own = call(
-        fifth_kernel,
-        [head_term, tall_b],
+    i2 = after(i2, gy_a)
+    i3 = [loop(rows, mask=1) for rows in jnp.split(i2, 2)]
+    blocks = []
+    for block, i in enumerate(([i2], i3)):
+        blocks += call(
+            functools.partial(block_kernel, block),
+            [tall_b, block_w, block_w],
+            [tall, block_dots, block_dots],
+            (*i, image_head, y_a, y_b),
+            8,
+        )
+    *text_parts, dq_own = call(
+        last_kernel,
+        [((part, width), BF16)] * QUAD + [tall_b],
         [wide, wide, wide_b, wide_b],
-        (x_2, w_2a, w_2b, x_3, w_3a, w_3b, q_a, q_b, gy_a, gy_b, text_pick),
+        (*blocks, q_a, q_b, gy_a, gy_b, pick_a, pick_b),
         14,
-        macs=4 * macs,
-    )
-    text_terms = quads(text_term)
-    image_grad = dot_nt(dp_a[:half], image_head)
-    text_grad = dot_nt(dq_own, text_head)
-    image_sum, text_sum = (
-        jnp.sum(terms.reshape(QUAD, part, width).astype(F32), axis=0)
-        for terms in (image_terms, text_terms)
-    )
-    kept = jnp.where(upper == 1, text_sum, image_sum)
-    sent = jnp.where(upper == 1, image_sum, text_sum).astype(BF16)
-    mine = (kept + cuts(sent, mask=QUAD).astype(F32)).astype(BF16)
-    theirs = cuts(mine, mask=QUAD)
-    mine_all = quads(jnp.tile(mine, (QUAD, 1)))
-    theirs_all = quads(jnp.tile(theirs, (QUAD, 1)))
-    image_out = jnp.where(upper == 1, theirs_all, mine_all).astype(F32)
-    text_out = jnp.where(upper == 1, mine_all, theirs_all).astype(F32)
-    return (image_grad, text_grad, image_out, text_out)
+    )
+    text_sum = add(text_parts[0], [cuts(text_parts[k], mask=k) for k in range(1, QUAD)])
+    image_others = [after(other, dq_own) for other in image_others]
+    image_sum = add(image_parts[0], image_others)
+    image_sum = add(image_sum[:part], [loop(image_sum[part:], mask=2)])
+    image_out = finish(image_sum)
+    text_out = finish(text_sum)
+    grads = [
+        call(grad_kernel, [tall], [], (back, head), 4, macs=macs, keep=False)[0]
+        for back, head in ((after(dp_a, dq_own), image_head), (dq_own, text_head))
+    ]
+    return (*grads, image_out, text_out)
 
 
 def solution(mesh):

time: 131 us -> 88.9 us (0.68)
  local copies, waits for them, and re-layouts: 26.2 us -> 5.74 us
  blocking collectives: 15.2 us -> 0 us
  other arithmetic: 7.48 us -> 0.48 us
  Pallas kernels: 24 us -> 29.6 us
  matrix products: 5.32 us -> 0 us
  starting transfers between devices: 20.1 us -> 21.6 us
    unnamed x56 -> x12, local copies, waits for them, and re-layouts: 23.5 us -> 5.63 us
    ppermute x9 -> x25, starting transfers between devices: 6.2 us -> 21.6 us  [swap(): return lax.ppermute(array, axis, [(i, i ^ mask) for i in range(size)])]
    all_to_all x1 -> x0, blocking collectives: 15.2 us -> none  [per_device(): text_terms = quads(text_term)]
    all_to_all x3 -> x0, starting transfers between devices: 14 us -> none  [the longest x1 5.61 us: per_device(): theirs_all = quads(jnp.tile(theirs, (QUAD, 1)))]
    all_to_all x3 -> x0, waiting for transfers between devices: 13.8 us -> none  [the longest x1 7.06 us: per_device(): image_terms = quads(image_term)]
    ppermute x9 -> x25, waiting for transfers between devices: 17 us -> 30.3 us  [swap(): return lax.ppermute(array, axis, [(i, i ^ mask) for i in range(size)])]
    pallas_call x5 -> x10, Pallas kernels: 24 us -> 29.6 us  [call(): pl.pallas_call(kernel, out_shape=[shape(s, t) for s, t in outs], in_specs...]
    dot_general x2 -> x0, matrix products: 5.32 us -> none  [dot_nt(): lax.dot_general(left, right, (((1,), (1,)), ((), ())), preferred_element_...]
  transfers between devices with their start and end apart: 12 -> 25, of which waited for: 7 -> 13; matrix products, arithmetic and copies ran while one was open for 6% -> 1% of each run, Pallas kernels for 12% -> 32%
where the time goes in v4:
time: 88.9 us; the launch traced here: 88.6 us
  waiting for transfers between devices  30.3 us (34%)
  Pallas kernels  29.6 us (33%)
  starting transfers between devices  21.6 us (24%)
  local copies, waits for them, and re-layouts  5.74 us (6%)
    ppermute x25, waiting for transfers between devices, swap(): return lax.ppermute(array, axis, [(i, i ^ mask) for i in range(size)])  30.3 us
    pallas_call x10, Pallas kernels, call(): pl.pallas_call(kernel, out_shape=[shape(s, t) for s, t in outs], in_specs...  29.6 us
    ppermute x25, starting transfers between devices, swap(): return lax.ppermute(array, axis, [(i, i ^ mask) for i in range(size)])  21.6 us
    unnamed x12, local copies, waits for them, and re-layouts  5.63 us
  transfers between devices with their start and end apart: 25, of which 13 were waited for; matrix products, arithmetic and copies ran while one was open for 1% of the time, Pallas kernels for 32%

profile of v4, /device:TPU:0, one launch (start us, length us, event | category | flops | bytes accessed | tf_op | source)
XLA Modules:
  0.0 88.6 jit_solution(9617352495956767261)
XLA Ops:
  1.2 2.9 %collective-permute-start = (bf16[256,1152]{1,0:T(8,128)(2,1)}, bf16[256,1152]{1,0:T(8,128)(2,1)S(1)}, u32[]{:S(2)}, u32[]{:S(2)}) collective-permute-start(bf16[256,1152]{1,0:T(8,128)(2,1)} %t0), channel_id=1, source_target_pairs={{0,2},{1,3},{2,0},{3,1},{4,6},{5,7},{6,4},{7,5},{8,10},{9,11},{10,... | collective-permute-start | bytes 1769480 | tf_op jit(solution)/shard_map/ppermute | solution.py:232
  4.2 1.7 %copy-done = bf16[1152,1152]{1,0:T(8,128)(2,1)S(1)} copy-done((bf16[1152,1152]{1,0:T(8,128)(2,1)S(1)}, bf16[1152,1152]{1,0:T(8,128)(2,1)}, u32[]{:S(2)}) %copy-start) | copy-done | bytes 2654232
  6.0 1.7 %copy-done.2 = bf16[1152,1152]{1,0:T(8,128)(2,1)S(1)} copy-done((bf16[1152,1152]{1,0:T(8,128)(2,1)S(1)}, bf16[1152,1152]{1,0:T(8,128)(2,1)}, u32[]{:S(2)}) %copy-start.2) | copy-done | bytes 2654232
  7.7 1.1 %copy-done.4 = bf16[256,1152]{1,0:T(8,128)(2,1)S(1)} copy-done((bf16[256,1152]{1,0:T(8,128)(2,1)S(1)}, bf16[256,1152]{1,0:T(8,128)(2,1)}, u32[]{:S(2)}) %copy-start.4) | copy-done | bytes 589848
  8.8 1.1 %copy-done.5 = bf16[256,1152]{1,0:T(8,128)(2,1)S(1)} copy-done((bf16[256,1152]{1,0:T(8,128)(2,1)S(1)}, bf16[256,1152]{1,0:T(8,128)(2,1)}, u32[]{:S(2)}) %copy-start.5) | copy-done | bytes 589848
  9.8 6.4 %shard_map.75 = (f32[512,1152]{1,0:T(8,128)S(1)}, bf16[512,1152]{1,0:T(8,128)(2,1)S(1)}, f32[512,1152]{1,0:T(8,128)S(1)}, bf16[512,1152]{1,0:T(8,128)(2,1)S(1)},...) custom-call(s32[2]{0:T(128)S(1)} %pad_add_fusion.place, ...), custom_call_target="tpu_custom_call" | custom-call | flops 2 | tf_op jit(solution)/shard_map/pallas_call | solution.py:220
  16.3 2.2 %collective-permute-done.t2 = bf16[256,1152]{1,0:T(8,128)(2,1)S(1)} collective-permute-done((bf16[256,1152]{1,0:T(8,128)(2,1)}, bf16[256,1152]{1,0:T(8,128)(2,1)S(1)}, u32[]{:S(2)}, u32[]{:S(2)}) %collective-permute-start) | collective-permute-done | bytes 589856 | tf_op jit(solution)/shard_map/ppermute | solution.py:232
  20.7 5.6 %shard_map.76 = (f32[512,1152]{1,0:T(8,128)S(1)}, bf16[512,1152]{1,0:T(8,128)(2,1)S(1)}, bf16[512,512]{1,0:T(8,128)(2,1)S(1)}, bf16[512,1152]{1,0:T(8,128)(2,1)S...) custom-call(bf16[256,1152]{1,0:T(8,128)(2,1)S(1)} %collective-permut, ...), custom_call_target="tpu_custom_call" | custom-call | flops 2 | tf_op jit(solution)/shard_map/pallas_call | solution.py:220
  26.3 2.5 %shard_map.77 = (f32[512,1152]{1,0:T(8,128)S(1)}, f32[512,1152]{1,0:T(8,128)S(1)}, bf16[288,512]{1,0:T(8,128)(2,1)S(1)}) custom-call(s32[2]{0:T(128)S(1)} %pad_add_fusion.place, bf16[256,1152]{1,0:T(8,128)(2,1)S(1)} %collective-permute-done.t2, bf16[64,1152]{1,0:T(8,128)(2,1)S(1)} %collective-permute-done.3.t3, ...), custom_call_target="tpu_custom_call" | custom-call | flops 2 | tf_op jit(solution)/shard_map/pallas_call | solution.py:220
  28.8 1.8 %collective-permute-done.7.refs_0_ = bf16[256,1152]{1,0:T(8,128)(2,1)S(1)} collective-permute-done((bf16[256,1152]{1,0:T(8,128)(2,1)}, bf16[256,1152]{1,0:T(8,128)(2,1)S(1)}, u32[]{:S(2)}, u32[]{:S(2)}) %collective-permute-start.7) | collective-permute-done | bytes 589856 | tf_op jit(solution)/shard_map/ppermute | solution.py:232
  30.6 1.8 %collective-permute-start.10 = (bf16[144,1152]{1,0:T(8,128)(2,1)S(1)}, bf16[144,1152]{1,0:T(8,128)(2,1)S(1)}, u32[]{:S(2)}, u32[]{:S(2)}) collective-permute-start(bf16[144,1152]{1,0:T(8,128)(2,1)S(1)} %get-tuple-element.70), channel_id=1, source_target_pairs={{0,4},{4,0},{8,12},{12,8},{16,20},{20,16},{24,28},{28,24},{1,5},{5... | collective-permute-start | bytes 995336 | tf_op jit(solution)/shard_map/ppermute | solution.py:232
  32.4 1.6 %collective-permute-start.11 = (bf16[144,1152]{1,0:T(8,128)(2,1)S(1)}, bf16[144,1152]{1,0:T(8,128)(2,1)S(1)}, u32[]{:S(2)}, u32[]{:S(2)}) collective-permute-start(bf16[144,1152]{1,0:T(8,128)(2,1)S(1)} %get-tuple-element.72), channel_id=1, source_target_pairs={{0,8},{4,12},{8,0},{12,4},{16,24},{20,28},{24,16},{28,20},{1,9},{5... | collective-permute-start | bytes 995336 | tf_op jit(solution)/shard_map/ppermute | solution.py:232
  34.7 2.1 %shard_map.78 = (bf16[256,1152]{1,0:T(8,128)(2,1)S(1)}, bf16[256,512]{1,0:T(8,128)(2,1)S(1)}, bf16[256,512]{1,0:T(8,128)(2,1)S(1)}) custom-call(bf16[256,1152]{1,0:T(8,128)(2,1)S(1)} %collective-permute-done.7.refs_0_, bf16[1152,1152]{1,0:T(8,128)(2,1)S(1)} %copy-done.1, bf16[512,1152]{1,0:T(8,128)(2,1)S(1)} %get-tuple-element.47.y_a.refs_2_.refs_3_, ...), custom_call_target="tpu_custom_call" | custom-call | flops 2 | tf_op jit(solution)/shard_map/pallas_call | solution.py:220
  36.9 1.9 %shard_map.79 = (bf16[256,1152]{1,0:T(8,128)(2,1)S(1)}, bf16[256,512]{1,0:T(8,128)(2,1)S(1)}, bf16[256,512]{1,0:T(8,128)(2,1)S(1)}) custom-call(bf16[128,1152]{1,0:T(8,128)(2,1)S(1)} %collective-permute-done.8.refs_0_, bf16[128,1152]{1,0:T(8,128)(2,1)S(1)} %collective-permute-done.9.refs_1_, bf16[1152,1152]{1,0:T(8,128)(2,1)S(1)} %copy-done.1, ...), custom_call_target="tpu_custom_call" | custom-call | flops 2 | tf_op jit(solution)/shard_map/pallas_call | solution.py:220
  38.8 3.6 %shard_map.80 = (bf16[72,1152]{1,0:T(8,128)(2,1)S(1)}, bf16[72,1152]{1,0:T(8,128)(2,1)S(1)}, bf16[72,1152]{1,0:T(8,128)(2,1)S(1)}, bf16[72,1152]{1,0:T(8,128)(2,1)S(1)}, bf16[256,1152]{1,0:T(8,128)(2,1)S(1)}) custom-call(bf16[256,1152]{1,0:T(8,128)(2,1)S(1)} %get-tuple-element.56.x_2, bf16[256,512]{1,0:T(8,128)(2,1)S(1)} %get-tuple-element.57.w_2a, ...), custom_call_target="tpu_custom_call" | custom-call | flops 2 | tf_op jit(solution)/shard_map/pallas_call | solution.py:220
  42.4 1.8 %collective-permute-start.18 = (bf16[72,1152]{1,0:T(8,128)(2,1)S(1)}, bf16[72,1152]{1,0:T(8,128)(2,1)S(1)}, u32[]{:S(2)}, u32[]{:S(2)}) collective-permute-start(bf16[72,1152]{1,0:T(8,128)(2,1)S(1)} %get-tuple-element.77), channel_id=1, source_target_pairs={{0,4},{4,0},{8,12},{12,8},{16,20},{20,16},{24,28},{28,24},{1,5},{5... | collective-permute-start | bytes 497672 | tf_op jit(solution)/shard_map/ppermute | solution.py:232
  44.3 1.6 %collective-permute-start.19 = (bf16[72,1152]{1,0:T(8,128)(2,1)S(1)}, bf16[72,1152]{1,0:T(8,128)(2,1)S(1)}, u32[]{:S(2)}, u32[]{:S(2)}) collective-permute-start(bf16[72,1152]{1,0:T(8,128)(2,1)S(1)} %get-tuple-element.78), channel_id=1, source_target_pairs={{0,8},{4,12},{8,0},{12,4},{16,24},{20,28},{24,16},{28,20},{1,9},{5... | collective-permute-start | bytes 497672 | tf_op jit(solution)/shard_map/ppermute | solution.py:232
  46.0 3.8 %collective-permute-done.12 = bf16[144,1152]{1,0:T(8,128)(2,1)S(1)} collective-permute-done((bf16[144,1152]{1,0:T(8,128)(2,1)S(1)}, bf16[144,1152]{1,0:T(8,128)(2,1)S(1)}, u32[]{:S(2)}, u32[]{:S(2)}) %collective-permute-start.12) | collective-permute-done | bytes 331808 | tf_op jit(solution)/shard_map/ppermute | solution.py:232
  50.0 1.3 %collective-permute-start.13 = (bf16[72,1152]{1,0:T(8,128)(2,1)S(1)}, bf16[72,1152]{1,0:T(8,128)(2,1)S(1)}, u32[]{:S(2)}, u32[]{:S(2)}) collective-permute-start(bf16[72,1152]{1,0:T(8,128)(2,1)S(1)} %slice.9), channel_id=1, source_target_pairs={{0,2},{1,3},{2,0},{3,1},{4,6},{5,7},{6,4},{7,5},{8,10},{9,11},{10,... | collective-permute-start | bytes 497672 | tf_op jit(solution)/shard_map/ppermute | solution.py:232
  51.2 2.1 %collective-permute-done.18 = bf16[72,1152]{1,0:T(8,128)(2,1)S(1)} collective-permute-done((bf16[72,1152]{1,0:T(8,128)(2,1)S(1)}, bf16[72,1152]{1,0:T(8,128)(2,1)S(1)}, u32[]{:S(2)}, u32[]{:S(2)}) %collective-permute-start.18) | collective-permute-done | bytes 165920 | tf_op jit(solution)/shard_map/ppermute | solution.py:232
  53.3 1.9 %collective-permute-done.20 = bf16[72,1152]{1,0:T(8,128)(2,1)S(1)} collective-permute-done((bf16[72,1152]{1,0:T(8,128)(2,1)S(1)}, bf16[72,1152]{1,0:T(8,128)(2,1)S(1)}, u32[]{:S(2)}, u32[]{:S(2)}) %collective-permute-start.20) | collective-permute-done | bytes 165920 | tf_op jit(solution)/shard_map/ppermute | solution.py:232
  55.3 2.6 %collective-permute-start.21 = (bf16[72,1152]{1,0:T(8,128)(2,1)S(1)}, bf16[72,1152]{1,0:T(8,128)(2,1)S(1)}, u32[]{:S(2)}, u32[]{:S(2)}) collective-permute-start(bf16[72,1152]{1,0:T(8,128)(2,1)S(1)} %add_convert_fusion.2), channel_id=1, source_target_pairs={{0,16},{4,20},{8,24},{12,28},{16,0},{20,4},{24,8},{28,12},{1,17},{... | collective-permute-start | bytes 497672 | tf_op jit(solution)/shard_map/ppermute | solution.py:232
  58.4 10.9 %collective-permute-done.21 = bf16[72,1152]{1,0:T(8,128)(2,1)S(1)} collective-permute-done((bf16[72,1152]{1,0:T(8,128)(2,1)S(1)}, bf16[72,1152]{1,0:T(8,128)(2,1)S(1)}, u32[]{:S(2)}, u32[]{:S(2)}) %collective-permute-start.21) | collective-permute-done | bytes 165920 | tf_op jit(solution)/shard_map/ppermute | solution.py:232
  69.4 1.6 %collective-permute-start.22 = (bf16[72,1152]{1,0:T(8,128)(2,1)S(1)}, bf16[72,1152]{1,0:T(8,128)(2,1)S(1)}, u32[]{:S(2)}, u32[]{:S(2)}) collective-permute-start(bf16[72,1152]{1,0:T(8,128)(2,1)S(1)} %add_convert_fusion.1.h0), channel_id=1, source_target_pairs={{0,4},{4,0},{8,12},{12,8},{16,20},{20,16},{24,28},{28,24},{1,5},{5... | collective-permute-start | bytes 497672 | tf_op jit(solution)/shard_map/ppermute | solution.py:232
  71.0 2.0 %collective-permute-start.24 = (bf16[72,1152]{1,0:T(8,128)(2,1)S(1)}, bf16[72,1152]{1,0:T(8,128)(2,1)S(1)}, u32[]{:S(2)}, u32[]{:S(2)}) collective-permute-start(bf16[72,1152]{1,0:T(8,128)(2,1)S(1)} %add_convert_fusion.1.h0), channel_id=1, source_target_pairs={{0,12},{4,8},{8,4},{12,0},{16,28},{20,24},{24,20},{28,16},{1,13},{... | collective-permute-start | bytes 497672 | tf_op jit(solution)/shard_map/ppermute | solution.py:232
  73.0 1.6 %collective-permute-start.15 = (bf16[72,1152]{1,0:T(8,128)(2,1)S(1)}, bf16[72,1152]{1,0:T(8,128)(2,1)S(1)}, u32[]{:S(2)}, u32[]{:S(2)}) collective-permute-start(bf16[72,1152]{1,0:T(8,128)(2,1)S(1)} %add_convert_fusion.3.h0), channel_id=1, source_target_pairs={{0,4},{4,0},{8,12},{12,8},{16,20},{20,16},{24,28},{28,24},{1,5},{5... | collective-permute-start | bytes 497672 | tf_op jit(solution)/shard_map/ppermute | solution.py:232
  74.6 3.6 %collective-permute-done.22.h1 = bf16[72,1152]{1,0:T(8,128)(2,1)S(1)} collective-permute-done((bf16[72,1152]{1,0:T(8,128)(2,1)S(1)}, bf16[72,1152]{1,0:T(8,128)(2,1)S(1)}, u32[]{:S(2)}, u32[]{:S(2)}) %collective-permute-start.22) | collective-permute-done | bytes 165920 | tf_op jit(solution)/shard_map/ppermute | solution.py:232
  78.2 2.0 %shard_map.82 = f32[256,1152]{1,0:T(8,128)} custom-call(bf16[256,1152]{1,0:T(8,128)(2,1)S(1)} %get-tuple-element.67.back, bf16[1152,1152]{1,0:T(8,128)(2,1)S(1)} %copy-done.3), custom_call_target="tpu_custom_call" | custom-call | flops 679477248 | tf_op jit(solution)/shard_map/pallas_call | solution.py:220
  80.2 2.0 %shard_map.81 = f32[256,1152]{1,0:T(8,128)} custom-call(bf16[512,1152]{1,0:T(8,128)(2,1)S(1)} %get-tuple-element.68.back, bf16[1152,1152]{1,0:T(8,128)(2,1)S(1)} %copy-done.1), custom_call_target="tpu_custom_call" | custom-call | flops 679477248 | tf_op jit(solution)/shard_map/pallas_call | solution.py:220
  82.3 1.7 %shard_map.84 = f32[288,1152]{1,0:T(8,128)} custom-call(s32[2]{0:T(128)S(1)} %pad_add_fusion.place, bf16[72,1152]{1,0:T(8,128)(2,1)S(1)} %add_convert_fusion.1.h0, bf16[72,1152]{1,0:T(8,128)(2,1)S(1)} %collective-permute-done.22.h1, bf16[72,1152]{1,0:T(8,128)(2,1)S(1)} %collective-permute-done.23.h2, bf16[72,1152]{1,0:T(8,128)(2,1)S(1)} %collective-permute-done.24.h3), custom_call_target="tpu_custom_call" | custom-call | flops 2 | tf_op jit(solution)/shard_map/pallas_call | solution.py:220
  84.2 2.7 %collective-permute-done.17.h3 = bf16[72,1152]{1,0:T(8,128)(2,1)S(1)} collective-permute-done((bf16[72,1152]{1,0:T(8,128)(2,1)S(1)}, bf16[72,1152]{1,0:T(8,128)(2,1)S(1)}, u32[]{:S(2)}, u32[]{:S(2)}) %collective-permute-start.17) | collective-permute-done | bytes 165920 | tf_op jit(solution)/shard_map/ppermute | solution.py:232
  86.9 1.7 %shard_map.83 = f32[288,1152]{1,0:T(8,128)} custom-call(s32[2]{0:T(128)S(1)} %pad_add_fusion.place, bf16[72,1152]{1,0:T(8,128)(2,1)S(1)} %add_convert_fusion.3.h0, bf16[72,1152]{1,0:T(8,128)(2,1)S(1)} %collective-permute-done.15.h1, bf16[72,1152]{1,0:T(8,128)(2,1)S(1)} %collective-permute-done.16.h2, bf16[72,1152]{1,0:T(8,128)(2,1)S(1)} %collective-permute-done.17.h3), custom_call_target="tpu_custom_call" | custom-call | flops 2 | tf_op jit(solution)/shard_map/pallas_call | solution.py:220
  (49 shorter events, 4.9 us)
Async XLA Ops:
  0.7 3.5 %collective-permute-start.1 = (bf16[256,1152]{1,0:T(8,128)(2,1)}, bf16[256,1152]{1,0:T(8,128)(2,1)S(1)}, u32[]{:S(2)}, u32[]{:S(2)}) collective-permute-start(bf16[256,1152]{1,0:T(8,128)(2,1)} %t0), channel_id=1, source_target_pairs={{0,1},{1,0},{2,3},{3,2},{4,5},{5,4},{6,7},{7,6},{8,9},{9,8},{10,11... | collective-permute-start | bytes 1769480 | tf_op jit(solution)/shard_map/ppermute | solution.py:232
  1.2 3.0 %collective-permute-start.2 = (bf16[256,1152]{1,0:T(8,128)(2,1)}, bf16[256,1152]{1,0:T(8,128)(2,1)S(1)}, u32[]{:S(2)}, u32[]{:S(2)}) collective-permute-start(bf16[256,1152]{1,0:T(8,128)(2,1)} %i0), channel_id=1, source_target_pairs={{0,1},{1,0},{2,3},{3,2},{4,5},{5,4},{6,7},{7,6},{8,9},{9,8},{10,11... | collective-permute-start | bytes 1769480 | tf_op jit(solution)/shard_map/ppermute | solution.py:232
  1.2 17.3 %collective-permute-start = (bf16[256,1152]{1,0:T(8,128)(2,1)}, bf16[256,1152]{1,0:T(8,128)(2,1)S(1)}, u32[]{:S(2)}, u32[]{:S(2)}) collective-permute-start(bf16[256,1152]{1,0:T(8,128)(2,1)} %t0), channel_id=1, source_target_pairs={{0,2},{1,3},{2,0},{3,1},{4,6},{5,7},{6,4},{7,5},{8,10},{9,11},{10,... | collective-permute-start | bytes 1769480 | tf_op jit(solution)/shard_map/ppermute | solution.py:232
  4.2 26.4 %collective-permute-start.7 = (bf16[256,1152]{1,0:T(8,128)(2,1)}, bf16[256,1152]{1,0:T(8,128)(2,1)S(1)}, u32[]{:S(2)}, u32[]{:S(2)}) collective-permute-start(bf16[256,1152]{1,0:T(8,128)(2,1)} %i0), channel_id=1, source_target_pairs={{0,2},{1,3},{2,0},{3,1},{4,6},{5,7},{6,4},{7,5},{8,10},{9,11},{10,... | collective-permute-start | bytes 1769480 | tf_op jit(solution)/shard_map/ppermute | solution.py:232
  4.2 1.8 %copy-start = (bf16[1152,1152]{1,0:T(8,128)(2,1)S(1)}, bf16[1152,1152]{1,0:T(8,128)(2,1)}, u32[]{:S(2)}) copy-start(bf16[1152,1152]{1,0:T(8,128)(2,1)} %head.2) | copy-start | bytes 7962628
  6.0 1.7 %copy-start.2 = (bf16[1152,1152]{1,0:T(8,128)(2,1)S(1)}, bf16[1152,1152]{1,0:T(8,128)(2,1)}, u32[]{:S(2)}) copy-start(bf16[1152,1152]{1,0:T(8,128)(2,1)} %head.3) | copy-start | bytes 7962628
  7.7 1.1 %copy-start.4 = (bf16[256,1152]{1,0:T(8,128)(2,1)S(1)}, bf16[256,1152]{1,0:T(8,128)(2,1)}, u32[]{:S(2)}) copy-start(bf16[256,1152]{1,0:T(8,128)(2,1)} %t0) | copy-start | bytes 1769476
  8.8 1.1 %copy-start.5 = (bf16[256,1152]{1,0:T(8,128)(2,1)S(1)}, bf16[256,1152]{1,0:T(8,128)(2,1)}, u32[]{:S(2)}) copy-start(bf16[256,1152]{1,0:T(8,128)(2,1)} %i0) | copy-start | bytes 1769476
  9.8 10.9 %copy-start.3 = (bf16[1152,1152]{1,0:T(8,128)(2,1)S(1)}, bf16[1152,1152]{1,0:T(8,128)(2,1)}, u32[]{:S(2)}) copy-start(bf16[1152,1152]{1,0:T(8,128)(2,1)} %head.3) | copy-start | bytes 7962628
  18.6 1.4 %collective-permute-start.3 = (bf16[64,1152]{1,0:T(8,128)(2,1)S(1)}, bf16[64,1152]{1,0:T(8,128)(2,1)S(1)}, u32[]{:S(2)}, u32[]{:S(2)}) collective-permute-start(bf16[64,1152]{1,0:T(8,128)(2,1)S(1)} %get-tuple-element.85), channel_id=1, source_target_pairs={{0,1},{1,0},{2,3},{3,2},{4,5},{5,4},{6,7},{7,6},{8,9},{9,8},{10,11... | collective-permute-start | bytes 442376 | tf_op jit(solution)/shard_map/ppermute | solution.py:232
  18.6 1.6 %collective-permute-start.4 = (bf16[64,1152]{1,0:T(8,128)(2,1)S(1)}, bf16[64,1152]{1,0:T(8,128)(2,1)S(1)}, u32[]{:S(2)}, u32[]{:S(2)}) collective-permute-start(bf16[64,1152]{1,0:T(8,128)(2,1)S(1)} %get-tuple-element.84), channel_id=1, source_target_pairs={{0,1},{1,0},{2,3},{3,2},{4,5},{5,4},{6,7},{7,6},{8,9},{9,8},{10,11... | collective-permute-start | bytes 442376 | tf_op jit(solution)/shard_map/ppermute | solution.py:232
  19.1 1.4 %collective-permute-start.5 = (bf16[64,1152]{1,0:T(8,128)(2,1)S(1)}, bf16[64,1152]{1,0:T(8,128)(2,1)S(1)}, u32[]{:S(2)}, u32[]{:S(2)}) collective-permute-start(bf16[64,1152]{1,0:T(8,128)(2,1)S(1)} %get-tuple-element.83), channel_id=1, source_target_pairs={{0,1},{1,0},{2,3},{3,2},{4,5},{5,4},{6,7},{7,6},{8,9},{9,8},{10,11... | collective-permute-start | bytes 442376 | tf_op jit(solution)/shard_map/ppermute | solution.py:232
  19.2 1.5 %collective-permute-start.6 = (bf16[64,1152]{1,0:T(8,128)(2,1)S(1)}, bf16[64,1152]{1,0:T(8,128)(2,1)S(1)}, u32[]{:S(2)}, u32[]{:S(2)}) collective-permute-start(bf16[64,1152]{1,0:T(8,128)(2,1)S(1)} %get-tuple-element.82), channel_id=1, source_target_pairs={{0,1},{1,0},{2,3},{3,2},{4,5},{5,4},{6,7},{7,6},{8,9},{9,8},{10,11... | collective-permute-start | bytes 442376 | tf_op jit(solution)/shard_map/ppermute | solution.py:232
  26.3 8.4 %copy-start.1 = (bf16[1152,1152]{1,0:T(8,128)(2,1)S(1)}, bf16[1152,1152]{1,0:T(8,128)(2,1)}, u32[]{:S(2)}) copy-start(bf16[1152,1152]{1,0:T(8,128)(2,1)} %head.2) | copy-start | bytes 7962628
  30.6 15.3 %collective-permute-start.10 = (bf16[144,1152]{1,0:T(8,128)(2,1)S(1)}, bf16[144,1152]{1,0:T(8,128)(2,1)S(1)}, u32[]{:S(2)}, u32[]{:S(2)}) collective-permute-start(bf16[144,1152]{1,0:T(8,128)(2,1)S(1)} %get-tuple-element.70), channel_id=1, source_target_pairs={{0,4},{4,0},{8,12},{12,8},{16,20},{20,16},{24,28},{28,24},{1,5},{5... | collective-permute-start | bytes 995336 | tf_op jit(solution)/shard_map/ppermute | solution.py:232
  32.4 13.6 %collective-permute-start.11 = (bf16[144,1152]{1,0:T(8,128)(2,1)S(1)}, bf16[144,1152]{1,0:T(8,128)(2,1)S(1)}, u32[]{:S(2)}, u32[]{:S(2)}) collective-permute-start(bf16[144,1152]{1,0:T(8,128)(2,1)S(1)} %get-tuple-element.72), channel_id=1, source_target_pairs={{0,8},{4,12},{8,0},{12,4},{16,24},{20,28},{24,16},{28,20},{1,9},{5... | collective-permute-start | bytes 995336 | tf_op jit(solution)/shard_map/ppermute | solution.py:232
  33.9 15.8 %collective-permute-start.12 = (bf16[144,1152]{1,0:T(8,128)(2,1)S(1)}, bf16[144,1152]{1,0:T(8,128)(2,1)S(1)}, u32[]{:S(2)}, u32[]{:S(2)}) collective-permute-start(bf16[144,1152]{1,0:T(8,128)(2,1)S(1)} %get-tuple-element.74), channel_id=1, source_target_pairs={{0,12},{4,8},{8,4},{12,0},{16,28},{20,24},{24,20},{28,16},{1,13},{... | collective-permute-start | bytes 995336 | tf_op jit(solution)/shard_map/ppermute | solution.py:232
  34.1 2.7 %collective-permute-start.8 = (bf16[128,1152]{1,0:T(8,128)(2,1)S(1)}, bf16[128,1152]{1,0:T(8,128)(2,1)S(1)}, u32[]{:S(2)}, u32[]{:S(2)}) collective-permute-start(bf16[128,1152]{1,0:T(8,128)(2,1)S(1)} %get-tuple-element.81), channel_id=1, source_target_pairs={{0,1},{1,0},{2,3},{3,2},{4,5},{5,4},{6,7},{7,6},{8,9},{9,8},{10,11... | collective-permute-start | bytes 884744 | tf_op jit(solution)/shard_map/ppermute | solution.py:232
  34.2 2.7 %collective-permute-start.9 = (bf16[128,1152]{1,0:T(8,128)(2,1)S(1)}, bf16[128,1152]{1,0:T(8,128)(2,1)S(1)}, u32[]{:S(2)}, u32[]{:S(2)}) collective-permute-start(bf16[128,1152]{1,0:T(8,128)(2,1)S(1)} %get-tuple-element.80), channel_id=1, source_target_pairs={{0,1},{1,0},{2,3},{3,2},{4,5},{5,4},{6,7},{7,6},{8,9},{9,8},{10,11... | collective-permute-start | bytes 884744 | tf_op jit(solution)/shard_map/ppermute | solution.py:232
  42.4 10.9 %collective-permute-start.18 = (bf16[72,1152]{1,0:T(8,128)(2,1)S(1)}, bf16[72,1152]{1,0:T(8,128)(2,1)S(1)}, u32[]{:S(2)}, u32[]{:S(2)}) collective-permute-start(bf16[72,1152]{1,0:T(8,128)(2,1)S(1)} %get-tuple-element.77), channel_id=1, source_target_pairs={{0,4},{4,0},{8,12},{12,8},{16,20},{20,16},{24,28},{28,24},{1,5},{5... | collective-permute-start | bytes 497672 | tf_op jit(solution)/shard_map/ppermute | solution.py:232
  44.3 9.1 %collective-permute-start.19 = (bf16[72,1152]{1,0:T(8,128)(2,1)S(1)}, bf16[72,1152]{1,0:T(8,128)(2,1)S(1)}, u32[]{:S(2)}, u32[]{:S(2)}) collective-permute-start(bf16[72,1152]{1,0:T(8,128)(2,1)S(1)} %get-tuple-element.78), channel_id=1, source_target_pairs={{0,8},{4,12},{8,0},{12,4},{16,24},{20,28},{24,16},{28,20},{1,9},{5... | collective-permute-start | bytes 497672 | tf_op jit(solution)/shard_map/ppermute | solution.py:232
  45.8 9.4 %collective-permute-start.20 = (bf16[72,1152]{1,0:T(8,128)(2,1)S(1)}, bf16[72,1152]{1,0:T(8,128)(2,1)S(1)}, u32[]{:S(2)}, u32[]{:S(2)}) collective-permute-start(bf16[72,1152]{1,0:T(8,128)(2,1)S(1)} %get-tuple-element.79), channel_id=1, source_target_pairs={{0,12},{4,8},{8,4},{12,0},{16,28},{20,24},{24,20},{28,16},{1,13},{... | collective-permute-start | bytes 497672 | tf_op jit(solution)/shard_map/ppermute | solution.py:232
  50.0 8.0 %collective-permute-start.13 = (bf16[72,1152]{1,0:T(8,128)(2,1)S(1)}, bf16[72,1152]{1,0:T(8,128)(2,1)S(1)}, u32[]{:S(2)}, u32[]{:S(2)}) collective-permute-start(bf16[72,1152]{1,0:T(8,128)(2,1)S(1)} %slice.9), channel_id=1, source_target_pairs={{0,2},{1,3},{2,0},{3,1},{4,6},{5,7},{6,4},{7,5},{8,10},{9,11},{10,... | collective-permute-start | bytes 497672 | tf_op jit(solution)/shard_map/ppermute | solution.py:232
  55.3 14.0 %collective-permute-start.21 = (bf16[72,1152]{1,0:T(8,128)(2,1)S(1)}, bf16[72,1152]{1,0:T(8,128)(2,1)S(1)}, u32[]{:S(2)}, u32[]{:S(2)}) collective-permute-start(bf16[72,1152]{1,0:T(8,128)(2,1)S(1)} %add_convert_fusion.2), channel_id=1, source_target_pairs={{0,16},{4,20},{8,24},{12,28},{16,0},{20,4},{24,8},{28,12},{1,17},{... | collective-permute-start | bytes 497672 | tf_op jit(solution)/shard_map/ppermute | solution.py:232
  58.0 15.0 %collective-permute-start.14 = (bf16[72,1152]{1,0:T(8,128)(2,1)S(1)}, bf16[72,1152]{1,0:T(8,128)(2,1)S(1)}, u32[]{:S(2)}, u32[]{:S(2)}) collective-permute-start(bf16[72,1152]{1,0:T(8,128)(2,1)S(1)} %add_convert_fusion.4), channel_id=1, source_target_pairs={{0,16},{4,20},{8,24},{12,28},{16,0},{20,4},{24,8},{28,12},{1,17},{... | collective-permute-start | bytes 497672 | tf_op jit(solution)/shard_map/ppermute | solution.py:232
  69.4 8.7 %collective-permute-start.22 = (bf16[72,1152]{1,0:T(8,128)(2,1)S(1)}, bf16[72,1152]{1,0:T(8,128)(2,1)S(1)}, u32[]{:S(2)}, u32[]{:S(2)}) collective-permute-start(bf16[72,1152]{1,0:T(8,128)(2,1)S(1)} %add_convert_fusion.1.h0), channel_id=1, source_target_pairs={{0,4},{4,0},{8,12},{12,8},{16,20},{20,16},{24,28},{28,24},{1,5},{5... | collective-permute-start | bytes 497672 | tf_op jit(solution)/shard_map/ppermute | solution.py:232
  71.0 11.3 %collective-permute-start.23 = (bf16[72,1152]{1,0:T(8,128)(2,1)S(1)}, bf16[72,1152]{1,0:T(8,128)(2,1)S(1)}, u32[]{:S(2)}, u32[]{:S(2)}) collective-permute-start(bf16[72,1152]{1,0:T(8,128)(2,1)S(1)} %add_convert_fusion.1.h0), channel_id=1, source_target_pairs={{0,8},{4,12},{8,0},{12,4},{16,24},{20,28},{24,16},{28,20},{1,9},{5... | collective-permute-start | bytes 497672 | tf_op jit(solution)/shard_map/ppermute | solution.py:232
  71.0 11.3 %collective-permute-start.24 = (bf16[72,1152]{1,0:T(8,128)(2,1)S(1)}, bf16[72,1152]{1,0:T(8,128)(2,1)S(1)}, u32[]{:S(2)}, u32[]{:S(2)}) collective-permute-start(bf16[72,1152]{1,0:T(8,128)(2,1)S(1)} %add_convert_fusion.1.h0), channel_id=1, source_target_pairs={{0,12},{4,8},{8,4},{12,0},{16,28},{20,24},{24,20},{28,16},{1,13},{... | collective-permute-start | bytes 497672 | tf_op jit(solution)/shard_map/ppermute | solution.py:232
  73.0 10.9 %collective-permute-start.15 = (bf16[72,1152]{1,0:T(8,128)(2,1)S(1)}, bf16[72,1152]{1,0:T(8,128)(2,1)S(1)}, u32[]{:S(2)}, u32[]{:S(2)}) collective-permute-start(bf16[72,1152]{1,0:T(8,128)(2,1)S(1)} %add_convert_fusion.3.h0), channel_id=1, source_target_pairs={{0,4},{4,0},{8,12},{12,8},{16,20},{20,16},{24,28},{28,24},{1,5},{5... | collective-permute-start | bytes 497672 | tf_op jit(solution)/shard_map/ppermute | solution.py:232
  74.6 9.6 %collective-permute-start.16 = (bf16[72,1152]{1,0:T(8,128)(2,1)S(1)}, bf16[72,1152]{1,0:T(8,128)(2,1)S(1)}, u32[]{:S(2)}, u32[]{:S(2)}) collective-permute-start(bf16[72,1152]{1,0:T(8,128)(2,1)S(1)} %add_convert_fusion.3.h0), channel_id=1, source_target_pairs={{0,8},{4,12},{8,0},{12,4},{16,24},{20,28},{24,16},{28,20},{1,9},{5... | collective-permute-start | bytes 497672 | tf_op jit(solution)/shard_map/ppermute | solution.py:232
  78.2 8.8 %collective-permute-start.17 = (bf16[72,1152]{1,0:T(8,128)(2,1)S(1)}, bf16[72,1152]{1,0:T(8,128)(2,1)S(1)}, u32[]{:S(2)}, u32[]{:S(2)}) collective-permute-start(bf16[72,1152]{1,0:T(8,128)(2,1)S(1)} %add_convert_fusion.3.h0), channel_id=1, source_target_pairs={{0,12},{4,8},{8,4},{12,0},{16,28},{20,24},{24,20},{28,16},{1,13},{... | collective-permute-start | bytes 497672 | tf_op jit(solution)/shard_map/ppermute | solution.py:232

commit v5 on v4

--- a/solution.py
+++ b/solution.py
@@ -151,13 +151,11 @@
     pick_i[:, half:] = dot_nt(pick, i1[...]).astype(BF16)
 
 
-def image_kernel(
-    t2, t3, t4, t5, t6, text_head, y_a, p_a, x_a, w_aa, pick_i,
-    q_b, y_b, w_ab, dp_a, h0, h1, h2, h3, dots, gx,
-):
+def image_kernel(t2, *refs):
+    *far, text_head, y_a, p_a, x_a, w_aa, pick_i, q_b, y_b, w_ab, dp_a, h0, h1, h2, h3, dots, gx = refs
     half = t2.shape[0]
     q_b[:half, :] = dot_nn(t2[...], text_head[...])
-    q_b[half:, :] = dot_nn(jnp.concatenate([t3[...], t4[...], t5[...], t6[...]], axis=0), text_head[...])
+    q_b[half:, :] = dot_nn(jnp.concatenate([t[...] for t in far], axis=0), text_head[...])
     unit_rows(q_b, y_b)
     dots[...] = dot_nt(x_a[...], y_b[...])
     weight_rows(dots, w_ab)
@@ -166,13 +164,14 @@
     split_head(dot_nn(pick_i[...], dp_a[...]), (h0, h1, h2, h3))
 
 
-def pull_kernel(place, t2, t3, t4, t5, t6, x_a, w_aa, w_ab, gy_a, gy_b, pick_t):
+def pull_kernel(place, t2, *refs):
+    *far, x_a, w_aa, w_ab, gy_a, gy_b, pick_t = refs
     half = t2.shape[0]
     gy_a[...] = dot_tn(w_aa[...], x_a[...])
     gy_b[...] = dot_tn(w_ab[...], x_a[...])
     pick = picker(place, pick_t.shape[0], t2.shape[1], (0,))
     pick_t[:, :half] = dot_nt(pick, t2[...]).astype(BF16)
-    far = jnp.concatenate([t3[...], t4[...], t5[...], t6[...]], axis=0)
+    far = jnp.concatenate([t[...] for t in far], axis=0)
     pick_t[:, half:] = dot_nt(pick, far).astype(BF16)
 
 
@@ -211,7 +210,7 @@
         out[pl.ds(first, part), :] = piece[...].astype(F32)
 
 
-def call(kernel, outs, scratch, args, mib, place=None, macs=1, keep=True):
+def call(kernel, outs, scratch, args, mib, place=None, macs=0, keep=True):
     args = [pltpu.with_memory_space_constraint(a, pltpu.VMEM) for a in args]
     specs = [pl.BlockSpec(memory_space=pltpu.VMEM)] * len(args)
     if place is not None:
@@ -248,14 +247,15 @@
     def add(own, others):
         return sum((other.astype(F32) for other in others), own.astype(F32)).astype(BF16)
 
-    def finish(total):
-        total = add(total, [cuts(total, mask=QUAD)])
-        pieces = [total] + [cuts(total, mask=k) for k in range(1, QUAD)]
+    def spread(total):
+        return [total] + [cuts(total, mask=k) for k in range(1, QUAD)]
+
+    def placed(pieces):
         outs = [((rows_out, width), F32)]
         return call(place_kernel, outs, [], pieces, 4, place, keep=False)[0]
 
     t2 = loop(text_features, mask=2)
-    i2 = loop(image_features, mask=2)
+    i2 = [loop(rows, mask=2) for rows in jnp.split(image_features, 2)]
     place = jnp.stack([lax.axis_index("loop"), lax.axis_index("cuts") & (QUAD - 1)])
     place = place.astype(jnp.int32)
     t0, i0, place = lax.optimization_barrier((text_features, image_features, place))
@@ -275,7 +275,7 @@
         place,
     )
     t2 = after(t2, w_aa)
-    t3 = [loop(rows, mask=1) for rows in jnp.split(t2, 4)]
+    t3 = [loop(rows, mask=1) for rows in jnp.split(t2, 8)]
     q_b, y_b, w_ab, dp_a, *image_parts = call(
         image_kernel,
         [wide, wide_b, square, wide_b] + [((2 * part, width), BF16)] * QUAD,
@@ -292,10 +292,10 @@
         8,
         place,
     )
-    i2 = after(i2, gy_a)
-    i3 = [loop(rows, mask=1) for rows in jnp.split(i2, 2)]
+    i2 = [after(rows, gy_a) for rows in i2]
+    i3 = [loop(rows, mask=1) for rows in i2]
     blocks = []
-    for block, i in enumerate(([i2], i3)):
+    for block, i in enumerate((i2, i3)):
         blocks += call(
             functools.partial(block_kernel, block),
             [tall_b, block_w, block_w],
@@ -310,12 +310,16 @@
         (*blocks, q_a, q_b, gy_a, gy_b, pick_a, pick_b),
         14,
     )
-    text_sum = add(text_parts[0], [cuts(text_parts[k], mask=k) for k in range(1, QUAD)])
+    text_others = [cuts(text_parts[k], mask=k) for k in range(1, QUAD)]
     image_others = [after(other, dq_own) for other in image_others]
     image_sum = add(image_parts[0], image_others)
     image_sum = add(image_sum[:part], [loop(image_sum[part:], mask=2)])
-    image_out = finish(image_sum)
-    text_out = finish(text_sum)
+    image_sum = add(image_sum, [cuts(image_sum, mask=QUAD)])
+    image_pieces = spread(image_sum)
+    text_sum = add(text_parts[0], [after(other, image_sum) for other in text_others])
+    text_sum = add(text_sum, [after(cuts(text_sum, mask=QUAD), image_pieces[-1])])
+    image_out = placed(image_pieces)
+    text_out = placed(spread(text_sum))
     grads = [
         call(grad_kernel, [tall], [], (back, head), 4, macs=macs, keep=False)[0]
         for back, head in ((after(dp_a, dq_own), image_head), (dq_own, text_head))

time: 88.9 us -> 89.6 us (level)
  starting transfers between devices: 21.6 us -> 27.5 us
  waiting for transfers between devices: 30.3 us -> 26.3 us
  local copies, waits for them, and re-layouts: 5.74 us -> 4.67 us
    ppermute x25 -> x30, starting transfers between devices: 21.6 us -> 27.5 us  [swap(): return lax.ppermute(array, axis, [(i, i ^ mask) for i in range(size)])]
    ppermute x25 -> x30, waiting for transfers between devices: 30.3 us -> 26.3 us  [swap(): return lax.ppermute(array, axis, [(i, i ^ mask) for i in range(size)])]
    unnamed x12, local copies, waits for them, and re-layouts: 5.63 us -> 3.51 us
    split x2, local copies, waits for them, and re-layouts: 0.09 us -> 1.14 us  [the longest x1 1.1 us: per_device(): i2 = [loop(rows, mask=2) for rows in jnp.split(image_features, 2)]]
  transfers between devices with their start and end apart: 25 -> 30, of which waited for: 13 -> 12; matrix products, arithmetic and copies ran while one was open for 1% -> 1% of each run, Pallas kernels for 32% -> 31%
where the time goes in v5:
time: 89.6 us; the launch traced here: 89.4 us
  Pallas kernels  29.6 us (33%)
  starting transfers between devices  27.5 us (31%)
  waiting for transfers between devices  26.3 us (29%)
  local copies, waits for them, and re-layouts  4.67 us (5%)
    pallas_call x10, Pallas kernels, call(): pl.pallas_call(kernel, out_shape=[shape(s, t) for s, t in outs], in_specs...  29.6 us
    ppermute x30, starting transfers between devices, swap(): return lax.ppermute(array, axis, [(i, i ^ mask) for i in range(size)])  27.5 us
    ppermute x30, waiting for transfers between devices, swap(): return lax.ppermute(array, axis, [(i, i ^ mask) for i in range(size)])  26.3 us
    unnamed x12, local copies, waits for them, and re-layouts  3.51 us
  transfers between devices with their start and end apart: 30, of which 12 were waited for; matrix products, arithmetic and copies ran while one was open for 1% of the time, Pallas kernels for 31%

profile of v5, /device:TPU:0, one launch (start us, length us, event | category | flops | bytes accessed | tf_op | source)
XLA Modules:
  0.0 89.4 jit_solution(13622573838479492930)
XLA Ops:
  1.3 2.9 %collective-permute-start = (bf16[256,1152]{1,0:T(8,128)(2,1)}, bf16[256,1152]{1,0:T(8,128)(2,1)S(1)}, u32[]{:S(2)}, u32[]{:S(2)}) collective-permute-start(bf16[256,1152]{1,0:T(8,128)(2,1)} %t0), channel_id=1, source_target_pairs={{0,2},{1,3},{2,0},{3,1},{4,6},{5,7},{6,4},{7,5},{8,10},{9,11},{10,... | collective-permute-start | bytes 1769480 | tf_op jit(solution)/shard_map/ppermute | solution.py:231
  4.2 1.1 %fusion = (bf16[128,1152]{1,0:T(8,128)(2,1)S(1)}, bf16[128,1152]{1,0:T(8,128)(2,1)S(1)}) fusion(bf16[256,1152]{1,0:T(8,128)(2,1)} %i0), kind=kLoop, calls=%fused_computation.6 | loop fusion | bytes 1179648 | tf_op jit(solution)/shard_map/split | solution.py:258
  5.4 2.0 %collective-permute-start.11 = (bf16[128,1152]{1,0:T(8,128)(2,1)S(1)}, bf16[128,1152]{1,0:T(8,128)(2,1)S(1)}, u32[]{:S(2)}, u32[]{:S(2)}) collective-permute-start(bf16[128,1152]{1,0:T(8,128)(2,1)S(1)} %get-tuple-element.91), channel_id=1, source_target_pairs={{0,2},{1,3},{2,0},{3,1},{4,6},{5,7},{6,4},{7,5},{8,10},{9,11},{10,... | collective-permute-start | bytes 884744 | tf_op jit(solution)/shard_map/ppermute | solution.py:231
  7.4 1.7 %copy-done = bf16[1152,1152]{1,0:T(8,128)(2,1)S(1)} copy-done((bf16[1152,1152]{1,0:T(8,128)(2,1)S(1)}, bf16[1152,1152]{1,0:T(8,128)(2,1)}, u32[]{:S(2)}) %copy-start) | copy-done | bytes 2654232
  9.2 1.7 %copy-done.2 = bf16[1152,1152]{1,0:T(8,128)(2,1)S(1)} copy-done((bf16[1152,1152]{1,0:T(8,128)(2,1)S(1)}, bf16[1152,1152]{1,0:T(8,128)(2,1)}, u32[]{:S(2)}) %copy-start.2) | copy-done | bytes 2654232
  10.9 6.4 %shard_map.75 = (f32[512,1152]{1,0:T(8,128)S(1)}, bf16[512,1152]{1,0:T(8,128)(2,1)S(1)}, f32[512,1152]{1,0:T(8,128)S(1)}, bf16[512,1152]{1,0:T(8,128)(2,1)S(1)},...) custom-call(s32[2]{0:T(128)S(1)} %pad_add_fusion.place, ...), custom_call_target="tpu_custom_call" | custom-call | tf_op jit(solution)/shard_map/pallas_call | solution.py:219
  17.3 1.2 %collective-permute-done.t2 = bf16[256,1152]{1,0:T(8,128)(2,1)S(1)} collective-permute-done((bf16[256,1152]{1,0:T(8,128)(2,1)}, bf16[256,1152]{1,0:T(8,128)(2,1)S(1)}, u32[]{:S(2)}, u32[]{:S(2)}) %collective-permute-start) | collective-permute-done | bytes 589856 | tf_op jit(solution)/shard_map/ppermute | solution.py:231
  22.6 5.6 %shard_map.76 = (f32[512,1152]{1,0:T(8,128)S(1)}, bf16[512,1152]{1,0:T(8,128)(2,1)S(1)}, bf16[512,512]{1,0:T(8,128)(2,1)S(1)}, bf16[512,1152]{1,0:T(8,128)(2,1)S...) custom-call(bf16[256,1152]{1,0:T(8,128)(2,1)S(1)} %collective-permut, ...), custom_call_target="tpu_custom_call" | custom-call | tf_op jit(solution)/shard_map/pallas_call | solution.py:219
  28.2 2.2 %collective-permute-start.15 = (bf16[144,1152]{1,0:T(8,128)(2,1)S(1)}, bf16[144,1152]{1,0:T(8,128)(2,1)S(1)}, u32[]{:S(2)}, u32[]{:S(2)}) collective-permute-start(bf16[144,1152]{1,0:T(8,128)(2,1)S(1)} %get-tuple-element.76), channel_id=1, source_target_pairs={{0,4},{4,0},{8,12},{12,8},{16,20},{20,16},{24,28},{28,24},{1,5},{5... | collective-permute-start | bytes 995336 | tf_op jit(solution)/shard_map/ppermute | solution.py:231
  30.4 1.6 %collective-permute-start.16 = (bf16[144,1152]{1,0:T(8,128)(2,1)S(1)}, bf16[144,1152]{1,0:T(8,128)(2,1)S(1)}, u32[]{:S(2)}, u32[]{:S(2)}) collective-permute-start(bf16[144,1152]{1,0:T(8,128)(2,1)S(1)} %get-tuple-element.78), channel_id=1, source_target_pairs={{0,8},{4,12},{8,0},{12,4},{16,24},{20,28},{24,16},{28,20},{1,9},{5... | collective-permute-start | bytes 995336 | tf_op jit(solution)/shard_map/ppermute | solution.py:231
  31.9 2.5 %shard_map.77 = (f32[512,1152]{1,0:T(8,128)S(1)}, f32[512,1152]{1,0:T(8,128)S(1)}, bf16[288,512]{1,0:T(8,128)(2,1)S(1)}) custom-call(s32[2]{0:T(128)S(1)} %pad_add_fusion.place, bf16[256,1152]{1,0:T(8,128)(2,1)S(1)} %collective-permute-done.t2, bf16[32,1152]{1,0:T(8,128)(2,1)S(1)} %collective-permute-done.3.refs_0_, ...), custom_call_target="tpu_custom_call" | custom-call | tf_op jit(solution)/shard_map/pallas_call | solution.py:219
  35.0 2.1 %shard_map.78 = (bf16[256,1152]{1,0:T(8,128)(2,1)S(1)}, bf16[256,512]{1,0:T(8,128)(2,1)S(1)}, bf16[256,512]{1,0:T(8,128)(2,1)S(1)}) custom-call(bf16[128,1152]{1,0:T(8,128)(2,1)S(1)} %collective-permute-done.11.refs_0_, bf16[128,1152]{1,0:T(8,128)(2,1)S(1)} %collective-permute-done.12.refs_1_, bf16[1152,1152]{1,0:T(8,128)(2,1)S(1)} %copy-done.1, ...), custom_call_target="tpu_custom_call" | custom-call | tf_op jit(solution)/shard_map/pallas_call | solution.py:219
  37.2 1.9 %shard_map.79 = (bf16[256,1152]{1,0:T(8,128)(2,1)S(1)}, bf16[256,512]{1,0:T(8,128)(2,1)S(1)}, bf16[256,512]{1,0:T(8,128)(2,1)S(1)}) custom-call(bf16[128,1152]{1,0:T(8,128)(2,1)S(1)} %collective-permute-done.13.refs_0_, bf16[128,1152]{1,0:T(8,128)(2,1)S(1)} %collective-permute-done.14.refs_1_, bf16[1152,1152]{1,0:T(8,128)(2,1)S(1)} %copy-done.1, ...), custom_call_target="tpu_custom_call" | custom-call | tf_op jit(solution)/shard_map/pallas_call | solution.py:219
  39.1 3.6 %shard_map.80 = (bf16[72,1152]{1,0:T(8,128)(2,1)S(1)}, bf16[72,1152]{1,0:T(8,128)(2,1)S(1)}, bf16[72,1152]{1,0:T(8,128)(2,1)S(1)}, bf16[72,1152]{1,0:T(8,128)(2,1)S(1)}, bf16[256,1152]{1,0:T(8,128)(2,1)S(1)}) custom-call(bf16[256,1152]{1,0:T(8,128)(2,1)S(1)} %get-tuple-element.62.x_2, bf16[256,512]{1,0:T(8,128)(2,1)S(1)} %get-tuple-element.63.w_2a, ...), custom_call_target="tpu_custom_call" | custom-call | tf_op jit(solution)/shard_map/pallas_call | solution.py:219
  42.7 4.3 %collective-permute-done.17 = bf16[144,1152]{1,0:T(8,128)(2,1)S(1)} collective-permute-done((bf16[144,1152]{1,0:T(8,128)(2,1)S(1)}, bf16[144,1152]{1,0:T(8,128)(2,1)S(1)}, u32[]{:S(2)}, u32[]{:S(2)}) %collective-permute-start.17) | collective-permute-done | bytes 331808 | tf_op jit(solution)/shard_map/ppermute | solution.py:231
  47.3 1.7 %collective-permute-start.18 = (bf16[72,1152]{1,0:T(8,128)(2,1)S(1)}, bf16[72,1152]{1,0:T(8,128)(2,1)S(1)}, u32[]{:S(2)}, u32[]{:S(2)}) collective-permute-start(bf16[72,1152]{1,0:T(8,128)(2,1)S(1)} %slice.9), channel_id=1, source_target_pairs={{0,2},{1,3},{2,0},{3,1},{4,6},{5,7},{6,4},{7,5},{8,10},{9,11},{10,... | collective-permute-start | bytes 497672 | tf_op jit(solution)/shard_map/ppermute | solution.py:231
  49.0 4.1 %collective-permute-done.18 = bf16[72,1152]{1,0:T(8,128)(2,1)S(1)} collective-permute-done((bf16[72,1152]{1,0:T(8,128)(2,1)S(1)}, bf16[72,1152]{1,0:T(8,128)(2,1)S(1)}, u32[]{:S(2)}, u32[]{:S(2)}) %collective-permute-start.18) | collective-permute-done | bytes 165920 | tf_op jit(solution)/shard_map/ppermute | solution.py:231
  53.1 2.5 %collective-permute-start.19 = (bf16[72,1152]{1,0:T(8,128)(2,1)S(1)}, bf16[72,1152]{1,0:T(8,128)(2,1)S(1)}, u32[]{:S(2)}, u32[]{:S(2)}) collective-permute-start(bf16[72,1152]{1,0:T(8,128)(2,1)S(1)} %add_convert_fusion.4), channel_id=1, source_target_pairs={{0,16},{4,20},{8,24},{12,28},{16,0},{20,4},{24,8},{28,12},{1,17},{... | collective-permute-start | bytes 497672 | tf_op jit(solution)/shard_map/ppermute | solution.py:231
  55.5 1.5 %collective-permute-start.23 = (bf16[72,1152]{1,0:T(8,128)(2,1)S(1)}, bf16[72,1152]{1,0:T(8,128)(2,1)S(1)}, u32[]{:S(2)}, u32[]{:S(2)}) collective-permute-start(bf16[72,1152]{1,0:T(8,128)(2,1)S(1)} %get-tuple-element.83), channel_id=1, source_target_pairs={{0,4},{4,0},{8,12},{12,8},{16,20},{20,16},{24,28},{28,24},{1,5},{5... | collective-permute-start | bytes 497672 | tf_op jit(solution)/shard_map/ppermute | solution.py:231
  57.1 1.6 %collective-permute-start.24 = (bf16[72,1152]{1,0:T(8,128)(2,1)S(1)}, bf16[72,1152]{1,0:T(8,128)(2,1)S(1)}, u32[]{:S(2)}, u32[]{:S(2)}) collective-permute-start(bf16[72,1152]{1,0:T(8,128)(2,1)S(1)} %get-tuple-element.85), channel_id=1, source_target_pairs={{0,8},{4,12},{8,0},{12,4},{16,24},{20,28},{24,16},{28,20},{1,9},{5... | collective-permute-start | bytes 497672 | tf_op jit(solution)/shard_map/ppermute | solution.py:231
  59.0 3.4 %collective-permute-done.19 = bf16[72,1152]{1,0:T(8,128)(2,1)S(1)} collective-permute-done((bf16[72,1152]{1,0:T(8,128)(2,1)S(1)}, bf16[72,1152]{1,0:T(8,128)(2,1)S(1)}, u32[]{:S(2)}, u32[]{:S(2)}) %collective-permute-start.19) | collective-permute-done | bytes 165920 | tf_op jit(solution)/shard_map/ppermute | solution.py:231
  62.5 2.8 %collective-permute-done.24 = bf16[72,1152]{1,0:T(8,128)(2,1)S(1)} collective-permute-done((bf16[72,1152]{1,0:T(8,128)(2,1)S(1)}, bf16[72,1152]{1,0:T(8,128)(2,1)S(1)}, u32[]{:S(2)}, u32[]{:S(2)}) %collective-permute-start.24) | collective-permute-done | bytes 165920 | tf_op jit(solution)/shard_map/ppermute | solution.py:231
  65.3 1.3 %collective-permute-done.25 = bf16[72,1152]{1,0:T(8,128)(2,1)S(1)} collective-permute-done((bf16[72,1152]{1,0:T(8,128)(2,1)S(1)}, bf16[72,1152]{1,0:T(8,128)(2,1)S(1)}, u32[]{:S(2)}, u32[]{:S(2)}) %collective-permute-start.25) | collective-permute-done | bytes 165920 | tf_op jit(solution)/shard_map/ppermute | solution.py:231
  66.7 1.2 %collective-permute-start.26 = (bf16[72,1152]{1,0:T(8,128)(2,1)S(1)}, bf16[72,1152]{1,0:T(8,128)(2,1)S(1)}, u32[]{:S(2)}, u32[]{:S(2)}) collective-permute-start(bf16[72,1152]{1,0:T(8,128)(2,1)S(1)} %add_convert_fusion.2), channel_id=1, source_target_pairs={{0,16},{4,20},{8,24},{12,28},{16,0},{20,4},{24,8},{28,12},{1,17},{... | collective-permute-start | bytes 497672 | tf_op jit(solution)/shard_map/ppermute | solution.py:231
  67.9 2.9 %collective-permute-start.22 = (bf16[72,1152]{1,0:T(8,128)(2,1)S(1)}, bf16[72,1152]{1,0:T(8,128)(2,1)S(1)}, u32[]{:S(2)}, u32[]{:S(2)}) collective-permute-start(bf16[72,1152]{1,0:T(8,128)(2,1)S(1)} %add_convert_fusion.3.h0), channel_id=1, source_target_pairs={{0,12},{4,8},{8,4},{12,0},{16,28},{20,24},{24,20},{28,16},{1,13},{... | collective-permute-start | bytes 497672 | tf_op jit(solution)/shard_map/ppermute | solution.py:231
  71.4 3.9 %collective-permute-done.26 = bf16[72,1152]{1,0:T(8,128)(2,1)S(1)} collective-permute-done((bf16[72,1152]{1,0:T(8,128)(2,1)S(1)}, bf16[72,1152]{1,0:T(8,128)(2,1)S(1)}, u32[]{:S(2)}, u32[]{:S(2)}) %collective-permute-start.26) | collective-permute-done | bytes 165920 | tf_op jit(solution)/shard_map/ppermute | solution.py:231
  75.3 3.1 %collective-permute-done.22.h3 = bf16[72,1152]{1,0:T(8,128)(2,1)S(1)} collective-permute-done((bf16[72,1152]{1,0:T(8,128)(2,1)S(1)}, bf16[72,1152]{1,0:T(8,128)(2,1)S(1)}, u32[]{:S(2)}, u32[]{:S(2)}) %collective-permute-start.22) | collective-permute-done | bytes 165920 | tf_op jit(solution)/shard_map/ppermute | solution.py:231
  79.7 2.2 %collective-permute-start.29 = (bf16[72,1152]{1,0:T(8,128)(2,1)S(1)}, bf16[72,1152]{1,0:T(8,128)(2,1)S(1)}, u32[]{:S(2)}, u32[]{:S(2)}) collective-permute-start(bf16[72,1152]{1,0:T(8,128)(2,1)S(1)} %add_convert_fusion.1.h0), channel_id=1, source_target_pairs={{0,12},{4,8},{8,4},{12,0},{16,28},{20,24},{24,20},{28,16},{1,13},{... | collective-permute-start | bytes 497672 | tf_op jit(solution)/shard_map/ppermute | solution.py:231
  81.9 2.0 %shard_map.82 = f32[256,1152]{1,0:T(8,128)} custom-call(bf16[256,1152]{1,0:T(8,128)(2,1)S(1)} %get-tuple-element.73.back, bf16[1152,1152]{1,0:T(8,128)(2,1)S(1)} %copy-done.3), custom_call_target="tpu_custom_call" | custom-call | flops 679477248 | tf_op jit(solution)/shard_map/pallas_call | solution.py:219
  84.0 2.0 %shard_map.81 = f32[256,1152]{1,0:T(8,128)} custom-call(bf16[512,1152]{1,0:T(8,128)(2,1)S(1)} %get-tuple-element.74.back, bf16[1152,1152]{1,0:T(8,128)(2,1)S(1)} %copy-done.1), custom_call_target="tpu_custom_call" | custom-call | flops 679477248 | tf_op jit(solution)/shard_map/pallas_call | solution.py:219
  86.0 1.7 %shard_map.83 = f32[288,1152]{1,0:T(8,128)} custom-call(s32[2]{0:T(128)S(1)} %pad_add_fusion.place, bf16[72,1152]{1,0:T(8,128)(2,1)S(1)} %add_convert_fusion.3.h0, bf16[72,1152]{1,0:T(8,128)(2,1)S(1)} %collective-permute-done.20.h1, bf16[72,1152]{1,0:T(8,128)(2,1)S(1)} %collective-permute-done.21.h2, bf16[72,1152]{1,0:T(8,128)(2,1)S(1)} %collective-permute-done.22.h3), custom_call_target="tpu_custom_call" | custom-call | tf_op jit(solution)/shard_map/pallas_call | solution.py:219
  87.7 1.7 %shard_map.84 = f32[288,1152]{1,0:T(8,128)} custom-call(s32[2]{0:T(128)S(1)} %pad_add_fusion.place, bf16[72,1152]{1,0:T(8,128)(2,1)S(1)} %add_convert_fusion.1.h0, bf16[72,1152]{1,0:T(8,128)(2,1)S(1)} %collective-permute-done.27.h1, bf16[72,1152]{1,0:T(8,128)(2,1)S(1)} %collective-permute-done.28.h2, bf16[72,1152]{1,0:T(8,128)(2,1)S(1)} %collective-permute-done.29.h3), custom_call_target="tpu_custom_call" | custom-call | tf_op jit(solution)/shard_map/pallas_call | solution.py:219
  (59 shorter events, 8.1 us)
Async XLA Ops:
  0.6 6.8 %copy-start.4 = (bf16[256,1152]{1,0:T(8,128)(2,1)S(1)}, bf16[256,1152]{1,0:T(8,128)(2,1)}, u32[]{:S(2)}) copy-start(bf16[256,1152]{1,0:T(8,128)(2,1)} %i0) | copy-start | bytes 1769476
  0.7 6.6 %collective-permute-start.1 = (bf16[256,1152]{1,0:T(8,128)(2,1)}, bf16[256,1152]{1,0:T(8,128)(2,1)S(1)}, u32[]{:S(2)}, u32[]{:S(2)}) collective-permute-start(bf16[256,1152]{1,0:T(8,128)(2,1)} %t0), channel_id=1, source_target_pairs={{0,1},{1,0},{2,3},{3,2},{4,5},{5,4},{6,7},{7,6},{8,9},{9,8},{10,11... | collective-permute-start | bytes 1769480 | tf_op jit(solution)/shard_map/ppermute | solution.py:231
  1.2 6.2 %collective-permute-start.2 = (bf16[256,1152]{1,0:T(8,128)(2,1)}, bf16[256,1152]{1,0:T(8,128)(2,1)S(1)}, u32[]{:S(2)}, u32[]{:S(2)}) collective-permute-start(bf16[256,1152]{1,0:T(8,128)(2,1)} %i0), channel_id=1, source_target_pairs={{0,1},{1,0},{2,3},{3,2},{4,5},{5,4},{6,7},{7,6},{8,9},{9,8},{10,11... | collective-permute-start | bytes 1769480 | tf_op jit(solution)/shard_map/ppermute | solution.py:231
  1.3 17.3 %collective-permute-start = (bf16[256,1152]{1,0:T(8,128)(2,1)}, bf16[256,1152]{1,0:T(8,128)(2,1)S(1)}, u32[]{:S(2)}, u32[]{:S(2)}) collective-permute-start(bf16[256,1152]{1,0:T(8,128)(2,1)} %t0), channel_id=1, source_target_pairs={{0,2},{1,3},{2,0},{3,1},{4,6},{5,7},{6,4},{7,5},{8,10},{9,11},{10,... | collective-permute-start | bytes 1769480 | tf_op jit(solution)/shard_map/ppermute | solution.py:231
  5.3 29.1 %collective-permute-start.12 = (bf16[128,1152]{1,0:T(8,128)(2,1)S(1)}, bf16[128,1152]{1,0:T(8,128)(2,1)S(1)}, u32[]{:S(2)}, u32[]{:S(2)}) collective-permute-start(bf16[128,1152]{1,0:T(8,128)(2,1)S(1)} %get-tuple-element.90), channel_id=1, source_target_pairs={{0,2},{1,3},{2,0},{3,1},{4,6},{5,7},{6,4},{7,5},{8,10},{9,11},{10,... | collective-permute-start | bytes 884744 | tf_op jit(solution)/shard_map/ppermute | solution.py:231
  5.4 29.1 %collective-permute-start.11 = (bf16[128,1152]{1,0:T(8,128)(2,1)S(1)}, bf16[128,1152]{1,0:T(8,128)(2,1)S(1)}, u32[]{:S(2)}, u32[]{:S(2)}) collective-permute-start(bf16[128,1152]{1,0:T(8,128)(2,1)S(1)} %get-tuple-element.91), channel_id=1, source_target_pairs={{0,2},{1,3},{2,0},{3,1},{4,6},{5,7},{6,4},{7,5},{8,10},{9,11},{10,... | collective-permute-start | bytes 884744 | tf_op jit(solution)/shard_map/ppermute | solution.py:231
  10.9 11.7 %copy-start.3 = (bf16[1152,1152]{1,0:T(8,128)(2,1)S(1)}, bf16[1152,1152]{1,0:T(8,128)(2,1)}, u32[]{:S(2)}) copy-start(bf16[1152,1152]{1,0:T(8,128)(2,1)} %head.3) | copy-start | bytes 7962628
  18.6 1.3 %collective-permute-start.10 = (bf16[32,1152]{1,0:T(8,128)(2,1)S(1)}, bf16[32,1152]{1,0:T(8,128)(2,1)S(1)}, u32[]{:S(2)}, u32[]{:S(2)}) collective-permute-start(bf16[32,1152]{1,0:T(8,128)(2,1)S(1)} %get-tuple-element.92), channel_id=1, source_target_pairs={{0,1},{1,0},{2,3},{3,2},{4,5},{5,4},{6,7},{7,6},{8,9},{9,8},{10,11... | collective-permute-start | bytes 221192 | tf_op jit(solution)/shard_map/ppermute | solution.py:231
  18.7 1.4 %collective-permute-start.3 = (bf16[32,1152]{1,0:T(8,128)(2,1)S(1)}, bf16[32,1152]{1,0:T(8,128)(2,1)S(1)}, u32[]{:S(2)}, u32[]{:S(2)}) collective-permute-start(bf16[32,1152]{1,0:T(8,128)(2,1)S(1)} %get-tuple-element.99), channel_id=1, source_target_pairs={{0,1},{1,0},{2,3},{3,2},{4,5},{5,4},{6,7},{7,6},{8,9},{9,8},{10,11... | collective-permute-start | bytes 221192 | tf_op jit(solution)/shard_map/ppermute | solution.py:231
  19.2 1.3 %collective-permute-start.4 = (bf16[32,1152]{1,0:T(8,128)(2,1)S(1)}, bf16[32,1152]{1,0:T(8,128)(2,1)S(1)}, u32[]{:S(2)}, u32[]{:S(2)}) collective-permute-start(bf16[32,1152]{1,0:T(8,128)(2,1)S(1)} %get-tuple-element.98), channel_id=1, source_target_pairs={{0,1},{1,0},{2,3},{3,2},{4,5},{5,4},{6,7},{7,6},{8,9},{9,8},{10,11... | collective-permute-start | bytes 221192 | tf_op jit(solution)/shard_map/ppermute | solution.py:231
  19.9 1.3 %collective-permute-start.5 = (bf16[32,1152]{1,0:T(8,128)(2,1)S(1)}, bf16[32,1152]{1,0:T(8,128)(2,1)S(1)}, u32[]{:S(2)}, u32[]{:S(2)}) collective-permute-start(bf16[32,1152]{1,0:T(8,128)(2,1)S(1)} %get-tuple-element.97), channel_id=1, source_target_pairs={{0,1},{1,0},{2,3},{3,2},{4,5},{5,4},{6,7},{7,6},{8,9},{9,8},{10,11... | collective-permute-start | bytes 221192 | tf_op jit(solution)/shard_map/ppermute | solution.py:231
  20.1 1.3 %collective-permute-start.6 = (bf16[32,1152]{1,0:T(8,128)(2,1)S(1)}, bf16[32,1152]{1,0:T(8,128)(2,1)S(1)}, u32[]{:S(2)}, u32[]{:S(2)}) collective-permute-start(bf16[32,1152]{1,0:T(8,128)(2,1)S(1)} %get-tuple-element.96), channel_id=1, source_target_pairs={{0,1},{1,0},{2,3},{3,2},{4,5},{5,4},{6,7},{7,6},{8,9},{9,8},{10,11... | collective-permute-start | bytes 221192 | tf_op jit(solution)/shard_map/ppermute | solution.py:231
  20.4 1.3 %collective-permute-start.7 = (bf16[32,1152]{1,0:T(8,128)(2,1)S(1)}, bf16[32,1152]{1,0:T(8,128)(2,1)S(1)}, u32[]{:S(2)}, u32[]{:S(2)}) collective-permute-start(bf16[32,1152]{1,0:T(8,128)(2,1)S(1)} %get-tuple-element.95), channel_id=1, source_target_pairs={{0,1},{1,0},{2,3},{3,2},{4,5},{5,4},{6,7},{7,6},{8,9},{9,8},{10,11... | collective-permute-start | bytes 221192 | tf_op jit(solution)/shard_map/ppermute | solution.py:231
  21.2 1.3 %collective-permute-start.8 = (bf16[32,1152]{1,0:T(8,128)(2,1)S(1)}, bf16[32,1152]{1,0:T(8,128)(2,1)S(1)}, u32[]{:S(2)}, u32[]{:S(2)}) collective-permute-start(bf16[32,1152]{1,0:T(8,128)(2,1)S(1)} %get-tuple-element.94), channel_id=1, source_target_pairs={{0,1},{1,0},{2,3},{3,2},{4,5},{5,4},{6,7},{7,6},{8,9},{9,8},{10,11... | collective-permute-start | bytes 221192 | tf_op jit(solution)/shard_map/ppermute | solution.py:231
  21.3 1.3 %collective-permute-start.9 = (bf16[32,1152]{1,0:T(8,128)(2,1)S(1)}, bf16[32,1152]{1,0:T(8,128)(2,1)S(1)}, u32[]{:S(2)}, u32[]{:S(2)}) collective-permute-start(bf16[32,1152]{1,0:T(8,128)(2,1)S(1)} %get-tuple-element.93), channel_id=1, source_target_pairs={{0,1},{1,0},{2,3},{3,2},{4,5},{5,4},{6,7},{7,6},{8,9},{9,8},{10,11... | collective-permute-start | bytes 221192 | tf_op jit(solution)/shard_map/ppermute | solution.py:231
  28.2 14.5 %collective-permute-start.15 = (bf16[144,1152]{1,0:T(8,128)(2,1)S(1)}, bf16[144,1152]{1,0:T(8,128)(2,1)S(1)}, u32[]{:S(2)}, u32[]{:S(2)}) collective-permute-start(bf16[144,1152]{1,0:T(8,128)(2,1)S(1)} %get-tuple-element.76), channel_id=1, source_target_pairs={{0,4},{4,0},{8,12},{12,8},{16,20},{20,16},{24,28},{28,24},{1,5},{5... | collective-permute-start | bytes 995336 | tf_op jit(solution)/shard_map/ppermute | solution.py:231
  30.4 12.4 %collective-permute-start.16 = (bf16[144,1152]{1,0:T(8,128)(2,1)S(1)}, bf16[144,1152]{1,0:T(8,128)(2,1)S(1)}, u32[]{:S(2)}, u32[]{:S(2)}) collective-permute-start(bf16[144,1152]{1,0:T(8,128)(2,1)S(1)} %get-tuple-element.78), channel_id=1, source_target_pairs={{0,8},{4,12},{8,0},{12,4},{16,24},{20,28},{24,16},{28,20},{1,9},{5... | collective-permute-start | bytes 995336 | tf_op jit(solution)/shard_map/ppermute | solution.py:231
  31.9 15.1 %collective-permute-start.17 = (bf16[144,1152]{1,0:T(8,128)(2,1)S(1)}, bf16[144,1152]{1,0:T(8,128)(2,1)S(1)}, u32[]{:S(2)}, u32[]{:S(2)}) collective-permute-start(bf16[144,1152]{1,0:T(8,128)(2,1)S(1)} %get-tuple-element.80), channel_id=1, source_target_pairs={{0,12},{4,8},{8,4},{12,0},{16,28},{20,24},{24,20},{28,16},{1,13},{... | collective-permute-start | bytes 995336 | tf_op jit(solution)/shard_map/ppermute | solution.py:231
  34.4 2.7 %collective-permute-start.14 = (bf16[128,1152]{1,0:T(8,128)(2,1)S(1)}, bf16[128,1152]{1,0:T(8,128)(2,1)S(1)}, u32[]{:S(2)}, u32[]{:S(2)}) collective-permute-start(bf16[128,1152]{1,0:T(8,128)(2,1)S(1)} %collective-permute-done.12.refs_1_), channel_id=1, source_target_pairs={{0,1},{1,0},{2,3},{3,2},{4,5},{5,4},{6,7},{7,6},{8,9},{9,8},{10,11... | collective-permute-start | bytes 884744 | tf_op jit(solution)/shard_map/ppermute | solution.py:231
  34.5 2.6 %collective-permute-start.13 = (bf16[128,1152]{1,0:T(8,128)(2,1)S(1)}, bf16[128,1152]{1,0:T(8,128)(2,1)S(1)}, u32[]{:S(2)}, u32[]{:S(2)}) collective-permute-start(bf16[128,1152]{1,0:T(8,128)(2,1)S(1)} %collective-permute-done.11.refs_0_), channel_id=1, source_target_pairs={{0,1},{1,0},{2,3},{3,2},{4,5},{5,4},{6,7},{7,6},{8,9},{9,8},{10,11... | collective-permute-start | bytes 884744 | tf_op jit(solution)/shard_map/ppermute | solution.py:231
  47.3 5.8 %collective-permute-start.18 = (bf16[72,1152]{1,0:T(8,128)(2,1)S(1)}, bf16[72,1152]{1,0:T(8,128)(2,1)S(1)}, u32[]{:S(2)}, u32[]{:S(2)}) collective-permute-start(bf16[72,1152]{1,0:T(8,128)(2,1)S(1)} %slice.9), channel_id=1, source_target_pairs={{0,2},{1,3},{2,0},{3,1},{4,6},{5,7},{6,4},{7,5},{8,10},{9,11},{10,... | collective-permute-start | bytes 497672 | tf_op jit(solution)/shard_map/ppermute | solution.py:231
  53.1 9.4 %collective-permute-start.19 = (bf16[72,1152]{1,0:T(8,128)(2,1)S(1)}, bf16[72,1152]{1,0:T(8,128)(2,1)S(1)}, u32[]{:S(2)}, u32[]{:S(2)}) collective-permute-start(bf16[72,1152]{1,0:T(8,128)(2,1)S(1)} %add_convert_fusion.4), channel_id=1, source_target_pairs={{0,16},{4,20},{8,24},{12,28},{16,0},{20,4},{24,8},{28,12},{1,17},{... | collective-permute-start | bytes 497672 | tf_op jit(solution)/shard_map/ppermute | solution.py:231
  55.5 7.0 %collective-permute-start.23 = (bf16[72,1152]{1,0:T(8,128)(2,1)S(1)}, bf16[72,1152]{1,0:T(8,128)(2,1)S(1)}, u32[]{:S(2)}, u32[]{:S(2)}) collective-permute-start(bf16[72,1152]{1,0:T(8,128)(2,1)S(1)} %get-tuple-element.83), channel_id=1, source_target_pairs={{0,4},{4,0},{8,12},{12,8},{16,20},{20,16},{24,28},{28,24},{1,5},{5... | collective-permute-start | bytes 497672 | tf_op jit(solution)/shard_map/ppermute | solution.py:231
  57.1 8.3 %collective-permute-start.24 = (bf16[72,1152]{1,0:T(8,128)(2,1)S(1)}, bf16[72,1152]{1,0:T(8,128)(2,1)S(1)}, u32[]{:S(2)}, u32[]{:S(2)}) collective-permute-start(bf16[72,1152]{1,0:T(8,128)(2,1)S(1)} %get-tuple-element.85), channel_id=1, source_target_pairs={{0,8},{4,12},{8,0},{12,4},{16,24},{20,28},{24,16},{28,20},{1,9},{5... | collective-permute-start | bytes 497672 | tf_op jit(solution)/shard_map/ppermute | solution.py:231
  58.6 8.0 %collective-permute-start.25 = (bf16[72,1152]{1,0:T(8,128)(2,1)S(1)}, bf16[72,1152]{1,0:T(8,128)(2,1)S(1)}, u32[]{:S(2)}, u32[]{:S(2)}) collective-permute-start(bf16[72,1152]{1,0:T(8,128)(2,1)S(1)} %get-tuple-element.87), channel_id=1, source_target_pairs={{0,12},{4,8},{8,4},{12,0},{16,28},{20,24},{24,20},{28,16},{1,13},{... | collective-permute-start | bytes 497672 | tf_op jit(solution)/shard_map/ppermute | solution.py:231
  66.7 8.5 %collective-permute-start.26 = (bf16[72,1152]{1,0:T(8,128)(2,1)S(1)}, bf16[72,1152]{1,0:T(8,128)(2,1)S(1)}, u32[]{:S(2)}, u32[]{:S(2)}) collective-permute-start(bf16[72,1152]{1,0:T(8,128)(2,1)S(1)} %add_convert_fusion.2), channel_id=1, source_target_pairs={{0,16},{4,20},{8,24},{12,28},{16,0},{20,4},{24,8},{28,12},{1,17},{... | collective-permute-start | bytes 497672 | tf_op jit(solution)/shard_map/ppermute | solution.py:231
  67.9 10.4 %collective-permute-start.22 = (bf16[72,1152]{1,0:T(8,128)(2,1)S(1)}, bf16[72,1152]{1,0:T(8,128)(2,1)S(1)}, u32[]{:S(2)}, u32[]{:S(2)}) collective-permute-start(bf16[72,1152]{1,0:T(8,128)(2,1)S(1)} %add_convert_fusion.3.h0), channel_id=1, source_target_pairs={{0,12},{4,8},{8,4},{12,0},{16,28},{20,24},{24,20},{28,16},{1,13},{... | collective-permute-start | bytes 497672 | tf_op jit(solution)/shard_map/ppermute | solution.py:231
  70.8 15.3 %collective-permute-start.20 = (bf16[72,1152]{1,0:T(8,128)(2,1)S(1)}, bf16[72,1152]{1,0:T(8,128)(2,1)S(1)}, u32[]{:S(2)}, u32[]{:S(2)}) collective-permute-start(bf16[72,1152]{1,0:T(8,128)(2,1)S(1)} %add_convert_fusion.3.h0), channel_id=1, source_target_pairs={{0,4},{4,0},{8,12},{12,8},{16,20},{20,16},{24,28},{28,24},{1,5},{5... | collective-permute-start | bytes 497672 | tf_op jit(solution)/shard_map/ppermute | solution.py:231
  71.3 14.7 %collective-permute-start.21 = (bf16[72,1152]{1,0:T(8,128)(2,1)S(1)}, bf16[72,1152]{1,0:T(8,128)(2,1)S(1)}, u32[]{:S(2)}, u32[]{:S(2)}) collective-permute-start(bf16[72,1152]{1,0:T(8,128)(2,1)S(1)} %add_convert_fusion.3.h0), channel_id=1, source_target_pairs={{0,8},{4,12},{8,0},{12,4},{16,24},{20,28},{24,16},{28,20},{1,9},{5... | collective-permute-start | bytes 497672 | tf_op jit(solution)/shard_map/ppermute | solution.py:231
  78.4 9.4 %collective-permute-start.27 = (bf16[72,1152]{1,0:T(8,128)(2,1)S(1)}, bf16[72,1152]{1,0:T(8,128)(2,1)S(1)}, u32[]{:S(2)}, u32[]{:S(2)}) collective-permute-start(bf16[72,1152]{1,0:T(8,128)(2,1)S(1)} %add_convert_fusion.1.h0), channel_id=1, source_target_pairs={{0,4},{4,0},{8,12},{12,8},{16,20},{20,16},{24,28},{28,24},{1,5},{5... | collective-permute-start | bytes 497672 | tf_op jit(solution)/shard_map/ppermute | solution.py:231
  78.9 8.8 %collective-permute-start.28 = (bf16[72,1152]{1,0:T(8,128)(2,1)S(1)}, bf16[72,1152]{1,0:T(8,128)(2,1)S(1)}, u32[]{:S(2)}, u32[]{:S(2)}) collective-permute-start(bf16[72,1152]{1,0:T(8,128)(2,1)S(1)} %add_convert_fusion.1.h0), channel_id=1, source_target_pairs={{0,8},{4,12},{8,0},{12,4},{16,24},{20,28},{24,16},{28,20},{1,9},{5... | collective-permute-start | bytes 497672 | tf_op jit(solution)/shard_map/ppermute | solution.py:231
  79.7 8.0 %collective-permute-start.29 = (bf16[72,1152]{1,0:T(8,128)(2,1)S(1)}, bf16[72,1152]{1,0:T(8,128)(2,1)S(1)}, u32[]{:S(2)}, u32[]{:S(2)}) collective-permute-start(bf16[72,1152]{1,0:T(8,128)(2,1)S(1)} %add_convert_fusion.1.h0), channel_id=1, source_target_pairs={{0,12},{4,8},{8,4},{12,0},{16,28},{20,24},{24,20},{28,16},{1,13},{... | collective-permute-start | bytes 497672 | tf_op jit(solution)/shard_map/ppermute | solution.py:231
  (4 other events, 13.3 us)

commit v6 on v5

--- a/solution.py
+++ b/solution.py
@@ -83,13 +83,13 @@
         vectors_ref[first : first + STRIP, :] = (p * factor_of(p)).astype(BF16)
 
 
-def back_rows(projected_ref, gradient_ref, back_ref):
+def back_rows(projected_ref, gradient_ref, back_ref, at=0):
     for first in range(0, projected_ref.shape[0], STRIP):
         p = projected_ref[first : first + STRIP, :]
-        g = gradient_ref[first : first + STRIP, :]
+        g = gradient_ref[at + first : at + first + STRIP, :]
         factor = factor_of(p)
         along = factor * factor * factor * jnp.sum(p * g, axis=-1, keepdims=True)
-        back_ref[first : first + STRIP, :] = (factor * g - along * p).astype(BF16)
+        back_ref[at + first : at + first + STRIP, :] = (factor * g - along * p).astype(BF16)
 
 
 def weights_of(dots, pairs_from=None):
@@ -131,12 +131,25 @@
 
 
 def near_kernel(
-    place, t0, t1, i0, i1, text_head, image_head, q_a, y_a, p_a, x_a, w_aa, pick_i, pick_t, dots
+    place, t1, i1, t0_far, i0_far, text_head_far, image_head_far,
+    q_a, y_a, p_a, x_a, w_aa, gy_a, pick_i, pick_t, dots, t0, i0, text_head, image_head, sems,
 ):
     half = t0.shape[0]
+    copies = [
+        pltpu.make_async_copy(source, target, sems.at[n])
+        for n, (source, target) in enumerate(
+            ((t0_far, t0), (text_head_far, text_head), (i0_far, i0), (image_head_far, image_head))
+        )
+    ]
+    for copy in copies:
+        copy.start()
+    copies[0].wait()
+    copies[1].wait()
     q_a[:half, :] = dot_nn(t0[...], text_head[...])
     q_a[half:, :] = dot_nn(t1[...], text_head[...])
     unit_rows(q_a, y_a)
+    copies[2].wait()
+    copies[3].wait()
     p_a[:half, :] = dot_nn(i0[...], image_head[...])
     p_a[half:, :] = dot_nn(i1[...], image_head[...])
     unit_rows(p_a, x_a)
@@ -149,52 +162,65 @@
     pick = picker(place, rows, t0.shape[1], (0, 2))
     pick_i[:, :half] = dot_nt(pick, i0[...]).astype(BF16)
     pick_i[:, half:] = dot_nt(pick, i1[...]).astype(BF16)
-
-
-def image_kernel(t2, *refs):
-    *far, text_head, y_a, p_a, x_a, w_aa, pick_i, q_b, y_b, w_ab, dp_a, h0, h1, h2, h3, dots, gx = refs
-    half = t2.shape[0]
-    q_b[:half, :] = dot_nn(t2[...], text_head[...])
-    q_b[half:, :] = dot_nn(jnp.concatenate([t[...] for t in far], axis=0), text_head[...])
-    unit_rows(q_b, y_b)
-    dots[...] = dot_nt(x_a[...], y_b[...])
-    weight_rows(dots, w_ab)
-    gx[...] = dot_nn(w_aa[...], y_a[...]) + dot_nn(w_ab[...], y_b[...])
+    gy_a[...] = dot_tn(w_aa[...], x_a[...])
+
+
+def text_kernel(t2, text_head, y_a, x_a, w_aa, q_2, y_2, w_a2, gx, dots):
+    q_2[...] = dot_nn(t2[...], text_head[...])
+    unit_rows(q_2, y_2)
+    dots[...] = dot_nt(x_a[...], y_2[...])
+    weight_rows(dots, w_a2)
+    gx[...] = dot_nn(w_aa[...], y_a[...]) + dot_nn(w_a2[...], y_2[...])
+
+
+def image_kernel(*refs):
+    *features, text_head, p_a, x_a, gx_in, pick_i, q_3, y_3, w_a3, dp_a, h0, h1, h2, h3, dots, gx = refs
+    t3 = jnp.concatenate([t[...] for t in features], axis=0)
+    q_3[...] = dot_nn(t3, text_head[...])
+    unit_rows(q_3, y_3)
+    dots[...] = dot_nt(x_a[...], y_3[...])
+    weight_rows(dots, w_a3)
+    gx[...] = gx_in[...] + dot_nn(w_a3[...], y_3[...])
     back_rows(p_a, gx, dp_a)
     split_head(dot_nn(pick_i[...], dp_a[...]), (h0, h1, h2, h3))
 
 
 def pull_kernel(place, t2, *refs):
-    *far, x_a, w_aa, w_ab, gy_a, gy_b, pick_t = refs
+    *features, x_a, w_a2, w_a3, gy_2, gy_3, pick_t = refs
     half = t2.shape[0]
-    gy_a[...] = dot_tn(w_aa[...], x_a[...])
-    gy_b[...] = dot_tn(w_ab[...], x_a[...])
+    gy_2[...] = dot_tn(w_a2[...], x_a[...])
+    gy_3[...] = dot_tn(w_a3[...], x_a[...])
     pick = picker(place, pick_t.shape[0], t2.shape[1], (0,))
     pick_t[:, :half] = dot_nt(pick, t2[...]).astype(BF16)
-    far = jnp.concatenate([t[...] for t in far], axis=0)
-    pick_t[:, half:] = dot_nt(pick, far).astype(BF16)
+    t3 = jnp.concatenate([t[...] for t in features], axis=0)
+    pick_t[:, half:] = dot_nt(pick, t3).astype(BF16)
 
 
 def block_kernel(block, *refs):
-    *features, image_head, y_a, y_b, x_b, w_ba, w_bb, p_b, d_a, d_b = refs
+    *features, image_head, y_a, y_2, y_3, x_b, w_ba, w_bb, p_b, d_a, d_b = refs
+    half = x_b.shape[0]
     features = jnp.concatenate([i[...] for i in features], axis=0)
     p_b[...] = dot_nn(features, image_head[...])
     unit_rows(p_b, x_b)
     d_a[...] = dot_nt(x_b[...], y_a[...])
-    d_b[...] = dot_nt(x_b[...], y_b[...])
+    d_b[:, :half] = dot_nt(x_b[...], y_2[...])
+    d_b[:, half:] = dot_nt(x_b[...], y_3[...])
     weight_rows(d_a, w_ba)
-    weight_rows(d_b, w_bb, block * x_b.shape[0])
+    weight_rows(d_b, w_bb, block * half)
 
 
 def last_kernel(
-    x_2, w_2a, w_2b, x_3, w_3a, w_3b, q_a, q_b, gy_a_in, gy_b_in, pick_a, pick_b,
+    x_2, w_2a, w_2b, x_3, w_3a, w_3b, q_a, q_2, q_3, gy_a_in, gy_2, gy_3, pick_a, pick_b,
     h0, h1, h2, h3, dq_own, gy_a, gy_b, dq_a, dq_b,
 ):
     half = x_2.shape[0]
     gy_a[...] = gy_a_in[...] + dot_tn(w_2a[...], x_2[...]) + dot_tn(w_3a[...], x_3[...])
-    gy_b[...] = gy_b_in[...] + dot_tn(w_2b[...], x_2[...]) + dot_tn(w_3b[...], x_3[...])
     back_rows(q_a, gy_a, dq_a)
-    back_rows(q_b, gy_b, dq_b)
+    gy_b[...] = dot_tn(w_2b[...], x_2[...]) + dot_tn(w_3b[...], x_3[...])
+    gy_b[:half, :] += gy_2[...]
+    gy_b[half:, :] += gy_3[...]
+    back_rows(q_2, gy_b, dq_b, 0)
+    back_rows(q_3, gy_b, dq_b, half)
     dq_own[...] = dq_a[:half, :]
     split_head(dot_nn(pick_a[...], dq_a[...]) + dot_nn(pick_b[...], dq_b[...]), (h0, h1, h2, h3))
 
@@ -210,9 +236,10 @@
         out[pl.ds(first, part), :] = piece[...].astype(F32)
 
 
-def call(kernel, outs, scratch, args, mib, place=None, macs=0, keep=True):
-    args = [pltpu.with_memory_space_constraint(a, pltpu.VMEM) for a in args]
-    specs = [pl.BlockSpec(memory_space=pltpu.VMEM)] * len(args)
+def call(kernel, outs, scratch, args, mib, place=None, macs=0, keep=True, far=()):
+    args = [pltpu.with_memory_space_constraint(a, pltpu.VMEM) for a in args] + list(far)
+    specs = [pl.BlockSpec(memory_space=pltpu.VMEM)] * (len(args) - len(far))
+    specs += [pl.BlockSpec(memory_space=pl.ANY)] * len(far)
     if place is not None:
         args, specs = [place, *args], [pl.BlockSpec(memory_space=pltpu.SMEM), *specs]
     shape = pltpu.VMEM if keep else jax.ShapeDtypeStruct
@@ -221,7 +248,8 @@
         out_shape=[shape(s, t) for s, t in outs],
         in_specs=specs,
         out_specs=[pl.BlockSpec(memory_space=pltpu.VMEM)] * len(outs),
-        scratch_shapes=[pltpu.VMEM(s, t) for s, t in scratch],
+        scratch_shapes=[pltpu.VMEM(s, t) for s, t in scratch]
+        + [pltpu.SemaphoreType.DMA((len(far),))] * bool(far),
         compiler_params=pltpu.CompilerParams(vmem_limit_bytes=mib * 1024 * 1024),
         cost_estimate=pl.CostEstimate(flops=2 * macs, bytes_accessed=0, transcendentals=0),
     )(*args)
@@ -263,36 +291,46 @@
     i1 = loop(i0, mask=1)
     wide, wide_b = ((near, width), F32), ((near, width), BF16)
     tall, tall_b = ((half, width), F32), ((half, width), BF16)
-    square, dots = ((near, near), BF16), ((near, near), F32)
+    head_b = ((width, width), BF16)
     block_w, block_dots = ((half, near), BF16), ((half, near), F32)
+    side_w, side_dots = ((near, half), BF16), ((near, half), F32)
     pick_one, pick_two = ((rows_out, near), BF16), ((2 * rows_out, near), BF16)
-    q_a, y_a, p_a, x_a, w_aa, pick_i, pick_a = call(
+    q_a, y_a, p_a, x_a, w_aa, gy_a, pick_i, pick_a = call(
         near_kernel,
-        [wide, wide_b, wide, wide_b, square, pick_two, pick_one],
-        [dots],
-        (t0, t1, i0, i1, text_head, image_head),
+        [wide, wide_b, wide, wide_b, ((near, near), BF16), wide, pick_two, pick_one],
+        [((near, near), F32), tall_b, tall_b, head_b, head_b],
+        (t1, i1),
+        16,
+        place,
+        far=(t0, i0, text_head, image_head),
+    )
+    t2 = after(t2, w_aa)
+    t3 = [loop(rows, mask=1) for rows in jnp.split(t2, 8)]
+    q_2, y_2, w_a2, gx = call(
+        text_kernel,
+        [tall, tall_b, side_w, wide],
+        [side_dots],
+        (t2, text_head, y_a, x_a, w_aa),
+        8,
+    )
+    t3 = [after(rows, gx) for rows in t3]
+    q_3, y_3, w_a3, dp_a, *image_parts = call(
+        image_kernel,
+        [tall, tall_b, side_w, wide_b] + [((2 * part, width), BF16)] * QUAD,
+        [side_dots, wide],
+        (*t3, text_head, p_a, x_a, gx, pick_i),
+        8,
+    )
+    image_others = [cuts(image_parts[k], mask=k) for k in range(1, QUAD)]
+    gy_2, gy_3, pick_b = call(
+        pull_kernel,
+        [tall, tall, pick_one],
+        [],
+        (t2, *t3, x_a, w_a2, w_a3),
         8,
         place,
     )
-    t2 = after(t2, w_aa)
-    t3 = [loop(rows, mask=1) for rows in jnp.split(t2, 8)]
-    q_b, y_b, w_ab, dp_a, *image_parts = call(
-        image_kernel,
-        [wide, wide_b, square, wide_b] + [((2 * part, width), BF16)] * QUAD,
-        [dots, wide],
-        (t2, *t3, text_head, y_a, p_a, x_a, w_aa, pick_i),
-        8,
-    )
-    image_others = [cuts(image_parts[k], mask=k) for k in range(1, QUAD)]
-    gy_a, gy_b, pick_b = call(
-        pull_kernel,
-        [wide, wide, pick_one],
-        [],
-        (t2, *t3, x_a, w_aa, w_ab),
-        8,
-        place,
-    )
-    i2 = [after(rows, gy_a) for rows in i2]
+    i2 = [after(rows, gy_2) for rows in i2]
     i3 = [loop(rows, mask=1) for rows in i2]
     blocks = []
     for block, i in enumerate((i2, i3)):
@@ -300,30 +338,31 @@
             functools.partial(block_kernel, block),
             [tall_b, block_w, block_w],
             [tall, block_dots, block_dots],
-            (*i, image_head, y_a, y_b),
+            (*i, image_head, y_a, y_2, y_3),
             8,
         )
     *text_parts, dq_own = call(
         last_kernel,
         [((part, width), BF16)] * QUAD + [tall_b],
         [wide, wide, wide_b, wide_b],
-        (*blocks, q_a, q_b, gy_a, gy_b, pick_a, pick_b),
+        (*blocks, q_a, q_2, q_3, gy_a, gy_2, gy_3, pick_a, pick_b),
         14,
     )
     text_others = [cuts(text_parts[k], mask=k) for k in range(1, QUAD)]
     image_others = [after(other, dq_own) for other in image_others]
     image_sum = add(image_parts[0], image_others)
-    image_sum = add(image_sum[:part], [loop(image_sum[part:], mask=2)])
+    grads = [
+        call(grad_kernel, [tall], [], (after(back, image_sum), head), 4, macs=2 * macs, keep=False)[0]
+        for back, head in ((dp_a, image_head), (dq_own, text_head))
+    ]
+    image_sum = add(image_sum[:part], [after(loop(image_sum[part:], mask=2), grads)])
+    text_sum = add(text_parts[0], [after(other, image_sum) for other in text_others])
     image_sum = add(image_sum, [cuts(image_sum, mask=QUAD)])
     image_pieces = spread(image_sum)
-    text_sum = add(text_parts[0], [after(other, image_sum) for other in text_others])
+    text_sum = after(text_sum, image_sum)
     text_sum = add(text_sum, [after(cuts(text_sum, mask=QUAD), image_pieces[-1])])
     image_out = placed(image_pieces)
     text_out = placed(spread(text_sum))
-    grads = [
-        call(grad_kernel, [tall], [], (back, head), 4, macs=macs, keep=False)[0]
-        for back, head in ((after(dp_a, dq_own), image_head), (dq_own, text_head))
-    ]
     return (*grads, image_out, text_out)
 
 

time: 89.6 us -> 85.9 us (0.959)
  waiting for transfers between devices: 26.3 us -> 19.2 us
  Pallas kernels: 29.6 us -> 31.9 us
  starting transfers between devices: 27.5 us -> 28.6 us
    ppermute x30, waiting for transfers between devices: 26.3 us -> 19.2 us  [swap(): return lax.ppermute(array, axis, [(i, i ^ mask) for i in range(size)])]
    pallas_call x10 -> x11, Pallas kernels: 29.6 us -> 31.9 us  [call(): pl.pallas_call(kernel, out_shape=[shape(s, t) for s, t in outs], in_specs...]
    ppermute x30, starting transfers between devices: 27.5 us -> 28.6 us  [swap(): return lax.ppermute(array, axis, [(i, i ^ mask) for i in range(size)])]
  transfers between devices with their start and end apart: 30 -> 30, of which waited for: 12 -> 8; matrix products, arithmetic and copies ran while one was open for 1% -> 2% of each run, Pallas kernels for 31% -> 35%
where the time goes in v6:
time: 85.9 us; the launch traced here: 85.7 us
  Pallas kernels  31.9 us (37%)
  starting transfers between devices  28.6 us (33%)
  waiting for transfers between devices  19.2 us (22%)
  local copies, waits for them, and re-layouts  4.67 us (5%)
  between operations  0.89 us (1%)
    pallas_call x11, Pallas kernels, call(): pl.pallas_call(kernel, out_shape=[shape(s, t) for s, t in outs], in_specs...  31.9 us
    ppermute x30, starting transfers between devices, swap(): return lax.ppermute(array, axis, [(i, i ^ mask) for i in range(size)])  28.6 us
    ppermute x30, waiting for transfers between devices, swap(): return lax.ppermute(array, axis, [(i, i ^ mask) for i in range(size)])  19.2 us
    unnamed x12, local copies, waits for them, and re-layouts  3.51 us
  transfers between devices with their start and end apart: 30, of which 8 were waited for; matrix products, arithmetic and copies ran while one was open for 2% of the time, Pallas kernels for 35%

profile of v6, /device:TPU:0, one launch (start us, length us, event | category | flops | bytes accessed | tf_op | source)
XLA Modules:
  0.0 85.7 jit_solution(6518919985534552053)
XLA Ops:
  1.3 2.9 %collective-permute-start = (bf16[256,1152]{1,0:T(8,128)(2,1)}, bf16[256,1152]{1,0:T(8,128)(2,1)S(1)}, u32[]{:S(2)}, u32[]{:S(2)}) collective-permute-start(bf16[256,1152]{1,0:T(8,128)(2,1)} %t0_far), channel_id=1, source_target_pairs={{0,2},{1,3},{2,0},{3,1},{4,6},{5,7},{6,4},{7,5},{8,10},{9,11},{10,... | collective-permute-start | bytes 1769480 | tf_op jit(solution)/shard_map/ppermute | solution.py:259
  4.2 1.1 %fusion = (bf16[128,1152]{1,0:T(8,128)(2,1)S(1)}, bf16[128,1152]{1,0:T(8,128)(2,1)S(1)}) fusion(bf16[256,1152]{1,0:T(8,128)(2,1)} %i0_far), kind=kLoop, calls=%fused_computation.6 | loop fusion | bytes 1179648 | tf_op jit(solution)/shard_map/split | solution.py:286
  5.4 2.0 %collective-permute-start.12 = (bf16[128,1152]{1,0:T(8,128)(2,1)S(1)}, bf16[128,1152]{1,0:T(8,128)(2,1)S(1)}, u32[]{:S(2)}, u32[]{:S(2)}) collective-permute-start(bf16[128,1152]{1,0:T(8,128)(2,1)S(1)} %get-tuple-element.123), channel_id=1, source_target_pairs={{0,2},{1,3},{2,0},{3,1},{4,6},{5,7},{6,4},{7,5},{8,10},{9,11},{10,... | collective-permute-start | bytes 884744 | tf_op jit(solution)/shard_map/ppermute | solution.py:259
  7.4 1.7 %copy-done = bf16[1152,1152]{1,0:T(8,128)(2,1)S(1)} copy-done((bf16[1152,1152]{1,0:T(8,128)(2,1)S(1)}, bf16[1152,1152]{1,0:T(8,128)(2,1)}, u32[]{:S(2)}) %copy-start) | copy-done | bytes 2654232
  9.2 1.7 %copy-done.2 = bf16[1152,1152]{1,0:T(8,128)(2,1)S(1)} copy-done((bf16[1152,1152]{1,0:T(8,128)(2,1)S(1)}, bf16[1152,1152]{1,0:T(8,128)(2,1)}, u32[]{:S(2)}) %copy-start.2) | copy-done | bytes 2654232
  10.9 8.0 %shard_map.75 = (f32[512,1152]{1,0:T(8,128)S(1)}, bf16[512,1152]{1,0:T(8,128)(2,1)S(1)}, f32[512,1152]{1,0:T(8,128)S(1)}, bf16[512,1152]{1,0:T(8,128)(2,1)S(1)},...) custom-call(s32[2]{0:T(128)S(1)} %pad_add_fusion.place, ...), custom_call_target="tpu_custom_call" | custom-call | tf_op jit(solution)/shard_map/pallas_call | solution.py:246
  19.6 0.7 collective-permute-done.10.refs_7_
  22.1 2.7 %shard_map.76 = (f32[256,1152]{1,0:T(8,128)S(1)}, bf16[256,1152]{1,0:T(8,128)(2,1)S(1)}, bf16[512,256]{1,0:T(8,128)(2,1)S(1)}, f32[512,1152]{1,0:T(8,128)S(1)}) custom-call(bf16[256,1152]{1,0:T(8,128)(2,1)S(1)} %collective-permute-done.t2, bf16[1152,1152]{1,0:T(8,128)(2,1)S(1)} %copy-done, bf16[512,1152]{1,0:T(8,128)(2,1)S(1)} %get-tuple-element.68.y_a.refs_3_, ...), custom_call_target="tpu_custom_call" | custom-call | tf_op jit(solution)/shard_map/pallas_call | solution.py:246
  24.8 4.1 %shard_map.77 = (f32[256,1152]{1,0:T(8,128)S(1)}, bf16[256,1152]{1,0:T(8,128)(2,1)S(1)}, bf16[512,256]{1,0:T(8,128)(2,1)S(1)}, bf16[512,1152]{1,0:T(8,128)(2,1)S...) custom-call(bf16[32,1152]{1,0:T(8,128)(2,1)S(1)} %collective-permute, ...), custom_call_target="tpu_custom_call" | custom-call | tf_op jit(solution)/shard_map/pallas_call | solution.py:246
  28.8 1.8 %collective-permute-start.11 = (bf16[144,1152]{1,0:T(8,128)(2,1)S(1)}, bf16[144,1152]{1,0:T(8,128)(2,1)S(1)}, u32[]{:S(2)}, u32[]{:S(2)}) collective-permute-start(bf16[144,1152]{1,0:T(8,128)(2,1)S(1)} %get-tuple-element.83), channel_id=1, source_target_pairs={{0,4},{4,0},{8,12},{12,8},{16,20},{20,16},{24,28},{28,24},{1,5},{5... | collective-permute-start | bytes 995336 | tf_op jit(solution)/shard_map/ppermute | solution.py:259
  30.6 1.6 %collective-permute-start.16 = (bf16[144,1152]{1,0:T(8,128)(2,1)S(1)}, bf16[144,1152]{1,0:T(8,128)(2,1)S(1)}, u32[]{:S(2)}, u32[]{:S(2)}) collective-permute-start(bf16[144,1152]{1,0:T(8,128)(2,1)S(1)} %get-tuple-element.106), channel_id=1, source_target_pairs={{0,8},{4,12},{8,0},{12,4},{16,24},{20,28},{24,16},{28,20},{1,9},{5... | collective-permute-start | bytes 995336 | tf_op jit(solution)/shard_map/ppermute | solution.py:259
  32.4 2.0 %shard_map.78 = (f32[256,1152]{1,0:T(8,128)S(1)}, f32[256,1152]{1,0:T(8,128)S(1)}, bf16[288,512]{1,0:T(8,128)(2,1)S(1)}) custom-call(s32[2]{0:T(128)S(1)} %pad_add_fusion.place, bf16[256,1152]{1,0:T(8,128)(2,1)S(1)} %collective-permute-done.t2, bf16[32,1152]{1,0:T(8,128)(2,1)S(1)} %collective-permute-done.3.refs_0_, ...), custom_call_target="tpu_custom_call" | custom-call | tf_op jit(solution)/shard_map/pallas_call | solution.py:246
  35.0 1.9 %shard_map.79 = (bf16[256,1152]{1,0:T(8,128)(2,1)S(1)}, bf16[256,512]{1,0:T(8,128)(2,1)S(1)}, bf16[256,512]{1,0:T(8,128)(2,1)S(1)}) custom-call(bf16[128,1152]{1,0:T(8,128)(2,1)S(1)} %collective-permute-done.12.refs_0_, bf16[128,1152]{1,0:T(8,128)(2,1)S(1)} %collective-permute-done.13.refs_1_, bf16[1152,1152]{1,0:T(8,128)(2,1)S(1)} %copy-done.3, ...), custom_call_target="tpu_custom_call" | custom-call | tf_op jit(solution)/shard_map/pallas_call | solution.py:246
  37.0 1.9 %shard_map.80 = (bf16[256,1152]{1,0:T(8,128)(2,1)S(1)}, bf16[256,512]{1,0:T(8,128)(2,1)S(1)}, bf16[256,512]{1,0:T(8,128)(2,1)S(1)}) custom-call(bf16[128,1152]{1,0:T(8,128)(2,1)S(1)} %collective-permute-done.14.refs_0_, bf16[128,1152]{1,0:T(8,128)(2,1)S(1)} %collective-permute-done.15.refs_1_, bf16[1152,1152]{1,0:T(8,128)(2,1)S(1)} %copy-done.3, ...), custom_call_target="tpu_custom_call" | custom-call | tf_op jit(solution)/shard_map/pallas_call | solution.py:246
  38.9 3.9 %shard_map.81 = (bf16[72,1152]{1,0:T(8,128)(2,1)S(1)}, bf16[72,1152]{1,0:T(8,128)(2,1)S(1)}, bf16[72,1152]{1,0:T(8,128)(2,1)S(1)}, bf16[72,1152]{1,0:T(8,128)(2,1)S(1)}, bf16[256,1152]{1,0:T(8,128)(2,1)S(1)}) custom-call(bf16[256,1152]{1,0:T(8,128)(2,1)S(1)} %get-tuple-element.91.x_2, bf16[256,512]{1,0:T(8,128)(2,1)S(1)} %get-tuple-element.92.w_2a, ...), custom_call_target="tpu_custom_call" | custom-call | tf_op jit(solution)/shard_map/pallas_call | solution.py:246
  42.8 1.8 %collective-permute-start.23 = (bf16[72,1152]{1,0:T(8,128)(2,1)S(1)}, bf16[72,1152]{1,0:T(8,128)(2,1)S(1)}, u32[]{:S(2)}, u32[]{:S(2)}) collective-permute-start(bf16[72,1152]{1,0:T(8,128)(2,1)S(1)} %get-tuple-element.114), channel_id=1, source_target_pairs={{0,4},{4,0},{8,12},{12,8},{16,20},{20,16},{24,28},{28,24},{1,5},{5... | collective-permute-start | bytes 497672 | tf_op jit(solution)/shard_map/ppermute | solution.py:259
  44.6 1.6 %collective-permute-start.24 = (bf16[72,1152]{1,0:T(8,128)(2,1)S(1)}, bf16[72,1152]{1,0:T(8,128)(2,1)S(1)}, u32[]{:S(2)}, u32[]{:S(2)}) collective-permute-start(bf16[72,1152]{1,0:T(8,128)(2,1)S(1)} %get-tuple-element.116), channel_id=1, source_target_pairs={{0,8},{4,12},{8,0},{12,4},{16,24},{20,28},{24,16},{28,20},{1,9},{5... | collective-permute-start | bytes 497672 | tf_op jit(solution)/shard_map/ppermute | solution.py:259
  46.4 1.0 %collective-permute-done.17 = bf16[144,1152]{1,0:T(8,128)(2,1)S(1)} collective-permute-done((bf16[144,1152]{1,0:T(8,128)(2,1)S(1)}, bf16[144,1152]{1,0:T(8,128)(2,1)S(1)}, u32[]{:S(2)}, u32[]{:S(2)}) %collective-permute-start.17) | collective-permute-done | bytes 331808 | tf_op jit(solution)/shard_map/ppermute | solution.py:259
  47.6 1.7 %collective-permute-start.18 = (bf16[72,1152]{1,0:T(8,128)(2,1)S(1)}, bf16[72,1152]{1,0:T(8,128)(2,1)S(1)}, u32[]{:S(2)}, u32[]{:S(2)}) collective-permute-start(bf16[72,1152]{1,0:T(8,128)(2,1)S(1)} %slice.9), channel_id=1, source_target_pairs={{0,2},{1,3},{2,0},{3,1},{4,6},{5,7},{6,4},{7,5},{8,10},{9,11},{10,... | collective-permute-start | bytes 497672 | tf_op jit(solution)/shard_map/ppermute | solution.py:259
  49.3 2.0 %shard_map.83 = f32[256,1152]{1,0:T(8,128)} custom-call(bf16[256,1152]{1,0:T(8,128)(2,1)S(1)} %get-tuple-element.111.back, bf16[1152,1152]{1,0:T(8,128)(2,1)S(1)} %copy-done.1), custom_call_target="tpu_custom_call" | custom-call | flops 1358954496 | tf_op jit(solution)/shard_map/pallas_call | solution.py:246
  51.3 2.0 %shard_map.82 = f32[256,1152]{1,0:T(8,128)} custom-call(bf16[512,1152]{1,0:T(8,128)(2,1)S(1)} %get-tuple-element.110.back, bf16[1152,1152]{1,0:T(8,128)(2,1)S(1)} %copy-done.3), custom_call_target="tpu_custom_call" | custom-call | flops 1358954496 | tf_op jit(solution)/shard_map/pallas_call | solution.py:246
  53.4 2.6 %collective-permute-start.19 = (bf16[72,1152]{1,0:T(8,128)(2,1)S(1)}, bf16[72,1152]{1,0:T(8,128)(2,1)S(1)}, u32[]{:S(2)}, u32[]{:S(2)}) collective-permute-start(bf16[72,1152]{1,0:T(8,128)(2,1)S(1)} %add_convert_fusion.4), channel_id=1, source_target_pairs={{0,16},{4,20},{8,24},{12,28},{16,0},{20,4},{24,8},{28,12},{1,17},{... | collective-permute-start | bytes 497672 | tf_op jit(solution)/shard_map/ppermute | solution.py:259
  56.2 6.4 %collective-permute-done.19 = bf16[72,1152]{1,0:T(8,128)(2,1)S(1)} collective-permute-done((bf16[72,1152]{1,0:T(8,128)(2,1)S(1)}, bf16[72,1152]{1,0:T(8,128)(2,1)S(1)}, u32[]{:S(2)}, u32[]{:S(2)}) %collective-permute-start.19) | collective-permute-done | bytes 165920 | tf_op jit(solution)/shard_map/ppermute | solution.py:259
  62.7 5.0 %collective-permute-start.22 = (bf16[72,1152]{1,0:T(8,128)(2,1)S(1)}, bf16[72,1152]{1,0:T(8,128)(2,1)S(1)}, u32[]{:S(2)}, u32[]{:S(2)}) collective-permute-start(bf16[72,1152]{1,0:T(8,128)(2,1)S(1)} %add_convert_fusion.3.h0), channel_id=1, source_target_pairs={{0,12},{4,8},{8,4},{12,0},{16,28},{20,24},{24,20},{28,16},{1,13},{... | collective-permute-start | bytes 497672 | tf_op jit(solution)/shard_map/ppermute | solution.py:259
  68.3 4.1 %collective-permute-done.26 = bf16[72,1152]{1,0:T(8,128)(2,1)S(1)} collective-permute-done((bf16[72,1152]{1,0:T(8,128)(2,1)S(1)}, bf16[72,1152]{1,0:T(8,128)(2,1)S(1)}, u32[]{:S(2)}, u32[]{:S(2)}) %collective-permute-start.26) | collective-permute-done | bytes 165920 | tf_op jit(solution)/shard_map/ppermute | solution.py:259
  72.4 2.2 %collective-permute-done.22.h3 = bf16[72,1152]{1,0:T(8,128)(2,1)S(1)} collective-permute-done((bf16[72,1152]{1,0:T(8,128)(2,1)S(1)}, bf16[72,1152]{1,0:T(8,128)(2,1)S(1)}, u32[]{:S(2)}, u32[]{:S(2)}) %collective-permute-start.22) | collective-permute-done | bytes 165920 | tf_op jit(solution)/shard_map/ppermute | solution.py:259
  75.3 1.0 %collective-permute-start.28 = (bf16[72,1152]{1,0:T(8,128)(2,1)S(1)}, bf16[72,1152]{1,0:T(8,128)(2,1)S(1)}, u32[]{:S(2)}, u32[]{:S(2)}) collective-permute-start(bf16[72,1152]{1,0:T(8,128)(2,1)S(1)} %add_convert_fusion.1.h0), channel_id=1, source_target_pairs={{0,8},{4,12},{8,0},{12,4},{16,24},{20,28},{24,16},{28,20},{1,9},{5... | collective-permute-start | bytes 497672 | tf_op jit(solution)/shard_map/ppermute | solution.py:259
  76.2 2.0 %collective-permute-start.29 = (bf16[72,1152]{1,0:T(8,128)(2,1)S(1)}, bf16[72,1152]{1,0:T(8,128)(2,1)S(1)}, u32[]{:S(2)}, u32[]{:S(2)}) collective-permute-start(bf16[72,1152]{1,0:T(8,128)(2,1)S(1)} %add_convert_fusion.1.h0), channel_id=1, source_target_pairs={{0,12},{4,8},{8,4},{12,0},{16,28},{20,24},{24,20},{28,16},{1,13},{... | collective-permute-start | bytes 497672 | tf_op jit(solution)/shard_map/ppermute | solution.py:259
  78.2 1.7 %shard_map.84 = f32[288,1152]{1,0:T(8,128)} custom-call(s32[2]{0:T(128)S(1)} %pad_add_fusion.place, bf16[72,1152]{1,0:T(8,128)(2,1)S(1)} %add_convert_fusion.3.h0, bf16[72,1152]{1,0:T(8,128)(2,1)S(1)} %collective-permute-done.20.h1, bf16[72,1152]{1,0:T(8,128)(2,1)S(1)} %collective-permute-done.21.h2, bf16[72,1152]{1,0:T(8,128)(2,1)S(1)} %collective-permute-done.22.h3), custom_call_target="tpu_custom_call" | custom-call | tf_op jit(solution)/shard_map/pallas_call | solution.py:246
  79.9 1.9 %collective-permute-done.27.h1 = bf16[72,1152]{1,0:T(8,128)(2,1)S(1)} collective-permute-done((bf16[72,1152]{1,0:T(8,128)(2,1)S(1)}, bf16[72,1152]{1,0:T(8,128)(2,1)S(1)}, u32[]{:S(2)}, u32[]{:S(2)}) %collective-permute-start.27) | collective-permute-done | bytes 165920 | tf_op jit(solution)/shard_map/ppermute | solution.py:259
  81.8 2.2 %collective-permute-done.29.h3 = bf16[72,1152]{1,0:T(8,128)(2,1)S(1)} collective-permute-done((bf16[72,1152]{1,0:T(8,128)(2,1)S(1)}, bf16[72,1152]{1,0:T(8,128)(2,1)S(1)}, u32[]{:S(2)}, u32[]{:S(2)}) %collective-permute-start.29) | collective-permute-done | bytes 165920 | tf_op jit(solution)/shard_map/ppermute | solution.py:259
  84.0 1.7 %shard_map.85 = f32[288,1152]{1,0:T(8,128)} custom-call(s32[2]{0:T(128)S(1)} %pad_add_fusion.place, bf16[72,1152]{1,0:T(8,128)(2,1)S(1)} %add_convert_fusion.1.h0, bf16[72,1152]{1,0:T(8,128)(2,1)S(1)} %collective-permute-done.27.h1, bf16[72,1152]{1,0:T(8,128)(2,1)S(1)} %collective-permute-done.28.h2, bf16[72,1152]{1,0:T(8,128)(2,1)S(1)} %collective-permute-done.29.h3), custom_call_target="tpu_custom_call" | custom-call | tf_op jit(solution)/shard_map/pallas_call | solution.py:246
  (60 shorter events, 5.8 us)
Async XLA Ops:
  0.6 6.8 %copy-start.4 = (bf16[256,1152]{1,0:T(8,128)(2,1)S(1)}, bf16[256,1152]{1,0:T(8,128)(2,1)}, u32[]{:S(2)}) copy-start(bf16[256,1152]{1,0:T(8,128)(2,1)} %i0_far) | copy-start | bytes 1769476
  0.6 6.8 %copy-start.5 = (bf16[256,1152]{1,0:T(8,128)(2,1)S(1)}, bf16[256,1152]{1,0:T(8,128)(2,1)}, u32[]{:S(2)}) copy-start(bf16[256,1152]{1,0:T(8,128)(2,1)} %t0_far) | copy-start | bytes 1769476
  0.7 6.6 %collective-permute-start.1 = (bf16[256,1152]{1,0:T(8,128)(2,1)}, bf16[256,1152]{1,0:T(8,128)(2,1)S(1)}, u32[]{:S(2)}, u32[]{:S(2)}) collective-permute-start(bf16[256,1152]{1,0:T(8,128)(2,1)} %t0_far), channel_id=1, source_target_pairs={{0,1},{1,0},{2,3},{3,2},{4,5},{5,4},{6,7},{7,6},{8,9},{9,8},{10,11... | collective-permute-start | bytes 1769480 | tf_op jit(solution)/shard_map/ppermute | solution.py:259
  1.2 6.2 %collective-permute-start.2 = (bf16[256,1152]{1,0:T(8,128)(2,1)}, bf16[256,1152]{1,0:T(8,128)(2,1)S(1)}, u32[]{:S(2)}, u32[]{:S(2)}) collective-permute-start(bf16[256,1152]{1,0:T(8,128)(2,1)} %i0_far), channel_id=1, source_target_pairs={{0,1},{1,0},{2,3},{3,2},{4,5},{5,4},{6,7},{7,6},{8,9},{9,8},{10,11... | collective-permute-start | bytes 1769480 | tf_op jit(solution)/shard_map/ppermute | solution.py:259
  1.3 17.6 %collective-permute-start = (bf16[256,1152]{1,0:T(8,128)(2,1)}, bf16[256,1152]{1,0:T(8,128)(2,1)S(1)}, u32[]{:S(2)}, u32[]{:S(2)}) collective-permute-start(bf16[256,1152]{1,0:T(8,128)(2,1)} %t0_far), channel_id=1, source_target_pairs={{0,2},{1,3},{2,0},{3,1},{4,6},{5,7},{6,4},{7,5},{8,10},{9,11},{10,... | collective-permute-start | bytes 1769480 | tf_op jit(solution)/shard_map/ppermute | solution.py:259
  5.3 29.1 %collective-permute-start.13 = (bf16[128,1152]{1,0:T(8,128)(2,1)S(1)}, bf16[128,1152]{1,0:T(8,128)(2,1)S(1)}, u32[]{:S(2)}, u32[]{:S(2)}) collective-permute-start(bf16[128,1152]{1,0:T(8,128)(2,1)S(1)} %get-tuple-element.122), channel_id=1, source_target_pairs={{0,2},{1,3},{2,0},{3,1},{4,6},{5,7},{6,4},{7,5},{8,10},{9,11},{10,... | collective-permute-start | bytes 884744 | tf_op jit(solution)/shard_map/ppermute | solution.py:259
  5.4 29.1 %collective-permute-start.12 = (bf16[128,1152]{1,0:T(8,128)(2,1)S(1)}, bf16[128,1152]{1,0:T(8,128)(2,1)S(1)}, u32[]{:S(2)}, u32[]{:S(2)}) collective-permute-start(bf16[128,1152]{1,0:T(8,128)(2,1)S(1)} %get-tuple-element.123), channel_id=1, source_target_pairs={{0,2},{1,3},{2,0},{3,1},{4,6},{5,7},{6,4},{7,5},{8,10},{9,11},{10,... | collective-permute-start | bytes 884744 | tf_op jit(solution)/shard_map/ppermute | solution.py:259
  18.9 1.3 %collective-permute-start.10 = (bf16[32,1152]{1,0:T(8,128)(2,1)S(1)}, bf16[32,1152]{1,0:T(8,128)(2,1)S(1)}, u32[]{:S(2)}, u32[]{:S(2)}) collective-permute-start(bf16[32,1152]{1,0:T(8,128)(2,1)S(1)} %get-tuple-element.124), channel_id=1, source_target_pairs={{0,1},{1,0},{2,3},{3,2},{4,5},{5,4},{6,7},{7,6},{8,9},{9,8},{10,11... | collective-permute-start | bytes 221192 | tf_op jit(solution)/shard_map/ppermute | solution.py:259
  19.0 1.4 %collective-permute-start.9 = (bf16[32,1152]{1,0:T(8,128)(2,1)S(1)}, bf16[32,1152]{1,0:T(8,128)(2,1)S(1)}, u32[]{:S(2)}, u32[]{:S(2)}) collective-permute-start(bf16[32,1152]{1,0:T(8,128)(2,1)S(1)} %get-tuple-element.125), channel_id=1, source_target_pairs={{0,1},{1,0},{2,3},{3,2},{4,5},{5,4},{6,7},{7,6},{8,9},{9,8},{10,11... | collective-permute-start | bytes 221192 | tf_op jit(solution)/shard_map/ppermute | solution.py:259
  19.5 1.3 %collective-permute-start.8 = (bf16[32,1152]{1,0:T(8,128)(2,1)S(1)}, bf16[32,1152]{1,0:T(8,128)(2,1)S(1)}, u32[]{:S(2)}, u32[]{:S(2)}) collective-permute-start(bf16[32,1152]{1,0:T(8,128)(2,1)S(1)} %get-tuple-element.126), channel_id=1, source_target_pairs={{0,1},{1,0},{2,3},{3,2},{4,5},{5,4},{6,7},{7,6},{8,9},{9,8},{10,11... | collective-permute-start | bytes 221192 | tf_op jit(solution)/shard_map/ppermute | solution.py:259
  20.3 1.3 %collective-permute-start.7 = (bf16[32,1152]{1,0:T(8,128)(2,1)S(1)}, bf16[32,1152]{1,0:T(8,128)(2,1)S(1)}, u32[]{:S(2)}, u32[]{:S(2)}) collective-permute-start(bf16[32,1152]{1,0:T(8,128)(2,1)S(1)} %get-tuple-element.127), channel_id=1, source_target_pairs={{0,1},{1,0},{2,3},{3,2},{4,5},{5,4},{6,7},{7,6},{8,9},{9,8},{10,11... | collective-permute-start | bytes 221192 | tf_op jit(solution)/shard_map/ppermute | solution.py:259
  20.4 1.3 %collective-permute-start.6 = (bf16[32,1152]{1,0:T(8,128)(2,1)S(1)}, bf16[32,1152]{1,0:T(8,128)(2,1)S(1)}, u32[]{:S(2)}, u32[]{:S(2)}) collective-permute-start(bf16[32,1152]{1,0:T(8,128)(2,1)S(1)} %get-tuple-element.128), channel_id=1, source_target_pairs={{0,1},{1,0},{2,3},{3,2},{4,5},{5,4},{6,7},{7,6},{8,9},{9,8},{10,11... | collective-permute-start | bytes 221192 | tf_op jit(solution)/shard_map/ppermute | solution.py:259
  20.8 3.9 %collective-permute-start.5 = (bf16[32,1152]{1,0:T(8,128)(2,1)S(1)}, bf16[32,1152]{1,0:T(8,128)(2,1)S(1)}, u32[]{:S(2)}, u32[]{:S(2)}) collective-permute-start(bf16[32,1152]{1,0:T(8,128)(2,1)S(1)} %get-tuple-element.129), channel_id=1, source_target_pairs={{0,1},{1,0},{2,3},{3,2},{4,5},{5,4},{6,7},{7,6},{8,9},{9,8},{10,11... | collective-permute-start | bytes 221192 | tf_op jit(solution)/shard_map/ppermute | solution.py:259
  21.5 3.2 %collective-permute-start.4 = (bf16[32,1152]{1,0:T(8,128)(2,1)S(1)}, bf16[32,1152]{1,0:T(8,128)(2,1)S(1)}, u32[]{:S(2)}, u32[]{:S(2)}) collective-permute-start(bf16[32,1152]{1,0:T(8,128)(2,1)S(1)} %get-tuple-element.130), channel_id=1, source_target_pairs={{0,1},{1,0},{2,3},{3,2},{4,5},{5,4},{6,7},{7,6},{8,9},{9,8},{10,11... | collective-permute-start | bytes 221192 | tf_op jit(solution)/shard_map/ppermute | solution.py:259
  21.7 3.0 %collective-permute-start.3 = (bf16[32,1152]{1,0:T(8,128)(2,1)S(1)}, bf16[32,1152]{1,0:T(8,128)(2,1)S(1)}, u32[]{:S(2)}, u32[]{:S(2)}) collective-permute-start(bf16[32,1152]{1,0:T(8,128)(2,1)S(1)} %get-tuple-element.131), channel_id=1, source_target_pairs={{0,1},{1,0},{2,3},{3,2},{4,5},{5,4},{6,7},{7,6},{8,9},{9,8},{10,11... | collective-permute-start | bytes 221192 | tf_op jit(solution)/shard_map/ppermute | solution.py:259
  28.8 17.3 %collective-permute-start.11 = (bf16[144,1152]{1,0:T(8,128)(2,1)S(1)}, bf16[144,1152]{1,0:T(8,128)(2,1)S(1)}, u32[]{:S(2)}, u32[]{:S(2)}) collective-permute-start(bf16[144,1152]{1,0:T(8,128)(2,1)S(1)} %get-tuple-element.83), channel_id=1, source_target_pairs={{0,4},{4,0},{8,12},{12,8},{16,20},{20,16},{24,28},{28,24},{1,5},{5... | collective-permute-start | bytes 995336 | tf_op jit(solution)/shard_map/ppermute | solution.py:259
  30.6 15.7 %collective-permute-start.16 = (bf16[144,1152]{1,0:T(8,128)(2,1)S(1)}, bf16[144,1152]{1,0:T(8,128)(2,1)S(1)}, u32[]{:S(2)}, u32[]{:S(2)}) collective-permute-start(bf16[144,1152]{1,0:T(8,128)(2,1)S(1)} %get-tuple-element.106), channel_id=1, source_target_pairs={{0,8},{4,12},{8,0},{12,4},{16,24},{20,28},{24,16},{28,20},{1,9},{5... | collective-permute-start | bytes 995336 | tf_op jit(solution)/shard_map/ppermute | solution.py:259
  32.2 15.2 %collective-permute-start.17 = (bf16[144,1152]{1,0:T(8,128)(2,1)S(1)}, bf16[144,1152]{1,0:T(8,128)(2,1)S(1)}, u32[]{:S(2)}, u32[]{:S(2)}) collective-permute-start(bf16[144,1152]{1,0:T(8,128)(2,1)S(1)} %get-tuple-element.108), channel_id=1, source_target_pairs={{0,12},{4,8},{8,4},{12,0},{16,28},{20,24},{24,20},{28,16},{1,13},{... | collective-permute-start | bytes 995336 | tf_op jit(solution)/shard_map/ppermute | solution.py:259
  34.4 2.5 %collective-permute-start.15 = (bf16[128,1152]{1,0:T(8,128)(2,1)S(1)}, bf16[128,1152]{1,0:T(8,128)(2,1)S(1)}, u32[]{:S(2)}, u32[]{:S(2)}) collective-permute-start(bf16[128,1152]{1,0:T(8,128)(2,1)S(1)} %collective-permute-done.13.refs_1_), channel_id=1, source_target_pairs={{0,1},{1,0},{2,3},{3,2},{4,5},{5,4},{6,7},{7,6},{8,9},{9,8},{10,11... | collective-permute-start | bytes 884744 | tf_op jit(solution)/shard_map/ppermute | solution.py:259
  34.5 2.5 %collective-permute-start.14 = (bf16[128,1152]{1,0:T(8,128)(2,1)S(1)}, bf16[128,1152]{1,0:T(8,128)(2,1)S(1)}, u32[]{:S(2)}, u32[]{:S(2)}) collective-permute-start(bf16[128,1152]{1,0:T(8,128)(2,1)S(1)} %collective-permute-done.12.refs_0_), channel_id=1, source_target_pairs={{0,1},{1,0},{2,3},{3,2},{4,5},{5,4},{6,7},{7,6},{8,9},{9,8},{10,11... | collective-permute-start | bytes 884744 | tf_op jit(solution)/shard_map/ppermute | solution.py:259
  42.8 13.3 %collective-permute-start.23 = (bf16[72,1152]{1,0:T(8,128)(2,1)S(1)}, bf16[72,1152]{1,0:T(8,128)(2,1)S(1)}, u32[]{:S(2)}, u32[]{:S(2)}) collective-permute-start(bf16[72,1152]{1,0:T(8,128)(2,1)S(1)} %get-tuple-element.114), channel_id=1, source_target_pairs={{0,4},{4,0},{8,12},{12,8},{16,20},{20,16},{24,28},{28,24},{1,5},{5... | collective-permute-start | bytes 497672 | tf_op jit(solution)/shard_map/ppermute | solution.py:259
  44.6 11.5 %collective-permute-start.24 = (bf16[72,1152]{1,0:T(8,128)(2,1)S(1)}, bf16[72,1152]{1,0:T(8,128)(2,1)S(1)}, u32[]{:S(2)}, u32[]{:S(2)}) collective-permute-start(bf16[72,1152]{1,0:T(8,128)(2,1)S(1)} %get-tuple-element.116), channel_id=1, source_target_pairs={{0,8},{4,12},{8,0},{12,4},{16,24},{20,28},{24,16},{28,20},{1,9},{5... | collective-permute-start | bytes 497672 | tf_op jit(solution)/shard_map/ppermute | solution.py:259
  46.2 9.9 %collective-permute-start.25 = (bf16[72,1152]{1,0:T(8,128)(2,1)S(1)}, bf16[72,1152]{1,0:T(8,128)(2,1)S(1)}, u32[]{:S(2)}, u32[]{:S(2)}) collective-permute-start(bf16[72,1152]{1,0:T(8,128)(2,1)S(1)} %get-tuple-element.118), channel_id=1, source_target_pairs={{0,12},{4,8},{8,4},{12,0},{16,28},{20,24},{24,20},{28,16},{1,13},{... | collective-permute-start | bytes 497672 | tf_op jit(solution)/shard_map/ppermute | solution.py:259
  47.6 5.8 %collective-permute-start.18 = (bf16[72,1152]{1,0:T(8,128)(2,1)S(1)}, bf16[72,1152]{1,0:T(8,128)(2,1)S(1)}, u32[]{:S(2)}, u32[]{:S(2)}) collective-permute-start(bf16[72,1152]{1,0:T(8,128)(2,1)S(1)} %slice.9), channel_id=1, source_target_pairs={{0,2},{1,3},{2,0},{3,1},{4,6},{5,7},{6,4},{7,5},{8,10},{9,11},{10,... | collective-permute-start | bytes 497672 | tf_op jit(solution)/shard_map/ppermute | solution.py:259
  53.4 9.2 %collective-permute-start.19 = (bf16[72,1152]{1,0:T(8,128)(2,1)S(1)}, bf16[72,1152]{1,0:T(8,128)(2,1)S(1)}, u32[]{:S(2)}, u32[]{:S(2)}) collective-permute-start(bf16[72,1152]{1,0:T(8,128)(2,1)S(1)} %add_convert_fusion.4), channel_id=1, source_target_pairs={{0,16},{4,20},{8,24},{12,28},{16,0},{20,4},{24,8},{28,12},{1,17},{... | collective-permute-start | bytes 497672 | tf_op jit(solution)/shard_map/ppermute | solution.py:259
  62.6 9.7 %collective-permute-start.26 = (bf16[72,1152]{1,0:T(8,128)(2,1)S(1)}, bf16[72,1152]{1,0:T(8,128)(2,1)S(1)}, u32[]{:S(2)}, u32[]{:S(2)}) collective-permute-start(bf16[72,1152]{1,0:T(8,128)(2,1)S(1)} %add_convert_fusion.2), channel_id=1, source_target_pairs={{0,16},{4,20},{8,24},{12,28},{16,0},{20,4},{24,8},{28,12},{1,17},{... | collective-permute-start | bytes 497672 | tf_op jit(solution)/shard_map/ppermute | solution.py:259
  62.7 11.9 %collective-permute-start.22 = (bf16[72,1152]{1,0:T(8,128)(2,1)S(1)}, bf16[72,1152]{1,0:T(8,128)(2,1)S(1)}, u32[]{:S(2)}, u32[]{:S(2)}) collective-permute-start(bf16[72,1152]{1,0:T(8,128)(2,1)S(1)} %add_convert_fusion.3.h0), channel_id=1, source_target_pairs={{0,12},{4,8},{8,4},{12,0},{16,28},{20,24},{24,20},{28,16},{1,13},{... | collective-permute-start | bytes 497672 | tf_op jit(solution)/shard_map/ppermute | solution.py:259
  67.7 10.5 %collective-permute-start.20 = (bf16[72,1152]{1,0:T(8,128)(2,1)S(1)}, bf16[72,1152]{1,0:T(8,128)(2,1)S(1)}, u32[]{:S(2)}, u32[]{:S(2)}) collective-permute-start(bf16[72,1152]{1,0:T(8,128)(2,1)S(1)} %add_convert_fusion.3.h0), channel_id=1, source_target_pairs={{0,4},{4,0},{8,12},{12,8},{16,20},{20,16},{24,28},{28,24},{1,5},{5... | collective-permute-start | bytes 497672 | tf_op jit(solution)/shard_map/ppermute | solution.py:259
  68.2 10.0 %collective-permute-start.21 = (bf16[72,1152]{1,0:T(8,128)(2,1)S(1)}, bf16[72,1152]{1,0:T(8,128)(2,1)S(1)}, u32[]{:S(2)}, u32[]{:S(2)}) collective-permute-start(bf16[72,1152]{1,0:T(8,128)(2,1)S(1)} %add_convert_fusion.3.h0), channel_id=1, source_target_pairs={{0,8},{4,12},{8,0},{12,4},{16,24},{20,28},{24,16},{28,20},{1,9},{5... | collective-permute-start | bytes 497672 | tf_op jit(solution)/shard_map/ppermute | solution.py:259
  74.6 7.2 %collective-permute-start.27 = (bf16[72,1152]{1,0:T(8,128)(2,1)S(1)}, bf16[72,1152]{1,0:T(8,128)(2,1)S(1)}, u32[]{:S(2)}, u32[]{:S(2)}) collective-permute-start(bf16[72,1152]{1,0:T(8,128)(2,1)S(1)} %add_convert_fusion.1.h0), channel_id=1, source_target_pairs={{0,4},{4,0},{8,12},{12,8},{16,20},{20,16},{24,28},{28,24},{1,5},{5... | collective-permute-start | bytes 497672 | tf_op jit(solution)/shard_map/ppermute | solution.py:259
  75.3 6.6 %collective-permute-start.28 = (bf16[72,1152]{1,0:T(8,128)(2,1)S(1)}, bf16[72,1152]{1,0:T(8,128)(2,1)S(1)}, u32[]{:S(2)}, u32[]{:S(2)}) collective-permute-start(bf16[72,1152]{1,0:T(8,128)(2,1)S(1)} %add_convert_fusion.1.h0), channel_id=1, source_target_pairs={{0,8},{4,12},{8,0},{12,4},{16,24},{20,28},{24,16},{28,20},{1,9},{5... | collective-permute-start | bytes 497672 | tf_op jit(solution)/shard_map/ppermute | solution.py:259
  76.2 7.8 %collective-permute-start.29 = (bf16[72,1152]{1,0:T(8,128)(2,1)S(1)}, bf16[72,1152]{1,0:T(8,128)(2,1)S(1)}, u32[]{:S(2)}, u32[]{:S(2)}) collective-permute-start(bf16[72,1152]{1,0:T(8,128)(2,1)S(1)} %add_convert_fusion.1.h0), channel_id=1, source_target_pairs={{0,12},{4,8},{8,4},{12,0},{16,28},{20,24},{24,20},{28,16},{1,13},{... | collective-permute-start | bytes 497672 | tf_op jit(solution)/shard_map/ppermute | solution.py:259
  (4 other events, 8.8 us)

commit v7 on v6

--- a/solution.py
+++ b/solution.py
@@ -131,8 +131,8 @@
 
 
 def near_kernel(
-    place, t1, i1, t0_far, i0_far, text_head_far, image_head_far,
-    q_a, y_a, p_a, x_a, w_aa, gy_a, pick_i, pick_t, dots, t0, i0, text_head, image_head, sems,
+    t1, i1, t0_far, i0_far, text_head_far, image_head_far,
+    q_a, y_a, p_a, x_a, w_aa, t0, i0, text_head, image_head, dots, sems,
 ):
     half = t0.shape[0]
     copies = [
@@ -155,18 +155,27 @@
     unit_rows(p_a, x_a)
     dots[...] = dot_nt(x_a[...], y_a[...])
     weight_rows(dots, w_aa, 0)
+
+
+def near_pull_kernel(place, t0, t1, i0, i1, x_a, w_aa, gy_a, pick_i, pick_t):
+    half = t0.shape[0]
     rows = pick_t.shape[0]
+    pick = picker(place, rows, t0.shape[1], (0, 2))
+    pick_i[:, :half] = dot_nt(pick, i0[...]).astype(BF16)
+    pick_i[:, half:] = dot_nt(pick, i1[...]).astype(BF16)
     pick = picker(place, rows, t0.shape[1], (0,))
     pick_t[:, :half] = dot_nt(pick, t0[...]).astype(BF16)
     pick_t[:, half:] = dot_nt(pick, t1[...]).astype(BF16)
-    pick = picker(place, rows, t0.shape[1], (0, 2))
-    pick_i[:, :half] = dot_nt(pick, i0[...]).astype(BF16)
-    pick_i[:, half:] = dot_nt(pick, i1[...]).astype(BF16)
     gy_a[...] = dot_tn(w_aa[...], x_a[...])
 
 
-def text_kernel(t2, text_head, y_a, x_a, w_aa, q_2, y_2, w_a2, gx, dots):
-    q_2[...] = dot_nn(t2[...], text_head[...])
+def rows_of(refs):
+    return jnp.concatenate([ref[...] for ref in refs], axis=0)
+
+
+def text_kernel(*refs):
+    *features, text_head, y_a, x_a, w_aa, q_2, y_2, w_a2, gx, dots = refs
+    q_2[...] = dot_nn(rows_of(features), text_head[...])
     unit_rows(q_2, y_2)
     dots[...] = dot_nt(x_a[...], y_2[...])
     weight_rows(dots, w_a2)
@@ -175,8 +184,7 @@
 
 def image_kernel(*refs):
     *features, text_head, p_a, x_a, gx_in, pick_i, q_3, y_3, w_a3, dp_a, h0, h1, h2, h3, dots, gx = refs
-    t3 = jnp.concatenate([t[...] for t in features], axis=0)
-    q_3[...] = dot_nn(t3, text_head[...])
+    q_3[...] = dot_nn(rows_of(features), text_head[...])
     unit_rows(q_3, y_3)
     dots[...] = dot_nt(x_a[...], y_3[...])
     weight_rows(dots, w_a3)
@@ -185,22 +193,18 @@
     split_head(dot_nn(pick_i[...], dp_a[...]), (h0, h1, h2, h3))
 
 
-def pull_kernel(place, t2, *refs):
+def pull_kernel(place, *refs):
     *features, x_a, w_a2, w_a3, gy_2, gy_3, pick_t = refs
-    half = t2.shape[0]
     gy_2[...] = dot_tn(w_a2[...], x_a[...])
     gy_3[...] = dot_tn(w_a3[...], x_a[...])
-    pick = picker(place, pick_t.shape[0], t2.shape[1], (0,))
-    pick_t[:, :half] = dot_nt(pick, t2[...]).astype(BF16)
-    t3 = jnp.concatenate([t[...] for t in features], axis=0)
-    pick_t[:, half:] = dot_nt(pick, t3).astype(BF16)
+    pick = picker(place, pick_t.shape[0], x_a.shape[1], (0,))
+    pick_t[...] = dot_nt(pick, rows_of(features)).astype(BF16)
 
 
 def block_kernel(block, *refs):
     *features, image_head, y_a, y_2, y_3, x_b, w_ba, w_bb, p_b, d_a, d_b = refs
     half = x_b.shape[0]
-    features = jnp.concatenate([i[...] for i in features], axis=0)
-    p_b[...] = dot_nn(features, image_head[...])
+    p_b[...] = dot_nn(rows_of(features), image_head[...])
     unit_rows(p_b, x_b)
     d_a[...] = dot_nt(x_b[...], y_a[...])
     d_b[:, :half] = dot_nt(x_b[...], y_2[...])
@@ -237,9 +241,10 @@
 
 
 def call(kernel, outs, scratch, args, mib, place=None, macs=0, keep=True, far=()):
-    args = [pltpu.with_memory_space_constraint(a, pltpu.VMEM) for a in args] + list(far)
+    far = [pltpu.with_memory_space_constraint(a, pltpu.HBM) for a in far]
+    args = [pltpu.with_memory_space_constraint(a, pltpu.VMEM) for a in args] + far
     specs = [pl.BlockSpec(memory_space=pltpu.VMEM)] * (len(args) - len(far))
-    specs += [pl.BlockSpec(memory_space=pl.ANY)] * len(far)
+    specs += [pl.BlockSpec(memory_space=pltpu.HBM)] * len(far)
     if place is not None:
         args, specs = [place, *args], [pl.BlockSpec(memory_space=pltpu.SMEM), *specs]
     shape = pltpu.VMEM if keep else jax.ShapeDtypeStruct
@@ -272,6 +277,10 @@
     cuts = functools.partial(swap, axis="cuts", size=n_cuts)
     macs = half * width * width
 
+    def both(rows, order, count):
+        rows = after(rows, order)
+        return [rows] + [loop(piece, mask=1) for piece in jnp.split(rows, count)]
+
     def add(own, others):
         return sum((other.astype(F32) for other in others), own.astype(F32)).astype(BF16)
 
@@ -282,8 +291,10 @@
         outs = [((rows_out, width), F32)]
         return call(place_kernel, outs, [], pieces, 4, place, keep=False)[0]
 
-    t2 = loop(text_features, mask=2)
-    i2 = [loop(rows, mask=2) for rows in jnp.split(image_features, 2)]
+    t2, i2 = (
+        [loop(rows, mask=2) for rows in jnp.split(features, 2)]
+        for features in (text_features, image_features)
+    )
     place = jnp.stack([lax.axis_index("loop"), lax.axis_index("cuts") & (QUAD - 1)])
     place = place.astype(jnp.int32)
     t0, i0, place = lax.optimization_barrier((text_features, image_features, place))
@@ -295,30 +306,36 @@
     block_w, block_dots = ((half, near), BF16), ((half, near), F32)
     side_w, side_dots = ((near, half), BF16), ((near, half), F32)
     pick_one, pick_two = ((rows_out, near), BF16), ((2 * rows_out, near), BF16)
-    q_a, y_a, p_a, x_a, w_aa, gy_a, pick_i, pick_a = call(
+    q_a, y_a, p_a, x_a, w_aa, t0, i0, text_head, image_head = call(
         near_kernel,
-        [wide, wide_b, wide, wide_b, ((near, near), BF16), wide, pick_two, pick_one],
-        [((near, near), F32), tall_b, tall_b, head_b, head_b],
+        [wide, wide_b, wide, wide_b, ((near, near), BF16), tall_b, tall_b, head_b, head_b],
+        [((near, near), F32)],
         (t1, i1),
-        16,
-        place,
+        8,
         far=(t0, i0, text_head, image_head),
     )
-    t2 = after(t2, w_aa)
-    t3 = [loop(rows, mask=1) for rows in jnp.split(t2, 8)]
+    first = both(t2[0], w_aa, 2)
     q_2, y_2, w_a2, gx = call(
         text_kernel,
         [tall, tall_b, side_w, wide],
         [side_dots],
-        (t2, text_head, y_a, x_a, w_aa),
+        (*first, text_head, y_a, x_a, w_aa),
         8,
     )
-    t3 = [after(rows, gx) for rows in t3]
+    gy_a, pick_i, pick_a = call(
+        near_pull_kernel,
+        [wide, pick_two, pick_one],
+        [],
+        (t0, t1, i0, i1, after(x_a, gx), w_aa),
+        8,
+        place,
+    )
+    second = both(t2[1], gy_a, 2)
     q_3, y_3, w_a3, dp_a, *image_parts = call(
         image_kernel,
         [tall, tall_b, side_w, wide_b] + [((2 * part, width), BF16)] * QUAD,
         [side_dots, wide],
-        (*t3, text_head, p_a, x_a, gx, pick_i),
+        (*second, text_head, p_a, x_a, gx, pick_i),
         8,
     )
     image_others = [cuts(image_parts[k], mask=k) for k in range(1, QUAD)]
@@ -326,19 +343,17 @@
         pull_kernel,
         [tall, tall, pick_one],
         [],
-        (t2, *t3, x_a, w_a2, w_a3),
+        (*first, *second, x_a, w_a2, w_a3),
         8,
         place,
     )
-    i2 = [after(rows, gy_2) for rows in i2]
-    i3 = [loop(rows, mask=1) for rows in i2]
     blocks = []
-    for block, i in enumerate((i2, i3)):
+    for block, rows in enumerate(i2):
         blocks += call(
             functools.partial(block_kernel, block),
             [tall_b, block_w, block_w],
             [tall, block_dots, block_dots],
-            (*i, image_head, y_a, y_2, y_3),
+            (*both(rows, (blocks[-1], gy_2) if blocks else dp_a, 2), image_head, y_a, y_2, y_3),
             8,
         )
     *text_parts, dq_own = call(

time: 85.9 us -> 84.1 us (0.979)
  local copies, waits for them, and re-layouts: 4.67 us -> 1.26 us
  starting transfers between devices: 28.6 us -> 30.6 us
  waiting for transfers between devices: 19.2 us -> 18 us
  Pallas kernels: 31.9 us -> 32.8 us
    unnamed x12 -> x2, local copies, waits for them, and re-layouts: 3.51 us -> 0.01 us
    ppermute x30 -> x29, starting transfers between devices: 28.6 us -> 30.6 us  [swap(): return lax.ppermute(array, axis, [(i, i ^ mask) for i in range(size)])]
    ppermute x30 -> x29, waiting for transfers between devices: 19.2 us -> 18 us  [swap(): return lax.ppermute(array, axis, [(i, i ^ mask) for i in range(size)])]
    pallas_call x11 -> x12, Pallas kernels: 31.9 us -> 32.8 us  [call(): pl.pallas_call(kernel, out_shape=[shape(s, t) for s, t in outs], in_specs...]
  transfers between devices with their start and end apart: 30 -> 29, of which waited for: 8 -> 11; matrix products, arithmetic and copies ran while one was open for 2% -> 2% of each run, Pallas kernels for 35% -> 37%
where the time goes in v7:
time: 84.1 us; the launch traced here: 84 us
  Pallas kernels  32.8 us (39%)
  starting transfers between devices  30.6 us (36%)
  waiting for transfers between devices  18 us (21%)
  local copies, waits for them, and re-layouts  1.26 us (1%)
  between operations  0.85 us (1%)
    pallas_call x12, Pallas kernels, call(): pl.pallas_call(kernel, out_shape=[shape(s, t) for s, t in outs], in_specs...  32.8 us
    ppermute x29, starting transfers between devices, swap(): return lax.ppermute(array, axis, [(i, i ^ mask) for i in range(size)])  30.6 us
    ppermute x29, waiting for transfers between devices, swap(): return lax.ppermute(array, axis, [(i, i ^ mask) for i in range(size)])  18 us
  transfers between devices with their start and end apart: 29, of which 11 were waited for; matrix products, arithmetic and copies ran while one was open for 2% of the time, Pallas kernels for 37%

profile of v7, /device:TPU:0, one launch (start us, length us, event | category | flops | bytes accessed | tf_op | source)
XLA Modules:
  0.0 84.0 jit_solution(7367019696546212062)
XLA Ops:
  1.2 1.1 %fusion.1 = (bf16[128,1152]{1,0:T(8,128)(2,1)S(1)}, bf16[128,1152]{1,0:T(8,128)(2,1)S(1)}) fusion(bf16[256,1152]{1,0:T(8,128)(2,1)} %t0_far), kind=kLoop, calls=%fused_computation.7 | loop fusion | bytes 1179648 | tf_op jit(solution)/shard_map/split | solution.py:295
  2.3 3.0 %collective-permute-start.3 = (bf16[128,1152]{1,0:T(8,128)(2,1)S(1)}, bf16[128,1152]{1,0:T(8,128)(2,1)S(1)}, u32[]{:S(2)}, u32[]{:S(2)}) collective-permute-start(bf16[128,1152]{1,0:T(8,128)(2,1)S(1)} %get-tuple-element.120), channel_id=1, source_target_pairs={{0,2},{1,3},{2,0},{3,1},{4,6},{5,7},{6,4},{7,5},{8,10},{9,11},{10,... | collective-permute-start | bytes 884744 | tf_op jit(solution)/shard_map/ppermute | solution.py:264
  5.4 6.9 %shard_map.75 = (f32[512,1152]{1,0:T(8,128)S(1)}, bf16[512,1152]{1,0:T(8,128)(2,1)S(1)}, f32[512,1152]{1,0:T(8,128)S(1)}, bf16[512,1152]{1,0:T(8,128)(2,1)S(1)},...) custom-call(bf16[256,1152]{1,0:T(8,128)(2,1)S(1)} %collective-permut, ...), custom_call_target="tpu_custom_call" | custom-call | tf_op jit(solution)/shard_map/pallas_call | solution.py:251
  13.8 2.1 %collective-permute-start.9 = (bf16[128,1152]{1,0:T(8,128)(2,1)S(1)}, bf16[128,1152]{1,0:T(8,128)(2,1)S(1)}, u32[]{:S(2)}, u32[]{:S(2)}) collective-permute-start(bf16[128,1152]{1,0:T(8,128)(2,1)S(1)} %get-tuple-element.119), channel_id=1, source_target_pairs={{0,2},{1,3},{2,0},{3,1},{4,6},{5,7},{6,4},{7,5},{8,10},{9,11},{10,... | collective-permute-start | bytes 884744 | tf_op jit(solution)/shard_map/ppermute | solution.py:264
  15.9 2.7 %shard_map.76 = (f32[256,1152]{1,0:T(8,128)S(1)}, bf16[256,1152]{1,0:T(8,128)(2,1)S(1)}, bf16[512,256]{1,0:T(8,128)(2,1)S(1)}, f32[512,1152]{1,0:T(8,128)S(1)}) custom-call(bf16[128,1152]{1,0:T(8,128)(2,1)S(1)} %collective-permute-done.3.refs_0_, bf16[64,1152]{1,0:T(8,128)(2,1)S(1)} %collective-permute-done.4.refs_1_, ...), custom_call_target="tpu_custom_call" | custom-call | tf_op jit(solution)/shard_map/pallas_call | solution.py:251
  18.6 2.6 %shard_map.77 = (f32[512,1152]{1,0:T(8,128)S(1)}, bf16[576,512]{1,0:T(8,128)(2,1)S(1)}, bf16[288,512]{1,0:T(8,128)(2,1)S(1)}) custom-call(s32[2]{0:T(128)S(1)} %pad_add_fusion.place, bf16[256,1152]{1,0:T(8,128)(2,1)S(1)} %get-tuple-element.64.t0, bf16[256,1152]{1,0:T(8,128)(2,1)S(1)} %collective-permute-done.1.t1, ...), custom_call_target="tpu_custom_call" | custom-call | tf_op jit(solution)/shard_map/pallas_call | solution.py:251
  21.8 0.9 %collective-permute-start.12 = (bf16[128,1152]{1,0:T(8,128)(2,1)S(1)}, bf16[128,1152]{1,0:T(8,128)(2,1)S(1)}, u32[]{:S(2)}, u32[]{:S(2)}) collective-permute-start(bf16[128,1152]{1,0:T(8,128)(2,1)S(1)} %get-tuple-element.118), channel_id=1, source_target_pairs={{0,2},{1,3},{2,0},{3,1},{4,6},{5,7},{6,4},{7,5},{8,10},{9,11},{10,... | collective-permute-start | bytes 884744 | tf_op jit(solution)/shard_map/ppermute | solution.py:264
  22.9 3.9 %shard_map.78 = (f32[256,1152]{1,0:T(8,128)S(1)}, bf16[256,1152]{1,0:T(8,128)(2,1)S(1)}, bf16[512,256]{1,0:T(8,128)(2,1)S(1)}, bf16[512,1152]{1,0:T(8,128)(2,1)S...) custom-call(bf16[128,1152]{1,0:T(8,128)(2,1)S(1)} %collective-permut, ...), custom_call_target="tpu_custom_call" | custom-call | tf_op jit(solution)/shard_map/pallas_call | solution.py:251
  27.4 1.5 %collective-permute-start.8 = (bf16[144,1152]{1,0:T(8,128)(2,1)S(1)}, bf16[144,1152]{1,0:T(8,128)(2,1)S(1)}, u32[]{:S(2)}, u32[]{:S(2)}) collective-permute-start(bf16[144,1152]{1,0:T(8,128)(2,1)S(1)} %get-tuple-element.79), channel_id=1, source_target_pairs={{0,4},{4,0},{8,12},{12,8},{16,20},{20,16},{24,28},{28,24},{1,5},{5... | collective-permute-start | bytes 995336 | tf_op jit(solution)/shard_map/ppermute | solution.py:264
  28.9 1.6 %collective-permute-start.15 = (bf16[144,1152]{1,0:T(8,128)(2,1)S(1)}, bf16[144,1152]{1,0:T(8,128)(2,1)S(1)}, u32[]{:S(2)}, u32[]{:S(2)}) collective-permute-start(bf16[144,1152]{1,0:T(8,128)(2,1)S(1)} %get-tuple-element.102), channel_id=1, source_target_pairs={{0,8},{4,12},{8,0},{12,4},{16,24},{20,28},{24,16},{28,20},{1,9},{5... | collective-permute-start | bytes 995336 | tf_op jit(solution)/shard_map/ppermute | solution.py:264
  30.5 1.8 %shard_map.80 = (f32[256,1152]{1,0:T(8,128)S(1)}, f32[256,1152]{1,0:T(8,128)S(1)}, bf16[288,512]{1,0:T(8,128)(2,1)S(1)}) custom-call(s32[2]{0:T(128)S(1)} %pad_add_fusion.place, bf16[128,1152]{1,0:T(8,128)(2,1)S(1)} %collective-permute-done.3.refs_0_, bf16[64,1152]{1,0:T(8,128)(2,1)S(1)} %collective-permute-done.4.refs_1_, ...), custom_call_target="tpu_custom_call" | custom-call | tf_op jit(solution)/shard_map/pallas_call | solution.py:251
  32.8 1.9 %shard_map.79 = (bf16[256,1152]{1,0:T(8,128)(2,1)S(1)}, bf16[256,512]{1,0:T(8,128)(2,1)S(1)}, bf16[256,512]{1,0:T(8,128)(2,1)S(1)}) custom-call(bf16[128,1152]{1,0:T(8,128)(2,1)S(1)} %collective-permute-done.9.refs_0_, bf16[64,1152]{1,0:T(8,128)(2,1)S(1)} %collective-permute-done.10.refs_1_, bf16[64,1152]{1,0:T(8,128)(2,1)S(1)} %collective-permute-done.11.refs_2_, ...), custom_call_target="tpu_custom_call" | custom-call | tf_op jit(solution)/shard_map/pallas_call | solution.py:251
  35.3 0.9 %collective-permute-done.13.refs_1_ = bf16[64,1152]{1,0:T(8,128)(2,1)S(1)} collective-permute-done((bf16[64,1152]{1,0:T(8,128)(2,1)S(1)}, bf16[64,1152]{1,0:T(8,128)(2,1)S(1)}, u32[]{:S(2)}, u32[]{:S(2)}) %collective-permute-start.13) | collective-permute-done | bytes 147488 | tf_op jit(solution)/shard_map/ppermute | solution.py:264
  36.4 1.9 %shard_map.81 = (bf16[256,1152]{1,0:T(8,128)(2,1)S(1)}, bf16[256,512]{1,0:T(8,128)(2,1)S(1)}, bf16[256,512]{1,0:T(8,128)(2,1)S(1)}) custom-call(bf16[128,1152]{1,0:T(8,128)(2,1)S(1)} %collective-permute-done.12.refs_0_, bf16[64,1152]{1,0:T(8,128)(2,1)S(1)} %collective-permute-done.13.refs_1_, bf16[64,1152]{1,0:T(8,128)(2,1)S(1)} %collective-permute-done.14.refs_2_, ...), custom_call_target="tpu_custom_call" | custom-call | tf_op jit(solution)/shard_map/pallas_call | solution.py:251
  38.4 3.6 %shard_map.82 = (bf16[72,1152]{1,0:T(8,128)(2,1)S(1)}, bf16[72,1152]{1,0:T(8,128)(2,1)S(1)}, bf16[72,1152]{1,0:T(8,128)(2,1)S(1)}, bf16[72,1152]{1,0:T(8,128)(2,1)S(1)}, bf16[256,1152]{1,0:T(8,128)(2,1)S(1)}) custom-call(bf16[256,1152]{1,0:T(8,128)(2,1)S(1)} %get-tuple-element.84.x_2, bf16[256,512]{1,0:T(8,128)(2,1)S(1)} %get-tuple-element.85.w_2a, ...), custom_call_target="tpu_custom_call" | custom-call | tf_op jit(solution)/shard_map/pallas_call | solution.py:251
  42.0 1.6 %collective-permute-start.22 = (bf16[72,1152]{1,0:T(8,128)(2,1)S(1)}, bf16[72,1152]{1,0:T(8,128)(2,1)S(1)}, u32[]{:S(2)}, u32[]{:S(2)}) collective-permute-start(bf16[72,1152]{1,0:T(8,128)(2,1)S(1)} %get-tuple-element.110), channel_id=1, source_target_pairs={{0,4},{4,0},{8,12},{12,8},{16,20},{20,16},{24,28},{28,24},{1,5},{5... | collective-permute-start | bytes 497672 | tf_op jit(solution)/shard_map/ppermute | solution.py:264
  43.6 1.6 %collective-permute-start.23 = (bf16[72,1152]{1,0:T(8,128)(2,1)S(1)}, bf16[72,1152]{1,0:T(8,128)(2,1)S(1)}, u32[]{:S(2)}, u32[]{:S(2)}) collective-permute-start(bf16[72,1152]{1,0:T(8,128)(2,1)S(1)} %get-tuple-element.112), channel_id=1, source_target_pairs={{0,8},{4,12},{8,0},{12,4},{16,24},{20,28},{24,16},{28,20},{1,9},{5... | collective-permute-start | bytes 497672 | tf_op jit(solution)/shard_map/ppermute | solution.py:264
  46.0 1.0 %collective-permute-start.17 = (bf16[72,1152]{1,0:T(8,128)(2,1)S(1)}, bf16[72,1152]{1,0:T(8,128)(2,1)S(1)}, u32[]{:S(2)}, u32[]{:S(2)}) collective-permute-start(bf16[72,1152]{1,0:T(8,128)(2,1)S(1)} %slice.9), channel_id=1, source_target_pairs={{0,2},{1,3},{2,0},{3,1},{4,6},{5,7},{6,4},{7,5},{8,10},{9,11},{10,... | collective-permute-start | bytes 497672 | tf_op jit(solution)/shard_map/ppermute | solution.py:264
  47.0 2.0 %shard_map.84 = f32[256,1152]{1,0:T(8,128)} custom-call(bf16[256,1152]{1,0:T(8,128)(2,1)S(1)} %get-tuple-element.107.back, bf16[1152,1152]{1,0:T(8,128)(2,1)S(1)} %get-tuple-element.69.refs_3_.head), custom_call_target="tpu_custom_call" | custom-call | flops 1358954496 | tf_op jit(solution)/shard_map/pallas_call | solution.py:251
  49.0 2.0 %shard_map.83 = f32[256,1152]{1,0:T(8,128)} custom-call(bf16[512,1152]{1,0:T(8,128)(2,1)S(1)} %get-tuple-element.106.back, bf16[1152,1152]{1,0:T(8,128)(2,1)S(1)} %get-tuple-element.81.refs_3_.head), custom_call_target="tpu_custom_call" | custom-call | flops 1358954496 | tf_op jit(solution)/shard_map/pallas_call | solution.py:251
  51.5 2.7 %collective-permute-start.18 = (bf16[72,1152]{1,0:T(8,128)(2,1)S(1)}, bf16[72,1152]{1,0:T(8,128)(2,1)S(1)}, u32[]{:S(2)}, u32[]{:S(2)}) collective-permute-start(bf16[72,1152]{1,0:T(8,128)(2,1)S(1)} %add_convert_fusion.4), channel_id=1, source_target_pairs={{0,16},{4,20},{8,24},{12,28},{16,0},{20,4},{24,8},{28,12},{1,17},{... | collective-permute-start | bytes 497672 | tf_op jit(solution)/shard_map/ppermute | solution.py:264
  54.2 6.6 %collective-permute-done.18 = bf16[72,1152]{1,0:T(8,128)(2,1)S(1)} collective-permute-done((bf16[72,1152]{1,0:T(8,128)(2,1)S(1)}, bf16[72,1152]{1,0:T(8,128)(2,1)S(1)}, u32[]{:S(2)}, u32[]{:S(2)}) %collective-permute-start.18) | collective-permute-done | bytes 165920 | tf_op jit(solution)/shard_map/ppermute | solution.py:264
  61.0 5.0 %collective-permute-start.21 = (bf16[72,1152]{1,0:T(8,128)(2,1)S(1)}, bf16[72,1152]{1,0:T(8,128)(2,1)S(1)}, u32[]{:S(2)}, u32[]{:S(2)}) collective-permute-start(bf16[72,1152]{1,0:T(8,128)(2,1)S(1)} %add_convert_fusion.3.h0), channel_id=1, source_target_pairs={{0,12},{4,8},{8,4},{12,0},{16,28},{20,24},{24,20},{28,16},{1,13},{... | collective-permute-start | bytes 497672 | tf_op jit(solution)/shard_map/ppermute | solution.py:264
  66.0 2.3 %collective-permute-start.19 = (bf16[72,1152]{1,0:T(8,128)(2,1)S(1)}, bf16[72,1152]{1,0:T(8,128)(2,1)S(1)}, u32[]{:S(2)}, u32[]{:S(2)}) collective-permute-start(bf16[72,1152]{1,0:T(8,128)(2,1)S(1)} %add_convert_fusion.3.h0), channel_id=1, source_target_pairs={{0,4},{4,0},{8,12},{12,8},{16,20},{20,16},{24,28},{28,24},{1,5},{5... | collective-permute-start | bytes 497672 | tf_op jit(solution)/shard_map/ppermute | solution.py:264
  68.3 0.8 %collective-permute-done.25 = bf16[72,1152]{1,0:T(8,128)(2,1)S(1)} collective-permute-done((bf16[72,1152]{1,0:T(8,128)(2,1)S(1)}, bf16[72,1152]{1,0:T(8,128)(2,1)S(1)}, u32[]{:S(2)}, u32[]{:S(2)}) %collective-permute-start.25) | collective-permute-done | bytes 165920 | tf_op jit(solution)/shard_map/ppermute | solution.py:264
  69.1 3.5 %collective-permute-done.21.h3 = bf16[72,1152]{1,0:T(8,128)(2,1)S(1)} collective-permute-done((bf16[72,1152]{1,0:T(8,128)(2,1)S(1)}, bf16[72,1152]{1,0:T(8,128)(2,1)S(1)}, u32[]{:S(2)}, u32[]{:S(2)}) %collective-permute-start.21) | collective-permute-done | bytes 165920 | tf_op jit(solution)/shard_map/ppermute | solution.py:264
  72.7 1.3 %collective-permute-start.26 = (bf16[72,1152]{1,0:T(8,128)(2,1)S(1)}, bf16[72,1152]{1,0:T(8,128)(2,1)S(1)}, u32[]{:S(2)}, u32[]{:S(2)}) collective-permute-start(bf16[72,1152]{1,0:T(8,128)(2,1)S(1)} %add_convert_fusion.1.h0), channel_id=1, source_target_pairs={{0,4},{4,0},{8,12},{12,8},{16,20},{20,16},{24,28},{28,24},{1,5},{5... | collective-permute-start | bytes 497672 | tf_op jit(solution)/shard_map/ppermute | solution.py:264
  74.7 1.5 %collective-permute-start.28 = (bf16[72,1152]{1,0:T(8,128)(2,1)S(1)}, bf16[72,1152]{1,0:T(8,128)(2,1)S(1)}, u32[]{:S(2)}, u32[]{:S(2)}) collective-permute-start(bf16[72,1152]{1,0:T(8,128)(2,1)S(1)} %add_convert_fusion.1.h0), channel_id=1, source_target_pairs={{0,12},{4,8},{8,4},{12,0},{16,28},{20,24},{24,20},{28,16},{1,13},{... | collective-permute-start | bytes 497672 | tf_op jit(solution)/shard_map/ppermute | solution.py:264
  76.3 1.7 %shard_map.85 = f32[288,1152]{1,0:T(8,128)} custom-call(s32[2]{0:T(128)S(1)} %pad_add_fusion.place, bf16[72,1152]{1,0:T(8,128)(2,1)S(1)} %add_convert_fusion.3.h0, bf16[72,1152]{1,0:T(8,128)(2,1)S(1)} %collective-permute-done.19.h1, bf16[72,1152]{1,0:T(8,128)(2,1)S(1)} %collective-permute-done.20.h2, bf16[72,1152]{1,0:T(8,128)(2,1)S(1)} %collective-permute-done.21.h3), custom_call_target="tpu_custom_call" | custom-call | tf_op jit(solution)/shard_map/pallas_call | solution.py:251
  78.0 1.9 %collective-permute-done.26.h1 = bf16[72,1152]{1,0:T(8,128)(2,1)S(1)} collective-permute-done((bf16[72,1152]{1,0:T(8,128)(2,1)S(1)}, bf16[72,1152]{1,0:T(8,128)(2,1)S(1)}, u32[]{:S(2)}, u32[]{:S(2)}) %collective-permute-start.26) | collective-permute-done | bytes 165920 | tf_op jit(solution)/shard_map/ppermute | solution.py:264
  79.9 2.4 %collective-permute-done.28.h3 = bf16[72,1152]{1,0:T(8,128)(2,1)S(1)} collective-permute-done((bf16[72,1152]{1,0:T(8,128)(2,1)S(1)}, bf16[72,1152]{1,0:T(8,128)(2,1)S(1)}, u32[]{:S(2)}, u32[]{:S(2)}) %collective-permute-start.28) | collective-permute-done | bytes 165920 | tf_op jit(solution)/shard_map/ppermute | solution.py:264
  82.3 1.7 %shard_map.86 = f32[288,1152]{1,0:T(8,128)} custom-call(s32[2]{0:T(128)S(1)} %pad_add_fusion.place, bf16[72,1152]{1,0:T(8,128)(2,1)S(1)} %add_convert_fusion.1.h0, bf16[72,1152]{1,0:T(8,128)(2,1)S(1)} %collective-permute-done.26.h1, bf16[72,1152]{1,0:T(8,128)(2,1)S(1)} %collective-permute-done.27.h2, bf16[72,1152]{1,0:T(8,128)(2,1)S(1)} %collective-permute-done.28.h3), custom_call_target="tpu_custom_call" | custom-call | tf_op jit(solution)/shard_map/pallas_call | solution.py:251
  (53 shorter events, 7.0 us)
Async XLA Ops:
  0.7 4.7 %collective-permute-start.1 = (bf16[256,1152]{1,0:T(8,128)(2,1)}, bf16[256,1152]{1,0:T(8,128)(2,1)S(1)}, u32[]{:S(2)}, u32[]{:S(2)}) collective-permute-start(bf16[256,1152]{1,0:T(8,128)(2,1)} %t0_far), channel_id=1, source_target_pairs={{0,1},{1,0},{2,3},{3,2},{4,5},{5,4},{6,7},{7,6},{8,9},{9,8},{10,11... | collective-permute-start | bytes 1769480 | tf_op jit(solution)/shard_map/ppermute | solution.py:264
  1.2 4.3 %collective-permute-start.2 = (bf16[256,1152]{1,0:T(8,128)(2,1)}, bf16[256,1152]{1,0:T(8,128)(2,1)S(1)}, u32[]{:S(2)}, u32[]{:S(2)}) collective-permute-start(bf16[256,1152]{1,0:T(8,128)(2,1)} %i0_far), channel_id=1, source_target_pairs={{0,1},{1,0},{2,3},{3,2},{4,5},{5,4},{6,7},{7,6},{8,9},{9,8},{10,11... | collective-permute-start | bytes 1769480 | tf_op jit(solution)/shard_map/ppermute | solution.py:264
  2.3 10.8 %collective-permute-start.3 = (bf16[128,1152]{1,0:T(8,128)(2,1)S(1)}, bf16[128,1152]{1,0:T(8,128)(2,1)S(1)}, u32[]{:S(2)}, u32[]{:S(2)}) collective-permute-start(bf16[128,1152]{1,0:T(8,128)(2,1)S(1)} %get-tuple-element.120), channel_id=1, source_target_pairs={{0,2},{1,3},{2,0},{3,1},{4,6},{5,7},{6,4},{7,5},{8,10},{9,11},{10,... | collective-permute-start | bytes 884744 | tf_op jit(solution)/shard_map/ppermute | solution.py:264
  5.3 8.4 %copy-start = (bf16[256,1152]{1,0:T(8,128)(2,1)S(1)}, bf16[256,1152]{1,0:T(8,128)(2,1)}, u32[]{:S(2)}) copy-start(bf16[256,1152]{1,0:T(8,128)(2,1)} %i0_far) | copy-start | bytes 1769476
  5.3 15.9 %collective-permute-start = (bf16[128,1152]{1,0:T(8,128)(2,1)S(1)}, bf16[128,1152]{1,0:T(8,128)(2,1)S(1)}, u32[]{:S(2)}, u32[]{:S(2)}) collective-permute-start(bf16[128,1152]{1,0:T(8,128)(2,1)S(1)} %get-tuple-element.121), channel_id=1, source_target_pairs={{0,2},{1,3},{2,0},{3,1},{4,6},{5,7},{6,4},{7,5},{8,10},{9,11},{10,... | collective-permute-start | bytes 884744 | tf_op jit(solution)/shard_map/ppermute | solution.py:264
  13.2 2.8 %collective-permute-start.4 = (bf16[64,1152]{1,0:T(8,128)(2,1)S(1)}, bf16[64,1152]{1,0:T(8,128)(2,1)S(1)}, u32[]{:S(2)}, u32[]{:S(2)}) collective-permute-start(bf16[64,1152]{1,0:T(8,128)(2,1)S(1)} %get-tuple-element.129), channel_id=1, source_target_pairs={{0,1},{1,0},{2,3},{3,2},{4,5},{5,4},{6,7},{7,6},{8,9},{9,8},{10,11... | collective-permute-start | bytes 442376 | tf_op jit(solution)/shard_map/ppermute | solution.py:264
  13.2 2.7 %collective-permute-start.5 = (bf16[64,1152]{1,0:T(8,128)(2,1)S(1)}, bf16[64,1152]{1,0:T(8,128)(2,1)S(1)}, u32[]{:S(2)}, u32[]{:S(2)}) collective-permute-start(bf16[64,1152]{1,0:T(8,128)(2,1)S(1)} %get-tuple-element.128), channel_id=1, source_target_pairs={{0,1},{1,0},{2,3},{3,2},{4,5},{5,4},{6,7},{7,6},{8,9},{9,8},{10,11... | collective-permute-start | bytes 442376 | tf_op jit(solution)/shard_map/ppermute | solution.py:264
  13.8 13.0 %collective-permute-start.9 = (bf16[128,1152]{1,0:T(8,128)(2,1)S(1)}, bf16[128,1152]{1,0:T(8,128)(2,1)S(1)}, u32[]{:S(2)}, u32[]{:S(2)}) collective-permute-start(bf16[128,1152]{1,0:T(8,128)(2,1)S(1)} %get-tuple-element.119), channel_id=1, source_target_pairs={{0,2},{1,3},{2,0},{3,1},{4,6},{5,7},{6,4},{7,5},{8,10},{9,11},{10,... | collective-permute-start | bytes 884744 | tf_op jit(solution)/shard_map/ppermute | solution.py:264
  21.2 1.5 %collective-permute-start.6 = (bf16[64,1152]{1,0:T(8,128)(2,1)S(1)}, bf16[64,1152]{1,0:T(8,128)(2,1)S(1)}, u32[]{:S(2)}, u32[]{:S(2)}) collective-permute-start(bf16[64,1152]{1,0:T(8,128)(2,1)S(1)} %get-tuple-element.127), channel_id=1, source_target_pairs={{0,1},{1,0},{2,3},{3,2},{4,5},{5,4},{6,7},{7,6},{8,9},{9,8},{10,11... | collective-permute-start | bytes 442376 | tf_op jit(solution)/shard_map/ppermute | solution.py:264
  21.3 1.6 %collective-permute-start.7 = (bf16[64,1152]{1,0:T(8,128)(2,1)S(1)}, bf16[64,1152]{1,0:T(8,128)(2,1)S(1)}, u32[]{:S(2)}, u32[]{:S(2)}) collective-permute-start(bf16[64,1152]{1,0:T(8,128)(2,1)S(1)} %get-tuple-element.126), channel_id=1, source_target_pairs={{0,1},{1,0},{2,3},{3,2},{4,5},{5,4},{6,7},{7,6},{8,9},{9,8},{10,11... | collective-permute-start | bytes 442376 | tf_op jit(solution)/shard_map/ppermute | solution.py:264
  21.8 12.9 %collective-permute-start.12 = (bf16[128,1152]{1,0:T(8,128)(2,1)S(1)}, bf16[128,1152]{1,0:T(8,128)(2,1)S(1)}, u32[]{:S(2)}, u32[]{:S(2)}) collective-permute-start(bf16[128,1152]{1,0:T(8,128)(2,1)S(1)} %get-tuple-element.118), channel_id=1, source_target_pairs={{0,2},{1,3},{2,0},{3,1},{4,6},{5,7},{6,4},{7,5},{8,10},{9,11},{10,... | collective-permute-start | bytes 884744 | tf_op jit(solution)/shard_map/ppermute | solution.py:264
  26.8 5.5 %collective-permute-start.10 = (bf16[64,1152]{1,0:T(8,128)(2,1)S(1)}, bf16[64,1152]{1,0:T(8,128)(2,1)S(1)}, u32[]{:S(2)}, u32[]{:S(2)}) collective-permute-start(bf16[64,1152]{1,0:T(8,128)(2,1)S(1)} %get-tuple-element.125), channel_id=1, source_target_pairs={{0,1},{1,0},{2,3},{3,2},{4,5},{5,4},{6,7},{7,6},{8,9},{9,8},{10,11... | collective-permute-start | bytes 442376 | tf_op jit(solution)/shard_map/ppermute | solution.py:264
  27.2 5.6 %collective-permute-start.11 = (bf16[64,1152]{1,0:T(8,128)(2,1)S(1)}, bf16[64,1152]{1,0:T(8,128)(2,1)S(1)}, u32[]{:S(2)}, u32[]{:S(2)}) collective-permute-start(bf16[64,1152]{1,0:T(8,128)(2,1)S(1)} %get-tuple-element.124), channel_id=1, source_target_pairs={{0,1},{1,0},{2,3},{3,2},{4,5},{5,4},{6,7},{7,6},{8,9},{9,8},{10,11... | collective-permute-start | bytes 442376 | tf_op jit(solution)/shard_map/ppermute | solution.py:264
  27.4 17.7 %collective-permute-start.8 = (bf16[144,1152]{1,0:T(8,128)(2,1)S(1)}, bf16[144,1152]{1,0:T(8,128)(2,1)S(1)}, u32[]{:S(2)}, u32[]{:S(2)}) collective-permute-start(bf16[144,1152]{1,0:T(8,128)(2,1)S(1)} %get-tuple-element.79), channel_id=1, source_target_pairs={{0,4},{4,0},{8,12},{12,8},{16,20},{20,16},{24,28},{28,24},{1,5},{5... | collective-permute-start | bytes 995336 | tf_op jit(solution)/shard_map/ppermute | solution.py:264
  28.9 16.6 %collective-permute-start.15 = (bf16[144,1152]{1,0:T(8,128)(2,1)S(1)}, bf16[144,1152]{1,0:T(8,128)(2,1)S(1)}, u32[]{:S(2)}, u32[]{:S(2)}) collective-permute-start(bf16[144,1152]{1,0:T(8,128)(2,1)S(1)} %get-tuple-element.102), channel_id=1, source_target_pairs={{0,8},{4,12},{8,0},{12,4},{16,24},{20,28},{24,16},{28,20},{1,9},{5... | collective-permute-start | bytes 995336 | tf_op jit(solution)/shard_map/ppermute | solution.py:264
  32.3 13.5 %collective-permute-start.16 = (bf16[144,1152]{1,0:T(8,128)(2,1)S(1)}, bf16[144,1152]{1,0:T(8,128)(2,1)S(1)}, u32[]{:S(2)}, u32[]{:S(2)}) collective-permute-start(bf16[144,1152]{1,0:T(8,128)(2,1)S(1)} %get-tuple-element.104), channel_id=1, source_target_pairs={{0,12},{4,8},{8,4},{12,0},{16,28},{20,24},{24,20},{28,16},{1,13},{... | collective-permute-start | bytes 995336 | tf_op jit(solution)/shard_map/ppermute | solution.py:264
  34.8 1.4 %collective-permute-start.13 = (bf16[64,1152]{1,0:T(8,128)(2,1)S(1)}, bf16[64,1152]{1,0:T(8,128)(2,1)S(1)}, u32[]{:S(2)}, u32[]{:S(2)}) collective-permute-start(bf16[64,1152]{1,0:T(8,128)(2,1)S(1)} %get-tuple-element.123), channel_id=1, source_target_pairs={{0,1},{1,0},{2,3},{3,2},{4,5},{5,4},{6,7},{7,6},{8,9},{9,8},{10,11... | collective-permute-start | bytes 442376 | tf_op jit(solution)/shard_map/ppermute | solution.py:264
  34.9 1.6 %collective-permute-start.14 = (bf16[64,1152]{1,0:T(8,128)(2,1)S(1)}, bf16[64,1152]{1,0:T(8,128)(2,1)S(1)}, u32[]{:S(2)}, u32[]{:S(2)}) collective-permute-start(bf16[64,1152]{1,0:T(8,128)(2,1)S(1)} %get-tuple-element.122), channel_id=1, source_target_pairs={{0,1},{1,0},{2,3},{3,2},{4,5},{5,4},{6,7},{7,6},{8,9},{9,8},{10,11... | collective-permute-start | bytes 442376 | tf_op jit(solution)/shard_map/ppermute | solution.py:264
  42.0 12.1 %collective-permute-start.22 = (bf16[72,1152]{1,0:T(8,128)(2,1)S(1)}, bf16[72,1152]{1,0:T(8,128)(2,1)S(1)}, u32[]{:S(2)}, u32[]{:S(2)}) collective-permute-start(bf16[72,1152]{1,0:T(8,128)(2,1)S(1)} %get-tuple-element.110), channel_id=1, source_target_pairs={{0,4},{4,0},{8,12},{12,8},{16,20},{20,16},{24,28},{28,24},{1,5},{5... | collective-permute-start | bytes 497672 | tf_op jit(solution)/shard_map/ppermute | solution.py:264
  43.6 10.6 %collective-permute-start.23 = (bf16[72,1152]{1,0:T(8,128)(2,1)S(1)}, bf16[72,1152]{1,0:T(8,128)(2,1)S(1)}, u32[]{:S(2)}, u32[]{:S(2)}) collective-permute-start(bf16[72,1152]{1,0:T(8,128)(2,1)S(1)} %get-tuple-element.112), channel_id=1, source_target_pairs={{0,8},{4,12},{8,0},{12,4},{16,24},{20,28},{24,16},{28,20},{1,9},{5... | collective-permute-start | bytes 497672 | tf_op jit(solution)/shard_map/ppermute | solution.py:264
  45.2 9.0 %collective-permute-start.24 = (bf16[72,1152]{1,0:T(8,128)(2,1)S(1)}, bf16[72,1152]{1,0:T(8,128)(2,1)S(1)}, u32[]{:S(2)}, u32[]{:S(2)}) collective-permute-start(bf16[72,1152]{1,0:T(8,128)(2,1)S(1)} %get-tuple-element.114), channel_id=1, source_target_pairs={{0,12},{4,8},{8,4},{12,0},{16,28},{20,24},{24,20},{28,16},{1,13},{... | collective-permute-start | bytes 497672 | tf_op jit(solution)/shard_map/ppermute | solution.py:264
  46.0 5.4 %collective-permute-start.17 = (bf16[72,1152]{1,0:T(8,128)(2,1)S(1)}, bf16[72,1152]{1,0:T(8,128)(2,1)S(1)}, u32[]{:S(2)}, u32[]{:S(2)}) collective-permute-start(bf16[72,1152]{1,0:T(8,128)(2,1)S(1)} %slice.9), channel_id=1, source_target_pairs={{0,2},{1,3},{2,0},{3,1},{4,6},{5,7},{6,4},{7,5},{8,10},{9,11},{10,... | collective-permute-start | bytes 497672 | tf_op jit(solution)/shard_map/ppermute | solution.py:264
  51.5 9.4 %collective-permute-start.18 = (bf16[72,1152]{1,0:T(8,128)(2,1)S(1)}, bf16[72,1152]{1,0:T(8,128)(2,1)S(1)}, u32[]{:S(2)}, u32[]{:S(2)}) collective-permute-start(bf16[72,1152]{1,0:T(8,128)(2,1)S(1)} %add_convert_fusion.4), channel_id=1, source_target_pairs={{0,16},{4,20},{8,24},{12,28},{16,0},{20,4},{24,8},{28,12},{1,17},{... | collective-permute-start | bytes 497672 | tf_op jit(solution)/shard_map/ppermute | solution.py:264
  60.9 8.2 %collective-permute-start.25 = (bf16[72,1152]{1,0:T(8,128)(2,1)S(1)}, bf16[72,1152]{1,0:T(8,128)(2,1)S(1)}, u32[]{:S(2)}, u32[]{:S(2)}) collective-permute-start(bf16[72,1152]{1,0:T(8,128)(2,1)S(1)} %add_convert_fusion.2), channel_id=1, source_target_pairs={{0,16},{4,20},{8,24},{12,28},{16,0},{20,4},{24,8},{28,12},{1,17},{... | collective-permute-start | bytes 497672 | tf_op jit(solution)/shard_map/ppermute | solution.py:264
  61.0 11.7 %collective-permute-start.21 = (bf16[72,1152]{1,0:T(8,128)(2,1)S(1)}, bf16[72,1152]{1,0:T(8,128)(2,1)S(1)}, u32[]{:S(2)}, u32[]{:S(2)}) collective-permute-start(bf16[72,1152]{1,0:T(8,128)(2,1)S(1)} %add_convert_fusion.3.h0), channel_id=1, source_target_pairs={{0,12},{4,8},{8,4},{12,0},{16,28},{20,24},{24,20},{28,16},{1,13},{... | collective-permute-start | bytes 497672 | tf_op jit(solution)/shard_map/ppermute | solution.py:264
  66.0 10.3 %collective-permute-start.19 = (bf16[72,1152]{1,0:T(8,128)(2,1)S(1)}, bf16[72,1152]{1,0:T(8,128)(2,1)S(1)}, u32[]{:S(2)}, u32[]{:S(2)}) collective-permute-start(bf16[72,1152]{1,0:T(8,128)(2,1)S(1)} %add_convert_fusion.3.h0), channel_id=1, source_target_pairs={{0,4},{4,0},{8,12},{12,8},{16,20},{20,16},{24,28},{28,24},{1,5},{5... | collective-permute-start | bytes 497672 | tf_op jit(solution)/shard_map/ppermute | solution.py:264
  68.3 8.0 %collective-permute-start.20 = (bf16[72,1152]{1,0:T(8,128)(2,1)S(1)}, bf16[72,1152]{1,0:T(8,128)(2,1)S(1)}, u32[]{:S(2)}, u32[]{:S(2)}) collective-permute-start(bf16[72,1152]{1,0:T(8,128)(2,1)S(1)} %add_convert_fusion.3.h0), channel_id=1, source_target_pairs={{0,8},{4,12},{8,0},{12,4},{16,24},{20,28},{24,16},{28,20},{1,9},{5... | collective-permute-start | bytes 497672 | tf_op jit(solution)/shard_map/ppermute | solution.py:264
  72.7 7.2 %collective-permute-start.26 = (bf16[72,1152]{1,0:T(8,128)(2,1)S(1)}, bf16[72,1152]{1,0:T(8,128)(2,1)S(1)}, u32[]{:S(2)}, u32[]{:S(2)}) collective-permute-start(bf16[72,1152]{1,0:T(8,128)(2,1)S(1)} %add_convert_fusion.1.h0), channel_id=1, source_target_pairs={{0,4},{4,0},{8,12},{12,8},{16,20},{20,16},{24,28},{28,24},{1,5},{5... | collective-permute-start | bytes 497672 | tf_op jit(solution)/shard_map/ppermute | solution.py:264
  73.9 5.9 %collective-permute-start.27 = (bf16[72,1152]{1,0:T(8,128)(2,1)S(1)}, bf16[72,1152]{1,0:T(8,128)(2,1)S(1)}, u32[]{:S(2)}, u32[]{:S(2)}) collective-permute-start(bf16[72,1152]{1,0:T(8,128)(2,1)S(1)} %add_convert_fusion.1.h0), channel_id=1, source_target_pairs={{0,8},{4,12},{8,0},{12,4},{16,24},{20,28},{24,16},{28,20},{1,9},{5... | collective-permute-start | bytes 497672 | tf_op jit(solution)/shard_map/ppermute | solution.py:264
  74.7 7.6 %collective-permute-start.28 = (bf16[72,1152]{1,0:T(8,128)(2,1)S(1)}, bf16[72,1152]{1,0:T(8,128)(2,1)S(1)}, u32[]{:S(2)}, u32[]{:S(2)}) collective-permute-start(bf16[72,1152]{1,0:T(8,128)(2,1)S(1)} %add_convert_fusion.1.h0), channel_id=1, source_target_pairs={{0,12},{4,8},{8,4},{12,0},{16,28},{20,24},{24,20},{28,16},{1,13},{... | collective-permute-start | bytes 497672 | tf_op jit(solution)/shard_map/ppermute | solution.py:264

commit v8 on v7

--- a/solution.py
+++ b/solution.py
@@ -12,6 +12,7 @@
 EPSILON = 1e-06
 QUAD = 4
 STRIP = 16
+LANES = 128
 F32 = jnp.float32
 BF16 = jnp.bfloat16
 
@@ -73,39 +74,47 @@
     return (dot_nt(image_back, image_head), dot_nt(text_back, text_head), heads[0], heads[1])
 
 
-def factor_of(p):
+def factor_of(ref, rows):
+    p = ref[rows, :]
     return lax.rsqrt(jnp.sum(p * p, axis=-1, keepdims=True) + EPSILON)
 
 
 def unit_rows(projected_ref, vectors_ref):
     for first in range(0, projected_ref.shape[0], STRIP):
-        p = projected_ref[first : first + STRIP, :]
-        vectors_ref[first : first + STRIP, :] = (p * factor_of(p)).astype(BF16)
+        rows = slice(first, first + STRIP)
+        factor = factor_of(projected_ref, rows)
+        vectors_ref[rows, :] = (projected_ref[rows, :] * factor).astype(BF16)
 
 
 def back_rows(projected_ref, gradient_ref, back_ref, at=0):
     for first in range(0, projected_ref.shape[0], STRIP):
-        p = projected_ref[first : first + STRIP, :]
-        g = gradient_ref[at + first : at + first + STRIP, :]
-        factor = factor_of(p)
-        along = factor * factor * factor * jnp.sum(p * g, axis=-1, keepdims=True)
-        back_ref[at + first : at + first + STRIP, :] = (factor * g - along * p).astype(BF16)
-
-
-def weights_of(dots, pairs_from=None):
-    score = SCORE_SCALE * dots + SCORE_BIAS
-    if pairs_from is None:
-        return (SCORE_SCALE * jax.nn.sigmoid(score)).astype(BF16)
-    row = pairs_from + lax.broadcasted_iota(jnp.int32, dots.shape, 0)
-    same = row == lax.broadcasted_iota(jnp.int32, dots.shape, 1)
-    value = jax.nn.sigmoid(jnp.where(same, -score, score))
-    return (jnp.where(same, -SCORE_SCALE, SCORE_SCALE) * value).astype(BF16)
+        rows, target = slice(first, first + STRIP), slice(at + first, at + first + STRIP)
+        factor = factor_of(projected_ref, rows)
+        along = jnp.sum(projected_ref[rows, :] * gradient_ref[target, :], axis=-1, keepdims=True)
+        along = factor * factor * factor * along
+        back = factor * gradient_ref[target, :] - along * projected_ref[rows, :]
+        back_ref[target, :] = back.astype(BF16)
 
 
 def weight_rows(dots_ref, weights_ref, pairs_from=None):
+    half_scale = 0.5 * SCORE_SCALE
     for first in range(0, dots_ref.shape[0], STRIP):
-        pairs = None if pairs_from is None else pairs_from + first
-        weights_ref[first : first + STRIP, :] = weights_of(dots_ref[first : first + STRIP, :], pairs)
+        rows = slice(first, first + STRIP)
+        score = jnp.tanh(half_scale * dots_ref[rows, :] + 0.5 * SCORE_BIAS)
+        weights = half_scale + half_scale * score
+        if pairs_from is None:
+            weights_ref[rows, :] = weights.astype(BF16)
+            continue
+        pair = pairs_from + first
+        left = pair // LANES * LANES
+        right = min(left + LANES, weights.shape[1])
+        shape = (STRIP, right - left)
+        column = lax.broadcasted_iota(jnp.int32, shape, 1)
+        same = column == lax.broadcasted_iota(jnp.int32, shape, 0) + (pair - left)
+        middle = weights[:, left:right] - jnp.where(same, SCORE_SCALE, 0.0)
+        pieces = [weights[:, :left], middle, weights[:, right:]]
+        weights = jnp.concatenate([p for p in pieces if p.shape[1]], axis=1)
+        weights_ref[rows, :] = weights.astype(BF16)
 
 
 def one_hot(first, rows, width):
@@ -147,39 +156,38 @@
     copies[1].wait()
     q_a[:half, :] = dot_nn(t0[...], text_head[...])
     q_a[half:, :] = dot_nn(t1[...], text_head[...])
-    unit_rows(q_a, y_a)
     copies[2].wait()
     copies[3].wait()
     p_a[:half, :] = dot_nn(i0[...], image_head[...])
+    unit_rows(q_a, y_a)
     p_a[half:, :] = dot_nn(i1[...], image_head[...])
     unit_rows(p_a, x_a)
     dots[...] = dot_nt(x_a[...], y_a[...])
     weight_rows(dots, w_aa, 0)
 
 
-def near_pull_kernel(place, t0, t1, i0, i1, x_a, w_aa, gy_a, pick_i, pick_t):
+def rows_of(refs):
+    return jnp.concatenate([ref[...] for ref in refs], axis=0)
+
+
+def text_kernel(place, *refs):
+    *features, t0, t1, i0, i1, text_head, y_a, x_a, w_aa = refs[:-9]
+    q_2, y_2, w_a2, gx, gy_a, pick_i, pick_t, dots, near_gx = refs[-9:]
     half = t0.shape[0]
     rows = pick_t.shape[0]
+    q_2[...] = dot_nn(rows_of(features), text_head[...])
+    near_gx[...] = dot_nn(w_aa[...], y_a[...])
+    unit_rows(q_2, y_2)
+    dots[...] = dot_nt(x_a[...], y_2[...])
     pick = picker(place, rows, t0.shape[1], (0, 2))
     pick_i[:, :half] = dot_nt(pick, i0[...]).astype(BF16)
     pick_i[:, half:] = dot_nt(pick, i1[...]).astype(BF16)
+    weight_rows(dots, w_a2)
+    gx[...] = near_gx[...] + dot_nn(w_a2[...], y_2[...])
     pick = picker(place, rows, t0.shape[1], (0,))
     pick_t[:, :half] = dot_nt(pick, t0[...]).astype(BF16)
     pick_t[:, half:] = dot_nt(pick, t1[...]).astype(BF16)
     gy_a[...] = dot_tn(w_aa[...], x_a[...])
-
-
-def rows_of(refs):
-    return jnp.concatenate([ref[...] for ref in refs], axis=0)
-
-
-def text_kernel(*refs):
-    *features, text_head, y_a, x_a, w_aa, q_2, y_2, w_a2, gx, dots = refs
-    q_2[...] = dot_nn(rows_of(features), text_head[...])
-    unit_rows(q_2, y_2)
-    dots[...] = dot_nt(x_a[...], y_2[...])
-    weight_rows(dots, w_a2)
-    gx[...] = dot_nn(w_aa[...], y_a[...]) + dot_nn(w_a2[...], y_2[...])
 
 
 def image_kernel(*refs):
@@ -193,16 +201,7 @@
     split_head(dot_nn(pick_i[...], dp_a[...]), (h0, h1, h2, h3))
 
 
-def pull_kernel(place, *refs):
-    *features, x_a, w_a2, w_a3, gy_2, gy_3, pick_t = refs
-    gy_2[...] = dot_tn(w_a2[...], x_a[...])
-    gy_3[...] = dot_tn(w_a3[...], x_a[...])
-    pick = picker(place, pick_t.shape[0], x_a.shape[1], (0,))
-    pick_t[...] = dot_nt(pick, rows_of(features)).astype(BF16)
-
-
-def block_kernel(block, *refs):
-    *features, image_head, y_a, y_2, y_3, x_b, w_ba, w_bb, p_b, d_a, d_b = refs
+def block(number, features, image_head, y_a, y_2, y_3, x_b, w_ba, w_bb, p_b, d_a, d_b):
     half = x_b.shape[0]
     p_b[...] = dot_nn(rows_of(features), image_head[...])
     unit_rows(p_b, x_b)
@@ -210,23 +209,38 @@
     d_b[:, :half] = dot_nt(x_b[...], y_2[...])
     d_b[:, half:] = dot_nt(x_b[...], y_3[...])
     weight_rows(d_a, w_ba)
-    weight_rows(d_b, w_bb, block * half)
+    weight_rows(d_b, w_bb, number * half)
+
+
+def third_kernel(place, *refs):
+    *features, x_a, w_a2, w_a3, image_head, y_a, y_2, y_3 = refs[:-9]
+    x_b, w_ba, w_bb, gy_2, gy_3, pick_t, p_b, d_a, d_b = refs[-9:]
+    texts, images = features[: len(features) // 3 * 2], features[len(features) // 3 * 2 :]
+    gy_2[...] = dot_tn(w_a2[...], x_a[...])
+    block(0, images, image_head, y_a, y_2, y_3, x_b, w_ba, w_bb, p_b, d_a, d_b)
+    gy_3[...] = dot_tn(w_a3[...], x_a[...])
+    pick = picker(place, pick_t.shape[0], x_a.shape[1], (0,))
+    pick_t[...] = dot_nt(pick, rows_of(texts)).astype(BF16)
+
+
+def fourth_kernel(*refs):
+    block(1, refs[:-10], *refs[-10:])
 
 
 def last_kernel(
     x_2, w_2a, w_2b, x_3, w_3a, w_3b, q_a, q_2, q_3, gy_a_in, gy_2, gy_3, pick_a, pick_b,
-    h0, h1, h2, h3, dq_own, gy_a, gy_b, dq_a, dq_b,
+    h0, h1, h2, h3, dq_a, gy_a, gy_b, dq_b, near_head,
 ):
     half = x_2.shape[0]
     gy_a[...] = gy_a_in[...] + dot_tn(w_2a[...], x_2[...]) + dot_tn(w_3a[...], x_3[...])
+    gy_b[...] = dot_tn(w_2b[...], x_2[...]) + dot_tn(w_3b[...], x_3[...])
     back_rows(q_a, gy_a, dq_a)
-    gy_b[...] = dot_tn(w_2b[...], x_2[...]) + dot_tn(w_3b[...], x_3[...])
+    near_head[...] = dot_nn(pick_a[...], dq_a[...])
     gy_b[:half, :] += gy_2[...]
     gy_b[half:, :] += gy_3[...]
     back_rows(q_2, gy_b, dq_b, 0)
     back_rows(q_3, gy_b, dq_b, half)
-    dq_own[...] = dq_a[:half, :]
-    split_head(dot_nn(pick_a[...], dq_a[...]) + dot_nn(pick_b[...], dq_b[...]), (h0, h1, h2, h3))
+    split_head(near_head[...] + dot_nn(pick_b[...], dq_b[...]), (h0, h1, h2, h3))
 
 
 def grad_kernel(back, head, out):
@@ -315,18 +329,11 @@
         far=(t0, i0, text_head, image_head),
     )
     first = both(t2[0], w_aa, 2)
-    q_2, y_2, w_a2, gx = call(
+    q_2, y_2, w_a2, gx, gy_a, pick_i, pick_a = call(
         text_kernel,
-        [tall, tall_b, side_w, wide],
-        [side_dots],
-        (*first, text_head, y_a, x_a, w_aa),
-        8,
-    )
-    gy_a, pick_i, pick_a = call(
-        near_pull_kernel,
-        [wide, pick_two, pick_one],
-        [],
-        (t0, t1, i0, i1, after(x_a, gx), w_aa),
+        [tall, tall_b, side_w, wide, wide, pick_two, pick_one],
+        [side_dots, wide],
+        (*first, t0, t1, i0, i1, text_head, y_a, x_a, w_aa),
         8,
         place,
     )
@@ -339,43 +346,43 @@
         8,
     )
     image_others = [cuts(image_parts[k], mask=k) for k in range(1, QUAD)]
-    gy_2, gy_3, pick_b = call(
-        pull_kernel,
-        [tall, tall, pick_one],
-        [],
-        (*first, *second, x_a, w_a2, w_a3),
+    scratch = [tall, block_dots, block_dots]
+    x_2, w_2a, w_2b, gy_2, gy_3, pick_b = call(
+        third_kernel,
+        [tall_b, block_w, block_w, tall, tall, pick_one],
+        scratch,
+        (*first, *second, *both(i2[0], dp_a, 2), x_a, w_a2, w_a3, image_head, y_a, y_2, y_3),
         8,
         place,
     )
-    blocks = []
-    for block, rows in enumerate(i2):
-        blocks += call(
-            functools.partial(block_kernel, block),
-            [tall_b, block_w, block_w],
-            [tall, block_dots, block_dots],
-            (*both(rows, (blocks[-1], gy_2) if blocks else dp_a, 2), image_head, y_a, y_2, y_3),
-            8,
-        )
-    *text_parts, dq_own = call(
+    x_3, w_3a, w_3b = call(
+        fourth_kernel,
+        [tall_b, block_w, block_w],
+        scratch,
+        (*both(i2[1], gy_2, 2), image_head, y_a, y_2, y_3),
+        8,
+    )
+    blocks = (x_2, w_2a, w_2b, x_3, w_3a, w_3b)
+    *text_parts, dq_a = call(
         last_kernel,
-        [((part, width), BF16)] * QUAD + [tall_b],
-        [wide, wide, wide_b, wide_b],
+        [((part, width), BF16)] * QUAD + [wide_b],
+        [wide, wide, wide_b, ((rows_out, width), F32)],
         (*blocks, q_a, q_2, q_3, gy_a, gy_2, gy_3, pick_a, pick_b),
         14,
     )
     text_others = [cuts(text_parts[k], mask=k) for k in range(1, QUAD)]
-    image_others = [after(other, dq_own) for other in image_others]
+    image_others = [after(other, dq_a) for other in image_others]
     image_sum = add(image_parts[0], image_others)
     grads = [
         call(grad_kernel, [tall], [], (after(back, image_sum), head), 4, macs=2 * macs, keep=False)[0]
-        for back, head in ((dp_a, image_head), (dq_own, text_head))
+        for back, head in ((dp_a, image_head), (dq_a, text_head))
     ]
     image_sum = add(image_sum[:part], [after(loop(image_sum[part:], mask=2), grads)])
     text_sum = add(text_parts[0], [after(other, image_sum) for other in text_others])
     image_sum = add(image_sum, [cuts(image_sum, mask=QUAD)])
     image_pieces = spread(image_sum)
     text_sum = after(text_sum, image_sum)
-    text_sum = add(text_sum, [after(cuts(text_sum, mask=QUAD), image_pieces[-1])])
+    text_sum = add(text_sum, [after(cuts(text_sum, mask=QUAD), image_pieces[1])])
     image_out = placed(image_pieces)
     text_out = placed(spread(text_sum))
     return (*grads, image_out, text_out)

time: 84.1 us -> 84.2 us (level)
  waiting for transfers between devices: 18 us -> 20.2 us
  starting transfers between devices: 30.6 us -> 29 us
    ppermute x29, waiting for transfers between devices: 18 us -> 20.2 us  [swap(): return lax.ppermute(array, axis, [(i, i ^ mask) for i in range(size)])]
    ppermute x29, starting transfers between devices: 30.6 us -> 29 us  [swap(): return lax.ppermute(array, axis, [(i, i ^ mask) for i in range(size)])]
    pallas_call x12 -> x10, Pallas kernels: 32.8 us -> 32.3 us  [call(): pl.pallas_call(kernel, out_shape=[shape(s, t) for s, t in outs], in_specs...]
  transfers between devices with their start and end apart: 29 -> 29, of which waited for: 11 -> 11; matrix products, arithmetic and copies ran while one was open for 2% -> 2% of each run, Pallas kernels for 37% -> 36%
where the time goes in v8:
time: 84.2 us; the launch traced here: 84 us
  Pallas kernels  32.3 us (38%)
  starting transfers between devices  29 us (34%)
  waiting for transfers between devices  20.2 us (24%)
  local copies, waits for them, and re-layouts  1.26 us (1%)
    pallas_call x10, Pallas kernels, call(): pl.pallas_call(kernel, out_shape=[shape(s, t) for s, t in outs], in_specs...  32.3 us
    ppermute x29, starting transfers between devices, swap(): return lax.ppermute(array, axis, [(i, i ^ mask) for i in range(size)])  29 us
    ppermute x29, waiting for transfers between devices, swap(): return lax.ppermute(array, axis, [(i, i ^ mask) for i in range(size)])  20.2 us
  transfers between devices with their start and end apart: 29, of which 11 were waited for; matrix products, arithmetic and copies ran while one was open for 2% of the time, Pallas kernels for 36%

profile of v8, /device:TPU:0, one launch (start us, length us, event | category | flops | bytes accessed | tf_op | source)
XLA Modules:
  0.0 84.0 jit_solution(4038994398400143975)
XLA Ops:
  1.2 1.1 %fusion.1 = (bf16[128,1152]{1,0:T(8,128)(2,1)S(1)}, bf16[128,1152]{1,0:T(8,128)(2,1)S(1)}) fusion(bf16[256,1152]{1,0:T(8,128)(2,1)} %t0_far), kind=kLoop, calls=%fused_computation.7 | loop fusion | bytes 1179648 | tf_op jit(solution)/shard_map/split | solution.py:309
  2.3 3.0 %collective-permute-start.1 = (bf16[128,1152]{1,0:T(8,128)(2,1)S(1)}, bf16[128,1152]{1,0:T(8,128)(2,1)S(1)}, u32[]{:S(2)}, u32[]{:S(2)}) collective-permute-start(bf16[128,1152]{1,0:T(8,128)(2,1)S(1)} %get-tuple-element.118), channel_id=1, source_target_pairs={{0,2},{1,3},{2,0},{3,1},{4,6},{5,7},{6,4},{7,5},{8,10},{9,11},{10,... | collective-permute-start | bytes 884744 | tf_op jit(solution)/shard_map/ppermute | solution.py:278
  5.4 6.8 %shard_map.75 = (f32[512,1152]{1,0:T(8,128)S(1)}, bf16[512,1152]{1,0:T(8,128)(2,1)S(1)}, f32[512,1152]{1,0:T(8,128)S(1)}, bf16[512,1152]{1,0:T(8,128)(2,1)S(1)},...) custom-call(bf16[256,1152]{1,0:T(8,128)(2,1)S(1)} %collective-permut, ...), custom_call_target="tpu_custom_call" | custom-call | tf_op jit(solution)/shard_map/pallas_call | solution.py:265
  12.2 0.9 %collective-permute-done.1.refs_0_ = bf16[128,1152]{1,0:T(8,128)(2,1)S(1)} collective-permute-done((bf16[128,1152]{1,0:T(8,128)(2,1)S(1)}, bf16[128,1152]{1,0:T(8,128)(2,1)S(1)}, u32[]{:S(2)}, u32[]{:S(2)}) %collective-permute-start.1) | collective-permute-done | bytes 294944 | tf_op jit(solution)/shard_map/ppermute | solution.py:278
  13.8 2.1 %collective-permute-start.9 = (bf16[128,1152]{1,0:T(8,128)(2,1)S(1)}, bf16[128,1152]{1,0:T(8,128)(2,1)S(1)}, u32[]{:S(2)}, u32[]{:S(2)}) collective-permute-start(bf16[128,1152]{1,0:T(8,128)(2,1)S(1)} %get-tuple-element.117), channel_id=1, source_target_pairs={{0,2},{1,3},{2,0},{3,1},{4,6},{5,7},{6,4},{7,5},{8,10},{9,11},{10,... | collective-permute-start | bytes 884744 | tf_op jit(solution)/shard_map/ppermute | solution.py:278
  15.9 4.9 %shard_map.76 = (f32[256,1152]{1,0:T(8,128)S(1)}, bf16[256,1152]{1,0:T(8,128)(2,1)S(1)}, bf16[512,256]{1,0:T(8,128)(2,1)S(1)}, f32[512,1152]{1,0:T(8,128)S(1)}, ...) custom-call(s32[2]{0:T(128)S(1)} %pad_add_fusion.place, ...), custom_call_target="tpu_custom_call" | custom-call | tf_op jit(solution)/shard_map/pallas_call | solution.py:265
  21.4 0.9 %collective-permute-start.12 = (bf16[128,1152]{1,0:T(8,128)(2,1)S(1)}, bf16[128,1152]{1,0:T(8,128)(2,1)S(1)}, u32[]{:S(2)}, u32[]{:S(2)}) collective-permute-start(bf16[128,1152]{1,0:T(8,128)(2,1)S(1)} %get-tuple-element.116), channel_id=1, source_target_pairs={{0,2},{1,3},{2,0},{3,1},{4,6},{5,7},{6,4},{7,5},{8,10},{9,11},{10,... | collective-permute-start | bytes 884744 | tf_op jit(solution)/shard_map/ppermute | solution.py:278
  22.5 3.9 %shard_map.77 = (f32[256,1152]{1,0:T(8,128)S(1)}, bf16[256,1152]{1,0:T(8,128)(2,1)S(1)}, bf16[512,256]{1,0:T(8,128)(2,1)S(1)}, bf16[512,1152]{1,0:T(8,128)(2,1)S...) custom-call(bf16[128,1152]{1,0:T(8,128)(2,1)S(1)} %collective-permut, ...), custom_call_target="tpu_custom_call" | custom-call | tf_op jit(solution)/shard_map/pallas_call | solution.py:265
  27.1 1.5 %collective-permute-start.8 = (bf16[144,1152]{1,0:T(8,128)(2,1)S(1)}, bf16[144,1152]{1,0:T(8,128)(2,1)S(1)}, u32[]{:S(2)}, u32[]{:S(2)}) collective-permute-start(bf16[144,1152]{1,0:T(8,128)(2,1)S(1)} %get-tuple-element.77), channel_id=1, source_target_pairs={{0,4},{4,0},{8,12},{12,8},{16,20},{20,16},{24,28},{28,24},{1,5},{5... | collective-permute-start | bytes 995336 | tf_op jit(solution)/shard_map/ppermute | solution.py:278
  28.6 1.6 %collective-permute-start.15 = (bf16[144,1152]{1,0:T(8,128)(2,1)S(1)}, bf16[144,1152]{1,0:T(8,128)(2,1)S(1)}, u32[]{:S(2)}, u32[]{:S(2)}) collective-permute-start(bf16[144,1152]{1,0:T(8,128)(2,1)S(1)} %get-tuple-element.100), channel_id=1, source_target_pairs={{0,8},{4,12},{8,0},{12,4},{16,24},{20,28},{24,16},{28,20},{1,9},{5... | collective-permute-start | bytes 995336 | tf_op jit(solution)/shard_map/ppermute | solution.py:278
  30.6 3.7 %shard_map.78 = (bf16[256,1152]{1,0:T(8,128)(2,1)S(1)}, bf16[256,512]{1,0:T(8,128)(2,1)S(1)}, bf16[256,512]{1,0:T(8,128)(2,1)S(1)}, f32[256,1152]{1,0:T(8,128)S(...) custom-call(s32[2]{0:T(128)S(1)} %pad_add_fusion.place, bf16[128,1152]{1,0:T(8,128)(2,1)S(1)} %collective-permute-done.1.refs_0_, ...), custom_call_target="tpu_custom_call" | custom-call | tf_op jit(solution)/shard_map/pallas_call | solution.py:265
  34.9 0.9 %collective-permute-done.13.refs_1_ = bf16[64,1152]{1,0:T(8,128)(2,1)S(1)} collective-permute-done((bf16[64,1152]{1,0:T(8,128)(2,1)S(1)}, bf16[64,1152]{1,0:T(8,128)(2,1)S(1)}, u32[]{:S(2)}, u32[]{:S(2)}) %collective-permute-start.13) | collective-permute-done | bytes 147488 | tf_op jit(solution)/shard_map/ppermute | solution.py:278
  36.0 1.9 %shard_map.79 = (bf16[256,1152]{1,0:T(8,128)(2,1)S(1)}, bf16[256,512]{1,0:T(8,128)(2,1)S(1)}, bf16[256,512]{1,0:T(8,128)(2,1)S(1)}) custom-call(bf16[128,1152]{1,0:T(8,128)(2,1)S(1)} %collective-permute-done.12.refs_0_, bf16[64,1152]{1,0:T(8,128)(2,1)S(1)} %collective-permute-done.13.refs_1_, bf16[64,1152]{1,0:T(8,128)(2,1)S(1)} %collective-permute-done.14.refs_2_, ...), custom_call_target="tpu_custom_call" | custom-call | tf_op jit(solution)/shard_map/pallas_call | solution.py:265
  37.9 3.5 %shard_map.80 = (bf16[72,1152]{1,0:T(8,128)(2,1)S(1)}, bf16[72,1152]{1,0:T(8,128)(2,1)S(1)}, bf16[72,1152]{1,0:T(8,128)(2,1)S(1)}, bf16[72,1152]{1,0:T(8,128)(2,1)S(1)}, bf16[512,1152]{1,0:T(8,128)(2,1)S(1)}) custom-call(bf16[256,1152]{1,0:T(8,128)(2,1)S(1)} %get-tuple-element.84.x_2, bf16[256,512]{1,0:T(8,128)(2,1)S(1)} %get-tuple-element.85.w_2a, ...), custom_call_target="tpu_custom_call" | custom-call | tf_op jit(solution)/shard_map/pallas_call | solution.py:265
  41.4 1.6 %collective-permute-start.22 = (bf16[72,1152]{1,0:T(8,128)(2,1)S(1)}, bf16[72,1152]{1,0:T(8,128)(2,1)S(1)}, u32[]{:S(2)}, u32[]{:S(2)}) collective-permute-start(bf16[72,1152]{1,0:T(8,128)(2,1)S(1)} %get-tuple-element.108), channel_id=1, source_target_pairs={{0,4},{4,0},{8,12},{12,8},{16,20},{20,16},{24,28},{28,24},{1,5},{5... | collective-permute-start | bytes 497672 | tf_op jit(solution)/shard_map/ppermute | solution.py:278
  43.0 1.6 %collective-permute-start.23 = (bf16[72,1152]{1,0:T(8,128)(2,1)S(1)}, bf16[72,1152]{1,0:T(8,128)(2,1)S(1)}, u32[]{:S(2)}, u32[]{:S(2)}) collective-permute-start(bf16[72,1152]{1,0:T(8,128)(2,1)S(1)} %get-tuple-element.110), channel_id=1, source_target_pairs={{0,8},{4,12},{8,0},{12,4},{16,24},{20,28},{24,16},{28,20},{1,9},{5... | collective-permute-start | bytes 497672 | tf_op jit(solution)/shard_map/ppermute | solution.py:278
  45.7 1.2 %collective-permute-start.17 = (bf16[72,1152]{1,0:T(8,128)(2,1)S(1)}, bf16[72,1152]{1,0:T(8,128)(2,1)S(1)}, u32[]{:S(2)}, u32[]{:S(2)}) collective-permute-start(bf16[72,1152]{1,0:T(8,128)(2,1)S(1)} %slice.9), channel_id=1, source_target_pairs={{0,2},{1,3},{2,0},{3,1},{4,6},{5,7},{6,4},{7,5},{8,10},{9,11},{10,... | collective-permute-start | bytes 497672 | tf_op jit(solution)/shard_map/ppermute | solution.py:278
  46.9 2.0 %shard_map.82 = f32[256,1152]{1,0:T(8,128)} custom-call(bf16[512,1152]{1,0:T(8,128)(2,1)S(1)} %get-tuple-element.105.back, bf16[1152,1152]{1,0:T(8,128)(2,1)S(1)} %get-tuple-element.67.refs_7_.refs_3_.head), custom_call_target="tpu_custom_call" | custom-call | flops 1358954496 | tf_op jit(solution)/shard_map/pallas_call | solution.py:265
  48.9 2.0 %shard_map.81 = f32[256,1152]{1,0:T(8,128)} custom-call(bf16[512,1152]{1,0:T(8,128)(2,1)S(1)} %get-tuple-element.104.back, bf16[1152,1152]{1,0:T(8,128)(2,1)S(1)} %get-tuple-element.81.refs_12_.refs_3_.head), custom_call_target="tpu_custom_call" | custom-call | flops 1358954496 | tf_op jit(solution)/shard_map/pallas_call | solution.py:265
  51.1 2.7 %collective-permute-start.18 = (bf16[72,1152]{1,0:T(8,128)(2,1)S(1)}, bf16[72,1152]{1,0:T(8,128)(2,1)S(1)}, u32[]{:S(2)}, u32[]{:S(2)}) collective-permute-start(bf16[72,1152]{1,0:T(8,128)(2,1)S(1)} %add_convert_fusion.4), channel_id=1, source_target_pairs={{0,16},{4,20},{8,24},{12,28},{16,0},{20,4},{24,8},{28,12},{1,17},{... | collective-permute-start | bytes 497672 | tf_op jit(solution)/shard_map/ppermute | solution.py:278
  53.9 6.7 %collective-permute-done.18 = bf16[72,1152]{1,0:T(8,128)(2,1)S(1)} collective-permute-done((bf16[72,1152]{1,0:T(8,128)(2,1)S(1)}, bf16[72,1152]{1,0:T(8,128)(2,1)S(1)}, u32[]{:S(2)}, u32[]{:S(2)}) %collective-permute-start.18) | collective-permute-done | bytes 165920 | tf_op jit(solution)/shard_map/ppermute | solution.py:278
  60.8 1.6 %collective-permute-start.19 = (bf16[72,1152]{1,0:T(8,128)(2,1)S(1)}, bf16[72,1152]{1,0:T(8,128)(2,1)S(1)}, u32[]{:S(2)}, u32[]{:S(2)}) collective-permute-start(bf16[72,1152]{1,0:T(8,128)(2,1)S(1)} %add_convert_fusion.3.h0), channel_id=1, source_target_pairs={{0,4},{4,0},{8,12},{12,8},{16,20},{20,16},{24,28},{28,24},{1,5},{5... | collective-permute-start | bytes 497672 | tf_op jit(solution)/shard_map/ppermute | solution.py:278
  62.3 4.0 %collective-permute-start.20 = (bf16[72,1152]{1,0:T(8,128)(2,1)S(1)}, bf16[72,1152]{1,0:T(8,128)(2,1)S(1)}, u32[]{:S(2)}, u32[]{:S(2)}) collective-permute-start(bf16[72,1152]{1,0:T(8,128)(2,1)S(1)} %add_convert_fusion.3.h0), channel_id=1, source_target_pairs={{0,8},{4,12},{8,0},{12,4},{16,24},{20,28},{24,16},{28,20},{1,9},{5... | collective-permute-start | bytes 497672 | tf_op jit(solution)/shard_map/ppermute | solution.py:278
  66.3 3.9 %collective-permute-done.25 = bf16[72,1152]{1,0:T(8,128)(2,1)S(1)} collective-permute-done((bf16[72,1152]{1,0:T(8,128)(2,1)S(1)}, bf16[72,1152]{1,0:T(8,128)(2,1)S(1)}, u32[]{:S(2)}, u32[]{:S(2)}) %collective-permute-start.25) | collective-permute-done | bytes 165920 | tf_op jit(solution)/shard_map/ppermute | solution.py:278
  70.2 1.8 %collective-permute-start.26 = (bf16[72,1152]{1,0:T(8,128)(2,1)S(1)}, bf16[72,1152]{1,0:T(8,128)(2,1)S(1)}, u32[]{:S(2)}, u32[]{:S(2)}) collective-permute-start(bf16[72,1152]{1,0:T(8,128)(2,1)S(1)} %add_convert_fusion.1.h0), channel_id=1, source_target_pairs={{0,4},{4,0},{8,12},{12,8},{16,20},{20,16},{24,28},{28,24},{1,5},{5... | collective-permute-start | bytes 497672 | tf_op jit(solution)/shard_map/ppermute | solution.py:278
  72.0 0.7 collective-permute-start.27
  72.7 1.1 %collective-permute-start.28 = (bf16[72,1152]{1,0:T(8,128)(2,1)S(1)}, bf16[72,1152]{1,0:T(8,128)(2,1)S(1)}, u32[]{:S(2)}, u32[]{:S(2)}) collective-permute-start(bf16[72,1152]{1,0:T(8,128)(2,1)S(1)} %add_convert_fusion.1.h0), channel_id=1, source_target_pairs={{0,12},{4,8},{8,4},{12,0},{16,28},{20,24},{24,20},{28,16},{1,13},{... | collective-permute-start | bytes 497672 | tf_op jit(solution)/shard_map/ppermute | solution.py:278
  73.8 2.7 %collective-permute-done.21.h3 = bf16[72,1152]{1,0:T(8,128)(2,1)S(1)} collective-permute-done((bf16[72,1152]{1,0:T(8,128)(2,1)S(1)}, bf16[72,1152]{1,0:T(8,128)(2,1)S(1)}, u32[]{:S(2)}, u32[]{:S(2)}) %collective-permute-start.21) | collective-permute-done | bytes 165920 | tf_op jit(solution)/shard_map/ppermute | solution.py:278
  76.5 1.7 %shard_map.83 = f32[288,1152]{1,0:T(8,128)} custom-call(s32[2]{0:T(128)S(1)} %pad_add_fusion.place, bf16[72,1152]{1,0:T(8,128)(2,1)S(1)} %add_convert_fusion.3.h0, bf16[72,1152]{1,0:T(8,128)(2,1)S(1)} %collective-permute-done.19.h1, bf16[72,1152]{1,0:T(8,128)(2,1)S(1)} %collective-permute-done.20.h2, bf16[72,1152]{1,0:T(8,128)(2,1)S(1)} %collective-permute-done.21.h3), custom_call_target="tpu_custom_call" | custom-call | tf_op jit(solution)/shard_map/pallas_call | solution.py:265
  78.2 1.9 %collective-permute-done.27.h2 = bf16[72,1152]{1,0:T(8,128)(2,1)S(1)} collective-permute-done((bf16[72,1152]{1,0:T(8,128)(2,1)S(1)}, bf16[72,1152]{1,0:T(8,128)(2,1)S(1)}, u32[]{:S(2)}, u32[]{:S(2)}) %collective-permute-start.27) | collective-permute-done | bytes 165920 | tf_op jit(solution)/shard_map/ppermute | solution.py:278
  80.1 2.3 %collective-permute-done.28.h3 = bf16[72,1152]{1,0:T(8,128)(2,1)S(1)} collective-permute-done((bf16[72,1152]{1,0:T(8,128)(2,1)S(1)}, bf16[72,1152]{1,0:T(8,128)(2,1)S(1)}, u32[]{:S(2)}, u32[]{:S(2)}) %collective-permute-start.28) | collective-permute-done | bytes 165920 | tf_op jit(solution)/shard_map/ppermute | solution.py:278
  82.3 1.7 %shard_map.84 = f32[288,1152]{1,0:T(8,128)} custom-call(s32[2]{0:T(128)S(1)} %pad_add_fusion.place, bf16[72,1152]{1,0:T(8,128)(2,1)S(1)} %add_convert_fusion.1.h0, bf16[72,1152]{1,0:T(8,128)(2,1)S(1)} %collective-permute-done.26.h1, bf16[72,1152]{1,0:T(8,128)(2,1)S(1)} %collective-permute-done.27.h2, bf16[72,1152]{1,0:T(8,128)(2,1)S(1)} %collective-permute-done.28.h3), custom_call_target="tpu_custom_call" | custom-call | tf_op jit(solution)/shard_map/pallas_call | solution.py:265
  (51 shorter events, 5.4 us)
Async XLA Ops:
  0.7 4.7 %collective-permute-start.2 = (bf16[256,1152]{1,0:T(8,128)(2,1)}, bf16[256,1152]{1,0:T(8,128)(2,1)S(1)}, u32[]{:S(2)}, u32[]{:S(2)}) collective-permute-start(bf16[256,1152]{1,0:T(8,128)(2,1)} %t0_far), channel_id=1, source_target_pairs={{0,1},{1,0},{2,3},{3,2},{4,5},{5,4},{6,7},{7,6},{8,9},{9,8},{10,11... | collective-permute-start | bytes 1769480 | tf_op jit(solution)/shard_map/ppermute | solution.py:278
  1.2 4.3 %collective-permute-start.3 = (bf16[256,1152]{1,0:T(8,128)(2,1)}, bf16[256,1152]{1,0:T(8,128)(2,1)S(1)}, u32[]{:S(2)}, u32[]{:S(2)}) collective-permute-start(bf16[256,1152]{1,0:T(8,128)(2,1)} %i0_far), channel_id=1, source_target_pairs={{0,1},{1,0},{2,3},{3,2},{4,5},{5,4},{6,7},{7,6},{8,9},{9,8},{10,11... | collective-permute-start | bytes 1769480 | tf_op jit(solution)/shard_map/ppermute | solution.py:278
  2.3 10.8 %collective-permute-start.1 = (bf16[128,1152]{1,0:T(8,128)(2,1)S(1)}, bf16[128,1152]{1,0:T(8,128)(2,1)S(1)}, u32[]{:S(2)}, u32[]{:S(2)}) collective-permute-start(bf16[128,1152]{1,0:T(8,128)(2,1)S(1)} %get-tuple-element.118), channel_id=1, source_target_pairs={{0,2},{1,3},{2,0},{3,1},{4,6},{5,7},{6,4},{7,5},{8,10},{9,11},{10,... | collective-permute-start | bytes 884744 | tf_op jit(solution)/shard_map/ppermute | solution.py:278
  5.3 8.4 %copy-start = (bf16[256,1152]{1,0:T(8,128)(2,1)S(1)}, bf16[256,1152]{1,0:T(8,128)(2,1)}, u32[]{:S(2)}) copy-start(bf16[256,1152]{1,0:T(8,128)(2,1)} %i0_far) | copy-start | bytes 1769476
  5.3 15.5 %collective-permute-start = (bf16[128,1152]{1,0:T(8,128)(2,1)S(1)}, bf16[128,1152]{1,0:T(8,128)(2,1)S(1)}, u32[]{:S(2)}, u32[]{:S(2)}) collective-permute-start(bf16[128,1152]{1,0:T(8,128)(2,1)S(1)} %get-tuple-element.119), channel_id=1, source_target_pairs={{0,2},{1,3},{2,0},{3,1},{4,6},{5,7},{6,4},{7,5},{8,10},{9,11},{10,... | collective-permute-start | bytes 884744 | tf_op jit(solution)/shard_map/ppermute | solution.py:278
  13.2 2.8 %collective-permute-start.4 = (bf16[64,1152]{1,0:T(8,128)(2,1)S(1)}, bf16[64,1152]{1,0:T(8,128)(2,1)S(1)}, u32[]{:S(2)}, u32[]{:S(2)}) collective-permute-start(bf16[64,1152]{1,0:T(8,128)(2,1)S(1)} %get-tuple-element.127), channel_id=1, source_target_pairs={{0,1},{1,0},{2,3},{3,2},{4,5},{5,4},{6,7},{7,6},{8,9},{9,8},{10,11... | collective-permute-start | bytes 442376 | tf_op jit(solution)/shard_map/ppermute | solution.py:278
  13.2 2.7 %collective-permute-start.5 = (bf16[64,1152]{1,0:T(8,128)(2,1)S(1)}, bf16[64,1152]{1,0:T(8,128)(2,1)S(1)}, u32[]{:S(2)}, u32[]{:S(2)}) collective-permute-start(bf16[64,1152]{1,0:T(8,128)(2,1)S(1)} %get-tuple-element.126), channel_id=1, source_target_pairs={{0,1},{1,0},{2,3},{3,2},{4,5},{5,4},{6,7},{7,6},{8,9},{9,8},{10,11... | collective-permute-start | bytes 442376 | tf_op jit(solution)/shard_map/ppermute | solution.py:278
  13.8 12.7 %collective-permute-start.9 = (bf16[128,1152]{1,0:T(8,128)(2,1)S(1)}, bf16[128,1152]{1,0:T(8,128)(2,1)S(1)}, u32[]{:S(2)}, u32[]{:S(2)}) collective-permute-start(bf16[128,1152]{1,0:T(8,128)(2,1)S(1)} %get-tuple-element.117), channel_id=1, source_target_pairs={{0,2},{1,3},{2,0},{3,1},{4,6},{5,7},{6,4},{7,5},{8,10},{9,11},{10,... | collective-permute-start | bytes 884744 | tf_op jit(solution)/shard_map/ppermute | solution.py:278
  20.9 1.5 %collective-permute-start.6 = (bf16[64,1152]{1,0:T(8,128)(2,1)S(1)}, bf16[64,1152]{1,0:T(8,128)(2,1)S(1)}, u32[]{:S(2)}, u32[]{:S(2)}) collective-permute-start(bf16[64,1152]{1,0:T(8,128)(2,1)S(1)} %get-tuple-element.125), channel_id=1, source_target_pairs={{0,1},{1,0},{2,3},{3,2},{4,5},{5,4},{6,7},{7,6},{8,9},{9,8},{10,11... | collective-permute-start | bytes 442376 | tf_op jit(solution)/shard_map/ppermute | solution.py:278
  20.9 1.6 %collective-permute-start.7 = (bf16[64,1152]{1,0:T(8,128)(2,1)S(1)}, bf16[64,1152]{1,0:T(8,128)(2,1)S(1)}, u32[]{:S(2)}, u32[]{:S(2)}) collective-permute-start(bf16[64,1152]{1,0:T(8,128)(2,1)S(1)} %get-tuple-element.124), channel_id=1, source_target_pairs={{0,1},{1,0},{2,3},{3,2},{4,5},{5,4},{6,7},{7,6},{8,9},{9,8},{10,11... | collective-permute-start | bytes 442376 | tf_op jit(solution)/shard_map/ppermute | solution.py:278
  21.4 12.9 %collective-permute-start.12 = (bf16[128,1152]{1,0:T(8,128)(2,1)S(1)}, bf16[128,1152]{1,0:T(8,128)(2,1)S(1)}, u32[]{:S(2)}, u32[]{:S(2)}) collective-permute-start(bf16[128,1152]{1,0:T(8,128)(2,1)S(1)} %get-tuple-element.116), channel_id=1, source_target_pairs={{0,2},{1,3},{2,0},{3,1},{4,6},{5,7},{6,4},{7,5},{8,10},{9,11},{10,... | collective-permute-start | bytes 884744 | tf_op jit(solution)/shard_map/ppermute | solution.py:278
  26.5 3.7 %collective-permute-start.10 = (bf16[64,1152]{1,0:T(8,128)(2,1)S(1)}, bf16[64,1152]{1,0:T(8,128)(2,1)S(1)}, u32[]{:S(2)}, u32[]{:S(2)}) collective-permute-start(bf16[64,1152]{1,0:T(8,128)(2,1)S(1)} %get-tuple-element.123), channel_id=1, source_target_pairs={{0,1},{1,0},{2,3},{3,2},{4,5},{5,4},{6,7},{7,6},{8,9},{9,8},{10,11... | collective-permute-start | bytes 442376 | tf_op jit(solution)/shard_map/ppermute | solution.py:278
  26.9 3.7 %collective-permute-start.11 = (bf16[64,1152]{1,0:T(8,128)(2,1)S(1)}, bf16[64,1152]{1,0:T(8,128)(2,1)S(1)}, u32[]{:S(2)}, u32[]{:S(2)}) collective-permute-start(bf16[64,1152]{1,0:T(8,128)(2,1)S(1)} %get-tuple-element.122), channel_id=1, source_target_pairs={{0,1},{1,0},{2,3},{3,2},{4,5},{5,4},{6,7},{7,6},{8,9},{9,8},{10,11... | collective-permute-start | bytes 442376 | tf_op jit(solution)/shard_map/ppermute | solution.py:278
  27.1 17.5 %collective-permute-start.8 = (bf16[144,1152]{1,0:T(8,128)(2,1)S(1)}, bf16[144,1152]{1,0:T(8,128)(2,1)S(1)}, u32[]{:S(2)}, u32[]{:S(2)}) collective-permute-start(bf16[144,1152]{1,0:T(8,128)(2,1)S(1)} %get-tuple-element.77), channel_id=1, source_target_pairs={{0,4},{4,0},{8,12},{12,8},{16,20},{20,16},{24,28},{28,24},{1,5},{5... | collective-permute-start | bytes 995336 | tf_op jit(solution)/shard_map/ppermute | solution.py:278
  28.6 16.4 %collective-permute-start.15 = (bf16[144,1152]{1,0:T(8,128)(2,1)S(1)}, bf16[144,1152]{1,0:T(8,128)(2,1)S(1)}, u32[]{:S(2)}, u32[]{:S(2)}) collective-permute-start(bf16[144,1152]{1,0:T(8,128)(2,1)S(1)} %get-tuple-element.100), channel_id=1, source_target_pairs={{0,8},{4,12},{8,0},{12,4},{16,24},{20,28},{24,16},{28,20},{1,9},{5... | collective-permute-start | bytes 995336 | tf_op jit(solution)/shard_map/ppermute | solution.py:278
  30.2 15.3 %collective-permute-start.16 = (bf16[144,1152]{1,0:T(8,128)(2,1)S(1)}, bf16[144,1152]{1,0:T(8,128)(2,1)S(1)}, u32[]{:S(2)}, u32[]{:S(2)}) collective-permute-start(bf16[144,1152]{1,0:T(8,128)(2,1)S(1)} %get-tuple-element.102), channel_id=1, source_target_pairs={{0,12},{4,8},{8,4},{12,0},{16,28},{20,24},{24,20},{28,16},{1,13},{... | collective-permute-start | bytes 995336 | tf_op jit(solution)/shard_map/ppermute | solution.py:278
  34.4 1.4 %collective-permute-start.13 = (bf16[64,1152]{1,0:T(8,128)(2,1)S(1)}, bf16[64,1152]{1,0:T(8,128)(2,1)S(1)}, u32[]{:S(2)}, u32[]{:S(2)}) collective-permute-start(bf16[64,1152]{1,0:T(8,128)(2,1)S(1)} %get-tuple-element.121), channel_id=1, source_target_pairs={{0,1},{1,0},{2,3},{3,2},{4,5},{5,4},{6,7},{7,6},{8,9},{9,8},{10,11... | collective-permute-start | bytes 442376 | tf_op jit(solution)/shard_map/ppermute | solution.py:278
  34.4 1.6 %collective-permute-start.14 = (bf16[64,1152]{1,0:T(8,128)(2,1)S(1)}, bf16[64,1152]{1,0:T(8,128)(2,1)S(1)}, u32[]{:S(2)}, u32[]{:S(2)}) collective-permute-start(bf16[64,1152]{1,0:T(8,128)(2,1)S(1)} %get-tuple-element.120), channel_id=1, source_target_pairs={{0,1},{1,0},{2,3},{3,2},{4,5},{5,4},{6,7},{7,6},{8,9},{9,8},{10,11... | collective-permute-start | bytes 442376 | tf_op jit(solution)/shard_map/ppermute | solution.py:278
  41.4 12.4 %collective-permute-start.22 = (bf16[72,1152]{1,0:T(8,128)(2,1)S(1)}, bf16[72,1152]{1,0:T(8,128)(2,1)S(1)}, u32[]{:S(2)}, u32[]{:S(2)}) collective-permute-start(bf16[72,1152]{1,0:T(8,128)(2,1)S(1)} %get-tuple-element.108), channel_id=1, source_target_pairs={{0,4},{4,0},{8,12},{12,8},{16,20},{20,16},{24,28},{28,24},{1,5},{5... | collective-permute-start | bytes 497672 | tf_op jit(solution)/shard_map/ppermute | solution.py:278
  43.0 10.8 %collective-permute-start.23 = (bf16[72,1152]{1,0:T(8,128)(2,1)S(1)}, bf16[72,1152]{1,0:T(8,128)(2,1)S(1)}, u32[]{:S(2)}, u32[]{:S(2)}) collective-permute-start(bf16[72,1152]{1,0:T(8,128)(2,1)S(1)} %get-tuple-element.110), channel_id=1, source_target_pairs={{0,8},{4,12},{8,0},{12,4},{16,24},{20,28},{24,16},{28,20},{1,9},{5... | collective-permute-start | bytes 497672 | tf_op jit(solution)/shard_map/ppermute | solution.py:278
  44.6 9.2 %collective-permute-start.24 = (bf16[72,1152]{1,0:T(8,128)(2,1)S(1)}, bf16[72,1152]{1,0:T(8,128)(2,1)S(1)}, u32[]{:S(2)}, u32[]{:S(2)}) collective-permute-start(bf16[72,1152]{1,0:T(8,128)(2,1)S(1)} %get-tuple-element.112), channel_id=1, source_target_pairs={{0,12},{4,8},{8,4},{12,0},{16,28},{20,24},{24,20},{28,16},{1,13},{... | collective-permute-start | bytes 497672 | tf_op jit(solution)/shard_map/ppermute | solution.py:278
  45.7 5.4 %collective-permute-start.17 = (bf16[72,1152]{1,0:T(8,128)(2,1)S(1)}, bf16[72,1152]{1,0:T(8,128)(2,1)S(1)}, u32[]{:S(2)}, u32[]{:S(2)}) collective-permute-start(bf16[72,1152]{1,0:T(8,128)(2,1)S(1)} %slice.9), channel_id=1, source_target_pairs={{0,2},{1,3},{2,0},{3,1},{4,6},{5,7},{6,4},{7,5},{8,10},{9,11},{10,... | collective-permute-start | bytes 497672 | tf_op jit(solution)/shard_map/ppermute | solution.py:278
  51.1 9.5 %collective-permute-start.18 = (bf16[72,1152]{1,0:T(8,128)(2,1)S(1)}, bf16[72,1152]{1,0:T(8,128)(2,1)S(1)}, u32[]{:S(2)}, u32[]{:S(2)}) collective-permute-start(bf16[72,1152]{1,0:T(8,128)(2,1)S(1)} %add_convert_fusion.4), channel_id=1, source_target_pairs={{0,16},{4,20},{8,24},{12,28},{16,0},{20,4},{24,8},{28,12},{1,17},{... | collective-permute-start | bytes 497672 | tf_op jit(solution)/shard_map/ppermute | solution.py:278
  60.7 9.5 %collective-permute-start.25 = (bf16[72,1152]{1,0:T(8,128)(2,1)S(1)}, bf16[72,1152]{1,0:T(8,128)(2,1)S(1)}, u32[]{:S(2)}, u32[]{:S(2)}) collective-permute-start(bf16[72,1152]{1,0:T(8,128)(2,1)S(1)} %add_convert_fusion.2), channel_id=1, source_target_pairs={{0,16},{4,20},{8,24},{12,28},{16,0},{20,4},{24,8},{28,12},{1,17},{... | collective-permute-start | bytes 497672 | tf_op jit(solution)/shard_map/ppermute | solution.py:278
  60.8 9.4 %collective-permute-start.19 = (bf16[72,1152]{1,0:T(8,128)(2,1)S(1)}, bf16[72,1152]{1,0:T(8,128)(2,1)S(1)}, u32[]{:S(2)}, u32[]{:S(2)}) collective-permute-start(bf16[72,1152]{1,0:T(8,128)(2,1)S(1)} %add_convert_fusion.3.h0), channel_id=1, source_target_pairs={{0,4},{4,0},{8,12},{12,8},{16,20},{20,16},{24,28},{28,24},{1,5},{5... | collective-permute-start | bytes 497672 | tf_op jit(solution)/shard_map/ppermute | solution.py:278
  62.3 11.5 %collective-permute-start.20 = (bf16[72,1152]{1,0:T(8,128)(2,1)S(1)}, bf16[72,1152]{1,0:T(8,128)(2,1)S(1)}, u32[]{:S(2)}, u32[]{:S(2)}) collective-permute-start(bf16[72,1152]{1,0:T(8,128)(2,1)S(1)} %add_convert_fusion.3.h0), channel_id=1, source_target_pairs={{0,8},{4,12},{8,0},{12,4},{16,24},{20,28},{24,16},{28,20},{1,9},{5... | collective-permute-start | bytes 497672 | tf_op jit(solution)/shard_map/ppermute | solution.py:278
  66.3 10.2 %collective-permute-start.21 = (bf16[72,1152]{1,0:T(8,128)(2,1)S(1)}, bf16[72,1152]{1,0:T(8,128)(2,1)S(1)}, u32[]{:S(2)}, u32[]{:S(2)}) collective-permute-start(bf16[72,1152]{1,0:T(8,128)(2,1)S(1)} %add_convert_fusion.3.h0), channel_id=1, source_target_pairs={{0,12},{4,8},{8,4},{12,0},{16,28},{20,24},{24,20},{28,16},{1,13},{... | collective-permute-start | bytes 497672 | tf_op jit(solution)/shard_map/ppermute | solution.py:278
  70.2 7.9 %collective-permute-start.26 = (bf16[72,1152]{1,0:T(8,128)(2,1)S(1)}, bf16[72,1152]{1,0:T(8,128)(2,1)S(1)}, u32[]{:S(2)}, u32[]{:S(2)}) collective-permute-start(bf16[72,1152]{1,0:T(8,128)(2,1)S(1)} %add_convert_fusion.1.h0), channel_id=1, source_target_pairs={{0,4},{4,0},{8,12},{12,8},{16,20},{20,16},{24,28},{28,24},{1,5},{5... | collective-permute-start | bytes 497672 | tf_op jit(solution)/shard_map/ppermute | solution.py:278
  72.0 8.0 %collective-permute-start.27 = (bf16[72,1152]{1,0:T(8,128)(2,1)S(1)}, bf16[72,1152]{1,0:T(8,128)(2,1)S(1)}, u32[]{:S(2)}, u32[]{:S(2)}) collective-permute-start(bf16[72,1152]{1,0:T(8,128)(2,1)S(1)} %add_convert_fusion.1.h0), channel_id=1, source_target_pairs={{0,8},{4,12},{8,0},{12,4},{16,24},{20,28},{24,16},{28,20},{1,9},{5... | collective-permute-start | bytes 497672 | tf_op jit(solution)/shard_map/ppermute | solution.py:278
  72.7 9.6 %collective-permute-start.28 = (bf16[72,1152]{1,0:T(8,128)(2,1)S(1)}, bf16[72,1152]{1,0:T(8,128)(2,1)S(1)}, u32[]{:S(2)}, u32[]{:S(2)}) collective-permute-start(bf16[72,1152]{1,0:T(8,128)(2,1)S(1)} %add_convert_fusion.1.h0), channel_id=1, source_target_pairs={{0,12},{4,8},{8,4},{12,0},{16,28},{20,24},{24,20},{28,16},{1,13},{... | collective-permute-start | bytes 497672 | tf_op jit(solution)/shard_map/ppermute | solution.py:278

commit v9 on v8

--- a/solution.py
+++ b/solution.py
@@ -88,24 +88,24 @@
 
 def back_rows(projected_ref, gradient_ref, back_ref, at=0):
     for first in range(0, projected_ref.shape[0], STRIP):
-        rows, target = slice(first, first + STRIP), slice(at + first, at + first + STRIP)
+        rows = slice(first, first + STRIP)
         factor = factor_of(projected_ref, rows)
-        along = jnp.sum(projected_ref[rows, :] * gradient_ref[target, :], axis=-1, keepdims=True)
+        along = jnp.sum(projected_ref[rows, :] * gradient_ref[rows, :], axis=-1, keepdims=True)
         along = factor * factor * factor * along
-        back = factor * gradient_ref[target, :] - along * projected_ref[rows, :]
-        back_ref[target, :] = back.astype(BF16)
-
-
-def weight_rows(dots_ref, weights_ref, pairs_from=None):
+        back = factor * gradient_ref[rows, :] - along * projected_ref[rows, :]
+        back_ref[at + first : at + first + STRIP, :] = back.astype(BF16)
+
+
+def weight_rows(dots_ref, weights_ref, pairs_from=None, begin=0, end=None):
     half_scale = 0.5 * SCORE_SCALE
-    for first in range(0, dots_ref.shape[0], STRIP):
+    for first in range(begin, dots_ref.shape[0] if end is None else end, STRIP):
         rows = slice(first, first + STRIP)
         score = jnp.tanh(half_scale * dots_ref[rows, :] + 0.5 * SCORE_BIAS)
         weights = half_scale + half_scale * score
         if pairs_from is None:
             weights_ref[rows, :] = weights.astype(BF16)
             continue
-        pair = pairs_from + first
+        pair = pairs_from + first - begin
         left = pair // LANES * LANES
         right = min(left + LANES, weights.shape[1])
         shape = (STRIP, right - left)
@@ -201,45 +201,57 @@
     split_head(dot_nn(pick_i[...], dp_a[...]), (h0, h1, h2, h3))
 
 
-def block(number, features, image_head, y_a, y_2, y_3, x_b, w_ba, w_bb, p_b, d_a, d_b):
-    half = x_b.shape[0]
-    p_b[...] = dot_nn(rows_of(features), image_head[...])
-    unit_rows(p_b, x_b)
-    d_a[...] = dot_nt(x_b[...], y_a[...])
-    d_b[:, :half] = dot_nt(x_b[...], y_2[...])
-    d_b[:, half:] = dot_nt(x_b[...], y_3[...])
-    weight_rows(d_a, w_ba)
-    weight_rows(d_b, w_bb, number * half)
-
-
-def third_kernel(place, *refs):
-    *features, x_a, w_a2, w_a3, image_head, y_a, y_2, y_3 = refs[:-9]
-    x_b, w_ba, w_bb, gy_2, gy_3, pick_t, p_b, d_a, d_b = refs[-9:]
-    texts, images = features[: len(features) // 3 * 2], features[len(features) // 3 * 2 :]
+def text_pull_kernel(place, *refs):
+    *features, x_a, w_a2, w_a3, gy_2, gy_3, pick_t = refs
     gy_2[...] = dot_tn(w_a2[...], x_a[...])
-    block(0, images, image_head, y_a, y_2, y_3, x_b, w_ba, w_bb, p_b, d_a, d_b)
     gy_3[...] = dot_tn(w_a3[...], x_a[...])
     pick = picker(place, pick_t.shape[0], x_a.shape[1], (0,))
-    pick_t[...] = dot_nt(pick, rows_of(texts)).astype(BF16)
-
-
-def fourth_kernel(*refs):
-    block(1, refs[:-10], *refs[-10:])
+    pick_t[...] = dot_nt(pick, rows_of(features)).astype(BF16)
+
+
+def far_weights(core, x, y_a, y_2, y_3, w_a, w_2, w_3, d_a, d_2, d_3):
+    half = x.shape[0]
+    middle = half // 2
+    d_a[...] = dot_nt(x, y_a[...])
+    d_2[...] = dot_nt(x, y_2[...])
+    weight_rows(d_a, w_a)
+    d_3[...] = dot_nt(x, y_3[...])
+    weight_rows(d_2, w_2, core * middle, 0, middle)
+    weight_rows(d_2, w_2, None, middle, half)
+    weight_rows(d_3, w_3, None, 0, middle)
+    weight_rows(d_3, w_3, core * middle, middle, half)
+
+
+def block_kernel(i2, image_head, y_a, y_2, y_3, x_first, x_second, w_a, w_2, w_3, p_b, x_b, d_a, d_2, d_3):
+    middle = x_first.shape[0]
+    p_b[...] = dot_nn(i2[...], image_head[...])
+    unit_rows(p_b, x_b)
+    x_first[...] = x_b[:middle, :]
+    x_second[...] = x_b[middle:, :]
+    far_weights(0, x_b[...], y_a, y_2, y_3, w_a, w_2, w_3, d_a, d_2, d_3)
+
+
+def own_pull_kernel(x_first, x_second, w_a, w_2, w_3, gy_a_in, gy_2_in, gy_3_in, gy_a, gy_2, gy_3):
+    x = rows_of((x_first, x_second))
+    gy_a[...] = gy_a_in[...] + dot_tn(w_a[...], x)
+    gy_2[...] = gy_2_in[...] + dot_tn(w_2[...], x)
+    gy_3[...] = gy_3_in[...] + dot_tn(w_3[...], x)
 
 
 def last_kernel(
-    x_2, w_2a, w_2b, x_3, w_3a, w_3b, q_a, q_2, q_3, gy_a_in, gy_2, gy_3, pick_a, pick_b,
-    h0, h1, h2, h3, dq_a, gy_a, gy_b, dq_b, near_head,
+    x_first, x_second, y_a, y_2, y_3, q_a, q_2, q_3, gy_a_in, gy_2_in, gy_3_in, pick_a, pick_b,
+    h0, h1, h2, h3, dq_a, gy_a, gy_2, gy_3, dq_b, near_head, w_a, w_2, w_3, d_a, d_2, d_3,
 ):
-    half = x_2.shape[0]
-    gy_a[...] = gy_a_in[...] + dot_tn(w_2a[...], x_2[...]) + dot_tn(w_3a[...], x_3[...])
-    gy_b[...] = dot_tn(w_2b[...], x_2[...]) + dot_tn(w_3b[...], x_3[...])
+    half = q_2.shape[0]
+    x = rows_of((x_first, x_second))
+    far_weights(1, x, y_a, y_2, y_3, w_a, w_2, w_3, d_a, d_2, d_3)
+    gy_a[...] = gy_a_in[...] + dot_tn(w_a[...], x)
+    gy_2[...] = gy_2_in[...] + dot_tn(w_2[...], x)
     back_rows(q_a, gy_a, dq_a)
+    gy_3[...] = gy_3_in[...] + dot_tn(w_3[...], x)
     near_head[...] = dot_nn(pick_a[...], dq_a[...])
-    gy_b[:half, :] += gy_2[...]
-    gy_b[half:, :] += gy_3[...]
-    back_rows(q_2, gy_b, dq_b, 0)
-    back_rows(q_3, gy_b, dq_b, half)
+    back_rows(q_2, gy_2, dq_b, 0)
+    back_rows(q_3, gy_3, dq_b, half)
     split_head(near_head[...] + dot_nn(pick_b[...], dq_b[...]), (h0, h1, h2, h3))
 
 
@@ -247,11 +259,38 @@
     out[...] = dot_nt(back[: out.shape[0], :], head[...])
 
 
-def place_kernel(place, h0, h1, h2, h3, out):
-    part = h0.shape[0]
-    for k, piece in enumerate((h0, h1, h2, h3)):
+def place_kernel(place, ks, *refs):
+    out, buffer, sems = refs[-3:]
+    part = refs[0].shape[0]
+    copies = []
+    for n, k in enumerate(ks):
+        buffer[n] = refs[n][...].astype(F32)
         first = pl.multiple_of((place[1] ^ k) * part, part)
-        out[pl.ds(first, part), :] = piece[...].astype(F32)
+        copies.append(pltpu.make_async_copy(buffer.at[n], out.at[pl.ds(first, part), :], sems.at[n]))
+        copies[-1].start()
+    for copy in copies:
+        copy.wait()
+
+
+def place_pieces(place, pieces, ks, out=None):
+    rows, width = pieces[0].shape
+    args = [pltpu.with_memory_space_constraint(a, pltpu.VMEM) for a in pieces]
+    specs = [pl.BlockSpec(memory_space=pltpu.SMEM)]
+    specs += [pl.BlockSpec(memory_space=pltpu.VMEM)] * len(pieces)
+    if out is not None:
+        args, specs = args + [out], specs + [pl.BlockSpec(memory_space=pltpu.HBM)]
+    return pl.pallas_call(
+        lambda place_ref, *refs: place_kernel(place_ref, ks, *refs),
+        out_shape=pltpu.HBM((QUAD * rows, width), F32),
+        in_specs=specs,
+        out_specs=pl.BlockSpec(memory_space=pltpu.HBM),
+        scratch_shapes=[
+            pltpu.VMEM((len(ks), rows, width), F32), pltpu.SemaphoreType.DMA((len(ks),))
+        ],
+        input_output_aliases={} if out is None else {len(pieces) + 1: 0},
+        compiler_params=pltpu.CompilerParams(vmem_limit_bytes=4 * 1024 * 1024),
+        cost_estimate=pl.CostEstimate(flops=0, bytes_accessed=0, transcendentals=0),
+    )(place, *args)
 
 
 def call(kernel, outs, scratch, args, mib, place=None, macs=0, keep=True, far=()):
@@ -302,13 +341,11 @@
         return [total] + [cuts(total, mask=k) for k in range(1, QUAD)]
 
     def placed(pieces):
-        outs = [((rows_out, width), F32)]
-        return call(place_kernel, outs, [], pieces, 4, place, keep=False)[0]
-
-    t2, i2 = (
-        [loop(rows, mask=2) for rows in jnp.split(features, 2)]
-        for features in (text_features, image_features)
-    )
+        out = place_pieces(place, pieces[:-1], tuple(range(QUAD - 1)))
+        return place_pieces(place, pieces[-1:], (QUAD - 1,), out)
+
+    t2 = [loop(rows, mask=2) for rows in jnp.split(text_features, 2)]
+    i2 = loop(image_features, mask=2)
     place = jnp.stack([lax.axis_index("loop"), lax.axis_index("cuts") & (QUAD - 1)])
     place = place.astype(jnp.int32)
     t0, i0, place = lax.optimization_barrier((text_features, image_features, place))
@@ -346,29 +383,38 @@
         8,
     )
     image_others = [cuts(image_parts[k], mask=k) for k in range(1, QUAD)]
-    scratch = [tall, block_dots, block_dots]
-    x_2, w_2a, w_2b, gy_2, gy_3, pick_b = call(
-        third_kernel,
-        [tall_b, block_w, block_w, tall, tall, pick_one],
-        scratch,
-        (*first, *second, *both(i2[0], dp_a, 2), x_a, w_a2, w_a3, image_head, y_a, y_2, y_3),
+    gy_2, gy_3, pick_b = call(
+        text_pull_kernel,
+        [tall, tall, pick_one],
+        [],
+        (*first, *second, after(x_a, dp_a), w_a2, w_a3),
         8,
         place,
     )
-    x_3, w_3a, w_3b = call(
-        fourth_kernel,
-        [tall_b, block_w, block_w],
-        scratch,
-        (*both(i2[1], gy_2, 2), image_head, y_a, y_2, y_3),
-        8,
-    )
-    blocks = (x_2, w_2a, w_2b, x_3, w_3a, w_3b)
+    middle_b, corner, corner_dots = ((half // 2, width), BF16), ((half, half), BF16), ((half, half), F32)
+    *x_2, w_2a, w_22, w_23 = call(
+        block_kernel,
+        [middle_b, middle_b, block_w, corner, corner],
+        [tall, tall_b, block_dots, corner_dots, corner_dots],
+        (after(i2, gy_2), image_head, y_a, y_2, y_3),
+        8,
+    )
+    x_3 = [loop(rows, mask=1) for rows in x_2]
+    gy_a, gy_2, gy_3 = call(
+        own_pull_kernel,
+        [wide, tall, tall],
+        [],
+        (*x_2, w_2a, w_22, w_23, gy_a, gy_2, gy_3),
+        8,
+    )
+    x_3 = [after(rows, gy_a) for rows in x_3]
     *text_parts, dq_a = call(
         last_kernel,
         [((part, width), BF16)] * QUAD + [wide_b],
-        [wide, wide, wide_b, ((rows_out, width), F32)],
-        (*blocks, q_a, q_2, q_3, gy_a, gy_2, gy_3, pick_a, pick_b),
-        14,
+        [wide, tall, tall, wide_b, ((rows_out, width), F32), block_w, corner, corner]
+        + [block_dots, corner_dots, corner_dots],
+        (*x_3, y_a, y_2, y_3, q_a, q_2, q_3, gy_a, gy_2, gy_3, pick_a, pick_b),
+        16,
     )
     text_others = [cuts(text_parts[k], mask=k) for k in range(1, QUAD)]
     image_others = [after(other, dq_a) for other in image_others]

time: 84.2 us -> 84.3 us (level)
  waiting for transfers between devices: 20.2 us -> 14.6 us
  starting transfers between devices: 29 us -> 33.2 us
  Pallas kernels: 32.3 us -> 33.7 us
    pallas_call x0 -> x4, Pallas kernels: none -> 5.66 us  [place_pieces(): pl.pallas_call(lambda place_ref, *refs: place_kernel(place_ref, ks, *refs...]
    ppermute x29 -> x26, waiting for transfers between devices: 20.2 us -> 14.6 us  [swap(): return lax.ppermute(array, axis, [(i, i ^ mask) for i in range(size)])]
    pallas_call x10 -> x9, Pallas kernels: 32.3 us -> 28 us  [call(): pl.pallas_call(kernel, out_shape=[shape(s, t) for s, t in outs], in_specs...]
    ppermute x29 -> x26, starting transfers between devices: 29 us -> 33.2 us  [swap(): return lax.ppermute(array, axis, [(i, i ^ mask) for i in range(size)])]
  transfers between devices with their start and end apart: 29 -> 26, of which waited for: 11 -> 11; matrix products, arithmetic and copies ran while one was open for 2% -> 2% of each run, Pallas kernels for 36% -> 38%
where the time goes in v9:
time: 84.3 us; the launch traced here: 84.1 us
  Pallas kernels  33.7 us (40%)
  starting transfers between devices  33.2 us (39%)
  waiting for transfers between devices  14.6 us (17%)
  local copies, waits for them, and re-layouts  1.16 us (1%)
  between operations  0.99 us (1%)
    ppermute x26, starting transfers between devices, swap(): return lax.ppermute(array, axis, [(i, i ^ mask) for i in range(size)])  33.2 us
    pallas_call x9, Pallas kernels, call(): pl.pallas_call(kernel, out_shape=[shape(s, t) for s, t in outs], in_specs...  28 us
    ppermute x26, waiting for transfers between devices, swap(): return lax.ppermute(array, axis, [(i, i ^ mask) for i in range(size)])  14.6 us
    pallas_call x4, Pallas kernels, place_pieces(): pl.pallas_call(lambda place_ref, *refs: place_kernel(place_ref, ks, *refs...  5.66 us
  transfers between devices with their start and end apart: 26, of which 11 were waited for; matrix products, arithmetic and copies ran while one was open for 2% of the time, Pallas kernels for 38%

profile of v9, /device:TPU:0, one launch (start us, length us, event | category | flops | bytes accessed | tf_op | source)
XLA Modules:
  0.0 84.1 jit_solution(8151322732878013953)
XLA Ops:
  1.2 1.1 %fusion = (bf16[128,1152]{1,0:T(8,128)(2,1)S(1)}, bf16[128,1152]{1,0:T(8,128)(2,1)S(1)}) fusion(bf16[256,1152]{1,0:T(8,128)(2,1)} %t0_far), kind=kLoop, calls=%fused_computation.6 | loop fusion | bytes 1179648 | tf_op jit(solution)/shard_map/split | solution.py:347
  2.3 3.0 %collective-permute-start.1 = (bf16[128,1152]{1,0:T(8,128)(2,1)S(1)}, bf16[128,1152]{1,0:T(8,128)(2,1)S(1)}, u32[]{:S(2)}, u32[]{:S(2)}) collective-permute-start(bf16[128,1152]{1,0:T(8,128)(2,1)S(1)} %get-tuple-element.124), channel_id=1, source_target_pairs={{0,2},{1,3},{2,0},{3,1},{4,6},{5,7},{6,4},{7,5},{8,10},{9,11},{10,... | collective-permute-start | bytes 884744 | tf_op jit(solution)/shard_map/ppermute | solution.py:317
  5.4 6.8 %shard_map.75 = (f32[512,1152]{1,0:T(8,128)S(1)}, bf16[512,1152]{1,0:T(8,128)(2,1)S(1)}, f32[512,1152]{1,0:T(8,128)S(1)}, bf16[512,1152]{1,0:T(8,128)(2,1)S(1)},...) custom-call(bf16[256,1152]{1,0:T(8,128)(2,1)S(1)} %collective-permut, ...), custom_call_target="tpu_custom_call" | custom-call | tf_op jit(solution)/shard_map/pallas_call | solution.py:304
  12.3 0.9 %collective-permute-done.1.refs_0_ = bf16[128,1152]{1,0:T(8,128)(2,1)S(1)} collective-permute-done((bf16[128,1152]{1,0:T(8,128)(2,1)S(1)}, bf16[128,1152]{1,0:T(8,128)(2,1)S(1)}, u32[]{:S(2)}, u32[]{:S(2)}) %collective-permute-start.1) | collective-permute-done | bytes 294944 | tf_op jit(solution)/shard_map/ppermute | solution.py:317
  13.7 2.1 %collective-permute-start.9 = (bf16[256,1152]{1,0:T(8,128)(2,1)S(1)}, bf16[256,1152]{1,0:T(8,128)(2,1)S(1)}, u32[]{:S(2)}, u32[]{:S(2)}) collective-permute-start(bf16[256,1152]{1,0:T(8,128)(2,1)S(1)} %copy-done), channel_id=1, source_target_pairs={{0,2},{1,3},{2,0},{3,1},{4,6},{5,7},{6,4},{7,5},{8,10},{9,11},{10,... | collective-permute-start | bytes 1769480 | tf_op jit(solution)/shard_map/ppermute | solution.py:317
  15.8 4.9 %shard_map.76 = (f32[256,1152]{1,0:T(8,128)S(1)}, bf16[256,1152]{1,0:T(8,128)(2,1)S(1)}, bf16[512,256]{1,0:T(8,128)(2,1)S(1)}, f32[512,1152]{1,0:T(8,128)S(1)}, ...) custom-call(s32[2]{0:T(128)S(1)} %pad_add_fusion.place.place_ref, ...), custom_call_target="tpu_custom_call" | custom-call | tf_op jit(solution)/shard_map/pallas_call | solution.py:304
  21.3 0.9 %collective-permute-done.6.refs_1_.refs_4_ = bf16[64,1152]{1,0:T(8,128)(2,1)S(1)} collective-permute-done((bf16[64,1152]{1,0:T(8,128)(2,1)S(1)}, bf16[64,1152]{1,0:T(8,128)(2,1)S(1)}, u32[]{:S(2)}, u32[]{:S(2)}) %collective-permute-start.6) | collective-permute-done | bytes 147488 | tf_op jit(solution)/shard_map/ppermute | solution.py:317
  22.4 3.9 %shard_map.77 = (f32[256,1152]{1,0:T(8,128)S(1)}, bf16[256,1152]{1,0:T(8,128)(2,1)S(1)}, bf16[512,256]{1,0:T(8,128)(2,1)S(1)}, bf16[512,1152]{1,0:T(8,128)(2,1)S...) custom-call(bf16[128,1152]{1,0:T(8,128)(2,1)S(1)} %collective-permut, ...), custom_call_target="tpu_custom_call" | custom-call | tf_op jit(solution)/shard_map/pallas_call | solution.py:304
  26.4 1.6 %collective-permute-start.8 = (bf16[144,1152]{1,0:T(8,128)(2,1)S(1)}, bf16[144,1152]{1,0:T(8,128)(2,1)S(1)}, u32[]{:S(2)}, u32[]{:S(2)}) collective-permute-start(bf16[144,1152]{1,0:T(8,128)(2,1)S(1)} %get-tuple-element.81), channel_id=1, source_target_pairs={{0,4},{4,0},{8,12},{12,8},{16,20},{20,16},{24,28},{28,24},{1,5},{5... | collective-permute-start | bytes 995336 | tf_op jit(solution)/shard_map/ppermute | solution.py:317
  27.9 1.6 %collective-permute-start.12 = (bf16[144,1152]{1,0:T(8,128)(2,1)S(1)}, bf16[144,1152]{1,0:T(8,128)(2,1)S(1)}, u32[]{:S(2)}, u32[]{:S(2)}) collective-permute-start(bf16[144,1152]{1,0:T(8,128)(2,1)S(1)} %get-tuple-element.108), channel_id=1, source_target_pairs={{0,8},{4,12},{8,0},{12,4},{16,24},{20,28},{24,16},{28,20},{1,9},{5... | collective-permute-start | bytes 995336 | tf_op jit(solution)/shard_map/ppermute | solution.py:317
  29.9 2.0 %shard_map.78 = (f32[256,1152]{1,0:T(8,128)S(1)}, f32[256,1152]{1,0:T(8,128)S(1)}, bf16[288,512]{1,0:T(8,128)(2,1)S(1)}) custom-call(s32[2]{0:T(128)S(1)} %pad_add_fusion.place.place_ref, bf16[128,1152]{1,0:T(8,128)(2,1)S(1)} %collective-permute-done.1.refs_0_, bf16[64,1152]{1,0:T(8,128)(2,1)S(1)} %collective-permute-done.4.refs_1_, ...), custom_call_target="tpu_custom_call" | custom-call | tf_op jit(solution)/shard_map/pallas_call | solution.py:304
  31.9 1.9 %shard_map.79 = (bf16[128,1152]{1,0:T(8,128)(2,1)S(1)}, bf16[128,1152]{1,0:T(8,128)(2,1)S(1)}, bf16[256,512]{1,0:T(8,128)(2,1)S(1)}, bf16[256,256]{1,0:T(8,128)(2,1)S(1)}, bf16[256,256]{1,0:T(8,128)(2,1)S(1)}) custom-call(bf16[256,1152]{1,0:T(8,128)(2,1)S(1)} %collective-permute-done.9.i2, bf16[1152,1152]{1,0:T(8,128)(2,1)S(1)} %get-tuple-element.87.image_head.head, ...), custom_call_target="tpu_custom_call" | custom-call | tf_op jit(solution)/shard_map/pallas_call | solution.py:304
  34.4 0.9 %shard_map.80 = (f32[512,1152]{1,0:T(8,128)S(1)}, f32[256,1152]{1,0:T(8,128)S(1)}, f32[256,1152]{1,0:T(8,128)S(1)}) custom-call(bf16[128,1152]{1,0:T(8,128)(2,1)S(1)} %get-tuple-element.90.x_first, bf16[128,1152]{1,0:T(8,128)(2,1)S(1)} %get-tuple-element.91.x_second, bf16[256,512]{1,0:T(8,128)(2,1)S(1)} %get-tuple-element.92.w_a, ...), custom_call_target="tpu_custom_call" | custom-call | tf_op jit(solution)/shard_map/pallas_call | solution.py:304
  35.9 3.4 %shard_map.81 = (bf16[72,1152]{1,0:T(8,128)(2,1)S(1)}, bf16[72,1152]{1,0:T(8,128)(2,1)S(1)}, bf16[72,1152]{1,0:T(8,128)(2,1)S(1)}, bf16[72,1152]{1,0:T(8,128)(2,1)S(1)}, bf16[512,1152]{1,0:T(8,128)(2,1)S(1)}) custom-call(bf16[128,1152]{1,0:T(8,128)(2,1)S(1)} %collective-permute-done.10.x_first, bf16[128,1152]{1,0:T(8,128)(2,1)S(1)} %collective-permute-done.11.x_second, ...), custom_call_target="tpu_custom_call" | custom-call | tf_op jit(solution)/shard_map/pallas_call | solution.py:304
  39.4 1.6 %collective-permute-start.19 = (bf16[72,1152]{1,0:T(8,128)(2,1)S(1)}, bf16[72,1152]{1,0:T(8,128)(2,1)S(1)}, u32[]{:S(2)}, u32[]{:S(2)}) collective-permute-start(bf16[72,1152]{1,0:T(8,128)(2,1)S(1)} %get-tuple-element.116), channel_id=1, source_target_pairs={{0,4},{4,0},{8,12},{12,8},{16,20},{20,16},{24,28},{28,24},{1,5},{5... | collective-permute-start | bytes 497672 | tf_op jit(solution)/shard_map/ppermute | solution.py:317
  41.0 1.6 %collective-permute-start.20 = (bf16[72,1152]{1,0:T(8,128)(2,1)S(1)}, bf16[72,1152]{1,0:T(8,128)(2,1)S(1)}, u32[]{:S(2)}, u32[]{:S(2)}) collective-permute-start(bf16[72,1152]{1,0:T(8,128)(2,1)S(1)} %get-tuple-element.118), channel_id=1, source_target_pairs={{0,8},{4,12},{8,0},{12,4},{16,24},{20,28},{24,16},{28,20},{1,9},{5... | collective-permute-start | bytes 497672 | tf_op jit(solution)/shard_map/ppermute | solution.py:317
  42.9 2.7 %collective-permute-done.13 = bf16[144,1152]{1,0:T(8,128)(2,1)S(1)} collective-permute-done((bf16[144,1152]{1,0:T(8,128)(2,1)S(1)}, bf16[144,1152]{1,0:T(8,128)(2,1)S(1)}, u32[]{:S(2)}, u32[]{:S(2)}) %collective-permute-start.13) | collective-permute-done | bytes 331808 | tf_op jit(solution)/shard_map/ppermute | solution.py:317
  45.9 1.2 %collective-permute-start.14 = (bf16[72,1152]{1,0:T(8,128)(2,1)S(1)}, bf16[72,1152]{1,0:T(8,128)(2,1)S(1)}, u32[]{:S(2)}, u32[]{:S(2)}) collective-permute-start(bf16[72,1152]{1,0:T(8,128)(2,1)S(1)} %slice.9), channel_id=1, source_target_pairs={{0,2},{1,3},{2,0},{3,1},{4,6},{5,7},{6,4},{7,5},{8,10},{9,11},{10,... | collective-permute-start | bytes 497672 | tf_op jit(solution)/shard_map/ppermute | solution.py:317
  47.1 2.0 %shard_map.83 = f32[256,1152]{1,0:T(8,128)} custom-call(bf16[512,1152]{1,0:T(8,128)(2,1)S(1)} %get-tuple-element.113.back, bf16[1152,1152]{1,0:T(8,128)(2,1)S(1)} %get-tuple-element.71.refs_7_.refs_3_.head), custom_call_target="tpu_custom_call" | custom-call | flops 1358954496 | tf_op jit(solution)/shard_map/pallas_call | solution.py:304
  49.1 2.0 %shard_map.82 = f32[256,1152]{1,0:T(8,128)} custom-call(bf16[512,1152]{1,0:T(8,128)(2,1)S(1)} %get-tuple-element.112.back, bf16[1152,1152]{1,0:T(8,128)(2,1)S(1)} %get-tuple-element.87.image_head.head), custom_call_target="tpu_custom_call" | custom-call | flops 1358954496 | tf_op jit(solution)/shard_map/pallas_call | solution.py:304
  51.3 2.6 %collective-permute-start.15 = (bf16[72,1152]{1,0:T(8,128)(2,1)S(1)}, bf16[72,1152]{1,0:T(8,128)(2,1)S(1)}, u32[]{:S(2)}, u32[]{:S(2)}) collective-permute-start(bf16[72,1152]{1,0:T(8,128)(2,1)S(1)} %add_convert_fusion.4), channel_id=1, source_target_pairs={{0,16},{4,20},{8,24},{12,28},{16,0},{20,4},{24,8},{28,12},{1,17},{... | collective-permute-start | bytes 497672 | tf_op jit(solution)/shard_map/ppermute | solution.py:317
  54.1 5.6 %collective-permute-done.15 = bf16[72,1152]{1,0:T(8,128)(2,1)S(1)} collective-permute-done((bf16[72,1152]{1,0:T(8,128)(2,1)S(1)}, bf16[72,1152]{1,0:T(8,128)(2,1)S(1)}, u32[]{:S(2)}, u32[]{:S(2)}) %collective-permute-start.15) | collective-permute-done | bytes 165920 | tf_op jit(solution)/shard_map/ppermute | solution.py:317
  60.4 1.5 %collective-permute-start.17 = (bf16[72,1152]{1,0:T(8,128)(2,1)S(1)}, bf16[72,1152]{1,0:T(8,128)(2,1)S(1)}, u32[]{:S(2)}, u32[]{:S(2)}) collective-permute-start(bf16[72,1152]{1,0:T(8,128)(2,1)S(1)} %add_convert_fusion.3.refs_0_), channel_id=1, source_target_pairs={{0,4},{4,0},{8,12},{12,8},{16,20},{20,16},{24,28},{28,24},{1,5},{5... | collective-permute-start | bytes 497672 | tf_op jit(solution)/shard_map/ppermute | solution.py:317
  62.0 5.2 %collective-permute-start.18 = (bf16[72,1152]{1,0:T(8,128)(2,1)S(1)}, bf16[72,1152]{1,0:T(8,128)(2,1)S(1)}, u32[]{:S(2)}, u32[]{:S(2)}) collective-permute-start(bf16[72,1152]{1,0:T(8,128)(2,1)S(1)} %add_convert_fusion.3.refs_0_), channel_id=1, source_target_pairs={{0,8},{4,12},{8,0},{12,4},{16,24},{20,28},{24,16},{28,20},{1,9},{5... | collective-permute-start | bytes 497672 | tf_op jit(solution)/shard_map/ppermute | solution.py:317
  67.1 1.8 %collective-permute-done.22 = bf16[72,1152]{1,0:T(8,128)(2,1)S(1)} collective-permute-done((bf16[72,1152]{1,0:T(8,128)(2,1)S(1)}, bf16[72,1152]{1,0:T(8,128)(2,1)S(1)}, u32[]{:S(2)}, u32[]{:S(2)}) %collective-permute-start.22) | collective-permute-done | bytes 165920 | tf_op jit(solution)/shard_map/ppermute | solution.py:317
  69.0 1.5 %collective-permute-start.24 = (bf16[72,1152]{1,0:T(8,128)(2,1)S(1)}, bf16[72,1152]{1,0:T(8,128)(2,1)S(1)}, u32[]{:S(2)}, u32[]{:S(2)}) collective-permute-start(bf16[72,1152]{1,0:T(8,128)(2,1)S(1)} %add_convert_fusion.1.refs_0_), channel_id=1, source_target_pairs={{0,4},{4,0},{8,12},{12,8},{16,20},{20,16},{24,28},{28,24},{1,5},{5... | collective-permute-start | bytes 497672 | tf_op jit(solution)/shard_map/ppermute | solution.py:317
  70.5 5.9 %collective-permute-start.25 = (bf16[72,1152]{1,0:T(8,128)(2,1)S(1)}, bf16[72,1152]{1,0:T(8,128)(2,1)S(1)}, u32[]{:S(2)}, u32[]{:S(2)}) collective-permute-start(bf16[72,1152]{1,0:T(8,128)(2,1)S(1)} %add_convert_fusion.1.refs_0_), channel_id=1, source_target_pairs={{0,8},{4,12},{8,0},{12,4},{16,24},{20,28},{24,16},{28,20},{1,9},{5... | collective-permute-start | bytes 497672 | tf_op jit(solution)/shard_map/ppermute | solution.py:317
  76.4 1.5 %shard_map.84.refs_1_ = f32[288,1152]{1,0:T(8,128)} custom-call(s32[2]{0:T(128)S(1)} %pad_add_fusion.place.place_ref, bf16[72,1152]{1,0:T(8,128)(2,1)S(1)} %add_convert_fusion.3.refs_0_, bf16[72,1152]{1,0:T(8,128)(2,1)S(1)} %collective-permute-done.17.refs_1_, bf16[72,1152]{1,0:T(8,128)(2,1)S(1)} %collective-permute-done.18.refs_2_), custom_call_target="tpu_custom_call" | custom-call | tf_op jit(solution)/shard_map/pallas_call | solution.py:282
  78.0 1.3 %shard_map.85 = f32[288,1152]{1,0:T(8,128)} custom-call(s32[2]{0:T(128)S(1)} %pad_add_fusion.place.place_ref, bf16[72,1152]{1,0:T(8,128)(2,1)S(1)} %collective-permute-done.16.refs_0_, f32[288,1152]{1,0:T(8,128)} %shard_map.84.refs_1_), custom_call_target="tpu_custom_call", output_to_operand_aliasing={{}: (2, {})} | custom-call | tf_op jit(solution)/shard_map/pallas_call | solution.py:282
  79.9 1.5 %shard_map.86.refs_1_ = f32[288,1152]{1,0:T(8,128)} custom-call(s32[2]{0:T(128)S(1)} %pad_add_fusion.place.place_ref, bf16[72,1152]{1,0:T(8,128)(2,1)S(1)} %add_convert_fusion.1.refs_0_, bf16[72,1152]{1,0:T(8,128)(2,1)S(1)} %collective-permute-done.24.refs_1_, bf16[72,1152]{1,0:T(8,128)(2,1)S(1)} %collective-permute-done.25.refs_2_), custom_call_target="tpu_custom_call" | custom-call | tf_op jit(solution)/shard_map/pallas_call | solution.py:282
  81.4 1.2 %collective-permute-done.23.refs_0_ = bf16[72,1152]{1,0:T(8,128)(2,1)S(1)} collective-permute-done((bf16[72,1152]{1,0:T(8,128)(2,1)S(1)}, bf16[72,1152]{1,0:T(8,128)(2,1)S(1)}, u32[]{:S(2)}, u32[]{:S(2)}) %collective-permute-start.23) | collective-permute-done | bytes 165920 | tf_op jit(solution)/shard_map/ppermute | solution.py:317
  82.7 1.3 %shard_map.87 = f32[288,1152]{1,0:T(8,128)} custom-call(s32[2]{0:T(128)S(1)} %pad_add_fusion.place.place_ref, bf16[72,1152]{1,0:T(8,128)(2,1)S(1)} %collective-permute-done.23.refs_0_, f32[288,1152]{1,0:T(8,128)} %shard_map.86.refs_1_), custom_call_target="tpu_custom_call", output_to_operand_aliasing={{}: (2, {})} | custom-call | tf_op jit(solution)/shard_map/pallas_call | solution.py:282
  (45 shorter events, 5.9 us)
Async XLA Ops:
  0.7 4.7 %collective-permute-start.2 = (bf16[256,1152]{1,0:T(8,128)(2,1)}, bf16[256,1152]{1,0:T(8,128)(2,1)S(1)}, u32[]{:S(2)}, u32[]{:S(2)}) collective-permute-start(bf16[256,1152]{1,0:T(8,128)(2,1)} %t0_far), channel_id=1, source_target_pairs={{0,1},{1,0},{2,3},{3,2},{4,5},{5,4},{6,7},{7,6},{8,9},{9,8},{10,11... | collective-permute-start | bytes 1769480 | tf_op jit(solution)/shard_map/ppermute | solution.py:317
  1.2 4.3 %collective-permute-start.3 = (bf16[256,1152]{1,0:T(8,128)(2,1)}, bf16[256,1152]{1,0:T(8,128)(2,1)S(1)}, u32[]{:S(2)}, u32[]{:S(2)}) collective-permute-start(bf16[256,1152]{1,0:T(8,128)(2,1)} %i0_far), channel_id=1, source_target_pairs={{0,1},{1,0},{2,3},{3,2},{4,5},{5,4},{6,7},{7,6},{8,9},{9,8},{10,11... | collective-permute-start | bytes 1769480 | tf_op jit(solution)/shard_map/ppermute | solution.py:317
  2.3 10.8 %collective-permute-start.1 = (bf16[128,1152]{1,0:T(8,128)(2,1)S(1)}, bf16[128,1152]{1,0:T(8,128)(2,1)S(1)}, u32[]{:S(2)}, u32[]{:S(2)}) collective-permute-start(bf16[128,1152]{1,0:T(8,128)(2,1)S(1)} %get-tuple-element.124), channel_id=1, source_target_pairs={{0,2},{1,3},{2,0},{3,1},{4,6},{5,7},{6,4},{7,5},{8,10},{9,11},{10,... | collective-permute-start | bytes 884744 | tf_op jit(solution)/shard_map/ppermute | solution.py:317
  5.3 8.4 %copy-start = (bf16[256,1152]{1,0:T(8,128)(2,1)S(1)}, bf16[256,1152]{1,0:T(8,128)(2,1)}, u32[]{:S(2)}) copy-start(bf16[256,1152]{1,0:T(8,128)(2,1)} %i0_far) | copy-start | bytes 1769476
  5.3 15.4 %collective-permute-start = (bf16[128,1152]{1,0:T(8,128)(2,1)S(1)}, bf16[128,1152]{1,0:T(8,128)(2,1)S(1)}, u32[]{:S(2)}, u32[]{:S(2)}) collective-permute-start(bf16[128,1152]{1,0:T(8,128)(2,1)S(1)} %get-tuple-element.125), channel_id=1, source_target_pairs={{0,2},{1,3},{2,0},{3,1},{4,6},{5,7},{6,4},{7,5},{8,10},{9,11},{10,... | collective-permute-start | bytes 884744 | tf_op jit(solution)/shard_map/ppermute | solution.py:317
  13.2 2.6 %collective-permute-start.4 = (bf16[64,1152]{1,0:T(8,128)(2,1)S(1)}, bf16[64,1152]{1,0:T(8,128)(2,1)S(1)}, u32[]{:S(2)}, u32[]{:S(2)}) collective-permute-start(bf16[64,1152]{1,0:T(8,128)(2,1)S(1)} %get-tuple-element.129), channel_id=1, source_target_pairs={{0,1},{1,0},{2,3},{3,2},{4,5},{5,4},{6,7},{7,6},{8,9},{9,8},{10,11... | collective-permute-start | bytes 442376 | tf_op jit(solution)/shard_map/ppermute | solution.py:317
  13.2 2.6 %collective-permute-start.5 = (bf16[64,1152]{1,0:T(8,128)(2,1)S(1)}, bf16[64,1152]{1,0:T(8,128)(2,1)S(1)}, u32[]{:S(2)}, u32[]{:S(2)}) collective-permute-start(bf16[64,1152]{1,0:T(8,128)(2,1)S(1)} %get-tuple-element.128), channel_id=1, source_target_pairs={{0,1},{1,0},{2,3},{3,2},{4,5},{5,4},{6,7},{7,6},{8,9},{9,8},{10,11... | collective-permute-start | bytes 442376 | tf_op jit(solution)/shard_map/ppermute | solution.py:317
  13.7 18.2 %collective-permute-start.9 = (bf16[256,1152]{1,0:T(8,128)(2,1)S(1)}, bf16[256,1152]{1,0:T(8,128)(2,1)S(1)}, u32[]{:S(2)}, u32[]{:S(2)}) collective-permute-start(bf16[256,1152]{1,0:T(8,128)(2,1)S(1)} %copy-done), channel_id=1, source_target_pairs={{0,2},{1,3},{2,0},{3,1},{4,6},{5,7},{6,4},{7,5},{8,10},{9,11},{10,... | collective-permute-start | bytes 1769480 | tf_op jit(solution)/shard_map/ppermute | solution.py:317
  20.8 1.4 %collective-permute-start.6 = (bf16[64,1152]{1,0:T(8,128)(2,1)S(1)}, bf16[64,1152]{1,0:T(8,128)(2,1)S(1)}, u32[]{:S(2)}, u32[]{:S(2)}) collective-permute-start(bf16[64,1152]{1,0:T(8,128)(2,1)S(1)} %get-tuple-element.127), channel_id=1, source_target_pairs={{0,1},{1,0},{2,3},{3,2},{4,5},{5,4},{6,7},{7,6},{8,9},{9,8},{10,11... | collective-permute-start | bytes 442376 | tf_op jit(solution)/shard_map/ppermute | solution.py:317
  20.8 1.6 %collective-permute-start.7 = (bf16[64,1152]{1,0:T(8,128)(2,1)S(1)}, bf16[64,1152]{1,0:T(8,128)(2,1)S(1)}, u32[]{:S(2)}, u32[]{:S(2)}) collective-permute-start(bf16[64,1152]{1,0:T(8,128)(2,1)S(1)} %get-tuple-element.126), channel_id=1, source_target_pairs={{0,1},{1,0},{2,3},{3,2},{4,5},{5,4},{6,7},{7,6},{8,9},{9,8},{10,11... | collective-permute-start | bytes 442376 | tf_op jit(solution)/shard_map/ppermute | solution.py:317
  26.4 16.2 %collective-permute-start.8 = (bf16[144,1152]{1,0:T(8,128)(2,1)S(1)}, bf16[144,1152]{1,0:T(8,128)(2,1)S(1)}, u32[]{:S(2)}, u32[]{:S(2)}) collective-permute-start(bf16[144,1152]{1,0:T(8,128)(2,1)S(1)} %get-tuple-element.81), channel_id=1, source_target_pairs={{0,4},{4,0},{8,12},{12,8},{16,20},{20,16},{24,28},{28,24},{1,5},{5... | collective-permute-start | bytes 995336 | tf_op jit(solution)/shard_map/ppermute | solution.py:317
  27.9 15.0 %collective-permute-start.12 = (bf16[144,1152]{1,0:T(8,128)(2,1)S(1)}, bf16[144,1152]{1,0:T(8,128)(2,1)S(1)}, u32[]{:S(2)}, u32[]{:S(2)}) collective-permute-start(bf16[144,1152]{1,0:T(8,128)(2,1)S(1)} %get-tuple-element.108), channel_id=1, source_target_pairs={{0,8},{4,12},{8,0},{12,4},{16,24},{20,28},{24,16},{28,20},{1,9},{5... | collective-permute-start | bytes 995336 | tf_op jit(solution)/shard_map/ppermute | solution.py:317
  29.5 16.2 %collective-permute-start.13 = (bf16[144,1152]{1,0:T(8,128)(2,1)S(1)}, bf16[144,1152]{1,0:T(8,128)(2,1)S(1)}, u32[]{:S(2)}, u32[]{:S(2)}) collective-permute-start(bf16[144,1152]{1,0:T(8,128)(2,1)S(1)} %get-tuple-element.110), channel_id=1, source_target_pairs={{0,12},{4,8},{8,4},{12,0},{16,28},{20,24},{24,20},{28,16},{1,13},{... | collective-permute-start | bytes 995336 | tf_op jit(solution)/shard_map/ppermute | solution.py:317
  33.9 1.6 %collective-permute-start.11 = (bf16[128,1152]{1,0:T(8,128)(2,1)S(1)}, bf16[128,1152]{1,0:T(8,128)(2,1)S(1)}, u32[]{:S(2)}, u32[]{:S(2)}) collective-permute-start(bf16[128,1152]{1,0:T(8,128)(2,1)S(1)} %get-tuple-element.91.x_second), channel_id=1, source_target_pairs={{0,1},{1,0},{2,3},{3,2},{4,5},{5,4},{6,7},{7,6},{8,9},{9,8},{10,11... | collective-permute-start | bytes 884744 | tf_op jit(solution)/shard_map/ppermute | solution.py:317
  33.9 2.0 %collective-permute-start.10 = (bf16[128,1152]{1,0:T(8,128)(2,1)S(1)}, bf16[128,1152]{1,0:T(8,128)(2,1)S(1)}, u32[]{:S(2)}, u32[]{:S(2)}) collective-permute-start(bf16[128,1152]{1,0:T(8,128)(2,1)S(1)} %get-tuple-element.90.x_first), channel_id=1, source_target_pairs={{0,1},{1,0},{2,3},{3,2},{4,5},{5,4},{6,7},{7,6},{8,9},{9,8},{10,11... | collective-permute-start | bytes 884744 | tf_op jit(solution)/shard_map/ppermute | solution.py:317
  39.4 14.6 %collective-permute-start.19 = (bf16[72,1152]{1,0:T(8,128)(2,1)S(1)}, bf16[72,1152]{1,0:T(8,128)(2,1)S(1)}, u32[]{:S(2)}, u32[]{:S(2)}) collective-permute-start(bf16[72,1152]{1,0:T(8,128)(2,1)S(1)} %get-tuple-element.116), channel_id=1, source_target_pairs={{0,4},{4,0},{8,12},{12,8},{16,20},{20,16},{24,28},{28,24},{1,5},{5... | collective-permute-start | bytes 497672 | tf_op jit(solution)/shard_map/ppermute | solution.py:317
  41.0 13.0 %collective-permute-start.20 = (bf16[72,1152]{1,0:T(8,128)(2,1)S(1)}, bf16[72,1152]{1,0:T(8,128)(2,1)S(1)}, u32[]{:S(2)}, u32[]{:S(2)}) collective-permute-start(bf16[72,1152]{1,0:T(8,128)(2,1)S(1)} %get-tuple-element.118), channel_id=1, source_target_pairs={{0,8},{4,12},{8,0},{12,4},{16,24},{20,28},{24,16},{28,20},{1,9},{5... | collective-permute-start | bytes 497672 | tf_op jit(solution)/shard_map/ppermute | solution.py:317
  42.5 11.5 %collective-permute-start.21 = (bf16[72,1152]{1,0:T(8,128)(2,1)S(1)}, bf16[72,1152]{1,0:T(8,128)(2,1)S(1)}, u32[]{:S(2)}, u32[]{:S(2)}) collective-permute-start(bf16[72,1152]{1,0:T(8,128)(2,1)S(1)} %get-tuple-element.120), channel_id=1, source_target_pairs={{0,12},{4,8},{8,4},{12,0},{16,28},{20,24},{24,20},{28,16},{1,13},{... | collective-permute-start | bytes 497672 | tf_op jit(solution)/shard_map/ppermute | solution.py:317
  45.9 5.4 %collective-permute-start.14 = (bf16[72,1152]{1,0:T(8,128)(2,1)S(1)}, bf16[72,1152]{1,0:T(8,128)(2,1)S(1)}, u32[]{:S(2)}, u32[]{:S(2)}) collective-permute-start(bf16[72,1152]{1,0:T(8,128)(2,1)S(1)} %slice.9), channel_id=1, source_target_pairs={{0,2},{1,3},{2,0},{3,1},{4,6},{5,7},{6,4},{7,5},{8,10},{9,11},{10,... | collective-permute-start | bytes 497672 | tf_op jit(solution)/shard_map/ppermute | solution.py:317
  51.3 8.3 %collective-permute-start.15 = (bf16[72,1152]{1,0:T(8,128)(2,1)S(1)}, bf16[72,1152]{1,0:T(8,128)(2,1)S(1)}, u32[]{:S(2)}, u32[]{:S(2)}) collective-permute-start(bf16[72,1152]{1,0:T(8,128)(2,1)S(1)} %add_convert_fusion.4), channel_id=1, source_target_pairs={{0,16},{4,20},{8,24},{12,28},{16,0},{20,4},{24,8},{28,12},{1,17},{... | collective-permute-start | bytes 497672 | tf_op jit(solution)/shard_map/ppermute | solution.py:317
  59.7 9.2 %collective-permute-start.22 = (bf16[72,1152]{1,0:T(8,128)(2,1)S(1)}, bf16[72,1152]{1,0:T(8,128)(2,1)S(1)}, u32[]{:S(2)}, u32[]{:S(2)}) collective-permute-start(bf16[72,1152]{1,0:T(8,128)(2,1)S(1)} %add_convert_fusion.2), channel_id=1, source_target_pairs={{0,16},{4,20},{8,24},{12,28},{16,0},{20,4},{24,8},{28,12},{1,17},{... | collective-permute-start | bytes 497672 | tf_op jit(solution)/shard_map/ppermute | solution.py:317
  60.4 8.5 %collective-permute-start.17 = (bf16[72,1152]{1,0:T(8,128)(2,1)S(1)}, bf16[72,1152]{1,0:T(8,128)(2,1)S(1)}, u32[]{:S(2)}, u32[]{:S(2)}) collective-permute-start(bf16[72,1152]{1,0:T(8,128)(2,1)S(1)} %add_convert_fusion.3.refs_0_), channel_id=1, source_target_pairs={{0,4},{4,0},{8,12},{12,8},{16,20},{20,16},{24,28},{28,24},{1,5},{5... | collective-permute-start | bytes 497672 | tf_op jit(solution)/shard_map/ppermute | solution.py:317
  62.0 14.5 %collective-permute-start.18 = (bf16[72,1152]{1,0:T(8,128)(2,1)S(1)}, bf16[72,1152]{1,0:T(8,128)(2,1)S(1)}, u32[]{:S(2)}, u32[]{:S(2)}) collective-permute-start(bf16[72,1152]{1,0:T(8,128)(2,1)S(1)} %add_convert_fusion.3.refs_0_), channel_id=1, source_target_pairs={{0,8},{4,12},{8,0},{12,4},{16,24},{20,28},{24,16},{28,20},{1,9},{5... | collective-permute-start | bytes 497672 | tf_op jit(solution)/shard_map/ppermute | solution.py:317
  67.1 10.9 %collective-permute-start.16 = (bf16[72,1152]{1,0:T(8,128)(2,1)S(1)}, bf16[72,1152]{1,0:T(8,128)(2,1)S(1)}, u32[]{:S(2)}, u32[]{:S(2)}) collective-permute-start(bf16[72,1152]{1,0:T(8,128)(2,1)S(1)} %add_convert_fusion.3.refs_0_), channel_id=1, source_target_pairs={{0,12},{4,8},{8,4},{12,0},{16,28},{20,24},{24,20},{28,16},{1,13},{... | collective-permute-start | bytes 497672 | tf_op jit(solution)/shard_map/ppermute | solution.py:317
  69.0 10.3 %collective-permute-start.24 = (bf16[72,1152]{1,0:T(8,128)(2,1)S(1)}, bf16[72,1152]{1,0:T(8,128)(2,1)S(1)}, u32[]{:S(2)}, u32[]{:S(2)}) collective-permute-start(bf16[72,1152]{1,0:T(8,128)(2,1)S(1)} %add_convert_fusion.1.refs_0_), channel_id=1, source_target_pairs={{0,4},{4,0},{8,12},{12,8},{16,20},{20,16},{24,28},{28,24},{1,5},{5... | collective-permute-start | bytes 497672 | tf_op jit(solution)/shard_map/ppermute | solution.py:317
  70.5 9.4 %collective-permute-start.25 = (bf16[72,1152]{1,0:T(8,128)(2,1)S(1)}, bf16[72,1152]{1,0:T(8,128)(2,1)S(1)}, u32[]{:S(2)}, u32[]{:S(2)}) collective-permute-start(bf16[72,1152]{1,0:T(8,128)(2,1)S(1)} %add_convert_fusion.1.refs_0_), channel_id=1, source_target_pairs={{0,8},{4,12},{8,0},{12,4},{16,24},{20,28},{24,16},{28,20},{1,9},{5... | collective-permute-start | bytes 497672 | tf_op jit(solution)/shard_map/ppermute | solution.py:317
  76.4 6.2 %collective-permute-start.23 = (bf16[72,1152]{1,0:T(8,128)(2,1)S(1)}, bf16[72,1152]{1,0:T(8,128)(2,1)S(1)}, u32[]{:S(2)}, u32[]{:S(2)}) collective-permute-start(bf16[72,1152]{1,0:T(8,128)(2,1)S(1)} %add_convert_fusion.1.refs_0_), channel_id=1, source_target_pairs={{0,12},{4,8},{8,4},{12,0},{16,28},{20,24},{24,20},{28,16},{1,13},{... | collective-permute-start | bytes 497672 | tf_op jit(solution)/shard_map/ppermute | solution.py:317

commit v10 on v9

--- a/solution.py
+++ b/solution.py
@@ -191,14 +191,28 @@
 
 
 def image_kernel(*refs):
-    *features, text_head, p_a, x_a, gx_in, pick_i, q_3, y_3, w_a3, dp_a, h0, h1, h2, h3, dots, gx = refs
+    *features, text_head, p_a, x_a, gx_in, pick_i, q_3, y_3, w_a3, dp_a = refs[:-8]
+    near_0, near_2, near_sent, far_0, far_1, far_sent, dots, gx = refs[-8:]
     q_3[...] = dot_nn(rows_of(features), text_head[...])
     unit_rows(q_3, y_3)
     dots[...] = dot_nt(x_a[...], y_3[...])
     weight_rows(dots, w_a3)
     gx[...] = gx_in[...] + dot_nn(w_a3[...], y_3[...])
     back_rows(p_a, gx, dp_a)
-    split_head(dot_nn(pick_i[...], dp_a[...]), (h0, h1, h2, h3))
+    head = dot_nn(pick_i[...], dp_a[...]).astype(BF16)
+    part = near_0.shape[0]
+    near_side, far_side = (
+        [head[first : first + part, :] for first in range(side * part, 2 * QUAD * part, 2 * part)]
+        for side in range(2)
+    )
+    near_0[...] = near_side[0]
+    near_2[...] = near_side[2]
+    near_sent[:part, :] = near_side[1]
+    near_sent[part:, :] = near_side[3]
+    far_0[...] = far_side[0]
+    far_1[...] = far_side[1]
+    far_sent[:part, :] = far_side[2]
+    far_sent[part:, :] = far_side[3]
 
 
 def text_pull_kernel(place, *refs):
@@ -375,14 +389,15 @@
         place,
     )
     second = both(t2[1], gy_a, 2)
-    q_3, y_3, w_a3, dp_a, *image_parts = call(
+    part_b, parts_b = ((part, width), BF16), ((2 * part, width), BF16)
+    q_3, y_3, w_a3, dp_a, near_0, near_2, near_sent, far_0, far_1, far_sent = call(
         image_kernel,
-        [tall, tall_b, side_w, wide_b] + [((2 * part, width), BF16)] * QUAD,
+        [tall, tall_b, side_w, wide_b] + [part_b, part_b, parts_b] * 2,
         [side_dots, wide],
         (*second, text_head, p_a, x_a, gx, pick_i),
         8,
     )
-    image_others = [cuts(image_parts[k], mask=k) for k in range(1, QUAD)]
+    near_came, far_came = cuts(near_sent, mask=1), cuts(far_sent, mask=2)
     gy_2, gy_3, pick_b = call(
         text_pull_kernel,
         [tall, tall, pick_one],
@@ -407,7 +422,10 @@
         (*x_2, w_2a, w_22, w_23, gy_a, gy_2, gy_3),
         8,
     )
-    x_3 = [after(rows, gy_a) for rows in x_3]
+    near_came, far_came = after(near_came, gy_a), after(far_came, gy_a)
+    near_sent, far_sent = add(near_2, [near_came[part:]]), add(far_1, [far_came[part:]])
+    near_last, far_last = cuts(near_sent, mask=2), cuts(far_sent, mask=1)
+    x_3 = [after(rows, (gy_a, near_sent, far_sent)) for rows in x_3]
     *text_parts, dq_a = call(
         last_kernel,
         [((part, width), BF16)] * QUAD + [wide_b],
@@ -417,17 +435,16 @@
         16,
     )
     text_others = [cuts(text_parts[k], mask=k) for k in range(1, QUAD)]
-    image_others = [after(other, dq_a) for other in image_others]
-    image_sum = add(image_parts[0], image_others)
+    far_sum = add(far_0, [far_came[:part], after(far_last, dq_a)])
+    near_sum = add(near_0, [near_came[:part], after(near_last, dq_a)])
+    image_sum = add(near_sum, [loop(far_sum, mask=2)])
     grads = [
         call(grad_kernel, [tall], [], (after(back, image_sum), head), 4, macs=2 * macs, keep=False)[0]
         for back, head in ((dp_a, image_head), (dq_a, text_head))
     ]
-    image_sum = add(image_sum[:part], [after(loop(image_sum[part:], mask=2), grads)])
     text_sum = add(text_parts[0], [after(other, image_sum) for other in text_others])
-    image_sum = add(image_sum, [cuts(image_sum, mask=QUAD)])
+    image_sum = add(image_sum, [after(cuts(image_sum, mask=QUAD), grads)])
     image_pieces = spread(image_sum)
-    text_sum = after(text_sum, image_sum)
     text_sum = add(text_sum, [after(cuts(text_sum, mask=QUAD), image_pieces[1])])
     image_out = placed(image_pieces)
     text_out = placed(spread(text_sum))

time: 84.3 us -> 82.1 us (0.974)
  starting transfers between devices: 33.2 us -> 29.5 us
  waiting for transfers between devices: 14.6 us -> 16.1 us
    ppermute x26 -> x27, starting transfers between devices: 33.2 us -> 29.5 us  [swap(): return lax.ppermute(array, axis, [(i, i ^ mask) for i in range(size)])]
    ppermute x26 -> x27, waiting for transfers between devices: 14.6 us -> 16.1 us  [swap(): return lax.ppermute(array, axis, [(i, i ^ mask) for i in range(size)])]
  transfers between devices with their start and end apart: 26 -> 27, of which waited for: 11 -> 13; matrix products, arithmetic and copies ran while one was open for 2% -> 2% of each run, Pallas kernels for 38% -> 40%
where the time goes in v10:
time: 82.1 us; the launch traced here: 81.9 us
  Pallas kernels  33.7 us (41%)
  starting transfers between devices  29.5 us (36%)
  waiting for transfers between devices  16.1 us (20%)
  local copies, waits for them, and re-layouts  1.15 us (1%)
  between operations  0.98 us (1%)
    ppermute x27, starting transfers between devices, swap(): return lax.ppermute(array, axis, [(i, i ^ mask) for i in range(size)])  29.5 us
    pallas_call x9, Pallas kernels, call(): pl.pallas_call(kernel, out_shape=[shape(s, t) for s, t in outs], in_specs...  28.1 us
    ppermute x27, waiting for transfers between devices, swap(): return lax.ppermute(array, axis, [(i, i ^ mask) for i in range(size)])  16.1 us
    pallas_call x4, Pallas kernels, place_pieces(): pl.pallas_call(lambda place_ref, *refs: place_kernel(place_ref, ks, *refs...  5.66 us
  transfers between devices with their start and end apart: 27, of which 13 were waited for; matrix products, arithmetic and copies ran while one was open for 2% of the time, Pallas kernels for 40%

profile of v10, /device:TPU:0, one launch (start us, length us, event | category | flops | bytes accessed | tf_op | source)
XLA Modules:
  0.0 81.9 jit_solution(5714654687135848860)
XLA Ops:
  1.2 1.1 %fusion = (bf16[128,1152]{1,0:T(8,128)(2,1)S(1)}, bf16[128,1152]{1,0:T(8,128)(2,1)S(1)}) fusion(bf16[256,1152]{1,0:T(8,128)(2,1)} %t0_far), kind=kLoop, calls=%fused_computation.9 | loop fusion | bytes 1179648 | tf_op jit(solution)/shard_map/split | solution.py:361
  2.3 3.0 %collective-permute-start.1 = (bf16[128,1152]{1,0:T(8,128)(2,1)S(1)}, bf16[128,1152]{1,0:T(8,128)(2,1)S(1)}, u32[]{:S(2)}, u32[]{:S(2)}) collective-permute-start(bf16[128,1152]{1,0:T(8,128)(2,1)S(1)} %get-tuple-element.128), channel_id=1, source_target_pairs={{0,2},{1,3},{2,0},{3,1},{4,6},{5,7},{6,4},{7,5},{8,10},{9,11},{10,... | collective-permute-start | bytes 884744 | tf_op jit(solution)/shard_map/ppermute | solution.py:331
  5.4 6.8 %shard_map.75 = (f32[512,1152]{1,0:T(8,128)S(1)}, bf16[512,1152]{1,0:T(8,128)(2,1)S(1)}, f32[512,1152]{1,0:T(8,128)S(1)}, bf16[512,1152]{1,0:T(8,128)(2,1)S(1)},...) custom-call(bf16[256,1152]{1,0:T(8,128)(2,1)S(1)} %collective-permut, ...), custom_call_target="tpu_custom_call" | custom-call | tf_op jit(solution)/shard_map/pallas_call | solution.py:318
  13.7 2.1 %collective-permute-start.9 = (bf16[256,1152]{1,0:T(8,128)(2,1)S(1)}, bf16[256,1152]{1,0:T(8,128)(2,1)S(1)}, u32[]{:S(2)}, u32[]{:S(2)}) collective-permute-start(bf16[256,1152]{1,0:T(8,128)(2,1)S(1)} %copy-done), channel_id=1, source_target_pairs={{0,2},{1,3},{2,0},{3,1},{4,6},{5,7},{6,4},{7,5},{8,10},{9,11},{10,... | collective-permute-start | bytes 1769480 | tf_op jit(solution)/shard_map/ppermute | solution.py:331
  15.8 4.9 %shard_map.76 = (f32[256,1152]{1,0:T(8,128)S(1)}, bf16[256,1152]{1,0:T(8,128)(2,1)S(1)}, bf16[512,256]{1,0:T(8,128)(2,1)S(1)}, f32[512,1152]{1,0:T(8,128)S(1)}, ...) custom-call(s32[2]{0:T(128)S(1)} %pad_add_fusion.place.place_ref, ...), custom_call_target="tpu_custom_call" | custom-call | tf_op jit(solution)/shard_map/pallas_call | solution.py:318
  22.4 3.9 %shard_map.77 = (f32[256,1152]{1,0:T(8,128)S(1)}, bf16[256,1152]{1,0:T(8,128)(2,1)S(1)}, bf16[512,256]{1,0:T(8,128)(2,1)S(1)}, bf16[512,1152]{1,0:T(8,128)(2,1)S...) custom-call(bf16[128,1152]{1,0:T(8,128)(2,1)S(1)} %collective-permut, ...), custom_call_target="tpu_custom_call" | custom-call | tf_op jit(solution)/shard_map/pallas_call | solution.py:318
  26.4 1.6 %collective-permute-start.8 = (bf16[144,1152]{1,0:T(8,128)(2,1)S(1)}, bf16[144,1152]{1,0:T(8,128)(2,1)S(1)}, u32[]{:S(2)}, u32[]{:S(2)}) collective-permute-start(bf16[144,1152]{1,0:T(8,128)(2,1)S(1)} %get-tuple-element.83), channel_id=1, source_target_pairs={{0,4},{4,0},{8,12},{12,8},{16,20},{20,16},{24,28},{28,24},{1,5},{5... | collective-permute-start | bytes 995336 | tf_op jit(solution)/shard_map/ppermute | solution.py:331
  27.9 1.6 %collective-permute-start.12 = (bf16[144,1152]{1,0:T(8,128)(2,1)S(1)}, bf16[144,1152]{1,0:T(8,128)(2,1)S(1)}, u32[]{:S(2)}, u32[]{:S(2)}) collective-permute-start(bf16[144,1152]{1,0:T(8,128)(2,1)S(1)} %get-tuple-element.102), channel_id=1, source_target_pairs={{0,8},{4,12},{8,0},{12,4},{16,24},{20,28},{24,16},{28,20},{1,9},{5... | collective-permute-start | bytes 995336 | tf_op jit(solution)/shard_map/ppermute | solution.py:331
  29.5 2.0 %shard_map.78 = (f32[256,1152]{1,0:T(8,128)S(1)}, f32[256,1152]{1,0:T(8,128)S(1)}, bf16[288,512]{1,0:T(8,128)(2,1)S(1)}) custom-call(s32[2]{0:T(128)S(1)} %pad_add_fusion.place.place_ref, bf16[128,1152]{1,0:T(8,128)(2,1)S(1)} %collective-permute-done.1.refs_0_, bf16[64,1152]{1,0:T(8,128)(2,1)S(1)} %collective-permute-done.4.refs_1_, ...), custom_call_target="tpu_custom_call" | custom-call | tf_op jit(solution)/shard_map/pallas_call | solution.py:318
  31.5 1.9 %shard_map.79 = (bf16[128,1152]{1,0:T(8,128)(2,1)S(1)}, bf16[128,1152]{1,0:T(8,128)(2,1)S(1)}, bf16[256,512]{1,0:T(8,128)(2,1)S(1)}, bf16[256,256]{1,0:T(8,128)(2,1)S(1)}, bf16[256,256]{1,0:T(8,128)(2,1)S(1)}) custom-call(bf16[256,1152]{1,0:T(8,128)(2,1)S(1)} %collective-permute-done.9.i2, bf16[1152,1152]{1,0:T(8,128)(2,1)S(1)} %get-tuple-element.89.image_head.head, ...), custom_call_target="tpu_custom_call" | custom-call | tf_op jit(solution)/shard_map/pallas_call | solution.py:318
  34.9 1.5 %collective-permute-done.8 = bf16[144,1152]{1,0:T(8,128)(2,1)S(1)} collective-permute-done((bf16[144,1152]{1,0:T(8,128)(2,1)S(1)}, bf16[144,1152]{1,0:T(8,128)(2,1)S(1)}, u32[]{:S(2)}, u32[]{:S(2)}) %collective-permute-start.8) | collective-permute-done | bytes 331808 | tf_op jit(solution)/shard_map/ppermute | solution.py:331
  36.4 1.2 %collective-permute-done.12 = bf16[144,1152]{1,0:T(8,128)(2,1)S(1)} collective-permute-done((bf16[144,1152]{1,0:T(8,128)(2,1)S(1)}, bf16[144,1152]{1,0:T(8,128)(2,1)S(1)}, u32[]{:S(2)}, u32[]{:S(2)}) %collective-permute-start.12) | collective-permute-done | bytes 331808 | tf_op jit(solution)/shard_map/ppermute | solution.py:331
  38.3 1.6 %collective-permute-start.10 = (bf16[72,1152]{1,0:T(8,128)(2,1)S(1)}, bf16[72,1152]{1,0:T(8,128)(2,1)S(1)}, u32[]{:S(2)}, u32[]{:S(2)}) collective-permute-start(bf16[72,1152]{1,0:T(8,128)(2,1)S(1)} %add_convert_fusion.7), channel_id=1, source_target_pairs={{0,8},{4,12},{8,0},{12,4},{16,24},{20,28},{24,16},{28,20},{1,9},{5... | collective-permute-start | bytes 497672 | tf_op jit(solution)/shard_map/ppermute | solution.py:331
  40.0 3.5 %shard_map.81 = (bf16[72,1152]{1,0:T(8,128)(2,1)S(1)}, bf16[72,1152]{1,0:T(8,128)(2,1)S(1)}, bf16[72,1152]{1,0:T(8,128)(2,1)S(1)}, bf16[72,1152]{1,0:T(8,128)(2,1)S(1)}, bf16[512,1152]{1,0:T(8,128)(2,1)S(1)}) custom-call(bf16[128,1152]{1,0:T(8,128)(2,1)S(1)} %collective-permute-done.11.x_first, bf16[128,1152]{1,0:T(8,128)(2,1)S(1)} %collective-permute-done.13.x_second, ...), custom_call_target="tpu_custom_call" | custom-call | tf_op jit(solution)/shard_map/pallas_call | solution.py:318
  43.6 1.1 %collective-permute-start.15 = (bf16[72,1152]{1,0:T(8,128)(2,1)S(1)}, bf16[72,1152]{1,0:T(8,128)(2,1)S(1)}, u32[]{:S(2)}, u32[]{:S(2)}) collective-permute-start(bf16[72,1152]{1,0:T(8,128)(2,1)S(1)} %add_convert_fusion.4), channel_id=1, source_target_pairs={{0,2},{1,3},{2,0},{3,1},{4,6},{5,7},{6,4},{7,5},{8,10},{9,11},{10,... | collective-permute-start | bytes 497672 | tf_op jit(solution)/shard_map/ppermute | solution.py:331
  44.7 1.5 %collective-permute-start.20 = (bf16[72,1152]{1,0:T(8,128)(2,1)S(1)}, bf16[72,1152]{1,0:T(8,128)(2,1)S(1)}, u32[]{:S(2)}, u32[]{:S(2)}) collective-permute-start(bf16[72,1152]{1,0:T(8,128)(2,1)S(1)} %get-tuple-element.121), channel_id=1, source_target_pairs={{0,4},{4,0},{8,12},{12,8},{16,20},{20,16},{24,28},{28,24},{1,5},{5... | collective-permute-start | bytes 497672 | tf_op jit(solution)/shard_map/ppermute | solution.py:331
  46.7 1.5 %collective-permute-start.22 = (bf16[72,1152]{1,0:T(8,128)(2,1)S(1)}, bf16[72,1152]{1,0:T(8,128)(2,1)S(1)}, u32[]{:S(2)}, u32[]{:S(2)}) collective-permute-start(bf16[72,1152]{1,0:T(8,128)(2,1)S(1)} %get-tuple-element.125), channel_id=1, source_target_pairs={{0,12},{4,8},{8,4},{12,0},{16,28},{20,24},{24,20},{28,16},{1,13},{... | collective-permute-start | bytes 497672 | tf_op jit(solution)/shard_map/ppermute | solution.py:331
  49.1 2.7 %collective-permute-start.16 = (bf16[72,1152]{1,0:T(8,128)(2,1)S(1)}, bf16[72,1152]{1,0:T(8,128)(2,1)S(1)}, u32[]{:S(2)}, u32[]{:S(2)}) collective-permute-start(bf16[72,1152]{1,0:T(8,128)(2,1)S(1)} %add_convert_fusion.3), channel_id=1, source_target_pairs={{0,16},{4,20},{8,24},{12,28},{16,0},{20,4},{24,8},{28,12},{1,17},{... | collective-permute-start | bytes 497672 | tf_op jit(solution)/shard_map/ppermute | solution.py:331
  51.8 2.4 %collective-permute-done.21 = bf16[72,1152]{1,0:T(8,128)(2,1)S(1)} collective-permute-done((bf16[72,1152]{1,0:T(8,128)(2,1)S(1)}, bf16[72,1152]{1,0:T(8,128)(2,1)S(1)}, u32[]{:S(2)}, u32[]{:S(2)}) %collective-permute-start.21) | collective-permute-done | bytes 165920 | tf_op jit(solution)/shard_map/ppermute | solution.py:331
  54.3 2.8 %collective-permute-done.22 = bf16[72,1152]{1,0:T(8,128)(2,1)S(1)} collective-permute-done((bf16[72,1152]{1,0:T(8,128)(2,1)S(1)}, bf16[72,1152]{1,0:T(8,128)(2,1)S(1)}, u32[]{:S(2)}, u32[]{:S(2)}) %collective-permute-start.22) | collective-permute-done | bytes 165920 | tf_op jit(solution)/shard_map/ppermute | solution.py:331
  57.2 2.3 %collective-permute-start.23 = (bf16[72,1152]{1,0:T(8,128)(2,1)S(1)}, bf16[72,1152]{1,0:T(8,128)(2,1)S(1)}, u32[]{:S(2)}, u32[]{:S(2)}) collective-permute-start(bf16[72,1152]{1,0:T(8,128)(2,1)S(1)} %add_convert_fusion.1), channel_id=1, source_target_pairs={{0,16},{4,20},{8,24},{12,28},{16,0},{20,4},{24,8},{28,12},{1,17},{... | collective-permute-start | bytes 497672 | tf_op jit(solution)/shard_map/ppermute | solution.py:331
  59.5 2.0 %shard_map.83 = f32[256,1152]{1,0:T(8,128)} custom-call(bf16[512,1152]{1,0:T(8,128)(2,1)S(1)} %get-tuple-element.118.back, bf16[1152,1152]{1,0:T(8,128)(2,1)S(1)} %get-tuple-element.73.refs_7_.refs_3_.head), custom_call_target="tpu_custom_call" | custom-call | flops 1358954496 | tf_op jit(solution)/shard_map/pallas_call | solution.py:318
  61.6 2.1 %shard_map.82 = f32[256,1152]{1,0:T(8,128)} custom-call(bf16[512,1152]{1,0:T(8,128)(2,1)S(1)} %get-tuple-element.117.back, bf16[1152,1152]{1,0:T(8,128)(2,1)S(1)} %get-tuple-element.89.image_head.head), custom_call_target="tpu_custom_call" | custom-call | flops 1358954496 | tf_op jit(solution)/shard_map/pallas_call | solution.py:318
  63.7 1.7 %collective-permute-start.18 = (bf16[72,1152]{1,0:T(8,128)(2,1)S(1)}, bf16[72,1152]{1,0:T(8,128)(2,1)S(1)}, u32[]{:S(2)}, u32[]{:S(2)}) collective-permute-start(bf16[72,1152]{1,0:T(8,128)(2,1)S(1)} %add_convert_fusion.2.refs_0_), channel_id=1, source_target_pairs={{0,4},{4,0},{8,12},{12,8},{16,20},{20,16},{24,28},{28,24},{1,5},{5... | collective-permute-start | bytes 497672 | tf_op jit(solution)/shard_map/ppermute | solution.py:331
  65.6 1.6 %collective-permute-start.17 = (bf16[72,1152]{1,0:T(8,128)(2,1)S(1)}, bf16[72,1152]{1,0:T(8,128)(2,1)S(1)}, u32[]{:S(2)}, u32[]{:S(2)}) collective-permute-start(bf16[72,1152]{1,0:T(8,128)(2,1)S(1)} %add_convert_fusion.2.refs_0_), channel_id=1, source_target_pairs={{0,12},{4,8},{8,4},{12,0},{16,28},{20,24},{24,20},{28,16},{1,13},{... | collective-permute-start | bytes 497672 | tf_op jit(solution)/shard_map/ppermute | solution.py:331
  67.2 4.2 %collective-permute-done.18.refs_1_ = bf16[72,1152]{1,0:T(8,128)(2,1)S(1)} collective-permute-done((bf16[72,1152]{1,0:T(8,128)(2,1)S(1)}, bf16[72,1152]{1,0:T(8,128)(2,1)S(1)}, u32[]{:S(2)}, u32[]{:S(2)}) %collective-permute-start.18) | collective-permute-done | bytes 165920 | tf_op jit(solution)/shard_map/ppermute | solution.py:331
  71.5 1.7 %collective-permute-start.25 = (bf16[72,1152]{1,0:T(8,128)(2,1)S(1)}, bf16[72,1152]{1,0:T(8,128)(2,1)S(1)}, u32[]{:S(2)}, u32[]{:S(2)}) collective-permute-start(bf16[72,1152]{1,0:T(8,128)(2,1)S(1)} %add_convert_fusion.refs_0_), channel_id=1, source_target_pairs={{0,4},{4,0},{8,12},{12,8},{16,20},{20,16},{24,28},{28,24},{1,5},{5... | collective-permute-start | bytes 497672 | tf_op jit(solution)/shard_map/ppermute | solution.py:331
  73.2 1.0 %collective-permute-start.26 = (bf16[72,1152]{1,0:T(8,128)(2,1)S(1)}, bf16[72,1152]{1,0:T(8,128)(2,1)S(1)}, u32[]{:S(2)}, u32[]{:S(2)}) collective-permute-start(bf16[72,1152]{1,0:T(8,128)(2,1)S(1)} %add_convert_fusion.refs_0_), channel_id=1, source_target_pairs={{0,8},{4,12},{8,0},{12,4},{16,24},{20,28},{24,16},{28,20},{1,9},{5... | collective-permute-start | bytes 497672 | tf_op jit(solution)/shard_map/ppermute | solution.py:331
  75.1 1.5 %shard_map.84.refs_1_ = f32[288,1152]{1,0:T(8,128)} custom-call(s32[2]{0:T(128)S(1)} %pad_add_fusion.place.place_ref, bf16[72,1152]{1,0:T(8,128)(2,1)S(1)} %add_convert_fusion.2.refs_0_, bf16[72,1152]{1,0:T(8,128)(2,1)S(1)} %collective-permute-done.18.refs_1_, bf16[72,1152]{1,0:T(8,128)(2,1)S(1)} %collective-permute-done.19.refs_2_), custom_call_target="tpu_custom_call" | custom-call | tf_op jit(solution)/shard_map/pallas_call | solution.py:296
  76.6 1.3 %shard_map.85 = f32[288,1152]{1,0:T(8,128)} custom-call(s32[2]{0:T(128)S(1)} %pad_add_fusion.place.place_ref, bf16[72,1152]{1,0:T(8,128)(2,1)S(1)} %collective-permute-done.17.refs_0_, f32[288,1152]{1,0:T(8,128)} %shard_map.84.refs_1_), custom_call_target="tpu_custom_call", output_to_operand_aliasing={{}: (2, {})} | custom-call | tf_op jit(solution)/shard_map/pallas_call | solution.py:296
  78.6 1.5 %shard_map.86.refs_1_ = f32[288,1152]{1,0:T(8,128)} custom-call(s32[2]{0:T(128)S(1)} %pad_add_fusion.place.place_ref, bf16[72,1152]{1,0:T(8,128)(2,1)S(1)} %add_convert_fusion.refs_0_, bf16[72,1152]{1,0:T(8,128)(2,1)S(1)} %collective-permute-done.25.refs_1_, bf16[72,1152]{1,0:T(8,128)(2,1)S(1)} %collective-permute-done.26.refs_2_), custom_call_target="tpu_custom_call" | custom-call | tf_op jit(solution)/shard_map/pallas_call | solution.py:296
  80.5 1.3 %shard_map.87 = f32[288,1152]{1,0:T(8,128)} custom-call(s32[2]{0:T(128)S(1)} %pad_add_fusion.place.place_ref, bf16[72,1152]{1,0:T(8,128)(2,1)S(1)} %collective-permute-done.24.refs_0_, f32[288,1152]{1,0:T(8,128)} %shard_map.86.refs_1_), custom_call_target="tpu_custom_call", output_to_operand_aliasing={{}: (2, {})} | custom-call | tf_op jit(solution)/shard_map/pallas_call | solution.py:296
  (48 shorter events, 9.7 us)
Async XLA Ops:
  0.7 4.7 %collective-permute-start.2 = (bf16[256,1152]{1,0:T(8,128)(2,1)}, bf16[256,1152]{1,0:T(8,128)(2,1)S(1)}, u32[]{:S(2)}, u32[]{:S(2)}) collective-permute-start(bf16[256,1152]{1,0:T(8,128)(2,1)} %t0_far), channel_id=1, source_target_pairs={{0,1},{1,0},{2,3},{3,2},{4,5},{5,4},{6,7},{7,6},{8,9},{9,8},{10,11... | collective-permute-start | bytes 1769480 | tf_op jit(solution)/shard_map/ppermute | solution.py:331
  1.2 4.3 %collective-permute-start.3 = (bf16[256,1152]{1,0:T(8,128)(2,1)}, bf16[256,1152]{1,0:T(8,128)(2,1)S(1)}, u32[]{:S(2)}, u32[]{:S(2)}) collective-permute-start(bf16[256,1152]{1,0:T(8,128)(2,1)} %i0_far), channel_id=1, source_target_pairs={{0,1},{1,0},{2,3},{3,2},{4,5},{5,4},{6,7},{7,6},{8,9},{9,8},{10,11... | collective-permute-start | bytes 1769480 | tf_op jit(solution)/shard_map/ppermute | solution.py:331
  2.3 10.8 %collective-permute-start.1 = (bf16[128,1152]{1,0:T(8,128)(2,1)S(1)}, bf16[128,1152]{1,0:T(8,128)(2,1)S(1)}, u32[]{:S(2)}, u32[]{:S(2)}) collective-permute-start(bf16[128,1152]{1,0:T(8,128)(2,1)S(1)} %get-tuple-element.128), channel_id=1, source_target_pairs={{0,2},{1,3},{2,0},{3,1},{4,6},{5,7},{6,4},{7,5},{8,10},{9,11},{10,... | collective-permute-start | bytes 884744 | tf_op jit(solution)/shard_map/ppermute | solution.py:331
  5.3 8.4 %copy-start = (bf16[256,1152]{1,0:T(8,128)(2,1)S(1)}, bf16[256,1152]{1,0:T(8,128)(2,1)}, u32[]{:S(2)}) copy-start(bf16[256,1152]{1,0:T(8,128)(2,1)} %i0_far) | copy-start | bytes 1769476
  5.3 15.4 %collective-permute-start = (bf16[128,1152]{1,0:T(8,128)(2,1)S(1)}, bf16[128,1152]{1,0:T(8,128)(2,1)S(1)}, u32[]{:S(2)}, u32[]{:S(2)}) collective-permute-start(bf16[128,1152]{1,0:T(8,128)(2,1)S(1)} %get-tuple-element.129), channel_id=1, source_target_pairs={{0,2},{1,3},{2,0},{3,1},{4,6},{5,7},{6,4},{7,5},{8,10},{9,11},{10,... | collective-permute-start | bytes 884744 | tf_op jit(solution)/shard_map/ppermute | solution.py:331
  13.2 2.6 %collective-permute-start.4 = (bf16[64,1152]{1,0:T(8,128)(2,1)S(1)}, bf16[64,1152]{1,0:T(8,128)(2,1)S(1)}, u32[]{:S(2)}, u32[]{:S(2)}) collective-permute-start(bf16[64,1152]{1,0:T(8,128)(2,1)S(1)} %get-tuple-element.133), channel_id=1, source_target_pairs={{0,1},{1,0},{2,3},{3,2},{4,5},{5,4},{6,7},{7,6},{8,9},{9,8},{10,11... | collective-permute-start | bytes 442376 | tf_op jit(solution)/shard_map/ppermute | solution.py:331
  13.2 2.6 %collective-permute-start.5 = (bf16[64,1152]{1,0:T(8,128)(2,1)S(1)}, bf16[64,1152]{1,0:T(8,128)(2,1)S(1)}, u32[]{:S(2)}, u32[]{:S(2)}) collective-permute-start(bf16[64,1152]{1,0:T(8,128)(2,1)S(1)} %get-tuple-element.132), channel_id=1, source_target_pairs={{0,1},{1,0},{2,3},{3,2},{4,5},{5,4},{6,7},{7,6},{8,9},{9,8},{10,11... | collective-permute-start | bytes 442376 | tf_op jit(solution)/shard_map/ppermute | solution.py:331
  13.7 17.8 %collective-permute-start.9 = (bf16[256,1152]{1,0:T(8,128)(2,1)S(1)}, bf16[256,1152]{1,0:T(8,128)(2,1)S(1)}, u32[]{:S(2)}, u32[]{:S(2)}) collective-permute-start(bf16[256,1152]{1,0:T(8,128)(2,1)S(1)} %copy-done), channel_id=1, source_target_pairs={{0,2},{1,3},{2,0},{3,1},{4,6},{5,7},{6,4},{7,5},{8,10},{9,11},{10,... | collective-permute-start | bytes 1769480 | tf_op jit(solution)/shard_map/ppermute | solution.py:331
  20.8 1.4 %collective-permute-start.6 = (bf16[64,1152]{1,0:T(8,128)(2,1)S(1)}, bf16[64,1152]{1,0:T(8,128)(2,1)S(1)}, u32[]{:S(2)}, u32[]{:S(2)}) collective-permute-start(bf16[64,1152]{1,0:T(8,128)(2,1)S(1)} %get-tuple-element.131), channel_id=1, source_target_pairs={{0,1},{1,0},{2,3},{3,2},{4,5},{5,4},{6,7},{7,6},{8,9},{9,8},{10,11... | collective-permute-start | bytes 442376 | tf_op jit(solution)/shard_map/ppermute | solution.py:331
  20.8 1.6 %collective-permute-start.7 = (bf16[64,1152]{1,0:T(8,128)(2,1)S(1)}, bf16[64,1152]{1,0:T(8,128)(2,1)S(1)}, u32[]{:S(2)}, u32[]{:S(2)}) collective-permute-start(bf16[64,1152]{1,0:T(8,128)(2,1)S(1)} %get-tuple-element.130), channel_id=1, source_target_pairs={{0,1},{1,0},{2,3},{3,2},{4,5},{5,4},{6,7},{7,6},{8,9},{9,8},{10,11... | collective-permute-start | bytes 442376 | tf_op jit(solution)/shard_map/ppermute | solution.py:331
  26.4 10.1 %collective-permute-start.8 = (bf16[144,1152]{1,0:T(8,128)(2,1)S(1)}, bf16[144,1152]{1,0:T(8,128)(2,1)S(1)}, u32[]{:S(2)}, u32[]{:S(2)}) collective-permute-start(bf16[144,1152]{1,0:T(8,128)(2,1)S(1)} %get-tuple-element.83), channel_id=1, source_target_pairs={{0,4},{4,0},{8,12},{12,8},{16,20},{20,16},{24,28},{28,24},{1,5},{5... | collective-permute-start | bytes 995336 | tf_op jit(solution)/shard_map/ppermute | solution.py:331
  27.9 9.7 %collective-permute-start.12 = (bf16[144,1152]{1,0:T(8,128)(2,1)S(1)}, bf16[144,1152]{1,0:T(8,128)(2,1)S(1)}, u32[]{:S(2)}, u32[]{:S(2)}) collective-permute-start(bf16[144,1152]{1,0:T(8,128)(2,1)S(1)} %get-tuple-element.102), channel_id=1, source_target_pairs={{0,8},{4,12},{8,0},{12,4},{16,24},{20,28},{24,16},{28,20},{1,9},{5... | collective-permute-start | bytes 995336 | tf_op jit(solution)/shard_map/ppermute | solution.py:331
  33.5 6.5 %collective-permute-start.13 = (bf16[128,1152]{1,0:T(8,128)(2,1)S(1)}, bf16[128,1152]{1,0:T(8,128)(2,1)S(1)}, u32[]{:S(2)}, u32[]{:S(2)}) collective-permute-start(bf16[128,1152]{1,0:T(8,128)(2,1)S(1)} %get-tuple-element.93.x_second), channel_id=1, source_target_pairs={{0,1},{1,0},{2,3},{3,2},{4,5},{5,4},{6,7},{7,6},{8,9},{9,8},{10,11... | collective-permute-start | bytes 884744 | tf_op jit(solution)/shard_map/ppermute | solution.py:331
  33.6 6.4 %collective-permute-start.11 = (bf16[128,1152]{1,0:T(8,128)(2,1)S(1)}, bf16[128,1152]{1,0:T(8,128)(2,1)S(1)}, u32[]{:S(2)}, u32[]{:S(2)}) collective-permute-start(bf16[128,1152]{1,0:T(8,128)(2,1)S(1)} %get-tuple-element.92.x_first), channel_id=1, source_target_pairs={{0,1},{1,0},{2,3},{3,2},{4,5},{5,4},{6,7},{7,6},{8,9},{9,8},{10,11... | collective-permute-start | bytes 884744 | tf_op jit(solution)/shard_map/ppermute | solution.py:331
  37.7 5.8 %collective-permute-start.14 = (bf16[72,1152]{1,0:T(8,128)(2,1)S(1)}, bf16[72,1152]{1,0:T(8,128)(2,1)S(1)}, u32[]{:S(2)}, u32[]{:S(2)}) collective-permute-start(bf16[72,1152]{1,0:T(8,128)(2,1)S(1)} %add_convert_fusion.6), channel_id=1, source_target_pairs={{0,4},{4,0},{8,12},{12,8},{16,20},{20,16},{24,28},{28,24},{1,5},{5... | collective-permute-start | bytes 497672 | tf_op jit(solution)/shard_map/ppermute | solution.py:331
  38.3 9.9 %collective-permute-start.10 = (bf16[72,1152]{1,0:T(8,128)(2,1)S(1)}, bf16[72,1152]{1,0:T(8,128)(2,1)S(1)}, u32[]{:S(2)}, u32[]{:S(2)}) collective-permute-start(bf16[72,1152]{1,0:T(8,128)(2,1)S(1)} %add_convert_fusion.7), channel_id=1, source_target_pairs={{0,8},{4,12},{8,0},{12,4},{16,24},{20,28},{24,16},{28,20},{1,9},{5... | collective-permute-start | bytes 497672 | tf_op jit(solution)/shard_map/ppermute | solution.py:331
  43.6 5.4 %collective-permute-start.15 = (bf16[72,1152]{1,0:T(8,128)(2,1)S(1)}, bf16[72,1152]{1,0:T(8,128)(2,1)S(1)}, u32[]{:S(2)}, u32[]{:S(2)}) collective-permute-start(bf16[72,1152]{1,0:T(8,128)(2,1)S(1)} %add_convert_fusion.4), channel_id=1, source_target_pairs={{0,2},{1,3},{2,0},{3,1},{4,6},{5,7},{6,4},{7,5},{8,10},{9,11},{10,... | collective-permute-start | bytes 497672 | tf_op jit(solution)/shard_map/ppermute | solution.py:331
  44.7 7.1 %collective-permute-start.20 = (bf16[72,1152]{1,0:T(8,128)(2,1)S(1)}, bf16[72,1152]{1,0:T(8,128)(2,1)S(1)}, u32[]{:S(2)}, u32[]{:S(2)}) collective-permute-start(bf16[72,1152]{1,0:T(8,128)(2,1)S(1)} %get-tuple-element.121), channel_id=1, source_target_pairs={{0,4},{4,0},{8,12},{12,8},{16,20},{20,16},{24,28},{28,24},{1,5},{5... | collective-permute-start | bytes 497672 | tf_op jit(solution)/shard_map/ppermute | solution.py:331
  46.2 8.0 %collective-permute-start.21 = (bf16[72,1152]{1,0:T(8,128)(2,1)S(1)}, bf16[72,1152]{1,0:T(8,128)(2,1)S(1)}, u32[]{:S(2)}, u32[]{:S(2)}) collective-permute-start(bf16[72,1152]{1,0:T(8,128)(2,1)S(1)} %get-tuple-element.123), channel_id=1, source_target_pairs={{0,8},{4,12},{8,0},{12,4},{16,24},{20,28},{24,16},{28,20},{1,9},{5... | collective-permute-start | bytes 497672 | tf_op jit(solution)/shard_map/ppermute | solution.py:331
  46.7 10.4 %collective-permute-start.22 = (bf16[72,1152]{1,0:T(8,128)(2,1)S(1)}, bf16[72,1152]{1,0:T(8,128)(2,1)S(1)}, u32[]{:S(2)}, u32[]{:S(2)}) collective-permute-start(bf16[72,1152]{1,0:T(8,128)(2,1)S(1)} %get-tuple-element.125), channel_id=1, source_target_pairs={{0,12},{4,8},{8,4},{12,0},{16,28},{20,24},{24,20},{28,16},{1,13},{... | collective-permute-start | bytes 497672 | tf_op jit(solution)/shard_map/ppermute | solution.py:331
  49.1 14.5 %collective-permute-start.16 = (bf16[72,1152]{1,0:T(8,128)(2,1)S(1)}, bf16[72,1152]{1,0:T(8,128)(2,1)S(1)}, u32[]{:S(2)}, u32[]{:S(2)}) collective-permute-start(bf16[72,1152]{1,0:T(8,128)(2,1)S(1)} %add_convert_fusion.3), channel_id=1, source_target_pairs={{0,16},{4,20},{8,24},{12,28},{16,0},{20,4},{24,8},{28,12},{1,17},{... | collective-permute-start | bytes 497672 | tf_op jit(solution)/shard_map/ppermute | solution.py:331
  57.2 10.1 %collective-permute-start.23 = (bf16[72,1152]{1,0:T(8,128)(2,1)S(1)}, bf16[72,1152]{1,0:T(8,128)(2,1)S(1)}, u32[]{:S(2)}, u32[]{:S(2)}) collective-permute-start(bf16[72,1152]{1,0:T(8,128)(2,1)S(1)} %add_convert_fusion.1), channel_id=1, source_target_pairs={{0,16},{4,20},{8,24},{12,28},{16,0},{20,4},{24,8},{28,12},{1,17},{... | collective-permute-start | bytes 497672 | tf_op jit(solution)/shard_map/ppermute | solution.py:331
  63.7 7.8 %collective-permute-start.18 = (bf16[72,1152]{1,0:T(8,128)(2,1)S(1)}, bf16[72,1152]{1,0:T(8,128)(2,1)S(1)}, u32[]{:S(2)}, u32[]{:S(2)}) collective-permute-start(bf16[72,1152]{1,0:T(8,128)(2,1)S(1)} %add_convert_fusion.2.refs_0_), channel_id=1, source_target_pairs={{0,4},{4,0},{8,12},{12,8},{16,20},{20,16},{24,28},{28,24},{1,5},{5... | collective-permute-start | bytes 497672 | tf_op jit(solution)/shard_map/ppermute | solution.py:331
  65.4 9.7 %collective-permute-start.19 = (bf16[72,1152]{1,0:T(8,128)(2,1)S(1)}, bf16[72,1152]{1,0:T(8,128)(2,1)S(1)}, u32[]{:S(2)}, u32[]{:S(2)}) collective-permute-start(bf16[72,1152]{1,0:T(8,128)(2,1)S(1)} %add_convert_fusion.2.refs_0_), channel_id=1, source_target_pairs={{0,8},{4,12},{8,0},{12,4},{16,24},{20,28},{24,16},{28,20},{1,9},{5... | collective-permute-start | bytes 497672 | tf_op jit(solution)/shard_map/ppermute | solution.py:331
  65.6 11.0 %collective-permute-start.17 = (bf16[72,1152]{1,0:T(8,128)(2,1)S(1)}, bf16[72,1152]{1,0:T(8,128)(2,1)S(1)}, u32[]{:S(2)}, u32[]{:S(2)}) collective-permute-start(bf16[72,1152]{1,0:T(8,128)(2,1)S(1)} %add_convert_fusion.2.refs_0_), channel_id=1, source_target_pairs={{0,12},{4,8},{8,4},{12,0},{16,28},{20,24},{24,20},{28,16},{1,13},{... | collective-permute-start | bytes 497672 | tf_op jit(solution)/shard_map/ppermute | solution.py:331
  71.5 6.4 %collective-permute-start.25 = (bf16[72,1152]{1,0:T(8,128)(2,1)S(1)}, bf16[72,1152]{1,0:T(8,128)(2,1)S(1)}, u32[]{:S(2)}, u32[]{:S(2)}) collective-permute-start(bf16[72,1152]{1,0:T(8,128)(2,1)S(1)} %add_convert_fusion.refs_0_), channel_id=1, source_target_pairs={{0,4},{4,0},{8,12},{12,8},{16,20},{20,16},{24,28},{28,24},{1,5},{5... | collective-permute-start | bytes 497672 | tf_op jit(solution)/shard_map/ppermute | solution.py:331
  73.2 5.3 %collective-permute-start.26 = (bf16[72,1152]{1,0:T(8,128)(2,1)S(1)}, bf16[72,1152]{1,0:T(8,128)(2,1)S(1)}, u32[]{:S(2)}, u32[]{:S(2)}) collective-permute-start(bf16[72,1152]{1,0:T(8,128)(2,1)S(1)} %add_convert_fusion.refs_0_), channel_id=1, source_target_pairs={{0,8},{4,12},{8,0},{12,4},{16,24},{20,28},{24,16},{28,20},{1,9},{5... | collective-permute-start | bytes 497672 | tf_op jit(solution)/shard_map/ppermute | solution.py:331
  74.2 6.2 %collective-permute-start.24 = (bf16[72,1152]{1,0:T(8,128)(2,1)S(1)}, bf16[72,1152]{1,0:T(8,128)(2,1)S(1)}, u32[]{:S(2)}, u32[]{:S(2)}) collective-permute-start(bf16[72,1152]{1,0:T(8,128)(2,1)S(1)} %add_convert_fusion.refs_0_), channel_id=1, source_target_pairs={{0,12},{4,8},{8,4},{12,0},{16,28},{20,24},{24,20},{28,16},{1,13},{... | collective-permute-start | bytes 497672 | tf_op jit(solution)/shard_map/ppermute | solution.py:331

commit v11 on v10

--- a/solution.py
+++ b/solution.py
@@ -141,7 +141,7 @@
 
 def near_kernel(
     t1, i1, t0_far, i0_far, text_head_far, image_head_far,
-    q_a, y_a, p_a, x_a, w_aa, t0, i0, text_head, image_head, dots, sems,
+    q_a, y_a, p_a, x_a, w_aa, gx, t0, i0, text_head, image_head, dots, sems,
 ):
     half = t0.shape[0]
     copies = [
@@ -164,6 +164,7 @@
     unit_rows(p_a, x_a)
     dots[...] = dot_nt(x_a[...], y_a[...])
     weight_rows(dots, w_aa, 0)
+    gx[...] = dot_nn(w_aa[...], y_a[...])
 
 
 def rows_of(refs):
@@ -171,22 +172,17 @@
 
 
 def text_kernel(place, *refs):
-    *features, t0, t1, i0, i1, text_head, y_a, x_a, w_aa = refs[:-9]
-    q_2, y_2, w_a2, gx, gy_a, pick_i, pick_t, dots, near_gx = refs[-9:]
-    half = t0.shape[0]
-    rows = pick_t.shape[0]
+    *features, i0, i1, text_head, gx_in, x_a, w_aa = refs[:-7]
+    q_2, y_2, w_a2, gx, gy_a, pick_i, dots = refs[-7:]
+    half, width = i0.shape
     q_2[...] = dot_nn(rows_of(features), text_head[...])
-    near_gx[...] = dot_nn(w_aa[...], y_a[...])
+    pick = picker(place, pick_i.shape[0] // 2, width, (0, 2))
     unit_rows(q_2, y_2)
     dots[...] = dot_nt(x_a[...], y_2[...])
-    pick = picker(place, rows, t0.shape[1], (0, 2))
     pick_i[:, :half] = dot_nt(pick, i0[...]).astype(BF16)
     pick_i[:, half:] = dot_nt(pick, i1[...]).astype(BF16)
     weight_rows(dots, w_a2)
-    gx[...] = near_gx[...] + dot_nn(w_a2[...], y_2[...])
-    pick = picker(place, rows, t0.shape[1], (0,))
-    pick_t[:, :half] = dot_nt(pick, t0[...]).astype(BF16)
-    pick_t[:, half:] = dot_nt(pick, t1[...]).astype(BF16)
+    gx[...] = gx_in[...] + dot_nn(w_a2[...], y_2[...])
     gy_a[...] = dot_tn(w_aa[...], x_a[...])
 
 
@@ -216,11 +212,14 @@
 
 
 def text_pull_kernel(place, *refs):
-    *features, x_a, w_a2, w_a3, gy_2, gy_3, pick_t = refs
+    *features, t0, t1, x_a, w_a2, w_a3, gy_2, gy_3, pick_a, pick_b = refs
+    half = t0.shape[0]
     gy_2[...] = dot_tn(w_a2[...], x_a[...])
     gy_3[...] = dot_tn(w_a3[...], x_a[...])
-    pick = picker(place, pick_t.shape[0], x_a.shape[1], (0,))
-    pick_t[...] = dot_nt(pick, rows_of(features)).astype(BF16)
+    pick = picker(place, pick_a.shape[0], t0.shape[1], (0,))
+    pick_a[:, :half] = dot_nt(pick, t0[...]).astype(BF16)
+    pick_a[:, half:] = dot_nt(pick, t1[...]).astype(BF16)
+    pick_b[...] = dot_nt(pick, rows_of(features)).astype(BF16)
 
 
 def far_weights(core, x, y_a, y_2, y_3, w_a, w_2, w_3, d_a, d_2, d_3):
@@ -273,38 +272,36 @@
     out[...] = dot_nt(back[: out.shape[0], :], head[...])
 
 
-def place_kernel(place, ks, *refs):
-    out, buffer, sems = refs[-3:]
-    part = refs[0].shape[0]
+def place_kernel(place, *refs):
+    *pieces, out, buffer, sems = refs
+    part = pieces[0].shape[0]
     copies = []
-    for n, k in enumerate(ks):
-        buffer[n] = refs[n][...].astype(F32)
+    for k, piece in enumerate(pieces):
+        buffer[k] = piece[...].astype(F32)
         first = pl.multiple_of((place[1] ^ k) * part, part)
-        copies.append(pltpu.make_async_copy(buffer.at[n], out.at[pl.ds(first, part), :], sems.at[n]))
+        copies.append(pltpu.make_async_copy(buffer.at[k], out.at[pl.ds(first, part), :], sems.at[k]))
         copies[-1].start()
     for copy in copies:
         copy.wait()
 
 
-def place_pieces(place, pieces, ks, out=None):
+def placed(place, last_row, pieces):
     rows, width = pieces[0].shape
-    args = [pltpu.with_memory_space_constraint(a, pltpu.VMEM) for a in pieces]
-    specs = [pl.BlockSpec(memory_space=pltpu.SMEM)]
-    specs += [pl.BlockSpec(memory_space=pltpu.VMEM)] * len(pieces)
-    if out is not None:
-        args, specs = args + [out], specs + [pl.BlockSpec(memory_space=pltpu.HBM)]
-    return pl.pallas_call(
-        lambda place_ref, *refs: place_kernel(place_ref, ks, *refs),
+    *early, last = pieces
+    out = pl.pallas_call(
+        place_kernel,
         out_shape=pltpu.HBM((QUAD * rows, width), F32),
-        in_specs=specs,
+        in_specs=[pl.BlockSpec(memory_space=pltpu.SMEM)]
+        + [pl.BlockSpec(memory_space=pltpu.VMEM)] * len(early),
         out_specs=pl.BlockSpec(memory_space=pltpu.HBM),
         scratch_shapes=[
-            pltpu.VMEM((len(ks), rows, width), F32), pltpu.SemaphoreType.DMA((len(ks),))
+            pltpu.VMEM((len(early), rows, width), F32), pltpu.SemaphoreType.DMA((len(early),))
         ],
-        input_output_aliases={} if out is None else {len(pieces) + 1: 0},
         compiler_params=pltpu.CompilerParams(vmem_limit_bytes=4 * 1024 * 1024),
         cost_estimate=pl.CostEstimate(flops=0, bytes_accessed=0, transcendentals=0),
-    )(place, *args)
+    )(place, *(pltpu.with_memory_space_constraint(a, pltpu.VMEM) for a in early))
+    last = after(last, out)
+    return lax.dynamic_update_slice(out, last.astype(F32), (last_row, 0), allow_negative_indices=False)
 
 
 def call(kernel, outs, scratch, args, mib, place=None, macs=0, keep=True, far=()):
@@ -354,15 +351,14 @@
     def spread(total):
         return [total] + [cuts(total, mask=k) for k in range(1, QUAD)]
 
-    def placed(pieces):
-        out = place_pieces(place, pieces[:-1], tuple(range(QUAD - 1)))
-        return place_pieces(place, pieces[-1:], (QUAD - 1,), out)
-
     t2 = [loop(rows, mask=2) for rows in jnp.split(text_features, 2)]
     i2 = loop(image_features, mask=2)
     place = jnp.stack([lax.axis_index("loop"), lax.axis_index("cuts") & (QUAD - 1)])
+    last_row = ((place[1] ^ (QUAD - 1)) * part).astype(jnp.int32)
     place = place.astype(jnp.int32)
-    t0, i0, place = lax.optimization_barrier((text_features, image_features, place))
+    t0, i0, place, last_row = lax.optimization_barrier(
+        (text_features, image_features, place, last_row)
+    )
     t1 = loop(t0, mask=1)
     i1 = loop(i0, mask=1)
     wide, wide_b = ((near, width), F32), ((near, width), BF16)
@@ -371,20 +367,20 @@
     block_w, block_dots = ((half, near), BF16), ((half, near), F32)
     side_w, side_dots = ((near, half), BF16), ((near, half), F32)
     pick_one, pick_two = ((rows_out, near), BF16), ((2 * rows_out, near), BF16)
-    q_a, y_a, p_a, x_a, w_aa, t0, i0, text_head, image_head = call(
+    q_a, y_a, p_a, x_a, w_aa, gx, t0, i0, text_head, image_head = call(
         near_kernel,
-        [wide, wide_b, wide, wide_b, ((near, near), BF16), tall_b, tall_b, head_b, head_b],
+        [wide, wide_b, wide, wide_b, ((near, near), BF16), wide, tall_b, tall_b, head_b, head_b],
         [((near, near), F32)],
         (t1, i1),
         8,
         far=(t0, i0, text_head, image_head),
     )
     first = both(t2[0], w_aa, 2)
-    q_2, y_2, w_a2, gx, gy_a, pick_i, pick_a = call(
+    q_2, y_2, w_a2, gx, gy_a, pick_i = call(
         text_kernel,
-        [tall, tall_b, side_w, wide, wide, pick_two, pick_one],
-        [side_dots, wide],
-        (*first, t0, t1, i0, i1, text_head, y_a, x_a, w_aa),
+        [tall, tall_b, side_w, wide, wide, pick_two],
+        [side_dots],
+        (*first, i0, i1, text_head, gx, x_a, w_aa),
         8,
         place,
     )
@@ -398,11 +394,11 @@
         8,
     )
     near_came, far_came = cuts(near_sent, mask=1), cuts(far_sent, mask=2)
-    gy_2, gy_3, pick_b = call(
+    gy_2, gy_3, pick_a, pick_b = call(
         text_pull_kernel,
-        [tall, tall, pick_one],
+        [tall, tall, pick_one, pick_one],
         [],
-        (*first, *second, after(x_a, dp_a), w_a2, w_a3),
+        (*first, *second, t0, t1, after(x_a, dp_a), w_a2, w_a3),
         8,
         place,
     )
@@ -442,12 +438,12 @@
         call(grad_kernel, [tall], [], (after(back, image_sum), head), 4, macs=2 * macs, keep=False)[0]
         for back, head in ((dp_a, image_head), (dq_a, text_head))
     ]
-    text_sum = add(text_parts[0], [after(other, image_sum) for other in text_others])
-    image_sum = add(image_sum, [after(cuts(image_sum, mask=QUAD), grads)])
+    text_sum = add(text_parts[0], [after(other, (image_sum, grads)) for other in text_others])
+    image_sum = add(image_sum, [cuts(image_sum, mask=QUAD)])
     image_pieces = spread(image_sum)
     text_sum = add(text_sum, [after(cuts(text_sum, mask=QUAD), image_pieces[1])])
-    image_out = placed(image_pieces)
-    text_out = placed(spread(text_sum))
+    image_out = placed(place, last_row, image_pieces)
+    text_out = placed(place, last_row, spread(text_sum))
     return (*grads, image_out, text_out)
 
 

time: 82.1 us -> 78.8 us (0.960)
  waiting for transfers between devices: 16.1 us -> 10.5 us
  local copies, waits for them, and re-layouts: 1.15 us -> 4.67 us
  Pallas kernels: 33.7 us -> 31.4 us
  starting transfers between devices: 29.5 us -> 30.7 us
    ppermute x27, waiting for transfers between devices: 16.1 us -> 10.5 us  [swap(): return lax.ppermute(array, axis, [(i, i ^ mask) for i in range(size)])]
    dynamic_update_slice x0 -> x2, local copies, waits for them, and re-layouts: none -> 3.52 us  [placed(): lax.dynamic_update_slice(out, last.astype(F32), (last_row, 0), allow_nega...]
    pallas_call x4 -> x2, Pallas kernels: 5.66 us -> 3.07 us  [placed(): pl.pallas_call(place_kernel, out_shape=pltpu.HBM((QUAD * rows, width), F3...]
    ppermute x27, starting transfers between devices: 29.5 us -> 30.7 us  [swap(): return lax.ppermute(array, axis, [(i, i ^ mask) for i in range(size)])]
  transfers between devices with their start and end apart: 27 -> 27, of which waited for: 13 -> 12; matrix products, arithmetic and copies ran while one was open for 2% -> 4% of each run, Pallas kernels for 40% -> 40%
where the time goes in v11:
time: 78.8 us; the launch traced here: 78.6 us
  Pallas kernels  31.4 us (40%)
  starting transfers between devices  30.7 us (39%)
  waiting for transfers between devices  10.5 us (13%)
  local copies, waits for them, and re-layouts  4.67 us (6%)
  between operations  0.82 us (1%)
    ppermute x27, starting transfers between devices, swap(): return lax.ppermute(array, axis, [(i, i ^ mask) for i in range(size)])  30.7 us
    pallas_call x9, Pallas kernels, call(): pl.pallas_call(kernel, out_shape=[shape(s, t) for s, t in outs], in_specs...  28.3 us
    ppermute x27, waiting for transfers between devices, swap(): return lax.ppermute(array, axis, [(i, i ^ mask) for i in range(size)])  10.5 us
    dynamic_update_slice x2, local copies, waits for them, and re-layouts, placed(): lax.dynamic_update_slice(out, last.astype(F32), (last_row, 0), allow_nega...  3.52 us
    pallas_call x2, Pallas kernels, placed(): pl.pallas_call(place_kernel, out_shape=pltpu.HBM((QUAD * rows, width), F3...  3.07 us
  transfers between devices with their start and end apart: 27, of which 12 were waited for; matrix products, arithmetic and copies ran while one was open for 4% of the time, Pallas kernels for 40%

profile of v11, /device:TPU:0, one launch (start us, length us, event | category | flops | bytes accessed | tf_op | source)
XLA Modules:
  0.0 78.6 jit_solution(1708445238806171293)
XLA Ops:
  1.3 1.1 %fusion = (bf16[128,1152]{1,0:T(8,128)(2,1)S(1)}, bf16[128,1152]{1,0:T(8,128)(2,1)S(1)}) fusion(bf16[256,1152]{1,0:T(8,128)(2,1)} %t0_far), kind=kLoop, calls=%fused_computation.9 | loop fusion | bytes 1179648 | tf_op jit(solution)/shard_map/split | solution.py:354
  2.4 3.0 %collective-permute-start.1 = (bf16[128,1152]{1,0:T(8,128)(2,1)S(1)}, bf16[128,1152]{1,0:T(8,128)(2,1)S(1)}, u32[]{:S(2)}, u32[]{:S(2)}) collective-permute-start(bf16[128,1152]{1,0:T(8,128)(2,1)S(1)} %get-tuple-element.134), channel_id=1, source_target_pairs={{0,2},{1,3},{2,0},{3,1},{4,6},{5,7},{6,4},{7,5},{8,10},{9,11},{10,... | collective-permute-start | bytes 884744 | tf_op jit(solution)/shard_map/ppermute | solution.py:328
  5.4 7.5 %shard_map.75 = (f32[512,1152]{1,0:T(8,128)S(1)}, bf16[512,1152]{1,0:T(8,128)(2,1)S(1)}, f32[512,1152]{1,0:T(8,128)S(1)}, bf16[512,1152]{1,0:T(8,128)(2,1)S(1)},...) custom-call(bf16[256,1152]{1,0:T(8,128)(2,1)S(1)} %collective-permut, ...), custom_call_target="tpu_custom_call" | custom-call | tf_op jit(solution)/shard_map/pallas_call | solution.py:315
  13.8 2.1 %collective-permute-start.9 = (bf16[256,1152]{1,0:T(8,128)(2,1)S(1)}, bf16[256,1152]{1,0:T(8,128)(2,1)S(1)}, u32[]{:S(2)}, u32[]{:S(2)}) collective-permute-start(bf16[256,1152]{1,0:T(8,128)(2,1)S(1)} %copy-done), channel_id=1, source_target_pairs={{0,2},{1,3},{2,0},{3,1},{4,6},{5,7},{6,4},{7,5},{8,10},{9,11},{10,... | collective-permute-start | bytes 1769480 | tf_op jit(solution)/shard_map/ppermute | solution.py:328
  15.8 4.1 %shard_map.76 = (f32[256,1152]{1,0:T(8,128)S(1)}, bf16[256,1152]{1,0:T(8,128)(2,1)S(1)}, bf16[512,256]{1,0:T(8,128)(2,1)S(1)}, f32[512,1152]{1,0:T(8,128)S(1)}, ...) custom-call(s32[2]{0:T(128)S(1)} %pad_add_fusion.place, bf16[128,1152]{1,0:T(8,128)(2,1)S(1)} %collective-permute-done.1.refs_0_, ...), custom_call_target="tpu_custom_call" | custom-call | tf_op jit(solution)/shard_map/pallas_call | solution.py:315
  21.6 3.9 %shard_map.77 = (f32[256,1152]{1,0:T(8,128)S(1)}, bf16[256,1152]{1,0:T(8,128)(2,1)S(1)}, bf16[512,256]{1,0:T(8,128)(2,1)S(1)}, bf16[512,1152]{1,0:T(8,128)(2,1)S...) custom-call(bf16[128,1152]{1,0:T(8,128)(2,1)S(1)} %collective-permut, ...), custom_call_target="tpu_custom_call" | custom-call | tf_op jit(solution)/shard_map/pallas_call | solution.py:315
  25.5 1.7 %collective-permute-start.8 = (bf16[144,1152]{1,0:T(8,128)(2,1)S(1)}, bf16[144,1152]{1,0:T(8,128)(2,1)S(1)}, u32[]{:S(2)}, u32[]{:S(2)}) collective-permute-start(bf16[144,1152]{1,0:T(8,128)(2,1)S(1)} %get-tuple-element.85), channel_id=1, source_target_pairs={{0,4},{4,0},{8,12},{12,8},{16,20},{20,16},{24,28},{28,24},{1,5},{5... | collective-permute-start | bytes 995336 | tf_op jit(solution)/shard_map/ppermute | solution.py:328
  27.2 1.6 %collective-permute-start.12 = (bf16[144,1152]{1,0:T(8,128)(2,1)S(1)}, bf16[144,1152]{1,0:T(8,128)(2,1)S(1)}, u32[]{:S(2)}, u32[]{:S(2)}) collective-permute-start(bf16[144,1152]{1,0:T(8,128)(2,1)S(1)} %get-tuple-element.106), channel_id=1, source_target_pairs={{0,8},{4,12},{8,0},{12,4},{16,24},{20,28},{24,16},{28,20},{1,9},{5... | collective-permute-start | bytes 995336 | tf_op jit(solution)/shard_map/ppermute | solution.py:328
  28.8 2.4 %shard_map.78 = (f32[256,1152]{1,0:T(8,128)S(1)}, f32[256,1152]{1,0:T(8,128)S(1)}, bf16[288,512]{1,0:T(8,128)(2,1)S(1)}, bf16[288,512]{1,0:T(8,128)(2,1)S(1)}) custom-call(s32[2]{0:T(128)S(1)} %pad_add_fusion.place, bf16[128,1152]{1,0:T(8,128)(2,1)S(1)} %collective-permute-done.1.refs_0_, bf16[64,1152]{1,0:T(8,128)(2,1)S(1)} %collective-permute-done.4.refs_1_, ...), custom_call_target="tpu_custom_call" | custom-call | tf_op jit(solution)/shard_map/pallas_call | solution.py:315
  31.6 1.9 %shard_map.79 = (bf16[128,1152]{1,0:T(8,128)(2,1)S(1)}, bf16[128,1152]{1,0:T(8,128)(2,1)S(1)}, bf16[256,512]{1,0:T(8,128)(2,1)S(1)}, bf16[256,256]{1,0:T(8,128)(2,1)S(1)}, bf16[256,256]{1,0:T(8,128)(2,1)S(1)}) custom-call(bf16[256,1152]{1,0:T(8,128)(2,1)S(1)} %collective-permute-done.9.i2, bf16[1152,1152]{1,0:T(8,128)(2,1)S(1)} %get-tuple-element.92.image_head.head, ...), custom_call_target="tpu_custom_call" | custom-call | tf_op jit(solution)/shard_map/pallas_call | solution.py:315
  35.6 1.3 %collective-permute-done.12 = bf16[144,1152]{1,0:T(8,128)(2,1)S(1)} collective-permute-done((bf16[144,1152]{1,0:T(8,128)(2,1)S(1)}, bf16[144,1152]{1,0:T(8,128)(2,1)S(1)}, u32[]{:S(2)}, u32[]{:S(2)}) %collective-permute-start.12) | collective-permute-done | bytes 331808 | tf_op jit(solution)/shard_map/ppermute | solution.py:328
  37.5 1.7 %collective-permute-start.10 = (bf16[72,1152]{1,0:T(8,128)(2,1)S(1)}, bf16[72,1152]{1,0:T(8,128)(2,1)S(1)}, u32[]{:S(2)}, u32[]{:S(2)}) collective-permute-start(bf16[72,1152]{1,0:T(8,128)(2,1)S(1)} %add_convert_fusion.7), channel_id=1, source_target_pairs={{0,8},{4,12},{8,0},{12,4},{16,24},{20,28},{24,16},{28,20},{1,9},{5... | collective-permute-start | bytes 497672 | tf_op jit(solution)/shard_map/ppermute | solution.py:328
  39.2 3.5 %shard_map.81 = (bf16[72,1152]{1,0:T(8,128)(2,1)S(1)}, bf16[72,1152]{1,0:T(8,128)(2,1)S(1)}, bf16[72,1152]{1,0:T(8,128)(2,1)S(1)}, bf16[72,1152]{1,0:T(8,128)(2,1)S(1)}, bf16[512,1152]{1,0:T(8,128)(2,1)S(1)}) custom-call(bf16[128,1152]{1,0:T(8,128)(2,1)S(1)} %collective-permute-done.11.x_first, bf16[128,1152]{1,0:T(8,128)(2,1)S(1)} %collective-permute-done.13.x_second, ...), custom_call_target="tpu_custom_call" | custom-call | tf_op jit(solution)/shard_map/pallas_call | solution.py:315
  42.9 1.6 %collective-permute-start.15 = (bf16[72,1152]{1,0:T(8,128)(2,1)S(1)}, bf16[72,1152]{1,0:T(8,128)(2,1)S(1)}, u32[]{:S(2)}, u32[]{:S(2)}) collective-permute-start(bf16[72,1152]{1,0:T(8,128)(2,1)S(1)} %add_convert_fusion.4), channel_id=1, source_target_pairs={{0,2},{1,3},{2,0},{3,1},{4,6},{5,7},{6,4},{7,5},{8,10},{9,11},{10,... | collective-permute-start | bytes 497672 | tf_op jit(solution)/shard_map/ppermute | solution.py:328
  44.4 1.5 %collective-permute-start.20 = (bf16[72,1152]{1,0:T(8,128)(2,1)S(1)}, bf16[72,1152]{1,0:T(8,128)(2,1)S(1)}, u32[]{:S(2)}, u32[]{:S(2)}) collective-permute-start(bf16[72,1152]{1,0:T(8,128)(2,1)S(1)} %get-tuple-element.126), channel_id=1, source_target_pairs={{0,4},{4,0},{8,12},{12,8},{16,20},{20,16},{24,28},{28,24},{1,5},{5... | collective-permute-start | bytes 497672 | tf_op jit(solution)/shard_map/ppermute | solution.py:328
  46.4 1.5 %collective-permute-start.22 = (bf16[72,1152]{1,0:T(8,128)(2,1)S(1)}, bf16[72,1152]{1,0:T(8,128)(2,1)S(1)}, u32[]{:S(2)}, u32[]{:S(2)}) collective-permute-start(bf16[72,1152]{1,0:T(8,128)(2,1)S(1)} %get-tuple-element.130), channel_id=1, source_target_pairs={{0,12},{4,8},{8,4},{12,0},{16,28},{20,24},{24,20},{28,16},{1,13},{... | collective-permute-start | bytes 497672 | tf_op jit(solution)/shard_map/ppermute | solution.py:328
  48.3 2.7 %collective-permute-start.16 = (bf16[72,1152]{1,0:T(8,128)(2,1)S(1)}, bf16[72,1152]{1,0:T(8,128)(2,1)S(1)}, u32[]{:S(2)}, u32[]{:S(2)}) collective-permute-start(bf16[72,1152]{1,0:T(8,128)(2,1)S(1)} %add_convert_fusion.3), channel_id=1, source_target_pairs={{0,16},{4,20},{8,24},{12,28},{16,0},{20,4},{24,8},{28,12},{1,17},{... | collective-permute-start | bytes 497672 | tf_op jit(solution)/shard_map/ppermute | solution.py:328
  51.0 2.0 %shard_map.83 = f32[256,1152]{1,0:T(8,128)} custom-call(bf16[512,1152]{1,0:T(8,128)(2,1)S(1)} %get-tuple-element.122.back, bf16[1152,1152]{1,0:T(8,128)(2,1)S(1)} %get-tuple-element.75.refs_5_.refs_3_.head), custom_call_target="tpu_custom_call" | custom-call | flops 1358954496 | tf_op jit(solution)/shard_map/pallas_call | solution.py:315
  53.0 2.0 %shard_map.82 = f32[256,1152]{1,0:T(8,128)} custom-call(bf16[512,1152]{1,0:T(8,128)(2,1)S(1)} %get-tuple-element.121.back, bf16[1152,1152]{1,0:T(8,128)(2,1)S(1)} %get-tuple-element.92.image_head.head), custom_call_target="tpu_custom_call" | custom-call | flops 1358954496 | tf_op jit(solution)/shard_map/pallas_call | solution.py:315
  55.1 2.6 %collective-permute-done.22 = bf16[72,1152]{1,0:T(8,128)(2,1)S(1)} collective-permute-done((bf16[72,1152]{1,0:T(8,128)(2,1)S(1)}, bf16[72,1152]{1,0:T(8,128)(2,1)S(1)}, u32[]{:S(2)}, u32[]{:S(2)}) %collective-permute-start.22) | collective-permute-done | bytes 165920 | tf_op jit(solution)/shard_map/ppermute | solution.py:328
  57.7 1.5 %collective-permute-start.23 = (bf16[72,1152]{1,0:T(8,128)(2,1)S(1)}, bf16[72,1152]{1,0:T(8,128)(2,1)S(1)}, u32[]{:S(2)}, u32[]{:S(2)}) collective-permute-start(bf16[72,1152]{1,0:T(8,128)(2,1)S(1)} %add_convert_fusion.1), channel_id=1, source_target_pairs={{0,16},{4,20},{8,24},{12,28},{16,0},{20,4},{24,8},{28,12},{1,17},{... | collective-permute-start | bytes 497672 | tf_op jit(solution)/shard_map/ppermute | solution.py:328
  59.3 1.7 %collective-permute-start.17 = (bf16[72,1152]{1,0:T(8,128)(2,1)S(1)}, bf16[72,1152]{1,0:T(8,128)(2,1)S(1)}, u32[]{:S(2)}, u32[]{:S(2)}) collective-permute-start(bf16[72,1152]{1,0:T(8,128)(2,1)S(1)} %add_convert_fusion.2.refs_0_), channel_id=1, source_target_pairs={{0,4},{4,0},{8,12},{12,8},{16,20},{20,16},{24,28},{28,24},{1,5},{5... | collective-permute-start | bytes 497672 | tf_op jit(solution)/shard_map/ppermute | solution.py:328
  61.0 2.4 %collective-permute-start.18 = (bf16[72,1152]{1,0:T(8,128)(2,1)S(1)}, bf16[72,1152]{1,0:T(8,128)(2,1)S(1)}, u32[]{:S(2)}, u32[]{:S(2)}) collective-permute-start(bf16[72,1152]{1,0:T(8,128)(2,1)S(1)} %add_convert_fusion.2.refs_0_), channel_id=1, source_target_pairs={{0,8},{4,12},{8,0},{12,4},{16,24},{20,28},{24,16},{28,20},{1,9},{5... | collective-permute-start | bytes 497672 | tf_op jit(solution)/shard_map/ppermute | solution.py:328
  63.4 1.0 %collective-permute-start.19 = (bf16[72,1152]{1,0:T(8,128)(2,1)S(1)}, bf16[72,1152]{1,0:T(8,128)(2,1)S(1)}, u32[]{:S(2)}, u32[]{:S(2)}) collective-permute-start(bf16[72,1152]{1,0:T(8,128)(2,1)S(1)} %add_convert_fusion.2.refs_0_), channel_id=1, source_target_pairs={{0,12},{4,8},{8,4},{12,0},{16,28},{20,24},{24,20},{28,16},{1,13},{... | collective-permute-start | bytes 497672 | tf_op jit(solution)/shard_map/ppermute | solution.py:328
  64.4 1.4 %collective-permute-done.23 = bf16[72,1152]{1,0:T(8,128)(2,1)S(1)} collective-permute-done((bf16[72,1152]{1,0:T(8,128)(2,1)S(1)}, bf16[72,1152]{1,0:T(8,128)(2,1)S(1)}, u32[]{:S(2)}, u32[]{:S(2)}) %collective-permute-start.23) | collective-permute-done | bytes 165920 | tf_op jit(solution)/shard_map/ppermute | solution.py:328
  67.3 1.7 %collective-permute-start.25 = (bf16[72,1152]{1,0:T(8,128)(2,1)S(1)}, bf16[72,1152]{1,0:T(8,128)(2,1)S(1)}, u32[]{:S(2)}, u32[]{:S(2)}) collective-permute-start(bf16[72,1152]{1,0:T(8,128)(2,1)S(1)} %add_convert_fusion.refs_0_), channel_id=1, source_target_pairs={{0,8},{4,12},{8,0},{12,4},{16,24},{20,28},{24,16},{28,20},{1,9},{5... | collective-permute-start | bytes 497672 | tf_op jit(solution)/shard_map/ppermute | solution.py:328
  69.1 1.1 %collective-permute-start.26 = (bf16[72,1152]{1,0:T(8,128)(2,1)S(1)}, bf16[72,1152]{1,0:T(8,128)(2,1)S(1)}, u32[]{:S(2)}, u32[]{:S(2)}) collective-permute-start(bf16[72,1152]{1,0:T(8,128)(2,1)S(1)} %add_convert_fusion.refs_0_), channel_id=1, source_target_pairs={{0,12},{4,8},{8,4},{12,0},{16,28},{20,24},{24,20},{28,16},{1,13},{... | collective-permute-start | bytes 497672 | tf_op jit(solution)/shard_map/ppermute | solution.py:328
  70.2 1.5 %shard_map.84 = f32[288,1152]{1,0:T(8,128)} custom-call(s32[2]{0:T(128)S(1)} %pad_add_fusion.place, bf16[72,1152]{1,0:T(8,128)(2,1)S(1)} %add_convert_fusion.2.refs_0_, bf16[72,1152]{1,0:T(8,128)(2,1)S(1)} %collective-permute-done.17.refs_1_, bf16[72,1152]{1,0:T(8,128)(2,1)S(1)} %collective-permute-done.18.refs_2_), custom_call_target="tpu_custom_call" | custom-call | tf_op jit(solution)/shard_map/pallas_call | solution.py:291
  71.7 1.6 %collective-permute-done.19 = bf16[72,1152]{1,0:T(8,128)(2,1)S(1)} collective-permute-done((bf16[72,1152]{1,0:T(8,128)(2,1)S(1)}, bf16[72,1152]{1,0:T(8,128)(2,1)S(1)}, u32[]{:S(2)}, u32[]{:S(2)}) %collective-permute-start.19) | collective-permute-done | bytes 165920 | tf_op jit(solution)/shard_map/ppermute | solution.py:328
  73.3 1.8 %dynamic_update_slice.6 = f32[288,1152]{1,0:T(8,128)} dynamic-update-slice(f32[288,1152]{1,0:T(8,128)} %shard_map.84, f32[72,1152]{1,0:T(8,128)S(1)} %convert_element_type.110, s32[]{:T(128)S(6)} %mul.3, s32[]{:T(128)} %constant.14.clone.1) | dynamic-update-slice | bytes 663556 | tf_op jit(solution)/shard_map/dynamic_update_slice | solution.py:304
  75.1 1.5 %shard_map.85 = f32[288,1152]{1,0:T(8,128)} custom-call(s32[2]{0:T(128)S(1)} %pad_add_fusion.place, bf16[72,1152]{1,0:T(8,128)(2,1)S(1)} %add_convert_fusion.refs_0_, bf16[72,1152]{1,0:T(8,128)(2,1)S(1)} %collective-permute-done.24.refs_1_, bf16[72,1152]{1,0:T(8,128)(2,1)S(1)} %collective-permute-done.25.refs_2_), custom_call_target="tpu_custom_call" | custom-call | tf_op jit(solution)/shard_map/pallas_call | solution.py:291
  76.8 1.8 %dynamic_update_slice.7 = f32[288,1152]{1,0:T(8,128)} dynamic-update-slice(f32[288,1152]{1,0:T(8,128)} %shard_map.85, f32[72,1152]{1,0:T(8,128)S(1)} %convert_element_type.119, s32[]{:T(128)S(6)} %mul.3, s32[]{:T(128)} %constant.14.clone.1) | dynamic-update-slice | bytes 663556 | tf_op jit(solution)/shard_map/dynamic_update_slice | solution.py:304
  (50 shorter events, 9.0 us)
Async XLA Ops:
  0.7 4.7 %collective-permute-start.2 = (bf16[256,1152]{1,0:T(8,128)(2,1)}, bf16[256,1152]{1,0:T(8,128)(2,1)S(1)}, u32[]{:S(2)}, u32[]{:S(2)}) collective-permute-start(bf16[256,1152]{1,0:T(8,128)(2,1)} %t0_far), channel_id=1, source_target_pairs={{0,1},{1,0},{2,3},{3,2},{4,5},{5,4},{6,7},{7,6},{8,9},{9,8},{10,11... | collective-permute-start | bytes 1769480 | tf_op jit(solution)/shard_map/ppermute | solution.py:328
  1.2 4.3 %collective-permute-start.3 = (bf16[256,1152]{1,0:T(8,128)(2,1)}, bf16[256,1152]{1,0:T(8,128)(2,1)S(1)}, u32[]{:S(2)}, u32[]{:S(2)}) collective-permute-start(bf16[256,1152]{1,0:T(8,128)(2,1)} %i0_far), channel_id=1, source_target_pairs={{0,1},{1,0},{2,3},{3,2},{4,5},{5,4},{6,7},{7,6},{8,9},{9,8},{10,11... | collective-permute-start | bytes 1769480 | tf_op jit(solution)/shard_map/ppermute | solution.py:328
  2.4 10.8 %collective-permute-start.1 = (bf16[128,1152]{1,0:T(8,128)(2,1)S(1)}, bf16[128,1152]{1,0:T(8,128)(2,1)S(1)}, u32[]{:S(2)}, u32[]{:S(2)}) collective-permute-start(bf16[128,1152]{1,0:T(8,128)(2,1)S(1)} %get-tuple-element.134), channel_id=1, source_target_pairs={{0,2},{1,3},{2,0},{3,1},{4,6},{5,7},{6,4},{7,5},{8,10},{9,11},{10,... | collective-permute-start | bytes 884744 | tf_op jit(solution)/shard_map/ppermute | solution.py:328
  5.3 8.4 %copy-start = (bf16[256,1152]{1,0:T(8,128)(2,1)S(1)}, bf16[256,1152]{1,0:T(8,128)(2,1)}, u32[]{:S(2)}) copy-start(bf16[256,1152]{1,0:T(8,128)(2,1)} %i0_far) | copy-start | bytes 1769476
  5.3 14.6 %collective-permute-start = (bf16[128,1152]{1,0:T(8,128)(2,1)S(1)}, bf16[128,1152]{1,0:T(8,128)(2,1)S(1)}, u32[]{:S(2)}, u32[]{:S(2)}) collective-permute-start(bf16[128,1152]{1,0:T(8,128)(2,1)S(1)} %get-tuple-element.135), channel_id=1, source_target_pairs={{0,2},{1,3},{2,0},{3,1},{4,6},{5,7},{6,4},{7,5},{8,10},{9,11},{10,... | collective-permute-start | bytes 884744 | tf_op jit(solution)/shard_map/ppermute | solution.py:328
  13.2 2.6 %collective-permute-start.4 = (bf16[64,1152]{1,0:T(8,128)(2,1)S(1)}, bf16[64,1152]{1,0:T(8,128)(2,1)S(1)}, u32[]{:S(2)}, u32[]{:S(2)}) collective-permute-start(bf16[64,1152]{1,0:T(8,128)(2,1)S(1)} %get-tuple-element.139), channel_id=1, source_target_pairs={{0,1},{1,0},{2,3},{3,2},{4,5},{5,4},{6,7},{7,6},{8,9},{9,8},{10,11... | collective-permute-start | bytes 442376 | tf_op jit(solution)/shard_map/ppermute | solution.py:328
  13.2 2.6 %collective-permute-start.5 = (bf16[64,1152]{1,0:T(8,128)(2,1)S(1)}, bf16[64,1152]{1,0:T(8,128)(2,1)S(1)}, u32[]{:S(2)}, u32[]{:S(2)}) collective-permute-start(bf16[64,1152]{1,0:T(8,128)(2,1)S(1)} %get-tuple-element.138), channel_id=1, source_target_pairs={{0,1},{1,0},{2,3},{3,2},{4,5},{5,4},{6,7},{7,6},{8,9},{9,8},{10,11... | collective-permute-start | bytes 442376 | tf_op jit(solution)/shard_map/ppermute | solution.py:328
  13.8 17.8 %collective-permute-start.9 = (bf16[256,1152]{1,0:T(8,128)(2,1)S(1)}, bf16[256,1152]{1,0:T(8,128)(2,1)S(1)}, u32[]{:S(2)}, u32[]{:S(2)}) collective-permute-start(bf16[256,1152]{1,0:T(8,128)(2,1)S(1)} %copy-done), channel_id=1, source_target_pairs={{0,2},{1,3},{2,0},{3,1},{4,6},{5,7},{6,4},{7,5},{8,10},{9,11},{10,... | collective-permute-start | bytes 1769480 | tf_op jit(solution)/shard_map/ppermute | solution.py:328
  20.0 1.4 %collective-permute-start.6 = (bf16[64,1152]{1,0:T(8,128)(2,1)S(1)}, bf16[64,1152]{1,0:T(8,128)(2,1)S(1)}, u32[]{:S(2)}, u32[]{:S(2)}) collective-permute-start(bf16[64,1152]{1,0:T(8,128)(2,1)S(1)} %get-tuple-element.137), channel_id=1, source_target_pairs={{0,1},{1,0},{2,3},{3,2},{4,5},{5,4},{6,7},{7,6},{8,9},{9,8},{10,11... | collective-permute-start | bytes 442376 | tf_op jit(solution)/shard_map/ppermute | solution.py:328
  20.0 1.6 %collective-permute-start.7 = (bf16[64,1152]{1,0:T(8,128)(2,1)S(1)}, bf16[64,1152]{1,0:T(8,128)(2,1)S(1)}, u32[]{:S(2)}, u32[]{:S(2)}) collective-permute-start(bf16[64,1152]{1,0:T(8,128)(2,1)S(1)} %get-tuple-element.136), channel_id=1, source_target_pairs={{0,1},{1,0},{2,3},{3,2},{4,5},{5,4},{6,7},{7,6},{8,9},{9,8},{10,11... | collective-permute-start | bytes 442376 | tf_op jit(solution)/shard_map/ppermute | solution.py:328
  25.5 10.1 %collective-permute-start.8 = (bf16[144,1152]{1,0:T(8,128)(2,1)S(1)}, bf16[144,1152]{1,0:T(8,128)(2,1)S(1)}, u32[]{:S(2)}, u32[]{:S(2)}) collective-permute-start(bf16[144,1152]{1,0:T(8,128)(2,1)S(1)} %get-tuple-element.85), channel_id=1, source_target_pairs={{0,4},{4,0},{8,12},{12,8},{16,20},{20,16},{24,28},{28,24},{1,5},{5... | collective-permute-start | bytes 995336 | tf_op jit(solution)/shard_map/ppermute | solution.py:328
  27.2 9.7 %collective-permute-start.12 = (bf16[144,1152]{1,0:T(8,128)(2,1)S(1)}, bf16[144,1152]{1,0:T(8,128)(2,1)S(1)}, u32[]{:S(2)}, u32[]{:S(2)}) collective-permute-start(bf16[144,1152]{1,0:T(8,128)(2,1)S(1)} %get-tuple-element.106), channel_id=1, source_target_pairs={{0,8},{4,12},{8,0},{12,4},{16,24},{20,28},{24,16},{28,20},{1,9},{5... | collective-permute-start | bytes 995336 | tf_op jit(solution)/shard_map/ppermute | solution.py:328
  33.5 5.7 %collective-permute-start.13 = (bf16[128,1152]{1,0:T(8,128)(2,1)S(1)}, bf16[128,1152]{1,0:T(8,128)(2,1)S(1)}, u32[]{:S(2)}, u32[]{:S(2)}) collective-permute-start(bf16[128,1152]{1,0:T(8,128)(2,1)S(1)} %get-tuple-element.97.x_second), channel_id=1, source_target_pairs={{0,1},{1,0},{2,3},{3,2},{4,5},{5,4},{6,7},{7,6},{8,9},{9,8},{10,11... | collective-permute-start | bytes 884744 | tf_op jit(solution)/shard_map/ppermute | solution.py:328
  33.6 5.7 %collective-permute-start.11 = (bf16[128,1152]{1,0:T(8,128)(2,1)S(1)}, bf16[128,1152]{1,0:T(8,128)(2,1)S(1)}, u32[]{:S(2)}, u32[]{:S(2)}) collective-permute-start(bf16[128,1152]{1,0:T(8,128)(2,1)S(1)} %get-tuple-element.96.x_first), channel_id=1, source_target_pairs={{0,1},{1,0},{2,3},{3,2},{4,5},{5,4},{6,7},{7,6},{8,9},{9,8},{10,11... | collective-permute-start | bytes 884744 | tf_op jit(solution)/shard_map/ppermute | solution.py:328
  37.0 5.8 %collective-permute-start.14 = (bf16[72,1152]{1,0:T(8,128)(2,1)S(1)}, bf16[72,1152]{1,0:T(8,128)(2,1)S(1)}, u32[]{:S(2)}, u32[]{:S(2)}) collective-permute-start(bf16[72,1152]{1,0:T(8,128)(2,1)S(1)} %add_convert_fusion.6), channel_id=1, source_target_pairs={{0,4},{4,0},{8,12},{12,8},{16,20},{20,16},{24,28},{28,24},{1,5},{5... | collective-permute-start | bytes 497672 | tf_op jit(solution)/shard_map/ppermute | solution.py:328
  37.5 10.4 %collective-permute-start.10 = (bf16[72,1152]{1,0:T(8,128)(2,1)S(1)}, bf16[72,1152]{1,0:T(8,128)(2,1)S(1)}, u32[]{:S(2)}, u32[]{:S(2)}) collective-permute-start(bf16[72,1152]{1,0:T(8,128)(2,1)S(1)} %add_convert_fusion.7), channel_id=1, source_target_pairs={{0,8},{4,12},{8,0},{12,4},{16,24},{20,28},{24,16},{28,20},{1,9},{5... | collective-permute-start | bytes 497672 | tf_op jit(solution)/shard_map/ppermute | solution.py:328
  42.9 5.4 %collective-permute-start.15 = (bf16[72,1152]{1,0:T(8,128)(2,1)S(1)}, bf16[72,1152]{1,0:T(8,128)(2,1)S(1)}, u32[]{:S(2)}, u32[]{:S(2)}) collective-permute-start(bf16[72,1152]{1,0:T(8,128)(2,1)S(1)} %add_convert_fusion.4), channel_id=1, source_target_pairs={{0,2},{1,3},{2,0},{3,1},{4,6},{5,7},{6,4},{7,5},{8,10},{9,11},{10,... | collective-permute-start | bytes 497672 | tf_op jit(solution)/shard_map/ppermute | solution.py:328
  44.4 10.7 %collective-permute-start.20 = (bf16[72,1152]{1,0:T(8,128)(2,1)S(1)}, bf16[72,1152]{1,0:T(8,128)(2,1)S(1)}, u32[]{:S(2)}, u32[]{:S(2)}) collective-permute-start(bf16[72,1152]{1,0:T(8,128)(2,1)S(1)} %get-tuple-element.126), channel_id=1, source_target_pairs={{0,4},{4,0},{8,12},{12,8},{16,20},{20,16},{24,28},{28,24},{1,5},{5... | collective-permute-start | bytes 497672 | tf_op jit(solution)/shard_map/ppermute | solution.py:328
  45.9 9.2 %collective-permute-start.21 = (bf16[72,1152]{1,0:T(8,128)(2,1)S(1)}, bf16[72,1152]{1,0:T(8,128)(2,1)S(1)}, u32[]{:S(2)}, u32[]{:S(2)}) collective-permute-start(bf16[72,1152]{1,0:T(8,128)(2,1)S(1)} %get-tuple-element.128), channel_id=1, source_target_pairs={{0,8},{4,12},{8,0},{12,4},{16,24},{20,28},{24,16},{28,20},{1,9},{5... | collective-permute-start | bytes 497672 | tf_op jit(solution)/shard_map/ppermute | solution.py:328
  46.4 11.3 %collective-permute-start.22 = (bf16[72,1152]{1,0:T(8,128)(2,1)S(1)}, bf16[72,1152]{1,0:T(8,128)(2,1)S(1)}, u32[]{:S(2)}, u32[]{:S(2)}) collective-permute-start(bf16[72,1152]{1,0:T(8,128)(2,1)S(1)} %get-tuple-element.130), channel_id=1, source_target_pairs={{0,12},{4,8},{8,4},{12,0},{16,28},{20,24},{24,20},{28,16},{1,13},{... | collective-permute-start | bytes 497672 | tf_op jit(solution)/shard_map/ppermute | solution.py:328
  48.3 10.9 %collective-permute-start.16 = (bf16[72,1152]{1,0:T(8,128)(2,1)S(1)}, bf16[72,1152]{1,0:T(8,128)(2,1)S(1)}, u32[]{:S(2)}, u32[]{:S(2)}) collective-permute-start(bf16[72,1152]{1,0:T(8,128)(2,1)S(1)} %add_convert_fusion.3), channel_id=1, source_target_pairs={{0,16},{4,20},{8,24},{12,28},{16,0},{20,4},{24,8},{28,12},{1,17},{... | collective-permute-start | bytes 497672 | tf_op jit(solution)/shard_map/ppermute | solution.py:328
  57.7 8.1 %collective-permute-start.23 = (bf16[72,1152]{1,0:T(8,128)(2,1)S(1)}, bf16[72,1152]{1,0:T(8,128)(2,1)S(1)}, u32[]{:S(2)}, u32[]{:S(2)}) collective-permute-start(bf16[72,1152]{1,0:T(8,128)(2,1)S(1)} %add_convert_fusion.1), channel_id=1, source_target_pairs={{0,16},{4,20},{8,24},{12,28},{16,0},{20,4},{24,8},{28,12},{1,17},{... | collective-permute-start | bytes 497672 | tf_op jit(solution)/shard_map/ppermute | solution.py:328
  59.3 7.2 %collective-permute-start.17 = (bf16[72,1152]{1,0:T(8,128)(2,1)S(1)}, bf16[72,1152]{1,0:T(8,128)(2,1)S(1)}, u32[]{:S(2)}, u32[]{:S(2)}) collective-permute-start(bf16[72,1152]{1,0:T(8,128)(2,1)S(1)} %add_convert_fusion.2.refs_0_), channel_id=1, source_target_pairs={{0,4},{4,0},{8,12},{12,8},{16,20},{20,16},{24,28},{28,24},{1,5},{5... | collective-permute-start | bytes 497672 | tf_op jit(solution)/shard_map/ppermute | solution.py:328
  61.0 9.2 %collective-permute-start.18 = (bf16[72,1152]{1,0:T(8,128)(2,1)S(1)}, bf16[72,1152]{1,0:T(8,128)(2,1)S(1)}, u32[]{:S(2)}, u32[]{:S(2)}) collective-permute-start(bf16[72,1152]{1,0:T(8,128)(2,1)S(1)} %add_convert_fusion.2.refs_0_), channel_id=1, source_target_pairs={{0,8},{4,12},{8,0},{12,4},{16,24},{20,28},{24,16},{28,20},{1,9},{5... | collective-permute-start | bytes 497672 | tf_op jit(solution)/shard_map/ppermute | solution.py:328
  63.4 9.9 %collective-permute-start.19 = (bf16[72,1152]{1,0:T(8,128)(2,1)S(1)}, bf16[72,1152]{1,0:T(8,128)(2,1)S(1)}, u32[]{:S(2)}, u32[]{:S(2)}) collective-permute-start(bf16[72,1152]{1,0:T(8,128)(2,1)S(1)} %add_convert_fusion.2.refs_0_), channel_id=1, source_target_pairs={{0,12},{4,8},{8,4},{12,0},{16,28},{20,24},{24,20},{28,16},{1,13},{... | collective-permute-start | bytes 497672 | tf_op jit(solution)/shard_map/ppermute | solution.py:328
  66.6 8.5 %collective-permute-start.24 = (bf16[72,1152]{1,0:T(8,128)(2,1)S(1)}, bf16[72,1152]{1,0:T(8,128)(2,1)S(1)}, u32[]{:S(2)}, u32[]{:S(2)}) collective-permute-start(bf16[72,1152]{1,0:T(8,128)(2,1)S(1)} %add_convert_fusion.refs_0_), channel_id=1, source_target_pairs={{0,4},{4,0},{8,12},{12,8},{16,20},{20,16},{24,28},{28,24},{1,5},{5... | collective-permute-start | bytes 497672 | tf_op jit(solution)/shard_map/ppermute | solution.py:328
  67.3 7.8 %collective-permute-start.25 = (bf16[72,1152]{1,0:T(8,128)(2,1)S(1)}, bf16[72,1152]{1,0:T(8,128)(2,1)S(1)}, u32[]{:S(2)}, u32[]{:S(2)}) collective-permute-start(bf16[72,1152]{1,0:T(8,128)(2,1)S(1)} %add_convert_fusion.refs_0_), channel_id=1, source_target_pairs={{0,8},{4,12},{8,0},{12,4},{16,24},{20,28},{24,16},{28,20},{1,9},{5... | collective-permute-start | bytes 497672 | tf_op jit(solution)/shard_map/ppermute | solution.py:328
  69.1 7.7 %collective-permute-start.26 = (bf16[72,1152]{1,0:T(8,128)(2,1)S(1)}, bf16[72,1152]{1,0:T(8,128)(2,1)S(1)}, u32[]{:S(2)}, u32[]{:S(2)}) collective-permute-start(bf16[72,1152]{1,0:T(8,128)(2,1)S(1)} %add_convert_fusion.refs_0_), channel_id=1, source_target_pairs={{0,12},{4,8},{8,4},{12,0},{16,28},{20,24},{24,20},{28,16},{1,13},{... | collective-permute-start | bytes 497672 | tf_op jit(solution)/shard_map/ppermute | solution.py:328

commit v12 on v11

--- a/solution.py
+++ b/solution.py
@@ -143,7 +143,6 @@
     t1, i1, t0_far, i0_far, text_head_far, image_head_far,
     q_a, y_a, p_a, x_a, w_aa, gx, t0, i0, text_head, image_head, dots, sems,
 ):
-    half = t0.shape[0]
     copies = [
         pltpu.make_async_copy(source, target, sems.at[n])
         for n, (source, target) in enumerate(
@@ -154,13 +153,11 @@
         copy.start()
     copies[0].wait()
     copies[1].wait()
-    q_a[:half, :] = dot_nn(t0[...], text_head[...])
-    q_a[half:, :] = dot_nn(t1[...], text_head[...])
+    q_a[...] = dot_nn(rows_of((t0, t1)), text_head[...])
     copies[2].wait()
     copies[3].wait()
-    p_a[:half, :] = dot_nn(i0[...], image_head[...])
+    p_a[...] = dot_nn(rows_of((i0, i1)), image_head[...])
     unit_rows(q_a, y_a)
-    p_a[half:, :] = dot_nn(i1[...], image_head[...])
     unit_rows(p_a, x_a)
     dots[...] = dot_nt(x_a[...], y_a[...])
     weight_rows(dots, w_aa, 0)
@@ -273,35 +270,11 @@
 
 
 def place_kernel(place, *refs):
-    *pieces, out, buffer, sems = refs
+    *pieces, out = refs
     part = pieces[0].shape[0]
-    copies = []
     for k, piece in enumerate(pieces):
-        buffer[k] = piece[...].astype(F32)
         first = pl.multiple_of((place[1] ^ k) * part, part)
-        copies.append(pltpu.make_async_copy(buffer.at[k], out.at[pl.ds(first, part), :], sems.at[k]))
-        copies[-1].start()
-    for copy in copies:
-        copy.wait()
-
-
-def placed(place, last_row, pieces):
-    rows, width = pieces[0].shape
-    *early, last = pieces
-    out = pl.pallas_call(
-        place_kernel,
-        out_shape=pltpu.HBM((QUAD * rows, width), F32),
-        in_specs=[pl.BlockSpec(memory_space=pltpu.SMEM)]
-        + [pl.BlockSpec(memory_space=pltpu.VMEM)] * len(early),
-        out_specs=pl.BlockSpec(memory_space=pltpu.HBM),
-        scratch_shapes=[
-            pltpu.VMEM((len(early), rows, width), F32), pltpu.SemaphoreType.DMA((len(early),))
-        ],
-        compiler_params=pltpu.CompilerParams(vmem_limit_bytes=4 * 1024 * 1024),
-        cost_estimate=pl.CostEstimate(flops=0, bytes_accessed=0, transcendentals=0),
-    )(place, *(pltpu.with_memory_space_constraint(a, pltpu.VMEM) for a in early))
-    last = after(last, out)
-    return lax.dynamic_update_slice(out, last.astype(F32), (last_row, 0), allow_negative_indices=False)
+        out[pl.ds(first, part), :] = piece[...].astype(F32)
 
 
 def call(kernel, outs, scratch, args, mib, place=None, macs=0, keep=True, far=()):
@@ -351,14 +324,12 @@
     def spread(total):
         return [total] + [cuts(total, mask=k) for k in range(1, QUAD)]
 
-    t2 = [loop(rows, mask=2) for rows in jnp.split(text_features, 2)]
+    t2 = loop(text_features[: half // 2], mask=2)
     i2 = loop(image_features, mask=2)
     place = jnp.stack([lax.axis_index("loop"), lax.axis_index("cuts") & (QUAD - 1)])
-    last_row = ((place[1] ^ (QUAD - 1)) * part).astype(jnp.int32)
     place = place.astype(jnp.int32)
-    t0, i0, place, last_row = lax.optimization_barrier(
-        (text_features, image_features, place, last_row)
-    )
+    t0, i0, place = lax.optimization_barrier((text_features, image_features, place))
+    t2 = [t2, loop(t0[half // 2 :], mask=2)]
     t1 = loop(t0, mask=1)
     i1 = loop(i0, mask=1)
     wide, wide_b = ((near, width), F32), ((near, width), BF16)
@@ -442,8 +413,10 @@
     image_sum = add(image_sum, [cuts(image_sum, mask=QUAD)])
     image_pieces = spread(image_sum)
     text_sum = add(text_sum, [after(cuts(text_sum, mask=QUAD), image_pieces[1])])
-    image_out = placed(place, last_row, image_pieces)
-    text_out = placed(place, last_row, spread(text_sum))
+    image_out, text_out = (
+        call(place_kernel, [((rows_out, width), F32)], [], pieces, 4, place, keep=False)[0]
+        for pieces in (image_pieces, spread(text_sum))
+    )
     return (*grads, image_out, text_out)
 
 

time: 78.8 us -> 79.1 us (level)
  local copies, waits for them, and re-layouts: 4.67 us -> 2.02 us
  waiting for transfers between devices: 10.5 us -> 13.1 us
    pallas_call x9 -> x11, Pallas kernels: 28.3 us -> 31.9 us  [call(): pl.pallas_call(kernel, out_shape=[shape(s, t) for s, t in outs], in_specs...]
    dynamic_update_slice x2 -> x0, local copies, waits for them, and re-layouts: 3.52 us -> none  [placed(): lax.dynamic_update_slice(out, last.astype(F32), (last_row, 0), allow_nega...]
    pallas_call x2 -> x0, Pallas kernels: 3.07 us -> none  [placed(): pl.pallas_call(place_kernel, out_shape=pltpu.HBM((QUAD * rows, width), F3...]
    ppermute x27, waiting for transfers between devices: 10.5 us -> 13.1 us  [swap(): return lax.ppermute(array, axis, [(i, i ^ mask) for i in range(size)])]
    slice x0 -> x2, local copies, waits for them, and re-layouts: none -> 1.97 us  [the longest x1 0.98 us: per_device(): t2 = loop(text_features[:half // 2], mask=2)]
    split x1 -> x0, local copies, waits for them, and re-layouts: 1.1 us -> none  [per_device(): t2 = [loop(rows, mask=2) for rows in jnp.split(text_features, 2)]]
  transfers between devices with their start and end apart: 27 -> 27, of which waited for: 12 -> 9; matrix products, arithmetic and copies ran while one was open for 4% -> 3% of each run, Pallas kernels for 40% -> 38%
where the time goes in v12:
time: 79.1 us; the launch traced here: 78.9 us
  Pallas kernels  31.9 us (40%)
  starting transfers between devices  30.6 us (39%)
  waiting for transfers between devices  13.1 us (17%)
  local copies, waits for them, and re-layouts  2.02 us (3%)
  between operations  0.83 us (1%)
    pallas_call x11, Pallas kernels, call(): pl.pallas_call(kernel, out_shape=[shape(s, t) for s, t in outs], in_specs...  31.9 us
    ppermute x27, starting transfers between devices, swap(): return lax.ppermute(array, axis, [(i, i ^ mask) for i in range(size)])  30.6 us
    ppermute x27, waiting for transfers between devices, swap(): return lax.ppermute(array, axis, [(i, i ^ mask) for i in range(size)])  13.1 us
  transfers between devices with their start and end apart: 27, of which 9 were waited for; matrix products, arithmetic and copies ran while one was open for 3% of the time, Pallas kernels for 38%

profile of v12, /device:TPU:0, one launch (start us, length us, event | category | flops | bytes accessed | tf_op | source)
XLA Modules:
  0.0 78.9 jit_solution(11057287692355877479)
XLA Ops:
  1.2 1.0 %slice.19 = bf16[128,1152]{1,0:T(8,128)(2,1)S(1)} slice(bf16[256,1152]{1,0:T(8,128)(2,1)} %t0_far), slice={[0:128], [0:1152]} | slice | bytes 589824 | tf_op jit(solution)/shard_map/slice | solution.py:327
  2.2 3.0 %collective-permute-start.1 = (bf16[128,1152]{1,0:T(8,128)(2,1)S(1)}, bf16[128,1152]{1,0:T(8,128)(2,1)S(1)}, u32[]{:S(2)}, u32[]{:S(2)}) collective-permute-start(bf16[128,1152]{1,0:T(8,128)(2,1)S(1)} %slice.19), channel_id=1, source_target_pairs={{0,2},{1,3},{2,0},{3,1},{4,6},{5,7},{6,4},{7,5},{8,10},{9,11},{10,... | collective-permute-start | bytes 884744 | tf_op jit(solution)/shard_map/ppermute | solution.py:301
  5.2 1.0 %slice.18 = bf16[128,1152]{1,0:T(8,128)(2,1)S(1)} slice(bf16[256,1152]{1,0:T(8,128)(2,1)} %t0_far), slice={[128:256], [0:1152]} | slice | bytes 589824 | tf_op jit(solution)/shard_map/slice | solution.py:332
  6.3 7.8 %shard_map.75 = (f32[512,1152]{1,0:T(8,128)S(1)}, bf16[512,1152]{1,0:T(8,128)(2,1)S(1)}, f32[512,1152]{1,0:T(8,128)S(1)}, bf16[512,1152]{1,0:T(8,128)(2,1)S(1)},...) custom-call(bf16[256,1152]{1,0:T(8,128)(2,1)S(1)} %collective-permut, ...), custom_call_target="tpu_custom_call" | custom-call | tf_op jit(solution)/shard_map/pallas_call | solution.py:288
  14.7 1.9 %collective-permute-start.9 = (bf16[256,1152]{1,0:T(8,128)(2,1)S(1)}, bf16[256,1152]{1,0:T(8,128)(2,1)S(1)}, u32[]{:S(2)}, u32[]{:S(2)}) collective-permute-start(bf16[256,1152]{1,0:T(8,128)(2,1)S(1)} %copy-done), channel_id=1, source_target_pairs={{0,2},{1,3},{2,0},{3,1},{4,6},{5,7},{6,4},{7,5},{8,10},{9,11},{10,... | collective-permute-start | bytes 1769480 | tf_op jit(solution)/shard_map/ppermute | solution.py:301
  16.7 4.1 %shard_map.76 = (f32[256,1152]{1,0:T(8,128)S(1)}, bf16[256,1152]{1,0:T(8,128)(2,1)S(1)}, bf16[512,256]{1,0:T(8,128)(2,1)S(1)}, f32[512,1152]{1,0:T(8,128)S(1)}, ...) custom-call(s32[2]{0:T(128)S(1)} %pad_add_fusion.place, bf16[128,1152]{1,0:T(8,128)(2,1)S(1)} %collective-permute-done.1.refs_0_, ...), custom_call_target="tpu_custom_call" | custom-call | tf_op jit(solution)/shard_map/pallas_call | solution.py:288
  22.5 3.9 %shard_map.77 = (f32[256,1152]{1,0:T(8,128)S(1)}, bf16[256,1152]{1,0:T(8,128)(2,1)S(1)}, bf16[512,256]{1,0:T(8,128)(2,1)S(1)}, bf16[512,1152]{1,0:T(8,128)(2,1)S...) custom-call(bf16[128,1152]{1,0:T(8,128)(2,1)S(1)} %collective-permut, ...), custom_call_target="tpu_custom_call" | custom-call | tf_op jit(solution)/shard_map/pallas_call | solution.py:288
  26.4 1.6 %collective-permute-start.8 = (bf16[144,1152]{1,0:T(8,128)(2,1)S(1)}, bf16[144,1152]{1,0:T(8,128)(2,1)S(1)}, u32[]{:S(2)}, u32[]{:S(2)}) collective-permute-start(bf16[144,1152]{1,0:T(8,128)(2,1)S(1)} %get-tuple-element.82), channel_id=1, source_target_pairs={{0,4},{4,0},{8,12},{12,8},{16,20},{20,16},{24,28},{28,24},{1,5},{5... | collective-permute-start | bytes 995336 | tf_op jit(solution)/shard_map/ppermute | solution.py:301
  27.9 1.6 %collective-permute-start.12 = (bf16[144,1152]{1,0:T(8,128)(2,1)S(1)}, bf16[144,1152]{1,0:T(8,128)(2,1)S(1)}, u32[]{:S(2)}, u32[]{:S(2)}) collective-permute-start(bf16[144,1152]{1,0:T(8,128)(2,1)S(1)} %get-tuple-element.103), channel_id=1, source_target_pairs={{0,8},{4,12},{8,0},{12,4},{16,24},{20,28},{24,16},{28,20},{1,9},{5... | collective-permute-start | bytes 995336 | tf_op jit(solution)/shard_map/ppermute | solution.py:301
  29.5 2.4 %shard_map.78 = (f32[256,1152]{1,0:T(8,128)S(1)}, f32[256,1152]{1,0:T(8,128)S(1)}, bf16[288,512]{1,0:T(8,128)(2,1)S(1)}, bf16[288,512]{1,0:T(8,128)(2,1)S(1)}) custom-call(s32[2]{0:T(128)S(1)} %pad_add_fusion.place, bf16[128,1152]{1,0:T(8,128)(2,1)S(1)} %collective-permute-done.1.refs_0_, bf16[64,1152]{1,0:T(8,128)(2,1)S(1)} %collective-permute-done.4.refs_1_, ...), custom_call_target="tpu_custom_call" | custom-call | tf_op jit(solution)/shard_map/pallas_call | solution.py:288
  31.9 1.9 %shard_map.79 = (bf16[128,1152]{1,0:T(8,128)(2,1)S(1)}, bf16[128,1152]{1,0:T(8,128)(2,1)S(1)}, bf16[256,512]{1,0:T(8,128)(2,1)S(1)}, bf16[256,256]{1,0:T(8,128)(2,1)S(1)}, bf16[256,256]{1,0:T(8,128)(2,1)S(1)}) custom-call(bf16[256,1152]{1,0:T(8,128)(2,1)S(1)} %collective-permute-done.9.i2, bf16[1152,1152]{1,0:T(8,128)(2,1)S(1)} %get-tuple-element.89.image_head.head, ...), custom_call_target="tpu_custom_call" | custom-call | tf_op jit(solution)/shard_map/pallas_call | solution.py:288
  35.3 1.1 %collective-permute-done.8 = bf16[144,1152]{1,0:T(8,128)(2,1)S(1)} collective-permute-done((bf16[144,1152]{1,0:T(8,128)(2,1)S(1)}, bf16[144,1152]{1,0:T(8,128)(2,1)S(1)}, u32[]{:S(2)}, u32[]{:S(2)}) %collective-permute-start.8) | collective-permute-done | bytes 331808 | tf_op jit(solution)/shard_map/ppermute | solution.py:301
  36.4 1.2 %collective-permute-done.12 = bf16[144,1152]{1,0:T(8,128)(2,1)S(1)} collective-permute-done((bf16[144,1152]{1,0:T(8,128)(2,1)S(1)}, bf16[144,1152]{1,0:T(8,128)(2,1)S(1)}, u32[]{:S(2)}, u32[]{:S(2)}) %collective-permute-start.12) | collective-permute-done | bytes 331808 | tf_op jit(solution)/shard_map/ppermute | solution.py:301
  38.3 1.6 %collective-permute-start.10 = (bf16[72,1152]{1,0:T(8,128)(2,1)S(1)}, bf16[72,1152]{1,0:T(8,128)(2,1)S(1)}, u32[]{:S(2)}, u32[]{:S(2)}) collective-permute-start(bf16[72,1152]{1,0:T(8,128)(2,1)S(1)} %add_convert_fusion.7), channel_id=1, source_target_pairs={{0,8},{4,12},{8,0},{12,4},{16,24},{20,28},{24,16},{28,20},{1,9},{5... | collective-permute-start | bytes 497672 | tf_op jit(solution)/shard_map/ppermute | solution.py:301
  40.0 3.5 %shard_map.81 = (bf16[72,1152]{1,0:T(8,128)(2,1)S(1)}, bf16[72,1152]{1,0:T(8,128)(2,1)S(1)}, bf16[72,1152]{1,0:T(8,128)(2,1)S(1)}, bf16[72,1152]{1,0:T(8,128)(2,1)S(1)}, bf16[512,1152]{1,0:T(8,128)(2,1)S(1)}) custom-call(bf16[128,1152]{1,0:T(8,128)(2,1)S(1)} %collective-permute-done.11.x_first, bf16[128,1152]{1,0:T(8,128)(2,1)S(1)} %collective-permute-done.13.x_second, ...), custom_call_target="tpu_custom_call" | custom-call | tf_op jit(solution)/shard_map/pallas_call | solution.py:288
  43.6 1.1 %collective-permute-start.15 = (bf16[72,1152]{1,0:T(8,128)(2,1)S(1)}, bf16[72,1152]{1,0:T(8,128)(2,1)S(1)}, u32[]{:S(2)}, u32[]{:S(2)}) collective-permute-start(bf16[72,1152]{1,0:T(8,128)(2,1)S(1)} %add_convert_fusion.4), channel_id=1, source_target_pairs={{0,2},{1,3},{2,0},{3,1},{4,6},{5,7},{6,4},{7,5},{8,10},{9,11},{10,... | collective-permute-start | bytes 497672 | tf_op jit(solution)/shard_map/ppermute | solution.py:301
  44.7 1.5 %collective-permute-start.20 = (bf16[72,1152]{1,0:T(8,128)(2,1)S(1)}, bf16[72,1152]{1,0:T(8,128)(2,1)S(1)}, u32[]{:S(2)}, u32[]{:S(2)}) collective-permute-start(bf16[72,1152]{1,0:T(8,128)(2,1)S(1)} %get-tuple-element.121), channel_id=1, source_target_pairs={{0,4},{4,0},{8,12},{12,8},{16,20},{20,16},{24,28},{28,24},{1,5},{5... | collective-permute-start | bytes 497672 | tf_op jit(solution)/shard_map/ppermute | solution.py:301
  46.7 1.5 %collective-permute-start.22 = (bf16[72,1152]{1,0:T(8,128)(2,1)S(1)}, bf16[72,1152]{1,0:T(8,128)(2,1)S(1)}, u32[]{:S(2)}, u32[]{:S(2)}) collective-permute-start(bf16[72,1152]{1,0:T(8,128)(2,1)S(1)} %get-tuple-element.125), channel_id=1, source_target_pairs={{0,12},{4,8},{8,4},{12,0},{16,28},{20,24},{24,20},{28,16},{1,13},{... | collective-permute-start | bytes 497672 | tf_op jit(solution)/shard_map/ppermute | solution.py:301
  49.1 2.6 %collective-permute-start.16 = (bf16[72,1152]{1,0:T(8,128)(2,1)S(1)}, bf16[72,1152]{1,0:T(8,128)(2,1)S(1)}, u32[]{:S(2)}, u32[]{:S(2)}) collective-permute-start(bf16[72,1152]{1,0:T(8,128)(2,1)S(1)} %add_convert_fusion.3), channel_id=1, source_target_pairs={{0,16},{4,20},{8,24},{12,28},{16,0},{20,4},{24,8},{28,12},{1,17},{... | collective-permute-start | bytes 497672 | tf_op jit(solution)/shard_map/ppermute | solution.py:301
  51.7 2.0 %shard_map.83 = f32[256,1152]{1,0:T(8,128)} custom-call(bf16[512,1152]{1,0:T(8,128)(2,1)S(1)} %get-tuple-element.119.back, bf16[1152,1152]{1,0:T(8,128)(2,1)S(1)} %get-tuple-element.72.refs_5_.refs_3_.head), custom_call_target="tpu_custom_call" | custom-call | flops 1358954496 | tf_op jit(solution)/shard_map/pallas_call | solution.py:288
  53.8 2.0 %shard_map.82 = f32[256,1152]{1,0:T(8,128)} custom-call(bf16[512,1152]{1,0:T(8,128)(2,1)S(1)} %get-tuple-element.118.back, bf16[1152,1152]{1,0:T(8,128)(2,1)S(1)} %get-tuple-element.89.image_head.head), custom_call_target="tpu_custom_call" | custom-call | flops 1358954496 | tf_op jit(solution)/shard_map/pallas_call | solution.py:288
  55.8 1.8 %collective-permute-done.22 = bf16[72,1152]{1,0:T(8,128)(2,1)S(1)} collective-permute-done((bf16[72,1152]{1,0:T(8,128)(2,1)S(1)}, bf16[72,1152]{1,0:T(8,128)(2,1)S(1)}, u32[]{:S(2)}, u32[]{:S(2)}) %collective-permute-start.22) | collective-permute-done | bytes 165920 | tf_op jit(solution)/shard_map/ppermute | solution.py:301
  58.7 2.3 %collective-permute-start.17 = (bf16[72,1152]{1,0:T(8,128)(2,1)S(1)}, bf16[72,1152]{1,0:T(8,128)(2,1)S(1)}, u32[]{:S(2)}, u32[]{:S(2)}) collective-permute-start(bf16[72,1152]{1,0:T(8,128)(2,1)S(1)} %add_convert_fusion.2.refs_0_), channel_id=1, source_target_pairs={{0,4},{4,0},{8,12},{12,8},{16,20},{20,16},{24,28},{28,24},{1,5},{5... | collective-permute-start | bytes 497672 | tf_op jit(solution)/shard_map/ppermute | solution.py:301
  61.0 2.0 %collective-permute-start.18 = (bf16[72,1152]{1,0:T(8,128)(2,1)S(1)}, bf16[72,1152]{1,0:T(8,128)(2,1)S(1)}, u32[]{:S(2)}, u32[]{:S(2)}) collective-permute-start(bf16[72,1152]{1,0:T(8,128)(2,1)S(1)} %add_convert_fusion.2.refs_0_), channel_id=1, source_target_pairs={{0,8},{4,12},{8,0},{12,4},{16,24},{20,28},{24,16},{28,20},{1,9},{5... | collective-permute-start | bytes 497672 | tf_op jit(solution)/shard_map/ppermute | solution.py:301
  63.1 1.4 %collective-permute-start.19 = (bf16[72,1152]{1,0:T(8,128)(2,1)S(1)}, bf16[72,1152]{1,0:T(8,128)(2,1)S(1)}, u32[]{:S(2)}, u32[]{:S(2)}) collective-permute-start(bf16[72,1152]{1,0:T(8,128)(2,1)S(1)} %add_convert_fusion.2.refs_0_), channel_id=1, source_target_pairs={{0,12},{4,8},{8,4},{12,0},{16,28},{20,24},{24,20},{28,16},{1,13},{... | collective-permute-start | bytes 497672 | tf_op jit(solution)/shard_map/ppermute | solution.py:301
  64.4 1.4 %collective-permute-done.23 = bf16[72,1152]{1,0:T(8,128)(2,1)S(1)} collective-permute-done((bf16[72,1152]{1,0:T(8,128)(2,1)S(1)}, bf16[72,1152]{1,0:T(8,128)(2,1)S(1)}, u32[]{:S(2)}, u32[]{:S(2)}) %collective-permute-start.23) | collective-permute-done | bytes 165920 | tf_op jit(solution)/shard_map/ppermute | solution.py:301
  65.9 1.4 %collective-permute-start.24 = (bf16[72,1152]{1,0:T(8,128)(2,1)S(1)}, bf16[72,1152]{1,0:T(8,128)(2,1)S(1)}, u32[]{:S(2)}, u32[]{:S(2)}) collective-permute-start(bf16[72,1152]{1,0:T(8,128)(2,1)S(1)} %add_convert_fusion.refs_0_), channel_id=1, source_target_pairs={{0,4},{4,0},{8,12},{12,8},{16,20},{20,16},{24,28},{28,24},{1,5},{5... | collective-permute-start | bytes 497672 | tf_op jit(solution)/shard_map/ppermute | solution.py:301
  67.2 2.4 %collective-permute-start.25 = (bf16[72,1152]{1,0:T(8,128)(2,1)S(1)}, bf16[72,1152]{1,0:T(8,128)(2,1)S(1)}, u32[]{:S(2)}, u32[]{:S(2)}) collective-permute-start(bf16[72,1152]{1,0:T(8,128)(2,1)S(1)} %add_convert_fusion.refs_0_), channel_id=1, source_target_pairs={{0,8},{4,12},{8,0},{12,4},{16,24},{20,28},{24,16},{28,20},{1,9},{5... | collective-permute-start | bytes 497672 | tf_op jit(solution)/shard_map/ppermute | solution.py:301
  69.9 3.3 %collective-permute-done.19.refs_3_ = bf16[72,1152]{1,0:T(8,128)(2,1)S(1)} collective-permute-done((bf16[72,1152]{1,0:T(8,128)(2,1)S(1)}, bf16[72,1152]{1,0:T(8,128)(2,1)S(1)}, u32[]{:S(2)}, u32[]{:S(2)}) %collective-permute-start.19) | collective-permute-done | bytes 165920 | tf_op jit(solution)/shard_map/ppermute | solution.py:301
  73.2 1.7 %shard_map.84 = f32[288,1152]{1,0:T(8,128)} custom-call(s32[2]{0:T(128)S(1)} %pad_add_fusion.place, bf16[72,1152]{1,0:T(8,128)(2,1)S(1)} %add_convert_fusion.2.refs_0_, bf16[72,1152]{1,0:T(8,128)(2,1)S(1)} %collective-permute-done.17.refs_1_, bf16[72,1152]{1,0:T(8,128)(2,1)S(1)} %collective-permute-done.18.refs_2_, ...), custom_call_target="tpu_custom_call" | custom-call | tf_op jit(solution)/shard_map/pallas_call | solution.py:288
  74.9 2.4 %collective-permute-done.26.refs_3_ = bf16[72,1152]{1,0:T(8,128)(2,1)S(1)} collective-permute-done((bf16[72,1152]{1,0:T(8,128)(2,1)S(1)}, bf16[72,1152]{1,0:T(8,128)(2,1)S(1)}, u32[]{:S(2)}, u32[]{:S(2)}) %collective-permute-start.26) | collective-permute-done | bytes 165920 | tf_op jit(solution)/shard_map/ppermute | solution.py:301
  77.2 1.7 %shard_map.85 = f32[288,1152]{1,0:T(8,128)} custom-call(s32[2]{0:T(128)S(1)} %pad_add_fusion.place, bf16[72,1152]{1,0:T(8,128)(2,1)S(1)} %add_convert_fusion.refs_0_, bf16[72,1152]{1,0:T(8,128)(2,1)S(1)} %collective-permute-done.24.refs_1_, bf16[72,1152]{1,0:T(8,128)(2,1)S(1)} %collective-permute-done.25.refs_2_, ...), custom_call_target="tpu_custom_call" | custom-call | tf_op jit(solution)/shard_map/pallas_call | solution.py:288
  (47 shorter events, 7.9 us)
Async XLA Ops:
  0.7 5.6 %collective-permute-start.2 = (bf16[256,1152]{1,0:T(8,128)(2,1)}, bf16[256,1152]{1,0:T(8,128)(2,1)S(1)}, u32[]{:S(2)}, u32[]{:S(2)}) collective-permute-start(bf16[256,1152]{1,0:T(8,128)(2,1)} %t0_far), channel_id=1, source_target_pairs={{0,1},{1,0},{2,3},{3,2},{4,5},{5,4},{6,7},{7,6},{8,9},{9,8},{10,11... | collective-permute-start | bytes 1769480 | tf_op jit(solution)/shard_map/ppermute | solution.py:301
  1.2 5.1 %collective-permute-start.3 = (bf16[256,1152]{1,0:T(8,128)(2,1)}, bf16[256,1152]{1,0:T(8,128)(2,1)S(1)}, u32[]{:S(2)}, u32[]{:S(2)}) collective-permute-start(bf16[256,1152]{1,0:T(8,128)(2,1)} %i0_far), channel_id=1, source_target_pairs={{0,1},{1,0},{2,3},{3,2},{4,5},{5,4},{6,7},{7,6},{8,9},{9,8},{10,11... | collective-permute-start | bytes 1769480 | tf_op jit(solution)/shard_map/ppermute | solution.py:301
  2.2 11.9 %collective-permute-start.1 = (bf16[128,1152]{1,0:T(8,128)(2,1)S(1)}, bf16[128,1152]{1,0:T(8,128)(2,1)S(1)}, u32[]{:S(2)}, u32[]{:S(2)}) collective-permute-start(bf16[128,1152]{1,0:T(8,128)(2,1)S(1)} %slice.19), channel_id=1, source_target_pairs={{0,2},{1,3},{2,0},{3,1},{4,6},{5,7},{6,4},{7,5},{8,10},{9,11},{10,... | collective-permute-start | bytes 884744 | tf_op jit(solution)/shard_map/ppermute | solution.py:301
  6.2 8.5 %copy-start = (bf16[256,1152]{1,0:T(8,128)(2,1)S(1)}, bf16[256,1152]{1,0:T(8,128)(2,1)}, u32[]{:S(2)}) copy-start(bf16[256,1152]{1,0:T(8,128)(2,1)} %i0_far) | copy-start | bytes 1769476
  6.2 14.5 %collective-permute-start = (bf16[128,1152]{1,0:T(8,128)(2,1)S(1)}, bf16[128,1152]{1,0:T(8,128)(2,1)S(1)}, u32[]{:S(2)}, u32[]{:S(2)}) collective-permute-start(bf16[128,1152]{1,0:T(8,128)(2,1)S(1)} %slice.18), channel_id=1, source_target_pairs={{0,2},{1,3},{2,0},{3,1},{4,6},{5,7},{6,4},{7,5},{8,10},{9,11},{10,... | collective-permute-start | bytes 884744 | tf_op jit(solution)/shard_map/ppermute | solution.py:301
  14.1 2.5 %collective-permute-start.4 = (bf16[64,1152]{1,0:T(8,128)(2,1)S(1)}, bf16[64,1152]{1,0:T(8,128)(2,1)S(1)}, u32[]{:S(2)}, u32[]{:S(2)}) collective-permute-start(bf16[64,1152]{1,0:T(8,128)(2,1)S(1)} %get-tuple-element.131), channel_id=1, source_target_pairs={{0,1},{1,0},{2,3},{3,2},{4,5},{5,4},{6,7},{7,6},{8,9},{9,8},{10,11... | collective-permute-start | bytes 442376 | tf_op jit(solution)/shard_map/ppermute | solution.py:301
  14.2 2.5 %collective-permute-start.5 = (bf16[64,1152]{1,0:T(8,128)(2,1)S(1)}, bf16[64,1152]{1,0:T(8,128)(2,1)S(1)}, u32[]{:S(2)}, u32[]{:S(2)}) collective-permute-start(bf16[64,1152]{1,0:T(8,128)(2,1)S(1)} %get-tuple-element.130), channel_id=1, source_target_pairs={{0,1},{1,0},{2,3},{3,2},{4,5},{5,4},{6,7},{7,6},{8,9},{9,8},{10,11... | collective-permute-start | bytes 442376 | tf_op jit(solution)/shard_map/ppermute | solution.py:301
  14.7 17.2 %collective-permute-start.9 = (bf16[256,1152]{1,0:T(8,128)(2,1)S(1)}, bf16[256,1152]{1,0:T(8,128)(2,1)S(1)}, u32[]{:S(2)}, u32[]{:S(2)}) collective-permute-start(bf16[256,1152]{1,0:T(8,128)(2,1)S(1)} %copy-done), channel_id=1, source_target_pairs={{0,2},{1,3},{2,0},{3,1},{4,6},{5,7},{6,4},{7,5},{8,10},{9,11},{10,... | collective-permute-start | bytes 1769480 | tf_op jit(solution)/shard_map/ppermute | solution.py:301
  20.8 1.4 %collective-permute-start.6 = (bf16[64,1152]{1,0:T(8,128)(2,1)S(1)}, bf16[64,1152]{1,0:T(8,128)(2,1)S(1)}, u32[]{:S(2)}, u32[]{:S(2)}) collective-permute-start(bf16[64,1152]{1,0:T(8,128)(2,1)S(1)} %get-tuple-element.129), channel_id=1, source_target_pairs={{0,1},{1,0},{2,3},{3,2},{4,5},{5,4},{6,7},{7,6},{8,9},{9,8},{10,11... | collective-permute-start | bytes 442376 | tf_op jit(solution)/shard_map/ppermute | solution.py:301
  20.9 1.6 %collective-permute-start.7 = (bf16[64,1152]{1,0:T(8,128)(2,1)S(1)}, bf16[64,1152]{1,0:T(8,128)(2,1)S(1)}, u32[]{:S(2)}, u32[]{:S(2)}) collective-permute-start(bf16[64,1152]{1,0:T(8,128)(2,1)S(1)} %get-tuple-element.128), channel_id=1, source_target_pairs={{0,1},{1,0},{2,3},{3,2},{4,5},{5,4},{6,7},{7,6},{8,9},{9,8},{10,11... | collective-permute-start | bytes 442376 | tf_op jit(solution)/shard_map/ppermute | solution.py:301
  26.4 10.1 %collective-permute-start.8 = (bf16[144,1152]{1,0:T(8,128)(2,1)S(1)}, bf16[144,1152]{1,0:T(8,128)(2,1)S(1)}, u32[]{:S(2)}, u32[]{:S(2)}) collective-permute-start(bf16[144,1152]{1,0:T(8,128)(2,1)S(1)} %get-tuple-element.82), channel_id=1, source_target_pairs={{0,4},{4,0},{8,12},{12,8},{16,20},{20,16},{24,28},{28,24},{1,5},{5... | collective-permute-start | bytes 995336 | tf_op jit(solution)/shard_map/ppermute | solution.py:301
  27.9 9.7 %collective-permute-start.12 = (bf16[144,1152]{1,0:T(8,128)(2,1)S(1)}, bf16[144,1152]{1,0:T(8,128)(2,1)S(1)}, u32[]{:S(2)}, u32[]{:S(2)}) collective-permute-start(bf16[144,1152]{1,0:T(8,128)(2,1)S(1)} %get-tuple-element.103), channel_id=1, source_target_pairs={{0,8},{4,12},{8,0},{12,4},{16,24},{20,28},{24,16},{28,20},{1,9},{5... | collective-permute-start | bytes 995336 | tf_op jit(solution)/shard_map/ppermute | solution.py:301
  33.9 6.1 %collective-permute-start.13 = (bf16[128,1152]{1,0:T(8,128)(2,1)S(1)}, bf16[128,1152]{1,0:T(8,128)(2,1)S(1)}, u32[]{:S(2)}, u32[]{:S(2)}) collective-permute-start(bf16[128,1152]{1,0:T(8,128)(2,1)S(1)} %get-tuple-element.94.x_second), channel_id=1, source_target_pairs={{0,1},{1,0},{2,3},{3,2},{4,5},{5,4},{6,7},{7,6},{8,9},{9,8},{10,11... | collective-permute-start | bytes 884744 | tf_op jit(solution)/shard_map/ppermute | solution.py:301
  33.9 6.1 %collective-permute-start.11 = (bf16[128,1152]{1,0:T(8,128)(2,1)S(1)}, bf16[128,1152]{1,0:T(8,128)(2,1)S(1)}, u32[]{:S(2)}, u32[]{:S(2)}) collective-permute-start(bf16[128,1152]{1,0:T(8,128)(2,1)S(1)} %get-tuple-element.93.x_first), channel_id=1, source_target_pairs={{0,1},{1,0},{2,3},{3,2},{4,5},{5,4},{6,7},{7,6},{8,9},{9,8},{10,11... | collective-permute-start | bytes 884744 | tf_op jit(solution)/shard_map/ppermute | solution.py:301
  37.7 5.8 %collective-permute-start.14 = (bf16[72,1152]{1,0:T(8,128)(2,1)S(1)}, bf16[72,1152]{1,0:T(8,128)(2,1)S(1)}, u32[]{:S(2)}, u32[]{:S(2)}) collective-permute-start(bf16[72,1152]{1,0:T(8,128)(2,1)S(1)} %add_convert_fusion.6), channel_id=1, source_target_pairs={{0,4},{4,0},{8,12},{12,8},{16,20},{20,16},{24,28},{28,24},{1,5},{5... | collective-permute-start | bytes 497672 | tf_op jit(solution)/shard_map/ppermute | solution.py:301
  38.3 9.9 %collective-permute-start.10 = (bf16[72,1152]{1,0:T(8,128)(2,1)S(1)}, bf16[72,1152]{1,0:T(8,128)(2,1)S(1)}, u32[]{:S(2)}, u32[]{:S(2)}) collective-permute-start(bf16[72,1152]{1,0:T(8,128)(2,1)S(1)} %add_convert_fusion.7), channel_id=1, source_target_pairs={{0,8},{4,12},{8,0},{12,4},{16,24},{20,28},{24,16},{28,20},{1,9},{5... | collective-permute-start | bytes 497672 | tf_op jit(solution)/shard_map/ppermute | solution.py:301
  43.6 5.4 %collective-permute-start.15 = (bf16[72,1152]{1,0:T(8,128)(2,1)S(1)}, bf16[72,1152]{1,0:T(8,128)(2,1)S(1)}, u32[]{:S(2)}, u32[]{:S(2)}) collective-permute-start(bf16[72,1152]{1,0:T(8,128)(2,1)S(1)} %add_convert_fusion.4), channel_id=1, source_target_pairs={{0,2},{1,3},{2,0},{3,1},{4,6},{5,7},{6,4},{7,5},{8,10},{9,11},{10,... | collective-permute-start | bytes 497672 | tf_op jit(solution)/shard_map/ppermute | solution.py:301
  44.7 11.1 %collective-permute-start.20 = (bf16[72,1152]{1,0:T(8,128)(2,1)S(1)}, bf16[72,1152]{1,0:T(8,128)(2,1)S(1)}, u32[]{:S(2)}, u32[]{:S(2)}) collective-permute-start(bf16[72,1152]{1,0:T(8,128)(2,1)S(1)} %get-tuple-element.121), channel_id=1, source_target_pairs={{0,4},{4,0},{8,12},{12,8},{16,20},{20,16},{24,28},{28,24},{1,5},{5... | collective-permute-start | bytes 497672 | tf_op jit(solution)/shard_map/ppermute | solution.py:301
  46.2 9.6 %collective-permute-start.21 = (bf16[72,1152]{1,0:T(8,128)(2,1)S(1)}, bf16[72,1152]{1,0:T(8,128)(2,1)S(1)}, u32[]{:S(2)}, u32[]{:S(2)}) collective-permute-start(bf16[72,1152]{1,0:T(8,128)(2,1)S(1)} %get-tuple-element.123), channel_id=1, source_target_pairs={{0,8},{4,12},{8,0},{12,4},{16,24},{20,28},{24,16},{28,20},{1,9},{5... | collective-permute-start | bytes 497672 | tf_op jit(solution)/shard_map/ppermute | solution.py:301
  46.7 10.9 %collective-permute-start.22 = (bf16[72,1152]{1,0:T(8,128)(2,1)S(1)}, bf16[72,1152]{1,0:T(8,128)(2,1)S(1)}, u32[]{:S(2)}, u32[]{:S(2)}) collective-permute-start(bf16[72,1152]{1,0:T(8,128)(2,1)S(1)} %get-tuple-element.125), channel_id=1, source_target_pairs={{0,12},{4,8},{8,4},{12,0},{16,28},{20,24},{24,20},{28,16},{1,13},{... | collective-permute-start | bytes 497672 | tf_op jit(solution)/shard_map/ppermute | solution.py:301
  49.1 9.6 %collective-permute-start.16 = (bf16[72,1152]{1,0:T(8,128)(2,1)S(1)}, bf16[72,1152]{1,0:T(8,128)(2,1)S(1)}, u32[]{:S(2)}, u32[]{:S(2)}) collective-permute-start(bf16[72,1152]{1,0:T(8,128)(2,1)S(1)} %add_convert_fusion.3), channel_id=1, source_target_pairs={{0,16},{4,20},{8,24},{12,28},{16,0},{20,4},{24,8},{28,12},{1,17},{... | collective-permute-start | bytes 497672 | tf_op jit(solution)/shard_map/ppermute | solution.py:301
  57.7 8.1 %collective-permute-start.23 = (bf16[72,1152]{1,0:T(8,128)(2,1)S(1)}, bf16[72,1152]{1,0:T(8,128)(2,1)S(1)}, u32[]{:S(2)}, u32[]{:S(2)}) collective-permute-start(bf16[72,1152]{1,0:T(8,128)(2,1)S(1)} %add_convert_fusion.1), channel_id=1, source_target_pairs={{0,16},{4,20},{8,24},{12,28},{16,0},{20,4},{24,8},{28,12},{1,17},{... | collective-permute-start | bytes 497672 | tf_op jit(solution)/shard_map/ppermute | solution.py:301
  58.7 7.1 %collective-permute-start.17 = (bf16[72,1152]{1,0:T(8,128)(2,1)S(1)}, bf16[72,1152]{1,0:T(8,128)(2,1)S(1)}, u32[]{:S(2)}, u32[]{:S(2)}) collective-permute-start(bf16[72,1152]{1,0:T(8,128)(2,1)S(1)} %add_convert_fusion.2.refs_0_), channel_id=1, source_target_pairs={{0,4},{4,0},{8,12},{12,8},{16,20},{20,16},{24,28},{28,24},{1,5},{5... | collective-permute-start | bytes 497672 | tf_op jit(solution)/shard_map/ppermute | solution.py:301
  61.0 8.9 %collective-permute-start.18 = (bf16[72,1152]{1,0:T(8,128)(2,1)S(1)}, bf16[72,1152]{1,0:T(8,128)(2,1)S(1)}, u32[]{:S(2)}, u32[]{:S(2)}) collective-permute-start(bf16[72,1152]{1,0:T(8,128)(2,1)S(1)} %add_convert_fusion.2.refs_0_), channel_id=1, source_target_pairs={{0,8},{4,12},{8,0},{12,4},{16,24},{20,28},{24,16},{28,20},{1,9},{5... | collective-permute-start | bytes 497672 | tf_op jit(solution)/shard_map/ppermute | solution.py:301
  63.1 10.1 %collective-permute-start.19 = (bf16[72,1152]{1,0:T(8,128)(2,1)S(1)}, bf16[72,1152]{1,0:T(8,128)(2,1)S(1)}, u32[]{:S(2)}, u32[]{:S(2)}) collective-permute-start(bf16[72,1152]{1,0:T(8,128)(2,1)S(1)} %add_convert_fusion.2.refs_0_), channel_id=1, source_target_pairs={{0,12},{4,8},{8,4},{12,0},{16,28},{20,24},{24,20},{28,16},{1,13},{... | collective-permute-start | bytes 497672 | tf_op jit(solution)/shard_map/ppermute | solution.py:301
  65.9 9.0 %collective-permute-start.24 = (bf16[72,1152]{1,0:T(8,128)(2,1)S(1)}, bf16[72,1152]{1,0:T(8,128)(2,1)S(1)}, u32[]{:S(2)}, u32[]{:S(2)}) collective-permute-start(bf16[72,1152]{1,0:T(8,128)(2,1)S(1)} %add_convert_fusion.refs_0_), channel_id=1, source_target_pairs={{0,4},{4,0},{8,12},{12,8},{16,20},{20,16},{24,28},{28,24},{1,5},{5... | collective-permute-start | bytes 497672 | tf_op jit(solution)/shard_map/ppermute | solution.py:301
  67.2 7.6 %collective-permute-start.25 = (bf16[72,1152]{1,0:T(8,128)(2,1)S(1)}, bf16[72,1152]{1,0:T(8,128)(2,1)S(1)}, u32[]{:S(2)}, u32[]{:S(2)}) collective-permute-start(bf16[72,1152]{1,0:T(8,128)(2,1)S(1)} %add_convert_fusion.refs_0_), channel_id=1, source_target_pairs={{0,8},{4,12},{8,0},{12,4},{16,24},{20,28},{24,16},{28,20},{1,9},{5... | collective-permute-start | bytes 497672 | tf_op jit(solution)/shard_map/ppermute | solution.py:301
  69.6 7.6 %collective-permute-start.26 = (bf16[72,1152]{1,0:T(8,128)(2,1)S(1)}, bf16[72,1152]{1,0:T(8,128)(2,1)S(1)}, u32[]{:S(2)}, u32[]{:S(2)}) collective-permute-start(bf16[72,1152]{1,0:T(8,128)(2,1)S(1)} %add_convert_fusion.refs_0_), channel_id=1, source_target_pairs={{0,12},{4,8},{8,4},{12,0},{16,28},{20,24},{24,20},{28,16},{1,13},{... | collective-permute-start | bytes 497672 | tf_op jit(solution)/shard_map/ppermute | solution.py:301

commit v13 on v12

--- a/solution.py
+++ b/solution.py
@@ -133,16 +133,11 @@
     return jnp.concatenate(pieces, axis=0).astype(BF16)
 
 
-def split_head(head, outs):
-    part = head.shape[0] // QUAD
-    for k, out in enumerate(outs):
-        out[...] = head[k * part : (k + 1) * part, :].astype(BF16)
-
-
 def near_kernel(
     t1, i1, t0_far, i0_far, text_head_far, image_head_far,
     q_a, y_a, p_a, x_a, w_aa, gx, t0, i0, text_head, image_head, dots, sems,
 ):
+    half = t0.shape[0]
     copies = [
         pltpu.make_async_copy(source, target, sems.at[n])
         for n, (source, target) in enumerate(
@@ -153,11 +148,13 @@
         copy.start()
     copies[0].wait()
     copies[1].wait()
-    q_a[...] = dot_nn(rows_of((t0, t1)), text_head[...])
+    q_a[:half, :] = dot_nn(t0[...], text_head[...])
+    q_a[half:, :] = dot_nn(t1[...], text_head[...])
     copies[2].wait()
     copies[3].wait()
-    p_a[...] = dot_nn(rows_of((i0, i1)), image_head[...])
+    p_a[:half, :] = dot_nn(i0[...], image_head[...])
     unit_rows(q_a, y_a)
+    p_a[half:, :] = dot_nn(i1[...], image_head[...])
     unit_rows(p_a, x_a)
     dots[...] = dot_nt(x_a[...], y_a[...])
     weight_rows(dots, w_aa, 0)
@@ -169,8 +166,8 @@
 
 
 def text_kernel(place, *refs):
-    *features, i0, i1, text_head, gx_in, x_a, w_aa = refs[:-7]
-    q_2, y_2, w_a2, gx, gy_a, pick_i, dots = refs[-7:]
+    *features, i0, i1, text_head, gx_in, x_a = refs[:-6]
+    q_2, y_2, w_a2, gx, pick_i, dots = refs[-6:]
     half, width = i0.shape
     q_2[...] = dot_nn(rows_of(features), text_head[...])
     pick = picker(place, pick_i.shape[0] // 2, width, (0, 2))
@@ -180,7 +177,6 @@
     pick_i[:, half:] = dot_nt(pick, i1[...]).astype(BF16)
     weight_rows(dots, w_a2)
     gx[...] = gx_in[...] + dot_nn(w_a2[...], y_2[...])
-    gy_a[...] = dot_tn(w_aa[...], x_a[...])
 
 
 def image_kernel(*refs):
@@ -209,8 +205,9 @@
 
 
 def text_pull_kernel(place, *refs):
-    *features, t0, t1, x_a, w_a2, w_a3, gy_2, gy_3, pick_a, pick_b = refs
+    *features, t0, t1, x_a, w_aa, w_a2, w_a3, gy_a, gy_2, gy_3, pick_a, pick_b = refs
     half = t0.shape[0]
+    gy_a[...] = dot_tn(w_aa[...], x_a[...])
     gy_2[...] = dot_tn(w_a2[...], x_a[...])
     gy_3[...] = dot_tn(w_a3[...], x_a[...])
     pick = picker(place, pick_a.shape[0], t0.shape[1], (0,))
@@ -250,7 +247,7 @@
 
 def last_kernel(
     x_first, x_second, y_a, y_2, y_3, q_a, q_2, q_3, gy_a_in, gy_2_in, gy_3_in, pick_a, pick_b,
-    h0, h1, h2, h3, dq_a, gy_a, gy_2, gy_3, dq_b, near_head, w_a, w_2, w_3, d_a, d_2, d_3,
+    kept_0, kept_2, sent, dq_a, gy_a, gy_2, gy_3, dq_b, near_head, w_a, w_2, w_3, d_a, d_2, d_3,
 ):
     half = q_2.shape[0]
     x = rows_of((x_first, x_second))
@@ -262,7 +259,16 @@
     near_head[...] = dot_nn(pick_a[...], dq_a[...])
     back_rows(q_2, gy_2, dq_b, 0)
     back_rows(q_3, gy_3, dq_b, half)
-    split_head(near_head[...] + dot_nn(pick_b[...], dq_b[...]), (h0, h1, h2, h3))
+    head = (near_head[...] + dot_nn(pick_b[...], dq_b[...])).astype(BF16)
+    part = kept_0.shape[0]
+    kept_0[...] = head[:part, :]
+    kept_2[...] = head[2 * part : 3 * part, :]
+    sent[:part, :] = head[part : 2 * part, :]
+    sent[part:, :] = head[3 * part :, :]
+
+
+def add_kernel(left, right, out):
+    out[...] = (left[...].astype(F32) + right[...].astype(F32)).astype(BF16)
 
 
 def grad_kernel(back, head, out):
@@ -324,12 +330,11 @@
     def spread(total):
         return [total] + [cuts(total, mask=k) for k in range(1, QUAD)]
 
-    t2 = loop(text_features[: half // 2], mask=2)
+    t2 = [loop(rows, mask=2) for rows in jnp.split(text_features, 2)]
     i2 = loop(image_features, mask=2)
     place = jnp.stack([lax.axis_index("loop"), lax.axis_index("cuts") & (QUAD - 1)])
     place = place.astype(jnp.int32)
     t0, i0, place = lax.optimization_barrier((text_features, image_features, place))
-    t2 = [t2, loop(t0[half // 2 :], mask=2)]
     t1 = loop(t0, mask=1)
     i1 = loop(i0, mask=1)
     wide, wide_b = ((near, width), F32), ((near, width), BF16)
@@ -347,15 +352,15 @@
         far=(t0, i0, text_head, image_head),
     )
     first = both(t2[0], w_aa, 2)
-    q_2, y_2, w_a2, gx, gy_a, pick_i = call(
+    q_2, y_2, w_a2, gx, pick_i = call(
         text_kernel,
-        [tall, tall_b, side_w, wide, wide, pick_two],
+        [tall, tall_b, side_w, wide, pick_two],
         [side_dots],
-        (*first, i0, i1, text_head, gx, x_a, w_aa),
+        (*first, i0, i1, text_head, gx, x_a),
         8,
         place,
     )
-    second = both(t2[1], gy_a, 2)
+    second = both(t2[1], gx, 2)
     part_b, parts_b = ((part, width), BF16), ((2 * part, width), BF16)
     q_3, y_3, w_a3, dp_a, near_0, near_2, near_sent, far_0, far_1, far_sent = call(
         image_kernel,
@@ -365,11 +370,11 @@
         8,
     )
     near_came, far_came = cuts(near_sent, mask=1), cuts(far_sent, mask=2)
-    gy_2, gy_3, pick_a, pick_b = call(
+    gy_a, gy_2, gy_3, pick_a, pick_b = call(
         text_pull_kernel,
-        [tall, tall, pick_one, pick_one],
+        [wide, tall, tall, pick_one, pick_one],
         [],
-        (*first, *second, t0, t1, after(x_a, dp_a), w_a2, w_a3),
+        (*first, *second, t0, t1, after(x_a, dp_a), w_aa, w_a2, w_a3),
         8,
         place,
     )
@@ -393,15 +398,15 @@
     near_sent, far_sent = add(near_2, [near_came[part:]]), add(far_1, [far_came[part:]])
     near_last, far_last = cuts(near_sent, mask=2), cuts(far_sent, mask=1)
     x_3 = [after(rows, (gy_a, near_sent, far_sent)) for rows in x_3]
-    *text_parts, dq_a = call(
+    text_0, text_2, text_sent, dq_a = call(
         last_kernel,
-        [((part, width), BF16)] * QUAD + [wide_b],
+        [part_b, part_b, parts_b, wide_b],
         [wide, tall, tall, wide_b, ((rows_out, width), F32), block_w, corner, corner]
         + [block_dots, corner_dots, corner_dots],
         (*x_3, y_a, y_2, y_3, q_a, q_2, q_3, gy_a, gy_2, gy_3, pick_a, pick_b),
         16,
     )
-    text_others = [cuts(text_parts[k], mask=k) for k in range(1, QUAD)]
+    text_came = cuts(text_sent, mask=1)
     far_sum = add(far_0, [far_came[:part], after(far_last, dq_a)])
     near_sum = add(near_0, [near_came[:part], after(near_last, dq_a)])
     image_sum = add(near_sum, [loop(far_sum, mask=2)])
@@ -409,8 +414,12 @@
         call(grad_kernel, [tall], [], (after(back, image_sum), head), 4, macs=2 * macs, keep=False)[0]
         for back, head in ((dp_a, image_head), (dq_a, text_head))
     ]
-    text_sum = add(text_parts[0], [after(other, (image_sum, grads)) for other in text_others])
-    image_sum = add(image_sum, [cuts(image_sum, mask=QUAD)])
+    text_came = after(text_came, (image_sum, grads))
+    text_last = cuts(add(text_2, [text_came[part:]]), mask=2)
+    text_sum = add(text_0, [text_came[:part], text_last])
+    image_sum = call(
+        add_kernel, [part_b], [], (image_sum, cuts(image_sum, mask=QUAD)), 4, macs=4 * macs
+    )[0]
     image_pieces = spread(image_sum)
     text_sum = add(text_sum, [after(cuts(text_sum, mask=QUAD), image_pieces[1])])
     image_out, text_out = (

time: 79.1 us -> 81.1 us (1.025)
  waiting for transfers between devices: 13.1 us -> 17.1 us
  starting transfers between devices: 30.6 us -> 28.9 us
  local copies, waits for them, and re-layouts: 2.02 us -> 1.15 us
    ppermute x27 -> x26, waiting for transfers between devices: 13.1 us -> 17.1 us  [swap(): return lax.ppermute(array, axis, [(i, i ^ mask) for i in range(size)])]
    slice x2 -> x0, local copies, waits for them, and re-layouts: 1.97 us -> none  [the longest x1 0.98 us: per_device(): t2 = loop(text_features[:half // 2], mask=2)]
    ppermute x27 -> x26, starting transfers between devices: 30.6 us -> 28.9 us  [swap(): return lax.ppermute(array, axis, [(i, i ^ mask) for i in range(size)])]
    split x0 -> x1, local copies, waits for them, and re-layouts: none -> 1.1 us  [per_device(): t2 = [loop(rows, mask=2) for rows in jnp.split(text_features, 2)]]
    pallas_call x11 -> x12, Pallas kernels: 31.9 us -> 32.5 us  [call(): pl.pallas_call(kernel, out_shape=[shape(s, t) for s, t in outs], in_specs...]
  transfers between devices with their start and end apart: 27 -> 26, of which waited for: 9 -> 12; matrix products, arithmetic and copies ran while one was open for 3% -> 2% of each run, Pallas kernels for 38% -> 38%
where the time goes in v13:
time: 81.1 us; the launch traced here: 80.9 us
  Pallas kernels  32.5 us (40%)
  starting transfers between devices  28.9 us (36%)
  waiting for transfers between devices  17.1 us (21%)
  local copies, waits for them, and re-layouts  1.15 us (1%)
    pallas_call x12, Pallas kernels, call(): pl.pallas_call(kernel, out_shape=[shape(s, t) for s, t in outs], in_specs...  32.5 us
    ppermute x26, starting transfers between devices, swap(): return lax.ppermute(array, axis, [(i, i ^ mask) for i in range(size)])  28.9 us
    ppermute x26, waiting for transfers between devices, swap(): return lax.ppermute(array, axis, [(i, i ^ mask) for i in range(size)])  17.1 us
  transfers between devices with their start and end apart: 26, of which 12 were waited for; matrix products, arithmetic and copies ran while one was open for 2% of the time, Pallas kernels for 38%

profile of v13, /device:TPU:0, one launch (start us, length us, event | category | flops | bytes accessed | tf_op | source)
XLA Modules:
  0.0 80.9 jit_solution(14547778671816497681)
XLA Ops:
  1.2 1.1 %fusion = (bf16[128,1152]{1,0:T(8,128)(2,1)S(1)}, bf16[128,1152]{1,0:T(8,128)(2,1)S(1)}) fusion(bf16[256,1152]{1,0:T(8,128)(2,1)} %t0_far), kind=kLoop, calls=%fused_computation.9 | loop fusion | bytes 1179648 | tf_op jit(solution)/shard_map/split | solution.py:333
  2.3 3.0 %collective-permute-start.1 = (bf16[128,1152]{1,0:T(8,128)(2,1)S(1)}, bf16[128,1152]{1,0:T(8,128)(2,1)S(1)}, u32[]{:S(2)}, u32[]{:S(2)}) collective-permute-start(bf16[128,1152]{1,0:T(8,128)(2,1)S(1)} %get-tuple-element.122), channel_id=1, source_target_pairs={{0,2},{1,3},{2,0},{3,1},{4,6},{5,7},{6,4},{7,5},{8,10},{9,11},{10,... | collective-permute-start | bytes 884744 | tf_op jit(solution)/shard_map/ppermute | solution.py:307
  5.4 7.7 %shard_map.75 = (f32[512,1152]{1,0:T(8,128)S(1)}, bf16[512,1152]{1,0:T(8,128)(2,1)S(1)}, f32[512,1152]{1,0:T(8,128)S(1)}, bf16[512,1152]{1,0:T(8,128)(2,1)S(1)},...) custom-call(bf16[256,1152]{1,0:T(8,128)(2,1)S(1)} %collective-permut, ...), custom_call_target="tpu_custom_call" | custom-call | tf_op jit(solution)/shard_map/pallas_call | solution.py:294
  13.8 2.0 %collective-permute-start.9 = (bf16[256,1152]{1,0:T(8,128)(2,1)S(1)}, bf16[256,1152]{1,0:T(8,128)(2,1)S(1)}, u32[]{:S(2)}, u32[]{:S(2)}) collective-permute-start(bf16[256,1152]{1,0:T(8,128)(2,1)S(1)} %copy-done), channel_id=1, source_target_pairs={{0,2},{1,3},{2,0},{3,1},{4,6},{5,7},{6,4},{7,5},{8,10},{9,11},{10,... | collective-permute-start | bytes 1769480 | tf_op jit(solution)/shard_map/ppermute | solution.py:307
  15.8 3.3 %shard_map.76 = (f32[256,1152]{1,0:T(8,128)S(1)}, bf16[256,1152]{1,0:T(8,128)(2,1)S(1)}, bf16[512,256]{1,0:T(8,128)(2,1)S(1)}, f32[512,1152]{1,0:T(8,128)S(1)}, bf16[576,512]{1,0:T(8,128)(2,1)S(1)}) custom-call(s32[2]{0:T(128)S(1)} %pad_add_fusion.place, bf16[128,1152]{1,0:T(8,128)(2,1)S(1)} %collective-permute-done.1.refs_0_, ...), custom_call_target="tpu_custom_call" | custom-call | tf_op jit(solution)/shard_map/pallas_call | solution.py:294
  20.1 0.9 %collective-permute-done.7.refs_2_.refs_5_ = bf16[64,1152]{1,0:T(8,128)(2,1)S(1)} collective-permute-done((bf16[64,1152]{1,0:T(8,128)(2,1)S(1)}, bf16[64,1152]{1,0:T(8,128)(2,1)S(1)}, u32[]{:S(2)}, u32[]{:S(2)}) %collective-permute-start.7) | collective-permute-done | bytes 147488 | tf_op jit(solution)/shard_map/ppermute | solution.py:307
  21.1 4.1 %shard_map.77 = (f32[256,1152]{1,0:T(8,128)S(1)}, bf16[256,1152]{1,0:T(8,128)(2,1)S(1)}, bf16[512,256]{1,0:T(8,128)(2,1)S(1)}, bf16[512,1152]{1,0:T(8,128)(2,1)S...) custom-call(bf16[128,1152]{1,0:T(8,128)(2,1)S(1)} %collective-permut, ...), custom_call_target="tpu_custom_call" | custom-call | tf_op jit(solution)/shard_map/pallas_call | solution.py:294
  25.2 2.2 %collective-permute-start.12 = (bf16[144,1152]{1,0:T(8,128)(2,1)S(1)}, bf16[144,1152]{1,0:T(8,128)(2,1)S(1)}, u32[]{:S(2)}, u32[]{:S(2)}) collective-permute-start(bf16[144,1152]{1,0:T(8,128)(2,1)S(1)} %get-tuple-element.100), channel_id=1, source_target_pairs={{0,8},{4,12},{8,0},{12,4},{16,24},{20,28},{24,16},{28,20},{1,9},{5... | collective-permute-start | bytes 995336 | tf_op jit(solution)/shard_map/ppermute | solution.py:307
  27.4 1.5 %collective-permute-start.8 = (bf16[144,1152]{1,0:T(8,128)(2,1)S(1)}, bf16[144,1152]{1,0:T(8,128)(2,1)S(1)}, u32[]{:S(2)}, u32[]{:S(2)}) collective-permute-start(bf16[144,1152]{1,0:T(8,128)(2,1)S(1)} %get-tuple-element.78), channel_id=1, source_target_pairs={{0,4},{4,0},{8,12},{12,8},{16,20},{20,16},{24,28},{28,24},{1,5},{5... | collective-permute-start | bytes 995336 | tf_op jit(solution)/shard_map/ppermute | solution.py:307
  28.9 3.1 %shard_map.78 = (f32[512,1152]{1,0:T(8,128)S(1)}, f32[256,1152]{1,0:T(8,128)S(1)}, f32[256,1152]{1,0:T(8,128)S(1)}, bf16[288,512]{1,0:T(8,128)(2,1)S(1)}, bf16[288,512]{1,0:T(8,128)(2,1)S(1)}) custom-call(s32[2]{0:T(128)S(1)} %pad_add_fusion.place, bf16[128,1152]{1,0:T(8,128)(2,1)S(1)} %collective-permute-done.1.refs_0_, ...), custom_call_target="tpu_custom_call" | custom-call | tf_op jit(solution)/shard_map/pallas_call | solution.py:294
  32.0 2.0 %shard_map.79 = (bf16[128,1152]{1,0:T(8,128)(2,1)S(1)}, bf16[128,1152]{1,0:T(8,128)(2,1)S(1)}, bf16[256,512]{1,0:T(8,128)(2,1)S(1)}, bf16[256,256]{1,0:T(8,128)(2,1)S(1)}, bf16[256,256]{1,0:T(8,128)(2,1)S(1)}) custom-call(bf16[256,1152]{1,0:T(8,128)(2,1)S(1)} %collective-permute-done.9.i2, bf16[1152,1152]{1,0:T(8,128)(2,1)S(1)} %get-tuple-element.85.image_head.head, ...), custom_call_target="tpu_custom_call" | custom-call | tf_op jit(solution)/shard_map/pallas_call | solution.py:294
  34.6 0.9 %shard_map.80 = (f32[512,1152]{1,0:T(8,128)S(1)}, f32[256,1152]{1,0:T(8,128)S(1)}, f32[256,1152]{1,0:T(8,128)S(1)}) custom-call(bf16[128,1152]{1,0:T(8,128)(2,1)S(1)} %get-tuple-element.89.x_first, bf16[128,1152]{1,0:T(8,128)(2,1)S(1)} %get-tuple-element.90.x_second, bf16[256,512]{1,0:T(8,128)(2,1)S(1)} %get-tuple-element.91.w_a, ...), custom_call_target="tpu_custom_call" | custom-call | tf_op jit(solution)/shard_map/pallas_call | solution.py:294
  35.7 1.5 %collective-permute-done.8 = bf16[144,1152]{1,0:T(8,128)(2,1)S(1)} collective-permute-done((bf16[144,1152]{1,0:T(8,128)(2,1)S(1)}, bf16[144,1152]{1,0:T(8,128)(2,1)S(1)}, u32[]{:S(2)}, u32[]{:S(2)}) %collective-permute-start.8) | collective-permute-done | bytes 331808 | tf_op jit(solution)/shard_map/ppermute | solution.py:307
  37.2 1.6 %collective-permute-start.14 = (bf16[72,1152]{1,0:T(8,128)(2,1)S(1)}, bf16[72,1152]{1,0:T(8,128)(2,1)S(1)}, u32[]{:S(2)}, u32[]{:S(2)}) collective-permute-start(bf16[72,1152]{1,0:T(8,128)(2,1)S(1)} %add_convert_fusion.6), channel_id=1, source_target_pairs={{0,4},{4,0},{8,12},{12,8},{16,20},{20,16},{24,28},{28,24},{1,5},{5... | collective-permute-start | bytes 497672 | tf_op jit(solution)/shard_map/ppermute | solution.py:307
  39.4 3.9 %shard_map.81 = (bf16[72,1152]{1,0:T(8,128)(2,1)S(1)}, bf16[72,1152]{1,0:T(8,128)(2,1)S(1)}, bf16[144,1152]{1,0:T(8,128)(2,1)S(1)}, bf16[512,1152]{1,0:T(8,128)(2,1)S(1)}) custom-call(bf16[128,1152]{1,0:T(8,128)(2,1)S(1)} %collective-permute-done.11.x_first, bf16[128,1152]{1,0:T(8,128)(2,1)S(1)} %collective-permute-done.13.x_second, ...), custom_call_target="tpu_custom_call" | custom-call | tf_op jit(solution)/shard_map/pallas_call | solution.py:294
  43.4 1.6 %collective-permute-start.15 = (bf16[72,1152]{1,0:T(8,128)(2,1)S(1)}, bf16[72,1152]{1,0:T(8,128)(2,1)S(1)}, u32[]{:S(2)}, u32[]{:S(2)}) collective-permute-start(bf16[72,1152]{1,0:T(8,128)(2,1)S(1)} %add_convert_fusion.4), channel_id=1, source_target_pairs={{0,2},{1,3},{2,0},{3,1},{4,6},{5,7},{6,4},{7,5},{8,10},{9,11},{10,... | collective-permute-start | bytes 497672 | tf_op jit(solution)/shard_map/ppermute | solution.py:307
  44.9 0.8 %collective-permute-start.20 = (bf16[144,1152]{1,0:T(8,128)(2,1)S(1)}, bf16[144,1152]{1,0:T(8,128)(2,1)S(1)}, u32[]{:S(2)}, u32[]{:S(2)}) collective-permute-start(bf16[144,1152]{1,0:T(8,128)(2,1)S(1)} %get-tuple-element.118), channel_id=1, source_target_pairs={{0,4},{4,0},{8,12},{12,8},{16,20},{20,16},{24,28},{28,24},{1,5},{5... | collective-permute-start | bytes 995336 | tf_op jit(solution)/shard_map/ppermute | solution.py:307
  45.8 3.0 %collective-permute-done.15 = bf16[72,1152]{1,0:T(8,128)(2,1)S(1)} collective-permute-done((bf16[72,1152]{1,0:T(8,128)(2,1)S(1)}, bf16[72,1152]{1,0:T(8,128)(2,1)S(1)}, u32[]{:S(2)}, u32[]{:S(2)}) %collective-permute-start.15) | collective-permute-done | bytes 165920 | tf_op jit(solution)/shard_map/ppermute | solution.py:307
  48.9 2.7 %collective-permute-start.16 = (bf16[72,1152]{1,0:T(8,128)(2,1)S(1)}, bf16[72,1152]{1,0:T(8,128)(2,1)S(1)}, u32[]{:S(2)}, u32[]{:S(2)}) collective-permute-start(bf16[72,1152]{1,0:T(8,128)(2,1)S(1)} %add_convert_fusion.3.left), channel_id=1, source_target_pairs={{0,16},{4,20},{8,24},{12,28},{16,0},{20,4},{24,8},{28,12},{1,17},{... | collective-permute-start | bytes 497672 | tf_op jit(solution)/shard_map/ppermute | solution.py:307
  51.5 2.0 %shard_map.83 = f32[256,1152]{1,0:T(8,128)} custom-call(bf16[512,1152]{1,0:T(8,128)(2,1)S(1)} %get-tuple-element.116.back, bf16[1152,1152]{1,0:T(8,128)(2,1)S(1)} %get-tuple-element.69.refs_5_.refs_3_.head), custom_call_target="tpu_custom_call" | custom-call | flops 1358954496 | tf_op jit(solution)/shard_map/pallas_call | solution.py:294
  53.6 2.1 %shard_map.82 = f32[256,1152]{1,0:T(8,128)} custom-call(bf16[512,1152]{1,0:T(8,128)(2,1)S(1)} %get-tuple-element.115.back, bf16[1152,1152]{1,0:T(8,128)(2,1)S(1)} %get-tuple-element.85.image_head.head), custom_call_target="tpu_custom_call" | custom-call | flops 1358954496 | tf_op jit(solution)/shard_map/pallas_call | solution.py:294
  55.7 1.6 %collective-permute-start.21 = (bf16[72,1152]{1,0:T(8,128)(2,1)S(1)}, bf16[72,1152]{1,0:T(8,128)(2,1)S(1)}, u32[]{:S(2)}, u32[]{:S(2)}) collective-permute-start(bf16[72,1152]{1,0:T(8,128)(2,1)S(1)} %add_convert_fusion.2), channel_id=1, source_target_pairs={{0,8},{4,12},{8,0},{12,4},{16,24},{20,28},{24,16},{28,20},{1,9},{5... | collective-permute-start | bytes 497672 | tf_op jit(solution)/shard_map/ppermute | solution.py:307
  58.0 3.7 %collective-permute-done.21 = bf16[72,1152]{1,0:T(8,128)(2,1)S(1)} collective-permute-done((bf16[72,1152]{1,0:T(8,128)(2,1)S(1)}, bf16[72,1152]{1,0:T(8,128)(2,1)S(1)}, u32[]{:S(2)}, u32[]{:S(2)}) %collective-permute-start.21) | collective-permute-done | bytes 165920 | tf_op jit(solution)/shard_map/ppermute | solution.py:307
  61.9 2.4 %collective-permute-start.19 = (bf16[72,1152]{1,0:T(8,128)(2,1)S(1)}, bf16[72,1152]{1,0:T(8,128)(2,1)S(1)}, u32[]{:S(2)}, u32[]{:S(2)}) collective-permute-start(bf16[72,1152]{1,0:T(8,128)(2,1)S(1)} %shard_map.84.refs_0_), channel_id=1, source_target_pairs={{0,12},{4,8},{8,4},{12,0},{16,28},{20,24},{24,20},{28,16},{1,13},{... | collective-permute-start | bytes 497672 | tf_op jit(solution)/shard_map/ppermute | solution.py:307
  64.5 3.7 %collective-permute-done.22 = bf16[72,1152]{1,0:T(8,128)(2,1)S(1)} collective-permute-done((bf16[72,1152]{1,0:T(8,128)(2,1)S(1)}, bf16[72,1152]{1,0:T(8,128)(2,1)S(1)}, u32[]{:S(2)}, u32[]{:S(2)}) %collective-permute-start.22) | collective-permute-done | bytes 165920 | tf_op jit(solution)/shard_map/ppermute | solution.py:307
  68.2 4.0 %collective-permute-start.25 = (bf16[72,1152]{1,0:T(8,128)(2,1)S(1)}, bf16[72,1152]{1,0:T(8,128)(2,1)S(1)}, u32[]{:S(2)}, u32[]{:S(2)}) collective-permute-start(bf16[72,1152]{1,0:T(8,128)(2,1)S(1)} %add_convert_fusion.refs_0_), channel_id=1, source_target_pairs={{0,12},{4,8},{8,4},{12,0},{16,28},{20,24},{24,20},{28,16},{1,13},{... | collective-permute-start | bytes 497672 | tf_op jit(solution)/shard_map/ppermute | solution.py:307
  72.5 1.4 %collective-permute-start.23 = (bf16[72,1152]{1,0:T(8,128)(2,1)S(1)}, bf16[72,1152]{1,0:T(8,128)(2,1)S(1)}, u32[]{:S(2)}, u32[]{:S(2)}) collective-permute-start(bf16[72,1152]{1,0:T(8,128)(2,1)S(1)} %add_convert_fusion.refs_0_), channel_id=1, source_target_pairs={{0,4},{4,0},{8,12},{12,8},{16,20},{20,16},{24,28},{28,24},{1,5},{5... | collective-permute-start | bytes 497672 | tf_op jit(solution)/shard_map/ppermute | solution.py:307
  73.9 1.0 %collective-permute-done.18.refs_2_ = bf16[72,1152]{1,0:T(8,128)(2,1)S(1)} collective-permute-done((bf16[72,1152]{1,0:T(8,128)(2,1)S(1)}, bf16[72,1152]{1,0:T(8,128)(2,1)S(1)}, u32[]{:S(2)}, u32[]{:S(2)}) %collective-permute-start.18) | collective-permute-done | bytes 165920 | tf_op jit(solution)/shard_map/ppermute | solution.py:307
  75.0 1.7 %shard_map.85 = f32[288,1152]{1,0:T(8,128)} custom-call(s32[2]{0:T(128)S(1)} %pad_add_fusion.place, bf16[72,1152]{1,0:T(8,128)(2,1)S(1)} %shard_map.84.refs_0_, bf16[72,1152]{1,0:T(8,128)(2,1)S(1)} %collective-permute-done.17.refs_1_, bf16[72,1152]{1,0:T(8,128)(2,1)S(1)} %collective-permute-done.18.refs_2_, bf16[72,1152]{1,0:T(8,128)(2,1)S(1)} %collective-permute-done.19.refs_3_), custom_call_target="tpu_custom_call" | custom-call | tf_op jit(solution)/shard_map/pallas_call | solution.py:294
  76.6 1.3 %collective-permute-done.25.refs_3_ = bf16[72,1152]{1,0:T(8,128)(2,1)S(1)} collective-permute-done((bf16[72,1152]{1,0:T(8,128)(2,1)S(1)}, bf16[72,1152]{1,0:T(8,128)(2,1)S(1)}, u32[]{:S(2)}, u32[]{:S(2)}) %collective-permute-start.25) | collective-permute-done | bytes 165920 | tf_op jit(solution)/shard_map/ppermute | solution.py:307
  77.9 1.0 %collective-permute-done.24.refs_2_ = bf16[72,1152]{1,0:T(8,128)(2,1)S(1)} collective-permute-done((bf16[72,1152]{1,0:T(8,128)(2,1)S(1)}, bf16[72,1152]{1,0:T(8,128)(2,1)S(1)}, u32[]{:S(2)}, u32[]{:S(2)}) %collective-permute-start.24) | collective-permute-done | bytes 165920 | tf_op jit(solution)/shard_map/ppermute | solution.py:307
  79.2 1.7 %shard_map.86 = f32[288,1152]{1,0:T(8,128)} custom-call(s32[2]{0:T(128)S(1)} %pad_add_fusion.place, bf16[72,1152]{1,0:T(8,128)(2,1)S(1)} %add_convert_fusion.refs_0_, bf16[72,1152]{1,0:T(8,128)(2,1)S(1)} %collective-permute-done.23.refs_1_, bf16[72,1152]{1,0:T(8,128)(2,1)S(1)} %collective-permute-done.24.refs_2_, ...), custom_call_target="tpu_custom_call" | custom-call | tf_op jit(solution)/shard_map/pallas_call | solution.py:294
  (45 shorter events, 5.8 us)
Async XLA Ops:
  0.7 4.7 %collective-permute-start.2 = (bf16[256,1152]{1,0:T(8,128)(2,1)}, bf16[256,1152]{1,0:T(8,128)(2,1)S(1)}, u32[]{:S(2)}, u32[]{:S(2)}) collective-permute-start(bf16[256,1152]{1,0:T(8,128)(2,1)} %t0_far), channel_id=1, source_target_pairs={{0,1},{1,0},{2,3},{3,2},{4,5},{5,4},{6,7},{7,6},{8,9},{9,8},{10,11... | collective-permute-start | bytes 1769480 | tf_op jit(solution)/shard_map/ppermute | solution.py:307
  1.2 4.3 %collective-permute-start.3 = (bf16[256,1152]{1,0:T(8,128)(2,1)}, bf16[256,1152]{1,0:T(8,128)(2,1)S(1)}, u32[]{:S(2)}, u32[]{:S(2)}) collective-permute-start(bf16[256,1152]{1,0:T(8,128)(2,1)} %i0_far), channel_id=1, source_target_pairs={{0,1},{1,0},{2,3},{3,2},{4,5},{5,4},{6,7},{7,6},{8,9},{9,8},{10,11... | collective-permute-start | bytes 1769480 | tf_op jit(solution)/shard_map/ppermute | solution.py:307
  2.3 10.8 %collective-permute-start.1 = (bf16[128,1152]{1,0:T(8,128)(2,1)S(1)}, bf16[128,1152]{1,0:T(8,128)(2,1)S(1)}, u32[]{:S(2)}, u32[]{:S(2)}) collective-permute-start(bf16[128,1152]{1,0:T(8,128)(2,1)S(1)} %get-tuple-element.122), channel_id=1, source_target_pairs={{0,2},{1,3},{2,0},{3,1},{4,6},{5,7},{6,4},{7,5},{8,10},{9,11},{10,... | collective-permute-start | bytes 884744 | tf_op jit(solution)/shard_map/ppermute | solution.py:307
  5.3 8.4 %copy-start = (bf16[256,1152]{1,0:T(8,128)(2,1)S(1)}, bf16[256,1152]{1,0:T(8,128)(2,1)}, u32[]{:S(2)}) copy-start(bf16[256,1152]{1,0:T(8,128)(2,1)} %i0_far) | copy-start | bytes 1769476
  5.3 14.1 %collective-permute-start = (bf16[128,1152]{1,0:T(8,128)(2,1)S(1)}, bf16[128,1152]{1,0:T(8,128)(2,1)S(1)}, u32[]{:S(2)}, u32[]{:S(2)}) collective-permute-start(bf16[128,1152]{1,0:T(8,128)(2,1)S(1)} %get-tuple-element.123), channel_id=1, source_target_pairs={{0,2},{1,3},{2,0},{3,1},{4,6},{5,7},{6,4},{7,5},{8,10},{9,11},{10,... | collective-permute-start | bytes 884744 | tf_op jit(solution)/shard_map/ppermute | solution.py:307
  13.2 2.6 %collective-permute-start.5 = (bf16[64,1152]{1,0:T(8,128)(2,1)S(1)}, bf16[64,1152]{1,0:T(8,128)(2,1)S(1)}, u32[]{:S(2)}, u32[]{:S(2)}) collective-permute-start(bf16[64,1152]{1,0:T(8,128)(2,1)S(1)} %get-tuple-element.126), channel_id=1, source_target_pairs={{0,1},{1,0},{2,3},{3,2},{4,5},{5,4},{6,7},{7,6},{8,9},{9,8},{10,11... | collective-permute-start | bytes 442376 | tf_op jit(solution)/shard_map/ppermute | solution.py:307
  13.3 2.5 %collective-permute-start.4 = (bf16[64,1152]{1,0:T(8,128)(2,1)S(1)}, bf16[64,1152]{1,0:T(8,128)(2,1)S(1)}, u32[]{:S(2)}, u32[]{:S(2)}) collective-permute-start(bf16[64,1152]{1,0:T(8,128)(2,1)S(1)} %get-tuple-element.127), channel_id=1, source_target_pairs={{0,1},{1,0},{2,3},{3,2},{4,5},{5,4},{6,7},{7,6},{8,9},{9,8},{10,11... | collective-permute-start | bytes 442376 | tf_op jit(solution)/shard_map/ppermute | solution.py:307
  13.8 18.2 %collective-permute-start.9 = (bf16[256,1152]{1,0:T(8,128)(2,1)S(1)}, bf16[256,1152]{1,0:T(8,128)(2,1)S(1)}, u32[]{:S(2)}, u32[]{:S(2)}) collective-permute-start(bf16[256,1152]{1,0:T(8,128)(2,1)S(1)} %copy-done), channel_id=1, source_target_pairs={{0,2},{1,3},{2,0},{3,1},{4,6},{5,7},{6,4},{7,5},{8,10},{9,11},{10,... | collective-permute-start | bytes 1769480 | tf_op jit(solution)/shard_map/ppermute | solution.py:307
  19.5 1.4 %collective-permute-start.7 = (bf16[64,1152]{1,0:T(8,128)(2,1)S(1)}, bf16[64,1152]{1,0:T(8,128)(2,1)S(1)}, u32[]{:S(2)}, u32[]{:S(2)}) collective-permute-start(bf16[64,1152]{1,0:T(8,128)(2,1)S(1)} %get-tuple-element.124), channel_id=1, source_target_pairs={{0,1},{1,0},{2,3},{3,2},{4,5},{5,4},{6,7},{7,6},{8,9},{9,8},{10,11... | collective-permute-start | bytes 442376 | tf_op jit(solution)/shard_map/ppermute | solution.py:307
  19.6 1.6 %collective-permute-start.6 = (bf16[64,1152]{1,0:T(8,128)(2,1)S(1)}, bf16[64,1152]{1,0:T(8,128)(2,1)S(1)}, u32[]{:S(2)}, u32[]{:S(2)}) collective-permute-start(bf16[64,1152]{1,0:T(8,128)(2,1)S(1)} %get-tuple-element.125), channel_id=1, source_target_pairs={{0,1},{1,0},{2,3},{3,2},{4,5},{5,4},{6,7},{7,6},{8,9},{9,8},{10,11... | collective-permute-start | bytes 442376 | tf_op jit(solution)/shard_map/ppermute | solution.py:307
  25.2 10.5 %collective-permute-start.12 = (bf16[144,1152]{1,0:T(8,128)(2,1)S(1)}, bf16[144,1152]{1,0:T(8,128)(2,1)S(1)}, u32[]{:S(2)}, u32[]{:S(2)}) collective-permute-start(bf16[144,1152]{1,0:T(8,128)(2,1)S(1)} %get-tuple-element.100), channel_id=1, source_target_pairs={{0,8},{4,12},{8,0},{12,4},{16,24},{20,28},{24,16},{28,20},{1,9},{5... | collective-permute-start | bytes 995336 | tf_op jit(solution)/shard_map/ppermute | solution.py:307
  27.4 9.7 %collective-permute-start.8 = (bf16[144,1152]{1,0:T(8,128)(2,1)S(1)}, bf16[144,1152]{1,0:T(8,128)(2,1)S(1)}, u32[]{:S(2)}, u32[]{:S(2)}) collective-permute-start(bf16[144,1152]{1,0:T(8,128)(2,1)S(1)} %get-tuple-element.78), channel_id=1, source_target_pairs={{0,4},{4,0},{8,12},{12,8},{16,20},{20,16},{24,28},{28,24},{1,5},{5... | collective-permute-start | bytes 995336 | tf_op jit(solution)/shard_map/ppermute | solution.py:307
  34.0 5.3 %collective-permute-start.11 = (bf16[128,1152]{1,0:T(8,128)(2,1)S(1)}, bf16[128,1152]{1,0:T(8,128)(2,1)S(1)}, u32[]{:S(2)}, u32[]{:S(2)}) collective-permute-start(bf16[128,1152]{1,0:T(8,128)(2,1)S(1)} %get-tuple-element.89.x_first), channel_id=1, source_target_pairs={{0,1},{1,0},{2,3},{3,2},{4,5},{5,4},{6,7},{7,6},{8,9},{9,8},{10,11... | collective-permute-start | bytes 884744 | tf_op jit(solution)/shard_map/ppermute | solution.py:307
  34.1 5.3 %collective-permute-start.13 = (bf16[128,1152]{1,0:T(8,128)(2,1)S(1)}, bf16[128,1152]{1,0:T(8,128)(2,1)S(1)}, u32[]{:S(2)}, u32[]{:S(2)}) collective-permute-start(bf16[128,1152]{1,0:T(8,128)(2,1)S(1)} %get-tuple-element.90.x_second), channel_id=1, source_target_pairs={{0,1},{1,0},{2,3},{3,2},{4,5},{5,4},{6,7},{7,6},{8,9},{9,8},{10,11... | collective-permute-start | bytes 884744 | tf_op jit(solution)/shard_map/ppermute | solution.py:307
  37.2 6.1 %collective-permute-start.14 = (bf16[72,1152]{1,0:T(8,128)(2,1)S(1)}, bf16[72,1152]{1,0:T(8,128)(2,1)S(1)}, u32[]{:S(2)}, u32[]{:S(2)}) collective-permute-start(bf16[72,1152]{1,0:T(8,128)(2,1)S(1)} %add_convert_fusion.6), channel_id=1, source_target_pairs={{0,4},{4,0},{8,12},{12,8},{16,20},{20,16},{24,28},{28,24},{1,5},{5... | collective-permute-start | bytes 497672 | tf_op jit(solution)/shard_map/ppermute | solution.py:307
  38.8 6.9 %collective-permute-start.10 = (bf16[72,1152]{1,0:T(8,128)(2,1)S(1)}, bf16[72,1152]{1,0:T(8,128)(2,1)S(1)}, u32[]{:S(2)}, u32[]{:S(2)}) collective-permute-start(bf16[72,1152]{1,0:T(8,128)(2,1)S(1)} %add_convert_fusion.7), channel_id=1, source_target_pairs={{0,8},{4,12},{8,0},{12,4},{16,24},{20,28},{24,16},{28,20},{1,9},{5... | collective-permute-start | bytes 497672 | tf_op jit(solution)/shard_map/ppermute | solution.py:307
  43.4 5.4 %collective-permute-start.15 = (bf16[72,1152]{1,0:T(8,128)(2,1)S(1)}, bf16[72,1152]{1,0:T(8,128)(2,1)S(1)}, u32[]{:S(2)}, u32[]{:S(2)}) collective-permute-start(bf16[72,1152]{1,0:T(8,128)(2,1)S(1)} %add_convert_fusion.4), channel_id=1, source_target_pairs={{0,2},{1,3},{2,0},{3,1},{4,6},{5,7},{6,4},{7,5},{8,10},{9,11},{10,... | collective-permute-start | bytes 497672 | tf_op jit(solution)/shard_map/ppermute | solution.py:307
  44.9 10.7 %collective-permute-start.20 = (bf16[144,1152]{1,0:T(8,128)(2,1)S(1)}, bf16[144,1152]{1,0:T(8,128)(2,1)S(1)}, u32[]{:S(2)}, u32[]{:S(2)}) collective-permute-start(bf16[144,1152]{1,0:T(8,128)(2,1)S(1)} %get-tuple-element.118), channel_id=1, source_target_pairs={{0,4},{4,0},{8,12},{12,8},{16,20},{20,16},{24,28},{28,24},{1,5},{5... | collective-permute-start | bytes 995336 | tf_op jit(solution)/shard_map/ppermute | solution.py:307
  48.9 8.5 %collective-permute-start.16 = (bf16[72,1152]{1,0:T(8,128)(2,1)S(1)}, bf16[72,1152]{1,0:T(8,128)(2,1)S(1)}, u32[]{:S(2)}, u32[]{:S(2)}) collective-permute-start(bf16[72,1152]{1,0:T(8,128)(2,1)S(1)} %add_convert_fusion.3.left), channel_id=1, source_target_pairs={{0,16},{4,20},{8,24},{12,28},{16,0},{20,4},{24,8},{28,12},{1,17},{... | collective-permute-start | bytes 497672 | tf_op jit(solution)/shard_map/ppermute | solution.py:307
  55.7 6.0 %collective-permute-start.21 = (bf16[72,1152]{1,0:T(8,128)(2,1)S(1)}, bf16[72,1152]{1,0:T(8,128)(2,1)S(1)}, u32[]{:S(2)}, u32[]{:S(2)}) collective-permute-start(bf16[72,1152]{1,0:T(8,128)(2,1)S(1)} %add_convert_fusion.2), channel_id=1, source_target_pairs={{0,8},{4,12},{8,0},{12,4},{16,24},{20,28},{24,16},{28,20},{1,9},{5... | collective-permute-start | bytes 497672 | tf_op jit(solution)/shard_map/ppermute | solution.py:307
  57.4 7.2 %collective-permute-start.17 = (bf16[72,1152]{1,0:T(8,128)(2,1)S(1)}, bf16[72,1152]{1,0:T(8,128)(2,1)S(1)}, u32[]{:S(2)}, u32[]{:S(2)}) collective-permute-start(bf16[72,1152]{1,0:T(8,128)(2,1)S(1)} %shard_map.84.refs_0_), channel_id=1, source_target_pairs={{0,4},{4,0},{8,12},{12,8},{16,20},{20,16},{24,28},{28,24},{1,5},{5... | collective-permute-start | bytes 497672 | tf_op jit(solution)/shard_map/ppermute | solution.py:307
  61.8 6.4 %collective-permute-start.22 = (bf16[72,1152]{1,0:T(8,128)(2,1)S(1)}, bf16[72,1152]{1,0:T(8,128)(2,1)S(1)}, u32[]{:S(2)}, u32[]{:S(2)}) collective-permute-start(bf16[72,1152]{1,0:T(8,128)(2,1)S(1)} %add_convert_fusion.1), channel_id=1, source_target_pairs={{0,16},{4,20},{8,24},{12,28},{16,0},{20,4},{24,8},{28,12},{1,17},{... | collective-permute-start | bytes 497672 | tf_op jit(solution)/shard_map/ppermute | solution.py:307
  61.9 12.1 %collective-permute-start.19 = (bf16[72,1152]{1,0:T(8,128)(2,1)S(1)}, bf16[72,1152]{1,0:T(8,128)(2,1)S(1)}, u32[]{:S(2)}, u32[]{:S(2)}) collective-permute-start(bf16[72,1152]{1,0:T(8,128)(2,1)S(1)} %shard_map.84.refs_0_), channel_id=1, source_target_pairs={{0,12},{4,8},{8,4},{12,0},{16,28},{20,24},{24,20},{28,16},{1,13},{... | collective-permute-start | bytes 497672 | tf_op jit(solution)/shard_map/ppermute | solution.py:307
  64.3 10.7 %collective-permute-start.18 = (bf16[72,1152]{1,0:T(8,128)(2,1)S(1)}, bf16[72,1152]{1,0:T(8,128)(2,1)S(1)}, u32[]{:S(2)}, u32[]{:S(2)}) collective-permute-start(bf16[72,1152]{1,0:T(8,128)(2,1)S(1)} %shard_map.84.refs_0_), channel_id=1, source_target_pairs={{0,8},{4,12},{8,0},{12,4},{16,24},{20,28},{24,16},{28,20},{1,9},{5... | collective-permute-start | bytes 497672 | tf_op jit(solution)/shard_map/ppermute | solution.py:307
  68.2 9.7 %collective-permute-start.25 = (bf16[72,1152]{1,0:T(8,128)(2,1)S(1)}, bf16[72,1152]{1,0:T(8,128)(2,1)S(1)}, u32[]{:S(2)}, u32[]{:S(2)}) collective-permute-start(bf16[72,1152]{1,0:T(8,128)(2,1)S(1)} %add_convert_fusion.refs_0_), channel_id=1, source_target_pairs={{0,12},{4,8},{8,4},{12,0},{16,28},{20,24},{24,20},{28,16},{1,13},{... | collective-permute-start | bytes 497672 | tf_op jit(solution)/shard_map/ppermute | solution.py:307
  72.3 6.6 %collective-permute-start.24 = (bf16[72,1152]{1,0:T(8,128)(2,1)S(1)}, bf16[72,1152]{1,0:T(8,128)(2,1)S(1)}, u32[]{:S(2)}, u32[]{:S(2)}) collective-permute-start(bf16[72,1152]{1,0:T(8,128)(2,1)S(1)} %add_convert_fusion.refs_0_), channel_id=1, source_target_pairs={{0,8},{4,12},{8,0},{12,4},{16,24},{20,28},{24,16},{28,20},{1,9},{5... | collective-permute-start | bytes 497672 | tf_op jit(solution)/shard_map/ppermute | solution.py:307
  72.5 6.7 %collective-permute-start.23 = (bf16[72,1152]{1,0:T(8,128)(2,1)S(1)}, bf16[72,1152]{1,0:T(8,128)(2,1)S(1)}, u32[]{:S(2)}, u32[]{:S(2)}) collective-permute-start(bf16[72,1152]{1,0:T(8,128)(2,1)S(1)} %add_convert_fusion.refs_0_), channel_id=1, source_target_pairs={{0,4},{4,0},{8,12},{12,8},{16,20},{20,16},{24,28},{28,24},{1,5},{5... | collective-permute-start | bytes 497672 | tf_op jit(solution)/shard_map/ppermute | solution.py:307

commit v14 on v12

--- a/solution.py
+++ b/solution.py
@@ -86,26 +86,26 @@
         vectors_ref[rows, :] = (projected_ref[rows, :] * factor).astype(BF16)
 
 
-def back_rows(projected_ref, gradient_ref, back_ref, at=0):
+def back_rows(projected_ref, gradient_ref, back_ref):
     for first in range(0, projected_ref.shape[0], STRIP):
         rows = slice(first, first + STRIP)
         factor = factor_of(projected_ref, rows)
         along = jnp.sum(projected_ref[rows, :] * gradient_ref[rows, :], axis=-1, keepdims=True)
         along = factor * factor * factor * along
         back = factor * gradient_ref[rows, :] - along * projected_ref[rows, :]
-        back_ref[at + first : at + first + STRIP, :] = back.astype(BF16)
-
-
-def weight_rows(dots_ref, weights_ref, pairs_from=None, begin=0, end=None):
+        back_ref[rows, :] = back.astype(BF16)
+
+
+def weight_rows(dots_ref, weights_ref, pairs_from=None):
     half_scale = 0.5 * SCORE_SCALE
-    for first in range(begin, dots_ref.shape[0] if end is None else end, STRIP):
+    for first in range(0, dots_ref.shape[0], STRIP):
         rows = slice(first, first + STRIP)
         score = jnp.tanh(half_scale * dots_ref[rows, :] + 0.5 * SCORE_BIAS)
         weights = half_scale + half_scale * score
         if pairs_from is None:
             weights_ref[rows, :] = weights.astype(BF16)
             continue
-        pair = pairs_from + first - begin
+        pair = pairs_from + first
         left = pair // LANES * LANES
         right = min(left + LANES, weights.shape[1])
         shape = (STRIP, right - left)
@@ -143,6 +143,7 @@
     t1, i1, t0_far, i0_far, text_head_far, image_head_far,
     q_a, y_a, p_a, x_a, w_aa, gx, t0, i0, text_head, image_head, dots, sems,
 ):
+    half = t0.shape[0]
     copies = [
         pltpu.make_async_copy(source, target, sems.at[n])
         for n, (source, target) in enumerate(
@@ -153,11 +154,13 @@
         copy.start()
     copies[0].wait()
     copies[1].wait()
-    q_a[...] = dot_nn(rows_of((t0, t1)), text_head[...])
+    q_a[:half, :] = dot_nn(t0[...], text_head[...])
+    q_a[half:, :] = dot_nn(t1[...], text_head[...])
     copies[2].wait()
     copies[3].wait()
-    p_a[...] = dot_nn(rows_of((i0, i1)), image_head[...])
+    p_a[:half, :] = dot_nn(i0[...], image_head[...])
     unit_rows(q_a, y_a)
+    p_a[half:, :] = dot_nn(i1[...], image_head[...])
     unit_rows(p_a, x_a)
     dots[...] = dot_nt(x_a[...], y_a[...])
     weight_rows(dots, w_aa, 0)
@@ -168,29 +171,26 @@
     return jnp.concatenate([ref[...] for ref in refs], axis=0)
 
 
-def text_kernel(place, *refs):
-    *features, i0, i1, text_head, gx_in, x_a, w_aa = refs[:-7]
-    q_2, y_2, w_a2, gx, gy_a, pick_i, dots = refs[-7:]
-    half, width = i0.shape
-    q_2[...] = dot_nn(rows_of(features), text_head[...])
-    pick = picker(place, pick_i.shape[0] // 2, width, (0, 2))
-    unit_rows(q_2, y_2)
-    dots[...] = dot_nt(x_a[...], y_2[...])
+def near_pull_kernel(place, t0, t1, i0, i1, x_a, w_aa, gy_a, pick_i, pick_t):
+    half, width = t0.shape
+    rows = pick_t.shape[0]
+    pick = picker(place, rows, width, (0, 2))
     pick_i[:, :half] = dot_nt(pick, i0[...]).astype(BF16)
     pick_i[:, half:] = dot_nt(pick, i1[...]).astype(BF16)
-    weight_rows(dots, w_a2)
-    gx[...] = gx_in[...] + dot_nn(w_a2[...], y_2[...])
+    pick = picker(place, rows, width, (0,))
+    pick_t[:, :half] = dot_nt(pick, t0[...]).astype(BF16)
+    pick_t[:, half:] = dot_nt(pick, t1[...]).astype(BF16)
     gy_a[...] = dot_tn(w_aa[...], x_a[...])
 
 
 def image_kernel(*refs):
-    *features, text_head, p_a, x_a, gx_in, pick_i, q_3, y_3, w_a3, dp_a = refs[:-8]
+    *features, text_head, p_a, x_a, gx_in, pick_i, q_b, y_b, w_ab, dp_a = refs[:-8]
     near_0, near_2, near_sent, far_0, far_1, far_sent, dots, gx = refs[-8:]
-    q_3[...] = dot_nn(rows_of(features), text_head[...])
-    unit_rows(q_3, y_3)
-    dots[...] = dot_nt(x_a[...], y_3[...])
-    weight_rows(dots, w_a3)
-    gx[...] = gx_in[...] + dot_nn(w_a3[...], y_3[...])
+    q_b[...] = dot_nn(rows_of(features), text_head[...])
+    unit_rows(q_b, y_b)
+    dots[...] = dot_nt(x_a[...], y_b[...])
+    weight_rows(dots, w_ab)
+    gx[...] = gx_in[...] + dot_nn(w_ab[...], y_b[...])
     back_rows(p_a, gx, dp_a)
     head = dot_nn(pick_i[...], dp_a[...]).astype(BF16)
     part = near_0.shape[0]
@@ -209,59 +209,45 @@
 
 
 def text_pull_kernel(place, *refs):
-    *features, t0, t1, x_a, w_a2, w_a3, gy_2, gy_3, pick_a, pick_b = refs
-    half = t0.shape[0]
-    gy_2[...] = dot_tn(w_a2[...], x_a[...])
-    gy_3[...] = dot_tn(w_a3[...], x_a[...])
-    pick = picker(place, pick_a.shape[0], t0.shape[1], (0,))
-    pick_a[:, :half] = dot_nt(pick, t0[...]).astype(BF16)
-    pick_a[:, half:] = dot_nt(pick, t1[...]).astype(BF16)
+    *features, x_a, w_ab, gy_b, pick_b = refs
+    gy_b[...] = dot_tn(w_ab[...], x_a[...])
+    pick = picker(place, pick_b.shape[0], x_a.shape[1], (0,))
     pick_b[...] = dot_nt(pick, rows_of(features)).astype(BF16)
 
 
-def far_weights(core, x, y_a, y_2, y_3, w_a, w_2, w_3, d_a, d_2, d_3):
-    half = x.shape[0]
-    middle = half // 2
+def far_weights(core, x, y_a, y_b, w_a, w_b, d_a, d_b):
     d_a[...] = dot_nt(x, y_a[...])
-    d_2[...] = dot_nt(x, y_2[...])
+    d_b[...] = dot_nt(x, y_b[...])
     weight_rows(d_a, w_a)
-    d_3[...] = dot_nt(x, y_3[...])
-    weight_rows(d_2, w_2, core * middle, 0, middle)
-    weight_rows(d_2, w_2, None, middle, half)
-    weight_rows(d_3, w_3, None, 0, middle)
-    weight_rows(d_3, w_3, core * middle, middle, half)
-
-
-def block_kernel(i2, image_head, y_a, y_2, y_3, x_first, x_second, w_a, w_2, w_3, p_b, x_b, d_a, d_2, d_3):
+    weight_rows(d_b, w_b, core * x.shape[0])
+
+
+def block_kernel(i2, image_head, y_a, y_b, x_first, x_second, w_a, w_b, p_b, x_b, d_a, d_b):
     middle = x_first.shape[0]
     p_b[...] = dot_nn(i2[...], image_head[...])
     unit_rows(p_b, x_b)
     x_first[...] = x_b[:middle, :]
     x_second[...] = x_b[middle:, :]
-    far_weights(0, x_b[...], y_a, y_2, y_3, w_a, w_2, w_3, d_a, d_2, d_3)
-
-
-def own_pull_kernel(x_first, x_second, w_a, w_2, w_3, gy_a_in, gy_2_in, gy_3_in, gy_a, gy_2, gy_3):
+    far_weights(0, x_b[...], y_a, y_b, w_a, w_b, d_a, d_b)
+
+
+def own_pull_kernel(x_first, x_second, w_a, w_b, gy_a_in, gy_b_in, gy_a, gy_b):
     x = rows_of((x_first, x_second))
     gy_a[...] = gy_a_in[...] + dot_tn(w_a[...], x)
-    gy_2[...] = gy_2_in[...] + dot_tn(w_2[...], x)
-    gy_3[...] = gy_3_in[...] + dot_tn(w_3[...], x)
+    gy_b[...] = gy_b_in[...] + dot_tn(w_b[...], x)
 
 
 def last_kernel(
-    x_first, x_second, y_a, y_2, y_3, q_a, q_2, q_3, gy_a_in, gy_2_in, gy_3_in, pick_a, pick_b,
-    h0, h1, h2, h3, dq_a, gy_a, gy_2, gy_3, dq_b, near_head, w_a, w_2, w_3, d_a, d_2, d_3,
+    x_first, x_second, y_a, y_b, q_a, q_b, gy_a_in, gy_b_in, pick_a, pick_b,
+    h0, h1, h2, h3, dq_a, gy_a, gy_b, dq_b, near_head, w_a, w_b, d_a, d_b,
 ):
-    half = q_2.shape[0]
     x = rows_of((x_first, x_second))
-    far_weights(1, x, y_a, y_2, y_3, w_a, w_2, w_3, d_a, d_2, d_3)
+    far_weights(1, x, y_a, y_b, w_a, w_b, d_a, d_b)
     gy_a[...] = gy_a_in[...] + dot_tn(w_a[...], x)
-    gy_2[...] = gy_2_in[...] + dot_tn(w_2[...], x)
     back_rows(q_a, gy_a, dq_a)
-    gy_3[...] = gy_3_in[...] + dot_tn(w_3[...], x)
+    gy_b[...] = gy_b_in[...] + dot_tn(w_b[...], x)
     near_head[...] = dot_nn(pick_a[...], dq_a[...])
-    back_rows(q_2, gy_2, dq_b, 0)
-    back_rows(q_3, gy_3, dq_b, half)
+    back_rows(q_b, gy_b, dq_b)
     split_head(near_head[...] + dot_nn(pick_b[...], dq_b[...]), (h0, h1, h2, h3))
 
 
@@ -324,19 +310,17 @@
     def spread(total):
         return [total] + [cuts(total, mask=k) for k in range(1, QUAD)]
 
-    t2 = loop(text_features[: half // 2], mask=2)
+    t2 = loop(text_features, mask=2)
     i2 = loop(image_features, mask=2)
     place = jnp.stack([lax.axis_index("loop"), lax.axis_index("cuts") & (QUAD - 1)])
     place = place.astype(jnp.int32)
     t0, i0, place = lax.optimization_barrier((text_features, image_features, place))
-    t2 = [t2, loop(t0[half // 2 :], mask=2)]
     t1 = loop(t0, mask=1)
     i1 = loop(i0, mask=1)
     wide, wide_b = ((near, width), F32), ((near, width), BF16)
     tall, tall_b = ((half, width), F32), ((half, width), BF16)
     head_b = ((width, width), BF16)
     block_w, block_dots = ((half, near), BF16), ((half, near), F32)
-    side_w, side_dots = ((near, half), BF16), ((near, half), F32)
     pick_one, pick_two = ((rows_out, near), BF16), ((2 * rows_out, near), BF16)
     q_a, y_a, p_a, x_a, w_aa, gx, t0, i0, text_head, image_head = call(
         near_kernel,
@@ -346,47 +330,47 @@
         8,
         far=(t0, i0, text_head, image_head),
     )
-    first = both(t2[0], w_aa, 2)
-    q_2, y_2, w_a2, gx, gy_a, pick_i = call(
-        text_kernel,
-        [tall, tall_b, side_w, wide, wide, pick_two],
-        [side_dots],
-        (*first, i0, i1, text_head, gx, x_a, w_aa),
+    gy_a, pick_i, pick_a = call(
+        near_pull_kernel,
+        [wide, pick_two, pick_one],
+        [],
+        (t0, t1, i0, i1, x_a, w_aa),
         8,
         place,
     )
-    second = both(t2[1], gy_a, 2)
+    far_text = both(t2, gy_a, 4)
     part_b, parts_b = ((part, width), BF16), ((2 * part, width), BF16)
-    q_3, y_3, w_a3, dp_a, near_0, near_2, near_sent, far_0, far_1, far_sent = call(
+    square_b, square = ((near, near), BF16), ((near, near), F32)
+    q_b, y_b, w_ab, dp_a, near_0, near_2, near_sent, far_0, far_1, far_sent = call(
         image_kernel,
-        [tall, tall_b, side_w, wide_b] + [part_b, part_b, parts_b] * 2,
-        [side_dots, wide],
-        (*second, text_head, p_a, x_a, gx, pick_i),
+        [wide, wide_b, square_b, wide_b] + [part_b, part_b, parts_b] * 2,
+        [square, wide],
+        (*far_text, text_head, p_a, x_a, gx, pick_i),
         8,
     )
     near_came, far_came = cuts(near_sent, mask=1), cuts(far_sent, mask=2)
-    gy_2, gy_3, pick_a, pick_b = call(
+    gy_b, pick_b = call(
         text_pull_kernel,
-        [tall, tall, pick_one, pick_one],
+        [wide, pick_one],
         [],
-        (*first, *second, t0, t1, after(x_a, dp_a), w_a2, w_a3),
+        (*far_text, after(x_a, dp_a), w_ab),
         8,
         place,
     )
-    middle_b, corner, corner_dots = ((half // 2, width), BF16), ((half, half), BF16), ((half, half), F32)
-    *x_2, w_2a, w_22, w_23 = call(
+    middle_b = ((half // 2, width), BF16)
+    *x_2, w_2a, w_2b = call(
         block_kernel,
-        [middle_b, middle_b, block_w, corner, corner],
-        [tall, tall_b, block_dots, corner_dots, corner_dots],
-        (after(i2, gy_2), image_head, y_a, y_2, y_3),
+        [middle_b, middle_b, block_w, block_w],
+        [tall, tall_b, block_dots, block_dots],
+        (after(i2, gy_b), image_head, y_a, y_b),
         8,
     )
     x_3 = [loop(rows, mask=1) for rows in x_2]
-    gy_a, gy_2, gy_3 = call(
+    gy_a, gy_b = call(
         own_pull_kernel,
-        [wide, tall, tall],
+        [wide, wide],
         [],
-        (*x_2, w_2a, w_22, w_23, gy_a, gy_2, gy_3),
+        (*x_2, w_2a, w_2b, gy_a, gy_b),
         8,
     )
     near_came, far_came = after(near_came, gy_a), after(far_came, gy_a)
@@ -395,10 +379,9 @@
     x_3 = [after(rows, (gy_a, near_sent, far_sent)) for rows in x_3]
     *text_parts, dq_a = call(
         last_kernel,
-        [((part, width), BF16)] * QUAD + [wide_b],
-        [wide, tall, tall, wide_b, ((rows_out, width), F32), block_w, corner, corner]
-        + [block_dots, corner_dots, corner_dots],
-        (*x_3, y_a, y_2, y_3, q_a, q_2, q_3, gy_a, gy_2, gy_3, pick_a, pick_b),
+        [part_b] * QUAD + [wide_b],
+        [wide, wide, wide_b, ((rows_out, width), F32), block_w, block_w, block_dots, block_dots],
+        (*x_3, y_a, y_b, q_a, q_b, gy_a, gy_b, pick_a, pick_b),
         16,
     )
     text_others = [cuts(text_parts[k], mask=k) for k in range(1, QUAD)]

time: 79.1 us -> 79.3 us (level)
  waiting for transfers between devices: 13.1 us -> 18.1 us
  local copies, waits for them, and re-layouts: 2.02 us -> 0.05 us
  starting transfers between devices: 30.6 us -> 29 us
  Pallas kernels: 31.9 us -> 30.7 us
    ppermute x27 -> x26, waiting for transfers between devices: 13.1 us -> 18.1 us  [swap(): return lax.ppermute(array, axis, [(i, i ^ mask) for i in range(size)])]
    slice x2 -> x0, local copies, waits for them, and re-layouts: 1.97 us -> none  [the longest x1 0.98 us: per_device(): t2 = loop(text_features[:half // 2], mask=2)]
    ppermute x27 -> x26, starting transfers between devices: 30.6 us -> 29 us  [swap(): return lax.ppermute(array, axis, [(i, i ^ mask) for i in range(size)])]
    pallas_call x11, Pallas kernels: 31.9 us -> 30.7 us  [call(): pl.pallas_call(kernel, out_shape=[shape(s, t) for s, t in outs], in_specs...]
  transfers between devices with their start and end apart: 27 -> 26, of which waited for: 9 -> 13; matrix products, arithmetic and copies ran while one was open for 3% -> 1% of each run, Pallas kernels for 38% -> 37%
where the time goes in v14:
time: 79.3 us; the launch traced here: 79.2 us
  Pallas kernels  30.7 us (39%)
  starting transfers between devices  29 us (37%)
  waiting for transfers between devices  18.1 us (23%)
    pallas_call x11, Pallas kernels, call(): pl.pallas_call(kernel, out_shape=[shape(s, t) for s, t in outs], in_specs...  30.7 us
    ppermute x26, starting transfers between devices, swap(): return lax.ppermute(array, axis, [(i, i ^ mask) for i in range(size)])  29 us
    ppermute x26, waiting for transfers between devices, swap(): return lax.ppermute(array, axis, [(i, i ^ mask) for i in range(size)])  18.1 us
  transfers between devices with their start and end apart: 26, of which 13 were waited for; matrix products, arithmetic and copies ran while one was open for 1% of the time, Pallas kernels for 37%

profile of v14, /device:TPU:0, one launch (start us, length us, event | category | flops | bytes accessed | tf_op | source)
XLA Modules:
  0.0 79.2 jit_solution(5838494490180637)
XLA Ops:
  1.3 2.9 %collective-permute-start = (bf16[256,1152]{1,0:T(8,128)(2,1)}, bf16[256,1152]{1,0:T(8,128)(2,1)S(1)}, u32[]{:S(2)}, u32[]{:S(2)}) collective-permute-start(bf16[256,1152]{1,0:T(8,128)(2,1)} %t0_far), channel_id=1, source_target_pairs={{0,2},{1,3},{2,0},{3,1},{4,6},{5,7},{6,4},{7,5},{8,10},{9,11},{10,... | collective-permute-start | bytes 1769480 | tf_op jit(solution)/shard_map/ppermute | solution.py:287
  4.2 7.4 %shard_map.75 = (f32[512,1152]{1,0:T(8,128)S(1)}, bf16[512,1152]{1,0:T(8,128)(2,1)S(1)}, f32[512,1152]{1,0:T(8,128)S(1)}, bf16[512,1152]{1,0:T(8,128)(2,1)S(1)},...) custom-call(bf16[256,1152]{1,0:T(8,128)(2,1)S(1)} %collective-permut, ...), custom_call_target="tpu_custom_call" | custom-call | tf_op jit(solution)/shard_map/pallas_call | solution.py:274
  11.6 2.6 %shard_map.76 = (f32[512,1152]{1,0:T(8,128)S(1)}, bf16[576,512]{1,0:T(8,128)(2,1)S(1)}, bf16[288,512]{1,0:T(8,128)(2,1)S(1)}) custom-call(s32[2]{0:T(128)S(1)} %pad_add_fusion.place, bf16[256,1152]{1,0:T(8,128)(2,1)S(1)} %get-tuple-element.61.t0, bf16[256,1152]{1,0:T(8,128)(2,1)S(1)} %collective-permute-done.1.t1, ...), custom_call_target="tpu_custom_call" | custom-call | tf_op jit(solution)/shard_map/pallas_call | solution.py:274
  14.2 4.3 %collective-permute-done.refs_0_ = bf16[256,1152]{1,0:T(8,128)(2,1)S(1)} collective-permute-done((bf16[256,1152]{1,0:T(8,128)(2,1)}, bf16[256,1152]{1,0:T(8,128)(2,1)S(1)}, u32[]{:S(2)}, u32[]{:S(2)}) %collective-permute-start) | collective-permute-done | bytes 589856 | tf_op jit(solution)/shard_map/ppermute | solution.py:287
  20.7 5.2 %shard_map.77 = (f32[512,1152]{1,0:T(8,128)S(1)}, bf16[512,1152]{1,0:T(8,128)(2,1)S(1)}, bf16[512,512]{1,0:T(8,128)(2,1)S(1)}, bf16[512,1152]{1,0:T(8,128)(2,1)S...) custom-call(bf16[256,1152]{1,0:T(8,128)(2,1)S(1)} %collective-permut, ...), custom_call_target="tpu_custom_call" | custom-call | tf_op jit(solution)/shard_map/pallas_call | solution.py:274
  25.9 2.2 %collective-permute-start.7 = (bf16[144,1152]{1,0:T(8,128)(2,1)S(1)}, bf16[144,1152]{1,0:T(8,128)(2,1)S(1)}, u32[]{:S(2)}, u32[]{:S(2)}) collective-permute-start(bf16[144,1152]{1,0:T(8,128)(2,1)S(1)} %get-tuple-element.73), channel_id=1, source_target_pairs={{0,4},{4,0},{8,12},{12,8},{16,20},{20,16},{24,28},{28,24},{1,5},{5... | collective-permute-start | bytes 995336 | tf_op jit(solution)/shard_map/ppermute | solution.py:287
  28.1 1.6 %collective-permute-start.11 = (bf16[144,1152]{1,0:T(8,128)(2,1)S(1)}, bf16[144,1152]{1,0:T(8,128)(2,1)S(1)}, u32[]{:S(2)}, u32[]{:S(2)}) collective-permute-start(bf16[144,1152]{1,0:T(8,128)(2,1)S(1)} %get-tuple-element.89), channel_id=1, source_target_pairs={{0,8},{4,12},{8,0},{12,4},{16,24},{20,28},{24,16},{28,20},{1,9},{5... | collective-permute-start | bytes 995336 | tf_op jit(solution)/shard_map/ppermute | solution.py:287
  29.6 2.0 %shard_map.78 = (f32[512,1152]{1,0:T(8,128)S(1)}, bf16[288,512]{1,0:T(8,128)(2,1)S(1)}) custom-call(s32[2]{0:T(128)S(1)} %pad_add_fusion.place, bf16[256,1152]{1,0:T(8,128)(2,1)S(1)} %collective-permute-done.refs_0_, bf16[64,1152]{1,0:T(8,128)(2,1)S(1)} %collective-permute-done.3.refs_1_, bf16[64,1152]{1,0:T(8,128)(2,1)S(1)} %collective-permute-done.4.refs_2_, ...), custom_call_target="tpu_custom_call" | custom-call | tf_op jit(solution)/shard_map/pallas_call | solution.py:274
  31.7 1.9 %shard_map.79 = (bf16[128,1152]{1,0:T(8,128)(2,1)S(1)}, bf16[128,1152]{1,0:T(8,128)(2,1)S(1)}, bf16[256,512]{1,0:T(8,128)(2,1)S(1)}, bf16[256,512]{1,0:T(8,128)(2,1)S(1)}) custom-call(bf16[256,1152]{1,0:T(8,128)(2,1)S(1)} %collective-permute-done.8.i2, bf16[1152,1152]{1,0:T(8,128)(2,1)S(1)} %get-tuple-element.78.image_head.head, ...), custom_call_target="tpu_custom_call" | custom-call | tf_op jit(solution)/shard_map/pallas_call | solution.py:274
  35.0 1.3 %collective-permute-done.7 = bf16[144,1152]{1,0:T(8,128)(2,1)S(1)} collective-permute-done((bf16[144,1152]{1,0:T(8,128)(2,1)S(1)}, bf16[144,1152]{1,0:T(8,128)(2,1)S(1)}, u32[]{:S(2)}, u32[]{:S(2)}) %collective-permute-start.7) | collective-permute-done | bytes 331808 | tf_op jit(solution)/shard_map/ppermute | solution.py:287
  36.3 1.5 %collective-permute-done.11 = bf16[144,1152]{1,0:T(8,128)(2,1)S(1)} collective-permute-done((bf16[144,1152]{1,0:T(8,128)(2,1)S(1)}, bf16[144,1152]{1,0:T(8,128)(2,1)S(1)}, u32[]{:S(2)}, u32[]{:S(2)}) %collective-permute-start.11) | collective-permute-done | bytes 331808 | tf_op jit(solution)/shard_map/ppermute | solution.py:287
  38.3 1.8 %collective-permute-start.9 = (bf16[72,1152]{1,0:T(8,128)(2,1)S(1)}, bf16[72,1152]{1,0:T(8,128)(2,1)S(1)}, u32[]{:S(2)}, u32[]{:S(2)}) collective-permute-start(bf16[72,1152]{1,0:T(8,128)(2,1)S(1)} %add_convert_fusion.7), channel_id=1, source_target_pairs={{0,8},{4,12},{8,0},{12,4},{16,24},{20,28},{24,16},{28,20},{1,9},{5... | collective-permute-start | bytes 497672 | tf_op jit(solution)/shard_map/ppermute | solution.py:287
  40.1 3.3 %shard_map.81 = (bf16[72,1152]{1,0:T(8,128)(2,1)S(1)}, bf16[72,1152]{1,0:T(8,128)(2,1)S(1)}, bf16[72,1152]{1,0:T(8,128)(2,1)S(1)}, bf16[72,1152]{1,0:T(8,128)(2,1)S(1)}, bf16[512,1152]{1,0:T(8,128)(2,1)S(1)}) custom-call(bf16[128,1152]{1,0:T(8,128)(2,1)S(1)} %collective-permute-done.10.x_first, bf16[128,1152]{1,0:T(8,128)(2,1)S(1)} %collective-permute-done.12.x_second, ...), custom_call_target="tpu_custom_call" | custom-call | tf_op jit(solution)/shard_map/pallas_call | solution.py:274
  43.5 1.6 %collective-permute-start.14 = (bf16[72,1152]{1,0:T(8,128)(2,1)S(1)}, bf16[72,1152]{1,0:T(8,128)(2,1)S(1)}, u32[]{:S(2)}, u32[]{:S(2)}) collective-permute-start(bf16[72,1152]{1,0:T(8,128)(2,1)S(1)} %add_convert_fusion.4), channel_id=1, source_target_pairs={{0,2},{1,3},{2,0},{3,1},{4,6},{5,7},{6,4},{7,5},{8,10},{9,11},{10,... | collective-permute-start | bytes 497672 | tf_op jit(solution)/shard_map/ppermute | solution.py:287
  45.0 1.5 %collective-permute-start.19 = (bf16[72,1152]{1,0:T(8,128)(2,1)S(1)}, bf16[72,1152]{1,0:T(8,128)(2,1)S(1)}, u32[]{:S(2)}, u32[]{:S(2)}) collective-permute-start(bf16[72,1152]{1,0:T(8,128)(2,1)S(1)} %get-tuple-element.105), channel_id=1, source_target_pairs={{0,4},{4,0},{8,12},{12,8},{16,20},{20,16},{24,28},{28,24},{1,5},{5... | collective-permute-start | bytes 497672 | tf_op jit(solution)/shard_map/ppermute | solution.py:287
  47.0 1.5 %collective-permute-start.21 = (bf16[72,1152]{1,0:T(8,128)(2,1)S(1)}, bf16[72,1152]{1,0:T(8,128)(2,1)S(1)}, u32[]{:S(2)}, u32[]{:S(2)}) collective-permute-start(bf16[72,1152]{1,0:T(8,128)(2,1)S(1)} %get-tuple-element.109), channel_id=1, source_target_pairs={{0,12},{4,8},{8,4},{12,0},{16,28},{20,24},{24,20},{28,16},{1,13},{... | collective-permute-start | bytes 497672 | tf_op jit(solution)/shard_map/ppermute | solution.py:287
  49.0 2.7 %collective-permute-start.15 = (bf16[72,1152]{1,0:T(8,128)(2,1)S(1)}, bf16[72,1152]{1,0:T(8,128)(2,1)S(1)}, u32[]{:S(2)}, u32[]{:S(2)}) collective-permute-start(bf16[72,1152]{1,0:T(8,128)(2,1)S(1)} %add_convert_fusion.3), channel_id=1, source_target_pairs={{0,16},{4,20},{8,24},{12,28},{16,0},{20,4},{24,8},{28,12},{1,17},{... | collective-permute-start | bytes 497672 | tf_op jit(solution)/shard_map/ppermute | solution.py:287
  51.6 2.0 %shard_map.83 = f32[256,1152]{1,0:T(8,128)} custom-call(bf16[512,1152]{1,0:T(8,128)(2,1)S(1)} %get-tuple-element.103.back, bf16[1152,1152]{1,0:T(8,128)(2,1)S(1)} %get-tuple-element.67.refs_5_.head), custom_call_target="tpu_custom_call" | custom-call | flops 1358954496 | tf_op jit(solution)/shard_map/pallas_call | solution.py:274
  53.7 2.0 %shard_map.82 = f32[256,1152]{1,0:T(8,128)} custom-call(bf16[512,1152]{1,0:T(8,128)(2,1)S(1)} %get-tuple-element.102.back, bf16[1152,1152]{1,0:T(8,128)(2,1)S(1)} %get-tuple-element.78.image_head.head), custom_call_target="tpu_custom_call" | custom-call | flops 1358954496 | tf_op jit(solution)/shard_map/pallas_call | solution.py:274
  55.7 2.5 %collective-permute-done.21 = bf16[72,1152]{1,0:T(8,128)(2,1)S(1)} collective-permute-done((bf16[72,1152]{1,0:T(8,128)(2,1)S(1)}, bf16[72,1152]{1,0:T(8,128)(2,1)S(1)}, u32[]{:S(2)}, u32[]{:S(2)}) %collective-permute-start.21) | collective-permute-done | bytes 165920 | tf_op jit(solution)/shard_map/ppermute | solution.py:287
  58.3 1.3 %collective-permute-start.22 = (bf16[72,1152]{1,0:T(8,128)(2,1)S(1)}, bf16[72,1152]{1,0:T(8,128)(2,1)S(1)}, u32[]{:S(2)}, u32[]{:S(2)}) collective-permute-start(bf16[72,1152]{1,0:T(8,128)(2,1)S(1)} %add_convert_fusion.1), channel_id=1, source_target_pairs={{0,16},{4,20},{8,24},{12,28},{16,0},{20,4},{24,8},{28,12},{1,17},{... | collective-permute-start | bytes 497672 | tf_op jit(solution)/shard_map/ppermute | solution.py:287
  59.7 1.9 %collective-permute-start.16 = (bf16[72,1152]{1,0:T(8,128)(2,1)S(1)}, bf16[72,1152]{1,0:T(8,128)(2,1)S(1)}, u32[]{:S(2)}, u32[]{:S(2)}) collective-permute-start(bf16[72,1152]{1,0:T(8,128)(2,1)S(1)} %add_convert_fusion.2.refs_0_), channel_id=1, source_target_pairs={{0,4},{4,0},{8,12},{12,8},{16,20},{20,16},{24,28},{28,24},{1,5},{5... | collective-permute-start | bytes 497672 | tf_op jit(solution)/shard_map/ppermute | solution.py:287
  61.6 2.1 %collective-permute-start.17 = (bf16[72,1152]{1,0:T(8,128)(2,1)S(1)}, bf16[72,1152]{1,0:T(8,128)(2,1)S(1)}, u32[]{:S(2)}, u32[]{:S(2)}) collective-permute-start(bf16[72,1152]{1,0:T(8,128)(2,1)S(1)} %add_convert_fusion.2.refs_0_), channel_id=1, source_target_pairs={{0,8},{4,12},{8,0},{12,4},{16,24},{20,28},{24,16},{28,20},{1,9},{5... | collective-permute-start | bytes 497672 | tf_op jit(solution)/shard_map/ppermute | solution.py:287
  63.8 1.3 %collective-permute-start.18 = (bf16[72,1152]{1,0:T(8,128)(2,1)S(1)}, bf16[72,1152]{1,0:T(8,128)(2,1)S(1)}, u32[]{:S(2)}, u32[]{:S(2)}) collective-permute-start(bf16[72,1152]{1,0:T(8,128)(2,1)S(1)} %add_convert_fusion.2.refs_0_), channel_id=1, source_target_pairs={{0,12},{4,8},{8,4},{12,0},{16,28},{20,24},{24,20},{28,16},{1,13},{... | collective-permute-start | bytes 497672 | tf_op jit(solution)/shard_map/ppermute | solution.py:287
  65.1 1.3 %collective-permute-done.22 = bf16[72,1152]{1,0:T(8,128)(2,1)S(1)} collective-permute-done((bf16[72,1152]{1,0:T(8,128)(2,1)S(1)}, bf16[72,1152]{1,0:T(8,128)(2,1)S(1)}, u32[]{:S(2)}, u32[]{:S(2)}) %collective-permute-start.22) | collective-permute-done | bytes 165920 | tf_op jit(solution)/shard_map/ppermute | solution.py:287
  66.4 1.1 %collective-permute-done.16.refs_1_ = bf16[72,1152]{1,0:T(8,128)(2,1)S(1)} collective-permute-done((bf16[72,1152]{1,0:T(8,128)(2,1)S(1)}, bf16[72,1152]{1,0:T(8,128)(2,1)S(1)}, u32[]{:S(2)}, u32[]{:S(2)}) %collective-permute-start.16) | collective-permute-done | bytes 165920 | tf_op jit(solution)/shard_map/ppermute | solution.py:287
  67.9 1.7 %collective-permute-start.24 = (bf16[72,1152]{1,0:T(8,128)(2,1)S(1)}, bf16[72,1152]{1,0:T(8,128)(2,1)S(1)}, u32[]{:S(2)}, u32[]{:S(2)}) collective-permute-start(bf16[72,1152]{1,0:T(8,128)(2,1)S(1)} %add_convert_fusion.refs_0_), channel_id=1, source_target_pairs={{0,8},{4,12},{8,0},{12,4},{16,24},{20,28},{24,16},{28,20},{1,9},{5... | collective-permute-start | bytes 497672 | tf_op jit(solution)/shard_map/ppermute | solution.py:287
  69.7 1.4 %collective-permute-start.25 = (bf16[72,1152]{1,0:T(8,128)(2,1)S(1)}, bf16[72,1152]{1,0:T(8,128)(2,1)S(1)}, u32[]{:S(2)}, u32[]{:S(2)}) collective-permute-start(bf16[72,1152]{1,0:T(8,128)(2,1)S(1)} %add_convert_fusion.refs_0_), channel_id=1, source_target_pairs={{0,12},{4,8},{8,4},{12,0},{16,28},{20,24},{24,20},{28,16},{1,13},{... | collective-permute-start | bytes 497672 | tf_op jit(solution)/shard_map/ppermute | solution.py:287
  71.1 2.9 %collective-permute-done.18.refs_3_ = bf16[72,1152]{1,0:T(8,128)(2,1)S(1)} collective-permute-done((bf16[72,1152]{1,0:T(8,128)(2,1)S(1)}, bf16[72,1152]{1,0:T(8,128)(2,1)S(1)}, u32[]{:S(2)}, u32[]{:S(2)}) %collective-permute-start.18) | collective-permute-done | bytes 165920 | tf_op jit(solution)/shard_map/ppermute | solution.py:287
  74.0 1.7 %shard_map.84 = f32[288,1152]{1,0:T(8,128)} custom-call(s32[2]{0:T(128)S(1)} %pad_add_fusion.place, bf16[72,1152]{1,0:T(8,128)(2,1)S(1)} %add_convert_fusion.2.refs_0_, bf16[72,1152]{1,0:T(8,128)(2,1)S(1)} %collective-permute-done.16.refs_1_, bf16[72,1152]{1,0:T(8,128)(2,1)S(1)} %collective-permute-done.17.refs_2_, ...), custom_call_target="tpu_custom_call" | custom-call | tf_op jit(solution)/shard_map/pallas_call | solution.py:274
  75.7 1.8 %collective-permute-done.25.refs_3_ = bf16[72,1152]{1,0:T(8,128)(2,1)S(1)} collective-permute-done((bf16[72,1152]{1,0:T(8,128)(2,1)S(1)}, bf16[72,1152]{1,0:T(8,128)(2,1)S(1)}, u32[]{:S(2)}, u32[]{:S(2)}) %collective-permute-start.25) | collective-permute-done | bytes 165920 | tf_op jit(solution)/shard_map/ppermute | solution.py:287
  77.5 1.7 %shard_map.85 = f32[288,1152]{1,0:T(8,128)} custom-call(s32[2]{0:T(128)S(1)} %pad_add_fusion.place, bf16[72,1152]{1,0:T(8,128)(2,1)S(1)} %add_convert_fusion.refs_0_, bf16[72,1152]{1,0:T(8,128)(2,1)S(1)} %collective-permute-done.23.refs_1_, bf16[72,1152]{1,0:T(8,128)(2,1)S(1)} %collective-permute-done.24.refs_2_, ...), custom_call_target="tpu_custom_call" | custom-call | tf_op jit(solution)/shard_map/pallas_call | solution.py:274
  (40 shorter events, 6.4 us)
Async XLA Ops:
  0.7 3.5 %collective-permute-start.1 = (bf16[256,1152]{1,0:T(8,128)(2,1)}, bf16[256,1152]{1,0:T(8,128)(2,1)S(1)}, u32[]{:S(2)}, u32[]{:S(2)}) collective-permute-start(bf16[256,1152]{1,0:T(8,128)(2,1)} %t0_far), channel_id=1, source_target_pairs={{0,1},{1,0},{2,3},{3,2},{4,5},{5,4},{6,7},{7,6},{8,9},{9,8},{10,11... | collective-permute-start | bytes 1769480 | tf_op jit(solution)/shard_map/ppermute | solution.py:287
  1.2 3.0 %collective-permute-start.2 = (bf16[256,1152]{1,0:T(8,128)(2,1)}, bf16[256,1152]{1,0:T(8,128)(2,1)S(1)}, u32[]{:S(2)}, u32[]{:S(2)}) collective-permute-start(bf16[256,1152]{1,0:T(8,128)(2,1)} %i0_far), channel_id=1, source_target_pairs={{0,1},{1,0},{2,3},{3,2},{4,5},{5,4},{6,7},{7,6},{8,9},{9,8},{10,11... | collective-permute-start | bytes 1769480 | tf_op jit(solution)/shard_map/ppermute | solution.py:287
  1.3 17.2 %collective-permute-start = (bf16[256,1152]{1,0:T(8,128)(2,1)}, bf16[256,1152]{1,0:T(8,128)(2,1)S(1)}, u32[]{:S(2)}, u32[]{:S(2)}) collective-permute-start(bf16[256,1152]{1,0:T(8,128)(2,1)} %t0_far), channel_id=1, source_target_pairs={{0,2},{1,3},{2,0},{3,1},{4,6},{5,7},{6,4},{7,5},{8,10},{9,11},{10,... | collective-permute-start | bytes 1769480 | tf_op jit(solution)/shard_map/ppermute | solution.py:287
  4.2 27.5 %collective-permute-start.8 = (bf16[256,1152]{1,0:T(8,128)(2,1)}, bf16[256,1152]{1,0:T(8,128)(2,1)S(1)}, u32[]{:S(2)}, u32[]{:S(2)}) collective-permute-start(bf16[256,1152]{1,0:T(8,128)(2,1)} %i0_far), channel_id=1, source_target_pairs={{0,2},{1,3},{2,0},{3,1},{4,6},{5,7},{6,4},{7,5},{8,10},{9,11},{10,... | collective-permute-start | bytes 1769480 | tf_op jit(solution)/shard_map/ppermute | solution.py:287
  18.5 1.4 %collective-permute-start.3 = (bf16[64,1152]{1,0:T(8,128)(2,1)S(1)}, bf16[64,1152]{1,0:T(8,128)(2,1)S(1)}, u32[]{:S(2)}, u32[]{:S(2)}) collective-permute-start(bf16[64,1152]{1,0:T(8,128)(2,1)S(1)} %get-tuple-element.115), channel_id=1, source_target_pairs={{0,1},{1,0},{2,3},{3,2},{4,5},{5,4},{6,7},{7,6},{8,9},{9,8},{10,11... | collective-permute-start | bytes 442376 | tf_op jit(solution)/shard_map/ppermute | solution.py:287
  18.6 1.6 %collective-permute-start.4 = (bf16[64,1152]{1,0:T(8,128)(2,1)S(1)}, bf16[64,1152]{1,0:T(8,128)(2,1)S(1)}, u32[]{:S(2)}, u32[]{:S(2)}) collective-permute-start(bf16[64,1152]{1,0:T(8,128)(2,1)S(1)} %get-tuple-element.114), channel_id=1, source_target_pairs={{0,1},{1,0},{2,3},{3,2},{4,5},{5,4},{6,7},{7,6},{8,9},{9,8},{10,11... | collective-permute-start | bytes 442376 | tf_op jit(solution)/shard_map/ppermute | solution.py:287
  19.1 1.4 %collective-permute-start.5 = (bf16[64,1152]{1,0:T(8,128)(2,1)S(1)}, bf16[64,1152]{1,0:T(8,128)(2,1)S(1)}, u32[]{:S(2)}, u32[]{:S(2)}) collective-permute-start(bf16[64,1152]{1,0:T(8,128)(2,1)S(1)} %get-tuple-element.113), channel_id=1, source_target_pairs={{0,1},{1,0},{2,3},{3,2},{4,5},{5,4},{6,7},{7,6},{8,9},{9,8},{10,11... | collective-permute-start | bytes 442376 | tf_op jit(solution)/shard_map/ppermute | solution.py:287
  19.2 1.5 %collective-permute-start.6 = (bf16[64,1152]{1,0:T(8,128)(2,1)S(1)}, bf16[64,1152]{1,0:T(8,128)(2,1)S(1)}, u32[]{:S(2)}, u32[]{:S(2)}) collective-permute-start(bf16[64,1152]{1,0:T(8,128)(2,1)S(1)} %get-tuple-element.112), channel_id=1, source_target_pairs={{0,1},{1,0},{2,3},{3,2},{4,5},{5,4},{6,7},{7,6},{8,9},{9,8},{10,11... | collective-permute-start | bytes 442376 | tf_op jit(solution)/shard_map/ppermute | solution.py:287
  25.9 10.4 %collective-permute-start.7 = (bf16[144,1152]{1,0:T(8,128)(2,1)S(1)}, bf16[144,1152]{1,0:T(8,128)(2,1)S(1)}, u32[]{:S(2)}, u32[]{:S(2)}) collective-permute-start(bf16[144,1152]{1,0:T(8,128)(2,1)S(1)} %get-tuple-element.73), channel_id=1, source_target_pairs={{0,4},{4,0},{8,12},{12,8},{16,20},{20,16},{24,28},{28,24},{1,5},{5... | collective-permute-start | bytes 995336 | tf_op jit(solution)/shard_map/ppermute | solution.py:287
  28.1 9.7 %collective-permute-start.11 = (bf16[144,1152]{1,0:T(8,128)(2,1)S(1)}, bf16[144,1152]{1,0:T(8,128)(2,1)S(1)}, u32[]{:S(2)}, u32[]{:S(2)}) collective-permute-start(bf16[144,1152]{1,0:T(8,128)(2,1)S(1)} %get-tuple-element.89), channel_id=1, source_target_pairs={{0,8},{4,12},{8,0},{12,4},{16,24},{20,28},{24,16},{28,20},{1,9},{5... | collective-permute-start | bytes 995336 | tf_op jit(solution)/shard_map/ppermute | solution.py:287
  33.6 6.5 %collective-permute-start.12 = (bf16[128,1152]{1,0:T(8,128)(2,1)S(1)}, bf16[128,1152]{1,0:T(8,128)(2,1)S(1)}, u32[]{:S(2)}, u32[]{:S(2)}) collective-permute-start(bf16[128,1152]{1,0:T(8,128)(2,1)S(1)} %get-tuple-element.82.x_second), channel_id=1, source_target_pairs={{0,1},{1,0},{2,3},{3,2},{4,5},{5,4},{6,7},{7,6},{8,9},{9,8},{10,11... | collective-permute-start | bytes 884744 | tf_op jit(solution)/shard_map/ppermute | solution.py:287
  33.7 6.4 %collective-permute-start.10 = (bf16[128,1152]{1,0:T(8,128)(2,1)S(1)}, bf16[128,1152]{1,0:T(8,128)(2,1)S(1)}, u32[]{:S(2)}, u32[]{:S(2)}) collective-permute-start(bf16[128,1152]{1,0:T(8,128)(2,1)S(1)} %get-tuple-element.81.x_first), channel_id=1, source_target_pairs={{0,1},{1,0},{2,3},{3,2},{4,5},{5,4},{6,7},{7,6},{8,9},{9,8},{10,11... | collective-permute-start | bytes 884744 | tf_op jit(solution)/shard_map/ppermute | solution.py:287
  37.8 5.6 %collective-permute-start.13 = (bf16[72,1152]{1,0:T(8,128)(2,1)S(1)}, bf16[72,1152]{1,0:T(8,128)(2,1)S(1)}, u32[]{:S(2)}, u32[]{:S(2)}) collective-permute-start(bf16[72,1152]{1,0:T(8,128)(2,1)S(1)} %add_convert_fusion.6), channel_id=1, source_target_pairs={{0,4},{4,0},{8,12},{12,8},{16,20},{20,16},{24,28},{28,24},{1,5},{5... | collective-permute-start | bytes 497672 | tf_op jit(solution)/shard_map/ppermute | solution.py:287
  38.3 10.2 %collective-permute-start.9 = (bf16[72,1152]{1,0:T(8,128)(2,1)S(1)}, bf16[72,1152]{1,0:T(8,128)(2,1)S(1)}, u32[]{:S(2)}, u32[]{:S(2)}) collective-permute-start(bf16[72,1152]{1,0:T(8,128)(2,1)S(1)} %add_convert_fusion.7), channel_id=1, source_target_pairs={{0,8},{4,12},{8,0},{12,4},{16,24},{20,28},{24,16},{28,20},{1,9},{5... | collective-permute-start | bytes 497672 | tf_op jit(solution)/shard_map/ppermute | solution.py:287
  43.5 5.4 %collective-permute-start.14 = (bf16[72,1152]{1,0:T(8,128)(2,1)S(1)}, bf16[72,1152]{1,0:T(8,128)(2,1)S(1)}, u32[]{:S(2)}, u32[]{:S(2)}) collective-permute-start(bf16[72,1152]{1,0:T(8,128)(2,1)S(1)} %add_convert_fusion.4), channel_id=1, source_target_pairs={{0,2},{1,3},{2,0},{3,1},{4,6},{5,7},{6,4},{7,5},{8,10},{9,11},{10,... | collective-permute-start | bytes 497672 | tf_op jit(solution)/shard_map/ppermute | solution.py:287
  45.0 10.7 %collective-permute-start.19 = (bf16[72,1152]{1,0:T(8,128)(2,1)S(1)}, bf16[72,1152]{1,0:T(8,128)(2,1)S(1)}, u32[]{:S(2)}, u32[]{:S(2)}) collective-permute-start(bf16[72,1152]{1,0:T(8,128)(2,1)S(1)} %get-tuple-element.105), channel_id=1, source_target_pairs={{0,4},{4,0},{8,12},{12,8},{16,20},{20,16},{24,28},{28,24},{1,5},{5... | collective-permute-start | bytes 497672 | tf_op jit(solution)/shard_map/ppermute | solution.py:287
  46.6 9.2 %collective-permute-start.20 = (bf16[72,1152]{1,0:T(8,128)(2,1)S(1)}, bf16[72,1152]{1,0:T(8,128)(2,1)S(1)}, u32[]{:S(2)}, u32[]{:S(2)}) collective-permute-start(bf16[72,1152]{1,0:T(8,128)(2,1)S(1)} %get-tuple-element.107), channel_id=1, source_target_pairs={{0,8},{4,12},{8,0},{12,4},{16,24},{20,28},{24,16},{28,20},{1,9},{5... | collective-permute-start | bytes 497672 | tf_op jit(solution)/shard_map/ppermute | solution.py:287
  47.0 11.2 %collective-permute-start.21 = (bf16[72,1152]{1,0:T(8,128)(2,1)S(1)}, bf16[72,1152]{1,0:T(8,128)(2,1)S(1)}, u32[]{:S(2)}, u32[]{:S(2)}) collective-permute-start(bf16[72,1152]{1,0:T(8,128)(2,1)S(1)} %get-tuple-element.109), channel_id=1, source_target_pairs={{0,12},{4,8},{8,4},{12,0},{16,28},{20,24},{24,20},{28,16},{1,13},{... | collective-permute-start | bytes 497672 | tf_op jit(solution)/shard_map/ppermute | solution.py:287
  49.0 10.7 %collective-permute-start.15 = (bf16[72,1152]{1,0:T(8,128)(2,1)S(1)}, bf16[72,1152]{1,0:T(8,128)(2,1)S(1)}, u32[]{:S(2)}, u32[]{:S(2)}) collective-permute-start(bf16[72,1152]{1,0:T(8,128)(2,1)S(1)} %add_convert_fusion.3), channel_id=1, source_target_pairs={{0,16},{4,20},{8,24},{12,28},{16,0},{20,4},{24,8},{28,12},{1,17},{... | collective-permute-start | bytes 497672 | tf_op jit(solution)/shard_map/ppermute | solution.py:287
  58.3 8.1 %collective-permute-start.22 = (bf16[72,1152]{1,0:T(8,128)(2,1)S(1)}, bf16[72,1152]{1,0:T(8,128)(2,1)S(1)}, u32[]{:S(2)}, u32[]{:S(2)}) collective-permute-start(bf16[72,1152]{1,0:T(8,128)(2,1)S(1)} %add_convert_fusion.1), channel_id=1, source_target_pairs={{0,16},{4,20},{8,24},{12,28},{16,0},{20,4},{24,8},{28,12},{1,17},{... | collective-permute-start | bytes 497672 | tf_op jit(solution)/shard_map/ppermute | solution.py:287
  59.7 7.7 %collective-permute-start.16 = (bf16[72,1152]{1,0:T(8,128)(2,1)S(1)}, bf16[72,1152]{1,0:T(8,128)(2,1)S(1)}, u32[]{:S(2)}, u32[]{:S(2)}) collective-permute-start(bf16[72,1152]{1,0:T(8,128)(2,1)S(1)} %add_convert_fusion.2.refs_0_), channel_id=1, source_target_pairs={{0,4},{4,0},{8,12},{12,8},{16,20},{20,16},{24,28},{28,24},{1,5},{5... | collective-permute-start | bytes 497672 | tf_op jit(solution)/shard_map/ppermute | solution.py:287
  61.6 9.4 %collective-permute-start.17 = (bf16[72,1152]{1,0:T(8,128)(2,1)S(1)}, bf16[72,1152]{1,0:T(8,128)(2,1)S(1)}, u32[]{:S(2)}, u32[]{:S(2)}) collective-permute-start(bf16[72,1152]{1,0:T(8,128)(2,1)S(1)} %add_convert_fusion.2.refs_0_), channel_id=1, source_target_pairs={{0,8},{4,12},{8,0},{12,4},{16,24},{20,28},{24,16},{28,20},{1,9},{5... | collective-permute-start | bytes 497672 | tf_op jit(solution)/shard_map/ppermute | solution.py:287
  63.8 10.2 %collective-permute-start.18 = (bf16[72,1152]{1,0:T(8,128)(2,1)S(1)}, bf16[72,1152]{1,0:T(8,128)(2,1)S(1)}, u32[]{:S(2)}, u32[]{:S(2)}) collective-permute-start(bf16[72,1152]{1,0:T(8,128)(2,1)S(1)} %add_convert_fusion.2.refs_0_), channel_id=1, source_target_pairs={{0,12},{4,8},{8,4},{12,0},{16,28},{20,24},{24,20},{28,16},{1,13},{... | collective-permute-start | bytes 497672 | tf_op jit(solution)/shard_map/ppermute | solution.py:287
  67.5 8.2 %collective-permute-start.23 = (bf16[72,1152]{1,0:T(8,128)(2,1)S(1)}, bf16[72,1152]{1,0:T(8,128)(2,1)S(1)}, u32[]{:S(2)}, u32[]{:S(2)}) collective-permute-start(bf16[72,1152]{1,0:T(8,128)(2,1)S(1)} %add_convert_fusion.refs_0_), channel_id=1, source_target_pairs={{0,4},{4,0},{8,12},{12,8},{16,20},{20,16},{24,28},{28,24},{1,5},{5... | collective-permute-start | bytes 497672 | tf_op jit(solution)/shard_map/ppermute | solution.py:287
  67.9 7.7 %collective-permute-start.24 = (bf16[72,1152]{1,0:T(8,128)(2,1)S(1)}, bf16[72,1152]{1,0:T(8,128)(2,1)S(1)}, u32[]{:S(2)}, u32[]{:S(2)}) collective-permute-start(bf16[72,1152]{1,0:T(8,128)(2,1)S(1)} %add_convert_fusion.refs_0_), channel_id=1, source_target_pairs={{0,8},{4,12},{8,0},{12,4},{16,24},{20,28},{24,16},{28,20},{1,9},{5... | collective-permute-start | bytes 497672 | tf_op jit(solution)/shard_map/ppermute | solution.py:287
  69.7 7.8 %collective-permute-start.25 = (bf16[72,1152]{1,0:T(8,128)(2,1)S(1)}, bf16[72,1152]{1,0:T(8,128)(2,1)S(1)}, u32[]{:S(2)}, u32[]{:S(2)}) collective-permute-start(bf16[72,1152]{1,0:T(8,128)(2,1)S(1)} %add_convert_fusion.refs_0_), channel_id=1, source_target_pairs={{0,12},{4,8},{8,4},{12,0},{16,28},{20,24},{24,20},{28,16},{1,13},{... | collective-permute-start | bytes 497672 | tf_op jit(solution)/shard_map/ppermute | solution.py:287

commit v15 on v14

--- a/solution.py
+++ b/solution.py
@@ -394,7 +394,8 @@
     ]
     text_sum = add(text_parts[0], [after(other, (image_sum, grads)) for other in text_others])
     image_sum = add(image_sum, [cuts(image_sum, mask=QUAD)])
-    image_pieces = spread(image_sum)
+    image_pieces = [image_sum, cuts(image_sum, mask=1), cuts(image_sum, mask=2)]
+    image_pieces.append(cuts(image_pieces[2], mask=1))
     text_sum = add(text_sum, [after(cuts(text_sum, mask=QUAD), image_pieces[1])])
     image_out, text_out = (
         call(place_kernel, [((rows_out, width), F32)], [], pieces, 4, place, keep=False)[0]

time: 79.3 us -> 81.7 us (1.030)
  waiting for transfers between devices: 18.1 us -> 20.5 us
    ppermute x26, waiting for transfers between devices: 18.1 us -> 20.5 us  [swap(): return lax.ppermute(array, axis, [(i, i ^ mask) for i in range(size)])]
  transfers between devices with their start and end apart: 26 -> 26, of which waited for: 13 -> 15; matrix products, arithmetic and copies ran while one was open for 1% -> 1% of each run, Pallas kernels for 37% -> 36%
where the time goes in v15:
time: 81.7 us; the launch traced here: 81.6 us
  Pallas kernels  30.7 us (38%)
  starting transfers between devices  29 us (35%)
  waiting for transfers between devices  20.5 us (25%)
    pallas_call x11, Pallas kernels, call(): pl.pallas_call(kernel, out_shape=[shape(s, t) for s, t in outs], in_specs...  30.7 us
    ppermute x26, starting transfers between devices, swap(): return lax.ppermute(array, axis, [(i, i ^ mask) for i in range(size)])  29 us
    ppermute x26, waiting for transfers between devices, swap(): return lax.ppermute(array, axis, [(i, i ^ mask) for i in range(size)])  20.5 us
  transfers between devices with their start and end apart: 26, of which 15 were waited for; matrix products, arithmetic and copies ran while one was open for 1% of the time, Pallas kernels for 36%

profile of v15, /device:TPU:0, one launch (start us, length us, event | category | flops | bytes accessed | tf_op | source)
XLA Modules:
  0.0 81.6 jit_solution(17938639411788059506)
XLA Ops:
  1.3 2.9 %collective-permute-start = (bf16[256,1152]{1,0:T(8,128)(2,1)}, bf16[256,1152]{1,0:T(8,128)(2,1)S(1)}, u32[]{:S(2)}, u32[]{:S(2)}) collective-permute-start(bf16[256,1152]{1,0:T(8,128)(2,1)} %t0_far), channel_id=1, source_target_pairs={{0,2},{1,3},{2,0},{3,1},{4,6},{5,7},{6,4},{7,5},{8,10},{9,11},{10,... | collective-permute-start | bytes 1769480 | tf_op jit(solution)/shard_map/ppermute | solution.py:287
  4.2 7.4 %shard_map.75 = (f32[512,1152]{1,0:T(8,128)S(1)}, bf16[512,1152]{1,0:T(8,128)(2,1)S(1)}, f32[512,1152]{1,0:T(8,128)S(1)}, bf16[512,1152]{1,0:T(8,128)(2,1)S(1)},...) custom-call(bf16[256,1152]{1,0:T(8,128)(2,1)S(1)} %collective-permut, ...), custom_call_target="tpu_custom_call" | custom-call | tf_op jit(solution)/shard_map/pallas_call | solution.py:274
  11.6 2.6 %shard_map.76 = (f32[512,1152]{1,0:T(8,128)S(1)}, bf16[576,512]{1,0:T(8,128)(2,1)S(1)}, bf16[288,512]{1,0:T(8,128)(2,1)S(1)}) custom-call(s32[2]{0:T(128)S(1)} %pad_add_fusion.place, bf16[256,1152]{1,0:T(8,128)(2,1)S(1)} %get-tuple-element.61.t0, bf16[256,1152]{1,0:T(8,128)(2,1)S(1)} %collective-permute-done.1.t1, ...), custom_call_target="tpu_custom_call" | custom-call | tf_op jit(solution)/shard_map/pallas_call | solution.py:274
  14.2 4.3 %collective-permute-done.refs_0_ = bf16[256,1152]{1,0:T(8,128)(2,1)S(1)} collective-permute-done((bf16[256,1152]{1,0:T(8,128)(2,1)}, bf16[256,1152]{1,0:T(8,128)(2,1)S(1)}, u32[]{:S(2)}, u32[]{:S(2)}) %collective-permute-start) | collective-permute-done | bytes 589856 | tf_op jit(solution)/shard_map/ppermute | solution.py:287
  20.7 5.2 %shard_map.77 = (f32[512,1152]{1,0:T(8,128)S(1)}, bf16[512,1152]{1,0:T(8,128)(2,1)S(1)}, bf16[512,512]{1,0:T(8,128)(2,1)S(1)}, bf16[512,1152]{1,0:T(8,128)(2,1)S...) custom-call(bf16[256,1152]{1,0:T(8,128)(2,1)S(1)} %collective-permut, ...), custom_call_target="tpu_custom_call" | custom-call | tf_op jit(solution)/shard_map/pallas_call | solution.py:274
  25.9 2.2 %collective-permute-start.7 = (bf16[144,1152]{1,0:T(8,128)(2,1)S(1)}, bf16[144,1152]{1,0:T(8,128)(2,1)S(1)}, u32[]{:S(2)}, u32[]{:S(2)}) collective-permute-start(bf16[144,1152]{1,0:T(8,128)(2,1)S(1)} %get-tuple-element.73), channel_id=1, source_target_pairs={{0,4},{4,0},{8,12},{12,8},{16,20},{20,16},{24,28},{28,24},{1,5},{5... | collective-permute-start | bytes 995336 | tf_op jit(solution)/shard_map/ppermute | solution.py:287
  28.1 1.6 %collective-permute-start.11 = (bf16[144,1152]{1,0:T(8,128)(2,1)S(1)}, bf16[144,1152]{1,0:T(8,128)(2,1)S(1)}, u32[]{:S(2)}, u32[]{:S(2)}) collective-permute-start(bf16[144,1152]{1,0:T(8,128)(2,1)S(1)} %get-tuple-element.89), channel_id=1, source_target_pairs={{0,8},{4,12},{8,0},{12,4},{16,24},{20,28},{24,16},{28,20},{1,9},{5... | collective-permute-start | bytes 995336 | tf_op jit(solution)/shard_map/ppermute | solution.py:287
  29.6 2.0 %shard_map.78 = (f32[512,1152]{1,0:T(8,128)S(1)}, bf16[288,512]{1,0:T(8,128)(2,1)S(1)}) custom-call(s32[2]{0:T(128)S(1)} %pad_add_fusion.place, bf16[256,1152]{1,0:T(8,128)(2,1)S(1)} %collective-permute-done.refs_0_, bf16[64,1152]{1,0:T(8,128)(2,1)S(1)} %collective-permute-done.3.refs_1_, bf16[64,1152]{1,0:T(8,128)(2,1)S(1)} %collective-permute-done.4.refs_2_, ...), custom_call_target="tpu_custom_call" | custom-call | tf_op jit(solution)/shard_map/pallas_call | solution.py:274
  31.7 1.9 %shard_map.79 = (bf16[128,1152]{1,0:T(8,128)(2,1)S(1)}, bf16[128,1152]{1,0:T(8,128)(2,1)S(1)}, bf16[256,512]{1,0:T(8,128)(2,1)S(1)}, bf16[256,512]{1,0:T(8,128)(2,1)S(1)}) custom-call(bf16[256,1152]{1,0:T(8,128)(2,1)S(1)} %collective-permute-done.8.i2, bf16[1152,1152]{1,0:T(8,128)(2,1)S(1)} %get-tuple-element.78.image_head.head, ...), custom_call_target="tpu_custom_call" | custom-call | tf_op jit(solution)/shard_map/pallas_call | solution.py:274
  34.2 0.9 %shard_map.80 = (f32[512,1152]{1,0:T(8,128)S(1)}, f32[512,1152]{1,0:T(8,128)S(1)}) custom-call(bf16[128,1152]{1,0:T(8,128)(2,1)S(1)} %get-tuple-element.81.x_first, bf16[128,1152]{1,0:T(8,128)(2,1)S(1)} %get-tuple-element.82.x_second, bf16[256,512]{1,0:T(8,128)(2,1)S(1)} %get-tuple-element.83.w_a, bf16[256,512]{1,0:T(8,128)(2,1)S(1)} %get-tuple-element.84.w_b, ...), custom_call_target="tpu_custom_call" | custom-call | tf_op jit(solution)/shard_map/pallas_call | solution.py:274
  35.0 1.3 %collective-permute-done.7 = bf16[144,1152]{1,0:T(8,128)(2,1)S(1)} collective-permute-done((bf16[144,1152]{1,0:T(8,128)(2,1)S(1)}, bf16[144,1152]{1,0:T(8,128)(2,1)S(1)}, u32[]{:S(2)}, u32[]{:S(2)}) %collective-permute-start.7) | collective-permute-done | bytes 331808 | tf_op jit(solution)/shard_map/ppermute | solution.py:287
  36.3 1.5 %collective-permute-done.11 = bf16[144,1152]{1,0:T(8,128)(2,1)S(1)} collective-permute-done((bf16[144,1152]{1,0:T(8,128)(2,1)S(1)}, bf16[144,1152]{1,0:T(8,128)(2,1)S(1)}, u32[]{:S(2)}, u32[]{:S(2)}) %collective-permute-start.11) | collective-permute-done | bytes 331808 | tf_op jit(solution)/shard_map/ppermute | solution.py:287
  38.3 1.8 %collective-permute-start.9 = (bf16[72,1152]{1,0:T(8,128)(2,1)S(1)}, bf16[72,1152]{1,0:T(8,128)(2,1)S(1)}, u32[]{:S(2)}, u32[]{:S(2)}) collective-permute-start(bf16[72,1152]{1,0:T(8,128)(2,1)S(1)} %add_convert_fusion.7), channel_id=1, source_target_pairs={{0,8},{4,12},{8,0},{12,4},{16,24},{20,28},{24,16},{28,20},{1,9},{5... | collective-permute-start | bytes 497672 | tf_op jit(solution)/shard_map/ppermute | solution.py:287
  40.1 3.3 %shard_map.81 = (bf16[72,1152]{1,0:T(8,128)(2,1)S(1)}, bf16[72,1152]{1,0:T(8,128)(2,1)S(1)}, bf16[72,1152]{1,0:T(8,128)(2,1)S(1)}, bf16[72,1152]{1,0:T(8,128)(2,1)S(1)}, bf16[512,1152]{1,0:T(8,128)(2,1)S(1)}) custom-call(bf16[128,1152]{1,0:T(8,128)(2,1)S(1)} %collective-permute-done.10.x_first, bf16[128,1152]{1,0:T(8,128)(2,1)S(1)} %collective-permute-done.12.x_second, ...), custom_call_target="tpu_custom_call" | custom-call | tf_op jit(solution)/shard_map/pallas_call | solution.py:274
  43.5 1.6 %collective-permute-start.14 = (bf16[72,1152]{1,0:T(8,128)(2,1)S(1)}, bf16[72,1152]{1,0:T(8,128)(2,1)S(1)}, u32[]{:S(2)}, u32[]{:S(2)}) collective-permute-start(bf16[72,1152]{1,0:T(8,128)(2,1)S(1)} %add_convert_fusion.4), channel_id=1, source_target_pairs={{0,2},{1,3},{2,0},{3,1},{4,6},{5,7},{6,4},{7,5},{8,10},{9,11},{10,... | collective-permute-start | bytes 497672 | tf_op jit(solution)/shard_map/ppermute | solution.py:287
  45.0 1.5 %collective-permute-start.19 = (bf16[72,1152]{1,0:T(8,128)(2,1)S(1)}, bf16[72,1152]{1,0:T(8,128)(2,1)S(1)}, u32[]{:S(2)}, u32[]{:S(2)}) collective-permute-start(bf16[72,1152]{1,0:T(8,128)(2,1)S(1)} %get-tuple-element.105), channel_id=1, source_target_pairs={{0,4},{4,0},{8,12},{12,8},{16,20},{20,16},{24,28},{28,24},{1,5},{5... | collective-permute-start | bytes 497672 | tf_op jit(solution)/shard_map/ppermute | solution.py:287
  47.0 1.5 %collective-permute-start.21 = (bf16[72,1152]{1,0:T(8,128)(2,1)S(1)}, bf16[72,1152]{1,0:T(8,128)(2,1)S(1)}, u32[]{:S(2)}, u32[]{:S(2)}) collective-permute-start(bf16[72,1152]{1,0:T(8,128)(2,1)S(1)} %get-tuple-element.109), channel_id=1, source_target_pairs={{0,12},{4,8},{8,4},{12,0},{16,28},{20,24},{24,20},{28,16},{1,13},{... | collective-permute-start | bytes 497672 | tf_op jit(solution)/shard_map/ppermute | solution.py:287
  49.0 2.7 %collective-permute-start.15 = (bf16[72,1152]{1,0:T(8,128)(2,1)S(1)}, bf16[72,1152]{1,0:T(8,128)(2,1)S(1)}, u32[]{:S(2)}, u32[]{:S(2)}) collective-permute-start(bf16[72,1152]{1,0:T(8,128)(2,1)S(1)} %add_convert_fusion.3), channel_id=1, source_target_pairs={{0,16},{4,20},{8,24},{12,28},{16,0},{20,4},{24,8},{28,12},{1,17},{... | collective-permute-start | bytes 497672 | tf_op jit(solution)/shard_map/ppermute | solution.py:287
  51.6 2.0 %shard_map.83 = f32[256,1152]{1,0:T(8,128)} custom-call(bf16[512,1152]{1,0:T(8,128)(2,1)S(1)} %get-tuple-element.103.back, bf16[1152,1152]{1,0:T(8,128)(2,1)S(1)} %get-tuple-element.67.refs_5_.head), custom_call_target="tpu_custom_call" | custom-call | flops 1358954496 | tf_op jit(solution)/shard_map/pallas_call | solution.py:274
  53.7 2.0 %shard_map.82 = f32[256,1152]{1,0:T(8,128)} custom-call(bf16[512,1152]{1,0:T(8,128)(2,1)S(1)} %get-tuple-element.102.back, bf16[1152,1152]{1,0:T(8,128)(2,1)S(1)} %get-tuple-element.78.image_head.head), custom_call_target="tpu_custom_call" | custom-call | flops 1358954496 | tf_op jit(solution)/shard_map/pallas_call | solution.py:274
  55.7 2.5 %collective-permute-done.21 = bf16[72,1152]{1,0:T(8,128)(2,1)S(1)} collective-permute-done((bf16[72,1152]{1,0:T(8,128)(2,1)S(1)}, bf16[72,1152]{1,0:T(8,128)(2,1)S(1)}, u32[]{:S(2)}, u32[]{:S(2)}) %collective-permute-start.21) | collective-permute-done | bytes 165920 | tf_op jit(solution)/shard_map/ppermute | solution.py:287
  58.3 1.3 %collective-permute-start.22 = (bf16[72,1152]{1,0:T(8,128)(2,1)S(1)}, bf16[72,1152]{1,0:T(8,128)(2,1)S(1)}, u32[]{:S(2)}, u32[]{:S(2)}) collective-permute-start(bf16[72,1152]{1,0:T(8,128)(2,1)S(1)} %add_convert_fusion.1), channel_id=1, source_target_pairs={{0,16},{4,20},{8,24},{12,28},{16,0},{20,4},{24,8},{28,12},{1,17},{... | collective-permute-start | bytes 497672 | tf_op jit(solution)/shard_map/ppermute | solution.py:287
  59.7 1.9 %collective-permute-start.16 = (bf16[72,1152]{1,0:T(8,128)(2,1)S(1)}, bf16[72,1152]{1,0:T(8,128)(2,1)S(1)}, u32[]{:S(2)}, u32[]{:S(2)}) collective-permute-start(bf16[72,1152]{1,0:T(8,128)(2,1)S(1)} %add_convert_fusion.2.refs_0_), channel_id=1, source_target_pairs={{0,4},{4,0},{8,12},{12,8},{16,20},{20,16},{24,28},{28,24},{1,5},{5... | collective-permute-start | bytes 497672 | tf_op jit(solution)/shard_map/ppermute | solution.py:287
  61.6 2.1 %collective-permute-start.17 = (bf16[72,1152]{1,0:T(8,128)(2,1)S(1)}, bf16[72,1152]{1,0:T(8,128)(2,1)S(1)}, u32[]{:S(2)}, u32[]{:S(2)}) collective-permute-start(bf16[72,1152]{1,0:T(8,128)(2,1)S(1)} %add_convert_fusion.2.refs_0_), channel_id=1, source_target_pairs={{0,8},{4,12},{8,0},{12,4},{16,24},{20,28},{24,16},{28,20},{1,9},{5... | collective-permute-start | bytes 497672 | tf_op jit(solution)/shard_map/ppermute | solution.py:287
  63.8 2.8 %collective-permute-done.22 = bf16[72,1152]{1,0:T(8,128)(2,1)S(1)} collective-permute-done((bf16[72,1152]{1,0:T(8,128)(2,1)S(1)}, bf16[72,1152]{1,0:T(8,128)(2,1)S(1)}, u32[]{:S(2)}, u32[]{:S(2)}) %collective-permute-start.22) | collective-permute-done | bytes 165920 | tf_op jit(solution)/shard_map/ppermute | solution.py:287
  66.6 3.3 %collective-permute-done.17.refs_2_ = bf16[72,1152]{1,0:T(8,128)(2,1)S(1)} collective-permute-done((bf16[72,1152]{1,0:T(8,128)(2,1)S(1)}, bf16[72,1152]{1,0:T(8,128)(2,1)S(1)}, u32[]{:S(2)}, u32[]{:S(2)}) %collective-permute-start.17) | collective-permute-done | bytes 165920 | tf_op jit(solution)/shard_map/ppermute | solution.py:287
  69.9 1.3 %collective-permute-start.18 = (bf16[72,1152]{1,0:T(8,128)(2,1)S(1)}, bf16[72,1152]{1,0:T(8,128)(2,1)S(1)}, u32[]{:S(2)}, u32[]{:S(2)}) collective-permute-start(bf16[72,1152]{1,0:T(8,128)(2,1)S(1)} %collective-permute-done.17.refs_2_), channel_id=1, source_target_pairs={{0,4},{4,0},{8,12},{12,8},{16,20},{20,16},{24,28},{28,24},{1,5},{5... | collective-permute-start | bytes 497672 | tf_op jit(solution)/shard_map/ppermute | solution.py:287
  72.0 1.4 %collective-permute-start.24 = (bf16[72,1152]{1,0:T(8,128)(2,1)S(1)}, bf16[72,1152]{1,0:T(8,128)(2,1)S(1)}, u32[]{:S(2)}, u32[]{:S(2)}) collective-permute-start(bf16[72,1152]{1,0:T(8,128)(2,1)S(1)} %add_convert_fusion.refs_0_), channel_id=1, source_target_pairs={{0,8},{4,12},{8,0},{12,4},{16,24},{20,28},{24,16},{28,20},{1,9},{5... | collective-permute-start | bytes 497672 | tf_op jit(solution)/shard_map/ppermute | solution.py:287
  73.4 1.4 %collective-permute-start.25 = (bf16[72,1152]{1,0:T(8,128)(2,1)S(1)}, bf16[72,1152]{1,0:T(8,128)(2,1)S(1)}, u32[]{:S(2)}, u32[]{:S(2)}) collective-permute-start(bf16[72,1152]{1,0:T(8,128)(2,1)S(1)} %add_convert_fusion.refs_0_), channel_id=1, source_target_pairs={{0,12},{4,8},{8,4},{12,0},{16,28},{20,24},{24,20},{28,16},{1,13},{... | collective-permute-start | bytes 497672 | tf_op jit(solution)/shard_map/ppermute | solution.py:287
  75.2 1.7 %shard_map.84 = f32[288,1152]{1,0:T(8,128)} custom-call(s32[2]{0:T(128)S(1)} %pad_add_fusion.place, bf16[72,1152]{1,0:T(8,128)(2,1)S(1)} %add_convert_fusion.2.refs_0_, bf16[72,1152]{1,0:T(8,128)(2,1)S(1)} %collective-permute-done.16.refs_1_, bf16[72,1152]{1,0:T(8,128)(2,1)S(1)} %collective-permute-done.17.refs_2_, ...), custom_call_target="tpu_custom_call" | custom-call | tf_op jit(solution)/shard_map/pallas_call | solution.py:274
  77.4 2.5 %collective-permute-done.25.refs_3_ = bf16[72,1152]{1,0:T(8,128)(2,1)S(1)} collective-permute-done((bf16[72,1152]{1,0:T(8,128)(2,1)S(1)}, bf16[72,1152]{1,0:T(8,128)(2,1)S(1)}, u32[]{:S(2)}, u32[]{:S(2)}) %collective-permute-start.25) | collective-permute-done | bytes 165920 | tf_op jit(solution)/shard_map/ppermute | solution.py:287
  79.9 1.7 %shard_map.85 = f32[288,1152]{1,0:T(8,128)} custom-call(s32[2]{0:T(128)S(1)} %pad_add_fusion.place, bf16[72,1152]{1,0:T(8,128)(2,1)S(1)} %add_convert_fusion.refs_0_, bf16[72,1152]{1,0:T(8,128)(2,1)S(1)} %collective-permute-done.23.refs_1_, bf16[72,1152]{1,0:T(8,128)(2,1)S(1)} %collective-permute-done.24.refs_2_, ...), custom_call_target="tpu_custom_call" | custom-call | tf_op jit(solution)/shard_map/pallas_call | solution.py:274
  (40 shorter events, 6.8 us)
Async XLA Ops:
  0.7 3.5 %collective-permute-start.1 = (bf16[256,1152]{1,0:T(8,128)(2,1)}, bf16[256,1152]{1,0:T(8,128)(2,1)S(1)}, u32[]{:S(2)}, u32[]{:S(2)}) collective-permute-start(bf16[256,1152]{1,0:T(8,128)(2,1)} %t0_far), channel_id=1, source_target_pairs={{0,1},{1,0},{2,3},{3,2},{4,5},{5,4},{6,7},{7,6},{8,9},{9,8},{10,11... | collective-permute-start | bytes 1769480 | tf_op jit(solution)/shard_map/ppermute | solution.py:287
  1.2 3.0 %collective-permute-start.2 = (bf16[256,1152]{1,0:T(8,128)(2,1)}, bf16[256,1152]{1,0:T(8,128)(2,1)S(1)}, u32[]{:S(2)}, u32[]{:S(2)}) collective-permute-start(bf16[256,1152]{1,0:T(8,128)(2,1)} %i0_far), channel_id=1, source_target_pairs={{0,1},{1,0},{2,3},{3,2},{4,5},{5,4},{6,7},{7,6},{8,9},{9,8},{10,11... | collective-permute-start | bytes 1769480 | tf_op jit(solution)/shard_map/ppermute | solution.py:287
  1.3 17.2 %collective-permute-start = (bf16[256,1152]{1,0:T(8,128)(2,1)}, bf16[256,1152]{1,0:T(8,128)(2,1)S(1)}, u32[]{:S(2)}, u32[]{:S(2)}) collective-permute-start(bf16[256,1152]{1,0:T(8,128)(2,1)} %t0_far), channel_id=1, source_target_pairs={{0,2},{1,3},{2,0},{3,1},{4,6},{5,7},{6,4},{7,5},{8,10},{9,11},{10,... | collective-permute-start | bytes 1769480 | tf_op jit(solution)/shard_map/ppermute | solution.py:287
  4.2 27.5 %collective-permute-start.8 = (bf16[256,1152]{1,0:T(8,128)(2,1)}, bf16[256,1152]{1,0:T(8,128)(2,1)S(1)}, u32[]{:S(2)}, u32[]{:S(2)}) collective-permute-start(bf16[256,1152]{1,0:T(8,128)(2,1)} %i0_far), channel_id=1, source_target_pairs={{0,2},{1,3},{2,0},{3,1},{4,6},{5,7},{6,4},{7,5},{8,10},{9,11},{10,... | collective-permute-start | bytes 1769480 | tf_op jit(solution)/shard_map/ppermute | solution.py:287
  18.5 1.4 %collective-permute-start.3 = (bf16[64,1152]{1,0:T(8,128)(2,1)S(1)}, bf16[64,1152]{1,0:T(8,128)(2,1)S(1)}, u32[]{:S(2)}, u32[]{:S(2)}) collective-permute-start(bf16[64,1152]{1,0:T(8,128)(2,1)S(1)} %get-tuple-element.115), channel_id=1, source_target_pairs={{0,1},{1,0},{2,3},{3,2},{4,5},{5,4},{6,7},{7,6},{8,9},{9,8},{10,11... | collective-permute-start | bytes 442376 | tf_op jit(solution)/shard_map/ppermute | solution.py:287
  18.6 1.6 %collective-permute-start.4 = (bf16[64,1152]{1,0:T(8,128)(2,1)S(1)}, bf16[64,1152]{1,0:T(8,128)(2,1)S(1)}, u32[]{:S(2)}, u32[]{:S(2)}) collective-permute-start(bf16[64,1152]{1,0:T(8,128)(2,1)S(1)} %get-tuple-element.114), channel_id=1, source_target_pairs={{0,1},{1,0},{2,3},{3,2},{4,5},{5,4},{6,7},{7,6},{8,9},{9,8},{10,11... | collective-permute-start | bytes 442376 | tf_op jit(solution)/shard_map/ppermute | solution.py:287
  19.1 1.4 %collective-permute-start.5 = (bf16[64,1152]{1,0:T(8,128)(2,1)S(1)}, bf16[64,1152]{1,0:T(8,128)(2,1)S(1)}, u32[]{:S(2)}, u32[]{:S(2)}) collective-permute-start(bf16[64,1152]{1,0:T(8,128)(2,1)S(1)} %get-tuple-element.113), channel_id=1, source_target_pairs={{0,1},{1,0},{2,3},{3,2},{4,5},{5,4},{6,7},{7,6},{8,9},{9,8},{10,11... | collective-permute-start | bytes 442376 | tf_op jit(solution)/shard_map/ppermute | solution.py:287
  19.2 1.5 %collective-permute-start.6 = (bf16[64,1152]{1,0:T(8,128)(2,1)S(1)}, bf16[64,1152]{1,0:T(8,128)(2,1)S(1)}, u32[]{:S(2)}, u32[]{:S(2)}) collective-permute-start(bf16[64,1152]{1,0:T(8,128)(2,1)S(1)} %get-tuple-element.112), channel_id=1, source_target_pairs={{0,1},{1,0},{2,3},{3,2},{4,5},{5,4},{6,7},{7,6},{8,9},{9,8},{10,11... | collective-permute-start | bytes 442376 | tf_op jit(solution)/shard_map/ppermute | solution.py:287
  25.9 10.4 %collective-permute-start.7 = (bf16[144,1152]{1,0:T(8,128)(2,1)S(1)}, bf16[144,1152]{1,0:T(8,128)(2,1)S(1)}, u32[]{:S(2)}, u32[]{:S(2)}) collective-permute-start(bf16[144,1152]{1,0:T(8,128)(2,1)S(1)} %get-tuple-element.73), channel_id=1, source_target_pairs={{0,4},{4,0},{8,12},{12,8},{16,20},{20,16},{24,28},{28,24},{1,5},{5... | collective-permute-start | bytes 995336 | tf_op jit(solution)/shard_map/ppermute | solution.py:287
  28.1 9.7 %collective-permute-start.11 = (bf16[144,1152]{1,0:T(8,128)(2,1)S(1)}, bf16[144,1152]{1,0:T(8,128)(2,1)S(1)}, u32[]{:S(2)}, u32[]{:S(2)}) collective-permute-start(bf16[144,1152]{1,0:T(8,128)(2,1)S(1)} %get-tuple-element.89), channel_id=1, source_target_pairs={{0,8},{4,12},{8,0},{12,4},{16,24},{20,28},{24,16},{28,20},{1,9},{5... | collective-permute-start | bytes 995336 | tf_op jit(solution)/shard_map/ppermute | solution.py:287
  33.6 6.5 %collective-permute-start.12 = (bf16[128,1152]{1,0:T(8,128)(2,1)S(1)}, bf16[128,1152]{1,0:T(8,128)(2,1)S(1)}, u32[]{:S(2)}, u32[]{:S(2)}) collective-permute-start(bf16[128,1152]{1,0:T(8,128)(2,1)S(1)} %get-tuple-element.82.x_second), channel_id=1, source_target_pairs={{0,1},{1,0},{2,3},{3,2},{4,5},{5,4},{6,7},{7,6},{8,9},{9,8},{10,11... | collective-permute-start | bytes 884744 | tf_op jit(solution)/shard_map/ppermute | solution.py:287
  33.7 6.4 %collective-permute-start.10 = (bf16[128,1152]{1,0:T(8,128)(2,1)S(1)}, bf16[128,1152]{1,0:T(8,128)(2,1)S(1)}, u32[]{:S(2)}, u32[]{:S(2)}) collective-permute-start(bf16[128,1152]{1,0:T(8,128)(2,1)S(1)} %get-tuple-element.81.x_first), channel_id=1, source_target_pairs={{0,1},{1,0},{2,3},{3,2},{4,5},{5,4},{6,7},{7,6},{8,9},{9,8},{10,11... | collective-permute-start | bytes 884744 | tf_op jit(solution)/shard_map/ppermute | solution.py:287
  37.8 5.6 %collective-permute-start.13 = (bf16[72,1152]{1,0:T(8,128)(2,1)S(1)}, bf16[72,1152]{1,0:T(8,128)(2,1)S(1)}, u32[]{:S(2)}, u32[]{:S(2)}) collective-permute-start(bf16[72,1152]{1,0:T(8,128)(2,1)S(1)} %add_convert_fusion.6), channel_id=1, source_target_pairs={{0,4},{4,0},{8,12},{12,8},{16,20},{20,16},{24,28},{28,24},{1,5},{5... | collective-permute-start | bytes 497672 | tf_op jit(solution)/shard_map/ppermute | solution.py:287
  38.3 10.2 %collective-permute-start.9 = (bf16[72,1152]{1,0:T(8,128)(2,1)S(1)}, bf16[72,1152]{1,0:T(8,128)(2,1)S(1)}, u32[]{:S(2)}, u32[]{:S(2)}) collective-permute-start(bf16[72,1152]{1,0:T(8,128)(2,1)S(1)} %add_convert_fusion.7), channel_id=1, source_target_pairs={{0,8},{4,12},{8,0},{12,4},{16,24},{20,28},{24,16},{28,20},{1,9},{5... | collective-permute-start | bytes 497672 | tf_op jit(solution)/shard_map/ppermute | solution.py:287
  43.5 5.4 %collective-permute-start.14 = (bf16[72,1152]{1,0:T(8,128)(2,1)S(1)}, bf16[72,1152]{1,0:T(8,128)(2,1)S(1)}, u32[]{:S(2)}, u32[]{:S(2)}) collective-permute-start(bf16[72,1152]{1,0:T(8,128)(2,1)S(1)} %add_convert_fusion.4), channel_id=1, source_target_pairs={{0,2},{1,3},{2,0},{3,1},{4,6},{5,7},{6,4},{7,5},{8,10},{9,11},{10,... | collective-permute-start | bytes 497672 | tf_op jit(solution)/shard_map/ppermute | solution.py:287
  45.0 10.7 %collective-permute-start.19 = (bf16[72,1152]{1,0:T(8,128)(2,1)S(1)}, bf16[72,1152]{1,0:T(8,128)(2,1)S(1)}, u32[]{:S(2)}, u32[]{:S(2)}) collective-permute-start(bf16[72,1152]{1,0:T(8,128)(2,1)S(1)} %get-tuple-element.105), channel_id=1, source_target_pairs={{0,4},{4,0},{8,12},{12,8},{16,20},{20,16},{24,28},{28,24},{1,5},{5... | collective-permute-start | bytes 497672 | tf_op jit(solution)/shard_map/ppermute | solution.py:287
  46.6 9.2 %collective-permute-start.20 = (bf16[72,1152]{1,0:T(8,128)(2,1)S(1)}, bf16[72,1152]{1,0:T(8,128)(2,1)S(1)}, u32[]{:S(2)}, u32[]{:S(2)}) collective-permute-start(bf16[72,1152]{1,0:T(8,128)(2,1)S(1)} %get-tuple-element.107), channel_id=1, source_target_pairs={{0,8},{4,12},{8,0},{12,4},{16,24},{20,28},{24,16},{28,20},{1,9},{5... | collective-permute-start | bytes 497672 | tf_op jit(solution)/shard_map/ppermute | solution.py:287
  47.0 11.2 %collective-permute-start.21 = (bf16[72,1152]{1,0:T(8,128)(2,1)S(1)}, bf16[72,1152]{1,0:T(8,128)(2,1)S(1)}, u32[]{:S(2)}, u32[]{:S(2)}) collective-permute-start(bf16[72,1152]{1,0:T(8,128)(2,1)S(1)} %get-tuple-element.109), channel_id=1, source_target_pairs={{0,12},{4,8},{8,4},{12,0},{16,28},{20,24},{24,20},{28,16},{1,13},{... | collective-permute-start | bytes 497672 | tf_op jit(solution)/shard_map/ppermute | solution.py:287
  49.0 10.7 %collective-permute-start.15 = (bf16[72,1152]{1,0:T(8,128)(2,1)S(1)}, bf16[72,1152]{1,0:T(8,128)(2,1)S(1)}, u32[]{:S(2)}, u32[]{:S(2)}) collective-permute-start(bf16[72,1152]{1,0:T(8,128)(2,1)S(1)} %add_convert_fusion.3), channel_id=1, source_target_pairs={{0,16},{4,20},{8,24},{12,28},{16,0},{20,4},{24,8},{28,12},{1,17},{... | collective-permute-start | bytes 497672 | tf_op jit(solution)/shard_map/ppermute | solution.py:287
  58.3 8.2 %collective-permute-start.22 = (bf16[72,1152]{1,0:T(8,128)(2,1)S(1)}, bf16[72,1152]{1,0:T(8,128)(2,1)S(1)}, u32[]{:S(2)}, u32[]{:S(2)}) collective-permute-start(bf16[72,1152]{1,0:T(8,128)(2,1)S(1)} %add_convert_fusion.1), channel_id=1, source_target_pairs={{0,16},{4,20},{8,24},{12,28},{16,0},{20,4},{24,8},{28,12},{1,17},{... | collective-permute-start | bytes 497672 | tf_op jit(solution)/shard_map/ppermute | solution.py:287
  59.7 6.8 %collective-permute-start.16 = (bf16[72,1152]{1,0:T(8,128)(2,1)S(1)}, bf16[72,1152]{1,0:T(8,128)(2,1)S(1)}, u32[]{:S(2)}, u32[]{:S(2)}) collective-permute-start(bf16[72,1152]{1,0:T(8,128)(2,1)S(1)} %add_convert_fusion.2.refs_0_), channel_id=1, source_target_pairs={{0,4},{4,0},{8,12},{12,8},{16,20},{20,16},{24,28},{28,24},{1,5},{5... | collective-permute-start | bytes 497672 | tf_op jit(solution)/shard_map/ppermute | solution.py:287
  61.6 8.2 %collective-permute-start.17 = (bf16[72,1152]{1,0:T(8,128)(2,1)S(1)}, bf16[72,1152]{1,0:T(8,128)(2,1)S(1)}, u32[]{:S(2)}, u32[]{:S(2)}) collective-permute-start(bf16[72,1152]{1,0:T(8,128)(2,1)S(1)} %add_convert_fusion.2.refs_0_), channel_id=1, source_target_pairs={{0,8},{4,12},{8,0},{12,4},{16,24},{20,28},{24,16},{28,20},{1,9},{5... | collective-permute-start | bytes 497672 | tf_op jit(solution)/shard_map/ppermute | solution.py:287
  69.9 5.3 %collective-permute-start.18 = (bf16[72,1152]{1,0:T(8,128)(2,1)S(1)}, bf16[72,1152]{1,0:T(8,128)(2,1)S(1)}, u32[]{:S(2)}, u32[]{:S(2)}) collective-permute-start(bf16[72,1152]{1,0:T(8,128)(2,1)S(1)} %collective-permute-done.17.refs_2_), channel_id=1, source_target_pairs={{0,4},{4,0},{8,12},{12,8},{16,20},{20,16},{24,28},{28,24},{1,5},{5... | collective-permute-start | bytes 497672 | tf_op jit(solution)/shard_map/ppermute | solution.py:287
  71.2 5.8 %collective-permute-start.23 = (bf16[72,1152]{1,0:T(8,128)(2,1)S(1)}, bf16[72,1152]{1,0:T(8,128)(2,1)S(1)}, u32[]{:S(2)}, u32[]{:S(2)}) collective-permute-start(bf16[72,1152]{1,0:T(8,128)(2,1)S(1)} %add_convert_fusion.refs_0_), channel_id=1, source_target_pairs={{0,4},{4,0},{8,12},{12,8},{16,20},{20,16},{24,28},{28,24},{1,5},{5... | collective-permute-start | bytes 497672 | tf_op jit(solution)/shard_map/ppermute | solution.py:287
  72.0 5.3 %collective-permute-start.24 = (bf16[72,1152]{1,0:T(8,128)(2,1)S(1)}, bf16[72,1152]{1,0:T(8,128)(2,1)S(1)}, u32[]{:S(2)}, u32[]{:S(2)}) collective-permute-start(bf16[72,1152]{1,0:T(8,128)(2,1)S(1)} %add_convert_fusion.refs_0_), channel_id=1, source_target_pairs={{0,8},{4,12},{8,0},{12,4},{16,24},{20,28},{24,16},{28,20},{1,9},{5... | collective-permute-start | bytes 497672 | tf_op jit(solution)/shard_map/ppermute | solution.py:287
  73.4 6.5 %collective-permute-start.25 = (bf16[72,1152]{1,0:T(8,128)(2,1)S(1)}, bf16[72,1152]{1,0:T(8,128)(2,1)S(1)}, u32[]{:S(2)}, u32[]{:S(2)}) collective-permute-start(bf16[72,1152]{1,0:T(8,128)(2,1)S(1)} %add_convert_fusion.refs_0_), channel_id=1, source_target_pairs={{0,12},{4,8},{8,4},{12,0},{16,28},{20,24},{24,20},{28,16},{1,13},{... | collective-permute-start | bytes 497672 | tf_op jit(solution)/shard_map/ppermute | solution.py:287

commit v16 on v15

--- a/solution.py
+++ b/solution.py
@@ -307,6 +307,10 @@
     def add(own, others):
         return sum((other.astype(F32) for other in others), own.astype(F32)).astype(BF16)
 
+    def placed(pieces):
+        outs = [((rows_out, width), F32)]
+        return call(place_kernel, outs, [], pieces, 4, place, keep=False)[0]
+
     def spread(total):
         return [total] + [cuts(total, mask=k) for k in range(1, QUAD)]
 
@@ -395,12 +399,10 @@
     text_sum = add(text_parts[0], [after(other, (image_sum, grads)) for other in text_others])
     image_sum = add(image_sum, [cuts(image_sum, mask=QUAD)])
     image_pieces = [image_sum, cuts(image_sum, mask=1), cuts(image_sum, mask=2)]
-    image_pieces.append(cuts(image_pieces[2], mask=1))
     text_sum = add(text_sum, [after(cuts(text_sum, mask=QUAD), image_pieces[1])])
-    image_out, text_out = (
-        call(place_kernel, [((rows_out, width), F32)], [], pieces, 4, place, keep=False)[0]
-        for pieces in (image_pieces, spread(text_sum))
-    )
+    text_out = placed(spread(text_sum))
+    image_pieces.append(after(cuts(image_pieces[2], mask=1), text_out))
+    image_out = placed(image_pieces)
     return (*grads, image_out, text_out)
 
 

time: 81.7 us -> 82.4 us (level)
  starting transfers between devices: 29 us -> 31.8 us
  waiting for transfers between devices: 20.5 us -> 18.4 us
    ppermute x26, starting transfers between devices: 29 us -> 31.8 us  [swap(): return lax.ppermute(array, axis, [(i, i ^ mask) for i in range(size)])]
    ppermute x26, waiting for transfers between devices: 20.5 us -> 18.4 us  [swap(): return lax.ppermute(array, axis, [(i, i ^ mask) for i in range(size)])]
  transfers between devices with their start and end apart: 26 -> 26, of which waited for: 15 -> 12; matrix products, arithmetic and copies ran while one was open for 1% -> 1% of each run, Pallas kernels for 36% -> 35%
where the time goes in v16:
time: 82.4 us; the launch traced here: 82.3 us
  starting transfers between devices  31.8 us (39%)
  Pallas kernels  30.7 us (37%)
  waiting for transfers between devices  18.4 us (22%)
    ppermute x26, starting transfers between devices, swap(): return lax.ppermute(array, axis, [(i, i ^ mask) for i in range(size)])  31.8 us
    pallas_call x11, Pallas kernels, call(): pl.pallas_call(kernel, out_shape=[shape(s, t) for s, t in outs], in_specs...  30.7 us
    ppermute x26, waiting for transfers between devices, swap(): return lax.ppermute(array, axis, [(i, i ^ mask) for i in range(size)])  18.4 us
  transfers between devices with their start and end apart: 26, of which 12 were waited for; matrix products, arithmetic and copies ran while one was open for 1% of the time, Pallas kernels for 35%

profile of v16, /device:TPU:0, one launch (start us, length us, event | category | flops | bytes accessed | tf_op | source)
XLA Modules:
  0.0 82.3 jit_solution(6814178600978264146)
XLA Ops:
  1.3 2.9 %collective-permute-start = (bf16[256,1152]{1,0:T(8,128)(2,1)}, bf16[256,1152]{1,0:T(8,128)(2,1)S(1)}, u32[]{:S(2)}, u32[]{:S(2)}) collective-permute-start(bf16[256,1152]{1,0:T(8,128)(2,1)} %t0_far), channel_id=1, source_target_pairs={{0,2},{1,3},{2,0},{3,1},{4,6},{5,7},{6,4},{7,5},{8,10},{9,11},{10,... | collective-permute-start | bytes 1769480 | tf_op jit(solution)/shard_map/ppermute | solution.py:287
  4.2 7.4 %shard_map.75 = (f32[512,1152]{1,0:T(8,128)S(1)}, bf16[512,1152]{1,0:T(8,128)(2,1)S(1)}, f32[512,1152]{1,0:T(8,128)S(1)}, bf16[512,1152]{1,0:T(8,128)(2,1)S(1)},...) custom-call(bf16[256,1152]{1,0:T(8,128)(2,1)S(1)} %collective-permut, ...), custom_call_target="tpu_custom_call" | custom-call | tf_op jit(solution)/shard_map/pallas_call | solution.py:274
  11.6 2.6 %shard_map.76 = (f32[512,1152]{1,0:T(8,128)S(1)}, bf16[576,512]{1,0:T(8,128)(2,1)S(1)}, bf16[288,512]{1,0:T(8,128)(2,1)S(1)}) custom-call(s32[2]{0:T(128)S(1)} %pad_add_fusion.place, bf16[256,1152]{1,0:T(8,128)(2,1)S(1)} %get-tuple-element.62.t0, bf16[256,1152]{1,0:T(8,128)(2,1)S(1)} %collective-permute-done.1.t1, ...), custom_call_target="tpu_custom_call" | custom-call | tf_op jit(solution)/shard_map/pallas_call | solution.py:274
  14.2 4.3 %collective-permute-done.refs_0_ = bf16[256,1152]{1,0:T(8,128)(2,1)S(1)} collective-permute-done((bf16[256,1152]{1,0:T(8,128)(2,1)}, bf16[256,1152]{1,0:T(8,128)(2,1)S(1)}, u32[]{:S(2)}, u32[]{:S(2)}) %collective-permute-start) | collective-permute-done | bytes 589856 | tf_op jit(solution)/shard_map/ppermute | solution.py:287
  20.7 5.2 %shard_map.77 = (f32[512,1152]{1,0:T(8,128)S(1)}, bf16[512,1152]{1,0:T(8,128)(2,1)S(1)}, bf16[512,512]{1,0:T(8,128)(2,1)S(1)}, bf16[512,1152]{1,0:T(8,128)(2,1)S...) custom-call(bf16[256,1152]{1,0:T(8,128)(2,1)S(1)} %collective-permut, ...), custom_call_target="tpu_custom_call" | custom-call | tf_op jit(solution)/shard_map/pallas_call | solution.py:274
  25.9 2.2 %collective-permute-start.7 = (bf16[144,1152]{1,0:T(8,128)(2,1)S(1)}, bf16[144,1152]{1,0:T(8,128)(2,1)S(1)}, u32[]{:S(2)}, u32[]{:S(2)}) collective-permute-start(bf16[144,1152]{1,0:T(8,128)(2,1)S(1)} %get-tuple-element.74), channel_id=1, source_target_pairs={{0,4},{4,0},{8,12},{12,8},{16,20},{20,16},{24,28},{28,24},{1,5},{5... | collective-permute-start | bytes 995336 | tf_op jit(solution)/shard_map/ppermute | solution.py:287
  28.1 1.6 %collective-permute-start.11 = (bf16[144,1152]{1,0:T(8,128)(2,1)S(1)}, bf16[144,1152]{1,0:T(8,128)(2,1)S(1)}, u32[]{:S(2)}, u32[]{:S(2)}) collective-permute-start(bf16[144,1152]{1,0:T(8,128)(2,1)S(1)} %get-tuple-element.90), channel_id=1, source_target_pairs={{0,8},{4,12},{8,0},{12,4},{16,24},{20,28},{24,16},{28,20},{1,9},{5... | collective-permute-start | bytes 995336 | tf_op jit(solution)/shard_map/ppermute | solution.py:287
  29.6 2.0 %shard_map.78 = (f32[512,1152]{1,0:T(8,128)S(1)}, bf16[288,512]{1,0:T(8,128)(2,1)S(1)}) custom-call(s32[2]{0:T(128)S(1)} %pad_add_fusion.place, bf16[256,1152]{1,0:T(8,128)(2,1)S(1)} %collective-permute-done.refs_0_, bf16[64,1152]{1,0:T(8,128)(2,1)S(1)} %collective-permute-done.3.refs_1_, bf16[64,1152]{1,0:T(8,128)(2,1)S(1)} %collective-permute-done.4.refs_2_, ...), custom_call_target="tpu_custom_call" | custom-call | tf_op jit(solution)/shard_map/pallas_call | solution.py:274
  31.7 1.9 %shard_map.79 = (bf16[128,1152]{1,0:T(8,128)(2,1)S(1)}, bf16[128,1152]{1,0:T(8,128)(2,1)S(1)}, bf16[256,512]{1,0:T(8,128)(2,1)S(1)}, bf16[256,512]{1,0:T(8,128)(2,1)S(1)}) custom-call(bf16[256,1152]{1,0:T(8,128)(2,1)S(1)} %collective-permute-done.8.i2, bf16[1152,1152]{1,0:T(8,128)(2,1)S(1)} %get-tuple-element.79.image_head.head, ...), custom_call_target="tpu_custom_call" | custom-call | tf_op jit(solution)/shard_map/pallas_call | solution.py:274
  34.2 0.9 %shard_map.80 = (f32[512,1152]{1,0:T(8,128)S(1)}, f32[512,1152]{1,0:T(8,128)S(1)}) custom-call(bf16[128,1152]{1,0:T(8,128)(2,1)S(1)} %get-tuple-element.82.x_first, bf16[128,1152]{1,0:T(8,128)(2,1)S(1)} %get-tuple-element.83.x_second, bf16[256,512]{1,0:T(8,128)(2,1)S(1)} %get-tuple-element.84.w_a, bf16[256,512]{1,0:T(8,128)(2,1)S(1)} %get-tuple-element.85.w_b, ...), custom_call_target="tpu_custom_call" | custom-call | tf_op jit(solution)/shard_map/pallas_call | solution.py:274
  35.0 1.3 %collective-permute-done.7 = bf16[144,1152]{1,0:T(8,128)(2,1)S(1)} collective-permute-done((bf16[144,1152]{1,0:T(8,128)(2,1)S(1)}, bf16[144,1152]{1,0:T(8,128)(2,1)S(1)}, u32[]{:S(2)}, u32[]{:S(2)}) %collective-permute-start.7) | collective-permute-done | bytes 331808 | tf_op jit(solution)/shard_map/ppermute | solution.py:287
  36.3 1.5 %collective-permute-done.11 = bf16[144,1152]{1,0:T(8,128)(2,1)S(1)} collective-permute-done((bf16[144,1152]{1,0:T(8,128)(2,1)S(1)}, bf16[144,1152]{1,0:T(8,128)(2,1)S(1)}, u32[]{:S(2)}, u32[]{:S(2)}) %collective-permute-start.11) | collective-permute-done | bytes 331808 | tf_op jit(solution)/shard_map/ppermute | solution.py:287
  38.3 1.8 %collective-permute-start.9 = (bf16[72,1152]{1,0:T(8,128)(2,1)S(1)}, bf16[72,1152]{1,0:T(8,128)(2,1)S(1)}, u32[]{:S(2)}, u32[]{:S(2)}) collective-permute-start(bf16[72,1152]{1,0:T(8,128)(2,1)S(1)} %add_convert_fusion.7), channel_id=1, source_target_pairs={{0,8},{4,12},{8,0},{12,4},{16,24},{20,28},{24,16},{28,20},{1,9},{5... | collective-permute-start | bytes 497672 | tf_op jit(solution)/shard_map/ppermute | solution.py:287
  40.1 3.3 %shard_map.81 = (bf16[72,1152]{1,0:T(8,128)(2,1)S(1)}, bf16[72,1152]{1,0:T(8,128)(2,1)S(1)}, bf16[72,1152]{1,0:T(8,128)(2,1)S(1)}, bf16[72,1152]{1,0:T(8,128)(2,1)S(1)}, bf16[512,1152]{1,0:T(8,128)(2,1)S(1)}) custom-call(bf16[128,1152]{1,0:T(8,128)(2,1)S(1)} %collective-permute-done.10.x_first, bf16[128,1152]{1,0:T(8,128)(2,1)S(1)} %collective-permute-done.12.x_second, ...), custom_call_target="tpu_custom_call" | custom-call | tf_op jit(solution)/shard_map/pallas_call | solution.py:274
  43.5 1.6 %collective-permute-start.14 = (bf16[72,1152]{1,0:T(8,128)(2,1)S(1)}, bf16[72,1152]{1,0:T(8,128)(2,1)S(1)}, u32[]{:S(2)}, u32[]{:S(2)}) collective-permute-start(bf16[72,1152]{1,0:T(8,128)(2,1)S(1)} %add_convert_fusion.4), channel_id=1, source_target_pairs={{0,2},{1,3},{2,0},{3,1},{4,6},{5,7},{6,4},{7,5},{8,10},{9,11},{10,... | collective-permute-start | bytes 497672 | tf_op jit(solution)/shard_map/ppermute | solution.py:287
  45.0 1.5 %collective-permute-start.19 = (bf16[72,1152]{1,0:T(8,128)(2,1)S(1)}, bf16[72,1152]{1,0:T(8,128)(2,1)S(1)}, u32[]{:S(2)}, u32[]{:S(2)}) collective-permute-start(bf16[72,1152]{1,0:T(8,128)(2,1)S(1)} %get-tuple-element.106), channel_id=1, source_target_pairs={{0,4},{4,0},{8,12},{12,8},{16,20},{20,16},{24,28},{28,24},{1,5},{5... | collective-permute-start | bytes 497672 | tf_op jit(solution)/shard_map/ppermute | solution.py:287
  47.0 1.5 %collective-permute-start.21 = (bf16[72,1152]{1,0:T(8,128)(2,1)S(1)}, bf16[72,1152]{1,0:T(8,128)(2,1)S(1)}, u32[]{:S(2)}, u32[]{:S(2)}) collective-permute-start(bf16[72,1152]{1,0:T(8,128)(2,1)S(1)} %get-tuple-element.110), channel_id=1, source_target_pairs={{0,12},{4,8},{8,4},{12,0},{16,28},{20,24},{24,20},{28,16},{1,13},{... | collective-permute-start | bytes 497672 | tf_op jit(solution)/shard_map/ppermute | solution.py:287
  49.0 2.7 %collective-permute-start.15 = (bf16[72,1152]{1,0:T(8,128)(2,1)S(1)}, bf16[72,1152]{1,0:T(8,128)(2,1)S(1)}, u32[]{:S(2)}, u32[]{:S(2)}) collective-permute-start(bf16[72,1152]{1,0:T(8,128)(2,1)S(1)} %add_convert_fusion.3), channel_id=1, source_target_pairs={{0,16},{4,20},{8,24},{12,28},{16,0},{20,4},{24,8},{28,12},{1,17},{... | collective-permute-start | bytes 497672 | tf_op jit(solution)/shard_map/ppermute | solution.py:287
  51.6 2.0 %shard_map.83 = f32[256,1152]{1,0:T(8,128)} custom-call(bf16[512,1152]{1,0:T(8,128)(2,1)S(1)} %get-tuple-element.104.back, bf16[1152,1152]{1,0:T(8,128)(2,1)S(1)} %get-tuple-element.68.refs_5_.head), custom_call_target="tpu_custom_call" | custom-call | flops 1358954496 | tf_op jit(solution)/shard_map/pallas_call | solution.py:274
  53.7 2.0 %shard_map.82 = f32[256,1152]{1,0:T(8,128)} custom-call(bf16[512,1152]{1,0:T(8,128)(2,1)S(1)} %get-tuple-element.103.back, bf16[1152,1152]{1,0:T(8,128)(2,1)S(1)} %get-tuple-element.79.image_head.head), custom_call_target="tpu_custom_call" | custom-call | flops 1358954496 | tf_op jit(solution)/shard_map/pallas_call | solution.py:274
  55.7 2.5 %collective-permute-done.21 = bf16[72,1152]{1,0:T(8,128)(2,1)S(1)} collective-permute-done((bf16[72,1152]{1,0:T(8,128)(2,1)S(1)}, bf16[72,1152]{1,0:T(8,128)(2,1)S(1)}, u32[]{:S(2)}, u32[]{:S(2)}) %collective-permute-start.21) | collective-permute-done | bytes 165920 | tf_op jit(solution)/shard_map/ppermute | solution.py:287
  58.3 1.3 %collective-permute-start.22 = (bf16[72,1152]{1,0:T(8,128)(2,1)S(1)}, bf16[72,1152]{1,0:T(8,128)(2,1)S(1)}, u32[]{:S(2)}, u32[]{:S(2)}) collective-permute-start(bf16[72,1152]{1,0:T(8,128)(2,1)S(1)} %add_convert_fusion.1), channel_id=1, source_target_pairs={{0,16},{4,20},{8,24},{12,28},{16,0},{20,4},{24,8},{28,12},{1,17},{... | collective-permute-start | bytes 497672 | tf_op jit(solution)/shard_map/ppermute | solution.py:287
  59.7 1.9 %collective-permute-start.16 = (bf16[72,1152]{1,0:T(8,128)(2,1)S(1)}, bf16[72,1152]{1,0:T(8,128)(2,1)S(1)}, u32[]{:S(2)}, u32[]{:S(2)}) collective-permute-start(bf16[72,1152]{1,0:T(8,128)(2,1)S(1)} %add_convert_fusion.2.refs_0_), channel_id=1, source_target_pairs={{0,4},{4,0},{8,12},{12,8},{16,20},{20,16},{24,28},{28,24},{1,5},{5... | collective-permute-start | bytes 497672 | tf_op jit(solution)/shard_map/ppermute | solution.py:287
  61.6 2.1 %collective-permute-start.17 = (bf16[72,1152]{1,0:T(8,128)(2,1)S(1)}, bf16[72,1152]{1,0:T(8,128)(2,1)S(1)}, u32[]{:S(2)}, u32[]{:S(2)}) collective-permute-start(bf16[72,1152]{1,0:T(8,128)(2,1)S(1)} %add_convert_fusion.2.refs_0_), channel_id=1, source_target_pairs={{0,8},{4,12},{8,0},{12,4},{16,24},{20,28},{24,16},{28,20},{1,9},{5... | collective-permute-start | bytes 497672 | tf_op jit(solution)/shard_map/ppermute | solution.py:287
  63.8 2.8 %collective-permute-done.22 = bf16[72,1152]{1,0:T(8,128)(2,1)S(1)} collective-permute-done((bf16[72,1152]{1,0:T(8,128)(2,1)S(1)}, bf16[72,1152]{1,0:T(8,128)(2,1)S(1)}, u32[]{:S(2)}, u32[]{:S(2)}) %collective-permute-start.22) | collective-permute-done | bytes 165920 | tf_op jit(solution)/shard_map/ppermute | solution.py:287
  66.6 1.3 %collective-permute-start.23 = (bf16[72,1152]{1,0:T(8,128)(2,1)S(1)}, bf16[72,1152]{1,0:T(8,128)(2,1)S(1)}, u32[]{:S(2)}, u32[]{:S(2)}) collective-permute-start(bf16[72,1152]{1,0:T(8,128)(2,1)S(1)} %add_convert_fusion.refs_0_), channel_id=1, source_target_pairs={{0,4},{4,0},{8,12},{12,8},{16,20},{20,16},{24,28},{28,24},{1,5},{5... | collective-permute-start | bytes 497672 | tf_op jit(solution)/shard_map/ppermute | solution.py:287
  67.9 4.4 %collective-permute-start.24 = (bf16[72,1152]{1,0:T(8,128)(2,1)S(1)}, bf16[72,1152]{1,0:T(8,128)(2,1)S(1)}, u32[]{:S(2)}, u32[]{:S(2)}) collective-permute-start(bf16[72,1152]{1,0:T(8,128)(2,1)S(1)} %add_convert_fusion.refs_0_), channel_id=1, source_target_pairs={{0,8},{4,12},{8,0},{12,4},{16,24},{20,28},{24,16},{28,20},{1,9},{5... | collective-permute-start | bytes 497672 | tf_op jit(solution)/shard_map/ppermute | solution.py:287
  72.3 1.4 %collective-permute-start.25 = (bf16[72,1152]{1,0:T(8,128)(2,1)S(1)}, bf16[72,1152]{1,0:T(8,128)(2,1)S(1)}, u32[]{:S(2)}, u32[]{:S(2)}) collective-permute-start(bf16[72,1152]{1,0:T(8,128)(2,1)S(1)} %add_convert_fusion.refs_0_), channel_id=1, source_target_pairs={{0,12},{4,8},{8,4},{12,0},{16,28},{20,24},{24,20},{28,16},{1,13},{... | collective-permute-start | bytes 497672 | tf_op jit(solution)/shard_map/ppermute | solution.py:287
  74.3 1.4 %collective-permute-done.24.refs_2_ = bf16[72,1152]{1,0:T(8,128)(2,1)S(1)} collective-permute-done((bf16[72,1152]{1,0:T(8,128)(2,1)S(1)}, bf16[72,1152]{1,0:T(8,128)(2,1)S(1)}, u32[]{:S(2)}, u32[]{:S(2)}) %collective-permute-start.24) | collective-permute-done | bytes 165920 | tf_op jit(solution)/shard_map/ppermute | solution.py:287
  75.6 3.3 %collective-permute-done.25.refs_3_ = bf16[72,1152]{1,0:T(8,128)(2,1)S(1)} collective-permute-done((bf16[72,1152]{1,0:T(8,128)(2,1)S(1)}, bf16[72,1152]{1,0:T(8,128)(2,1)S(1)}, u32[]{:S(2)}, u32[]{:S(2)}) %collective-permute-start.25) | collective-permute-done | bytes 165920 | tf_op jit(solution)/shard_map/ppermute | solution.py:287
  78.9 1.7 %shard_map.84 = f32[288,1152]{1,0:T(8,128)} custom-call(s32[2]{0:T(128)S(1)} %pad_add_fusion.place, bf16[72,1152]{1,0:T(8,128)(2,1)S(1)} %add_convert_fusion.refs_0_, bf16[72,1152]{1,0:T(8,128)(2,1)S(1)} %collective-permute-done.23.refs_1_, bf16[72,1152]{1,0:T(8,128)(2,1)S(1)} %collective-permute-done.24.refs_2_, ...), custom_call_target="tpu_custom_call" | custom-call | tf_op jit(solution)/shard_map/pallas_call | solution.py:274
  80.6 1.7 %shard_map.85 = f32[288,1152]{1,0:T(8,128)} custom-call(s32[2]{0:T(128)S(1)} %pad_add_fusion.place, bf16[72,1152]{1,0:T(8,128)(2,1)S(1)} %add_convert_fusion.2.refs_0_, bf16[72,1152]{1,0:T(8,128)(2,1)S(1)} %collective-permute-done.16.refs_1_, bf16[72,1152]{1,0:T(8,128)(2,1)S(1)} %collective-permute-done.17.refs_2_, ...), custom_call_target="tpu_custom_call" | custom-call | tf_op jit(solution)/shard_map/pallas_call | solution.py:274
  (40 shorter events, 5.7 us)
Async XLA Ops:
  0.7 3.5 %collective-permute-start.1 = (bf16[256,1152]{1,0:T(8,128)(2,1)}, bf16[256,1152]{1,0:T(8,128)(2,1)S(1)}, u32[]{:S(2)}, u32[]{:S(2)}) collective-permute-start(bf16[256,1152]{1,0:T(8,128)(2,1)} %t0_far), channel_id=1, source_target_pairs={{0,1},{1,0},{2,3},{3,2},{4,5},{5,4},{6,7},{7,6},{8,9},{9,8},{10,11... | collective-permute-start | bytes 1769480 | tf_op jit(solution)/shard_map/ppermute | solution.py:287
  1.2 3.0 %collective-permute-start.2 = (bf16[256,1152]{1,0:T(8,128)(2,1)}, bf16[256,1152]{1,0:T(8,128)(2,1)S(1)}, u32[]{:S(2)}, u32[]{:S(2)}) collective-permute-start(bf16[256,1152]{1,0:T(8,128)(2,1)} %i0_far), channel_id=1, source_target_pairs={{0,1},{1,0},{2,3},{3,2},{4,5},{5,4},{6,7},{7,6},{8,9},{9,8},{10,11... | collective-permute-start | bytes 1769480 | tf_op jit(solution)/shard_map/ppermute | solution.py:287
  1.3 17.2 %collective-permute-start = (bf16[256,1152]{1,0:T(8,128)(2,1)}, bf16[256,1152]{1,0:T(8,128)(2,1)S(1)}, u32[]{:S(2)}, u32[]{:S(2)}) collective-permute-start(bf16[256,1152]{1,0:T(8,128)(2,1)} %t0_far), channel_id=1, source_target_pairs={{0,2},{1,3},{2,0},{3,1},{4,6},{5,7},{6,4},{7,5},{8,10},{9,11},{10,... | collective-permute-start | bytes 1769480 | tf_op jit(solution)/shard_map/ppermute | solution.py:287
  4.2 27.5 %collective-permute-start.8 = (bf16[256,1152]{1,0:T(8,128)(2,1)}, bf16[256,1152]{1,0:T(8,128)(2,1)S(1)}, u32[]{:S(2)}, u32[]{:S(2)}) collective-permute-start(bf16[256,1152]{1,0:T(8,128)(2,1)} %i0_far), channel_id=1, source_target_pairs={{0,2},{1,3},{2,0},{3,1},{4,6},{5,7},{6,4},{7,5},{8,10},{9,11},{10,... | collective-permute-start | bytes 1769480 | tf_op jit(solution)/shard_map/ppermute | solution.py:287
  18.5 1.4 %collective-permute-start.3 = (bf16[64,1152]{1,0:T(8,128)(2,1)S(1)}, bf16[64,1152]{1,0:T(8,128)(2,1)S(1)}, u32[]{:S(2)}, u32[]{:S(2)}) collective-permute-start(bf16[64,1152]{1,0:T(8,128)(2,1)S(1)} %get-tuple-element.117), channel_id=1, source_target_pairs={{0,1},{1,0},{2,3},{3,2},{4,5},{5,4},{6,7},{7,6},{8,9},{9,8},{10,11... | collective-permute-start | bytes 442376 | tf_op jit(solution)/shard_map/ppermute | solution.py:287
  18.6 1.6 %collective-permute-start.4 = (bf16[64,1152]{1,0:T(8,128)(2,1)S(1)}, bf16[64,1152]{1,0:T(8,128)(2,1)S(1)}, u32[]{:S(2)}, u32[]{:S(2)}) collective-permute-start(bf16[64,1152]{1,0:T(8,128)(2,1)S(1)} %get-tuple-element.116), channel_id=1, source_target_pairs={{0,1},{1,0},{2,3},{3,2},{4,5},{5,4},{6,7},{7,6},{8,9},{9,8},{10,11... | collective-permute-start | bytes 442376 | tf_op jit(solution)/shard_map/ppermute | solution.py:287
  19.1 1.4 %collective-permute-start.5 = (bf16[64,1152]{1,0:T(8,128)(2,1)S(1)}, bf16[64,1152]{1,0:T(8,128)(2,1)S(1)}, u32[]{:S(2)}, u32[]{:S(2)}) collective-permute-start(bf16[64,1152]{1,0:T(8,128)(2,1)S(1)} %get-tuple-element.115), channel_id=1, source_target_pairs={{0,1},{1,0},{2,3},{3,2},{4,5},{5,4},{6,7},{7,6},{8,9},{9,8},{10,11... | collective-permute-start | bytes 442376 | tf_op jit(solution)/shard_map/ppermute | solution.py:287
  19.2 1.5 %collective-permute-start.6 = (bf16[64,1152]{1,0:T(8,128)(2,1)S(1)}, bf16[64,1152]{1,0:T(8,128)(2,1)S(1)}, u32[]{:S(2)}, u32[]{:S(2)}) collective-permute-start(bf16[64,1152]{1,0:T(8,128)(2,1)S(1)} %get-tuple-element.114), channel_id=1, source_target_pairs={{0,1},{1,0},{2,3},{3,2},{4,5},{5,4},{6,7},{7,6},{8,9},{9,8},{10,11... | collective-permute-start | bytes 442376 | tf_op jit(solution)/shard_map/ppermute | solution.py:287
  25.9 10.4 %collective-permute-start.7 = (bf16[144,1152]{1,0:T(8,128)(2,1)S(1)}, bf16[144,1152]{1,0:T(8,128)(2,1)S(1)}, u32[]{:S(2)}, u32[]{:S(2)}) collective-permute-start(bf16[144,1152]{1,0:T(8,128)(2,1)S(1)} %get-tuple-element.74), channel_id=1, source_target_pairs={{0,4},{4,0},{8,12},{12,8},{16,20},{20,16},{24,28},{28,24},{1,5},{5... | collective-permute-start | bytes 995336 | tf_op jit(solution)/shard_map/ppermute | solution.py:287
  28.1 9.7 %collective-permute-start.11 = (bf16[144,1152]{1,0:T(8,128)(2,1)S(1)}, bf16[144,1152]{1,0:T(8,128)(2,1)S(1)}, u32[]{:S(2)}, u32[]{:S(2)}) collective-permute-start(bf16[144,1152]{1,0:T(8,128)(2,1)S(1)} %get-tuple-element.90), channel_id=1, source_target_pairs={{0,8},{4,12},{8,0},{12,4},{16,24},{20,28},{24,16},{28,20},{1,9},{5... | collective-permute-start | bytes 995336 | tf_op jit(solution)/shard_map/ppermute | solution.py:287
  33.6 6.5 %collective-permute-start.12 = (bf16[128,1152]{1,0:T(8,128)(2,1)S(1)}, bf16[128,1152]{1,0:T(8,128)(2,1)S(1)}, u32[]{:S(2)}, u32[]{:S(2)}) collective-permute-start(bf16[128,1152]{1,0:T(8,128)(2,1)S(1)} %get-tuple-element.83.x_second), channel_id=1, source_target_pairs={{0,1},{1,0},{2,3},{3,2},{4,5},{5,4},{6,7},{7,6},{8,9},{9,8},{10,11... | collective-permute-start | bytes 884744 | tf_op jit(solution)/shard_map/ppermute | solution.py:287
  33.7 6.4 %collective-permute-start.10 = (bf16[128,1152]{1,0:T(8,128)(2,1)S(1)}, bf16[128,1152]{1,0:T(8,128)(2,1)S(1)}, u32[]{:S(2)}, u32[]{:S(2)}) collective-permute-start(bf16[128,1152]{1,0:T(8,128)(2,1)S(1)} %get-tuple-element.82.x_first), channel_id=1, source_target_pairs={{0,1},{1,0},{2,3},{3,2},{4,5},{5,4},{6,7},{7,6},{8,9},{9,8},{10,11... | collective-permute-start | bytes 884744 | tf_op jit(solution)/shard_map/ppermute | solution.py:287
  37.8 5.6 %collective-permute-start.13 = (bf16[72,1152]{1,0:T(8,128)(2,1)S(1)}, bf16[72,1152]{1,0:T(8,128)(2,1)S(1)}, u32[]{:S(2)}, u32[]{:S(2)}) collective-permute-start(bf16[72,1152]{1,0:T(8,128)(2,1)S(1)} %add_convert_fusion.6), channel_id=1, source_target_pairs={{0,4},{4,0},{8,12},{12,8},{16,20},{20,16},{24,28},{28,24},{1,5},{5... | collective-permute-start | bytes 497672 | tf_op jit(solution)/shard_map/ppermute | solution.py:287
  38.3 10.2 %collective-permute-start.9 = (bf16[72,1152]{1,0:T(8,128)(2,1)S(1)}, bf16[72,1152]{1,0:T(8,128)(2,1)S(1)}, u32[]{:S(2)}, u32[]{:S(2)}) collective-permute-start(bf16[72,1152]{1,0:T(8,128)(2,1)S(1)} %add_convert_fusion.7), channel_id=1, source_target_pairs={{0,8},{4,12},{8,0},{12,4},{16,24},{20,28},{24,16},{28,20},{1,9},{5... | collective-permute-start | bytes 497672 | tf_op jit(solution)/shard_map/ppermute | solution.py:287
  43.5 5.4 %collective-permute-start.14 = (bf16[72,1152]{1,0:T(8,128)(2,1)S(1)}, bf16[72,1152]{1,0:T(8,128)(2,1)S(1)}, u32[]{:S(2)}, u32[]{:S(2)}) collective-permute-start(bf16[72,1152]{1,0:T(8,128)(2,1)S(1)} %add_convert_fusion.4), channel_id=1, source_target_pairs={{0,2},{1,3},{2,0},{3,1},{4,6},{5,7},{6,4},{7,5},{8,10},{9,11},{10,... | collective-permute-start | bytes 497672 | tf_op jit(solution)/shard_map/ppermute | solution.py:287
  45.0 10.7 %collective-permute-start.19 = (bf16[72,1152]{1,0:T(8,128)(2,1)S(1)}, bf16[72,1152]{1,0:T(8,128)(2,1)S(1)}, u32[]{:S(2)}, u32[]{:S(2)}) collective-permute-start(bf16[72,1152]{1,0:T(8,128)(2,1)S(1)} %get-tuple-element.106), channel_id=1, source_target_pairs={{0,4},{4,0},{8,12},{12,8},{16,20},{20,16},{24,28},{28,24},{1,5},{5... | collective-permute-start | bytes 497672 | tf_op jit(solution)/shard_map/ppermute | solution.py:287
  46.6 9.2 %collective-permute-start.20 = (bf16[72,1152]{1,0:T(8,128)(2,1)S(1)}, bf16[72,1152]{1,0:T(8,128)(2,1)S(1)}, u32[]{:S(2)}, u32[]{:S(2)}) collective-permute-start(bf16[72,1152]{1,0:T(8,128)(2,1)S(1)} %get-tuple-element.108), channel_id=1, source_target_pairs={{0,8},{4,12},{8,0},{12,4},{16,24},{20,28},{24,16},{28,20},{1,9},{5... | collective-permute-start | bytes 497672 | tf_op jit(solution)/shard_map/ppermute | solution.py:287
  47.0 11.2 %collective-permute-start.21 = (bf16[72,1152]{1,0:T(8,128)(2,1)S(1)}, bf16[72,1152]{1,0:T(8,128)(2,1)S(1)}, u32[]{:S(2)}, u32[]{:S(2)}) collective-permute-start(bf16[72,1152]{1,0:T(8,128)(2,1)S(1)} %get-tuple-element.110), channel_id=1, source_target_pairs={{0,12},{4,8},{8,4},{12,0},{16,28},{20,24},{24,20},{28,16},{1,13},{... | collective-permute-start | bytes 497672 | tf_op jit(solution)/shard_map/ppermute | solution.py:287
  49.0 10.7 %collective-permute-start.15 = (bf16[72,1152]{1,0:T(8,128)(2,1)S(1)}, bf16[72,1152]{1,0:T(8,128)(2,1)S(1)}, u32[]{:S(2)}, u32[]{:S(2)}) collective-permute-start(bf16[72,1152]{1,0:T(8,128)(2,1)S(1)} %add_convert_fusion.3), channel_id=1, source_target_pairs={{0,16},{4,20},{8,24},{12,28},{16,0},{20,4},{24,8},{28,12},{1,17},{... | collective-permute-start | bytes 497672 | tf_op jit(solution)/shard_map/ppermute | solution.py:287
  58.3 8.2 %collective-permute-start.22 = (bf16[72,1152]{1,0:T(8,128)(2,1)S(1)}, bf16[72,1152]{1,0:T(8,128)(2,1)S(1)}, u32[]{:S(2)}, u32[]{:S(2)}) collective-permute-start(bf16[72,1152]{1,0:T(8,128)(2,1)S(1)} %add_convert_fusion.1), channel_id=1, source_target_pairs={{0,16},{4,20},{8,24},{12,28},{16,0},{20,4},{24,8},{28,12},{1,17},{... | collective-permute-start | bytes 497672 | tf_op jit(solution)/shard_map/ppermute | solution.py:287
  59.7 6.8 %collective-permute-start.16 = (bf16[72,1152]{1,0:T(8,128)(2,1)S(1)}, bf16[72,1152]{1,0:T(8,128)(2,1)S(1)}, u32[]{:S(2)}, u32[]{:S(2)}) collective-permute-start(bf16[72,1152]{1,0:T(8,128)(2,1)S(1)} %add_convert_fusion.2.refs_0_), channel_id=1, source_target_pairs={{0,4},{4,0},{8,12},{12,8},{16,20},{20,16},{24,28},{28,24},{1,5},{5... | collective-permute-start | bytes 497672 | tf_op jit(solution)/shard_map/ppermute | solution.py:287
  61.6 12.1 %collective-permute-start.17 = (bf16[72,1152]{1,0:T(8,128)(2,1)S(1)}, bf16[72,1152]{1,0:T(8,128)(2,1)S(1)}, u32[]{:S(2)}, u32[]{:S(2)}) collective-permute-start(bf16[72,1152]{1,0:T(8,128)(2,1)S(1)} %add_convert_fusion.2.refs_0_), channel_id=1, source_target_pairs={{0,8},{4,12},{8,0},{12,4},{16,24},{20,28},{24,16},{28,20},{1,9},{5... | collective-permute-start | bytes 497672 | tf_op jit(solution)/shard_map/ppermute | solution.py:287
  66.6 7.7 %collective-permute-start.23 = (bf16[72,1152]{1,0:T(8,128)(2,1)S(1)}, bf16[72,1152]{1,0:T(8,128)(2,1)S(1)}, u32[]{:S(2)}, u32[]{:S(2)}) collective-permute-start(bf16[72,1152]{1,0:T(8,128)(2,1)S(1)} %add_convert_fusion.refs_0_), channel_id=1, source_target_pairs={{0,4},{4,0},{8,12},{12,8},{16,20},{20,16},{24,28},{28,24},{1,5},{5... | collective-permute-start | bytes 497672 | tf_op jit(solution)/shard_map/ppermute | solution.py:287
  67.9 7.7 %collective-permute-start.24 = (bf16[72,1152]{1,0:T(8,128)(2,1)S(1)}, bf16[72,1152]{1,0:T(8,128)(2,1)S(1)}, u32[]{:S(2)}, u32[]{:S(2)}) collective-permute-start(bf16[72,1152]{1,0:T(8,128)(2,1)S(1)} %add_convert_fusion.refs_0_), channel_id=1, source_target_pairs={{0,8},{4,12},{8,0},{12,4},{16,24},{20,28},{24,16},{28,20},{1,9},{5... | collective-permute-start | bytes 497672 | tf_op jit(solution)/shard_map/ppermute | solution.py:287
  72.3 6.6 %collective-permute-start.25 = (bf16[72,1152]{1,0:T(8,128)(2,1)S(1)}, bf16[72,1152]{1,0:T(8,128)(2,1)S(1)}, u32[]{:S(2)}, u32[]{:S(2)}) collective-permute-start(bf16[72,1152]{1,0:T(8,128)(2,1)S(1)} %add_convert_fusion.refs_0_), channel_id=1, source_target_pairs={{0,12},{4,8},{8,4},{12,0},{16,28},{20,24},{24,20},{28,16},{1,13},{... | collective-permute-start | bytes 497672 | tf_op jit(solution)/shard_map/ppermute | solution.py:287
  73.7 6.9 %collective-permute-start.18 = (bf16[72,1152]{1,0:T(8,128)(2,1)S(1)}, bf16[72,1152]{1,0:T(8,128)(2,1)S(1)}, u32[]{:S(2)}, u32[]{:S(2)}) collective-permute-start(bf16[72,1152]{1,0:T(8,128)(2,1)S(1)} %collective-permute-done.17.refs_2_), channel_id=1, source_target_pairs={{0,4},{4,0},{8,12},{12,8},{16,20},{20,16},{24,28},{28,24},{1,5},{5... | collective-permute-start | bytes 497672 | tf_op jit(solution)/shard_map/ppermute | solution.py:287

commit v17 on v14

--- a/solution.py
+++ b/solution.py
@@ -123,12 +123,17 @@
     return jnp.where(wanted == column, 1.0, 0.0)
 
 
+def slot_masks(place_ref):
+    core = place_ref[0] & 1
+    return (0, 1 + core, 2 - core, 3)
+
+
 def picker(place_ref, rows, width, sides):
     part = rows // QUAD
     pieces = []
-    for k in range(QUAD):
+    for mask in slot_masks(place_ref):
         for side in sides:
-            first = (place_ref[0] ^ side) * rows + (place_ref[1] ^ k) * part
+            first = (place_ref[0] ^ side) * rows + (place_ref[1] ^ mask) * part
             pieces.append(one_hot(first, part, width))
     return jnp.concatenate(pieces, axis=0).astype(BF16)
 
@@ -258,8 +263,8 @@
 def place_kernel(place, *refs):
     *pieces, out = refs
     part = pieces[0].shape[0]
-    for k, piece in enumerate(pieces):
-        first = pl.multiple_of((place[1] ^ k) * part, part)
+    for mask, piece in zip(slot_masks(place), pieces):
+        first = pl.multiple_of((place[1] ^ mask) * part, part)
         out[pl.ds(first, part), :] = piece[...].astype(F32)
 
 
@@ -287,6 +292,14 @@
     return lax.ppermute(array, axis, [(i, i ^ mask) for i in range(size)])
 
 
+def swap_slot(array, slot, n_cuts, n_loop):
+    masks = ((1, 2), (2, 1), (3, 3))[slot - 1]
+    pairs = [
+        (c * n_loop + l, (c ^ masks[l % 2]) * n_loop + l) for c in range(n_cuts) for l in range(n_loop)
+    ]
+    return lax.ppermute(array, ("cuts", "loop"), pairs)
+
+
 def after(value, other):
     return lax.optimization_barrier((value, other))[0]
 
@@ -298,6 +311,7 @@
     part = rows_out // QUAD
     loop = functools.partial(swap, axis="loop", size=n_loop)
     cuts = functools.partial(swap, axis="cuts", size=n_cuts)
+    quad = functools.partial(swap_slot, n_cuts=n_cuts, n_loop=n_loop)
     macs = half * width * width
 
     def both(rows, order, count):
@@ -308,7 +322,7 @@
         return sum((other.astype(F32) for other in others), own.astype(F32)).astype(BF16)
 
     def spread(total):
-        return [total] + [cuts(total, mask=k) for k in range(1, QUAD)]
+        return [total] + [quad(total, slot=slot) for slot in range(1, QUAD)]
 
     t2 = loop(text_features, mask=2)
     i2 = loop(image_features, mask=2)
@@ -348,7 +362,7 @@
         (*far_text, text_head, p_a, x_a, gx, pick_i),
         8,
     )
-    near_came, far_came = cuts(near_sent, mask=1), cuts(far_sent, mask=2)
+    near_came, far_came = quad(near_sent, slot=1), quad(far_sent, slot=2)
     gy_b, pick_b = call(
         text_pull_kernel,
         [wide, pick_one],
@@ -375,7 +389,7 @@
     )
     near_came, far_came = after(near_came, gy_a), after(far_came, gy_a)
     near_sent, far_sent = add(near_2, [near_came[part:]]), add(far_1, [far_came[part:]])
-    near_last, far_last = cuts(near_sent, mask=2), cuts(far_sent, mask=1)
+    near_last, far_last = quad(near_sent, slot=2), quad(far_sent, slot=1)
     x_3 = [after(rows, (gy_a, near_sent, far_sent)) for rows in x_3]
     *text_parts, dq_a = call(
         last_kernel,
@@ -384,7 +398,7 @@
         (*x_3, y_a, y_b, q_a, q_b, gy_a, gy_b, pick_a, pick_b),
         16,
     )
-    text_others = [cuts(text_parts[k], mask=k) for k in range(1, QUAD)]
+    text_others = [quad(text_parts[slot], slot=slot) for slot in range(1, QUAD)]
     far_sum = add(far_0, [far_came[:part], after(far_last, dq_a)])
     near_sum = add(near_0, [near_came[:part], after(near_last, dq_a)])
     image_sum = add(near_sum, [loop(far_sum, mask=2)])

time: 79.3 us -> 81.7 us (1.030)
  the two profiles are of different devices: /device:TPU:0 before, /device:TPU:2 now
where the time goes in v17:
time: 81.7 us; the launch traced here: 81.5 us
  starting transfers between devices  33.6 us (41%)
  Pallas kernels  30.7 us (38%)
  waiting for transfers between devices  15.8 us (19%)
    pallas_call x11, Pallas kernels, call(): pl.pallas_call(kernel, out_shape=[shape(s, t) for s, t in outs], in_specs...  30.7 us
    ppermute x13, starting transfers between devices, swap_slot(): return lax.ppermute(array, ('cuts', 'loop'), pairs)  25.9 us
    ppermute x13, waiting for transfers between devices, swap(): return lax.ppermute(array, axis, [(i, i ^ mask) for i in range(size)])  8.28 us
    ppermute x13, starting transfers between devices, swap(): return lax.ppermute(array, axis, [(i, i ^ mask) for i in range(size)])  7.72 us
    ppermute x13, waiting for transfers between devices, swap_slot(): return lax.ppermute(array, ('cuts', 'loop'), pairs)  7.55 us
  transfers between devices with their start and end apart: 26, of which 13 were waited for; matrix products, arithmetic and copies ran while one was open for 1% of the time, Pallas kernels for 36%

profile of v17, /device:TPU:2, one launch (start us, length us, event | category | flops | bytes accessed | tf_op | source)
XLA Modules:
  0.0 81.5 jit_solution(11943946035714573318)
XLA Ops:
  1.2 2.0 %collective-permute-start.8 = (bf16[256,1152]{1,0:T(8,128)(2,1)}, bf16[256,1152]{1,0:T(8,128)(2,1)S(1)}, u32[]{:S(2)}, u32[]{:S(2)}) collective-permute-start(bf16[256,1152]{1,0:T(8,128)(2,1)} %i0_far), channel_id=1, source_target_pairs={{0,2},{1,3},{2,0},{3,1},{4,6},{5,7},{6,4},{7,5},{8,10},{9,11},{10,... | collective-permute-start | bytes 1769480 | tf_op jit(solution)/shard_map/ppermute | solution.py:292
  3.3 0.5 collective-permute-done.2.i1
  3.8 7.4 %shard_map.75 = (f32[512,1152]{1,0:T(8,128)S(1)}, bf16[512,1152]{1,0:T(8,128)(2,1)S(1)}, f32[512,1152]{1,0:T(8,128)S(1)}, bf16[512,1152]{1,0:T(8,128)(2,1)S(1)},...) custom-call(bf16[256,1152]{1,0:T(8,128)(2,1)S(1)} %collective-permut, ...), custom_call_target="tpu_custom_call" | custom-call | tf_op jit(solution)/shard_map/pallas_call | solution.py:279
  11.2 2.6 %shard_map.76 = (f32[512,1152]{1,0:T(8,128)S(1)}, bf16[576,512]{1,0:T(8,128)(2,1)S(1)}, bf16[288,512]{1,0:T(8,128)(2,1)S(1)}) custom-call(s32[2]{0:T(128)S(1)} %pad_add_fusion.place, bf16[256,1152]{1,0:T(8,128)(2,1)S(1)} %get-tuple-element.61.t0, bf16[256,1152]{1,0:T(8,128)(2,1)S(1)} %collective-permute-done.1.t1, ...), custom_call_target="tpu_custom_call" | custom-call | tf_op jit(solution)/shard_map/pallas_call | solution.py:279
  13.8 3.9 %collective-permute-done.refs_0_ = bf16[256,1152]{1,0:T(8,128)(2,1)S(1)} collective-permute-done((bf16[256,1152]{1,0:T(8,128)(2,1)}, bf16[256,1152]{1,0:T(8,128)(2,1)S(1)}, u32[]{:S(2)}, u32[]{:S(2)}) %collective-permute-start) | collective-permute-done | bytes 589856 | tf_op jit(solution)/shard_map/ppermute | solution.py:292
  19.8 5.2 %shard_map.77 = (f32[512,1152]{1,0:T(8,128)S(1)}, bf16[512,1152]{1,0:T(8,128)(2,1)S(1)}, bf16[512,512]{1,0:T(8,128)(2,1)S(1)}, bf16[512,1152]{1,0:T(8,128)(2,1)S...) custom-call(bf16[256,1152]{1,0:T(8,128)(2,1)S(1)} %collective-permut, ...), custom_call_target="tpu_custom_call" | custom-call | tf_op jit(solution)/shard_map/pallas_call | solution.py:279
  25.0 1.6 %collective-permute-start.7 = (bf16[144,1152]{1,0:T(8,128)(2,1)S(1)}, bf16[144,1152]{1,0:T(8,128)(2,1)S(1)}, u32[]{:S(2)}, u32[]{:S(2)}) collective-permute-start(bf16[144,1152]{1,0:T(8,128)(2,1)S(1)} %get-tuple-element.73), channel_id=1, source_target_pairs={{0,4},{1,9},{2,6},{3,11},{4,0},{5,13},{6,2},{7,15},{8,12},{9,1},{1... | collective-permute-start | bytes 995336 | tf_op jit(solution)/shard_map/ppermute | solution.py:300
  26.6 1.6 %collective-permute-start.11 = (bf16[144,1152]{1,0:T(8,128)(2,1)S(1)}, bf16[144,1152]{1,0:T(8,128)(2,1)S(1)}, u32[]{:S(2)}, u32[]{:S(2)}) collective-permute-start(bf16[144,1152]{1,0:T(8,128)(2,1)S(1)} %get-tuple-element.89), channel_id=1, source_target_pairs={{0,8},{1,5},{2,10},{3,7},{4,12},{5,1},{6,14},{7,3},{8,0},{9,13},{1... | collective-permute-start | bytes 995336 | tf_op jit(solution)/shard_map/ppermute | solution.py:300
  28.2 2.0 %shard_map.78 = (f32[512,1152]{1,0:T(8,128)S(1)}, bf16[288,512]{1,0:T(8,128)(2,1)S(1)}) custom-call(s32[2]{0:T(128)S(1)} %pad_add_fusion.place, bf16[256,1152]{1,0:T(8,128)(2,1)S(1)} %collective-permute-done.refs_0_, bf16[64,1152]{1,0:T(8,128)(2,1)S(1)} %collective-permute-done.3.refs_1_, bf16[64,1152]{1,0:T(8,128)(2,1)S(1)} %collective-permute-done.4.refs_2_, ...), custom_call_target="tpu_custom_call" | custom-call | tf_op jit(solution)/shard_map/pallas_call | solution.py:279
  30.2 1.9 %shard_map.79 = (bf16[128,1152]{1,0:T(8,128)(2,1)S(1)}, bf16[128,1152]{1,0:T(8,128)(2,1)S(1)}, bf16[256,512]{1,0:T(8,128)(2,1)S(1)}, bf16[256,512]{1,0:T(8,128)(2,1)S(1)}) custom-call(bf16[256,1152]{1,0:T(8,128)(2,1)S(1)} %collective-permute-done.8.i2, bf16[1152,1152]{1,0:T(8,128)(2,1)S(1)} %get-tuple-element.78.image_head.head, ...), custom_call_target="tpu_custom_call" | custom-call | tf_op jit(solution)/shard_map/pallas_call | solution.py:279
  32.7 0.9 %shard_map.80 = (f32[512,1152]{1,0:T(8,128)S(1)}, f32[512,1152]{1,0:T(8,128)S(1)}) custom-call(bf16[128,1152]{1,0:T(8,128)(2,1)S(1)} %get-tuple-element.81.x_first, bf16[128,1152]{1,0:T(8,128)(2,1)S(1)} %get-tuple-element.82.x_second, bf16[256,512]{1,0:T(8,128)(2,1)S(1)} %get-tuple-element.83.w_a, bf16[256,512]{1,0:T(8,128)(2,1)S(1)} %get-tuple-element.84.w_b, ...), custom_call_target="tpu_custom_call" | custom-call | tf_op jit(solution)/shard_map/pallas_call | solution.py:279
  33.6 1.6 %collective-permute-done.7 = bf16[144,1152]{1,0:T(8,128)(2,1)S(1)} collective-permute-done((bf16[144,1152]{1,0:T(8,128)(2,1)S(1)}, bf16[144,1152]{1,0:T(8,128)(2,1)S(1)}, u32[]{:S(2)}, u32[]{:S(2)}) %collective-permute-start.7) | collective-permute-done | bytes 331808 | tf_op jit(solution)/shard_map/ppermute | solution.py:300
  35.2 1.6 %collective-permute-start.13 = (bf16[72,1152]{1,0:T(8,128)(2,1)S(1)}, bf16[72,1152]{1,0:T(8,128)(2,1)S(1)}, u32[]{:S(2)}, u32[]{:S(2)}) collective-permute-start(bf16[72,1152]{1,0:T(8,128)(2,1)S(1)} %add_convert_fusion.6), channel_id=1, source_target_pairs={{0,4},{1,9},{2,6},{3,11},{4,0},{5,13},{6,2},{7,15},{8,12},{9,1},{1... | collective-permute-start | bytes 497672 | tf_op jit(solution)/shard_map/ppermute | solution.py:300
  36.9 1.7 %collective-permute-start.9 = (bf16[72,1152]{1,0:T(8,128)(2,1)S(1)}, bf16[72,1152]{1,0:T(8,128)(2,1)S(1)}, u32[]{:S(2)}, u32[]{:S(2)}) collective-permute-start(bf16[72,1152]{1,0:T(8,128)(2,1)S(1)} %add_convert_fusion.7), channel_id=1, source_target_pairs={{0,8},{1,5},{2,10},{3,7},{4,12},{5,1},{6,14},{7,3},{8,0},{9,13},{1... | collective-permute-start | bytes 497672 | tf_op jit(solution)/shard_map/ppermute | solution.py:300
  38.6 3.3 %shard_map.81 = (bf16[72,1152]{1,0:T(8,128)(2,1)S(1)}, bf16[72,1152]{1,0:T(8,128)(2,1)S(1)}, bf16[72,1152]{1,0:T(8,128)(2,1)S(1)}, bf16[72,1152]{1,0:T(8,128)(2,1)S(1)}, bf16[512,1152]{1,0:T(8,128)(2,1)S(1)}) custom-call(bf16[128,1152]{1,0:T(8,128)(2,1)S(1)} %collective-permute-done.10.x_first, bf16[128,1152]{1,0:T(8,128)(2,1)S(1)} %collective-permute-done.12.x_second, ...), custom_call_target="tpu_custom_call" | custom-call | tf_op jit(solution)/shard_map/pallas_call | solution.py:279
  42.6 1.8 %collective-permute-start.19 = (bf16[72,1152]{1,0:T(8,128)(2,1)S(1)}, bf16[72,1152]{1,0:T(8,128)(2,1)S(1)}, u32[]{:S(2)}, u32[]{:S(2)}) collective-permute-start(bf16[72,1152]{1,0:T(8,128)(2,1)S(1)} %get-tuple-element.105), channel_id=1, source_target_pairs={{0,4},{1,9},{2,6},{3,11},{4,0},{5,13},{6,2},{7,15},{8,12},{9,1},{1... | collective-permute-start | bytes 497672 | tf_op jit(solution)/shard_map/ppermute | solution.py:300
  44.4 1.5 %collective-permute-start.20 = (bf16[72,1152]{1,0:T(8,128)(2,1)S(1)}, bf16[72,1152]{1,0:T(8,128)(2,1)S(1)}, u32[]{:S(2)}, u32[]{:S(2)}) collective-permute-start(bf16[72,1152]{1,0:T(8,128)(2,1)S(1)} %get-tuple-element.107), channel_id=1, source_target_pairs={{0,8},{1,5},{2,10},{3,7},{4,12},{5,1},{6,14},{7,3},{8,0},{9,13},{1... | collective-permute-start | bytes 497672 | tf_op jit(solution)/shard_map/ppermute | solution.py:300
  46.1 1.6 %collective-permute-done.14 = bf16[72,1152]{1,0:T(8,128)(2,1)S(1)} collective-permute-done((bf16[72,1152]{1,0:T(8,128)(2,1)S(1)}, bf16[72,1152]{1,0:T(8,128)(2,1)S(1)}, u32[]{:S(2)}, u32[]{:S(2)}) %collective-permute-start.14) | collective-permute-done | bytes 165920 | tf_op jit(solution)/shard_map/ppermute | solution.py:292
  47.8 2.7 %collective-permute-start.15 = (bf16[72,1152]{1,0:T(8,128)(2,1)S(1)}, bf16[72,1152]{1,0:T(8,128)(2,1)S(1)}, u32[]{:S(2)}, u32[]{:S(2)}) collective-permute-start(bf16[72,1152]{1,0:T(8,128)(2,1)S(1)} %add_convert_fusion.3), channel_id=1, source_target_pairs={{0,16},{4,20},{8,24},{12,28},{16,0},{20,4},{24,8},{28,12},{1,17},{... | collective-permute-start | bytes 497672 | tf_op jit(solution)/shard_map/ppermute | solution.py:292
  50.5 2.0 %shard_map.83 = f32[256,1152]{1,0:T(8,128)} custom-call(bf16[512,1152]{1,0:T(8,128)(2,1)S(1)} %get-tuple-element.103.back, bf16[1152,1152]{1,0:T(8,128)(2,1)S(1)} %get-tuple-element.67.refs_5_.head), custom_call_target="tpu_custom_call" | custom-call | flops 1358954496 | tf_op jit(solution)/shard_map/pallas_call | solution.py:279
  52.5 2.1 %shard_map.82 = f32[256,1152]{1,0:T(8,128)} custom-call(bf16[512,1152]{1,0:T(8,128)(2,1)S(1)} %get-tuple-element.102.back, bf16[1152,1152]{1,0:T(8,128)(2,1)S(1)} %get-tuple-element.78.image_head.head), custom_call_target="tpu_custom_call" | custom-call | flops 1358954496 | tf_op jit(solution)/shard_map/pallas_call | solution.py:279
  54.6 1.1 %collective-permute-done.21 = bf16[72,1152]{1,0:T(8,128)(2,1)S(1)} collective-permute-done((bf16[72,1152]{1,0:T(8,128)(2,1)S(1)}, bf16[72,1152]{1,0:T(8,128)(2,1)S(1)}, u32[]{:S(2)}, u32[]{:S(2)}) %collective-permute-start.21) | collective-permute-done | bytes 165920 | tf_op jit(solution)/shard_map/ppermute | solution.py:300
  55.7 0.6 collective-permute-start.22
  56.4 1.0 %collective-permute-start.16 = (bf16[72,1152]{1,0:T(8,128)(2,1)S(1)}, bf16[72,1152]{1,0:T(8,128)(2,1)S(1)}, u32[]{:S(2)}, u32[]{:S(2)}) collective-permute-start(bf16[72,1152]{1,0:T(8,128)(2,1)S(1)} %add_convert_fusion.2.refs_0_), channel_id=1, source_target_pairs={{0,4},{1,9},{2,6},{3,11},{4,0},{5,13},{6,2},{7,15},{8,12},{9,1},{1... | collective-permute-start | bytes 497672 | tf_op jit(solution)/shard_map/ppermute | solution.py:300
  57.5 5.4 %collective-permute-start.17 = (bf16[72,1152]{1,0:T(8,128)(2,1)S(1)}, bf16[72,1152]{1,0:T(8,128)(2,1)S(1)}, u32[]{:S(2)}, u32[]{:S(2)}) collective-permute-start(bf16[72,1152]{1,0:T(8,128)(2,1)S(1)} %add_convert_fusion.2.refs_0_), channel_id=1, source_target_pairs={{0,8},{1,5},{2,10},{3,7},{4,12},{5,1},{6,14},{7,3},{8,0},{9,13},{1... | collective-permute-start | bytes 497672 | tf_op jit(solution)/shard_map/ppermute | solution.py:300
  62.9 1.2 %collective-permute-done.22 = bf16[72,1152]{1,0:T(8,128)(2,1)S(1)} collective-permute-done((bf16[72,1152]{1,0:T(8,128)(2,1)S(1)}, bf16[72,1152]{1,0:T(8,128)(2,1)S(1)}, u32[]{:S(2)}, u32[]{:S(2)}) %collective-permute-start.22) | collective-permute-done | bytes 165920 | tf_op jit(solution)/shard_map/ppermute | solution.py:292
  64.1 1.0 %collective-permute-start.23 = (bf16[72,1152]{1,0:T(8,128)(2,1)S(1)}, bf16[72,1152]{1,0:T(8,128)(2,1)S(1)}, u32[]{:S(2)}, u32[]{:S(2)}) collective-permute-start(bf16[72,1152]{1,0:T(8,128)(2,1)S(1)} %add_convert_fusion.refs_0_), channel_id=1, source_target_pairs={{0,4},{1,9},{2,6},{3,11},{4,0},{5,13},{6,2},{7,15},{8,12},{9,1},{1... | collective-permute-start | bytes 497672 | tf_op jit(solution)/shard_map/ppermute | solution.py:300
  65.1 8.5 %collective-permute-start.24 = (bf16[72,1152]{1,0:T(8,128)(2,1)S(1)}, bf16[72,1152]{1,0:T(8,128)(2,1)S(1)}, u32[]{:S(2)}, u32[]{:S(2)}) collective-permute-start(bf16[72,1152]{1,0:T(8,128)(2,1)S(1)} %add_convert_fusion.refs_0_), channel_id=1, source_target_pairs={{0,8},{1,5},{2,10},{3,7},{4,12},{5,1},{6,14},{7,3},{8,0},{9,13},{1... | collective-permute-start | bytes 497672 | tf_op jit(solution)/shard_map/ppermute | solution.py:300
  73.6 1.7 %shard_map.84 = f32[288,1152]{1,0:T(8,128)} custom-call(s32[2]{0:T(128)S(1)} %pad_add_fusion.place, bf16[72,1152]{1,0:T(8,128)(2,1)S(1)} %add_convert_fusion.2.refs_0_, bf16[72,1152]{1,0:T(8,128)(2,1)S(1)} %collective-permute-done.16.refs_1_, bf16[72,1152]{1,0:T(8,128)(2,1)S(1)} %collective-permute-done.17.refs_2_, ...), custom_call_target="tpu_custom_call" | custom-call | tf_op jit(solution)/shard_map/pallas_call | solution.py:279
  75.3 1.6 %collective-permute-done.24.refs_2_ = bf16[72,1152]{1,0:T(8,128)(2,1)S(1)} collective-permute-done((bf16[72,1152]{1,0:T(8,128)(2,1)S(1)}, bf16[72,1152]{1,0:T(8,128)(2,1)S(1)}, u32[]{:S(2)}, u32[]{:S(2)}) %collective-permute-start.24) | collective-permute-done | bytes 165920 | tf_op jit(solution)/shard_map/ppermute | solution.py:300
  76.9 2.9 %collective-permute-done.25.refs_3_ = bf16[72,1152]{1,0:T(8,128)(2,1)S(1)} collective-permute-done((bf16[72,1152]{1,0:T(8,128)(2,1)S(1)}, bf16[72,1152]{1,0:T(8,128)(2,1)S(1)}, u32[]{:S(2)}, u32[]{:S(2)}) %collective-permute-start.25) | collective-permute-done | bytes 165920 | tf_op jit(solution)/shard_map/ppermute | solution.py:300
  79.8 1.7 %shard_map.85 = f32[288,1152]{1,0:T(8,128)} custom-call(s32[2]{0:T(128)S(1)} %pad_add_fusion.place, bf16[72,1152]{1,0:T(8,128)(2,1)S(1)} %add_convert_fusion.refs_0_, bf16[72,1152]{1,0:T(8,128)(2,1)S(1)} %collective-permute-done.23.refs_1_, bf16[72,1152]{1,0:T(8,128)(2,1)S(1)} %collective-permute-done.24.refs_2_, ...), custom_call_target="tpu_custom_call" | custom-call | tf_op jit(solution)/shard_map/pallas_call | solution.py:279
  (40 shorter events, 4.6 us)
Async XLA Ops:
  0.7 2.5 %collective-permute-start.1 = (bf16[256,1152]{1,0:T(8,128)(2,1)}, bf16[256,1152]{1,0:T(8,128)(2,1)S(1)}, u32[]{:S(2)}, u32[]{:S(2)}) collective-permute-start(bf16[256,1152]{1,0:T(8,128)(2,1)} %t0_far), channel_id=1, source_target_pairs={{0,1},{1,0},{2,3},{3,2},{4,5},{5,4},{6,7},{7,6},{8,9},{9,8},{10,11... | collective-permute-start | bytes 1769480 | tf_op jit(solution)/shard_map/ppermute | solution.py:292
  0.7 3.0 %collective-permute-start.2 = (bf16[256,1152]{1,0:T(8,128)(2,1)}, bf16[256,1152]{1,0:T(8,128)(2,1)S(1)}, u32[]{:S(2)}, u32[]{:S(2)}) collective-permute-start(bf16[256,1152]{1,0:T(8,128)(2,1)} %i0_far), channel_id=1, source_target_pairs={{0,1},{1,0},{2,3},{3,2},{4,5},{5,4},{6,7},{7,6},{8,9},{9,8},{10,11... | collective-permute-start | bytes 1769480 | tf_op jit(solution)/shard_map/ppermute | solution.py:292
  1.2 16.4 %collective-permute-start = (bf16[256,1152]{1,0:T(8,128)(2,1)}, bf16[256,1152]{1,0:T(8,128)(2,1)S(1)}, u32[]{:S(2)}, u32[]{:S(2)}) collective-permute-start(bf16[256,1152]{1,0:T(8,128)(2,1)} %t0_far), channel_id=1, source_target_pairs={{0,2},{1,3},{2,0},{3,1},{4,6},{5,7},{6,4},{7,5},{8,10},{9,11},{10,... | collective-permute-start | bytes 1769480 | tf_op jit(solution)/shard_map/ppermute | solution.py:292
  1.2 29.0 %collective-permute-start.8 = (bf16[256,1152]{1,0:T(8,128)(2,1)}, bf16[256,1152]{1,0:T(8,128)(2,1)S(1)}, u32[]{:S(2)}, u32[]{:S(2)}) collective-permute-start(bf16[256,1152]{1,0:T(8,128)(2,1)} %i0_far), channel_id=1, source_target_pairs={{0,2},{1,3},{2,0},{3,1},{4,6},{5,7},{6,4},{7,5},{8,10},{9,11},{10,... | collective-permute-start | bytes 1769480 | tf_op jit(solution)/shard_map/ppermute | solution.py:292
  17.7 1.4 %collective-permute-start.3 = (bf16[64,1152]{1,0:T(8,128)(2,1)S(1)}, bf16[64,1152]{1,0:T(8,128)(2,1)S(1)}, u32[]{:S(2)}, u32[]{:S(2)}) collective-permute-start(bf16[64,1152]{1,0:T(8,128)(2,1)S(1)} %get-tuple-element.115), channel_id=1, source_target_pairs={{0,1},{1,0},{2,3},{3,2},{4,5},{5,4},{6,7},{7,6},{8,9},{9,8},{10,11... | collective-permute-start | bytes 442376 | tf_op jit(solution)/shard_map/ppermute | solution.py:292
  17.8 1.6 %collective-permute-start.4 = (bf16[64,1152]{1,0:T(8,128)(2,1)S(1)}, bf16[64,1152]{1,0:T(8,128)(2,1)S(1)}, u32[]{:S(2)}, u32[]{:S(2)}) collective-permute-start(bf16[64,1152]{1,0:T(8,128)(2,1)S(1)} %get-tuple-element.114), channel_id=1, source_target_pairs={{0,1},{1,0},{2,3},{3,2},{4,5},{5,4},{6,7},{7,6},{8,9},{9,8},{10,11... | collective-permute-start | bytes 442376 | tf_op jit(solution)/shard_map/ppermute | solution.py:292
  18.2 1.4 %collective-permute-start.5 = (bf16[64,1152]{1,0:T(8,128)(2,1)S(1)}, bf16[64,1152]{1,0:T(8,128)(2,1)S(1)}, u32[]{:S(2)}, u32[]{:S(2)}) collective-permute-start(bf16[64,1152]{1,0:T(8,128)(2,1)S(1)} %get-tuple-element.113), channel_id=1, source_target_pairs={{0,1},{1,0},{2,3},{3,2},{4,5},{5,4},{6,7},{7,6},{8,9},{9,8},{10,11... | collective-permute-start | bytes 442376 | tf_op jit(solution)/shard_map/ppermute | solution.py:292
  18.3 1.5 %collective-permute-start.6 = (bf16[64,1152]{1,0:T(8,128)(2,1)S(1)}, bf16[64,1152]{1,0:T(8,128)(2,1)S(1)}, u32[]{:S(2)}, u32[]{:S(2)}) collective-permute-start(bf16[64,1152]{1,0:T(8,128)(2,1)S(1)} %get-tuple-element.112), channel_id=1, source_target_pairs={{0,1},{1,0},{2,3},{3,2},{4,5},{5,4},{6,7},{7,6},{8,9},{9,8},{10,11... | collective-permute-start | bytes 442376 | tf_op jit(solution)/shard_map/ppermute | solution.py:292
  25.0 10.2 %collective-permute-start.7 = (bf16[144,1152]{1,0:T(8,128)(2,1)S(1)}, bf16[144,1152]{1,0:T(8,128)(2,1)S(1)}, u32[]{:S(2)}, u32[]{:S(2)}) collective-permute-start(bf16[144,1152]{1,0:T(8,128)(2,1)S(1)} %get-tuple-element.73), channel_id=1, source_target_pairs={{0,4},{1,9},{2,6},{3,11},{4,0},{5,13},{6,2},{7,15},{8,12},{9,1},{1... | collective-permute-start | bytes 995336 | tf_op jit(solution)/shard_map/ppermute | solution.py:300
  26.6 8.6 %collective-permute-start.11 = (bf16[144,1152]{1,0:T(8,128)(2,1)S(1)}, bf16[144,1152]{1,0:T(8,128)(2,1)S(1)}, u32[]{:S(2)}, u32[]{:S(2)}) collective-permute-start(bf16[144,1152]{1,0:T(8,128)(2,1)S(1)} %get-tuple-element.89), channel_id=1, source_target_pairs={{0,8},{1,5},{2,10},{3,7},{4,12},{5,1},{6,14},{7,3},{8,0},{9,13},{1... | collective-permute-start | bytes 995336 | tf_op jit(solution)/shard_map/ppermute | solution.py:300
  32.2 6.4 %collective-permute-start.12 = (bf16[128,1152]{1,0:T(8,128)(2,1)S(1)}, bf16[128,1152]{1,0:T(8,128)(2,1)S(1)}, u32[]{:S(2)}, u32[]{:S(2)}) collective-permute-start(bf16[128,1152]{1,0:T(8,128)(2,1)S(1)} %get-tuple-element.82.x_second), channel_id=1, source_target_pairs={{0,1},{1,0},{2,3},{3,2},{4,5},{5,4},{6,7},{7,6},{8,9},{9,8},{10,11... | collective-permute-start | bytes 884744 | tf_op jit(solution)/shard_map/ppermute | solution.py:292
  32.2 6.4 %collective-permute-start.10 = (bf16[128,1152]{1,0:T(8,128)(2,1)S(1)}, bf16[128,1152]{1,0:T(8,128)(2,1)S(1)}, u32[]{:S(2)}, u32[]{:S(2)}) collective-permute-start(bf16[128,1152]{1,0:T(8,128)(2,1)S(1)} %get-tuple-element.81.x_first), channel_id=1, source_target_pairs={{0,1},{1,0},{2,3},{3,2},{4,5},{5,4},{6,7},{7,6},{8,9},{9,8},{10,11... | collective-permute-start | bytes 884744 | tf_op jit(solution)/shard_map/ppermute | solution.py:292
  35.2 7.0 %collective-permute-start.13 = (bf16[72,1152]{1,0:T(8,128)(2,1)S(1)}, bf16[72,1152]{1,0:T(8,128)(2,1)S(1)}, u32[]{:S(2)}, u32[]{:S(2)}) collective-permute-start(bf16[72,1152]{1,0:T(8,128)(2,1)S(1)} %add_convert_fusion.6), channel_id=1, source_target_pairs={{0,4},{1,9},{2,6},{3,11},{4,0},{5,13},{6,2},{7,15},{8,12},{9,1},{1... | collective-permute-start | bytes 497672 | tf_op jit(solution)/shard_map/ppermute | solution.py:300
  36.9 9.2 %collective-permute-start.9 = (bf16[72,1152]{1,0:T(8,128)(2,1)S(1)}, bf16[72,1152]{1,0:T(8,128)(2,1)S(1)}, u32[]{:S(2)}, u32[]{:S(2)}) collective-permute-start(bf16[72,1152]{1,0:T(8,128)(2,1)S(1)} %add_convert_fusion.7), channel_id=1, source_target_pairs={{0,8},{1,5},{2,10},{3,7},{4,12},{5,1},{6,14},{7,3},{8,0},{9,13},{1... | collective-permute-start | bytes 497672 | tf_op jit(solution)/shard_map/ppermute | solution.py:300
  42.3 5.4 %collective-permute-start.14 = (bf16[72,1152]{1,0:T(8,128)(2,1)S(1)}, bf16[72,1152]{1,0:T(8,128)(2,1)S(1)}, u32[]{:S(2)}, u32[]{:S(2)}) collective-permute-start(bf16[72,1152]{1,0:T(8,128)(2,1)S(1)} %add_convert_fusion.4), channel_id=1, source_target_pairs={{0,2},{1,3},{2,0},{3,1},{4,6},{5,7},{6,4},{7,5},{8,10},{9,11},{10,... | collective-permute-start | bytes 497672 | tf_op jit(solution)/shard_map/ppermute | solution.py:292
  42.6 12.0 %collective-permute-start.19 = (bf16[72,1152]{1,0:T(8,128)(2,1)S(1)}, bf16[72,1152]{1,0:T(8,128)(2,1)S(1)}, u32[]{:S(2)}, u32[]{:S(2)}) collective-permute-start(bf16[72,1152]{1,0:T(8,128)(2,1)S(1)} %get-tuple-element.105), channel_id=1, source_target_pairs={{0,4},{1,9},{2,6},{3,11},{4,0},{5,13},{6,2},{7,15},{8,12},{9,1},{1... | collective-permute-start | bytes 497672 | tf_op jit(solution)/shard_map/ppermute | solution.py:300
  44.4 10.1 %collective-permute-start.20 = (bf16[72,1152]{1,0:T(8,128)(2,1)S(1)}, bf16[72,1152]{1,0:T(8,128)(2,1)S(1)}, u32[]{:S(2)}, u32[]{:S(2)}) collective-permute-start(bf16[72,1152]{1,0:T(8,128)(2,1)S(1)} %get-tuple-element.107), channel_id=1, source_target_pairs={{0,8},{1,5},{2,10},{3,7},{4,12},{5,1},{6,14},{7,3},{8,0},{9,13},{1... | collective-permute-start | bytes 497672 | tf_op jit(solution)/shard_map/ppermute | solution.py:300
  45.9 9.8 %collective-permute-start.21 = (bf16[72,1152]{1,0:T(8,128)(2,1)S(1)}, bf16[72,1152]{1,0:T(8,128)(2,1)S(1)}, u32[]{:S(2)}, u32[]{:S(2)}) collective-permute-start(bf16[72,1152]{1,0:T(8,128)(2,1)S(1)} %get-tuple-element.109), channel_id=1, source_target_pairs={{0,12},{1,13},{2,14},{3,15},{4,8},{5,9},{6,10},{7,11},{8,4},{9,5},... | collective-permute-start | bytes 497672 | tf_op jit(solution)/shard_map/ppermute | solution.py:300
  47.8 8.6 %collective-permute-start.15 = (bf16[72,1152]{1,0:T(8,128)(2,1)S(1)}, bf16[72,1152]{1,0:T(8,128)(2,1)S(1)}, u32[]{:S(2)}, u32[]{:S(2)}) collective-permute-start(bf16[72,1152]{1,0:T(8,128)(2,1)S(1)} %add_convert_fusion.3), channel_id=1, source_target_pairs={{0,16},{4,20},{8,24},{12,28},{16,0},{20,4},{24,8},{28,12},{1,17},{... | collective-permute-start | bytes 497672 | tf_op jit(solution)/shard_map/ppermute | solution.py:292
  55.7 8.3 %collective-permute-start.22 = (bf16[72,1152]{1,0:T(8,128)(2,1)S(1)}, bf16[72,1152]{1,0:T(8,128)(2,1)S(1)}, u32[]{:S(2)}, u32[]{:S(2)}) collective-permute-start(bf16[72,1152]{1,0:T(8,128)(2,1)S(1)} %add_convert_fusion.1), channel_id=1, source_target_pairs={{0,16},{4,20},{8,24},{12,28},{16,0},{20,4},{24,8},{28,12},{1,17},{... | collective-permute-start | bytes 497672 | tf_op jit(solution)/shard_map/ppermute | solution.py:292
  56.4 7.7 %collective-permute-start.16 = (bf16[72,1152]{1,0:T(8,128)(2,1)S(1)}, bf16[72,1152]{1,0:T(8,128)(2,1)S(1)}, u32[]{:S(2)}, u32[]{:S(2)}) collective-permute-start(bf16[72,1152]{1,0:T(8,128)(2,1)S(1)} %add_convert_fusion.2.refs_0_), channel_id=1, source_target_pairs={{0,4},{1,9},{2,6},{3,11},{4,0},{5,13},{6,2},{7,15},{8,12},{9,1},{1... | collective-permute-start | bytes 497672 | tf_op jit(solution)/shard_map/ppermute | solution.py:300
  57.5 16.1 %collective-permute-start.17 = (bf16[72,1152]{1,0:T(8,128)(2,1)S(1)}, bf16[72,1152]{1,0:T(8,128)(2,1)S(1)}, u32[]{:S(2)}, u32[]{:S(2)}) collective-permute-start(bf16[72,1152]{1,0:T(8,128)(2,1)S(1)} %add_convert_fusion.2.refs_0_), channel_id=1, source_target_pairs={{0,8},{1,5},{2,10},{3,7},{4,12},{5,1},{6,14},{7,3},{8,0},{9,13},{1... | collective-permute-start | bytes 497672 | tf_op jit(solution)/shard_map/ppermute | solution.py:300
  62.9 10.7 %collective-permute-start.18 = (bf16[72,1152]{1,0:T(8,128)(2,1)S(1)}, bf16[72,1152]{1,0:T(8,128)(2,1)S(1)}, u32[]{:S(2)}, u32[]{:S(2)}) collective-permute-start(bf16[72,1152]{1,0:T(8,128)(2,1)S(1)} %add_convert_fusion.2.refs_0_), channel_id=1, source_target_pairs={{0,12},{1,13},{2,14},{3,15},{4,8},{5,9},{6,10},{7,11},{8,4},{9,5},... | collective-permute-start | bytes 497672 | tf_op jit(solution)/shard_map/ppermute | solution.py:300
  64.1 11.2 %collective-permute-start.23 = (bf16[72,1152]{1,0:T(8,128)(2,1)S(1)}, bf16[72,1152]{1,0:T(8,128)(2,1)S(1)}, u32[]{:S(2)}, u32[]{:S(2)}) collective-permute-start(bf16[72,1152]{1,0:T(8,128)(2,1)S(1)} %add_convert_fusion.refs_0_), channel_id=1, source_target_pairs={{0,4},{1,9},{2,6},{3,11},{4,0},{5,13},{6,2},{7,15},{8,12},{9,1},{1... | collective-permute-start | bytes 497672 | tf_op jit(solution)/shard_map/ppermute | solution.py:300
  65.1 11.8 %collective-permute-start.24 = (bf16[72,1152]{1,0:T(8,128)(2,1)S(1)}, bf16[72,1152]{1,0:T(8,128)(2,1)S(1)}, u32[]{:S(2)}, u32[]{:S(2)}) collective-permute-start(bf16[72,1152]{1,0:T(8,128)(2,1)S(1)} %add_convert_fusion.refs_0_), channel_id=1, source_target_pairs={{0,8},{1,5},{2,10},{3,7},{4,12},{5,1},{6,14},{7,3},{8,0},{9,13},{1... | collective-permute-start | bytes 497672 | tf_op jit(solution)/shard_map/ppermute | solution.py:300
  73.6 6.2 %collective-permute-start.25 = (bf16[72,1152]{1,0:T(8,128)(2,1)S(1)}, bf16[72,1152]{1,0:T(8,128)(2,1)S(1)}, u32[]{:S(2)}, u32[]{:S(2)}) collective-permute-start(bf16[72,1152]{1,0:T(8,128)(2,1)S(1)} %add_convert_fusion.refs_0_), channel_id=1, source_target_pairs={{0,12},{1,13},{2,14},{3,15},{4,8},{5,9},{6,10},{7,11},{8,4},{9,5},... | collective-permute-start | bytes 497672 | tf_op jit(solution)/shard_map/ppermute | solution.py:300

commit v18 on v14

--- a/solution.py
+++ b/solution.py
@@ -237,15 +237,17 @@
     gy_b[...] = gy_b_in[...] + dot_tn(w_b[...], x)
 
 
-def last_kernel(
-    x_first, x_second, y_a, y_b, q_a, q_b, gy_a_in, gy_b_in, pick_a, pick_b,
-    h0, h1, h2, h3, dq_a, gy_a, gy_b, dq_b, near_head, w_a, w_b, d_a, d_b,
+def other_pull_kernel(
+    x_first, x_second, y_a, y_b, gy_a_in, gy_b_in, gy_a, gy_b, w_a, w_b, d_a, d_b
 ):
     x = rows_of((x_first, x_second))
     far_weights(1, x, y_a, y_b, w_a, w_b, d_a, d_b)
     gy_a[...] = gy_a_in[...] + dot_tn(w_a[...], x)
+    gy_b[...] = gy_b_in[...] + dot_tn(w_b[...], x)
+
+
+def last_kernel(q_a, q_b, gy_a, gy_b, pick_a, pick_b, h0, h1, h2, h3, dq_a, dq_b, near_head):
     back_rows(q_a, gy_a, dq_a)
-    gy_b[...] = gy_b_in[...] + dot_tn(w_b[...], x)
     near_head[...] = dot_nn(pick_a[...], dq_a[...])
     back_rows(q_b, gy_b, dq_b)
     split_head(near_head[...] + dot_nn(pick_b[...], dq_b[...]), (h0, h1, h2, h3))
@@ -373,16 +375,23 @@
         (*x_2, w_2a, w_2b, gy_a, gy_b),
         8,
     )
+    x_3 = [after(rows, gy_a) for rows in x_3]
+    gy_a, gy_b = call(
+        other_pull_kernel,
+        [wide, wide],
+        [block_w, block_w, block_dots, block_dots],
+        (*x_3, y_a, y_b, gy_a, gy_b),
+        8,
+    )
     near_came, far_came = after(near_came, gy_a), after(far_came, gy_a)
     near_sent, far_sent = add(near_2, [near_came[part:]]), add(far_1, [far_came[part:]])
     near_last, far_last = cuts(near_sent, mask=2), cuts(far_sent, mask=1)
-    x_3 = [after(rows, (gy_a, near_sent, far_sent)) for rows in x_3]
     *text_parts, dq_a = call(
         last_kernel,
         [part_b] * QUAD + [wide_b],
-        [wide, wide, wide_b, ((rows_out, width), F32), block_w, block_w, block_dots, block_dots],
-        (*x_3, y_a, y_b, q_a, q_b, gy_a, gy_b, pick_a, pick_b),
-        16,
+        [wide_b, ((rows_out, width), F32)],
+        (q_a, q_b, after(gy_a, (near_sent, far_sent)), gy_b, pick_a, pick_b),
+        12,
     )
     text_others = [cuts(text_parts[k], mask=k) for k in range(1, QUAD)]
     far_sum = add(far_0, [far_came[:part], after(far_last, dq_a)])

time: 79.3 us -> 79.3 us (level)
    pallas_call x11 -> x12, Pallas kernels: 30.7 us -> 30.9 us  [call(): pl.pallas_call(kernel, out_shape=[shape(s, t) for s, t in outs], in_specs...]
  transfers between devices with their start and end apart: 26 -> 26, of which waited for: 13 -> 16; matrix products, arithmetic and copies ran while one was open for 1% -> 1% of each run, Pallas kernels for 37% -> 37%
where the time goes in v18:
time: 79.3 us; the launch traced here: 79.2 us
  Pallas kernels  30.9 us (39%)
  starting transfers between devices  28.6 us (36%)
  waiting for transfers between devices  18.4 us (23%)
    pallas_call x12, Pallas kernels, call(): pl.pallas_call(kernel, out_shape=[shape(s, t) for s, t in outs], in_specs...  30.9 us
    ppermute x26, starting transfers between devices, swap(): return lax.ppermute(array, axis, [(i, i ^ mask) for i in range(size)])  28.6 us
    ppermute x26, waiting for transfers between devices, swap(): return lax.ppermute(array, axis, [(i, i ^ mask) for i in range(size)])  18.4 us
  transfers between devices with their start and end apart: 26, of which 16 were waited for; matrix products, arithmetic and copies ran while one was open for 1% of the time, Pallas kernels for 37%

profile of v18, /device:TPU:0, one launch (start us, length us, event | category | flops | bytes accessed | tf_op | source)
XLA Modules:
  0.0 79.2 jit_solution(15454887048112925676)
XLA Ops:
  1.3 2.9 %collective-permute-start = (bf16[256,1152]{1,0:T(8,128)(2,1)}, bf16[256,1152]{1,0:T(8,128)(2,1)S(1)}, u32[]{:S(2)}, u32[]{:S(2)}) collective-permute-start(bf16[256,1152]{1,0:T(8,128)(2,1)} %t0_far), channel_id=1, source_target_pairs={{0,2},{1,3},{2,0},{3,1},{4,6},{5,7},{6,4},{7,5},{8,10},{9,11},{10,... | collective-permute-start | bytes 1769480 | tf_op jit(solution)/shard_map/ppermute | solution.py:289
  4.2 7.4 %shard_map.75 = (f32[512,1152]{1,0:T(8,128)S(1)}, bf16[512,1152]{1,0:T(8,128)(2,1)S(1)}, f32[512,1152]{1,0:T(8,128)S(1)}, bf16[512,1152]{1,0:T(8,128)(2,1)S(1)},...) custom-call(bf16[256,1152]{1,0:T(8,128)(2,1)S(1)} %collective-permut, ...), custom_call_target="tpu_custom_call" | custom-call | tf_op jit(solution)/shard_map/pallas_call | solution.py:276
  11.6 2.6 %shard_map.76 = (f32[512,1152]{1,0:T(8,128)S(1)}, bf16[576,512]{1,0:T(8,128)(2,1)S(1)}, bf16[288,512]{1,0:T(8,128)(2,1)S(1)}) custom-call(s32[2]{0:T(128)S(1)} %pad_add_fusion.place, bf16[256,1152]{1,0:T(8,128)(2,1)S(1)} %get-tuple-element.64.t0, bf16[256,1152]{1,0:T(8,128)(2,1)S(1)} %collective-permute-done.1.t1, ...), custom_call_target="tpu_custom_call" | custom-call | tf_op jit(solution)/shard_map/pallas_call | solution.py:276
  14.2 4.3 %collective-permute-done.refs_0_ = bf16[256,1152]{1,0:T(8,128)(2,1)S(1)} collective-permute-done((bf16[256,1152]{1,0:T(8,128)(2,1)}, bf16[256,1152]{1,0:T(8,128)(2,1)S(1)}, u32[]{:S(2)}, u32[]{:S(2)}) %collective-permute-start) | collective-permute-done | bytes 589856 | tf_op jit(solution)/shard_map/ppermute | solution.py:289
  20.7 5.2 %shard_map.77 = (f32[512,1152]{1,0:T(8,128)S(1)}, bf16[512,1152]{1,0:T(8,128)(2,1)S(1)}, bf16[512,512]{1,0:T(8,128)(2,1)S(1)}, bf16[512,1152]{1,0:T(8,128)(2,1)S...) custom-call(bf16[256,1152]{1,0:T(8,128)(2,1)S(1)} %collective-permut, ...), custom_call_target="tpu_custom_call" | custom-call | tf_op jit(solution)/shard_map/pallas_call | solution.py:276
  25.9 2.2 %collective-permute-start.7 = (bf16[144,1152]{1,0:T(8,128)(2,1)S(1)}, bf16[144,1152]{1,0:T(8,128)(2,1)S(1)}, u32[]{:S(2)}, u32[]{:S(2)}) collective-permute-start(bf16[144,1152]{1,0:T(8,128)(2,1)S(1)} %get-tuple-element.76), channel_id=1, source_target_pairs={{0,4},{4,0},{8,12},{12,8},{16,20},{20,16},{24,28},{28,24},{1,5},{5... | collective-permute-start | bytes 995336 | tf_op jit(solution)/shard_map/ppermute | solution.py:289
  28.1 1.6 %collective-permute-start.12 = (bf16[144,1152]{1,0:T(8,128)(2,1)S(1)}, bf16[144,1152]{1,0:T(8,128)(2,1)S(1)}, u32[]{:S(2)}, u32[]{:S(2)}) collective-permute-start(bf16[144,1152]{1,0:T(8,128)(2,1)S(1)} %get-tuple-element.98), channel_id=1, source_target_pairs={{0,8},{4,12},{8,0},{12,4},{16,24},{20,28},{24,16},{28,20},{1,9},{5... | collective-permute-start | bytes 995336 | tf_op jit(solution)/shard_map/ppermute | solution.py:289
  29.6 2.0 %shard_map.78 = (f32[512,1152]{1,0:T(8,128)S(1)}, bf16[288,512]{1,0:T(8,128)(2,1)S(1)}) custom-call(s32[2]{0:T(128)S(1)} %pad_add_fusion.place, bf16[256,1152]{1,0:T(8,128)(2,1)S(1)} %collective-permute-done.refs_0_, bf16[64,1152]{1,0:T(8,128)(2,1)S(1)} %collective-permute-done.3.refs_1_, bf16[64,1152]{1,0:T(8,128)(2,1)S(1)} %collective-permute-done.4.refs_2_, ...), custom_call_target="tpu_custom_call" | custom-call | tf_op jit(solution)/shard_map/pallas_call | solution.py:276
  31.6 1.9 %shard_map.79 = (bf16[128,1152]{1,0:T(8,128)(2,1)S(1)}, bf16[128,1152]{1,0:T(8,128)(2,1)S(1)}, bf16[256,512]{1,0:T(8,128)(2,1)S(1)}, bf16[256,512]{1,0:T(8,128)(2,1)S(1)}) custom-call(bf16[256,1152]{1,0:T(8,128)(2,1)S(1)} %collective-permute-done.8.i2, bf16[1152,1152]{1,0:T(8,128)(2,1)S(1)} %get-tuple-element.81.image_head.head, ...), custom_call_target="tpu_custom_call" | custom-call | tf_op jit(solution)/shard_map/pallas_call | solution.py:276
  34.2 0.9 %shard_map.80 = (f32[512,1152]{1,0:T(8,128)S(1)}, f32[512,1152]{1,0:T(8,128)S(1)}) custom-call(bf16[128,1152]{1,0:T(8,128)(2,1)S(1)} %get-tuple-element.84.x_first, bf16[128,1152]{1,0:T(8,128)(2,1)S(1)} %get-tuple-element.85.x_second, bf16[256,512]{1,0:T(8,128)(2,1)S(1)} %get-tuple-element.86.w_a, bf16[256,512]{1,0:T(8,128)(2,1)S(1)} %get-tuple-element.87.w_b, ...), custom_call_target="tpu_custom_call" | custom-call | tf_op jit(solution)/shard_map/pallas_call | solution.py:276
  35.7 1.6 %shard_map.81 = (f32[512,1152]{1,0:T(8,128)S(1)}, f32[512,1152]{1,0:T(8,128)S(1)}) custom-call(bf16[128,1152]{1,0:T(8,128)(2,1)S(1)} %collective-permute-done.9.x_first, bf16[128,1152]{1,0:T(8,128)(2,1)S(1)} %collective-permute-done.10.x_second, bf16[512,1152]{1,0:T(8,128)(2,1)S(1)} %get-tuple-element.82.y_a, bf16[512,1152]{1,0:T(8,128)(2,1)S(1)} %get-tuple-element.83.y_b, ...), custom_call_target="tpu_custom_call" | custom-call | tf_op jit(solution)/shard_map/pallas_call | solution.py:276
  38.3 1.8 %collective-permute-start.11 = (bf16[72,1152]{1,0:T(8,128)(2,1)S(1)}, bf16[72,1152]{1,0:T(8,128)(2,1)S(1)}, u32[]{:S(2)}, u32[]{:S(2)}) collective-permute-start(bf16[72,1152]{1,0:T(8,128)(2,1)S(1)} %add_convert_fusion.7), channel_id=1, source_target_pairs={{0,8},{4,12},{8,0},{12,4},{16,24},{20,28},{24,16},{28,20},{1,9},{5... | collective-permute-start | bytes 497672 | tf_op jit(solution)/shard_map/ppermute | solution.py:289
  40.1 1.8 %shard_map.82 = (bf16[72,1152]{1,0:T(8,128)(2,1)S(1)}, bf16[72,1152]{1,0:T(8,128)(2,1)S(1)}, bf16[72,1152]{1,0:T(8,128)(2,1)S(1)}, bf16[72,1152]{1,0:T(8,128)(2,1)S(1)}, bf16[512,1152]{1,0:T(8,128)(2,1)S(1)}) custom-call(f32[512,1152]{1,0:T(8,128)S(1)} %get-tuple-element.95.q_a, f32[512,1152]{1,0:T(8,128)S(1)} %get-tuple-element.96.q_b, ...), custom_call_target="tpu_custom_call" | custom-call | tf_op jit(solution)/shard_map/pallas_call | solution.py:276
  41.9 1.7 %collective-permute-done.13 = bf16[72,1152]{1,0:T(8,128)(2,1)S(1)} collective-permute-done((bf16[72,1152]{1,0:T(8,128)(2,1)S(1)}, bf16[72,1152]{1,0:T(8,128)(2,1)S(1)}, u32[]{:S(2)}, u32[]{:S(2)}) %collective-permute-start.13) | collective-permute-done | bytes 165920 | tf_op jit(solution)/shard_map/ppermute | solution.py:289
  43.7 1.6 %collective-permute-start.14 = (bf16[72,1152]{1,0:T(8,128)(2,1)S(1)}, bf16[72,1152]{1,0:T(8,128)(2,1)S(1)}, u32[]{:S(2)}, u32[]{:S(2)}) collective-permute-start(bf16[72,1152]{1,0:T(8,128)(2,1)S(1)} %add_convert_fusion.4), channel_id=1, source_target_pairs={{0,2},{1,3},{2,0},{3,1},{4,6},{5,7},{6,4},{7,5},{8,10},{9,11},{10,... | collective-permute-start | bytes 497672 | tf_op jit(solution)/shard_map/ppermute | solution.py:289
  45.3 0.7 collective-permute-start.19
  46.0 1.6 %collective-permute-start.20 = (bf16[72,1152]{1,0:T(8,128)(2,1)S(1)}, bf16[72,1152]{1,0:T(8,128)(2,1)S(1)}, u32[]{:S(2)}, u32[]{:S(2)}) collective-permute-start(bf16[72,1152]{1,0:T(8,128)(2,1)S(1)} %get-tuple-element.113), channel_id=1, source_target_pairs={{0,8},{4,12},{8,0},{12,4},{16,24},{20,28},{24,16},{28,20},{1,9},{5... | collective-permute-start | bytes 497672 | tf_op jit(solution)/shard_map/ppermute | solution.py:289
  47.6 1.2 %collective-permute-start.21 = (bf16[72,1152]{1,0:T(8,128)(2,1)S(1)}, bf16[72,1152]{1,0:T(8,128)(2,1)S(1)}, u32[]{:S(2)}, u32[]{:S(2)}) collective-permute-start(bf16[72,1152]{1,0:T(8,128)(2,1)S(1)} %get-tuple-element.115), channel_id=1, source_target_pairs={{0,12},{4,8},{8,4},{12,0},{16,28},{20,24},{24,20},{28,16},{1,13},{... | collective-permute-start | bytes 497672 | tf_op jit(solution)/shard_map/ppermute | solution.py:289
  49.2 2.7 %collective-permute-start.15 = (bf16[72,1152]{1,0:T(8,128)(2,1)S(1)}, bf16[72,1152]{1,0:T(8,128)(2,1)S(1)}, u32[]{:S(2)}, u32[]{:S(2)}) collective-permute-start(bf16[72,1152]{1,0:T(8,128)(2,1)S(1)} %add_convert_fusion.3), channel_id=1, source_target_pairs={{0,16},{4,20},{8,24},{12,28},{16,0},{20,4},{24,8},{28,12},{1,17},{... | collective-permute-start | bytes 497672 | tf_op jit(solution)/shard_map/ppermute | solution.py:289
  51.9 2.0 %shard_map.84 = f32[256,1152]{1,0:T(8,128)} custom-call(bf16[512,1152]{1,0:T(8,128)(2,1)S(1)} %get-tuple-element.109.back, bf16[1152,1152]{1,0:T(8,128)(2,1)S(1)} %get-tuple-element.70.refs_5_.head), custom_call_target="tpu_custom_call" | custom-call | flops 1358954496 | tf_op jit(solution)/shard_map/pallas_call | solution.py:276
  53.9 2.0 %shard_map.83 = f32[256,1152]{1,0:T(8,128)} custom-call(bf16[512,1152]{1,0:T(8,128)(2,1)S(1)} %get-tuple-element.108.back, bf16[1152,1152]{1,0:T(8,128)(2,1)S(1)} %get-tuple-element.81.image_head.head), custom_call_target="tpu_custom_call" | custom-call | flops 1358954496 | tf_op jit(solution)/shard_map/pallas_call | solution.py:276
  56.0 2.9 %collective-permute-done.21 = bf16[72,1152]{1,0:T(8,128)(2,1)S(1)} collective-permute-done((bf16[72,1152]{1,0:T(8,128)(2,1)S(1)}, bf16[72,1152]{1,0:T(8,128)(2,1)S(1)}, u32[]{:S(2)}, u32[]{:S(2)}) %collective-permute-start.21) | collective-permute-done | bytes 165920 | tf_op jit(solution)/shard_map/ppermute | solution.py:289
  59.5 1.6 %collective-permute-start.16 = (bf16[72,1152]{1,0:T(8,128)(2,1)S(1)}, bf16[72,1152]{1,0:T(8,128)(2,1)S(1)}, u32[]{:S(2)}, u32[]{:S(2)}) collective-permute-start(bf16[72,1152]{1,0:T(8,128)(2,1)S(1)} %add_convert_fusion.2.refs_0_), channel_id=1, source_target_pairs={{0,4},{4,0},{8,12},{12,8},{16,20},{20,16},{24,28},{28,24},{1,5},{5... | collective-permute-start | bytes 497672 | tf_op jit(solution)/shard_map/ppermute | solution.py:289
  61.1 2.5 %collective-permute-start.17 = (bf16[72,1152]{1,0:T(8,128)(2,1)S(1)}, bf16[72,1152]{1,0:T(8,128)(2,1)S(1)}, u32[]{:S(2)}, u32[]{:S(2)}) collective-permute-start(bf16[72,1152]{1,0:T(8,128)(2,1)S(1)} %add_convert_fusion.2.refs_0_), channel_id=1, source_target_pairs={{0,8},{4,12},{8,0},{12,4},{16,24},{20,28},{24,16},{28,20},{1,9},{5... | collective-permute-start | bytes 497672 | tf_op jit(solution)/shard_map/ppermute | solution.py:289
  63.6 0.9 %collective-permute-start.18 = (bf16[72,1152]{1,0:T(8,128)(2,1)S(1)}, bf16[72,1152]{1,0:T(8,128)(2,1)S(1)}, u32[]{:S(2)}, u32[]{:S(2)}) collective-permute-start(bf16[72,1152]{1,0:T(8,128)(2,1)S(1)} %add_convert_fusion.2.refs_0_), channel_id=1, source_target_pairs={{0,12},{4,8},{8,4},{12,0},{16,28},{20,24},{24,20},{28,16},{1,13},{... | collective-permute-start | bytes 497672 | tf_op jit(solution)/shard_map/ppermute | solution.py:289
  64.5 2.1 %collective-permute-done.22 = bf16[72,1152]{1,0:T(8,128)(2,1)S(1)} collective-permute-done((bf16[72,1152]{1,0:T(8,128)(2,1)S(1)}, bf16[72,1152]{1,0:T(8,128)(2,1)S(1)}, u32[]{:S(2)}, u32[]{:S(2)}) %collective-permute-start.22) | collective-permute-done | bytes 165920 | tf_op jit(solution)/shard_map/ppermute | solution.py:289
  66.8 1.9 %collective-permute-start.23 = (bf16[72,1152]{1,0:T(8,128)(2,1)S(1)}, bf16[72,1152]{1,0:T(8,128)(2,1)S(1)}, u32[]{:S(2)}, u32[]{:S(2)}) collective-permute-start(bf16[72,1152]{1,0:T(8,128)(2,1)S(1)} %add_convert_fusion.refs_0_), channel_id=1, source_target_pairs={{0,4},{4,0},{8,12},{12,8},{16,20},{20,16},{24,28},{28,24},{1,5},{5... | collective-permute-start | bytes 497672 | tf_op jit(solution)/shard_map/ppermute | solution.py:289
  68.8 2.4 %collective-permute-start.24 = (bf16[72,1152]{1,0:T(8,128)(2,1)S(1)}, bf16[72,1152]{1,0:T(8,128)(2,1)S(1)}, u32[]{:S(2)}, u32[]{:S(2)}) collective-permute-start(bf16[72,1152]{1,0:T(8,128)(2,1)S(1)} %add_convert_fusion.refs_0_), channel_id=1, source_target_pairs={{0,8},{4,12},{8,0},{12,4},{16,24},{20,28},{24,16},{28,20},{1,9},{5... | collective-permute-start | bytes 497672 | tf_op jit(solution)/shard_map/ppermute | solution.py:289
  71.2 2.4 %collective-permute-done.18.refs_3_ = bf16[72,1152]{1,0:T(8,128)(2,1)S(1)} collective-permute-done((bf16[72,1152]{1,0:T(8,128)(2,1)S(1)}, bf16[72,1152]{1,0:T(8,128)(2,1)S(1)}, u32[]{:S(2)}, u32[]{:S(2)}) %collective-permute-start.18) | collective-permute-done | bytes 165920 | tf_op jit(solution)/shard_map/ppermute | solution.py:289
  73.6 1.7 %shard_map.85 = f32[288,1152]{1,0:T(8,128)} custom-call(s32[2]{0:T(128)S(1)} %pad_add_fusion.place, bf16[72,1152]{1,0:T(8,128)(2,1)S(1)} %add_convert_fusion.2.refs_0_, bf16[72,1152]{1,0:T(8,128)(2,1)S(1)} %collective-permute-done.16.refs_1_, bf16[72,1152]{1,0:T(8,128)(2,1)S(1)} %collective-permute-done.17.refs_2_, ...), custom_call_target="tpu_custom_call" | custom-call | tf_op jit(solution)/shard_map/pallas_call | solution.py:276
  75.5 2.0 %collective-permute-done.25.refs_3_ = bf16[72,1152]{1,0:T(8,128)(2,1)S(1)} collective-permute-done((bf16[72,1152]{1,0:T(8,128)(2,1)S(1)}, bf16[72,1152]{1,0:T(8,128)(2,1)S(1)}, u32[]{:S(2)}, u32[]{:S(2)}) %collective-permute-start.25) | collective-permute-done | bytes 165920 | tf_op jit(solution)/shard_map/ppermute | solution.py:289
  77.5 1.7 %shard_map.86 = f32[288,1152]{1,0:T(8,128)} custom-call(s32[2]{0:T(128)S(1)} %pad_add_fusion.place, bf16[72,1152]{1,0:T(8,128)(2,1)S(1)} %add_convert_fusion.refs_0_, bf16[72,1152]{1,0:T(8,128)(2,1)S(1)} %collective-permute-done.23.refs_1_, bf16[72,1152]{1,0:T(8,128)(2,1)S(1)} %collective-permute-done.24.refs_2_, ...), custom_call_target="tpu_custom_call" | custom-call | tf_op jit(solution)/shard_map/pallas_call | solution.py:276
  (41 shorter events, 6.5 us)
Async XLA Ops:
  0.7 3.5 %collective-permute-start.1 = (bf16[256,1152]{1,0:T(8,128)(2,1)}, bf16[256,1152]{1,0:T(8,128)(2,1)S(1)}, u32[]{:S(2)}, u32[]{:S(2)}) collective-permute-start(bf16[256,1152]{1,0:T(8,128)(2,1)} %t0_far), channel_id=1, source_target_pairs={{0,1},{1,0},{2,3},{3,2},{4,5},{5,4},{6,7},{7,6},{8,9},{9,8},{10,11... | collective-permute-start | bytes 1769480 | tf_op jit(solution)/shard_map/ppermute | solution.py:289
  1.2 3.0 %collective-permute-start.2 = (bf16[256,1152]{1,0:T(8,128)(2,1)}, bf16[256,1152]{1,0:T(8,128)(2,1)S(1)}, u32[]{:S(2)}, u32[]{:S(2)}) collective-permute-start(bf16[256,1152]{1,0:T(8,128)(2,1)} %i0_far), channel_id=1, source_target_pairs={{0,1},{1,0},{2,3},{3,2},{4,5},{5,4},{6,7},{7,6},{8,9},{9,8},{10,11... | collective-permute-start | bytes 1769480 | tf_op jit(solution)/shard_map/ppermute | solution.py:289
  1.3 17.2 %collective-permute-start = (bf16[256,1152]{1,0:T(8,128)(2,1)}, bf16[256,1152]{1,0:T(8,128)(2,1)S(1)}, u32[]{:S(2)}, u32[]{:S(2)}) collective-permute-start(bf16[256,1152]{1,0:T(8,128)(2,1)} %t0_far), channel_id=1, source_target_pairs={{0,2},{1,3},{2,0},{3,1},{4,6},{5,7},{6,4},{7,5},{8,10},{9,11},{10,... | collective-permute-start | bytes 1769480 | tf_op jit(solution)/shard_map/ppermute | solution.py:289
  4.2 27.5 %collective-permute-start.8 = (bf16[256,1152]{1,0:T(8,128)(2,1)}, bf16[256,1152]{1,0:T(8,128)(2,1)S(1)}, u32[]{:S(2)}, u32[]{:S(2)}) collective-permute-start(bf16[256,1152]{1,0:T(8,128)(2,1)} %i0_far), channel_id=1, source_target_pairs={{0,2},{1,3},{2,0},{3,1},{4,6},{5,7},{6,4},{7,5},{8,10},{9,11},{10,... | collective-permute-start | bytes 1769480 | tf_op jit(solution)/shard_map/ppermute | solution.py:289
  18.5 1.4 %collective-permute-start.3 = (bf16[64,1152]{1,0:T(8,128)(2,1)S(1)}, bf16[64,1152]{1,0:T(8,128)(2,1)S(1)}, u32[]{:S(2)}, u32[]{:S(2)}) collective-permute-start(bf16[64,1152]{1,0:T(8,128)(2,1)S(1)} %get-tuple-element.121), channel_id=1, source_target_pairs={{0,1},{1,0},{2,3},{3,2},{4,5},{5,4},{6,7},{7,6},{8,9},{9,8},{10,11... | collective-permute-start | bytes 442376 | tf_op jit(solution)/shard_map/ppermute | solution.py:289
  18.6 1.6 %collective-permute-start.4 = (bf16[64,1152]{1,0:T(8,128)(2,1)S(1)}, bf16[64,1152]{1,0:T(8,128)(2,1)S(1)}, u32[]{:S(2)}, u32[]{:S(2)}) collective-permute-start(bf16[64,1152]{1,0:T(8,128)(2,1)S(1)} %get-tuple-element.120), channel_id=1, source_target_pairs={{0,1},{1,0},{2,3},{3,2},{4,5},{5,4},{6,7},{7,6},{8,9},{9,8},{10,11... | collective-permute-start | bytes 442376 | tf_op jit(solution)/shard_map/ppermute | solution.py:289
  19.1 1.4 %collective-permute-start.5 = (bf16[64,1152]{1,0:T(8,128)(2,1)S(1)}, bf16[64,1152]{1,0:T(8,128)(2,1)S(1)}, u32[]{:S(2)}, u32[]{:S(2)}) collective-permute-start(bf16[64,1152]{1,0:T(8,128)(2,1)S(1)} %get-tuple-element.119), channel_id=1, source_target_pairs={{0,1},{1,0},{2,3},{3,2},{4,5},{5,4},{6,7},{7,6},{8,9},{9,8},{10,11... | collective-permute-start | bytes 442376 | tf_op jit(solution)/shard_map/ppermute | solution.py:289
  19.2 1.5 %collective-permute-start.6 = (bf16[64,1152]{1,0:T(8,128)(2,1)S(1)}, bf16[64,1152]{1,0:T(8,128)(2,1)S(1)}, u32[]{:S(2)}, u32[]{:S(2)}) collective-permute-start(bf16[64,1152]{1,0:T(8,128)(2,1)S(1)} %get-tuple-element.118), channel_id=1, source_target_pairs={{0,1},{1,0},{2,3},{3,2},{4,5},{5,4},{6,7},{7,6},{8,9},{9,8},{10,11... | collective-permute-start | bytes 442376 | tf_op jit(solution)/shard_map/ppermute | solution.py:289
  25.9 11.4 %collective-permute-start.7 = (bf16[144,1152]{1,0:T(8,128)(2,1)S(1)}, bf16[144,1152]{1,0:T(8,128)(2,1)S(1)}, u32[]{:S(2)}, u32[]{:S(2)}) collective-permute-start(bf16[144,1152]{1,0:T(8,128)(2,1)S(1)} %get-tuple-element.76), channel_id=1, source_target_pairs={{0,4},{4,0},{8,12},{12,8},{16,20},{20,16},{24,28},{28,24},{1,5},{5... | collective-permute-start | bytes 995336 | tf_op jit(solution)/shard_map/ppermute | solution.py:289
  28.1 9.7 %collective-permute-start.12 = (bf16[144,1152]{1,0:T(8,128)(2,1)S(1)}, bf16[144,1152]{1,0:T(8,128)(2,1)S(1)}, u32[]{:S(2)}, u32[]{:S(2)}) collective-permute-start(bf16[144,1152]{1,0:T(8,128)(2,1)S(1)} %get-tuple-element.98), channel_id=1, source_target_pairs={{0,8},{4,12},{8,0},{12,4},{16,24},{20,28},{24,16},{28,20},{1,9},{5... | collective-permute-start | bytes 995336 | tf_op jit(solution)/shard_map/ppermute | solution.py:289
  33.6 1.6 %collective-permute-start.10 = (bf16[128,1152]{1,0:T(8,128)(2,1)S(1)}, bf16[128,1152]{1,0:T(8,128)(2,1)S(1)}, u32[]{:S(2)}, u32[]{:S(2)}) collective-permute-start(bf16[128,1152]{1,0:T(8,128)(2,1)S(1)} %get-tuple-element.85.x_second), channel_id=1, source_target_pairs={{0,1},{1,0},{2,3},{3,2},{4,5},{5,4},{6,7},{7,6},{8,9},{9,8},{10,11... | collective-permute-start | bytes 884744 | tf_op jit(solution)/shard_map/ppermute | solution.py:289
  33.7 2.0 %collective-permute-start.9 = (bf16[128,1152]{1,0:T(8,128)(2,1)S(1)}, bf16[128,1152]{1,0:T(8,128)(2,1)S(1)}, u32[]{:S(2)}, u32[]{:S(2)}) collective-permute-start(bf16[128,1152]{1,0:T(8,128)(2,1)S(1)} %get-tuple-element.84.x_first), channel_id=1, source_target_pairs={{0,1},{1,0},{2,3},{3,2},{4,5},{5,4},{6,7},{7,6},{8,9},{9,8},{10,11... | collective-permute-start | bytes 884744 | tf_op jit(solution)/shard_map/ppermute | solution.py:289
  37.8 5.8 %collective-permute-start.13 = (bf16[72,1152]{1,0:T(8,128)(2,1)S(1)}, bf16[72,1152]{1,0:T(8,128)(2,1)S(1)}, u32[]{:S(2)}, u32[]{:S(2)}) collective-permute-start(bf16[72,1152]{1,0:T(8,128)(2,1)S(1)} %add_convert_fusion.6), channel_id=1, source_target_pairs={{0,4},{4,0},{8,12},{12,8},{16,20},{20,16},{24,28},{28,24},{1,5},{5... | collective-permute-start | bytes 497672 | tf_op jit(solution)/shard_map/ppermute | solution.py:289
  38.3 10.5 %collective-permute-start.11 = (bf16[72,1152]{1,0:T(8,128)(2,1)S(1)}, bf16[72,1152]{1,0:T(8,128)(2,1)S(1)}, u32[]{:S(2)}, u32[]{:S(2)}) collective-permute-start(bf16[72,1152]{1,0:T(8,128)(2,1)S(1)} %add_convert_fusion.7), channel_id=1, source_target_pairs={{0,8},{4,12},{8,0},{12,4},{16,24},{20,28},{24,16},{28,20},{1,9},{5... | collective-permute-start | bytes 497672 | tf_op jit(solution)/shard_map/ppermute | solution.py:289
  43.7 5.4 %collective-permute-start.14 = (bf16[72,1152]{1,0:T(8,128)(2,1)S(1)}, bf16[72,1152]{1,0:T(8,128)(2,1)S(1)}, u32[]{:S(2)}, u32[]{:S(2)}) collective-permute-start(bf16[72,1152]{1,0:T(8,128)(2,1)S(1)} %add_convert_fusion.4), channel_id=1, source_target_pairs={{0,2},{1,3},{2,0},{3,1},{4,6},{5,7},{6,4},{7,5},{8,10},{9,11},{10,... | collective-permute-start | bytes 497672 | tf_op jit(solution)/shard_map/ppermute | solution.py:289
  45.3 10.7 %collective-permute-start.19 = (bf16[72,1152]{1,0:T(8,128)(2,1)S(1)}, bf16[72,1152]{1,0:T(8,128)(2,1)S(1)}, u32[]{:S(2)}, u32[]{:S(2)}) collective-permute-start(bf16[72,1152]{1,0:T(8,128)(2,1)S(1)} %get-tuple-element.111), channel_id=1, source_target_pairs={{0,4},{4,0},{8,12},{12,8},{16,20},{20,16},{24,28},{28,24},{1,5},{5... | collective-permute-start | bytes 497672 | tf_op jit(solution)/shard_map/ppermute | solution.py:289
  46.0 10.0 %collective-permute-start.20 = (bf16[72,1152]{1,0:T(8,128)(2,1)S(1)}, bf16[72,1152]{1,0:T(8,128)(2,1)S(1)}, u32[]{:S(2)}, u32[]{:S(2)}) collective-permute-start(bf16[72,1152]{1,0:T(8,128)(2,1)S(1)} %get-tuple-element.113), channel_id=1, source_target_pairs={{0,8},{4,12},{8,0},{12,4},{16,24},{20,28},{24,16},{28,20},{1,9},{5... | collective-permute-start | bytes 497672 | tf_op jit(solution)/shard_map/ppermute | solution.py:289
  47.6 11.4 %collective-permute-start.21 = (bf16[72,1152]{1,0:T(8,128)(2,1)S(1)}, bf16[72,1152]{1,0:T(8,128)(2,1)S(1)}, u32[]{:S(2)}, u32[]{:S(2)}) collective-permute-start(bf16[72,1152]{1,0:T(8,128)(2,1)S(1)} %get-tuple-element.115), channel_id=1, source_target_pairs={{0,12},{4,8},{8,4},{12,0},{16,28},{20,24},{24,20},{28,16},{1,13},{... | collective-permute-start | bytes 497672 | tf_op jit(solution)/shard_map/ppermute | solution.py:289
  49.2 10.2 %collective-permute-start.15 = (bf16[72,1152]{1,0:T(8,128)(2,1)S(1)}, bf16[72,1152]{1,0:T(8,128)(2,1)S(1)}, u32[]{:S(2)}, u32[]{:S(2)}) collective-permute-start(bf16[72,1152]{1,0:T(8,128)(2,1)S(1)} %add_convert_fusion.3), channel_id=1, source_target_pairs={{0,16},{4,20},{8,24},{12,28},{16,0},{20,4},{24,8},{28,12},{1,17},{... | collective-permute-start | bytes 497672 | tf_op jit(solution)/shard_map/ppermute | solution.py:289
  59.0 7.6 %collective-permute-start.22 = (bf16[72,1152]{1,0:T(8,128)(2,1)S(1)}, bf16[72,1152]{1,0:T(8,128)(2,1)S(1)}, u32[]{:S(2)}, u32[]{:S(2)}) collective-permute-start(bf16[72,1152]{1,0:T(8,128)(2,1)S(1)} %add_convert_fusion.1), channel_id=1, source_target_pairs={{0,16},{4,20},{8,24},{12,28},{16,0},{20,4},{24,8},{28,12},{1,17},{... | collective-permute-start | bytes 497672 | tf_op jit(solution)/shard_map/ppermute | solution.py:289
  59.5 7.3 %collective-permute-start.16 = (bf16[72,1152]{1,0:T(8,128)(2,1)S(1)}, bf16[72,1152]{1,0:T(8,128)(2,1)S(1)}, u32[]{:S(2)}, u32[]{:S(2)}) collective-permute-start(bf16[72,1152]{1,0:T(8,128)(2,1)S(1)} %add_convert_fusion.2.refs_0_), channel_id=1, source_target_pairs={{0,4},{4,0},{8,12},{12,8},{16,20},{20,16},{24,28},{28,24},{1,5},{5... | collective-permute-start | bytes 497672 | tf_op jit(solution)/shard_map/ppermute | solution.py:289
  61.1 10.1 %collective-permute-start.17 = (bf16[72,1152]{1,0:T(8,128)(2,1)S(1)}, bf16[72,1152]{1,0:T(8,128)(2,1)S(1)}, u32[]{:S(2)}, u32[]{:S(2)}) collective-permute-start(bf16[72,1152]{1,0:T(8,128)(2,1)S(1)} %add_convert_fusion.2.refs_0_), channel_id=1, source_target_pairs={{0,8},{4,12},{8,0},{12,4},{16,24},{20,28},{24,16},{28,20},{1,9},{5... | collective-permute-start | bytes 497672 | tf_op jit(solution)/shard_map/ppermute | solution.py:289
  63.6 10.0 %collective-permute-start.18 = (bf16[72,1152]{1,0:T(8,128)(2,1)S(1)}, bf16[72,1152]{1,0:T(8,128)(2,1)S(1)}, u32[]{:S(2)}, u32[]{:S(2)}) collective-permute-start(bf16[72,1152]{1,0:T(8,128)(2,1)S(1)} %add_convert_fusion.2.refs_0_), channel_id=1, source_target_pairs={{0,12},{4,8},{8,4},{12,0},{16,28},{20,24},{24,20},{28,16},{1,13},{... | collective-permute-start | bytes 497672 | tf_op jit(solution)/shard_map/ppermute | solution.py:289
  66.8 8.7 %collective-permute-start.23 = (bf16[72,1152]{1,0:T(8,128)(2,1)S(1)}, bf16[72,1152]{1,0:T(8,128)(2,1)S(1)}, u32[]{:S(2)}, u32[]{:S(2)}) collective-permute-start(bf16[72,1152]{1,0:T(8,128)(2,1)S(1)} %add_convert_fusion.refs_0_), channel_id=1, source_target_pairs={{0,4},{4,0},{8,12},{12,8},{16,20},{20,16},{24,28},{28,24},{1,5},{5... | collective-permute-start | bytes 497672 | tf_op jit(solution)/shard_map/ppermute | solution.py:289
  68.8 6.8 %collective-permute-start.24 = (bf16[72,1152]{1,0:T(8,128)(2,1)S(1)}, bf16[72,1152]{1,0:T(8,128)(2,1)S(1)}, u32[]{:S(2)}, u32[]{:S(2)}) collective-permute-start(bf16[72,1152]{1,0:T(8,128)(2,1)S(1)} %add_convert_fusion.refs_0_), channel_id=1, source_target_pairs={{0,8},{4,12},{8,0},{12,4},{16,24},{20,28},{24,16},{28,20},{1,9},{5... | collective-permute-start | bytes 497672 | tf_op jit(solution)/shard_map/ppermute | solution.py:289
  71.2 6.3 %collective-permute-start.25 = (bf16[72,1152]{1,0:T(8,128)(2,1)S(1)}, bf16[72,1152]{1,0:T(8,128)(2,1)S(1)}, u32[]{:S(2)}, u32[]{:S(2)}) collective-permute-start(bf16[72,1152]{1,0:T(8,128)(2,1)S(1)} %add_convert_fusion.refs_0_), channel_id=1, source_target_pairs={{0,12},{4,8},{8,4},{12,0},{16,28},{20,24},{24,20},{28,16},{1,13},{... | collective-permute-start | bytes 497672 | tf_op jit(solution)/shard_map/ppermute | solution.py:289

commit v19 on v14

--- a/solution.py
+++ b/solution.py
@@ -184,28 +184,15 @@
 
 
 def image_kernel(*refs):
-    *features, text_head, p_a, x_a, gx_in, pick_i, q_b, y_b, w_ab, dp_a = refs[:-8]
-    near_0, near_2, near_sent, far_0, far_1, far_sent, dots, gx = refs[-8:]
+    *features, text_head, p_a, x_a, gx_in, pick_i, q_b, y_b, w_ab, dp_a = refs[:-6]
+    *parts, dots, gx = refs[-6:]
     q_b[...] = dot_nn(rows_of(features), text_head[...])
     unit_rows(q_b, y_b)
     dots[...] = dot_nt(x_a[...], y_b[...])
     weight_rows(dots, w_ab)
     gx[...] = gx_in[...] + dot_nn(w_ab[...], y_b[...])
     back_rows(p_a, gx, dp_a)
-    head = dot_nn(pick_i[...], dp_a[...]).astype(BF16)
-    part = near_0.shape[0]
-    near_side, far_side = (
-        [head[first : first + part, :] for first in range(side * part, 2 * QUAD * part, 2 * part)]
-        for side in range(2)
-    )
-    near_0[...] = near_side[0]
-    near_2[...] = near_side[2]
-    near_sent[:part, :] = near_side[1]
-    near_sent[part:, :] = near_side[3]
-    far_0[...] = far_side[0]
-    far_1[...] = far_side[1]
-    far_sent[:part, :] = far_side[2]
-    far_sent[part:, :] = far_side[3]
+    split_head(dot_nn(pick_i[...], dp_a[...]), parts)
 
 
 def text_pull_kernel(place, *refs):
@@ -341,14 +328,14 @@
     far_text = both(t2, gy_a, 4)
     part_b, parts_b = ((part, width), BF16), ((2 * part, width), BF16)
     square_b, square = ((near, near), BF16), ((near, near), F32)
-    q_b, y_b, w_ab, dp_a, near_0, near_2, near_sent, far_0, far_1, far_sent = call(
+    q_b, y_b, w_ab, dp_a, *image_parts = call(
         image_kernel,
-        [wide, wide_b, square_b, wide_b] + [part_b, part_b, parts_b] * 2,
+        [wide, wide_b, square_b, wide_b] + [parts_b] * QUAD,
         [square, wide],
         (*far_text, text_head, p_a, x_a, gx, pick_i),
         8,
     )
-    near_came, far_came = cuts(near_sent, mask=1), cuts(far_sent, mask=2)
+    image_others = [cuts(image_parts[k], mask=k) for k in range(1, QUAD)]
     gy_b, pick_b = call(
         text_pull_kernel,
         [wide, pick_one],
@@ -373,10 +360,7 @@
         (*x_2, w_2a, w_2b, gy_a, gy_b),
         8,
     )
-    near_came, far_came = after(near_came, gy_a), after(far_came, gy_a)
-    near_sent, far_sent = add(near_2, [near_came[part:]]), add(far_1, [far_came[part:]])
-    near_last, far_last = cuts(near_sent, mask=2), cuts(far_sent, mask=1)
-    x_3 = [after(rows, (gy_a, near_sent, far_sent)) for rows in x_3]
+    x_3 = [after(rows, gy_a) for rows in x_3]
     *text_parts, dq_a = call(
         last_kernel,
         [part_b] * QUAD + [wide_b],
@@ -385,20 +369,21 @@
         16,
     )
     text_others = [cuts(text_parts[k], mask=k) for k in range(1, QUAD)]
-    far_sum = add(far_0, [far_came[:part], after(far_last, dq_a)])
-    near_sum = add(near_0, [near_came[:part], after(near_last, dq_a)])
-    image_sum = add(near_sum, [loop(far_sum, mask=2)])
+    both_sides = add(image_parts[0], [after(other, dq_a) for other in image_others])
+    came = loop(both_sides[part:], mask=2)
+    text_sum = add(text_parts[0], [after(other, both_sides) for other in text_others])
+    text_other = cuts(text_sum, mask=QUAD)
+    image_sum = add(both_sides[:part], [after(came, text_sum)])
+    image_other = cuts(image_sum, mask=QUAD)
     grads = [
         call(grad_kernel, [tall], [], (after(back, image_sum), head), 4, macs=2 * macs, keep=False)[0]
         for back, head in ((dp_a, image_head), (dq_a, text_head))
     ]
-    text_sum = add(text_parts[0], [after(other, (image_sum, grads)) for other in text_others])
-    image_sum = add(image_sum, [cuts(image_sum, mask=QUAD)])
-    image_pieces = spread(image_sum)
-    text_sum = add(text_sum, [after(cuts(text_sum, mask=QUAD), image_pieces[1])])
-    image_out, text_out = (
+    text_pieces = spread(add(text_sum, [after(text_other, grads)]))
+    image_pieces = spread(add(image_sum, [after(image_other, text_pieces[1])]))
+    text_out, image_out = (
         call(place_kernel, [((rows_out, width), F32)], [], pieces, 4, place, keep=False)[0]
-        for pieces in (image_pieces, spread(text_sum))
+        for pieces in (text_pieces, image_pieces)
     )
     return (*grads, image_out, text_out)
 

time: 79.3 us -> 86 us (1.084)
  waiting for transfers between devices: 18.1 us -> 28.6 us
  starting transfers between devices: 29 us -> 25.1 us
    ppermute x26 -> x25, waiting for transfers between devices: 18.1 us -> 28.6 us  [swap(): return lax.ppermute(array, axis, [(i, i ^ mask) for i in range(size)])]
    ppermute x26 -> x25, starting transfers between devices: 29 us -> 25.1 us  [swap(): return lax.ppermute(array, axis, [(i, i ^ mask) for i in range(size)])]
  transfers between devices with their start and end apart: 26 -> 25, of which waited for: 13 -> 16; matrix products, arithmetic and copies ran while one was open for 1% -> 1% of each run, Pallas kernels for 37% -> 34%
where the time goes in v19:
time: 86 us; the launch traced here: 85.9 us
  Pallas kernels  30.9 us (36%)
  waiting for transfers between devices  28.6 us (33%)
  starting transfers between devices  25.1 us (29%)
    pallas_call x11, Pallas kernels, call(): pl.pallas_call(kernel, out_shape=[shape(s, t) for s, t in outs], in_specs...  30.9 us
    ppermute x25, waiting for transfers between devices, swap(): return lax.ppermute(array, axis, [(i, i ^ mask) for i in range(size)])  28.6 us
    ppermute x25, starting transfers between devices, swap(): return lax.ppermute(array, axis, [(i, i ^ mask) for i in range(size)])  25.1 us
  transfers between devices with their start and end apart: 25, of which 16 were waited for; matrix products, arithmetic and copies ran while one was open for 1% of the time, Pallas kernels for 34%

profile of v19, /device:TPU:0, one launch (start us, length us, event | category | flops | bytes accessed | tf_op | source)
XLA Modules:
  0.0 85.9 jit_solution(585041498106514378)
XLA Ops:
  1.3 2.9 %collective-permute-start = (bf16[256,1152]{1,0:T(8,128)(2,1)}, bf16[256,1152]{1,0:T(8,128)(2,1)S(1)}, u32[]{:S(2)}, u32[]{:S(2)}) collective-permute-start(bf16[256,1152]{1,0:T(8,128)(2,1)} %t0_far), channel_id=1, source_target_pairs={{0,2},{1,3},{2,0},{3,1},{4,6},{5,7},{6,4},{7,5},{8,10},{9,11},{10,... | collective-permute-start | bytes 1769480 | tf_op jit(solution)/shard_map/ppermute | solution.py:274
  4.2 7.4 %shard_map.75 = (f32[512,1152]{1,0:T(8,128)S(1)}, bf16[512,1152]{1,0:T(8,128)(2,1)S(1)}, f32[512,1152]{1,0:T(8,128)S(1)}, bf16[512,1152]{1,0:T(8,128)(2,1)S(1)},...) custom-call(bf16[256,1152]{1,0:T(8,128)(2,1)S(1)} %collective-permut, ...), custom_call_target="tpu_custom_call" | custom-call | tf_op jit(solution)/shard_map/pallas_call | solution.py:261
  11.6 2.6 %shard_map.76 = (f32[512,1152]{1,0:T(8,128)S(1)}, bf16[576,512]{1,0:T(8,128)(2,1)S(1)}, bf16[288,512]{1,0:T(8,128)(2,1)S(1)}) custom-call(s32[2]{0:T(128)S(1)} %pad_add_fusion.place, bf16[256,1152]{1,0:T(8,128)(2,1)S(1)} %get-tuple-element.60.t0, bf16[256,1152]{1,0:T(8,128)(2,1)S(1)} %collective-permute-done.1.t1, ...), custom_call_target="tpu_custom_call" | custom-call | tf_op jit(solution)/shard_map/pallas_call | solution.py:261
  14.2 4.3 %collective-permute-done.refs_0_ = bf16[256,1152]{1,0:T(8,128)(2,1)S(1)} collective-permute-done((bf16[256,1152]{1,0:T(8,128)(2,1)}, bf16[256,1152]{1,0:T(8,128)(2,1)S(1)}, u32[]{:S(2)}, u32[]{:S(2)}) %collective-permute-start) | collective-permute-done | bytes 589856 | tf_op jit(solution)/shard_map/ppermute | solution.py:274
  20.7 5.2 %shard_map.77 = (f32[512,1152]{1,0:T(8,128)S(1)}, bf16[512,1152]{1,0:T(8,128)(2,1)S(1)}, bf16[512,512]{1,0:T(8,128)(2,1)S(1)}, bf16[512,1152]{1,0:T(8,128)(2,1)S...) custom-call(bf16[256,1152]{1,0:T(8,128)(2,1)S(1)} %collective-permut, ...), custom_call_target="tpu_custom_call" | custom-call | tf_op jit(solution)/shard_map/pallas_call | solution.py:261
  25.9 2.2 %collective-permute-start.7 = (bf16[144,1152]{1,0:T(8,128)(2,1)S(1)}, bf16[144,1152]{1,0:T(8,128)(2,1)S(1)}, u32[]{:S(2)}, u32[]{:S(2)}) collective-permute-start(bf16[144,1152]{1,0:T(8,128)(2,1)S(1)} %get-tuple-element.72), channel_id=1, source_target_pairs={{0,4},{4,0},{8,12},{12,8},{16,20},{20,16},{24,28},{28,24},{1,5},{5... | collective-permute-start | bytes 995336 | tf_op jit(solution)/shard_map/ppermute | solution.py:274
  28.1 1.6 %collective-permute-start.11 = (bf16[144,1152]{1,0:T(8,128)(2,1)S(1)}, bf16[144,1152]{1,0:T(8,128)(2,1)S(1)}, u32[]{:S(2)}, u32[]{:S(2)}) collective-permute-start(bf16[144,1152]{1,0:T(8,128)(2,1)S(1)} %get-tuple-element.94), channel_id=1, source_target_pairs={{0,8},{4,12},{8,0},{12,4},{16,24},{20,28},{24,16},{28,20},{1,9},{5... | collective-permute-start | bytes 995336 | tf_op jit(solution)/shard_map/ppermute | solution.py:274
  29.6 2.0 %shard_map.78 = (f32[512,1152]{1,0:T(8,128)S(1)}, bf16[288,512]{1,0:T(8,128)(2,1)S(1)}) custom-call(s32[2]{0:T(128)S(1)} %pad_add_fusion.place, bf16[256,1152]{1,0:T(8,128)(2,1)S(1)} %collective-permute-done.refs_0_, bf16[64,1152]{1,0:T(8,128)(2,1)S(1)} %collective-permute-done.3.refs_1_, bf16[64,1152]{1,0:T(8,128)(2,1)S(1)} %collective-permute-done.4.refs_2_, ...), custom_call_target="tpu_custom_call" | custom-call | tf_op jit(solution)/shard_map/pallas_call | solution.py:261
  31.7 1.9 %shard_map.79 = (bf16[128,1152]{1,0:T(8,128)(2,1)S(1)}, bf16[128,1152]{1,0:T(8,128)(2,1)S(1)}, bf16[256,512]{1,0:T(8,128)(2,1)S(1)}, bf16[256,512]{1,0:T(8,128)(2,1)S(1)}) custom-call(bf16[256,1152]{1,0:T(8,128)(2,1)S(1)} %collective-permute-done.8.i2, bf16[1152,1152]{1,0:T(8,128)(2,1)S(1)} %get-tuple-element.77.image_head.head, ...), custom_call_target="tpu_custom_call" | custom-call | tf_op jit(solution)/shard_map/pallas_call | solution.py:261
  34.2 0.9 %shard_map.80 = (f32[512,1152]{1,0:T(8,128)S(1)}, f32[512,1152]{1,0:T(8,128)S(1)}) custom-call(bf16[128,1152]{1,0:T(8,128)(2,1)S(1)} %get-tuple-element.80.x_first, bf16[128,1152]{1,0:T(8,128)(2,1)S(1)} %get-tuple-element.81.x_second, bf16[256,512]{1,0:T(8,128)(2,1)S(1)} %get-tuple-element.82.w_a, bf16[256,512]{1,0:T(8,128)(2,1)S(1)} %get-tuple-element.83.w_b, ...), custom_call_target="tpu_custom_call" | custom-call | tf_op jit(solution)/shard_map/pallas_call | solution.py:261
  35.7 3.4 %shard_map.81 = (bf16[72,1152]{1,0:T(8,128)(2,1)S(1)}, bf16[72,1152]{1,0:T(8,128)(2,1)S(1)}, bf16[72,1152]{1,0:T(8,128)(2,1)S(1)}, bf16[72,1152]{1,0:T(8,128)(2,1)S(1)}, bf16[512,1152]{1,0:T(8,128)(2,1)S(1)}) custom-call(bf16[128,1152]{1,0:T(8,128)(2,1)S(1)} %collective-permute-done.9.x_first, bf16[128,1152]{1,0:T(8,128)(2,1)S(1)} %collective-permute-done.10.x_second, ...), custom_call_target="tpu_custom_call" | custom-call | tf_op jit(solution)/shard_map/pallas_call | solution.py:261
  39.1 2.0 %collective-permute-start.14 = (bf16[72,1152]{1,0:T(8,128)(2,1)S(1)}, bf16[72,1152]{1,0:T(8,128)(2,1)S(1)}, u32[]{:S(2)}, u32[]{:S(2)}) collective-permute-start(bf16[72,1152]{1,0:T(8,128)(2,1)S(1)} %get-tuple-element.99), channel_id=1, source_target_pairs={{0,4},{4,0},{8,12},{12,8},{16,20},{20,16},{24,28},{28,24},{1,5},{5... | collective-permute-start | bytes 497672 | tf_op jit(solution)/shard_map/ppermute | solution.py:274
  41.1 1.6 %collective-permute-start.15 = (bf16[72,1152]{1,0:T(8,128)(2,1)S(1)}, bf16[72,1152]{1,0:T(8,128)(2,1)S(1)}, u32[]{:S(2)}, u32[]{:S(2)}) collective-permute-start(bf16[72,1152]{1,0:T(8,128)(2,1)S(1)} %get-tuple-element.101), channel_id=1, source_target_pairs={{0,8},{4,12},{8,0},{12,4},{16,24},{20,28},{24,16},{28,20},{1,9},{5... | collective-permute-start | bytes 497672 | tf_op jit(solution)/shard_map/ppermute | solution.py:274
  42.7 2.7 %collective-permute-done.12 = bf16[144,1152]{1,0:T(8,128)(2,1)S(1)} collective-permute-done((bf16[144,1152]{1,0:T(8,128)(2,1)S(1)}, bf16[144,1152]{1,0:T(8,128)(2,1)S(1)}, u32[]{:S(2)}, u32[]{:S(2)}) %collective-permute-start.12) | collective-permute-done | bytes 331808 | tf_op jit(solution)/shard_map/ppermute | solution.py:274
  45.5 2.0 %collective-permute-start.13 = (bf16[72,1152]{1,0:T(8,128)(2,1)S(1)}, bf16[72,1152]{1,0:T(8,128)(2,1)S(1)}, u32[]{:S(2)}, u32[]{:S(2)}) collective-permute-start(bf16[72,1152]{1,0:T(8,128)(2,1)S(1)} %slice.9), channel_id=1, source_target_pairs={{0,2},{1,3},{2,0},{3,1},{4,6},{5,7},{6,4},{7,5},{8,10},{9,11},{10,... | collective-permute-start | bytes 497672 | tf_op jit(solution)/shard_map/ppermute | solution.py:274
  47.5 1.3 %collective-permute-done.14 = bf16[72,1152]{1,0:T(8,128)(2,1)S(1)} collective-permute-done((bf16[72,1152]{1,0:T(8,128)(2,1)S(1)}, bf16[72,1152]{1,0:T(8,128)(2,1)S(1)}, u32[]{:S(2)}, u32[]{:S(2)}) %collective-permute-start.14) | collective-permute-done | bytes 165920 | tf_op jit(solution)/shard_map/ppermute | solution.py:274
  48.8 0.6 collective-permute-done.15
  49.4 2.4 %collective-permute-done.16 = bf16[72,1152]{1,0:T(8,128)(2,1)S(1)} collective-permute-done((bf16[72,1152]{1,0:T(8,128)(2,1)S(1)}, bf16[72,1152]{1,0:T(8,128)(2,1)S(1)}, u32[]{:S(2)}, u32[]{:S(2)}) %collective-permute-start.16) | collective-permute-done | bytes 165920 | tf_op jit(solution)/shard_map/ppermute | solution.py:274
  51.9 2.8 %collective-permute-start.18 = (bf16[72,1152]{1,0:T(8,128)(2,1)S(1)}, bf16[72,1152]{1,0:T(8,128)(2,1)S(1)}, u32[]{:S(2)}, u32[]{:S(2)}) collective-permute-start(bf16[72,1152]{1,0:T(8,128)(2,1)S(1)} %add_convert_fusion.4), channel_id=1, source_target_pairs={{0,16},{4,20},{8,24},{12,28},{16,0},{20,4},{24,8},{28,12},{1,17},{... | collective-permute-start | bytes 497672 | tf_op jit(solution)/shard_map/ppermute | solution.py:274
  55.0 2.0 %shard_map.83 = f32[256,1152]{1,0:T(8,128)} custom-call(bf16[512,1152]{1,0:T(8,128)(2,1)S(1)} %get-tuple-element.107.back, bf16[1152,1152]{1,0:T(8,128)(2,1)S(1)} %get-tuple-element.66.refs_5_.head), custom_call_target="tpu_custom_call" | custom-call | flops 1358954496 | tf_op jit(solution)/shard_map/pallas_call | solution.py:261
  57.1 2.1 %shard_map.82 = f32[256,1152]{1,0:T(8,128)} custom-call(bf16[512,1152]{1,0:T(8,128)(2,1)S(1)} %get-tuple-element.106.back, bf16[1152,1152]{1,0:T(8,128)(2,1)S(1)} %get-tuple-element.77.image_head.head), custom_call_target="tpu_custom_call" | custom-call | flops 1358954496 | tf_op jit(solution)/shard_map/pallas_call | solution.py:261
  59.1 7.5 %collective-permute-done.18 = bf16[72,1152]{1,0:T(8,128)(2,1)S(1)} collective-permute-done((bf16[72,1152]{1,0:T(8,128)(2,1)S(1)}, bf16[72,1152]{1,0:T(8,128)(2,1)S(1)}, u32[]{:S(2)}, u32[]{:S(2)}) %collective-permute-start.18) | collective-permute-done | bytes 165920 | tf_op jit(solution)/shard_map/ppermute | solution.py:274
  66.7 1.6 %collective-permute-start.19 = (bf16[72,1152]{1,0:T(8,128)(2,1)S(1)}, bf16[72,1152]{1,0:T(8,128)(2,1)S(1)}, u32[]{:S(2)}, u32[]{:S(2)}) collective-permute-start(bf16[72,1152]{1,0:T(8,128)(2,1)S(1)} %add_convert_fusion.2.refs_0_), channel_id=1, source_target_pairs={{0,4},{4,0},{8,12},{12,8},{16,20},{20,16},{24,28},{28,24},{1,5},{5... | collective-permute-start | bytes 497672 | tf_op jit(solution)/shard_map/ppermute | solution.py:274
  68.2 2.0 %collective-permute-start.24 = (bf16[72,1152]{1,0:T(8,128)(2,1)S(1)}, bf16[72,1152]{1,0:T(8,128)(2,1)S(1)}, u32[]{:S(2)}, u32[]{:S(2)}) collective-permute-start(bf16[72,1152]{1,0:T(8,128)(2,1)S(1)} %add_convert_fusion.2.refs_0_), channel_id=1, source_target_pairs={{0,12},{4,8},{8,4},{12,0},{16,28},{20,24},{24,20},{28,16},{1,13},{... | collective-permute-start | bytes 497672 | tf_op jit(solution)/shard_map/ppermute | solution.py:274
  70.2 3.7 %collective-permute-done.19.refs_1_ = bf16[72,1152]{1,0:T(8,128)(2,1)S(1)} collective-permute-done((bf16[72,1152]{1,0:T(8,128)(2,1)S(1)}, bf16[72,1152]{1,0:T(8,128)(2,1)S(1)}, u32[]{:S(2)}, u32[]{:S(2)}) %collective-permute-start.19) | collective-permute-done | bytes 165920 | tf_op jit(solution)/shard_map/ppermute | solution.py:274
  73.9 2.5 %collective-permute-start.20 = (bf16[72,1152]{1,0:T(8,128)(2,1)S(1)}, bf16[72,1152]{1,0:T(8,128)(2,1)S(1)}, u32[]{:S(2)}, u32[]{:S(2)}) collective-permute-start(bf16[72,1152]{1,0:T(8,128)(2,1)S(1)} %add_convert_fusion.1.refs_0_), channel_id=1, source_target_pairs={{0,4},{4,0},{8,12},{12,8},{16,20},{20,16},{24,28},{28,24},{1,5},{5... | collective-permute-start | bytes 497672 | tf_op jit(solution)/shard_map/ppermute | solution.py:274
  76.5 1.5 %collective-permute-start.22 = (bf16[72,1152]{1,0:T(8,128)(2,1)S(1)}, bf16[72,1152]{1,0:T(8,128)(2,1)S(1)}, u32[]{:S(2)}, u32[]{:S(2)}) collective-permute-start(bf16[72,1152]{1,0:T(8,128)(2,1)S(1)} %add_convert_fusion.1.refs_0_), channel_id=1, source_target_pairs={{0,12},{4,8},{8,4},{12,0},{16,28},{20,24},{24,20},{28,16},{1,13},{... | collective-permute-start | bytes 497672 | tf_op jit(solution)/shard_map/ppermute | solution.py:274
  78.0 0.9 %collective-permute-done.24.refs_3_ = bf16[72,1152]{1,0:T(8,128)(2,1)S(1)} collective-permute-done((bf16[72,1152]{1,0:T(8,128)(2,1)S(1)}, bf16[72,1152]{1,0:T(8,128)(2,1)S(1)}, u32[]{:S(2)}, u32[]{:S(2)}) %collective-permute-start.24) | collective-permute-done | bytes 165920 | tf_op jit(solution)/shard_map/ppermute | solution.py:274
  78.9 1.7 %shard_map.85 = f32[288,1152]{1,0:T(8,128)} custom-call(s32[2]{0:T(128)S(1)} %pad_add_fusion.place, bf16[72,1152]{1,0:T(8,128)(2,1)S(1)} %add_convert_fusion.2.refs_0_, bf16[72,1152]{1,0:T(8,128)(2,1)S(1)} %collective-permute-done.19.refs_1_, bf16[72,1152]{1,0:T(8,128)(2,1)S(1)} %collective-permute-done.23.refs_2_, ...), custom_call_target="tpu_custom_call" | custom-call | tf_op jit(solution)/shard_map/pallas_call | solution.py:261
  80.6 1.4 %collective-permute-done.20.refs_1_ = bf16[72,1152]{1,0:T(8,128)(2,1)S(1)} collective-permute-done((bf16[72,1152]{1,0:T(8,128)(2,1)S(1)}, bf16[72,1152]{1,0:T(8,128)(2,1)S(1)}, u32[]{:S(2)}, u32[]{:S(2)}) %collective-permute-start.20) | collective-permute-done | bytes 165920 | tf_op jit(solution)/shard_map/ppermute | solution.py:274
  82.0 2.1 %collective-permute-done.22.refs_3_ = bf16[72,1152]{1,0:T(8,128)(2,1)S(1)} collective-permute-done((bf16[72,1152]{1,0:T(8,128)(2,1)S(1)}, bf16[72,1152]{1,0:T(8,128)(2,1)S(1)}, u32[]{:S(2)}, u32[]{:S(2)}) %collective-permute-start.22) | collective-permute-done | bytes 165920 | tf_op jit(solution)/shard_map/ppermute | solution.py:274
  84.2 1.7 %shard_map.84 = f32[288,1152]{1,0:T(8,128)} custom-call(s32[2]{0:T(128)S(1)} %pad_add_fusion.place, bf16[72,1152]{1,0:T(8,128)(2,1)S(1)} %add_convert_fusion.1.refs_0_, bf16[72,1152]{1,0:T(8,128)(2,1)S(1)} %collective-permute-done.20.refs_1_, bf16[72,1152]{1,0:T(8,128)(2,1)S(1)} %collective-permute-done.21.refs_2_, ...), custom_call_target="tpu_custom_call" | custom-call | tf_op jit(solution)/shard_map/pallas_call | solution.py:261
  (37 shorter events, 4.8 us)
Async XLA Ops:
  0.7 3.5 %collective-permute-start.1 = (bf16[256,1152]{1,0:T(8,128)(2,1)}, bf16[256,1152]{1,0:T(8,128)(2,1)S(1)}, u32[]{:S(2)}, u32[]{:S(2)}) collective-permute-start(bf16[256,1152]{1,0:T(8,128)(2,1)} %t0_far), channel_id=1, source_target_pairs={{0,1},{1,0},{2,3},{3,2},{4,5},{5,4},{6,7},{7,6},{8,9},{9,8},{10,11... | collective-permute-start | bytes 1769480 | tf_op jit(solution)/shard_map/ppermute | solution.py:274
  1.2 3.0 %collective-permute-start.2 = (bf16[256,1152]{1,0:T(8,128)(2,1)}, bf16[256,1152]{1,0:T(8,128)(2,1)S(1)}, u32[]{:S(2)}, u32[]{:S(2)}) collective-permute-start(bf16[256,1152]{1,0:T(8,128)(2,1)} %i0_far), channel_id=1, source_target_pairs={{0,1},{1,0},{2,3},{3,2},{4,5},{5,4},{6,7},{7,6},{8,9},{9,8},{10,11... | collective-permute-start | bytes 1769480 | tf_op jit(solution)/shard_map/ppermute | solution.py:274
  1.3 17.2 %collective-permute-start = (bf16[256,1152]{1,0:T(8,128)(2,1)}, bf16[256,1152]{1,0:T(8,128)(2,1)S(1)}, u32[]{:S(2)}, u32[]{:S(2)}) collective-permute-start(bf16[256,1152]{1,0:T(8,128)(2,1)} %t0_far), channel_id=1, source_target_pairs={{0,2},{1,3},{2,0},{3,1},{4,6},{5,7},{6,4},{7,5},{8,10},{9,11},{10,... | collective-permute-start | bytes 1769480 | tf_op jit(solution)/shard_map/ppermute | solution.py:274
  4.2 27.5 %collective-permute-start.8 = (bf16[256,1152]{1,0:T(8,128)(2,1)}, bf16[256,1152]{1,0:T(8,128)(2,1)S(1)}, u32[]{:S(2)}, u32[]{:S(2)}) collective-permute-start(bf16[256,1152]{1,0:T(8,128)(2,1)} %i0_far), channel_id=1, source_target_pairs={{0,2},{1,3},{2,0},{3,1},{4,6},{5,7},{6,4},{7,5},{8,10},{9,11},{10,... | collective-permute-start | bytes 1769480 | tf_op jit(solution)/shard_map/ppermute | solution.py:274
  18.5 1.4 %collective-permute-start.3 = (bf16[64,1152]{1,0:T(8,128)(2,1)S(1)}, bf16[64,1152]{1,0:T(8,128)(2,1)S(1)}, u32[]{:S(2)}, u32[]{:S(2)}) collective-permute-start(bf16[64,1152]{1,0:T(8,128)(2,1)S(1)} %get-tuple-element.113), channel_id=1, source_target_pairs={{0,1},{1,0},{2,3},{3,2},{4,5},{5,4},{6,7},{7,6},{8,9},{9,8},{10,11... | collective-permute-start | bytes 442376 | tf_op jit(solution)/shard_map/ppermute | solution.py:274
  18.6 1.6 %collective-permute-start.4 = (bf16[64,1152]{1,0:T(8,128)(2,1)S(1)}, bf16[64,1152]{1,0:T(8,128)(2,1)S(1)}, u32[]{:S(2)}, u32[]{:S(2)}) collective-permute-start(bf16[64,1152]{1,0:T(8,128)(2,1)S(1)} %get-tuple-element.112), channel_id=1, source_target_pairs={{0,1},{1,0},{2,3},{3,2},{4,5},{5,4},{6,7},{7,6},{8,9},{9,8},{10,11... | collective-permute-start | bytes 442376 | tf_op jit(solution)/shard_map/ppermute | solution.py:274
  19.1 1.4 %collective-permute-start.5 = (bf16[64,1152]{1,0:T(8,128)(2,1)S(1)}, bf16[64,1152]{1,0:T(8,128)(2,1)S(1)}, u32[]{:S(2)}, u32[]{:S(2)}) collective-permute-start(bf16[64,1152]{1,0:T(8,128)(2,1)S(1)} %get-tuple-element.111), channel_id=1, source_target_pairs={{0,1},{1,0},{2,3},{3,2},{4,5},{5,4},{6,7},{7,6},{8,9},{9,8},{10,11... | collective-permute-start | bytes 442376 | tf_op jit(solution)/shard_map/ppermute | solution.py:274
  19.2 1.5 %collective-permute-start.6 = (bf16[64,1152]{1,0:T(8,128)(2,1)S(1)}, bf16[64,1152]{1,0:T(8,128)(2,1)S(1)}, u32[]{:S(2)}, u32[]{:S(2)}) collective-permute-start(bf16[64,1152]{1,0:T(8,128)(2,1)S(1)} %get-tuple-element.110), channel_id=1, source_target_pairs={{0,1},{1,0},{2,3},{3,2},{4,5},{5,4},{6,7},{7,6},{8,9},{9,8},{10,11... | collective-permute-start | bytes 442376 | tf_op jit(solution)/shard_map/ppermute | solution.py:274
  25.9 16.8 %collective-permute-start.7 = (bf16[144,1152]{1,0:T(8,128)(2,1)S(1)}, bf16[144,1152]{1,0:T(8,128)(2,1)S(1)}, u32[]{:S(2)}, u32[]{:S(2)}) collective-permute-start(bf16[144,1152]{1,0:T(8,128)(2,1)S(1)} %get-tuple-element.72), channel_id=1, source_target_pairs={{0,4},{4,0},{8,12},{12,8},{16,20},{20,16},{24,28},{28,24},{1,5},{5... | collective-permute-start | bytes 995336 | tf_op jit(solution)/shard_map/ppermute | solution.py:274
  28.1 14.6 %collective-permute-start.11 = (bf16[144,1152]{1,0:T(8,128)(2,1)S(1)}, bf16[144,1152]{1,0:T(8,128)(2,1)S(1)}, u32[]{:S(2)}, u32[]{:S(2)}) collective-permute-start(bf16[144,1152]{1,0:T(8,128)(2,1)S(1)} %get-tuple-element.94), channel_id=1, source_target_pairs={{0,8},{4,12},{8,0},{12,4},{16,24},{20,28},{24,16},{28,20},{1,9},{5... | collective-permute-start | bytes 995336 | tf_op jit(solution)/shard_map/ppermute | solution.py:274
  29.6 15.7 %collective-permute-start.12 = (bf16[144,1152]{1,0:T(8,128)(2,1)S(1)}, bf16[144,1152]{1,0:T(8,128)(2,1)S(1)}, u32[]{:S(2)}, u32[]{:S(2)}) collective-permute-start(bf16[144,1152]{1,0:T(8,128)(2,1)S(1)} %get-tuple-element.96), channel_id=1, source_target_pairs={{0,12},{4,8},{8,4},{12,0},{16,28},{20,24},{24,20},{28,16},{1,13},{... | collective-permute-start | bytes 995336 | tf_op jit(solution)/shard_map/ppermute | solution.py:274
  33.6 1.6 %collective-permute-start.10 = (bf16[128,1152]{1,0:T(8,128)(2,1)S(1)}, bf16[128,1152]{1,0:T(8,128)(2,1)S(1)}, u32[]{:S(2)}, u32[]{:S(2)}) collective-permute-start(bf16[128,1152]{1,0:T(8,128)(2,1)S(1)} %get-tuple-element.81.x_second), channel_id=1, source_target_pairs={{0,1},{1,0},{2,3},{3,2},{4,5},{5,4},{6,7},{7,6},{8,9},{9,8},{10,11... | collective-permute-start | bytes 884744 | tf_op jit(solution)/shard_map/ppermute | solution.py:274
  33.7 2.0 %collective-permute-start.9 = (bf16[128,1152]{1,0:T(8,128)(2,1)S(1)}, bf16[128,1152]{1,0:T(8,128)(2,1)S(1)}, u32[]{:S(2)}, u32[]{:S(2)}) collective-permute-start(bf16[128,1152]{1,0:T(8,128)(2,1)S(1)} %get-tuple-element.80.x_first), channel_id=1, source_target_pairs={{0,1},{1,0},{2,3},{3,2},{4,5},{5,4},{6,7},{7,6},{8,9},{9,8},{10,11... | collective-permute-start | bytes 884744 | tf_op jit(solution)/shard_map/ppermute | solution.py:274
  39.1 9.7 %collective-permute-start.14 = (bf16[72,1152]{1,0:T(8,128)(2,1)S(1)}, bf16[72,1152]{1,0:T(8,128)(2,1)S(1)}, u32[]{:S(2)}, u32[]{:S(2)}) collective-permute-start(bf16[72,1152]{1,0:T(8,128)(2,1)S(1)} %get-tuple-element.99), channel_id=1, source_target_pairs={{0,4},{4,0},{8,12},{12,8},{16,20},{20,16},{24,28},{28,24},{1,5},{5... | collective-permute-start | bytes 497672 | tf_op jit(solution)/shard_map/ppermute | solution.py:274
  41.1 8.3 %collective-permute-start.15 = (bf16[72,1152]{1,0:T(8,128)(2,1)S(1)}, bf16[72,1152]{1,0:T(8,128)(2,1)S(1)}, u32[]{:S(2)}, u32[]{:S(2)}) collective-permute-start(bf16[72,1152]{1,0:T(8,128)(2,1)S(1)} %get-tuple-element.101), channel_id=1, source_target_pairs={{0,8},{4,12},{8,0},{12,4},{16,24},{20,28},{24,16},{28,20},{1,9},{5... | collective-permute-start | bytes 497672 | tf_op jit(solution)/shard_map/ppermute | solution.py:274
  42.7 9.2 %collective-permute-start.16 = (bf16[72,1152]{1,0:T(8,128)(2,1)S(1)}, bf16[72,1152]{1,0:T(8,128)(2,1)S(1)}, u32[]{:S(2)}, u32[]{:S(2)}) collective-permute-start(bf16[72,1152]{1,0:T(8,128)(2,1)S(1)} %get-tuple-element.103), channel_id=1, source_target_pairs={{0,12},{4,8},{8,4},{12,0},{16,28},{20,24},{24,20},{28,16},{1,13},{... | collective-permute-start | bytes 497672 | tf_op jit(solution)/shard_map/ppermute | solution.py:274
  45.5 9.2 %collective-permute-start.13 = (bf16[72,1152]{1,0:T(8,128)(2,1)S(1)}, bf16[72,1152]{1,0:T(8,128)(2,1)S(1)}, u32[]{:S(2)}, u32[]{:S(2)}) collective-permute-start(bf16[72,1152]{1,0:T(8,128)(2,1)S(1)} %slice.9), channel_id=1, source_target_pairs={{0,2},{1,3},{2,0},{3,1},{4,6},{5,7},{6,4},{7,5},{8,10},{9,11},{10,... | collective-permute-start | bytes 497672 | tf_op jit(solution)/shard_map/ppermute | solution.py:274
  51.9 14.7 %collective-permute-start.18 = (bf16[72,1152]{1,0:T(8,128)(2,1)S(1)}, bf16[72,1152]{1,0:T(8,128)(2,1)S(1)}, u32[]{:S(2)}, u32[]{:S(2)}) collective-permute-start(bf16[72,1152]{1,0:T(8,128)(2,1)S(1)} %add_convert_fusion.4), channel_id=1, source_target_pairs={{0,16},{4,20},{8,24},{12,28},{16,0},{20,4},{24,8},{28,12},{1,17},{... | collective-permute-start | bytes 497672 | tf_op jit(solution)/shard_map/ppermute | solution.py:274
  54.7 15.5 %collective-permute-start.17 = (bf16[72,1152]{1,0:T(8,128)(2,1)S(1)}, bf16[72,1152]{1,0:T(8,128)(2,1)S(1)}, u32[]{:S(2)}, u32[]{:S(2)}) collective-permute-start(bf16[72,1152]{1,0:T(8,128)(2,1)S(1)} %add_convert_fusion.3), channel_id=1, source_target_pairs={{0,16},{4,20},{8,24},{12,28},{16,0},{20,4},{24,8},{28,12},{1,17},{... | collective-permute-start | bytes 497672 | tf_op jit(solution)/shard_map/ppermute | solution.py:274
  66.7 7.2 %collective-permute-start.19 = (bf16[72,1152]{1,0:T(8,128)(2,1)S(1)}, bf16[72,1152]{1,0:T(8,128)(2,1)S(1)}, u32[]{:S(2)}, u32[]{:S(2)}) collective-permute-start(bf16[72,1152]{1,0:T(8,128)(2,1)S(1)} %add_convert_fusion.2.refs_0_), channel_id=1, source_target_pairs={{0,4},{4,0},{8,12},{12,8},{16,20},{20,16},{24,28},{28,24},{1,5},{5... | collective-permute-start | bytes 497672 | tf_op jit(solution)/shard_map/ppermute | solution.py:274
  68.2 9.8 %collective-permute-start.23 = (bf16[72,1152]{1,0:T(8,128)(2,1)S(1)}, bf16[72,1152]{1,0:T(8,128)(2,1)S(1)}, u32[]{:S(2)}, u32[]{:S(2)}) collective-permute-start(bf16[72,1152]{1,0:T(8,128)(2,1)S(1)} %add_convert_fusion.2.refs_0_), channel_id=1, source_target_pairs={{0,8},{4,12},{8,0},{12,4},{16,24},{20,28},{24,16},{28,20},{1,9},{5... | collective-permute-start | bytes 497672 | tf_op jit(solution)/shard_map/ppermute | solution.py:274
  68.2 10.7 %collective-permute-start.24 = (bf16[72,1152]{1,0:T(8,128)(2,1)S(1)}, bf16[72,1152]{1,0:T(8,128)(2,1)S(1)}, u32[]{:S(2)}, u32[]{:S(2)}) collective-permute-start(bf16[72,1152]{1,0:T(8,128)(2,1)S(1)} %add_convert_fusion.2.refs_0_), channel_id=1, source_target_pairs={{0,12},{4,8},{8,4},{12,0},{16,28},{20,24},{24,20},{28,16},{1,13},{... | collective-permute-start | bytes 497672 | tf_op jit(solution)/shard_map/ppermute | solution.py:274
  73.9 8.1 %collective-permute-start.20 = (bf16[72,1152]{1,0:T(8,128)(2,1)S(1)}, bf16[72,1152]{1,0:T(8,128)(2,1)S(1)}, u32[]{:S(2)}, u32[]{:S(2)}) collective-permute-start(bf16[72,1152]{1,0:T(8,128)(2,1)S(1)} %add_convert_fusion.1.refs_0_), channel_id=1, source_target_pairs={{0,4},{4,0},{8,12},{12,8},{16,20},{20,16},{24,28},{28,24},{1,5},{5... | collective-permute-start | bytes 497672 | tf_op jit(solution)/shard_map/ppermute | solution.py:274
  76.5 5.6 %collective-permute-start.21 = (bf16[72,1152]{1,0:T(8,128)(2,1)S(1)}, bf16[72,1152]{1,0:T(8,128)(2,1)S(1)}, u32[]{:S(2)}, u32[]{:S(2)}) collective-permute-start(bf16[72,1152]{1,0:T(8,128)(2,1)S(1)} %add_convert_fusion.1.refs_0_), channel_id=1, source_target_pairs={{0,8},{4,12},{8,0},{12,4},{16,24},{20,28},{24,16},{28,20},{1,9},{5... | collective-permute-start | bytes 497672 | tf_op jit(solution)/shard_map/ppermute | solution.py:274
  76.5 7.7 %collective-permute-start.22 = (bf16[72,1152]{1,0:T(8,128)(2,1)S(1)}, bf16[72,1152]{1,0:T(8,128)(2,1)S(1)}, u32[]{:S(2)}, u32[]{:S(2)}) collective-permute-start(bf16[72,1152]{1,0:T(8,128)(2,1)S(1)} %add_convert_fusion.1.refs_0_), channel_id=1, source_target_pairs={{0,12},{4,8},{8,4},{12,0},{16,28},{20,24},{24,20},{28,16},{1,13},{... | collective-permute-start | bytes 497672 | tf_op jit(solution)/shard_map/ppermute | solution.py:274

commit v20 on v13

--- a/solution.py
+++ b/solution.py
@@ -410,15 +410,16 @@
     far_sum = add(far_0, [far_came[:part], after(far_last, dq_a)])
     near_sum = add(near_0, [near_came[:part], after(near_last, dq_a)])
     image_sum = add(near_sum, [loop(far_sum, mask=2)])
+    text_came = after(text_came, image_sum)
+    text_middle = add(text_2, [text_came[part:]])
+    text_last = cuts(text_middle, mask=2)
     grads = [
-        call(grad_kernel, [tall], [], (after(back, image_sum), head), 4, macs=2 * macs, keep=False)[0]
+        call(grad_kernel, [tall], [], (after(back, text_middle), head), 4, keep=False)[0]
         for back, head in ((dp_a, image_head), (dq_a, text_head))
     ]
-    text_came = after(text_came, (image_sum, grads))
-    text_last = cuts(add(text_2, [text_came[part:]]), mask=2)
     text_sum = add(text_0, [text_came[:part], text_last])
     image_sum = call(
-        add_kernel, [part_b], [], (image_sum, cuts(image_sum, mask=QUAD)), 4, macs=4 * macs
+        add_kernel, [part_b], [], (image_sum, after(cuts(image_sum, mask=QUAD), grads)), 4, macs=4 * macs
     )[0]
     image_pieces = spread(image_sum)
     text_sum = add(text_sum, [after(cuts(text_sum, mask=QUAD), image_pieces[1])])

time: 81.1 us -> 81.5 us (level)
  transfers between devices with their start and end apart: 26 -> 26, of which waited for: 12 -> 11; matrix products, arithmetic and copies ran while one was open for 2% -> 2% of each run, Pallas kernels for 38% -> 38%
where the time goes in v20:
time: 81.5 us; the launch traced here: 81.3 us
  Pallas kernels  32.5 us (40%)
  starting transfers between devices  29.5 us (36%)
  waiting for transfers between devices  16.9 us (21%)
  local copies, waits for them, and re-layouts  1.15 us (1%)
    pallas_call x12, Pallas kernels, call(): pl.pallas_call(kernel, out_shape=[shape(s, t) for s, t in outs], in_specs...  32.5 us
    ppermute x26, starting transfers between devices, swap(): return lax.ppermute(array, axis, [(i, i ^ mask) for i in range(size)])  29.5 us
    ppermute x26, waiting for transfers between devices, swap(): return lax.ppermute(array, axis, [(i, i ^ mask) for i in range(size)])  16.9 us
  transfers between devices with their start and end apart: 26, of which 11 were waited for; matrix products, arithmetic and copies ran while one was open for 2% of the time, Pallas kernels for 38%

profile of v20, /device:TPU:0, one launch (start us, length us, event | category | flops | bytes accessed | tf_op | source)
XLA Modules:
  0.0 81.3 jit_solution(1638035331589733997)
XLA Ops:
  1.2 1.1 %fusion = (bf16[128,1152]{1,0:T(8,128)(2,1)S(1)}, bf16[128,1152]{1,0:T(8,128)(2,1)S(1)}) fusion(bf16[256,1152]{1,0:T(8,128)(2,1)} %t0_far), kind=kLoop, calls=%fused_computation.9 | loop fusion | bytes 1179648 | tf_op jit(solution)/shard_map/split | solution.py:333
  2.3 3.0 %collective-permute-start.1 = (bf16[128,1152]{1,0:T(8,128)(2,1)S(1)}, bf16[128,1152]{1,0:T(8,128)(2,1)S(1)}, u32[]{:S(2)}, u32[]{:S(2)}) collective-permute-start(bf16[128,1152]{1,0:T(8,128)(2,1)S(1)} %get-tuple-element.124), channel_id=1, source_target_pairs={{0,2},{1,3},{2,0},{3,1},{4,6},{5,7},{6,4},{7,5},{8,10},{9,11},{10,... | collective-permute-start | bytes 884744 | tf_op jit(solution)/shard_map/ppermute | solution.py:307
  5.4 7.7 %shard_map.75 = (f32[512,1152]{1,0:T(8,128)S(1)}, bf16[512,1152]{1,0:T(8,128)(2,1)S(1)}, f32[512,1152]{1,0:T(8,128)S(1)}, bf16[512,1152]{1,0:T(8,128)(2,1)S(1)},...) custom-call(bf16[256,1152]{1,0:T(8,128)(2,1)S(1)} %collective-permut, ...), custom_call_target="tpu_custom_call" | custom-call | tf_op jit(solution)/shard_map/pallas_call | solution.py:294
  13.8 2.0 %collective-permute-start.8 = (bf16[256,1152]{1,0:T(8,128)(2,1)S(1)}, bf16[256,1152]{1,0:T(8,128)(2,1)S(1)}, u32[]{:S(2)}, u32[]{:S(2)}) collective-permute-start(bf16[256,1152]{1,0:T(8,128)(2,1)S(1)} %copy-done), channel_id=1, source_target_pairs={{0,2},{1,3},{2,0},{3,1},{4,6},{5,7},{6,4},{7,5},{8,10},{9,11},{10,... | collective-permute-start | bytes 1769480 | tf_op jit(solution)/shard_map/ppermute | solution.py:307
  15.8 3.3 %shard_map.76 = (f32[256,1152]{1,0:T(8,128)S(1)}, bf16[256,1152]{1,0:T(8,128)(2,1)S(1)}, bf16[512,256]{1,0:T(8,128)(2,1)S(1)}, f32[512,1152]{1,0:T(8,128)S(1)}, bf16[576,512]{1,0:T(8,128)(2,1)S(1)}) custom-call(s32[2]{0:T(128)S(1)} %pad_add_fusion.place, bf16[128,1152]{1,0:T(8,128)(2,1)S(1)} %collective-permute-done.1.refs_0_, ...), custom_call_target="tpu_custom_call" | custom-call | tf_op jit(solution)/shard_map/pallas_call | solution.py:294
  21.1 4.1 %shard_map.77 = (f32[256,1152]{1,0:T(8,128)S(1)}, bf16[256,1152]{1,0:T(8,128)(2,1)S(1)}, bf16[512,256]{1,0:T(8,128)(2,1)S(1)}, bf16[512,1152]{1,0:T(8,128)(2,1)S...) custom-call(bf16[128,1152]{1,0:T(8,128)(2,1)S(1)} %collective-permut, ...), custom_call_target="tpu_custom_call" | custom-call | tf_op jit(solution)/shard_map/pallas_call | solution.py:294
  25.2 2.2 %collective-permute-start.11 = (bf16[144,1152]{1,0:T(8,128)(2,1)S(1)}, bf16[144,1152]{1,0:T(8,128)(2,1)S(1)}, u32[]{:S(2)}, u32[]{:S(2)}) collective-permute-start(bf16[144,1152]{1,0:T(8,128)(2,1)S(1)} %get-tuple-element.100), channel_id=1, source_target_pairs={{0,8},{4,12},{8,0},{12,4},{16,24},{20,28},{24,16},{28,20},{1,9},{5... | collective-permute-start | bytes 995336 | tf_op jit(solution)/shard_map/ppermute | solution.py:307
  27.4 1.5 %collective-permute-start.10 = (bf16[144,1152]{1,0:T(8,128)(2,1)S(1)}, bf16[144,1152]{1,0:T(8,128)(2,1)S(1)}, u32[]{:S(2)}, u32[]{:S(2)}) collective-permute-start(bf16[144,1152]{1,0:T(8,128)(2,1)S(1)} %get-tuple-element.97), channel_id=1, source_target_pairs={{0,4},{4,0},{8,12},{12,8},{16,20},{20,16},{24,28},{28,24},{1,5},{5... | collective-permute-start | bytes 995336 | tf_op jit(solution)/shard_map/ppermute | solution.py:307
  28.9 3.1 %shard_map.78 = (f32[512,1152]{1,0:T(8,128)S(1)}, f32[256,1152]{1,0:T(8,128)S(1)}, f32[256,1152]{1,0:T(8,128)S(1)}, bf16[288,512]{1,0:T(8,128)(2,1)S(1)}, bf16[288,512]{1,0:T(8,128)(2,1)S(1)}) custom-call(s32[2]{0:T(128)S(1)} %pad_add_fusion.place, bf16[128,1152]{1,0:T(8,128)(2,1)S(1)} %collective-permute-done.1.refs_0_, ...), custom_call_target="tpu_custom_call" | custom-call | tf_op jit(solution)/shard_map/pallas_call | solution.py:294
  32.0 2.0 %shard_map.79 = (bf16[128,1152]{1,0:T(8,128)(2,1)S(1)}, bf16[128,1152]{1,0:T(8,128)(2,1)S(1)}, bf16[256,512]{1,0:T(8,128)(2,1)S(1)}, bf16[256,256]{1,0:T(8,128)(2,1)S(1)}, bf16[256,256]{1,0:T(8,128)(2,1)S(1)}) custom-call(bf16[256,1152]{1,0:T(8,128)(2,1)S(1)} %collective-permute-done.8.i2, bf16[1152,1152]{1,0:T(8,128)(2,1)S(1)} %get-tuple-element.84.image_head.head, ...), custom_call_target="tpu_custom_call" | custom-call | tf_op jit(solution)/shard_map/pallas_call | solution.py:294
  35.7 1.5 %collective-permute-done.10 = bf16[144,1152]{1,0:T(8,128)(2,1)S(1)} collective-permute-done((bf16[144,1152]{1,0:T(8,128)(2,1)S(1)}, bf16[144,1152]{1,0:T(8,128)(2,1)S(1)}, u32[]{:S(2)}, u32[]{:S(2)}) %collective-permute-start.10) | collective-permute-done | bytes 331808 | tf_op jit(solution)/shard_map/ppermute | solution.py:307
  37.2 1.6 %collective-permute-start.15 = (bf16[72,1152]{1,0:T(8,128)(2,1)S(1)}, bf16[72,1152]{1,0:T(8,128)(2,1)S(1)}, u32[]{:S(2)}, u32[]{:S(2)}) collective-permute-start(bf16[72,1152]{1,0:T(8,128)(2,1)S(1)} %add_convert_fusion.6), channel_id=1, source_target_pairs={{0,4},{4,0},{8,12},{12,8},{16,20},{20,16},{24,28},{28,24},{1,5},{5... | collective-permute-start | bytes 497672 | tf_op jit(solution)/shard_map/ppermute | solution.py:307
  39.4 3.9 %shard_map.81 = (bf16[72,1152]{1,0:T(8,128)(2,1)S(1)}, bf16[72,1152]{1,0:T(8,128)(2,1)S(1)}, bf16[144,1152]{1,0:T(8,128)(2,1)S(1)}, bf16[512,1152]{1,0:T(8,128)(2,1)S(1)}) custom-call(bf16[128,1152]{1,0:T(8,128)(2,1)S(1)} %collective-permute-done.9.x_first, bf16[128,1152]{1,0:T(8,128)(2,1)S(1)} %collective-permute-done.12.x_second, ...), custom_call_target="tpu_custom_call" | custom-call | tf_op jit(solution)/shard_map/pallas_call | solution.py:294
  43.4 1.6 %collective-permute-start.16 = (bf16[72,1152]{1,0:T(8,128)(2,1)S(1)}, bf16[72,1152]{1,0:T(8,128)(2,1)S(1)}, u32[]{:S(2)}, u32[]{:S(2)}) collective-permute-start(bf16[72,1152]{1,0:T(8,128)(2,1)S(1)} %add_convert_fusion.4), channel_id=1, source_target_pairs={{0,2},{1,3},{2,0},{3,1},{4,6},{5,7},{6,4},{7,5},{8,10},{9,11},{10,... | collective-permute-start | bytes 497672 | tf_op jit(solution)/shard_map/ppermute | solution.py:307
  45.8 3.0 %collective-permute-done.16 = bf16[72,1152]{1,0:T(8,128)(2,1)S(1)} collective-permute-done((bf16[72,1152]{1,0:T(8,128)(2,1)S(1)}, bf16[72,1152]{1,0:T(8,128)(2,1)S(1)}, u32[]{:S(2)}, u32[]{:S(2)}) %collective-permute-start.16) | collective-permute-done | bytes 165920 | tf_op jit(solution)/shard_map/ppermute | solution.py:307
  48.9 2.6 %collective-permute-start.17 = (bf16[72,1152]{1,0:T(8,128)(2,1)S(1)}, bf16[72,1152]{1,0:T(8,128)(2,1)S(1)}, u32[]{:S(2)}, u32[]{:S(2)}) collective-permute-start(bf16[72,1152]{1,0:T(8,128)(2,1)S(1)} %add_convert_fusion.3.left), channel_id=1, source_target_pairs={{0,16},{4,20},{8,24},{12,28},{16,0},{20,4},{24,8},{28,12},{1,17},{... | collective-permute-start | bytes 497672 | tf_op jit(solution)/shard_map/ppermute | solution.py:307
  51.5 1.6 %collective-permute-done.13 = bf16[144,1152]{1,0:T(8,128)(2,1)S(1)} collective-permute-done((bf16[144,1152]{1,0:T(8,128)(2,1)S(1)}, bf16[144,1152]{1,0:T(8,128)(2,1)S(1)}, u32[]{:S(2)}, u32[]{:S(2)}) %collective-permute-start.13) | collective-permute-done | bytes 331808 | tf_op jit(solution)/shard_map/ppermute | solution.py:307
  53.1 1.5 %collective-permute-start.21 = (bf16[72,1152]{1,0:T(8,128)(2,1)S(1)}, bf16[72,1152]{1,0:T(8,128)(2,1)S(1)}, u32[]{:S(2)}, u32[]{:S(2)}) collective-permute-start(bf16[72,1152]{1,0:T(8,128)(2,1)S(1)} %add_convert_fusion.2), channel_id=1, source_target_pairs={{0,8},{4,12},{8,0},{12,4},{16,24},{20,28},{24,16},{28,20},{1,9},{5... | collective-permute-start | bytes 497672 | tf_op jit(solution)/shard_map/ppermute | solution.py:307
  54.6 2.0 %shard_map.83 = f32[256,1152]{1,0:T(8,128)} custom-call(bf16[512,1152]{1,0:T(8,128)(2,1)S(1)} %get-tuple-element.120.back, bf16[1152,1152]{1,0:T(8,128)(2,1)S(1)} %get-tuple-element.70.refs_5_.refs_3_.head), custom_call_target="tpu_custom_call" | custom-call | tf_op jit(solution)/shard_map/pallas_call | solution.py:294
  56.7 2.0 %shard_map.82 = f32[256,1152]{1,0:T(8,128)} custom-call(bf16[512,1152]{1,0:T(8,128)(2,1)S(1)} %get-tuple-element.119.back, bf16[1152,1152]{1,0:T(8,128)(2,1)S(1)} %get-tuple-element.84.image_head.head), custom_call_target="tpu_custom_call" | custom-call | tf_op jit(solution)/shard_map/pallas_call | solution.py:294
  59.4 2.7 %collective-permute-start.22 = (bf16[72,1152]{1,0:T(8,128)(2,1)S(1)}, bf16[72,1152]{1,0:T(8,128)(2,1)S(1)}, u32[]{:S(2)}, u32[]{:S(2)}) collective-permute-start(bf16[72,1152]{1,0:T(8,128)(2,1)S(1)} %add_convert_fusion.1), channel_id=1, source_target_pairs={{0,16},{4,20},{8,24},{12,28},{16,0},{20,4},{24,8},{28,12},{1,17},{... | collective-permute-start | bytes 497672 | tf_op jit(solution)/shard_map/ppermute | solution.py:307
  62.1 1.6 %collective-permute-start.20 = (bf16[72,1152]{1,0:T(8,128)(2,1)S(1)}, bf16[72,1152]{1,0:T(8,128)(2,1)S(1)}, u32[]{:S(2)}, u32[]{:S(2)}) collective-permute-start(bf16[72,1152]{1,0:T(8,128)(2,1)S(1)} %shard_map.84.refs_0_), channel_id=1, source_target_pairs={{0,12},{4,8},{8,4},{12,0},{16,28},{20,24},{24,20},{28,16},{1,13},{... | collective-permute-start | bytes 497672 | tf_op jit(solution)/shard_map/ppermute | solution.py:307
  63.6 1.4 %collective-permute-start.19 = (bf16[72,1152]{1,0:T(8,128)(2,1)S(1)}, bf16[72,1152]{1,0:T(8,128)(2,1)S(1)}, u32[]{:S(2)}, u32[]{:S(2)}) collective-permute-start(bf16[72,1152]{1,0:T(8,128)(2,1)S(1)} %shard_map.84.refs_0_), channel_id=1, source_target_pairs={{0,8},{4,12},{8,0},{12,4},{16,24},{20,28},{24,16},{28,20},{1,9},{5... | collective-permute-start | bytes 497672 | tf_op jit(solution)/shard_map/ppermute | solution.py:307
  65.1 2.9 %collective-permute-done.22 = bf16[72,1152]{1,0:T(8,128)(2,1)S(1)} collective-permute-done((bf16[72,1152]{1,0:T(8,128)(2,1)S(1)}, bf16[72,1152]{1,0:T(8,128)(2,1)S(1)}, u32[]{:S(2)}, u32[]{:S(2)}) %collective-permute-start.22) | collective-permute-done | bytes 165920 | tf_op jit(solution)/shard_map/ppermute | solution.py:307
  68.0 1.0 %collective-permute-start.25 = (bf16[72,1152]{1,0:T(8,128)(2,1)S(1)}, bf16[72,1152]{1,0:T(8,128)(2,1)S(1)}, u32[]{:S(2)}, u32[]{:S(2)}) collective-permute-start(bf16[72,1152]{1,0:T(8,128)(2,1)S(1)} %add_convert_fusion.refs_0_), channel_id=1, source_target_pairs={{0,12},{4,8},{8,4},{12,0},{16,28},{20,24},{24,20},{28,16},{1,13},{... | collective-permute-start | bytes 497672 | tf_op jit(solution)/shard_map/ppermute | solution.py:307
  69.0 1.6 %collective-permute-start.24 = (bf16[72,1152]{1,0:T(8,128)(2,1)S(1)}, bf16[72,1152]{1,0:T(8,128)(2,1)S(1)}, u32[]{:S(2)}, u32[]{:S(2)}) collective-permute-start(bf16[72,1152]{1,0:T(8,128)(2,1)S(1)} %add_convert_fusion.refs_0_), channel_id=1, source_target_pairs={{0,8},{4,12},{8,0},{12,4},{16,24},{20,28},{24,16},{28,20},{1,9},{5... | collective-permute-start | bytes 497672 | tf_op jit(solution)/shard_map/ppermute | solution.py:307
  70.6 1.0 %collective-permute-start.23 = (bf16[72,1152]{1,0:T(8,128)(2,1)S(1)}, bf16[72,1152]{1,0:T(8,128)(2,1)S(1)}, u32[]{:S(2)}, u32[]{:S(2)}) collective-permute-start(bf16[72,1152]{1,0:T(8,128)(2,1)S(1)} %add_convert_fusion.refs_0_), channel_id=1, source_target_pairs={{0,4},{4,0},{8,12},{12,8},{16,20},{20,16},{24,28},{28,24},{1,5},{5... | collective-permute-start | bytes 497672 | tf_op jit(solution)/shard_map/ppermute | solution.py:307
  71.6 3.0 %collective-permute-done.19.refs_2_ = bf16[72,1152]{1,0:T(8,128)(2,1)S(1)} collective-permute-done((bf16[72,1152]{1,0:T(8,128)(2,1)S(1)}, bf16[72,1152]{1,0:T(8,128)(2,1)S(1)}, u32[]{:S(2)}, u32[]{:S(2)}) %collective-permute-start.19) | collective-permute-done | bytes 165920 | tf_op jit(solution)/shard_map/ppermute | solution.py:307
  74.6 1.7 %shard_map.85 = f32[288,1152]{1,0:T(8,128)} custom-call(s32[2]{0:T(128)S(1)} %pad_add_fusion.place, bf16[72,1152]{1,0:T(8,128)(2,1)S(1)} %shard_map.84.refs_0_, bf16[72,1152]{1,0:T(8,128)(2,1)S(1)} %collective-permute-done.18.refs_1_, bf16[72,1152]{1,0:T(8,128)(2,1)S(1)} %collective-permute-done.19.refs_2_, bf16[72,1152]{1,0:T(8,128)(2,1)S(1)} %collective-permute-done.20.refs_3_), custom_call_target="tpu_custom_call" | custom-call | tf_op jit(solution)/shard_map/pallas_call | solution.py:294
  76.3 1.7 %collective-permute-done.25.refs_3_ = bf16[72,1152]{1,0:T(8,128)(2,1)S(1)} collective-permute-done((bf16[72,1152]{1,0:T(8,128)(2,1)S(1)}, bf16[72,1152]{1,0:T(8,128)(2,1)S(1)}, u32[]{:S(2)}, u32[]{:S(2)}) %collective-permute-start.25) | collective-permute-done | bytes 165920 | tf_op jit(solution)/shard_map/ppermute | solution.py:307
  78.0 1.6 %collective-permute-done.24.refs_2_ = bf16[72,1152]{1,0:T(8,128)(2,1)S(1)} collective-permute-done((bf16[72,1152]{1,0:T(8,128)(2,1)S(1)}, bf16[72,1152]{1,0:T(8,128)(2,1)S(1)}, u32[]{:S(2)}, u32[]{:S(2)}) %collective-permute-start.24) | collective-permute-done | bytes 165920 | tf_op jit(solution)/shard_map/ppermute | solution.py:307
  79.6 1.7 %shard_map.86 = f32[288,1152]{1,0:T(8,128)} custom-call(s32[2]{0:T(128)S(1)} %pad_add_fusion.place, bf16[72,1152]{1,0:T(8,128)(2,1)S(1)} %add_convert_fusion.refs_0_, bf16[72,1152]{1,0:T(8,128)(2,1)S(1)} %collective-permute-done.23.refs_1_, bf16[72,1152]{1,0:T(8,128)(2,1)S(1)} %collective-permute-done.24.refs_2_, ...), custom_call_target="tpu_custom_call" | custom-call | tf_op jit(solution)/shard_map/pallas_call | solution.py:294
  (45 shorter events, 7.3 us)
Async XLA Ops:
  0.7 4.7 %collective-permute-start.2 = (bf16[256,1152]{1,0:T(8,128)(2,1)}, bf16[256,1152]{1,0:T(8,128)(2,1)S(1)}, u32[]{:S(2)}, u32[]{:S(2)}) collective-permute-start(bf16[256,1152]{1,0:T(8,128)(2,1)} %t0_far), channel_id=1, source_target_pairs={{0,1},{1,0},{2,3},{3,2},{4,5},{5,4},{6,7},{7,6},{8,9},{9,8},{10,11... | collective-permute-start | bytes 1769480 | tf_op jit(solution)/shard_map/ppermute | solution.py:307
  1.2 4.3 %collective-permute-start.3 = (bf16[256,1152]{1,0:T(8,128)(2,1)}, bf16[256,1152]{1,0:T(8,128)(2,1)S(1)}, u32[]{:S(2)}, u32[]{:S(2)}) collective-permute-start(bf16[256,1152]{1,0:T(8,128)(2,1)} %i0_far), channel_id=1, source_target_pairs={{0,1},{1,0},{2,3},{3,2},{4,5},{5,4},{6,7},{7,6},{8,9},{9,8},{10,11... | collective-permute-start | bytes 1769480 | tf_op jit(solution)/shard_map/ppermute | solution.py:307
  2.3 10.8 %collective-permute-start.1 = (bf16[128,1152]{1,0:T(8,128)(2,1)S(1)}, bf16[128,1152]{1,0:T(8,128)(2,1)S(1)}, u32[]{:S(2)}, u32[]{:S(2)}) collective-permute-start(bf16[128,1152]{1,0:T(8,128)(2,1)S(1)} %get-tuple-element.124), channel_id=1, source_target_pairs={{0,2},{1,3},{2,0},{3,1},{4,6},{5,7},{6,4},{7,5},{8,10},{9,11},{10,... | collective-permute-start | bytes 884744 | tf_op jit(solution)/shard_map/ppermute | solution.py:307
  5.3 8.4 %copy-start = (bf16[256,1152]{1,0:T(8,128)(2,1)S(1)}, bf16[256,1152]{1,0:T(8,128)(2,1)}, u32[]{:S(2)}) copy-start(bf16[256,1152]{1,0:T(8,128)(2,1)} %i0_far) | copy-start | bytes 1769476
  5.3 14.1 %collective-permute-start = (bf16[128,1152]{1,0:T(8,128)(2,1)S(1)}, bf16[128,1152]{1,0:T(8,128)(2,1)S(1)}, u32[]{:S(2)}, u32[]{:S(2)}) collective-permute-start(bf16[128,1152]{1,0:T(8,128)(2,1)S(1)} %get-tuple-element.125), channel_id=1, source_target_pairs={{0,2},{1,3},{2,0},{3,1},{4,6},{5,7},{6,4},{7,5},{8,10},{9,11},{10,... | collective-permute-start | bytes 884744 | tf_op jit(solution)/shard_map/ppermute | solution.py:307
  13.2 2.6 %collective-permute-start.5 = (bf16[64,1152]{1,0:T(8,128)(2,1)S(1)}, bf16[64,1152]{1,0:T(8,128)(2,1)S(1)}, u32[]{:S(2)}, u32[]{:S(2)}) collective-permute-start(bf16[64,1152]{1,0:T(8,128)(2,1)S(1)} %get-tuple-element.128), channel_id=1, source_target_pairs={{0,1},{1,0},{2,3},{3,2},{4,5},{5,4},{6,7},{7,6},{8,9},{9,8},{10,11... | collective-permute-start | bytes 442376 | tf_op jit(solution)/shard_map/ppermute | solution.py:307
  13.3 2.5 %collective-permute-start.4 = (bf16[64,1152]{1,0:T(8,128)(2,1)S(1)}, bf16[64,1152]{1,0:T(8,128)(2,1)S(1)}, u32[]{:S(2)}, u32[]{:S(2)}) collective-permute-start(bf16[64,1152]{1,0:T(8,128)(2,1)S(1)} %get-tuple-element.129), channel_id=1, source_target_pairs={{0,1},{1,0},{2,3},{3,2},{4,5},{5,4},{6,7},{7,6},{8,9},{9,8},{10,11... | collective-permute-start | bytes 442376 | tf_op jit(solution)/shard_map/ppermute | solution.py:307
  13.8 18.3 %collective-permute-start.8 = (bf16[256,1152]{1,0:T(8,128)(2,1)S(1)}, bf16[256,1152]{1,0:T(8,128)(2,1)S(1)}, u32[]{:S(2)}, u32[]{:S(2)}) collective-permute-start(bf16[256,1152]{1,0:T(8,128)(2,1)S(1)} %copy-done), channel_id=1, source_target_pairs={{0,2},{1,3},{2,0},{3,1},{4,6},{5,7},{6,4},{7,5},{8,10},{9,11},{10,... | collective-permute-start | bytes 1769480 | tf_op jit(solution)/shard_map/ppermute | solution.py:307
  19.5 1.4 %collective-permute-start.7 = (bf16[64,1152]{1,0:T(8,128)(2,1)S(1)}, bf16[64,1152]{1,0:T(8,128)(2,1)S(1)}, u32[]{:S(2)}, u32[]{:S(2)}) collective-permute-start(bf16[64,1152]{1,0:T(8,128)(2,1)S(1)} %get-tuple-element.126), channel_id=1, source_target_pairs={{0,1},{1,0},{2,3},{3,2},{4,5},{5,4},{6,7},{7,6},{8,9},{9,8},{10,11... | collective-permute-start | bytes 442376 | tf_op jit(solution)/shard_map/ppermute | solution.py:307
  19.6 1.6 %collective-permute-start.6 = (bf16[64,1152]{1,0:T(8,128)(2,1)S(1)}, bf16[64,1152]{1,0:T(8,128)(2,1)S(1)}, u32[]{:S(2)}, u32[]{:S(2)}) collective-permute-start(bf16[64,1152]{1,0:T(8,128)(2,1)S(1)} %get-tuple-element.127), channel_id=1, source_target_pairs={{0,1},{1,0},{2,3},{3,2},{4,5},{5,4},{6,7},{7,6},{8,9},{9,8},{10,11... | collective-permute-start | bytes 442376 | tf_op jit(solution)/shard_map/ppermute | solution.py:307
  25.2 10.5 %collective-permute-start.11 = (bf16[144,1152]{1,0:T(8,128)(2,1)S(1)}, bf16[144,1152]{1,0:T(8,128)(2,1)S(1)}, u32[]{:S(2)}, u32[]{:S(2)}) collective-permute-start(bf16[144,1152]{1,0:T(8,128)(2,1)S(1)} %get-tuple-element.100), channel_id=1, source_target_pairs={{0,8},{4,12},{8,0},{12,4},{16,24},{20,28},{24,16},{28,20},{1,9},{5... | collective-permute-start | bytes 995336 | tf_op jit(solution)/shard_map/ppermute | solution.py:307
  27.4 9.7 %collective-permute-start.10 = (bf16[144,1152]{1,0:T(8,128)(2,1)S(1)}, bf16[144,1152]{1,0:T(8,128)(2,1)S(1)}, u32[]{:S(2)}, u32[]{:S(2)}) collective-permute-start(bf16[144,1152]{1,0:T(8,128)(2,1)S(1)} %get-tuple-element.97), channel_id=1, source_target_pairs={{0,4},{4,0},{8,12},{12,8},{16,20},{20,16},{24,28},{28,24},{1,5},{5... | collective-permute-start | bytes 995336 | tf_op jit(solution)/shard_map/ppermute | solution.py:307
  34.0 5.3 %collective-permute-start.9 = (bf16[128,1152]{1,0:T(8,128)(2,1)S(1)}, bf16[128,1152]{1,0:T(8,128)(2,1)S(1)}, u32[]{:S(2)}, u32[]{:S(2)}) collective-permute-start(bf16[128,1152]{1,0:T(8,128)(2,1)S(1)} %get-tuple-element.88.x_first), channel_id=1, source_target_pairs={{0,1},{1,0},{2,3},{3,2},{4,5},{5,4},{6,7},{7,6},{8,9},{9,8},{10,11... | collective-permute-start | bytes 884744 | tf_op jit(solution)/shard_map/ppermute | solution.py:307
  34.1 5.3 %collective-permute-start.12 = (bf16[128,1152]{1,0:T(8,128)(2,1)S(1)}, bf16[128,1152]{1,0:T(8,128)(2,1)S(1)}, u32[]{:S(2)}, u32[]{:S(2)}) collective-permute-start(bf16[128,1152]{1,0:T(8,128)(2,1)S(1)} %get-tuple-element.89.x_second), channel_id=1, source_target_pairs={{0,1},{1,0},{2,3},{3,2},{4,5},{5,4},{6,7},{7,6},{8,9},{9,8},{10,11... | collective-permute-start | bytes 884744 | tf_op jit(solution)/shard_map/ppermute | solution.py:307
  37.2 6.1 %collective-permute-start.15 = (bf16[72,1152]{1,0:T(8,128)(2,1)S(1)}, bf16[72,1152]{1,0:T(8,128)(2,1)S(1)}, u32[]{:S(2)}, u32[]{:S(2)}) collective-permute-start(bf16[72,1152]{1,0:T(8,128)(2,1)S(1)} %add_convert_fusion.6), channel_id=1, source_target_pairs={{0,4},{4,0},{8,12},{12,8},{16,20},{20,16},{24,28},{28,24},{1,5},{5... | collective-permute-start | bytes 497672 | tf_op jit(solution)/shard_map/ppermute | solution.py:307
  38.8 6.9 %collective-permute-start.14 = (bf16[72,1152]{1,0:T(8,128)(2,1)S(1)}, bf16[72,1152]{1,0:T(8,128)(2,1)S(1)}, u32[]{:S(2)}, u32[]{:S(2)}) collective-permute-start(bf16[72,1152]{1,0:T(8,128)(2,1)S(1)} %add_convert_fusion.7), channel_id=1, source_target_pairs={{0,8},{4,12},{8,0},{12,4},{16,24},{20,28},{24,16},{28,20},{1,9},{5... | collective-permute-start | bytes 497672 | tf_op jit(solution)/shard_map/ppermute | solution.py:307
  43.4 5.4 %collective-permute-start.16 = (bf16[72,1152]{1,0:T(8,128)(2,1)S(1)}, bf16[72,1152]{1,0:T(8,128)(2,1)S(1)}, u32[]{:S(2)}, u32[]{:S(2)}) collective-permute-start(bf16[72,1152]{1,0:T(8,128)(2,1)S(1)} %add_convert_fusion.4), channel_id=1, source_target_pairs={{0,2},{1,3},{2,0},{3,1},{4,6},{5,7},{6,4},{7,5},{8,10},{9,11},{10,... | collective-permute-start | bytes 497672 | tf_op jit(solution)/shard_map/ppermute | solution.py:307
  44.9 8.2 %collective-permute-start.13 = (bf16[144,1152]{1,0:T(8,128)(2,1)S(1)}, bf16[144,1152]{1,0:T(8,128)(2,1)S(1)}, u32[]{:S(2)}, u32[]{:S(2)}) collective-permute-start(bf16[144,1152]{1,0:T(8,128)(2,1)S(1)} %get-tuple-element.112), channel_id=1, source_target_pairs={{0,4},{4,0},{8,12},{12,8},{16,20},{20,16},{24,28},{28,24},{1,5},{5... | collective-permute-start | bytes 995336 | tf_op jit(solution)/shard_map/ppermute | solution.py:307
  48.9 9.9 %collective-permute-start.17 = (bf16[72,1152]{1,0:T(8,128)(2,1)S(1)}, bf16[72,1152]{1,0:T(8,128)(2,1)S(1)}, u32[]{:S(2)}, u32[]{:S(2)}) collective-permute-start(bf16[72,1152]{1,0:T(8,128)(2,1)S(1)} %add_convert_fusion.3.left), channel_id=1, source_target_pairs={{0,16},{4,20},{8,24},{12,28},{16,0},{20,4},{24,8},{28,12},{1,17},{... | collective-permute-start | bytes 497672 | tf_op jit(solution)/shard_map/ppermute | solution.py:307
  53.1 6.2 %collective-permute-start.21 = (bf16[72,1152]{1,0:T(8,128)(2,1)S(1)}, bf16[72,1152]{1,0:T(8,128)(2,1)S(1)}, u32[]{:S(2)}, u32[]{:S(2)}) collective-permute-start(bf16[72,1152]{1,0:T(8,128)(2,1)S(1)} %add_convert_fusion.2), channel_id=1, source_target_pairs={{0,8},{4,12},{8,0},{12,4},{16,24},{20,28},{24,16},{28,20},{1,9},{5... | collective-permute-start | bytes 497672 | tf_op jit(solution)/shard_map/ppermute | solution.py:307
  58.8 6.3 %collective-permute-start.18 = (bf16[72,1152]{1,0:T(8,128)(2,1)S(1)}, bf16[72,1152]{1,0:T(8,128)(2,1)S(1)}, u32[]{:S(2)}, u32[]{:S(2)}) collective-permute-start(bf16[72,1152]{1,0:T(8,128)(2,1)S(1)} %shard_map.84.refs_0_), channel_id=1, source_target_pairs={{0,4},{4,0},{8,12},{12,8},{16,20},{20,16},{24,28},{28,24},{1,5},{5... | collective-permute-start | bytes 497672 | tf_op jit(solution)/shard_map/ppermute | solution.py:307
  59.4 8.6 %collective-permute-start.22 = (bf16[72,1152]{1,0:T(8,128)(2,1)S(1)}, bf16[72,1152]{1,0:T(8,128)(2,1)S(1)}, u32[]{:S(2)}, u32[]{:S(2)}) collective-permute-start(bf16[72,1152]{1,0:T(8,128)(2,1)S(1)} %add_convert_fusion.1), channel_id=1, source_target_pairs={{0,16},{4,20},{8,24},{12,28},{16,0},{20,4},{24,8},{28,12},{1,17},{... | collective-permute-start | bytes 497672 | tf_op jit(solution)/shard_map/ppermute | solution.py:307
  62.1 9.5 %collective-permute-start.20 = (bf16[72,1152]{1,0:T(8,128)(2,1)S(1)}, bf16[72,1152]{1,0:T(8,128)(2,1)S(1)}, u32[]{:S(2)}, u32[]{:S(2)}) collective-permute-start(bf16[72,1152]{1,0:T(8,128)(2,1)S(1)} %shard_map.84.refs_0_), channel_id=1, source_target_pairs={{0,12},{4,8},{8,4},{12,0},{16,28},{20,24},{24,20},{28,16},{1,13},{... | collective-permute-start | bytes 497672 | tf_op jit(solution)/shard_map/ppermute | solution.py:307
  63.6 11.0 %collective-permute-start.19 = (bf16[72,1152]{1,0:T(8,128)(2,1)S(1)}, bf16[72,1152]{1,0:T(8,128)(2,1)S(1)}, u32[]{:S(2)}, u32[]{:S(2)}) collective-permute-start(bf16[72,1152]{1,0:T(8,128)(2,1)S(1)} %shard_map.84.refs_0_), channel_id=1, source_target_pairs={{0,8},{4,12},{8,0},{12,4},{16,24},{20,28},{24,16},{28,20},{1,9},{5... | collective-permute-start | bytes 497672 | tf_op jit(solution)/shard_map/ppermute | solution.py:307
  68.0 10.0 %collective-permute-start.25 = (bf16[72,1152]{1,0:T(8,128)(2,1)S(1)}, bf16[72,1152]{1,0:T(8,128)(2,1)S(1)}, u32[]{:S(2)}, u32[]{:S(2)}) collective-permute-start(bf16[72,1152]{1,0:T(8,128)(2,1)S(1)} %add_convert_fusion.refs_0_), channel_id=1, source_target_pairs={{0,12},{4,8},{8,4},{12,0},{16,28},{20,24},{24,20},{28,16},{1,13},{... | collective-permute-start | bytes 497672 | tf_op jit(solution)/shard_map/ppermute | solution.py:307
  69.0 10.6 %collective-permute-start.24 = (bf16[72,1152]{1,0:T(8,128)(2,1)S(1)}, bf16[72,1152]{1,0:T(8,128)(2,1)S(1)}, u32[]{:S(2)}, u32[]{:S(2)}) collective-permute-start(bf16[72,1152]{1,0:T(8,128)(2,1)S(1)} %add_convert_fusion.refs_0_), channel_id=1, source_target_pairs={{0,8},{4,12},{8,0},{12,4},{16,24},{20,28},{24,16},{28,20},{1,9},{5... | collective-permute-start | bytes 497672 | tf_op jit(solution)/shard_map/ppermute | solution.py:307
  70.6 9.0 %collective-permute-start.23 = (bf16[72,1152]{1,0:T(8,128)(2,1)S(1)}, bf16[72,1152]{1,0:T(8,128)(2,1)S(1)}, u32[]{:S(2)}, u32[]{:S(2)}) collective-permute-start(bf16[72,1152]{1,0:T(8,128)(2,1)S(1)} %add_convert_fusion.refs_0_), channel_id=1, source_target_pairs={{0,4},{4,0},{8,12},{12,8},{16,20},{20,16},{24,28},{28,24},{1,5},{5... | collective-permute-start | bytes 497672 | tf_op jit(solution)/shard_map/ppermute | solution.py:307

commit v21 on v12

--- a/solution.py
+++ b/solution.py
@@ -143,6 +143,7 @@
     t1, i1, t0_far, i0_far, text_head_far, image_head_far,
     q_a, y_a, p_a, x_a, w_aa, gx, t0, i0, text_head, image_head, dots, sems,
 ):
+    half = t0.shape[0]
     copies = [
         pltpu.make_async_copy(source, target, sems.at[n])
         for n, (source, target) in enumerate(
@@ -153,11 +154,13 @@
         copy.start()
     copies[0].wait()
     copies[1].wait()
-    q_a[...] = dot_nn(rows_of((t0, t1)), text_head[...])
+    q_a[:half, :] = dot_nn(t0[...], text_head[...])
+    q_a[half:, :] = dot_nn(t1[...], text_head[...])
     copies[2].wait()
     copies[3].wait()
-    p_a[...] = dot_nn(rows_of((i0, i1)), image_head[...])
+    p_a[:half, :] = dot_nn(i0[...], image_head[...])
     unit_rows(q_a, y_a)
+    p_a[half:, :] = dot_nn(i1[...], image_head[...])
     unit_rows(p_a, x_a)
     dots[...] = dot_nt(x_a[...], y_a[...])
     weight_rows(dots, w_aa, 0)
@@ -324,12 +327,11 @@
     def spread(total):
         return [total] + [cuts(total, mask=k) for k in range(1, QUAD)]
 
-    t2 = loop(text_features[: half // 2], mask=2)
+    t2 = [loop(rows, mask=2) for rows in jnp.split(text_features, 2)]
     i2 = loop(image_features, mask=2)
     place = jnp.stack([lax.axis_index("loop"), lax.axis_index("cuts") & (QUAD - 1)])
     place = place.astype(jnp.int32)
     t0, i0, place = lax.optimization_barrier((text_features, image_features, place))
-    t2 = [t2, loop(t0[half // 2 :], mask=2)]
     t1 = loop(t0, mask=1)
     i1 = loop(i0, mask=1)
     wide, wide_b = ((near, width), F32), ((near, width), BF16)

time: 79.1 us -> 78.6 us (level)
  local copies, waits for them, and re-layouts: 2.02 us -> 1.15 us
    slice x2 -> x0, local copies, waits for them, and re-layouts: 1.97 us -> none  [the longest x1 0.98 us: per_device(): t2 = loop(text_features[:half // 2], mask=2)]
    split x0 -> x1, local copies, waits for them, and re-layouts: none -> 1.1 us  [per_device(): t2 = [loop(rows, mask=2) for rows in jnp.split(text_features, 2)]]
  transfers between devices with their start and end apart: 27 -> 27, of which waited for: 9 -> 12; matrix products, arithmetic and copies ran while one was open for 3% -> 2% of each run, Pallas kernels for 38% -> 38%
where the time goes in v21:
time: 78.6 us; the launch traced here: 78.5 us
  Pallas kernels  31.7 us (40%)
  starting transfers between devices  30.7 us (39%)
  waiting for transfers between devices  13.6 us (17%)
  local copies, waits for them, and re-layouts  1.15 us (1%)
  between operations  0.79 us (1%)
    pallas_call x11, Pallas kernels, call(): pl.pallas_call(kernel, out_shape=[shape(s, t) for s, t in outs], in_specs...  31.7 us
    ppermute x27, starting transfers between devices, swap(): return lax.ppermute(array, axis, [(i, i ^ mask) for i in range(size)])  30.7 us
    ppermute x27, waiting for transfers between devices, swap(): return lax.ppermute(array, axis, [(i, i ^ mask) for i in range(size)])  13.6 us
  transfers between devices with their start and end apart: 27, of which 12 were waited for; matrix products, arithmetic and copies ran while one was open for 2% of the time, Pallas kernels for 38%

profile of v21, /device:TPU:0, one launch (start us, length us, event | category | flops | bytes accessed | tf_op | source)
XLA Modules:
  0.0 78.5 jit_solution(15344904868524791730)
XLA Ops:
  1.2 1.1 %fusion = (bf16[128,1152]{1,0:T(8,128)(2,1)S(1)}, bf16[128,1152]{1,0:T(8,128)(2,1)S(1)}) fusion(bf16[256,1152]{1,0:T(8,128)(2,1)} %t0_far), kind=kLoop, calls=%fused_computation.9 | loop fusion | bytes 1179648 | tf_op jit(solution)/shard_map/split | solution.py:330
  2.3 3.0 %collective-permute-start.1 = (bf16[128,1152]{1,0:T(8,128)(2,1)S(1)}, bf16[128,1152]{1,0:T(8,128)(2,1)S(1)}, u32[]{:S(2)}, u32[]{:S(2)}) collective-permute-start(bf16[128,1152]{1,0:T(8,128)(2,1)S(1)} %get-tuple-element.128), channel_id=1, source_target_pairs={{0,2},{1,3},{2,0},{3,1},{4,6},{5,7},{6,4},{7,5},{8,10},{9,11},{10,... | collective-permute-start | bytes 884744 | tf_op jit(solution)/shard_map/ppermute | solution.py:304
  5.4 7.5 %shard_map.75 = (f32[512,1152]{1,0:T(8,128)S(1)}, bf16[512,1152]{1,0:T(8,128)(2,1)S(1)}, f32[512,1152]{1,0:T(8,128)S(1)}, bf16[512,1152]{1,0:T(8,128)(2,1)S(1)},...) custom-call(bf16[256,1152]{1,0:T(8,128)(2,1)S(1)} %collective-permut, ...), custom_call_target="tpu_custom_call" | custom-call | tf_op jit(solution)/shard_map/pallas_call | solution.py:291
  13.7 2.1 %collective-permute-start.9 = (bf16[256,1152]{1,0:T(8,128)(2,1)S(1)}, bf16[256,1152]{1,0:T(8,128)(2,1)S(1)}, u32[]{:S(2)}, u32[]{:S(2)}) collective-permute-start(bf16[256,1152]{1,0:T(8,128)(2,1)S(1)} %copy-done), channel_id=1, source_target_pairs={{0,2},{1,3},{2,0},{3,1},{4,6},{5,7},{6,4},{7,5},{8,10},{9,11},{10,... | collective-permute-start | bytes 1769480 | tf_op jit(solution)/shard_map/ppermute | solution.py:304
  15.8 4.1 %shard_map.76 = (f32[256,1152]{1,0:T(8,128)S(1)}, bf16[256,1152]{1,0:T(8,128)(2,1)S(1)}, bf16[512,256]{1,0:T(8,128)(2,1)S(1)}, f32[512,1152]{1,0:T(8,128)S(1)}, ...) custom-call(s32[2]{0:T(128)S(1)} %pad_add_fusion.place, bf16[128,1152]{1,0:T(8,128)(2,1)S(1)} %collective-permute-done.1.refs_0_, ...), custom_call_target="tpu_custom_call" | custom-call | tf_op jit(solution)/shard_map/pallas_call | solution.py:291
  21.6 3.9 %shard_map.77 = (f32[256,1152]{1,0:T(8,128)S(1)}, bf16[256,1152]{1,0:T(8,128)(2,1)S(1)}, bf16[512,256]{1,0:T(8,128)(2,1)S(1)}, bf16[512,1152]{1,0:T(8,128)(2,1)S...) custom-call(bf16[128,1152]{1,0:T(8,128)(2,1)S(1)} %collective-permut, ...), custom_call_target="tpu_custom_call" | custom-call | tf_op jit(solution)/shard_map/pallas_call | solution.py:291
  25.5 1.7 %collective-permute-start.8 = (bf16[144,1152]{1,0:T(8,128)(2,1)S(1)}, bf16[144,1152]{1,0:T(8,128)(2,1)S(1)}, u32[]{:S(2)}, u32[]{:S(2)}) collective-permute-start(bf16[144,1152]{1,0:T(8,128)(2,1)S(1)} %get-tuple-element.82), channel_id=1, source_target_pairs={{0,4},{4,0},{8,12},{12,8},{16,20},{20,16},{24,28},{28,24},{1,5},{5... | collective-permute-start | bytes 995336 | tf_op jit(solution)/shard_map/ppermute | solution.py:304
  27.2 1.6 %collective-permute-start.12 = (bf16[144,1152]{1,0:T(8,128)(2,1)S(1)}, bf16[144,1152]{1,0:T(8,128)(2,1)S(1)}, u32[]{:S(2)}, u32[]{:S(2)}) collective-permute-start(bf16[144,1152]{1,0:T(8,128)(2,1)S(1)} %get-tuple-element.103), channel_id=1, source_target_pairs={{0,8},{4,12},{8,0},{12,4},{16,24},{20,28},{24,16},{28,20},{1,9},{5... | collective-permute-start | bytes 995336 | tf_op jit(solution)/shard_map/ppermute | solution.py:304
  28.8 2.4 %shard_map.78 = (f32[256,1152]{1,0:T(8,128)S(1)}, f32[256,1152]{1,0:T(8,128)S(1)}, bf16[288,512]{1,0:T(8,128)(2,1)S(1)}, bf16[288,512]{1,0:T(8,128)(2,1)S(1)}) custom-call(s32[2]{0:T(128)S(1)} %pad_add_fusion.place, bf16[128,1152]{1,0:T(8,128)(2,1)S(1)} %collective-permute-done.1.refs_0_, bf16[64,1152]{1,0:T(8,128)(2,1)S(1)} %collective-permute-done.4.refs_1_, ...), custom_call_target="tpu_custom_call" | custom-call | tf_op jit(solution)/shard_map/pallas_call | solution.py:291
  31.5 1.9 %shard_map.79 = (bf16[128,1152]{1,0:T(8,128)(2,1)S(1)}, bf16[128,1152]{1,0:T(8,128)(2,1)S(1)}, bf16[256,512]{1,0:T(8,128)(2,1)S(1)}, bf16[256,256]{1,0:T(8,128)(2,1)S(1)}, bf16[256,256]{1,0:T(8,128)(2,1)S(1)}) custom-call(bf16[256,1152]{1,0:T(8,128)(2,1)S(1)} %collective-permute-done.9.i2, bf16[1152,1152]{1,0:T(8,128)(2,1)S(1)} %get-tuple-element.89.image_head.head, ...), custom_call_target="tpu_custom_call" | custom-call | tf_op jit(solution)/shard_map/pallas_call | solution.py:291
  34.1 0.9 %shard_map.80 = (f32[512,1152]{1,0:T(8,128)S(1)}, f32[256,1152]{1,0:T(8,128)S(1)}, f32[256,1152]{1,0:T(8,128)S(1)}) custom-call(bf16[128,1152]{1,0:T(8,128)(2,1)S(1)} %get-tuple-element.93.x_first, bf16[128,1152]{1,0:T(8,128)(2,1)S(1)} %get-tuple-element.94.x_second, bf16[256,512]{1,0:T(8,128)(2,1)S(1)} %get-tuple-element.95.w_a, ...), custom_call_target="tpu_custom_call" | custom-call | tf_op jit(solution)/shard_map/pallas_call | solution.py:291
  35.6 1.3 %collective-permute-done.12 = bf16[144,1152]{1,0:T(8,128)(2,1)S(1)} collective-permute-done((bf16[144,1152]{1,0:T(8,128)(2,1)S(1)}, bf16[144,1152]{1,0:T(8,128)(2,1)S(1)}, u32[]{:S(2)}, u32[]{:S(2)}) %collective-permute-start.12) | collective-permute-done | bytes 331808 | tf_op jit(solution)/shard_map/ppermute | solution.py:304
  37.5 1.7 %collective-permute-start.10 = (bf16[72,1152]{1,0:T(8,128)(2,1)S(1)}, bf16[72,1152]{1,0:T(8,128)(2,1)S(1)}, u32[]{:S(2)}, u32[]{:S(2)}) collective-permute-start(bf16[72,1152]{1,0:T(8,128)(2,1)S(1)} %add_convert_fusion.7), channel_id=1, source_target_pairs={{0,8},{4,12},{8,0},{12,4},{16,24},{20,28},{24,16},{28,20},{1,9},{5... | collective-permute-start | bytes 497672 | tf_op jit(solution)/shard_map/ppermute | solution.py:304
  39.2 3.5 %shard_map.81 = (bf16[72,1152]{1,0:T(8,128)(2,1)S(1)}, bf16[72,1152]{1,0:T(8,128)(2,1)S(1)}, bf16[72,1152]{1,0:T(8,128)(2,1)S(1)}, bf16[72,1152]{1,0:T(8,128)(2,1)S(1)}, bf16[512,1152]{1,0:T(8,128)(2,1)S(1)}) custom-call(bf16[128,1152]{1,0:T(8,128)(2,1)S(1)} %collective-permute-done.11.x_first, bf16[128,1152]{1,0:T(8,128)(2,1)S(1)} %collective-permute-done.13.x_second, ...), custom_call_target="tpu_custom_call" | custom-call | tf_op jit(solution)/shard_map/pallas_call | solution.py:291
  42.8 1.6 %collective-permute-start.15 = (bf16[72,1152]{1,0:T(8,128)(2,1)S(1)}, bf16[72,1152]{1,0:T(8,128)(2,1)S(1)}, u32[]{:S(2)}, u32[]{:S(2)}) collective-permute-start(bf16[72,1152]{1,0:T(8,128)(2,1)S(1)} %add_convert_fusion.4), channel_id=1, source_target_pairs={{0,2},{1,3},{2,0},{3,1},{4,6},{5,7},{6,4},{7,5},{8,10},{9,11},{10,... | collective-permute-start | bytes 497672 | tf_op jit(solution)/shard_map/ppermute | solution.py:304
  44.4 1.5 %collective-permute-start.20 = (bf16[72,1152]{1,0:T(8,128)(2,1)S(1)}, bf16[72,1152]{1,0:T(8,128)(2,1)S(1)}, u32[]{:S(2)}, u32[]{:S(2)}) collective-permute-start(bf16[72,1152]{1,0:T(8,128)(2,1)S(1)} %get-tuple-element.121), channel_id=1, source_target_pairs={{0,4},{4,0},{8,12},{12,8},{16,20},{20,16},{24,28},{28,24},{1,5},{5... | collective-permute-start | bytes 497672 | tf_op jit(solution)/shard_map/ppermute | solution.py:304
  46.4 1.5 %collective-permute-start.22 = (bf16[72,1152]{1,0:T(8,128)(2,1)S(1)}, bf16[72,1152]{1,0:T(8,128)(2,1)S(1)}, u32[]{:S(2)}, u32[]{:S(2)}) collective-permute-start(bf16[72,1152]{1,0:T(8,128)(2,1)S(1)} %get-tuple-element.125), channel_id=1, source_target_pairs={{0,12},{4,8},{8,4},{12,0},{16,28},{20,24},{24,20},{28,16},{1,13},{... | collective-permute-start | bytes 497672 | tf_op jit(solution)/shard_map/ppermute | solution.py:304
  48.3 2.7 %collective-permute-start.16 = (bf16[72,1152]{1,0:T(8,128)(2,1)S(1)}, bf16[72,1152]{1,0:T(8,128)(2,1)S(1)}, u32[]{:S(2)}, u32[]{:S(2)}) collective-permute-start(bf16[72,1152]{1,0:T(8,128)(2,1)S(1)} %add_convert_fusion.3), channel_id=1, source_target_pairs={{0,16},{4,20},{8,24},{12,28},{16,0},{20,4},{24,8},{28,12},{1,17},{... | collective-permute-start | bytes 497672 | tf_op jit(solution)/shard_map/ppermute | solution.py:304
  51.0 2.0 %shard_map.83 = f32[256,1152]{1,0:T(8,128)} custom-call(bf16[512,1152]{1,0:T(8,128)(2,1)S(1)} %get-tuple-element.119.back, bf16[1152,1152]{1,0:T(8,128)(2,1)S(1)} %get-tuple-element.72.refs_5_.refs_3_.head), custom_call_target="tpu_custom_call" | custom-call | flops 1358954496 | tf_op jit(solution)/shard_map/pallas_call | solution.py:291
  53.0 2.0 %shard_map.82 = f32[256,1152]{1,0:T(8,128)} custom-call(bf16[512,1152]{1,0:T(8,128)(2,1)S(1)} %get-tuple-element.118.back, bf16[1152,1152]{1,0:T(8,128)(2,1)S(1)} %get-tuple-element.89.image_head.head), custom_call_target="tpu_custom_call" | custom-call | flops 1358954496 | tf_op jit(solution)/shard_map/pallas_call | solution.py:291
  55.1 2.6 %collective-permute-done.22 = bf16[72,1152]{1,0:T(8,128)(2,1)S(1)} collective-permute-done((bf16[72,1152]{1,0:T(8,128)(2,1)S(1)}, bf16[72,1152]{1,0:T(8,128)(2,1)S(1)}, u32[]{:S(2)}, u32[]{:S(2)}) %collective-permute-start.22) | collective-permute-done | bytes 165920 | tf_op jit(solution)/shard_map/ppermute | solution.py:304
  57.7 1.5 %collective-permute-start.23 = (bf16[72,1152]{1,0:T(8,128)(2,1)S(1)}, bf16[72,1152]{1,0:T(8,128)(2,1)S(1)}, u32[]{:S(2)}, u32[]{:S(2)}) collective-permute-start(bf16[72,1152]{1,0:T(8,128)(2,1)S(1)} %add_convert_fusion.1), channel_id=1, source_target_pairs={{0,16},{4,20},{8,24},{12,28},{16,0},{20,4},{24,8},{28,12},{1,17},{... | collective-permute-start | bytes 497672 | tf_op jit(solution)/shard_map/ppermute | solution.py:304
  59.3 1.7 %collective-permute-start.17 = (bf16[72,1152]{1,0:T(8,128)(2,1)S(1)}, bf16[72,1152]{1,0:T(8,128)(2,1)S(1)}, u32[]{:S(2)}, u32[]{:S(2)}) collective-permute-start(bf16[72,1152]{1,0:T(8,128)(2,1)S(1)} %add_convert_fusion.2.refs_0_), channel_id=1, source_target_pairs={{0,4},{4,0},{8,12},{12,8},{16,20},{20,16},{24,28},{28,24},{1,5},{5... | collective-permute-start | bytes 497672 | tf_op jit(solution)/shard_map/ppermute | solution.py:304
  61.0 2.4 %collective-permute-start.18 = (bf16[72,1152]{1,0:T(8,128)(2,1)S(1)}, bf16[72,1152]{1,0:T(8,128)(2,1)S(1)}, u32[]{:S(2)}, u32[]{:S(2)}) collective-permute-start(bf16[72,1152]{1,0:T(8,128)(2,1)S(1)} %add_convert_fusion.2.refs_0_), channel_id=1, source_target_pairs={{0,8},{4,12},{8,0},{12,4},{16,24},{20,28},{24,16},{28,20},{1,9},{5... | collective-permute-start | bytes 497672 | tf_op jit(solution)/shard_map/ppermute | solution.py:304
  63.4 1.1 %collective-permute-start.19 = (bf16[72,1152]{1,0:T(8,128)(2,1)S(1)}, bf16[72,1152]{1,0:T(8,128)(2,1)S(1)}, u32[]{:S(2)}, u32[]{:S(2)}) collective-permute-start(bf16[72,1152]{1,0:T(8,128)(2,1)S(1)} %add_convert_fusion.2.refs_0_), channel_id=1, source_target_pairs={{0,12},{4,8},{8,4},{12,0},{16,28},{20,24},{24,20},{28,16},{1,13},{... | collective-permute-start | bytes 497672 | tf_op jit(solution)/shard_map/ppermute | solution.py:304
  64.4 1.4 %collective-permute-done.23 = bf16[72,1152]{1,0:T(8,128)(2,1)S(1)} collective-permute-done((bf16[72,1152]{1,0:T(8,128)(2,1)S(1)}, bf16[72,1152]{1,0:T(8,128)(2,1)S(1)}, u32[]{:S(2)}, u32[]{:S(2)}) %collective-permute-start.23) | collective-permute-done | bytes 165920 | tf_op jit(solution)/shard_map/ppermute | solution.py:304
  67.4 1.6 %collective-permute-start.25 = (bf16[72,1152]{1,0:T(8,128)(2,1)S(1)}, bf16[72,1152]{1,0:T(8,128)(2,1)S(1)}, u32[]{:S(2)}, u32[]{:S(2)}) collective-permute-start(bf16[72,1152]{1,0:T(8,128)(2,1)S(1)} %add_convert_fusion.refs_0_), channel_id=1, source_target_pairs={{0,8},{4,12},{8,0},{12,4},{16,24},{20,28},{24,16},{28,20},{1,9},{5... | collective-permute-start | bytes 497672 | tf_op jit(solution)/shard_map/ppermute | solution.py:304
  69.1 1.1 %collective-permute-start.26 = (bf16[72,1152]{1,0:T(8,128)(2,1)S(1)}, bf16[72,1152]{1,0:T(8,128)(2,1)S(1)}, u32[]{:S(2)}, u32[]{:S(2)}) collective-permute-start(bf16[72,1152]{1,0:T(8,128)(2,1)S(1)} %add_convert_fusion.refs_0_), channel_id=1, source_target_pairs={{0,12},{4,8},{8,4},{12,0},{16,28},{20,24},{24,20},{28,16},{1,13},{... | collective-permute-start | bytes 497672 | tf_op jit(solution)/shard_map/ppermute | solution.py:304
  70.2 3.1 %collective-permute-done.19.refs_3_ = bf16[72,1152]{1,0:T(8,128)(2,1)S(1)} collective-permute-done((bf16[72,1152]{1,0:T(8,128)(2,1)S(1)}, bf16[72,1152]{1,0:T(8,128)(2,1)S(1)}, u32[]{:S(2)}, u32[]{:S(2)}) %collective-permute-start.19) | collective-permute-done | bytes 165920 | tf_op jit(solution)/shard_map/ppermute | solution.py:304
  73.3 1.7 %shard_map.84 = f32[288,1152]{1,0:T(8,128)} custom-call(s32[2]{0:T(128)S(1)} %pad_add_fusion.place, bf16[72,1152]{1,0:T(8,128)(2,1)S(1)} %add_convert_fusion.2.refs_0_, bf16[72,1152]{1,0:T(8,128)(2,1)S(1)} %collective-permute-done.17.refs_1_, bf16[72,1152]{1,0:T(8,128)(2,1)S(1)} %collective-permute-done.18.refs_2_, ...), custom_call_target="tpu_custom_call" | custom-call | tf_op jit(solution)/shard_map/pallas_call | solution.py:291
  75.0 1.8 %collective-permute-done.26.refs_3_ = bf16[72,1152]{1,0:T(8,128)(2,1)S(1)} collective-permute-done((bf16[72,1152]{1,0:T(8,128)(2,1)S(1)}, bf16[72,1152]{1,0:T(8,128)(2,1)S(1)}, u32[]{:S(2)}, u32[]{:S(2)}) %collective-permute-start.26) | collective-permute-done | bytes 165920 | tf_op jit(solution)/shard_map/ppermute | solution.py:304
  76.8 1.7 %shard_map.85 = f32[288,1152]{1,0:T(8,128)} custom-call(s32[2]{0:T(128)S(1)} %pad_add_fusion.place, bf16[72,1152]{1,0:T(8,128)(2,1)S(1)} %add_convert_fusion.refs_0_, bf16[72,1152]{1,0:T(8,128)(2,1)S(1)} %collective-permute-done.24.refs_1_, bf16[72,1152]{1,0:T(8,128)(2,1)S(1)} %collective-permute-done.25.refs_2_, ...), custom_call_target="tpu_custom_call" | custom-call | tf_op jit(solution)/shard_map/pallas_call | solution.py:291
  (46 shorter events, 8.0 us)
Async XLA Ops:
  0.7 4.7 %collective-permute-start.2 = (bf16[256,1152]{1,0:T(8,128)(2,1)}, bf16[256,1152]{1,0:T(8,128)(2,1)S(1)}, u32[]{:S(2)}, u32[]{:S(2)}) collective-permute-start(bf16[256,1152]{1,0:T(8,128)(2,1)} %t0_far), channel_id=1, source_target_pairs={{0,1},{1,0},{2,3},{3,2},{4,5},{5,4},{6,7},{7,6},{8,9},{9,8},{10,11... | collective-permute-start | bytes 1769480 | tf_op jit(solution)/shard_map/ppermute | solution.py:304
  1.2 4.3 %collective-permute-start.3 = (bf16[256,1152]{1,0:T(8,128)(2,1)}, bf16[256,1152]{1,0:T(8,128)(2,1)S(1)}, u32[]{:S(2)}, u32[]{:S(2)}) collective-permute-start(bf16[256,1152]{1,0:T(8,128)(2,1)} %i0_far), channel_id=1, source_target_pairs={{0,1},{1,0},{2,3},{3,2},{4,5},{5,4},{6,7},{7,6},{8,9},{9,8},{10,11... | collective-permute-start | bytes 1769480 | tf_op jit(solution)/shard_map/ppermute | solution.py:304
  2.3 10.8 %collective-permute-start.1 = (bf16[128,1152]{1,0:T(8,128)(2,1)S(1)}, bf16[128,1152]{1,0:T(8,128)(2,1)S(1)}, u32[]{:S(2)}, u32[]{:S(2)}) collective-permute-start(bf16[128,1152]{1,0:T(8,128)(2,1)S(1)} %get-tuple-element.128), channel_id=1, source_target_pairs={{0,2},{1,3},{2,0},{3,1},{4,6},{5,7},{6,4},{7,5},{8,10},{9,11},{10,... | collective-permute-start | bytes 884744 | tf_op jit(solution)/shard_map/ppermute | solution.py:304
  5.3 8.4 %copy-start = (bf16[256,1152]{1,0:T(8,128)(2,1)S(1)}, bf16[256,1152]{1,0:T(8,128)(2,1)}, u32[]{:S(2)}) copy-start(bf16[256,1152]{1,0:T(8,128)(2,1)} %i0_far) | copy-start | bytes 1769476
  5.3 14.6 %collective-permute-start = (bf16[128,1152]{1,0:T(8,128)(2,1)S(1)}, bf16[128,1152]{1,0:T(8,128)(2,1)S(1)}, u32[]{:S(2)}, u32[]{:S(2)}) collective-permute-start(bf16[128,1152]{1,0:T(8,128)(2,1)S(1)} %get-tuple-element.129), channel_id=1, source_target_pairs={{0,2},{1,3},{2,0},{3,1},{4,6},{5,7},{6,4},{7,5},{8,10},{9,11},{10,... | collective-permute-start | bytes 884744 | tf_op jit(solution)/shard_map/ppermute | solution.py:304
  13.2 2.6 %collective-permute-start.4 = (bf16[64,1152]{1,0:T(8,128)(2,1)S(1)}, bf16[64,1152]{1,0:T(8,128)(2,1)S(1)}, u32[]{:S(2)}, u32[]{:S(2)}) collective-permute-start(bf16[64,1152]{1,0:T(8,128)(2,1)S(1)} %get-tuple-element.133), channel_id=1, source_target_pairs={{0,1},{1,0},{2,3},{3,2},{4,5},{5,4},{6,7},{7,6},{8,9},{9,8},{10,11... | collective-permute-start | bytes 442376 | tf_op jit(solution)/shard_map/ppermute | solution.py:304
  13.2 2.6 %collective-permute-start.5 = (bf16[64,1152]{1,0:T(8,128)(2,1)S(1)}, bf16[64,1152]{1,0:T(8,128)(2,1)S(1)}, u32[]{:S(2)}, u32[]{:S(2)}) collective-permute-start(bf16[64,1152]{1,0:T(8,128)(2,1)S(1)} %get-tuple-element.132), channel_id=1, source_target_pairs={{0,1},{1,0},{2,3},{3,2},{4,5},{5,4},{6,7},{7,6},{8,9},{9,8},{10,11... | collective-permute-start | bytes 442376 | tf_op jit(solution)/shard_map/ppermute | solution.py:304
  13.7 17.8 %collective-permute-start.9 = (bf16[256,1152]{1,0:T(8,128)(2,1)S(1)}, bf16[256,1152]{1,0:T(8,128)(2,1)S(1)}, u32[]{:S(2)}, u32[]{:S(2)}) collective-permute-start(bf16[256,1152]{1,0:T(8,128)(2,1)S(1)} %copy-done), channel_id=1, source_target_pairs={{0,2},{1,3},{2,0},{3,1},{4,6},{5,7},{6,4},{7,5},{8,10},{9,11},{10,... | collective-permute-start | bytes 1769480 | tf_op jit(solution)/shard_map/ppermute | solution.py:304
  20.0 1.4 %collective-permute-start.6 = (bf16[64,1152]{1,0:T(8,128)(2,1)S(1)}, bf16[64,1152]{1,0:T(8,128)(2,1)S(1)}, u32[]{:S(2)}, u32[]{:S(2)}) collective-permute-start(bf16[64,1152]{1,0:T(8,128)(2,1)S(1)} %get-tuple-element.131), channel_id=1, source_target_pairs={{0,1},{1,0},{2,3},{3,2},{4,5},{5,4},{6,7},{7,6},{8,9},{9,8},{10,11... | collective-permute-start | bytes 442376 | tf_op jit(solution)/shard_map/ppermute | solution.py:304
  20.0 1.6 %collective-permute-start.7 = (bf16[64,1152]{1,0:T(8,128)(2,1)S(1)}, bf16[64,1152]{1,0:T(8,128)(2,1)S(1)}, u32[]{:S(2)}, u32[]{:S(2)}) collective-permute-start(bf16[64,1152]{1,0:T(8,128)(2,1)S(1)} %get-tuple-element.130), channel_id=1, source_target_pairs={{0,1},{1,0},{2,3},{3,2},{4,5},{5,4},{6,7},{7,6},{8,9},{9,8},{10,11... | collective-permute-start | bytes 442376 | tf_op jit(solution)/shard_map/ppermute | solution.py:304
  25.5 10.1 %collective-permute-start.8 = (bf16[144,1152]{1,0:T(8,128)(2,1)S(1)}, bf16[144,1152]{1,0:T(8,128)(2,1)S(1)}, u32[]{:S(2)}, u32[]{:S(2)}) collective-permute-start(bf16[144,1152]{1,0:T(8,128)(2,1)S(1)} %get-tuple-element.82), channel_id=1, source_target_pairs={{0,4},{4,0},{8,12},{12,8},{16,20},{20,16},{24,28},{28,24},{1,5},{5... | collective-permute-start | bytes 995336 | tf_op jit(solution)/shard_map/ppermute | solution.py:304
  27.2 9.7 %collective-permute-start.12 = (bf16[144,1152]{1,0:T(8,128)(2,1)S(1)}, bf16[144,1152]{1,0:T(8,128)(2,1)S(1)}, u32[]{:S(2)}, u32[]{:S(2)}) collective-permute-start(bf16[144,1152]{1,0:T(8,128)(2,1)S(1)} %get-tuple-element.103), channel_id=1, source_target_pairs={{0,8},{4,12},{8,0},{12,4},{16,24},{20,28},{24,16},{28,20},{1,9},{5... | collective-permute-start | bytes 995336 | tf_op jit(solution)/shard_map/ppermute | solution.py:304
  33.5 5.7 %collective-permute-start.13 = (bf16[128,1152]{1,0:T(8,128)(2,1)S(1)}, bf16[128,1152]{1,0:T(8,128)(2,1)S(1)}, u32[]{:S(2)}, u32[]{:S(2)}) collective-permute-start(bf16[128,1152]{1,0:T(8,128)(2,1)S(1)} %get-tuple-element.94.x_second), channel_id=1, source_target_pairs={{0,1},{1,0},{2,3},{3,2},{4,5},{5,4},{6,7},{7,6},{8,9},{9,8},{10,11... | collective-permute-start | bytes 884744 | tf_op jit(solution)/shard_map/ppermute | solution.py:304
  33.6 5.7 %collective-permute-start.11 = (bf16[128,1152]{1,0:T(8,128)(2,1)S(1)}, bf16[128,1152]{1,0:T(8,128)(2,1)S(1)}, u32[]{:S(2)}, u32[]{:S(2)}) collective-permute-start(bf16[128,1152]{1,0:T(8,128)(2,1)S(1)} %get-tuple-element.93.x_first), channel_id=1, source_target_pairs={{0,1},{1,0},{2,3},{3,2},{4,5},{5,4},{6,7},{7,6},{8,9},{9,8},{10,11... | collective-permute-start | bytes 884744 | tf_op jit(solution)/shard_map/ppermute | solution.py:304
  37.0 5.8 %collective-permute-start.14 = (bf16[72,1152]{1,0:T(8,128)(2,1)S(1)}, bf16[72,1152]{1,0:T(8,128)(2,1)S(1)}, u32[]{:S(2)}, u32[]{:S(2)}) collective-permute-start(bf16[72,1152]{1,0:T(8,128)(2,1)S(1)} %add_convert_fusion.6), channel_id=1, source_target_pairs={{0,4},{4,0},{8,12},{12,8},{16,20},{20,16},{24,28},{28,24},{1,5},{5... | collective-permute-start | bytes 497672 | tf_op jit(solution)/shard_map/ppermute | solution.py:304
  37.5 10.4 %collective-permute-start.10 = (bf16[72,1152]{1,0:T(8,128)(2,1)S(1)}, bf16[72,1152]{1,0:T(8,128)(2,1)S(1)}, u32[]{:S(2)}, u32[]{:S(2)}) collective-permute-start(bf16[72,1152]{1,0:T(8,128)(2,1)S(1)} %add_convert_fusion.7), channel_id=1, source_target_pairs={{0,8},{4,12},{8,0},{12,4},{16,24},{20,28},{24,16},{28,20},{1,9},{5... | collective-permute-start | bytes 497672 | tf_op jit(solution)/shard_map/ppermute | solution.py:304
  42.8 5.4 %collective-permute-start.15 = (bf16[72,1152]{1,0:T(8,128)(2,1)S(1)}, bf16[72,1152]{1,0:T(8,128)(2,1)S(1)}, u32[]{:S(2)}, u32[]{:S(2)}) collective-permute-start(bf16[72,1152]{1,0:T(8,128)(2,1)S(1)} %add_convert_fusion.4), channel_id=1, source_target_pairs={{0,2},{1,3},{2,0},{3,1},{4,6},{5,7},{6,4},{7,5},{8,10},{9,11},{10,... | collective-permute-start | bytes 497672 | tf_op jit(solution)/shard_map/ppermute | solution.py:304
  44.4 10.7 %collective-permute-start.20 = (bf16[72,1152]{1,0:T(8,128)(2,1)S(1)}, bf16[72,1152]{1,0:T(8,128)(2,1)S(1)}, u32[]{:S(2)}, u32[]{:S(2)}) collective-permute-start(bf16[72,1152]{1,0:T(8,128)(2,1)S(1)} %get-tuple-element.121), channel_id=1, source_target_pairs={{0,4},{4,0},{8,12},{12,8},{16,20},{20,16},{24,28},{28,24},{1,5},{5... | collective-permute-start | bytes 497672 | tf_op jit(solution)/shard_map/ppermute | solution.py:304
  45.9 9.2 %collective-permute-start.21 = (bf16[72,1152]{1,0:T(8,128)(2,1)S(1)}, bf16[72,1152]{1,0:T(8,128)(2,1)S(1)}, u32[]{:S(2)}, u32[]{:S(2)}) collective-permute-start(bf16[72,1152]{1,0:T(8,128)(2,1)S(1)} %get-tuple-element.123), channel_id=1, source_target_pairs={{0,8},{4,12},{8,0},{12,4},{16,24},{20,28},{24,16},{28,20},{1,9},{5... | collective-permute-start | bytes 497672 | tf_op jit(solution)/shard_map/ppermute | solution.py:304
  46.4 11.3 %collective-permute-start.22 = (bf16[72,1152]{1,0:T(8,128)(2,1)S(1)}, bf16[72,1152]{1,0:T(8,128)(2,1)S(1)}, u32[]{:S(2)}, u32[]{:S(2)}) collective-permute-start(bf16[72,1152]{1,0:T(8,128)(2,1)S(1)} %get-tuple-element.125), channel_id=1, source_target_pairs={{0,12},{4,8},{8,4},{12,0},{16,28},{20,24},{24,20},{28,16},{1,13},{... | collective-permute-start | bytes 497672 | tf_op jit(solution)/shard_map/ppermute | solution.py:304
  48.3 10.9 %collective-permute-start.16 = (bf16[72,1152]{1,0:T(8,128)(2,1)S(1)}, bf16[72,1152]{1,0:T(8,128)(2,1)S(1)}, u32[]{:S(2)}, u32[]{:S(2)}) collective-permute-start(bf16[72,1152]{1,0:T(8,128)(2,1)S(1)} %add_convert_fusion.3), channel_id=1, source_target_pairs={{0,16},{4,20},{8,24},{12,28},{16,0},{20,4},{24,8},{28,12},{1,17},{... | collective-permute-start | bytes 497672 | tf_op jit(solution)/shard_map/ppermute | solution.py:304
  57.7 8.1 %collective-permute-start.23 = (bf16[72,1152]{1,0:T(8,128)(2,1)S(1)}, bf16[72,1152]{1,0:T(8,128)(2,1)S(1)}, u32[]{:S(2)}, u32[]{:S(2)}) collective-permute-start(bf16[72,1152]{1,0:T(8,128)(2,1)S(1)} %add_convert_fusion.1), channel_id=1, source_target_pairs={{0,16},{4,20},{8,24},{12,28},{16,0},{20,4},{24,8},{28,12},{1,17},{... | collective-permute-start | bytes 497672 | tf_op jit(solution)/shard_map/ppermute | solution.py:304
  59.3 7.3 %collective-permute-start.17 = (bf16[72,1152]{1,0:T(8,128)(2,1)S(1)}, bf16[72,1152]{1,0:T(8,128)(2,1)S(1)}, u32[]{:S(2)}, u32[]{:S(2)}) collective-permute-start(bf16[72,1152]{1,0:T(8,128)(2,1)S(1)} %add_convert_fusion.2.refs_0_), channel_id=1, source_target_pairs={{0,4},{4,0},{8,12},{12,8},{16,20},{20,16},{24,28},{28,24},{1,5},{5... | collective-permute-start | bytes 497672 | tf_op jit(solution)/shard_map/ppermute | solution.py:304
  61.0 9.2 %collective-permute-start.18 = (bf16[72,1152]{1,0:T(8,128)(2,1)S(1)}, bf16[72,1152]{1,0:T(8,128)(2,1)S(1)}, u32[]{:S(2)}, u32[]{:S(2)}) collective-permute-start(bf16[72,1152]{1,0:T(8,128)(2,1)S(1)} %add_convert_fusion.2.refs_0_), channel_id=1, source_target_pairs={{0,8},{4,12},{8,0},{12,4},{16,24},{20,28},{24,16},{28,20},{1,9},{5... | collective-permute-start | bytes 497672 | tf_op jit(solution)/shard_map/ppermute | solution.py:304
  63.4 9.9 %collective-permute-start.19 = (bf16[72,1152]{1,0:T(8,128)(2,1)S(1)}, bf16[72,1152]{1,0:T(8,128)(2,1)S(1)}, u32[]{:S(2)}, u32[]{:S(2)}) collective-permute-start(bf16[72,1152]{1,0:T(8,128)(2,1)S(1)} %add_convert_fusion.2.refs_0_), channel_id=1, source_target_pairs={{0,12},{4,8},{8,4},{12,0},{16,28},{20,24},{24,20},{28,16},{1,13},{... | collective-permute-start | bytes 497672 | tf_op jit(solution)/shard_map/ppermute | solution.py:304
  66.6 8.4 %collective-permute-start.24 = (bf16[72,1152]{1,0:T(8,128)(2,1)S(1)}, bf16[72,1152]{1,0:T(8,128)(2,1)S(1)}, u32[]{:S(2)}, u32[]{:S(2)}) collective-permute-start(bf16[72,1152]{1,0:T(8,128)(2,1)S(1)} %add_convert_fusion.refs_0_), channel_id=1, source_target_pairs={{0,4},{4,0},{8,12},{12,8},{16,20},{20,16},{24,28},{28,24},{1,5},{5... | collective-permute-start | bytes 497672 | tf_op jit(solution)/shard_map/ppermute | solution.py:304
  67.4 7.6 %collective-permute-start.25 = (bf16[72,1152]{1,0:T(8,128)(2,1)S(1)}, bf16[72,1152]{1,0:T(8,128)(2,1)S(1)}, u32[]{:S(2)}, u32[]{:S(2)}) collective-permute-start(bf16[72,1152]{1,0:T(8,128)(2,1)S(1)} %add_convert_fusion.refs_0_), channel_id=1, source_target_pairs={{0,8},{4,12},{8,0},{12,4},{16,24},{20,28},{24,16},{28,20},{1,9},{5... | collective-permute-start | bytes 497672 | tf_op jit(solution)/shard_map/ppermute | solution.py:304
  69.1 7.7 %collective-permute-start.26 = (bf16[72,1152]{1,0:T(8,128)(2,1)S(1)}, bf16[72,1152]{1,0:T(8,128)(2,1)S(1)}, u32[]{:S(2)}, u32[]{:S(2)}) collective-permute-start(bf16[72,1152]{1,0:T(8,128)(2,1)S(1)} %add_convert_fusion.refs_0_), channel_id=1, source_target_pairs={{0,12},{4,8},{8,4},{12,0},{16,28},{20,24},{24,20},{28,16},{1,13},{... | collective-permute-start | bytes 497672 | tf_op jit(solution)/shard_map/ppermute | solution.py:304

commit v22 on v21

--- a/solution.py
+++ b/solution.py
@@ -172,8 +172,8 @@
 
 
 def text_kernel(place, *refs):
-    *features, i0, i1, text_head, gx_in, x_a, w_aa = refs[:-7]
-    q_2, y_2, w_a2, gx, gy_a, pick_i, dots = refs[-7:]
+    *features, i0, i1, text_head, gx_in, x_a = refs[:-6]
+    q_2, y_2, w_a2, gx, pick_i, dots = refs[-6:]
     half, width = i0.shape
     q_2[...] = dot_nn(rows_of(features), text_head[...])
     pick = picker(place, pick_i.shape[0] // 2, width, (0, 2))
@@ -183,7 +183,6 @@
     pick_i[:, half:] = dot_nt(pick, i1[...]).astype(BF16)
     weight_rows(dots, w_a2)
     gx[...] = gx_in[...] + dot_nn(w_a2[...], y_2[...])
-    gy_a[...] = dot_tn(w_aa[...], x_a[...])
 
 
 def image_kernel(*refs):
@@ -212,8 +211,9 @@
 
 
 def text_pull_kernel(place, *refs):
-    *features, t0, t1, x_a, w_a2, w_a3, gy_2, gy_3, pick_a, pick_b = refs
+    *features, t0, t1, x_a, w_aa, w_a2, w_a3, gy_a, gy_2, gy_3, pick_a, pick_b = refs
     half = t0.shape[0]
+    gy_a[...] = dot_tn(w_aa[...], x_a[...])
     gy_2[...] = dot_tn(w_a2[...], x_a[...])
     gy_3[...] = dot_tn(w_a3[...], x_a[...])
     pick = picker(place, pick_a.shape[0], t0.shape[1], (0,))
@@ -349,15 +349,15 @@
         far=(t0, i0, text_head, image_head),
     )
     first = both(t2[0], w_aa, 2)
-    q_2, y_2, w_a2, gx, gy_a, pick_i = call(
+    q_2, y_2, w_a2, gx, pick_i = call(
         text_kernel,
-        [tall, tall_b, side_w, wide, wide, pick_two],
+        [tall, tall_b, side_w, wide, pick_two],
         [side_dots],
-        (*first, i0, i1, text_head, gx, x_a, w_aa),
+        (*first, i0, i1, text_head, gx, x_a),
         8,
         place,
     )
-    second = both(t2[1], gy_a, 2)
+    second = both(t2[1], gx, 2)
     part_b, parts_b = ((part, width), BF16), ((2 * part, width), BF16)
     q_3, y_3, w_a3, dp_a, near_0, near_2, near_sent, far_0, far_1, far_sent = call(
         image_kernel,
@@ -367,11 +367,11 @@
         8,
     )
     near_came, far_came = cuts(near_sent, mask=1), cuts(far_sent, mask=2)
-    gy_2, gy_3, pick_a, pick_b = call(
+    gy_a, gy_2, gy_3, pick_a, pick_b = call(
         text_pull_kernel,
-        [tall, tall, pick_one, pick_one],
+        [wide, tall, tall, pick_one, pick_one],
         [],
-        (*first, *second, t0, t1, after(x_a, dp_a), w_a2, w_a3),
+        (*first, *second, t0, t1, after(x_a, dp_a), w_aa, w_a2, w_a3),
         8,
         place,
     )

time: 78.6 us -> 79.8 us (1.015)
  starting transfers between devices: 30.7 us -> 35.1 us
  waiting for transfers between devices: 13.6 us -> 10.1 us
    ppermute x27, starting transfers between devices: 30.7 us -> 35.1 us  [swap(): return lax.ppermute(array, axis, [(i, i ^ mask) for i in range(size)])]
    ppermute x27, waiting for transfers between devices: 13.6 us -> 10.1 us  [swap(): return lax.ppermute(array, axis, [(i, i ^ mask) for i in range(size)])]
  transfers between devices with their start and end apart: 27 -> 27, of which waited for: 12 -> 10; matrix products, arithmetic and copies ran while one was open for 2% -> 2% of each run, Pallas kernels for 38% -> 38%
where the time goes in v22:
time: 79.8 us; the launch traced here: 79.6 us
  starting transfers between devices  35.1 us (44%)
  Pallas kernels  31.9 us (40%)
  waiting for transfers between devices  10.1 us (13%)
  local copies, waits for them, and re-layouts  1.15 us (1%)
    ppermute x27, starting transfers between devices, swap(): return lax.ppermute(array, axis, [(i, i ^ mask) for i in range(size)])  35.1 us
    pallas_call x11, Pallas kernels, call(): pl.pallas_call(kernel, out_shape=[shape(s, t) for s, t in outs], in_specs...  31.9 us
    ppermute x27, waiting for transfers between devices, swap(): return lax.ppermute(array, axis, [(i, i ^ mask) for i in range(size)])  10.1 us
  transfers between devices with their start and end apart: 27, of which 10 were waited for; matrix products, arithmetic and copies ran while one was open for 2% of the time, Pallas kernels for 38%

profile of v22, /device:TPU:0, one launch (start us, length us, event | category | flops | bytes accessed | tf_op | source)
XLA Modules:
  0.0 79.6 jit_solution(7127273611390130963)
XLA Ops:
  1.2 1.1 %fusion = (bf16[128,1152]{1,0:T(8,128)(2,1)S(1)}, bf16[128,1152]{1,0:T(8,128)(2,1)S(1)}) fusion(bf16[256,1152]{1,0:T(8,128)(2,1)} %t0_far), kind=kLoop, calls=%fused_computation.9 | loop fusion | bytes 1179648 | tf_op jit(solution)/shard_map/split | solution.py:330
  2.3 3.0 %collective-permute-start.1 = (bf16[128,1152]{1,0:T(8,128)(2,1)S(1)}, bf16[128,1152]{1,0:T(8,128)(2,1)S(1)}, u32[]{:S(2)}, u32[]{:S(2)}) collective-permute-start(bf16[128,1152]{1,0:T(8,128)(2,1)S(1)} %get-tuple-element.128), channel_id=1, source_target_pairs={{0,2},{1,3},{2,0},{3,1},{4,6},{5,7},{6,4},{7,5},{8,10},{9,11},{10,... | collective-permute-start | bytes 884744 | tf_op jit(solution)/shard_map/ppermute | solution.py:304
  5.4 7.7 %shard_map.75 = (f32[512,1152]{1,0:T(8,128)S(1)}, bf16[512,1152]{1,0:T(8,128)(2,1)S(1)}, f32[512,1152]{1,0:T(8,128)S(1)}, bf16[512,1152]{1,0:T(8,128)(2,1)S(1)},...) custom-call(bf16[256,1152]{1,0:T(8,128)(2,1)S(1)} %collective-permut, ...), custom_call_target="tpu_custom_call" | custom-call | tf_op jit(solution)/shard_map/pallas_call | solution.py:291
  13.7 2.1 %collective-permute-start.9 = (bf16[256,1152]{1,0:T(8,128)(2,1)S(1)}, bf16[256,1152]{1,0:T(8,128)(2,1)S(1)}, u32[]{:S(2)}, u32[]{:S(2)}) collective-permute-start(bf16[256,1152]{1,0:T(8,128)(2,1)S(1)} %copy-done), channel_id=1, source_target_pairs={{0,2},{1,3},{2,0},{3,1},{4,6},{5,7},{6,4},{7,5},{8,10},{9,11},{10,... | collective-permute-start | bytes 1769480 | tf_op jit(solution)/shard_map/ppermute | solution.py:304
  15.8 3.3 %shard_map.76 = (f32[256,1152]{1,0:T(8,128)S(1)}, bf16[256,1152]{1,0:T(8,128)(2,1)S(1)}, bf16[512,256]{1,0:T(8,128)(2,1)S(1)}, f32[512,1152]{1,0:T(8,128)S(1)}, bf16[576,512]{1,0:T(8,128)(2,1)S(1)}) custom-call(s32[2]{0:T(128)S(1)} %pad_add_fusion.place, bf16[128,1152]{1,0:T(8,128)(2,1)S(1)} %collective-permute-done.1.refs_0_, ...), custom_call_target="tpu_custom_call" | custom-call | tf_op jit(solution)/shard_map/pallas_call | solution.py:291
  20.1 0.9 %collective-permute-done.7.refs_2_.refs_5_ = bf16[64,1152]{1,0:T(8,128)(2,1)S(1)} collective-permute-done((bf16[64,1152]{1,0:T(8,128)(2,1)S(1)}, bf16[64,1152]{1,0:T(8,128)(2,1)S(1)}, u32[]{:S(2)}, u32[]{:S(2)}) %collective-permute-start.7) | collective-permute-done | bytes 147488 | tf_op jit(solution)/shard_map/ppermute | solution.py:304
  21.1 4.1 %shard_map.77 = (f32[256,1152]{1,0:T(8,128)S(1)}, bf16[256,1152]{1,0:T(8,128)(2,1)S(1)}, bf16[512,256]{1,0:T(8,128)(2,1)S(1)}, bf16[512,1152]{1,0:T(8,128)(2,1)S...) custom-call(bf16[128,1152]{1,0:T(8,128)(2,1)S(1)} %collective-permut, ...), custom_call_target="tpu_custom_call" | custom-call | tf_op jit(solution)/shard_map/pallas_call | solution.py:291
  25.2 2.2 %collective-permute-start.12 = (bf16[144,1152]{1,0:T(8,128)(2,1)S(1)}, bf16[144,1152]{1,0:T(8,128)(2,1)S(1)}, u32[]{:S(2)}, u32[]{:S(2)}) collective-permute-start(bf16[144,1152]{1,0:T(8,128)(2,1)S(1)} %get-tuple-element.103), channel_id=1, source_target_pairs={{0,8},{4,12},{8,0},{12,4},{16,24},{20,28},{24,16},{28,20},{1,9},{5... | collective-permute-start | bytes 995336 | tf_op jit(solution)/shard_map/ppermute | solution.py:304
  27.4 1.5 %collective-permute-start.8 = (bf16[144,1152]{1,0:T(8,128)(2,1)S(1)}, bf16[144,1152]{1,0:T(8,128)(2,1)S(1)}, u32[]{:S(2)}, u32[]{:S(2)}) collective-permute-start(bf16[144,1152]{1,0:T(8,128)(2,1)S(1)} %get-tuple-element.81), channel_id=1, source_target_pairs={{0,4},{4,0},{8,12},{12,8},{16,20},{20,16},{24,28},{28,24},{1,5},{5... | collective-permute-start | bytes 995336 | tf_op jit(solution)/shard_map/ppermute | solution.py:304
  28.9 3.1 %shard_map.78 = (f32[512,1152]{1,0:T(8,128)S(1)}, f32[256,1152]{1,0:T(8,128)S(1)}, f32[256,1152]{1,0:T(8,128)S(1)}, bf16[288,512]{1,0:T(8,128)(2,1)S(1)}, bf16[288,512]{1,0:T(8,128)(2,1)S(1)}) custom-call(s32[2]{0:T(128)S(1)} %pad_add_fusion.place, bf16[128,1152]{1,0:T(8,128)(2,1)S(1)} %collective-permute-done.1.refs_0_, ...), custom_call_target="tpu_custom_call" | custom-call | tf_op jit(solution)/shard_map/pallas_call | solution.py:291
  32.0 1.9 %shard_map.79 = (bf16[128,1152]{1,0:T(8,128)(2,1)S(1)}, bf16[128,1152]{1,0:T(8,128)(2,1)S(1)}, bf16[256,512]{1,0:T(8,128)(2,1)S(1)}, bf16[256,256]{1,0:T(8,128)(2,1)S(1)}, bf16[256,256]{1,0:T(8,128)(2,1)S(1)}) custom-call(bf16[256,1152]{1,0:T(8,128)(2,1)S(1)} %collective-permute-done.9.i2, bf16[1152,1152]{1,0:T(8,128)(2,1)S(1)} %get-tuple-element.88.image_head.head, ...), custom_call_target="tpu_custom_call" | custom-call | tf_op jit(solution)/shard_map/pallas_call | solution.py:291
  34.5 0.9 %shard_map.80 = (f32[512,1152]{1,0:T(8,128)S(1)}, f32[256,1152]{1,0:T(8,128)S(1)}, f32[256,1152]{1,0:T(8,128)S(1)}) custom-call(bf16[128,1152]{1,0:T(8,128)(2,1)S(1)} %get-tuple-element.92.x_first, bf16[128,1152]{1,0:T(8,128)(2,1)S(1)} %get-tuple-element.93.x_second, bf16[256,512]{1,0:T(8,128)(2,1)S(1)} %get-tuple-element.94.w_a, ...), custom_call_target="tpu_custom_call" | custom-call | tf_op jit(solution)/shard_map/pallas_call | solution.py:291
  35.7 1.5 %collective-permute-done.8 = bf16[144,1152]{1,0:T(8,128)(2,1)S(1)} collective-permute-done((bf16[144,1152]{1,0:T(8,128)(2,1)S(1)}, bf16[144,1152]{1,0:T(8,128)(2,1)S(1)}, u32[]{:S(2)}, u32[]{:S(2)}) %collective-permute-start.8) | collective-permute-done | bytes 331808 | tf_op jit(solution)/shard_map/ppermute | solution.py:304
  37.2 1.6 %collective-permute-start.14 = (bf16[72,1152]{1,0:T(8,128)(2,1)S(1)}, bf16[72,1152]{1,0:T(8,128)(2,1)S(1)}, u32[]{:S(2)}, u32[]{:S(2)}) collective-permute-start(bf16[72,1152]{1,0:T(8,128)(2,1)S(1)} %add_convert_fusion.6), channel_id=1, source_target_pairs={{0,4},{4,0},{8,12},{12,8},{16,20},{20,16},{24,28},{28,24},{1,5},{5... | collective-permute-start | bytes 497672 | tf_op jit(solution)/shard_map/ppermute | solution.py:304
  39.3 3.5 %shard_map.81 = (bf16[72,1152]{1,0:T(8,128)(2,1)S(1)}, bf16[72,1152]{1,0:T(8,128)(2,1)S(1)}, bf16[72,1152]{1,0:T(8,128)(2,1)S(1)}, bf16[72,1152]{1,0:T(8,128)(2,1)S(1)}, bf16[512,1152]{1,0:T(8,128)(2,1)S(1)}) custom-call(bf16[128,1152]{1,0:T(8,128)(2,1)S(1)} %collective-permute-done.11.x_first, bf16[128,1152]{1,0:T(8,128)(2,1)S(1)} %collective-permute-done.13.x_second, ...), custom_call_target="tpu_custom_call" | custom-call | tf_op jit(solution)/shard_map/pallas_call | solution.py:291
  43.0 1.6 %collective-permute-start.15 = (bf16[72,1152]{1,0:T(8,128)(2,1)S(1)}, bf16[72,1152]{1,0:T(8,128)(2,1)S(1)}, u32[]{:S(2)}, u32[]{:S(2)}) collective-permute-start(bf16[72,1152]{1,0:T(8,128)(2,1)S(1)} %add_convert_fusion.4), channel_id=1, source_target_pairs={{0,2},{1,3},{2,0},{3,1},{4,6},{5,7},{6,4},{7,5},{8,10},{9,11},{10,... | collective-permute-start | bytes 497672 | tf_op jit(solution)/shard_map/ppermute | solution.py:304
  44.5 1.2 %collective-permute-start.20 = (bf16[72,1152]{1,0:T(8,128)(2,1)S(1)}, bf16[72,1152]{1,0:T(8,128)(2,1)S(1)}, u32[]{:S(2)}, u32[]{:S(2)}) collective-permute-start(bf16[72,1152]{1,0:T(8,128)(2,1)S(1)} %get-tuple-element.121), channel_id=1, source_target_pairs={{0,4},{4,0},{8,12},{12,8},{16,20},{20,16},{24,28},{28,24},{1,5},{5... | collective-permute-start | bytes 497672 | tf_op jit(solution)/shard_map/ppermute | solution.py:304
  45.7 0.9 %collective-permute-start.21 = (bf16[72,1152]{1,0:T(8,128)(2,1)S(1)}, bf16[72,1152]{1,0:T(8,128)(2,1)S(1)}, u32[]{:S(2)}, u32[]{:S(2)}) collective-permute-start(bf16[72,1152]{1,0:T(8,128)(2,1)S(1)} %get-tuple-element.123), channel_id=1, source_target_pairs={{0,8},{4,12},{8,0},{12,4},{16,24},{20,28},{24,16},{28,20},{1,9},{5... | collective-permute-start | bytes 497672 | tf_op jit(solution)/shard_map/ppermute | solution.py:304
  46.6 1.4 %collective-permute-start.22 = (bf16[72,1152]{1,0:T(8,128)(2,1)S(1)}, bf16[72,1152]{1,0:T(8,128)(2,1)S(1)}, u32[]{:S(2)}, u32[]{:S(2)}) collective-permute-start(bf16[72,1152]{1,0:T(8,128)(2,1)S(1)} %get-tuple-element.125), channel_id=1, source_target_pairs={{0,12},{4,8},{8,4},{12,0},{16,28},{20,24},{24,20},{28,16},{1,13},{... | collective-permute-start | bytes 497672 | tf_op jit(solution)/shard_map/ppermute | solution.py:304
  48.5 2.7 %collective-permute-start.16 = (bf16[72,1152]{1,0:T(8,128)(2,1)S(1)}, bf16[72,1152]{1,0:T(8,128)(2,1)S(1)}, u32[]{:S(2)}, u32[]{:S(2)}) collective-permute-start(bf16[72,1152]{1,0:T(8,128)(2,1)S(1)} %add_convert_fusion.3), channel_id=1, source_target_pairs={{0,16},{4,20},{8,24},{12,28},{16,0},{20,4},{24,8},{28,12},{1,17},{... | collective-permute-start | bytes 497672 | tf_op jit(solution)/shard_map/ppermute | solution.py:304
  51.1 2.0 %shard_map.83 = f32[256,1152]{1,0:T(8,128)} custom-call(bf16[512,1152]{1,0:T(8,128)(2,1)S(1)} %get-tuple-element.119.back, bf16[1152,1152]{1,0:T(8,128)(2,1)S(1)} %get-tuple-element.72.refs_5_.refs_3_.head), custom_call_target="tpu_custom_call" | custom-call | flops 1358954496 | tf_op jit(solution)/shard_map/pallas_call | solution.py:291
  53.2 2.1 %shard_map.82 = f32[256,1152]{1,0:T(8,128)} custom-call(bf16[512,1152]{1,0:T(8,128)(2,1)S(1)} %get-tuple-element.118.back, bf16[1152,1152]{1,0:T(8,128)(2,1)S(1)} %get-tuple-element.88.image_head.head), custom_call_target="tpu_custom_call" | custom-call | flops 1358954496 | tf_op jit(solution)/shard_map/pallas_call | solution.py:291
  55.2 2.9 %collective-permute-done.22 = bf16[72,1152]{1,0:T(8,128)(2,1)S(1)} collective-permute-done((bf16[72,1152]{1,0:T(8,128)(2,1)S(1)}, bf16[72,1152]{1,0:T(8,128)(2,1)S(1)}, u32[]{:S(2)}, u32[]{:S(2)}) %collective-permute-start.22) | collective-permute-done | bytes 165920 | tf_op jit(solution)/shard_map/ppermute | solution.py:304
  58.2 0.9 %collective-permute-start.23 = (bf16[72,1152]{1,0:T(8,128)(2,1)S(1)}, bf16[72,1152]{1,0:T(8,128)(2,1)S(1)}, u32[]{:S(2)}, u32[]{:S(2)}) collective-permute-start(bf16[72,1152]{1,0:T(8,128)(2,1)S(1)} %add_convert_fusion.1), channel_id=1, source_target_pairs={{0,16},{4,20},{8,24},{12,28},{16,0},{20,4},{24,8},{28,12},{1,17},{... | collective-permute-start | bytes 497672 | tf_op jit(solution)/shard_map/ppermute | solution.py:304
  59.2 1.5 %collective-permute-start.17 = (bf16[72,1152]{1,0:T(8,128)(2,1)S(1)}, bf16[72,1152]{1,0:T(8,128)(2,1)S(1)}, u32[]{:S(2)}, u32[]{:S(2)}) collective-permute-start(bf16[72,1152]{1,0:T(8,128)(2,1)S(1)} %add_convert_fusion.2.refs_0_), channel_id=1, source_target_pairs={{0,4},{4,0},{8,12},{12,8},{16,20},{20,16},{24,28},{28,24},{1,5},{5... | collective-permute-start | bytes 497672 | tf_op jit(solution)/shard_map/ppermute | solution.py:304
  60.7 3.4 %collective-permute-start.19 = (bf16[72,1152]{1,0:T(8,128)(2,1)S(1)}, bf16[72,1152]{1,0:T(8,128)(2,1)S(1)}, u32[]{:S(2)}, u32[]{:S(2)}) collective-permute-start(bf16[72,1152]{1,0:T(8,128)(2,1)S(1)} %add_convert_fusion.2.refs_0_), channel_id=1, source_target_pairs={{0,12},{4,8},{8,4},{12,0},{16,28},{20,24},{24,20},{28,16},{1,13},{... | collective-permute-start | bytes 497672 | tf_op jit(solution)/shard_map/ppermute | solution.py:304
  64.1 1.4 %collective-permute-done.23 = bf16[72,1152]{1,0:T(8,128)(2,1)S(1)} collective-permute-done((bf16[72,1152]{1,0:T(8,128)(2,1)S(1)}, bf16[72,1152]{1,0:T(8,128)(2,1)S(1)}, u32[]{:S(2)}, u32[]{:S(2)}) %collective-permute-start.23) | collective-permute-done | bytes 165920 | tf_op jit(solution)/shard_map/ppermute | solution.py:304
  65.6 6.8 %collective-permute-start.26 = (bf16[72,1152]{1,0:T(8,128)(2,1)S(1)}, bf16[72,1152]{1,0:T(8,128)(2,1)S(1)}, u32[]{:S(2)}, u32[]{:S(2)}) collective-permute-start(bf16[72,1152]{1,0:T(8,128)(2,1)S(1)} %add_convert_fusion.refs_0_), channel_id=1, source_target_pairs={{0,12},{4,8},{8,4},{12,0},{16,28},{20,24},{24,20},{28,16},{1,13},{... | collective-permute-start | bytes 497672 | tf_op jit(solution)/shard_map/ppermute | solution.py:304
  72.6 1.4 %collective-permute-start.24 = (bf16[72,1152]{1,0:T(8,128)(2,1)S(1)}, bf16[72,1152]{1,0:T(8,128)(2,1)S(1)}, u32[]{:S(2)}, u32[]{:S(2)}) collective-permute-start(bf16[72,1152]{1,0:T(8,128)(2,1)S(1)} %add_convert_fusion.refs_0_), channel_id=1, source_target_pairs={{0,4},{4,0},{8,12},{12,8},{16,20},{20,16},{24,28},{28,24},{1,5},{5... | collective-permute-start | bytes 497672 | tf_op jit(solution)/shard_map/ppermute | solution.py:304
  74.0 1.7 %shard_map.84 = f32[288,1152]{1,0:T(8,128)} custom-call(s32[2]{0:T(128)S(1)} %pad_add_fusion.place, bf16[72,1152]{1,0:T(8,128)(2,1)S(1)} %add_convert_fusion.2.refs_0_, bf16[72,1152]{1,0:T(8,128)(2,1)S(1)} %collective-permute-done.17.refs_1_, bf16[72,1152]{1,0:T(8,128)(2,1)S(1)} %collective-permute-done.18.refs_2_, ...), custom_call_target="tpu_custom_call" | custom-call | tf_op jit(solution)/shard_map/pallas_call | solution.py:291
  75.7 2.0 %collective-permute-done.25.refs_2_ = bf16[72,1152]{1,0:T(8,128)(2,1)S(1)} collective-permute-done((bf16[72,1152]{1,0:T(8,128)(2,1)S(1)}, bf16[72,1152]{1,0:T(8,128)(2,1)S(1)}, u32[]{:S(2)}, u32[]{:S(2)}) %collective-permute-start.25) | collective-permute-done | bytes 165920 | tf_op jit(solution)/shard_map/ppermute | solution.py:304
  77.9 1.7 %shard_map.85 = f32[288,1152]{1,0:T(8,128)} custom-call(s32[2]{0:T(128)S(1)} %pad_add_fusion.place, bf16[72,1152]{1,0:T(8,128)(2,1)S(1)} %add_convert_fusion.refs_0_, bf16[72,1152]{1,0:T(8,128)(2,1)S(1)} %collective-permute-done.24.refs_1_, bf16[72,1152]{1,0:T(8,128)(2,1)S(1)} %collective-permute-done.25.refs_2_, ...), custom_call_target="tpu_custom_call" | custom-call | tf_op jit(solution)/shard_map/pallas_call | solution.py:291
  (46 shorter events, 5.1 us)
Async XLA Ops:
  0.7 4.7 %collective-permute-start.2 = (bf16[256,1152]{1,0:T(8,128)(2,1)}, bf16[256,1152]{1,0:T(8,128)(2,1)S(1)}, u32[]{:S(2)}, u32[]{:S(2)}) collective-permute-start(bf16[256,1152]{1,0:T(8,128)(2,1)} %t0_far), channel_id=1, source_target_pairs={{0,1},{1,0},{2,3},{3,2},{4,5},{5,4},{6,7},{7,6},{8,9},{9,8},{10,11... | collective-permute-start | bytes 1769480 | tf_op jit(solution)/shard_map/ppermute | solution.py:304
  1.2 4.3 %collective-permute-start.3 = (bf16[256,1152]{1,0:T(8,128)(2,1)}, bf16[256,1152]{1,0:T(8,128)(2,1)S(1)}, u32[]{:S(2)}, u32[]{:S(2)}) collective-permute-start(bf16[256,1152]{1,0:T(8,128)(2,1)} %i0_far), channel_id=1, source_target_pairs={{0,1},{1,0},{2,3},{3,2},{4,5},{5,4},{6,7},{7,6},{8,9},{9,8},{10,11... | collective-permute-start | bytes 1769480 | tf_op jit(solution)/shard_map/ppermute | solution.py:304
  2.3 10.8 %collective-permute-start.1 = (bf16[128,1152]{1,0:T(8,128)(2,1)S(1)}, bf16[128,1152]{1,0:T(8,128)(2,1)S(1)}, u32[]{:S(2)}, u32[]{:S(2)}) collective-permute-start(bf16[128,1152]{1,0:T(8,128)(2,1)S(1)} %get-tuple-element.128), channel_id=1, source_target_pairs={{0,2},{1,3},{2,0},{3,1},{4,6},{5,7},{6,4},{7,5},{8,10},{9,11},{10,... | collective-permute-start | bytes 884744 | tf_op jit(solution)/shard_map/ppermute | solution.py:304
  5.3 8.4 %copy-start = (bf16[256,1152]{1,0:T(8,128)(2,1)S(1)}, bf16[256,1152]{1,0:T(8,128)(2,1)}, u32[]{:S(2)}) copy-start(bf16[256,1152]{1,0:T(8,128)(2,1)} %i0_far) | copy-start | bytes 1769476
  5.3 14.1 %collective-permute-start = (bf16[128,1152]{1,0:T(8,128)(2,1)S(1)}, bf16[128,1152]{1,0:T(8,128)(2,1)S(1)}, u32[]{:S(2)}, u32[]{:S(2)}) collective-permute-start(bf16[128,1152]{1,0:T(8,128)(2,1)S(1)} %get-tuple-element.129), channel_id=1, source_target_pairs={{0,2},{1,3},{2,0},{3,1},{4,6},{5,7},{6,4},{7,5},{8,10},{9,11},{10,... | collective-permute-start | bytes 884744 | tf_op jit(solution)/shard_map/ppermute | solution.py:304
  13.2 2.6 %collective-permute-start.5 = (bf16[64,1152]{1,0:T(8,128)(2,1)S(1)}, bf16[64,1152]{1,0:T(8,128)(2,1)S(1)}, u32[]{:S(2)}, u32[]{:S(2)}) collective-permute-start(bf16[64,1152]{1,0:T(8,128)(2,1)S(1)} %get-tuple-element.132), channel_id=1, source_target_pairs={{0,1},{1,0},{2,3},{3,2},{4,5},{5,4},{6,7},{7,6},{8,9},{9,8},{10,11... | collective-permute-start | bytes 442376 | tf_op jit(solution)/shard_map/ppermute | solution.py:304
  13.2 2.6 %collective-permute-start.4 = (bf16[64,1152]{1,0:T(8,128)(2,1)S(1)}, bf16[64,1152]{1,0:T(8,128)(2,1)S(1)}, u32[]{:S(2)}, u32[]{:S(2)}) collective-permute-start(bf16[64,1152]{1,0:T(8,128)(2,1)S(1)} %get-tuple-element.133), channel_id=1, source_target_pairs={{0,1},{1,0},{2,3},{3,2},{4,5},{5,4},{6,7},{7,6},{8,9},{9,8},{10,11... | collective-permute-start | bytes 442376 | tf_op jit(solution)/shard_map/ppermute | solution.py:304
  13.7 18.3 %collective-permute-start.9 = (bf16[256,1152]{1,0:T(8,128)(2,1)S(1)}, bf16[256,1152]{1,0:T(8,128)(2,1)S(1)}, u32[]{:S(2)}, u32[]{:S(2)}) collective-permute-start(bf16[256,1152]{1,0:T(8,128)(2,1)S(1)} %copy-done), channel_id=1, source_target_pairs={{0,2},{1,3},{2,0},{3,1},{4,6},{5,7},{6,4},{7,5},{8,10},{9,11},{10,... | collective-permute-start | bytes 1769480 | tf_op jit(solution)/shard_map/ppermute | solution.py:304
  19.5 1.4 %collective-permute-start.7 = (bf16[64,1152]{1,0:T(8,128)(2,1)S(1)}, bf16[64,1152]{1,0:T(8,128)(2,1)S(1)}, u32[]{:S(2)}, u32[]{:S(2)}) collective-permute-start(bf16[64,1152]{1,0:T(8,128)(2,1)S(1)} %get-tuple-element.130), channel_id=1, source_target_pairs={{0,1},{1,0},{2,3},{3,2},{4,5},{5,4},{6,7},{7,6},{8,9},{9,8},{10,11... | collective-permute-start | bytes 442376 | tf_op jit(solution)/shard_map/ppermute | solution.py:304
  19.6 1.6 %collective-permute-start.6 = (bf16[64,1152]{1,0:T(8,128)(2,1)S(1)}, bf16[64,1152]{1,0:T(8,128)(2,1)S(1)}, u32[]{:S(2)}, u32[]{:S(2)}) collective-permute-start(bf16[64,1152]{1,0:T(8,128)(2,1)S(1)} %get-tuple-element.131), channel_id=1, source_target_pairs={{0,1},{1,0},{2,3},{3,2},{4,5},{5,4},{6,7},{7,6},{8,9},{9,8},{10,11... | collective-permute-start | bytes 442376 | tf_op jit(solution)/shard_map/ppermute | solution.py:304
  25.2 10.5 %collective-permute-start.12 = (bf16[144,1152]{1,0:T(8,128)(2,1)S(1)}, bf16[144,1152]{1,0:T(8,128)(2,1)S(1)}, u32[]{:S(2)}, u32[]{:S(2)}) collective-permute-start(bf16[144,1152]{1,0:T(8,128)(2,1)S(1)} %get-tuple-element.103), channel_id=1, source_target_pairs={{0,8},{4,12},{8,0},{12,4},{16,24},{20,28},{24,16},{28,20},{1,9},{5... | collective-permute-start | bytes 995336 | tf_op jit(solution)/shard_map/ppermute | solution.py:304
  27.4 9.7 %collective-permute-start.8 = (bf16[144,1152]{1,0:T(8,128)(2,1)S(1)}, bf16[144,1152]{1,0:T(8,128)(2,1)S(1)}, u32[]{:S(2)}, u32[]{:S(2)}) collective-permute-start(bf16[144,1152]{1,0:T(8,128)(2,1)S(1)} %get-tuple-element.81), channel_id=1, source_target_pairs={{0,4},{4,0},{8,12},{12,8},{16,20},{20,16},{24,28},{28,24},{1,5},{5... | collective-permute-start | bytes 995336 | tf_op jit(solution)/shard_map/ppermute | solution.py:304
  34.0 5.4 %collective-permute-start.11 = (bf16[128,1152]{1,0:T(8,128)(2,1)S(1)}, bf16[128,1152]{1,0:T(8,128)(2,1)S(1)}, u32[]{:S(2)}, u32[]{:S(2)}) collective-permute-start(bf16[128,1152]{1,0:T(8,128)(2,1)S(1)} %get-tuple-element.92.x_first), channel_id=1, source_target_pairs={{0,1},{1,0},{2,3},{3,2},{4,5},{5,4},{6,7},{7,6},{8,9},{9,8},{10,11... | collective-permute-start | bytes 884744 | tf_op jit(solution)/shard_map/ppermute | solution.py:304
  34.0 5.3 %collective-permute-start.13 = (bf16[128,1152]{1,0:T(8,128)(2,1)S(1)}, bf16[128,1152]{1,0:T(8,128)(2,1)S(1)}, u32[]{:S(2)}, u32[]{:S(2)}) collective-permute-start(bf16[128,1152]{1,0:T(8,128)(2,1)S(1)} %get-tuple-element.93.x_second), channel_id=1, source_target_pairs={{0,1},{1,0},{2,3},{3,2},{4,5},{5,4},{6,7},{7,6},{8,9},{9,8},{10,11... | collective-permute-start | bytes 884744 | tf_op jit(solution)/shard_map/ppermute | solution.py:304
  37.2 5.7 %collective-permute-start.14 = (bf16[72,1152]{1,0:T(8,128)(2,1)S(1)}, bf16[72,1152]{1,0:T(8,128)(2,1)S(1)}, u32[]{:S(2)}, u32[]{:S(2)}) collective-permute-start(bf16[72,1152]{1,0:T(8,128)(2,1)S(1)} %add_convert_fusion.6), channel_id=1, source_target_pairs={{0,4},{4,0},{8,12},{12,8},{16,20},{20,16},{24,28},{28,24},{1,5},{5... | collective-permute-start | bytes 497672 | tf_op jit(solution)/shard_map/ppermute | solution.py:304
  38.8 9.2 %collective-permute-start.10 = (bf16[72,1152]{1,0:T(8,128)(2,1)S(1)}, bf16[72,1152]{1,0:T(8,128)(2,1)S(1)}, u32[]{:S(2)}, u32[]{:S(2)}) collective-permute-start(bf16[72,1152]{1,0:T(8,128)(2,1)S(1)} %add_convert_fusion.7), channel_id=1, source_target_pairs={{0,8},{4,12},{8,0},{12,4},{16,24},{20,28},{24,16},{28,20},{1,9},{5... | collective-permute-start | bytes 497672 | tf_op jit(solution)/shard_map/ppermute | solution.py:304
  43.0 5.4 %collective-permute-start.15 = (bf16[72,1152]{1,0:T(8,128)(2,1)S(1)}, bf16[72,1152]{1,0:T(8,128)(2,1)S(1)}, u32[]{:S(2)}, u32[]{:S(2)}) collective-permute-start(bf16[72,1152]{1,0:T(8,128)(2,1)S(1)} %add_convert_fusion.4), channel_id=1, source_target_pairs={{0,2},{1,3},{2,0},{3,1},{4,6},{5,7},{6,4},{7,5},{8,10},{9,11},{10,... | collective-permute-start | bytes 497672 | tf_op jit(solution)/shard_map/ppermute | solution.py:304
  44.5 10.7 %collective-permute-start.20 = (bf16[72,1152]{1,0:T(8,128)(2,1)S(1)}, bf16[72,1152]{1,0:T(8,128)(2,1)S(1)}, u32[]{:S(2)}, u32[]{:S(2)}) collective-permute-start(bf16[72,1152]{1,0:T(8,128)(2,1)S(1)} %get-tuple-element.121), channel_id=1, source_target_pairs={{0,4},{4,0},{8,12},{12,8},{16,20},{20,16},{24,28},{28,24},{1,5},{5... | collective-permute-start | bytes 497672 | tf_op jit(solution)/shard_map/ppermute | solution.py:304
  45.7 9.5 %collective-permute-start.21 = (bf16[72,1152]{1,0:T(8,128)(2,1)S(1)}, bf16[72,1152]{1,0:T(8,128)(2,1)S(1)}, u32[]{:S(2)}, u32[]{:S(2)}) collective-permute-start(bf16[72,1152]{1,0:T(8,128)(2,1)S(1)} %get-tuple-element.123), channel_id=1, source_target_pairs={{0,8},{4,12},{8,0},{12,4},{16,24},{20,28},{24,16},{28,20},{1,9},{5... | collective-permute-start | bytes 497672 | tf_op jit(solution)/shard_map/ppermute | solution.py:304
  46.6 11.5 %collective-permute-start.22 = (bf16[72,1152]{1,0:T(8,128)(2,1)S(1)}, bf16[72,1152]{1,0:T(8,128)(2,1)S(1)}, u32[]{:S(2)}, u32[]{:S(2)}) collective-permute-start(bf16[72,1152]{1,0:T(8,128)(2,1)S(1)} %get-tuple-element.125), channel_id=1, source_target_pairs={{0,12},{4,8},{8,4},{12,0},{16,28},{20,24},{24,20},{28,16},{1,13},{... | collective-permute-start | bytes 497672 | tf_op jit(solution)/shard_map/ppermute | solution.py:304
  48.5 10.7 %collective-permute-start.16 = (bf16[72,1152]{1,0:T(8,128)(2,1)S(1)}, bf16[72,1152]{1,0:T(8,128)(2,1)S(1)}, u32[]{:S(2)}, u32[]{:S(2)}) collective-permute-start(bf16[72,1152]{1,0:T(8,128)(2,1)S(1)} %add_convert_fusion.3), channel_id=1, source_target_pairs={{0,16},{4,20},{8,24},{12,28},{16,0},{20,4},{24,8},{28,12},{1,17},{... | collective-permute-start | bytes 497672 | tf_op jit(solution)/shard_map/ppermute | solution.py:304
  58.2 7.3 %collective-permute-start.23 = (bf16[72,1152]{1,0:T(8,128)(2,1)S(1)}, bf16[72,1152]{1,0:T(8,128)(2,1)S(1)}, u32[]{:S(2)}, u32[]{:S(2)}) collective-permute-start(bf16[72,1152]{1,0:T(8,128)(2,1)S(1)} %add_convert_fusion.1), channel_id=1, source_target_pairs={{0,16},{4,20},{8,24},{12,28},{16,0},{20,4},{24,8},{28,12},{1,17},{... | collective-permute-start | bytes 497672 | tf_op jit(solution)/shard_map/ppermute | solution.py:304
  59.2 6.4 %collective-permute-start.17 = (bf16[72,1152]{1,0:T(8,128)(2,1)S(1)}, bf16[72,1152]{1,0:T(8,128)(2,1)S(1)}, u32[]{:S(2)}, u32[]{:S(2)}) collective-permute-start(bf16[72,1152]{1,0:T(8,128)(2,1)S(1)} %add_convert_fusion.2.refs_0_), channel_id=1, source_target_pairs={{0,4},{4,0},{8,12},{12,8},{16,20},{20,16},{24,28},{28,24},{1,5},{5... | collective-permute-start | bytes 497672 | tf_op jit(solution)/shard_map/ppermute | solution.py:304
  60.7 13.3 %collective-permute-start.19 = (bf16[72,1152]{1,0:T(8,128)(2,1)S(1)}, bf16[72,1152]{1,0:T(8,128)(2,1)S(1)}, u32[]{:S(2)}, u32[]{:S(2)}) collective-permute-start(bf16[72,1152]{1,0:T(8,128)(2,1)S(1)} %add_convert_fusion.2.refs_0_), channel_id=1, source_target_pairs={{0,12},{4,8},{8,4},{12,0},{16,28},{20,24},{24,20},{28,16},{1,13},{... | collective-permute-start | bytes 497672 | tf_op jit(solution)/shard_map/ppermute | solution.py:304
  64.1 9.9 %collective-permute-start.18 = (bf16[72,1152]{1,0:T(8,128)(2,1)S(1)}, bf16[72,1152]{1,0:T(8,128)(2,1)S(1)}, u32[]{:S(2)}, u32[]{:S(2)}) collective-permute-start(bf16[72,1152]{1,0:T(8,128)(2,1)S(1)} %add_convert_fusion.2.refs_0_), channel_id=1, source_target_pairs={{0,8},{4,12},{8,0},{12,4},{16,24},{20,28},{24,16},{28,20},{1,9},{5... | collective-permute-start | bytes 497672 | tf_op jit(solution)/shard_map/ppermute | solution.py:304
  65.6 10.1 %collective-permute-start.26 = (bf16[72,1152]{1,0:T(8,128)(2,1)S(1)}, bf16[72,1152]{1,0:T(8,128)(2,1)S(1)}, u32[]{:S(2)}, u32[]{:S(2)}) collective-permute-start(bf16[72,1152]{1,0:T(8,128)(2,1)S(1)} %add_convert_fusion.refs_0_), channel_id=1, source_target_pairs={{0,12},{4,8},{8,4},{12,0},{16,28},{20,24},{24,20},{28,16},{1,13},{... | collective-permute-start | bytes 497672 | tf_op jit(solution)/shard_map/ppermute | solution.py:304
  72.4 5.3 %collective-permute-start.25 = (bf16[72,1152]{1,0:T(8,128)(2,1)S(1)}, bf16[72,1152]{1,0:T(8,128)(2,1)S(1)}, u32[]{:S(2)}, u32[]{:S(2)}) collective-permute-start(bf16[72,1152]{1,0:T(8,128)(2,1)S(1)} %add_convert_fusion.refs_0_), channel_id=1, source_target_pairs={{0,8},{4,12},{8,0},{12,4},{16,24},{20,28},{24,16},{28,20},{1,9},{5... | collective-permute-start | bytes 497672 | tf_op jit(solution)/shard_map/ppermute | solution.py:304
  72.6 5.3 %collective-permute-start.24 = (bf16[72,1152]{1,0:T(8,128)(2,1)S(1)}, bf16[72,1152]{1,0:T(8,128)(2,1)S(1)}, u32[]{:S(2)}, u32[]{:S(2)}) collective-permute-start(bf16[72,1152]{1,0:T(8,128)(2,1)S(1)} %add_convert_fusion.refs_0_), channel_id=1, source_target_pairs={{0,4},{4,0},{8,12},{12,8},{16,20},{20,16},{24,28},{28,24},{1,5},{5... | collective-permute-start | bytes 497672 | tf_op jit(solution)/shard_map/ppermute | solution.py:304
